TPU v7x, 32 devices: a whole 2x2x4 slice. The times are simulated.
32 devices in a mesh: dp: 8 (over z, x), group: 4 (over y, core).
Axes of the slice: x: 2, y: 2, z: 4, core: 2. Of those that a mesh axis runs over, the one named last changes fastest.
Arguments:
- tokens: bfloat16 [4096, 640], P(('dp', 'group')), may hold values from -6 to 6
- doc_ids: int32 [8, 512], P('dp'), may hold values from 0 to 2, as said below
- cotangent: bfloat16 [4096, 640], P(('dp', 'group')), may hold values from -6 to 6
- master: float32 [43520, 128], P(('dp', 'group'))
- first_moment: float32 [43520, 128], P(('dp', 'group')), may hold values from -38.4 to 38.4
- second_moment: float32 [43520, 128], P(('dp', 'group')), may hold values from 2.048 to 32.768
- gains: float32 [3072], replicated, may hold values from -0.5 to 0.5
- gain_first: float32 [3072], replicated, may hold values from -38.4 to 38.4
- gain_second: float32 [3072], replicated, may hold values from 2.048 to 32.768
Outputs:
- block_out: bfloat16 [4096, 640], P(('dp', 'group'))
- input_grad: bfloat16 [4096, 640], P(('dp', 'group'))
- moment_first: float32 [43520, 128], P(('dp', 'group'))
- moment_second: float32 [43520, 128], P(('dp', 'group'))
- master_new: float32 [43520, 128], P(('dp', 'group'))
- gain_moment_first: float32 [3072], replicated
- gain_moment_second: float32 [3072], replicated
- gains_new: float32 [3072], replicated
Inputs may be any that keep to these rules, and one draw needn't show every extreme that they name: `doc_ids`: each sequence holds three documents numbered 0, 1, 2 in order; document 1 begins within the first 128 tokens and ends within the last 128 tokens.
All inputs are finite; a program needn't handle non-finite values.
Results may differ from a plain program's by a relative error of at most 0.015.
Values may be sent and summed in bfloat16 or wider, within the bound.
No kernel may reach another device: no remote copies, remote signals or barrier semaphores. Data moves between devices by JAX's collectives and lax.ppermute only.
A program may use at most 128 MiB of HBM per device.

v0:
```python
import jax
import jax.numpy as jnp
from jax import lax
from jax.sharding import PartitionSpec as P

D = 640
HQ = 4
HD = 256
FF = 2048
WINDOW = 512
STEP = 10


norm_eps = 1e-06
rope_base = 10000.0
beta_first = 0.9
beta_second = 0.999
learn_rate = 0.05
gain_rate = 0.25
adam_floor = 1e-08
weight_decay = 0.1


def shifted(value, axis, steps):
    count = lax.axis_size(axis)
    initial, last = (max(0, -steps), min(count, count - steps))
    return lax.ppermute(value, axis, [(source, source + steps) for source in range(initial, last)])


def rms_norm(values, weight_vec):
    return (
        values
        * lax.rsqrt(jnp.mean(values * values, axis=-1, keepdims=True) + norm_eps)
        * (1.0 + weight_vec)
    )


def positions(doc_row):
    length = doc_row.shape[0]
    counter = jnp.arange(length, dtype=jnp.int32)
    starts_here = jnp.concatenate([jnp.ones((1,), jnp.bool_), doc_row[1:] != doc_row[:-1]])
    begins = lax.cummax(jnp.where(starts_here, counter, jnp.zeros_like(counter)), axis=0)
    return counter - begins


def angles_of(places):
    half_dim = HD // 2
    frequency = rope_base ** (-(jnp.arange(half_dim, dtype=jnp.float32) * 2.0 / HD))
    return places.astype(jnp.float32)[:, None] * frequency[None, :]


def rotate(values, angles):
    half_dim = values.shape[-1] // 2
    first_half = values[..., :half_dim]
    second_half = values[..., half_dim:]
    cosine = jnp.cos(angles)
    sine_part = jnp.sin(angles)
    return jnp.concatenate(
        [
            first_half * cosine - second_half * sine_part,
            second_half * cosine + first_half * sine_part,
        ],
        axis=-1,
    )


def geglu(gate_in, up_in):
    return jax.nn.gelu(gate_in, approximate=True) * up_in


def adam_update(gradient, first_old, second_old, params_old, rate, decay_rate):
    first_new = beta_first * first_old + (1.0 - beta_first) * gradient
    second_new = beta_second * second_old + (1.0 - beta_second) * gradient * gradient
    first_hat = first_new / (1.0 - beta_first**STEP)
    second_hat = second_new / (1.0 - beta_second**STEP)
    params_new = params_old - rate * (
        first_hat / (jnp.sqrt(second_hat) + adam_floor) + decay_rate * params_old
    )
    return (first_new, second_new, params_new)


def piece_rows(device_count):
    return [
        entries // (128 * device_count)
        for entries in (D * HQ * HD, D * HD, D * HD, HQ * HD * D, D * FF, D * FF, FF * D)
    ]


def piece_shapes():
    return [(D, HQ * HD), (D, HD), (D, HD), (HQ * HD, D), (D, FF), (D, FF), (FF, D)]


def split_rows(stacked, row_list):
    result = []
    row_start = 0
    for row_count in row_list:
        result.append(stacked[row_start : row_start + row_count])
        row_start = row_start + row_count
    return result


def matmul(left_side, right_side):
    return jnp.dot(left_side, right_side, preferred_element_type=jnp.float32)


def shards(
    tokens, doc_ids, cotangent, master, first_moment, second_moment, gains, gain_first, gain_second
):
    group_size = lax.axis_size("group")
    devices_all = lax.axis_size("dp") * group_size
    group_index = lax.axis_index("group")
    local_rows = tokens.shape[0]
    shard_parts = [
        part_rows.astype(jnp.bfloat16) for part_rows in split_rows(master, piece_rows(devices_all))
    ]
    gathered = (
        lax.all_gather(shard_parts[0], ("dp", "group"), axis=0, tiled=True),
        lax.all_gather(shard_parts[1], ("dp", "group"), axis=0, tiled=True),
        lax.all_gather(shard_parts[2], ("dp", "group"), axis=0, tiled=True),
        lax.all_gather(shard_parts[3], ("dp", "group"), axis=0, tiled=True),
        lax.all_gather(shard_parts[4], ("dp", "group"), axis=0, tiled=True),
        lax.all_gather(shard_parts[5], ("dp", "group"), axis=0, tiled=True),
        lax.all_gather(shard_parts[6], ("dp", "group"), axis=0, tiled=True),
    )
    query_weight, key_weight, value_weight, out_weight, gate_weight, up_weight, down_weight = [
        full_rows.reshape(shape_pair) for full_rows, shape_pair in zip(gathered, piece_shapes())
    ]
    norm_input = gains[0:D]
    norm_attn = gains[D : 2 * D]
    norm_ffin = gains[2 * D : 3 * D]
    norm_ffout = gains[3 * D : 4 * D]
    norm_query = gains[4 * D : 4 * D + HD]
    norm_key = gains[4 * D + HD : 4 * D + 2 * HD]
    doc_row = doc_ids[0]
    first_row = group_index * local_rows
    angles = lax.dynamic_slice_in_dim(angles_of(positions(doc_row)), first_row, local_rows, 0)
    query_docs = lax.dynamic_slice_in_dim(doc_row, first_row, local_rows, 0)
    inputs = tokens.astype(jnp.float32)
    normed, back_input = jax.vjp(rms_norm, inputs, norm_input)
    normed_low = normed.astype(jnp.bfloat16)
    query_proj = matmul(normed_low, query_weight)
    key_proj = matmul(normed_low, key_weight)
    value_proj = matmul(normed_low, value_weight)

    def query_prep(flat_rows, gain_vec):
        return rotate(rms_norm(flat_rows.reshape(local_rows, HQ, HD), gain_vec), angles[:, None, :])

    def key_prep(rows_in, gain_vec):
        return rotate(rms_norm(rows_in, gain_vec), angles)

    query_rot, back_query = jax.vjp(query_prep, query_proj, norm_query)
    key_rot, back_key = jax.vjp(key_prep, key_proj, norm_key)
    query_low = query_rot.astype(jnp.bfloat16)
    key_low = key_rot.astype(jnp.bfloat16)
    value_low = value_proj.astype(jnp.bfloat16)
    reach = min(-(-(WINDOW - 1) // local_rows), group_size - 1)
    key_list = [key_low]
    value_list = [value_low]
    for offset in range(1, reach + 1):
        key_far, value_far = shifted((key_low, value_low), "group", offset)
        key_list.insert(0, key_far)
        value_list.insert(0, value_far)
    key_all = jnp.concatenate(key_list, axis=0)
    value_all = jnp.concatenate(value_list, axis=0)
    key_count = (reach + 1) * local_rows
    doc_pad = jnp.concatenate([jnp.full((reach * local_rows,), -1, jnp.int32), doc_row])
    key_docs = lax.dynamic_slice_in_dim(doc_pad, first_row, key_count, 0)
    key_index = (group_index - reach) * local_rows + jnp.arange(key_count, dtype=jnp.int32)
    query_index = first_row + jnp.arange(local_rows, dtype=jnp.int32)
    distance = query_index[:, None] - key_index[None, :]
    allowed = (distance >= 0) & (distance < WINDOW) & (key_docs[None, :] == query_docs[:, None])

    def scores_of(key_rows_low):
        raw_scores = jnp.einsum(
            "qhd,kd->hqk", query_low, key_rows_low, preferred_element_type=jnp.float32
        ) * HD ** (-0.5)
        return jnp.where(allowed[None], raw_scores, -1e30)

    masked = scores_of(key_all)
    top_score = jnp.max(masked, axis=-1, keepdims=True)
    log_total = top_score + jnp.log(jnp.sum(jnp.exp(masked - top_score), axis=-1, keepdims=True))
    probs = jnp.exp(masked - log_total)
    attended = jnp.einsum(
        "hqk,kd->qhd", probs.astype(jnp.bfloat16), value_all, preferred_element_type=jnp.float32
    )
    attended_low = attended.reshape(local_rows, HQ * HD).astype(jnp.bfloat16)
    attn_out = matmul(attended_low, out_weight)
    branch_one, back_attn = jax.vjp(rms_norm, attn_out, norm_attn)
    middle = inputs + branch_one
    normed_two, back_ffin = jax.vjp(rms_norm, middle, norm_ffin)
    normed_two_low = normed_two.astype(jnp.bfloat16)
    gate_proj = matmul(normed_two_low, gate_weight)
    up_proj = matmul(normed_two_low, up_weight)
    hidden, back_hidden = jax.vjp(geglu, gate_proj, up_proj)
    hidden_low = hidden.astype(jnp.bfloat16)
    ffn_out = matmul(hidden_low, down_weight)
    branch_two, back_ffout = jax.vjp(rms_norm, ffn_out, norm_ffout)
    outputs = middle + branch_two
    grad_out = cotangent.astype(jnp.float32)
    grad_ffn, grad_gain_ffout = back_ffout(grad_out)
    grad_ffn_low = grad_ffn.astype(jnp.bfloat16)
    grad_down_w = jnp.einsum(
        "tf,td->fd", hidden_low, grad_ffn_low, preferred_element_type=jnp.float32
    )
    grad_hidden = jnp.einsum(
        "td,fd->tf", grad_ffn_low, down_weight, preferred_element_type=jnp.float32
    )
    grad_gate, grad_up = back_hidden(grad_hidden)
    grad_gate_low = grad_gate.astype(jnp.bfloat16)
    grad_up_low = grad_up.astype(jnp.bfloat16)
    grad_gate_w = jnp.einsum(
        "td,tf->df", normed_two_low, grad_gate_low, preferred_element_type=jnp.float32
    )
    grad_up_w = jnp.einsum(
        "td,tf->df", normed_two_low, grad_up_low, preferred_element_type=jnp.float32
    )
    grad_normed_two = jnp.einsum(
        "tf,df->td", grad_gate_low, gate_weight, preferred_element_type=jnp.float32
    ) + jnp.einsum("tf,df->td", grad_up_low, up_weight, preferred_element_type=jnp.float32)
    grad_middle_norm, grad_gain_ffin = back_ffin(grad_normed_two)
    grad_middle = grad_out + grad_middle_norm
    grad_attn, grad_gain_attn = back_attn(grad_middle)
    grad_attn_low = grad_attn.astype(jnp.bfloat16)
    grad_out_w = jnp.einsum(
        "to,td->od", attended_low, grad_attn_low, preferred_element_type=jnp.float32
    )
    grad_attended = jnp.einsum(
        "td,od->to", grad_attn_low, out_weight, preferred_element_type=jnp.float32
    )
    grad_attended_low = grad_attended.astype(jnp.bfloat16).reshape(local_rows, HQ, HD)
    probs_again = jnp.exp(scores_of(key_all) - log_total)
    grad_probs = jnp.einsum(
        "qhd,kd->hqk", grad_attended_low, value_all, preferred_element_type=jnp.float32
    )
    grad_value_all = jnp.einsum(
        "hqk,qhd->kd",
        probs_again.astype(jnp.bfloat16),
        grad_attended_low,
        preferred_element_type=jnp.float32,
    )
    grad_scores = probs_again * (
        grad_probs - jnp.sum(probs_again * grad_probs, axis=-1, keepdims=True)
    )
    grad_scores_low = (grad_scores * HD ** (-0.5)).astype(jnp.bfloat16)
    grad_query = jnp.einsum(
        "hqk,kd->qhd", grad_scores_low, key_all, preferred_element_type=jnp.float32
    )
    grad_key_all = jnp.einsum(
        "hqk,qhd->kd", grad_scores_low, query_low, preferred_element_type=jnp.float32
    )
    key_total = grad_key_all[reach * local_rows :]
    value_total = grad_value_all[reach * local_rows :]
    for offset in range(1, reach + 1):
        row_start = (reach - offset) * local_rows
        key_back, value_back = (
            shifted(
                grad_key_all[row_start : row_start + local_rows].astype(jnp.bfloat16),
                "group",
                -offset,
            ).astype(jnp.float32),
            shifted(
                grad_value_all[row_start : row_start + local_rows].astype(jnp.bfloat16),
                "group",
                -offset,
            ).astype(jnp.float32),
        )
        key_total = key_total + key_back
        value_total = value_total + value_back
    grad_query_proj, grad_gain_query = back_query(grad_query)
    grad_key_proj, grad_gain_key = back_key(key_total)
    grad_query_low = grad_query_proj.astype(jnp.bfloat16)
    grad_key_low = grad_key_proj.astype(jnp.bfloat16)
    grad_value_low = value_total.astype(jnp.bfloat16)
    grad_query_w = jnp.einsum(
        "td,te->de", normed_low, grad_query_low, preferred_element_type=jnp.float32
    )
    grad_key_w = jnp.einsum(
        "td,te->de", normed_low, grad_key_low, preferred_element_type=jnp.float32
    )
    grad_value_w = jnp.einsum(
        "td,te->de", normed_low, grad_value_low, preferred_element_type=jnp.float32
    )
    grad_normed = jnp.einsum(
        "te,de->td", grad_query_low, query_weight, preferred_element_type=jnp.float32
    )
    grad_normed = grad_normed + jnp.einsum(
        "te,de->td", grad_key_low, key_weight, preferred_element_type=jnp.float32
    )
    grad_normed = grad_normed + jnp.einsum(
        "te,de->td", grad_value_low, value_weight, preferred_element_type=jnp.float32
    )
    grad_input_norm, grad_gain_input = back_input(grad_normed)
    grad_inputs = grad_middle + grad_input_norm
    flat_query = grad_query_w.reshape(-1, 128)
    flat_key = grad_key_w.reshape(-1, 128)
    flat_value = grad_value_w.reshape(-1, 128)
    flat_out = grad_out_w.reshape(-1, 128)
    flat_gate = grad_gate_w.reshape(-1, 128)
    flat_up = grad_up_w.reshape(-1, 128)
    flat_down = grad_down_w.reshape(-1, 128)
    reduced = (
        lax.psum_scatter(flat_query, ("dp", "group"), scatter_dimension=0, tiled=True),
        lax.psum_scatter(flat_key, ("dp", "group"), scatter_dimension=0, tiled=True),
        lax.psum_scatter(flat_value, ("dp", "group"), scatter_dimension=0, tiled=True),
        lax.psum_scatter(flat_out, ("dp", "group"), scatter_dimension=0, tiled=True),
        lax.psum_scatter(flat_gate, ("dp", "group"), scatter_dimension=0, tiled=True),
        lax.psum_scatter(flat_up, ("dp", "group"), scatter_dimension=0, tiled=True),
        lax.psum_scatter(flat_down, ("dp", "group"), scatter_dimension=0, tiled=True),
    )
    grads_local = jnp.concatenate(list(reduced), axis=0)
    gain_grads = lax.psum(
        jnp.concatenate(
            [
                grad_gain_input,
                grad_gain_attn,
                grad_gain_ffin,
                grad_gain_ffout,
                grad_gain_query,
                grad_gain_key,
            ]
        ),
        ("dp", "group"),
    )
    moment_first, moment_second, master_new = adam_update(
        grads_local, first_moment, second_moment, master, learn_rate, weight_decay
    )
    gain_moment_first, gain_moment_second, gains_new = adam_update(
        gain_grads, gain_first, gain_second, gains, gain_rate, 0.0
    )
    return (
        outputs.astype(jnp.bfloat16),
        grad_inputs.astype(jnp.bfloat16),
        moment_first,
        moment_second,
        master_new,
        gain_moment_first,
        gain_moment_second,
        gains_new,
    )


def solution(mesh):
    placed = (
        P(("dp", "group"), None),
        P("dp", None),
        P(("dp", "group"), None),
        P(("dp", "group"), None),
        P(("dp", "group"), None),
        P(("dp", "group"), None),
        P(),
        P(),
        P(),
    )
    return jax.shard_map(
        shards,
        mesh=mesh,
        in_specs=placed,
        out_specs=(
            P(("dp", "group"), None),
            P(("dp", "group"), None),
            P(("dp", "group"), None),
            P(("dp", "group"), None),
            P(("dp", "group"), None),
            P(),
            P(),
            P(),
        ),
        check_vma=False,
    )
```

profile of v0, /device:TPU:0, one launch (start us, length us, event | category | flops | bytes accessed | tf_op | source)
XLA Modules:
  0.0 1306.4 jit_solution(4234668894196478791)
XLA Ops:
  11.2 44.2 %all_gather.21 = bf16[1280,128]{1,0:T(8,128)(2,1)S(1)} all-gather(bf16[40,128]{1,0:T(8,128)(2,1)S(1)} %get-tuple-element.40), channel_id=1, replica_groups=mesh['dp'=8,'group'=4] {'dp','group'}, dimensions={0}, use_global_device_ids=true | all-gather | bytes 337920 | tf_op jit(solution)/shard_map/all_gather | solution.py:119
  56.6 2.9 collective-permute-start.2
  62.3 37.2 %all_gather.22 = bf16[1280,128]{1,0:T(8,128)(2,1)S(1)} all-gather(bf16[40,128]{1,0:T(8,128)(2,1)S(1)} %get-tuple-element.41), channel_id=1, replica_groups=mesh['dp'=8,'group'=4] {'dp','group'}, dimensions={0}, use_global_device_ids=true | all-gather | bytes 337920 | tf_op jit(solution)/shard_map/all_gather | solution.py:118
  101.6 2.9 collective-permute-start.5
  104.5 3.9 collective-permute-start.4
  118.4 7.0 all-gather.8.cloned.1.call-done
  131.0 54.8 %all-gather.12.cloned.1.call-done = bf16[10240,128]{1,0:T(8,128)(2,1)} async-done(((bf16[320,128]{1,0:T(8,128)(2,1)}), bf16[10240,128]{1,0:T(8,128)(2,1)}) %all-gather.12.cloned.1.call-update) | async-done | bytes 2621456 | tf_op jit(solution)/shard_map/all_gather | solution.py:122
  185.8 3.8 reshape.317
  189.6 56.4 %all-gather.10.cloned.1.call-done = bf16[10240,128]{1,0:T(8,128)(2,1)} async-done(((bf16[320,128]{1,0:T(8,128)(2,1)}), bf16[10240,128]{1,0:T(8,128)(2,1)}) %all-gather.10.cloned.1.call-update) | async-done | bytes 2621456 | tf_op jit(solution)/shard_map/all_gather | solution.py:121
  246.0 5.2 reshape.316
  256.4 49.9 %all-gather.14.cloned.1.call-done = bf16[10240,128]{1,0:T(8,128)(2,1)} async-done(((bf16[320,128]{1,0:T(8,128)(2,1)}), bf16[10240,128]{1,0:T(8,128)(2,1)}) %all-gather.14.cloned.1.call-update) | async-done | bytes 2621456 | tf_op jit(solution)/shard_map/all_gather | solution.py:123
  306.3 5.5 reshape.318
  311.8 2.7 multiply_reduce_fusion.8
  326.0 2.7 convolution_bitcast_fusion.3
  339.9 3.0 collective-permute-done.8
  343.0 2.8 collective-permute-done.7
  352.5 3.0 collective-permute-done.11
  363.2 3.3 fusion.115
  366.5 6.8 reshape.324
  374.3 3.2 fusion.116
  377.4 6.8 reshape.325
  385.3 3.2 fusion.117
  388.4 6.5 reshape.326
  398.7 38.5 %psum.7 = f32[3072]{0:T(1024)S(1)} all-reduce(f32[3072]{0:T(1024)S(1)} %constant_dynamic-update-slice_fusion.8), channel_id=1, replica_groups=mesh['dp'=8,'group'=4] {'dp','group'}, use_global_device_ids=true, to_apply=%region_30.31 | all-reduce | flops 3072 | bytes 24576 | tf_op jit(solution)/shard_map/psum | solution.py:311
  438.6 30.8 %reduce-scatter.14.cloned.1.call-done = f32[160,128]{1,0:T(8,128)} async-done(((f32[5120,128]{1,0:T(8,128)}), f32[160,128]{1,0:T(8,128)}) %reduce-scatter.14.cloned.1.call-update) | async-done | bytes 81936 | tf_op jit(solution)/shard_map/reduce_scatter | solution.py:302
  470.3 132.2 %reduce-scatter.24.cloned.1.call-done = f32[40,128]{1,0:T(8,128)} async-done(((f32[1280,128]{1,0:T(8,128)}), f32[40,128]{1,0:T(8,128)}) %reduce-scatter.24.cloned.1.call-update) | async-done | bytes 20496
  603.3 132.5 %reduce-scatter.26.cloned.1.call-done = f32[40,128]{1,0:T(8,128)} async-done(((f32[1280,128]{1,0:T(8,128)}), f32[40,128]{1,0:T(8,128)}) %reduce-scatter.26.cloned.1.call-update) | async-done | bytes 20496
  736.5 135.1 %reduce-scatter.16.cloned.1.call-done = f32[160,128]{1,0:T(8,128)} async-done(((f32[5120,128]{1,0:T(8,128)}), f32[160,128]{1,0:T(8,128)}) %reduce-scatter.16.cloned.1.call-update) | async-done | bytes 81936 | tf_op jit(solution)/shard_map/reduce_scatter | solution.py:305
  872.4 140.6 %reduce-scatter.18.cloned.1.call-done = f32[320,128]{1,0:T(8,128)} async-done(((f32[10240,128]{1,0:T(8,128)}), f32[320,128]{1,0:T(8,128)}) %reduce-scatter.18.cloned.1.call-update) | async-done | bytes 163856 | tf_op jit(solution)/shard_map/reduce_scatter | solution.py:306
  1013.9 140.5 %reduce-scatter.20.cloned.1.call-done = f32[320,128]{1,0:T(8,128)} async-done(((f32[10240,128]{1,0:T(8,128)}), f32[320,128]{1,0:T(8,128)}) %reduce-scatter.20.cloned.1.call-update) | async-done | bytes 163856 | tf_op jit(solution)/shard_map/reduce_scatter | solution.py:307
  1155.4 140.5 %reduce-scatter.22.cloned.1.call-done = f32[320,128]{1,0:T(8,128)} async-done(((f32[10240,128]{1,0:T(8,128)}), f32[320,128]{1,0:T(8,128)}) %reduce-scatter.22.cloned.1.call-update) | async-done | bytes 163856 | tf_op jit(solution)/shard_map/reduce_scatter | solution.py:308
  1296.9 2.7 multiply_subtract_fusion
  (334 shorter events, 79.9 us)
Async XLA Ops:
  7.2 48.5 %copy-start.50 = (f32[3072]{0:T(1024)S(1)}, f32[3072]{0:T(1024)}, u32[]{:S(2)}) copy-start(f32[3072]{0:T(1024)} %param.15) | copy-start | bytes 36868
  7.2 54.3 %copy-start.57 = (s32[1,512]{1,0:T(1,128)S(1)}, s32[1,512]{1,0:T(1,128)}, u32[]{:S(2)}) copy-start(s32[1,512]{1,0:T(1,128)} %param.10) | copy-start | bytes 6148
  7.2 104.0 %all-gather.6.cloned.1.call-start = ((), (), s32[]{:S(2)}) async-start(), calls=%async_computation.7 | async-start | bytes 1351680 | tf_op jit(solution)/shard_map/all_gather | solution.py:117
  9.1 116.3 %all-gather.8.cloned.1.call-start = ((), (), s32[]{:S(2)}) async-start(), calls=%async_computation.8 | async-start | bytes 1351680 | tf_op jit(solution)/shard_map/all_gather | solution.py:120
  9.8 176.0 %all-gather.12.cloned.1.call-start = ((), (), s32[]{:S(2)}) async-start(), calls=%async_computation.10 | async-start | bytes 2703360 | tf_op jit(solution)/shard_map/all_gather | solution.py:122
  10.6 235.4 %all-gather.10.cloned.1.call-start = ((), (), s32[]{:S(2)}) async-start(), calls=%async_computation.9 | async-start | bytes 2703360 | tf_op jit(solution)/shard_map/all_gather | solution.py:121
  11.2 295.1 %all-gather.14.cloned.1.call-start = ((), (), s32[]{:S(2)}) async-start(), calls=%async_computation.11 | async-start | bytes 2703360 | tf_op jit(solution)/shard_map/all_gather | solution.py:123
  55.7 58.7 %copy-start.60 = (f32[128]{0:T(128)}, f32[128]{0:T(128)S(1)}, u32[]{:S(2)}) copy-start(f32[128]{0:T(128)S(1)} %fusion.77) | copy-start | bytes 1540
  56.6 71.4 %collective-permute-start.2 = (bf16[128,256]{1,0:T(8,128)(2,1)}, bf16[128,256]{1,0:T(8,128)(2,1)}, u32[]{:S(2)}, u32[]{:S(2)}) collective-permute-start(bf16[128,256]{1,0:T(8,128)(2,1)} %convolution_convert_fusion.2), channel_id=1, source_target_pairs={{0,1},{1,2},{2,3},{4,5},{5,6},{6,7},{8,9},{9,10},{10,11},{12,13},{... | collective-permute-start | bytes 196616 | tf_op jit(solution)/shard_map/ppermute | solution.py:27
  59.5 68.5 %collective-permute-start.1 = (bf16[128,256]{1,0:T(8,128)(2,1)}, bf16[128,256]{1,0:T(8,128)(2,1)}, u32[]{:S(2)}, u32[]{:S(2)}) collective-permute-start(bf16[128,256]{1,0:T(8,128)(2,1)} %convolution_convert_fusion.2), channel_id=1, source_target_pairs={{0,2},{1,3},{4,6},{5,7},{8,10},{9,11},{12,14},{13,15},{16,18},{17,... | collective-permute-start | bytes 196616 | tf_op jit(solution)/shard_map/ppermute | solution.py:27
  61.4 408.1 %reduce-scatter.14.cloned.1.call-start = ((), (), s32[]{:S(2)}) async-start(), calls=%async_computation.12 | async-start | bytes 2703360 | tf_op jit(solution)/shard_map/reduce_scatter | solution.py:302
  61.5 48.8 %copy-start.82 = (f32[128]{0:T(128)}, f32[128]{0:T(128)S(1)}, u32[]{:S(2)}) copy-start(f32[128]{0:T(128)S(1)} %negate_power_fusion) | copy-start | bytes 1540
  61.5 52.9 %copy-start.62 = (f32[256]{0:T(256)}, f32[256]{0:T(256)S(1)}, u32[]{:S(2)}) copy-start(f32[256]{0:T(256)S(1)} %get-tuple-element.58) | copy-start | bytes 3076
  61.5 53.6 %copy-start.67 = (f32[256]{0:T(256)}, f32[256]{0:T(256)S(1)}, u32[]{:S(2)}) copy-start(f32[256]{0:T(256)S(1)} %get-tuple-element.59) | copy-start | bytes 3076
  101.6 13.7 %collective-permute-start.5 = (bf16[128,256]{1,0:T(8,128)(2,1)}, bf16[128,256]{1,0:T(8,128)(2,1)}, u32[]{:S(2)}, u32[]{:S(2)}) collective-permute-start(bf16[128,256]{1,0:T(8,128)(2,1)} %pad_maximum_fusion.3), channel_id=1, source_target_pairs={{0,1},{1,2},{2,3},{4,5},{5,6},{6,7},{8,9},{9,10},{10,11},{12,13},{... | collective-permute-start | bytes 196616 | tf_op jit(solution)/shard_map/ppermute | solution.py:27
  104.5 12.4 collective-permute-start.4
  108.4 8.5 collective-permute-start.3
  115.4 12.6 collective-permute-start
  332.4 270.2 %reduce-scatter.24.cloned.1.call-start = ((), (), s32[]{:S(2)}) async-start(), calls=%async_computation.17 | async-start | bytes 675840
  335.7 4.3 collective-permute-start.6
  337.1 5.9 collective-permute-start.8
  338.4 7.3 collective-permute-start.7
  348.2 387.6 %reduce-scatter.26.cloned.1.call-start = ((), (), s32[]{:S(2)}) async-start(), calls=%async_computation.18 | async-start | bytes 675840
  348.6 3.9 collective-permute-start.9
  349.9 5.6 collective-permute-start.11
  351.2 6.5 collective-permute-start.10
  359.0 512.5 %reduce-scatter.16.cloned.1.call-start = ((), (), s32[]{:S(2)}) async-start(), calls=%async_computation.13 | async-start | bytes 2703360 | tf_op jit(solution)/shard_map/reduce_scatter | solution.py:305
  362.2 650.8 %reduce-scatter.18.cloned.1.call-start = ((), (), s32[]{:S(2)}) async-start(), calls=%async_computation.14 | async-start | bytes 5406720 | tf_op jit(solution)/shard_map/reduce_scatter | solution.py:306
  373.3 781.2 %reduce-scatter.20.cloned.1.call-start = ((), (), s32[]{:S(2)}) async-start(), calls=%async_computation.15 | async-start | bytes 5406720 | tf_op jit(solution)/shard_map/reduce_scatter | solution.py:307
  384.2 911.7 %reduce-scatter.22.cloned.1.call-start = ((), (), s32[]{:S(2)}) async-start(), calls=%async_computation.16 | async-start | bytes 5406720 | tf_op jit(solution)/shard_map/reduce_scatter | solution.py:308
  396.8 900.1 %copy-start.18 = (f32[1360,128]{1,0:T(8,128)S(1)}, f32[1360,128]{1,0:T(8,128)}, u32[]{:S(2)}) copy-start(f32[1360,128]{1,0:T(8,128)} %param.12) | copy-start | bytes 2088964
  396.8 900.1 %copy-start.35 = (f32[1360,128]{1,0:T(8,128)S(1)}, f32[1360,128]{1,0:T(8,128)}, u32[]{:S(2)}) copy-start(f32[1360,128]{1,0:T(8,128)} %param.14) | copy-start | bytes 2088964
  (86 other events, 650.8 us)
Sparse Core Ops, SparseCore 0:
  10.9 57.1 all-gather.5
  70.9 54.3 all-gather.7
  128.8 56.9 all-gather.11
  189.1 56.8 all-gather.9
  249.3 56.8 all-gather.13
  332.5 136.9 reduce-scatter.13
  472.3 130.2 reduce-scatter.23
  605.4 130.2 reduce-scatter.25
  738.0 133.4 reduce-scatter.15
  873.6 139.3 reduce-scatter.17
  1015.3 139.1 reduce-scatter.19
  1156.6 139.2 reduce-scatter.21
where the time goes:
time: 1310 us
  waiting for transfers between devices  1030 us (79%)
  blocking collectives  120 us (9%)
  local copies, waits for them, and re-layouts  61.9 us (5%)
  matrix products  37.4 us (3%)
  starting transfers between devices  23.5 us (2%)
  between operations  15.8 us (1%)
  other arithmetic  15.3 us (1%)
    unnamed x14, waiting for transfers between devices  266 us
    reduce_scatter x1, waiting for transfers between devices, shards(): lax.psum_scatter(flat_gate, ('dp', 'group'), scatter_dimension=0, tiled=T...  141 us
    reduce_scatter x1, waiting for transfers between devices, shards(): lax.psum_scatter(flat_down, ('dp', 'group'), scatter_dimension=0, tiled=T...  141 us
    reduce_scatter x1, waiting for transfers between devices, shards(): lax.psum_scatter(flat_up, ('dp', 'group'), scatter_dimension=0, tiled=True)  141 us
    reduce_scatter x1, waiting for transfers between devices, shards(): lax.psum_scatter(flat_out, ('dp', 'group'), scatter_dimension=0, tiled=True)  135 us
    all_gather x1, waiting for transfers between devices, shards(): lax.all_gather(shard_parts[4], ('dp', 'group'), axis=0, tiled=True)  56.4 us
    all_gather x1, waiting for transfers between devices, shards(): lax.all_gather(shard_parts[5], ('dp', 'group'), axis=0, tiled=True)  54.8 us
    all_gather x1, waiting for transfers between devices, shards(): lax.all_gather(shard_parts[6], ('dp', 'group'), axis=0, tiled=True)  49.9 us
  transfers between devices with their start and end apart: 24, of which 15 were waited for; matrix products, arithmetic and copies ran while one was open for 6% of the time, Pallas kernels for 0%

commit v1 on v0

--- a/solution.py
+++ b/solution.py
@@ -9,6 +9,7 @@
 FF = 2048
 WINDOW = 512
 STEP = 10
+ALL_AXES = ("dp", "group")
 
 
 norm_eps = 1e-06
@@ -103,6 +104,171 @@
     return jnp.dot(left_side, right_side, preferred_element_type=jnp.float32)
 
 
+LOW_COUNT = 8
+
+
+def aligned(device_count):
+    return device_count % LOW_COUNT == 0 and D % device_count == 0
+
+
+def swap(value, mask):
+    count = lax.axis_size(ALL_AXES)
+    return lax.ppermute(value, ALL_AXES, [(source, source ^ mask) for source in range(count)])
+
+
+def gather_high(rows):
+    high_count = lax.axis_size(ALL_AXES) // LOW_COUNT
+    high = lax.axis_index(ALL_AXES) // LOW_COUNT
+    parts = [rows] + [swap(rows, step * LOW_COUNT) for step in range(1, high_count)]
+    return jnp.stack([lax.select_n(high ^ place, *parts) for place in range(high_count)])
+
+
+def scatter_high(blocks):
+    high_count = blocks.shape[0]
+    high = lax.axis_index(ALL_AXES) // LOW_COUNT
+    total = lax.dynamic_index_in_dim(blocks, high, 0, keepdims=False).astype(jnp.float32)
+    sends = [
+        lax.dynamic_index_in_dim(blocks, high ^ step, 0, keepdims=False)
+        for step in range(1, high_count)
+    ]
+    for step, send in enumerate(sends, start=1):
+        total = total + swap(send, step * LOW_COUNT).astype(jnp.float32)
+    return total
+
+
+def gather_relative(block, masks):
+    for mask in masks:
+        block = jnp.concatenate([block, swap(block, mask)], axis=0)
+    return block
+
+
+def scatter_relative(total, masks):
+    for mask in masks:
+        half = total.shape[0] // 2
+        total = total[:half] + swap(total[half:].astype(jnp.bfloat16), mask).astype(jnp.float32)
+    return total
+
+
+def gather_placed(block, masks):
+    low = lax.axis_index(ALL_AXES) % LOW_COUNT
+    high_count, rows, columns = block.shape
+    block = block.reshape(high_count, 1, 1, 1, rows, columns)
+    for mask in masks:
+        axis = {4: 1, 2: 2, 1: 3}[mask]
+        other = swap(block, mask)
+        block = jnp.where(
+            (low & mask) == 0,
+            jnp.concatenate([block, other], axis=axis),
+            jnp.concatenate([other, block], axis=axis),
+        )
+    return block.reshape(high_count * LOW_COUNT * rows, columns)
+
+
+def scatter_placed(total, high_count, masks):
+    low = lax.axis_index(ALL_AXES) % LOW_COUNT
+    columns = total.shape[1]
+    rows = total.shape[0] // (high_count * LOW_COUNT)
+    total = total.reshape(high_count, 2, 2, 2, rows, columns)
+    for mask in masks:
+        axis = {4: 1, 2: 2, 1: 3}[mask]
+        bit = jnp.where((low & mask) == 0, 0, 1)
+        send = lax.dynamic_index_in_dim(total, 1 - bit, axis).astype(jnp.bfloat16)
+        total = lax.dynamic_index_in_dim(total, bit, axis) + swap(send, mask).astype(jnp.float32)
+    return total.reshape(high_count, rows, columns)
+
+
+RELATIVE_MASKS = (4, 2, 1)
+PLACED_MASKS = (2, 4, 1)
+
+
+def width_order(device_count):
+    low = lax.axis_index(ALL_AXES) % LOW_COUNT
+    rows = D // device_count
+    high_count = device_count // LOW_COUNT
+    column = jnp.arange(D, dtype=jnp.int32)
+    place = column // (rows * high_count)
+    mask = (place & 1) * RELATIVE_MASKS[0]
+    mask = mask + ((place >> 1) & 1) * RELATIVE_MASKS[1] + (place >> 2) * RELATIVE_MASKS[2]
+    high = (column // rows) % high_count
+    picked = (high * LOW_COUNT + (low ^ mask)) * rows + column % rows
+    return (jnp.arange(D, dtype=jnp.int32)[:, None] == picked[None, :]).astype(jnp.float32)
+
+
+def gather_weights(master, device_count):
+    shard_parts = [
+        part_rows.astype(jnp.bfloat16) for part_rows in split_rows(master, piece_rows(device_count))
+    ]
+    if not aligned(device_count):
+        full = [
+            lax.all_gather(part, ALL_AXES, axis=0, tiled=True).reshape(shape_pair)
+            for part, shape_pair in zip(shard_parts, piece_shapes())
+        ]
+        return (
+            jnp.concatenate(full[0:3], axis=1),
+            full[3],
+            jnp.concatenate(full[4:6], axis=1),
+            full[6],
+            None,
+        )
+    block_width = D // LOW_COUNT
+    high_count = device_count // LOW_COUNT
+    rows = piece_rows(device_count)
+
+    def high_pieces(first, last):
+        stacked = gather_high(jnp.concatenate(shard_parts[first:last], axis=0))
+        result = []
+        row_start = 0
+        for row_count in rows[first:last]:
+            result.append(stacked[:, row_start : row_start + row_count])
+            row_start = row_start + row_count
+        return result
+
+    query, key, value, out = high_pieces(0, 4)
+    gate, up, down = high_pieces(4, 7)
+    qkv = jnp.concatenate([piece.reshape(block_width, -1) for piece in (query, key, value)], axis=1)
+    gate_up = jnp.concatenate([piece.reshape(block_width, -1) for piece in (gate, up)], axis=1)
+    return (
+        gather_relative(qkv, RELATIVE_MASKS),
+        gather_placed(out.reshape(high_count, -1, D), PLACED_MASKS),
+        gather_relative(gate_up, RELATIVE_MASKS),
+        gather_placed(down.reshape(high_count, -1, D), PLACED_MASKS),
+        width_order(device_count),
+    )
+
+
+def scatter_weights(wide, tall, wide_columns, device_count):
+    splits = [sum(wide_columns[:count]) for count in range(1, len(wide_columns))]
+    if not aligned(device_count):
+        pieces = jnp.split(wide, splits, axis=1) + [tall]
+        return jnp.concatenate(
+            [
+                lax.psum_scatter(
+                    piece.reshape(-1, 128), ALL_AXES, scatter_dimension=0, tiled=True
+                )
+                for piece in pieces
+            ],
+            axis=0,
+        )
+    high_count = device_count // LOW_COUNT
+    wide = scatter_relative(wide, RELATIVE_MASKS[::-1]).astype(jnp.bfloat16)
+    tall = scatter_placed(tall, high_count, PLACED_MASKS[::-1]).astype(jnp.bfloat16)
+    flat = [
+        piece.reshape(high_count, -1, 128) for piece in jnp.split(wide, splits, axis=1) + [tall]
+    ]
+    return scatter_high(jnp.concatenate(flat, axis=1))
+
+
+def sum_gains(values, device_count):
+    if not aligned(device_count):
+        return lax.psum(values, ALL_AXES)
+    values = values.reshape(-1, 128)
+    mask = 1
+    while mask < device_count:
+        values = values + swap(values, mask)
+        mask = mask * 2
+    return values.reshape(-1)
+
+
 def shards(
     tokens, doc_ids, cotangent, master, first_moment, second_moment, gains, gain_first, gain_second
 ):
@@ -110,21 +276,9 @@
     devices_all = lax.axis_size("dp") * group_size
     group_index = lax.axis_index("group")
     local_rows = tokens.shape[0]
-    shard_parts = [
-        part_rows.astype(jnp.bfloat16) for part_rows in split_rows(master, piece_rows(devices_all))
-    ]
-    gathered = (
-        lax.all_gather(shard_parts[0], ("dp", "group"), axis=0, tiled=True),
-        lax.all_gather(shard_parts[1], ("dp", "group"), axis=0, tiled=True),
-        lax.all_gather(shard_parts[2], ("dp", "group"), axis=0, tiled=True),
-        lax.all_gather(shard_parts[3], ("dp", "group"), axis=0, tiled=True),
-        lax.all_gather(shard_parts[4], ("dp", "group"), axis=0, tiled=True),
-        lax.all_gather(shard_parts[5], ("dp", "group"), axis=0, tiled=True),
-        lax.all_gather(shard_parts[6], ("dp", "group"), axis=0, tiled=True),
-    )
-    query_weight, key_weight, value_weight, out_weight, gate_weight, up_weight, down_weight = [
-        full_rows.reshape(shape_pair) for full_rows, shape_pair in zip(gathered, piece_shapes())
-    ]
+    qkv_weight, out_weight, gate_up_weight, down_weight, order = gather_weights(
+        master, devices_all
+    )
     norm_input = gains[0:D]
     norm_attn = gains[D : 2 * D]
     norm_ffin = gains[2 * D : 3 * D]
@@ -135,12 +289,25 @@
     first_row = group_index * local_rows
     angles = lax.dynamic_slice_in_dim(angles_of(positions(doc_row)), first_row, local_rows, 0)
     query_docs = lax.dynamic_slice_in_dim(doc_row, first_row, local_rows, 0)
+
+    def ordered(rows_low):
+        if order is None:
+            return rows_low
+        return matmul(rows_low, order.astype(jnp.bfloat16)).astype(jnp.bfloat16)
+
+    def restored(rows_in):
+        if order is None:
+            return rows_in
+        return jnp.einsum("te,de->td", rows_in, order, precision=lax.Precision.HIGHEST)
+
     inputs = tokens.astype(jnp.float32)
     normed, back_input = jax.vjp(rms_norm, inputs, norm_input)
     normed_low = normed.astype(jnp.bfloat16)
-    query_proj = matmul(normed_low, query_weight)
-    key_proj = matmul(normed_low, key_weight)
-    value_proj = matmul(normed_low, value_weight)
+    normed_low = ordered(normed_low)
+    projections = matmul(normed_low, qkv_weight)
+    query_proj = projections[:, : HQ * HD]
+    key_proj = projections[:, HQ * HD : HQ * HD + HD]
+    value_proj = projections[:, HQ * HD + HD :]
 
     def query_prep(flat_rows, gain_vec):
         return rotate(rms_norm(flat_rows.reshape(local_rows, HQ, HD), gain_vec), angles[:, None, :])
@@ -154,14 +321,13 @@
     key_low = key_rot.astype(jnp.bfloat16)
     value_low = value_proj.astype(jnp.bfloat16)
     reach = min(-(-(WINDOW - 1) // local_rows), group_size - 1)
-    key_list = [key_low]
-    value_list = [value_low]
+    key_value = jnp.concatenate([key_low, value_low], axis=1)
+    key_value_list = [key_value]
     for offset in range(1, reach + 1):
-        key_far, value_far = shifted((key_low, value_low), "group", offset)
-        key_list.insert(0, key_far)
-        value_list.insert(0, value_far)
-    key_all = jnp.concatenate(key_list, axis=0)
-    value_all = jnp.concatenate(value_list, axis=0)
+        key_value_list.insert(0, shifted(key_value, "group", offset))
+    key_value_all = jnp.concatenate(key_value_list, axis=0)
+    key_all = key_value_all[:, :HD]
+    value_all = key_value_all[:, HD:]
     key_count = (reach + 1) * local_rows
     doc_pad = jnp.concatenate([jnp.full((reach * local_rows,), -1, jnp.int32), doc_row])
     key_docs = lax.dynamic_slice_in_dim(doc_pad, first_row, key_count, 0)
@@ -189,8 +355,10 @@
     middle = inputs + branch_one
     normed_two, back_ffin = jax.vjp(rms_norm, middle, norm_ffin)
     normed_two_low = normed_two.astype(jnp.bfloat16)
-    gate_proj = matmul(normed_two_low, gate_weight)
-    up_proj = matmul(normed_two_low, up_weight)
+    normed_two_low = ordered(normed_two_low)
+    gate_up_proj = matmul(normed_two_low, gate_up_weight)
+    gate_proj = gate_up_proj[:, :FF]
+    up_proj = gate_up_proj[:, FF:]
     hidden, back_hidden = jax.vjp(geglu, gate_proj, up_proj)
     hidden_low = hidden.astype(jnp.bfloat16)
     ffn_out = matmul(hidden_low, down_weight)
@@ -206,17 +374,16 @@
         "td,fd->tf", grad_ffn_low, down_weight, preferred_element_type=jnp.float32
     )
     grad_gate, grad_up = back_hidden(grad_hidden)
-    grad_gate_low = grad_gate.astype(jnp.bfloat16)
-    grad_up_low = grad_up.astype(jnp.bfloat16)
-    grad_gate_w = jnp.einsum(
-        "td,tf->df", normed_two_low, grad_gate_low, preferred_element_type=jnp.float32
-    )
-    grad_up_w = jnp.einsum(
-        "td,tf->df", normed_two_low, grad_up_low, preferred_element_type=jnp.float32
-    )
-    grad_normed_two = jnp.einsum(
-        "tf,df->td", grad_gate_low, gate_weight, preferred_element_type=jnp.float32
-    ) + jnp.einsum("tf,df->td", grad_up_low, up_weight, preferred_element_type=jnp.float32)
+    grad_gate_up_low = jnp.concatenate([grad_gate, grad_up], axis=1).astype(jnp.bfloat16)
+    grad_gate_up_w = jnp.einsum(
+        "td,tf->df", normed_two_low, grad_gate_up_low, preferred_element_type=jnp.float32
+    )
+    grads_ffn = scatter_weights(grad_gate_up_w, grad_down_w, (FF, FF), devices_all)
+    grad_normed_two = restored(
+        jnp.einsum(
+            "tf,df->td", grad_gate_up_low, gate_up_weight, preferred_element_type=jnp.float32
+        )
+    )
     grad_middle_norm, grad_gain_ffin = back_ffin(grad_normed_two)
     grad_middle = grad_out + grad_middle_norm
     grad_attn, grad_gain_attn = back_attn(grad_middle)
@@ -248,67 +415,33 @@
     grad_key_all = jnp.einsum(
         "hqk,qhd->kd", grad_scores_low, query_low, preferred_element_type=jnp.float32
     )
-    key_total = grad_key_all[reach * local_rows :]
-    value_total = grad_value_all[reach * local_rows :]
+    grad_both_all = jnp.concatenate([grad_key_all, grad_value_all], axis=1)
+    both_total = grad_both_all[reach * local_rows :]
     for offset in range(1, reach + 1):
         row_start = (reach - offset) * local_rows
-        key_back, value_back = (
-            shifted(
-                grad_key_all[row_start : row_start + local_rows].astype(jnp.bfloat16),
-                "group",
-                -offset,
-            ).astype(jnp.float32),
-            shifted(
-                grad_value_all[row_start : row_start + local_rows].astype(jnp.bfloat16),
-                "group",
-                -offset,
-            ).astype(jnp.float32),
-        )
-        key_total = key_total + key_back
-        value_total = value_total + value_back
+        both_total = both_total + shifted(
+            grad_both_all[row_start : row_start + local_rows].astype(jnp.bfloat16),
+            "group",
+            -offset,
+        ).astype(jnp.float32)
+    key_total = both_total[:, :HD]
+    value_total = both_total[:, HD:]
     grad_query_proj, grad_gain_query = back_query(grad_query)
     grad_key_proj, grad_gain_key = back_key(key_total)
-    grad_query_low = grad_query_proj.astype(jnp.bfloat16)
-    grad_key_low = grad_key_proj.astype(jnp.bfloat16)
-    grad_value_low = value_total.astype(jnp.bfloat16)
-    grad_query_w = jnp.einsum(
-        "td,te->de", normed_low, grad_query_low, preferred_element_type=jnp.float32
-    )
-    grad_key_w = jnp.einsum(
-        "td,te->de", normed_low, grad_key_low, preferred_element_type=jnp.float32
-    )
-    grad_value_w = jnp.einsum(
-        "td,te->de", normed_low, grad_value_low, preferred_element_type=jnp.float32
-    )
-    grad_normed = jnp.einsum(
-        "te,de->td", grad_query_low, query_weight, preferred_element_type=jnp.float32
-    )
-    grad_normed = grad_normed + jnp.einsum(
-        "te,de->td", grad_key_low, key_weight, preferred_element_type=jnp.float32
-    )
-    grad_normed = grad_normed + jnp.einsum(
-        "te,de->td", grad_value_low, value_weight, preferred_element_type=jnp.float32
+    grad_qkv_low = jnp.concatenate([grad_query_proj, grad_key_proj, value_total], axis=1).astype(
+        jnp.bfloat16
+    )
+    grad_qkv_w = jnp.einsum(
+        "td,te->de", normed_low, grad_qkv_low, preferred_element_type=jnp.float32
+    )
+    grads_attn = scatter_weights(grad_qkv_w, grad_out_w, (HQ * HD, HD, HD), devices_all)
+    grad_normed = restored(
+        jnp.einsum("te,de->td", grad_qkv_low, qkv_weight, preferred_element_type=jnp.float32)
     )
     grad_input_norm, grad_gain_input = back_input(grad_normed)
     grad_inputs = grad_middle + grad_input_norm
-    flat_query = grad_query_w.reshape(-1, 128)
-    flat_key = grad_key_w.reshape(-1, 128)
-    flat_value = grad_value_w.reshape(-1, 128)
-    flat_out = grad_out_w.reshape(-1, 128)
-    flat_gate = grad_gate_w.reshape(-1, 128)
-    flat_up = grad_up_w.reshape(-1, 128)
-    flat_down = grad_down_w.reshape(-1, 128)
-    reduced = (
-        lax.psum_scatter(flat_query, ("dp", "group"), scatter_dimension=0, tiled=True),
-        lax.psum_scatter(flat_key, ("dp", "group"), scatter_dimension=0, tiled=True),
-        lax.psum_scatter(flat_value, ("dp", "group"), scatter_dimension=0, tiled=True),
-        lax.psum_scatter(flat_out, ("dp", "group"), scatter_dimension=0, tiled=True),
-        lax.psum_scatter(flat_gate, ("dp", "group"), scatter_dimension=0, tiled=True),
-        lax.psum_scatter(flat_up, ("dp", "group"), scatter_dimension=0, tiled=True),
-        lax.psum_scatter(flat_down, ("dp", "group"), scatter_dimension=0, tiled=True),
-    )
-    grads_local = jnp.concatenate(list(reduced), axis=0)
-    gain_grads = lax.psum(
+    grads_local = jnp.concatenate([grads_attn, grads_ffn], axis=0)
+    gain_grads = sum_gains(
         jnp.concatenate(
             [
                 grad_gain_input,
@@ -319,7 +452,7 @@
                 grad_gain_key,
             ]
         ),
-        ("dp", "group"),
+        devices_all,
     )
     moment_first, moment_second, master_new = adam_update(
         grads_local, first_moment, second_moment, master, learn_rate, weight_decay

time: 1310 us -> 286 us (0.22)
  waiting for transfers between devices: 1030 us -> 101 us
  blocking collectives: 120 us -> 0 us
  other arithmetic: 15.3 us -> 51.5 us
  starting transfers between devices: 23.5 us -> 53.5 us
  local copies, waits for them, and re-layouts: 61.9 us -> 36.8 us
  between operations: 15.8 us -> 2.46 us
    reduce_scatter x5 -> x0, waiting for transfers between devices: 588 us -> none  [the longest x1 141 us: shards(): lax.psum_scatter(flat_gate, ('dp', 'group'), scatter_dimension=0, tiled=T...]
    unnamed x14 -> x0, waiting for transfers between devices: 266 us -> none
    all_gather x5 -> x0, waiting for transfers between devices: 168 us -> none  [the longest x1 56.4 us: shards(): lax.all_gather(shard_parts[4], ('dp', 'group'), axis=0, tiled=True)]
    ppermute x0 -> x41, waiting for transfers between devices: none -> 96.7 us  [swap(): lax.ppermute(value, ALL_AXES, [(source, source ^ mask) for source in rang...]
    all_gather x2 -> x0, blocking collectives: 81.4 us -> none  [the longest x1 44.2 us: shards(): lax.all_gather(shard_parts[2], ('dp', 'group'), axis=0, tiled=True)]
    ppermute x0 -> x41, starting transfers between devices: none -> 40.8 us  [swap(): lax.ppermute(value, ALL_AXES, [(source, source ^ mask) for source in rang...]
    reshape x15 -> x12, local copies, waits for them, and re-layouts: 45.5 us -> 6.77 us  [the longest x5 4.17 us: scatter_weights(): piece.reshape(high_count, -1, 128)]
    psum x1 -> x0, blocking collectives: 38.5 us -> none  [shards(): lax.psum(jnp.concatenate([grad_gain_input, grad_gain_attn, grad_gain_ffin...]
  transfers between devices with their start and end apart: 24 -> 47, of which waited for: 15 -> 22; matrix products, arithmetic and copies ran while one was open for 6% -> 29% of each run, Pallas kernels for 0% -> 0%
where the time goes in v1:
time: 286 us; the launch traced here: 285 us
  waiting for transfers between devices  101 us (35%)
  starting transfers between devices  53.5 us (19%)
  other arithmetic  51.5 us (18%)
  matrix products  39 us (14%)
  local copies, waits for them, and re-layouts  36.8 us (13%)
    ppermute x41, waiting for transfers between devices, swap(): lax.ppermute(value, ALL_AXES, [(source, source ^ mask) for source in rang...  96.7 us
    ppermute x41, starting transfers between devices, swap(): lax.ppermute(value, ALL_AXES, [(source, source ^ mask) for source in rang...  40.8 us
    ppermute x6, starting transfers between devices, shifted(): lax.ppermute(value, axis, [(source, source + steps) for source in range(i...  12.7 us
    dot_general x6, matrix products, matmul(): return jnp.dot(left_side, right_side, preferred_element_type=jnp.float32)  7.75 us
    unnamed x183, local copies, waits for them, and re-layouts  7.69 us
    slice x6, local copies, waits for them, and re-layouts, scatter_relative(): total[half:].astype(jnp.bfloat16)  7.58 us
    add x4, other arithmetic, scatter_relative(): total[:half]  6.79 us
    select_n x6, other arithmetic, gather_placed(): jnp.where(low & mask == 0, jnp.concatenate([block, other], axis=axis), jn...  5.93 us
  transfers between devices with their start and end apart: 47, of which 22 were waited for; matrix products, arithmetic and copies ran while one was open for 29% of the time, Pallas kernels for 0%

profile of v1, /device:TPU:0, one launch (start us, length us, event | category | flops | bytes accessed | tf_op | source)
XLA Modules:
  0.0 284.6 jit_solution(13603035734313217446)
XLA Ops:
  1.8 5.1 %collective-permute-start.2 = (bf16[400,128]{1,0:T(8,128)(2,1)S(1)}, bf16[400,128]{1,0:T(8,128)(2,1)S(1)}, u32[]{:S(2)}, u32[]{:S(2)}) collective-permute-start(bf16[400,128]{1,0:T(8,128)(2,1)S(1)} %slice.234), channel_id=1, source_target_pairs={{0,24},{1,25},{2,26},{3,27},{4,28},{5,29},{6,30},{7,31},{8,16},{9,... | collective-permute-start | bytes 307208 | tf_op jit(solution)/shard_map/ppermute | solution.py:116
  7.6 3.8 %collective-permute-start.14 = (bf16[960,128]{1,0:T(8,128)(2,1)S(1)}, bf16[960,128]{1,0:T(8,128)(2,1)S(1)}, u32[]{:S(2)}, u32[]{:S(2)}) collective-permute-start(bf16[960,128]{1,0:T(8,128)(2,1)S(1)} %slice.245), channel_id=1, source_target_pairs={{0,24},{1,25},{2,26},{3,27},{4,28},{5,29},{6,30},{7,31},{8,16},{9,... | collective-permute-start | bytes 737288 | tf_op jit(solution)/shard_map/ppermute | solution.py:116
  28.6 8.0 %collective-permute-done.13 = bf16[960,128]{1,0:T(8,128)(2,1)S(1)} collective-permute-done((bf16[960,128]{1,0:T(8,128)(2,1)S(1)}, bf16[960,128]{1,0:T(8,128)(2,1)S(1)}, u32[]{:S(2)}, u32[]{:S(2)}) %collective-permute-start.13) | collective-permute-done | bytes 245792 | tf_op jit(solution)/shard_map/ppermute | solution.py:116
  45.4 2.8 collective-permute-done.18
  49.9 7.2 %collective-permute-done.4 = bf16[160,1536]{1,0:T(8,128)(2,1)} collective-permute-done((bf16[160,1536]{1,0:T(8,128)(2,1)}, bf16[160,1536]{1,0:T(8,128)(2,1)}, u32[]{:S(2)}, u32[]{:S(2)}) %collective-permute-start.4) | collective-permute-done | bytes 491552 | tf_op jit(solution)/shard_map/ppermute | solution.py:116
  58.3 7.3 %collective-permute-done.10 = bf16[4,1,2,1,32,640]{5,4,3,2,1,0:T(8,128)(2,1)S(1)} collective-permute-done((bf16[4,1,2,1,32,640]{5,4,3,2,1,0:T(8,128)(2,1)S(1)}, bf16[4,1,2,1,32,640]{5,4,3,2,1,0:T(8,128)(2,1)S(1)}, u32[]{:S(2)}, u32[]{:S(2)}) %collective-permute-start.10) | collective-permute-done | bytes 327712 | tf_op jit(solution)/shard_map/ppermute | solution.py:116
  68.7 8.6 %collective-permute-done.19 = bf16[4,1,2,1,64,640]{5,4,3,2,1,0:T(8,128)(2,1)S(1)} collective-permute-done((bf16[4,1,2,1,64,640]{5,4,3,2,1,0:T(8,128)(2,1)S(1)}, bf16[4,1,2,1,64,640]{5,4,3,2,1,0:T(8,128)(2,1)S(1)}, u32[]{:S(2)}, u32[]{:S(2)}) %collective-permute-start.19) | collective-permute-done | bytes 655392 | tf_op jit(solution)/shard_map/ppermute | solution.py:116
  82.7 3.1 %collective-permute-start.8 = (bf16[128,512]{1,0:T(8,128)(2,1)}, bf16[128,512]{1,0:T(8,128)(2,1)}, u32[]{:S(2)}, u32[]{:S(2)}) collective-permute-start(bf16[128,512]{1,0:T(8,128)(2,1)} %pad_maximum_fusion.24), channel_id=1, source_target_pairs={{0,1},{1,2},{2,3},{4,5},{5,6},{6,7},{8,9},{9,10},{10,11},{12,13},{... | collective-permute-start | bytes 393224 | tf_op jit(solution)/shard_map/ppermute | solution.py:28
  85.8 3.6 %collective-permute-start.7 = (bf16[128,512]{1,0:T(8,128)(2,1)}, bf16[128,512]{1,0:T(8,128)(2,1)}, u32[]{:S(2)}, u32[]{:S(2)}) collective-permute-start(bf16[128,512]{1,0:T(8,128)(2,1)} %pad_maximum_fusion.24), channel_id=1, source_target_pairs={{0,2},{1,3},{4,6},{5,7},{8,10},{9,11},{12,14},{13,15},{16,18},{17,... | collective-permute-start | bytes 393224 | tf_op jit(solution)/shard_map/ppermute | solution.py:28
  94.5 4.2 %collective-permute-done.16 = bf16[160,4096]{1,0:T(8,128)(2,1)} collective-permute-done((bf16[160,4096]{1,0:T(8,128)(2,1)}, bf16[160,4096]{1,0:T(8,128)(2,1)}, u32[]{:S(2)}, u32[]{:S(2)}) %collective-permute-start.16) | collective-permute-done | bytes 1310752 | tf_op jit(solution)/shard_map/ppermute | solution.py:116
  100.9 2.4 collective-permute-done.6
  106.6 3.1 %maximum_select_fusion = bf16[4,2,2,2,64,640]{5,4,3,2,1,0:T(8,128)(2,1)S(1)} fusion(bf16[4,2,2,1,64,640]{5,4,3,2,1,0:T(8,128)(2,1)} %collective-permute-done.20, bf16[4,2,2,1,64,640]{5,4,3,2,1,0:T(8,128)(2,1)} %maximum_select_fusion.2, pred[]{:T(512)S(6)} %eq.66), kind=kLoop, calls=%fused_computation.7 | loop fusion | flops 3932160 | bytes 5242881 | tf_op jit(solution)/shard_map/jit(_where)/select_n | solution.py:159
  116.2 3.4 %fusion.23 = f32[128,640]{1,0:T(8,128)S(1)} fusion(bf16[320,4096]{1,0:T(8,128)(2,1)S(1)} %collective-permute-done.17, bf16[160,4096]{1,0:T(8,128)(2,1)} %collective-permute-done.16, bf16[80,4096]{1,0:T(8,128)(2,1)S(1)} %copy-done.10, bf16[80,4096]{1,0:T(8,128)(2,1)S(1)} %copy-done.5, bf16[128,2048]{1,0:T(8,128)(2,1)S(1)} %get-tuple-element.30, ...), kind=kOutput, calls=%fused_computation.68 | convolution fusion | flops 694157312 | bytes 6619136 | tf_op jit(solution)/shard_map/tf,df->td/dot_general | solution.py:383
  127.0 2.4 convolution_bitcast_fusion
  129.5 3.0 %convolution_bitcast_fusion.3 = f32[128,4,256]{2,0,1:T(8,128)} fusion(f32[4,128,512]{1,2,0:T(8,128)} %convolution_bitcast_fusion, f32[4,128,512]{1,2,0:T(8,128)S(1)} %get-tuple-element.76, f32[4,128]{1,0:T(4,128)S(1)} %copy-done.56, bf16[512,512]{1,0:T(8,128)(2,1)S(1)} %copy-done.15), kind=kOutput, calls=%fused_computation.42 | convolution fusion | flops 136053760 | bytes 4984832 | tf_op jit(solution)/shard_map/hqk,kd->qhd/dot_general | solution.py:412
  134.7 4.3 %fusion.137 = f32[2048,640]{1,0:T(8,128)} fusion(bf16[128,2048]{1,0:T(8,128)(2,1)S(1)} %multiply_convert_fusion.1, bf16[128,640]{1,0:T(8,128)(2,1)} %copy-done.30), kind=kOutput, calls=%fused_computation.324 | convolution fusion | flops 335544320 | bytes 5931008 | tf_op jit(solution)/shard_map/tf,td->fd/dot_general | solution.py:370
  139.1 5.6 %fusion.31 = f32[640,4096]{1,0:T(8,128)} fusion(bf16[128,640]{1,0:T(8,128)(2,1)S(1)} %copy-done.41, bf16[128,2048]{1,0:T(8,128)(2,1)S(1)} %copy-done.39, bf16[128,2048]{1,0:T(8,128)(2,1)S(1)} %copy-done.37), kind=kOutput, calls=%fused_computation.80 | convolution fusion | flops 673185792 | bytes 11698176 | tf_op jit(solution)/shard_map/td,tf->df/dot_general | solution.py:378
  166.1 3.0 %dynamic-slice_convert_fusion = bf16[4,2,2,1,64,640]{5,4,3,2,1,0:T(8,128)(2,1)} fusion(f32[4,2,2,2,64,640]{5,4,3,2,1,0:T(8,128)} %bitcast.139, s32[]{:T(128)S(6)} %select_n.546), kind=kLoop, calls=%fused_computation.9 | loop fusion | bytes 2621444 | tf_op jit(solution)/shard_map/convert_element_type | solution.py:175
  169.5 4.4 %slice.348 = bf16[320,4096]{1,0:T(8,128)(2,1)} slice(f32[640,4096]{1,0:T(8,128)} %fusion.31), slice={[320:640], [0:4096]} | slice | bytes 5242880 | tf_op jit(solution)/shard_map/slice | solution.py:148
  182.2 2.9 %collective-permute-done.45 = f32[24,128]{1,0:T(8,128)S(1)} collective-permute-done((f32[24,128]{1,0:T(8,128)S(1)}, f32[24,128]{1,0:T(8,128)S(1)}, u32[]{:S(2)}, u32[]{:S(2)}) %collective-permute-start.45) | collective-permute-done | bytes 12320 | tf_op jit(solution)/shard_map/ppermute | solution.py:116
  186.1 3.0 %collective-permute-done.28 = bf16[4,1,2,1,32,640]{5,4,3,2,1,0:T(8,128)(2,1)S(1)} collective-permute-done((bf16[4,1,2,1,32,640]{5,4,3,2,1,0:T(8,128)(2,1)S(1)}, bf16[4,1,2,1,32,640]{5,4,3,2,1,0:T(8,128)(2,1)S(1)}, u32[]{:S(2)}, u32[]{:S(2)}) %collective-permute-start.28) | collective-permute-done | bytes 327712 | tf_op jit(solution)/shard_map/ppermute | solution.py:116
  196.9 2.5 convert_add_fusion
  199.4 5.8 %collective-permute-done.25 = bf16[160,1536]{1,0:T(8,128)(2,1)S(1)} collective-permute-done((bf16[160,1536]{1,0:T(8,128)(2,1)}, bf16[160,1536]{1,0:T(8,128)(2,1)S(1)}, u32[]{:S(2)}, u32[]{:S(2)}) %collective-permute-start.25) | collective-permute-done | bytes 491552 | tf_op jit(solution)/shard_map/ppermute | solution.py:116
  206.0 4.1 %slice_add_fusion = f32[320,4096]{1,0:T(8,128)S(1)} fusion(f32[640,4096]{1,0:T(8,128)} %fusion.31, bf16[320,4096]{1,0:T(8,128)(2,1)} %collective-permute-done.33), kind=kLoop, calls=%fused_computation.2 | loop fusion | flops 2621440 | bytes 13107200 | tf_op jit(solution)/shard_map/add | solution.py:148
  222.5 6.8 %collective-permute-done.37 = bf16[4,1,2,1,64,640]{5,4,3,2,1,0:T(8,128)(2,1)} collective-permute-done((bf16[4,1,2,1,64,640]{5,4,3,2,1,0:T(8,128)(2,1)S(1)}, bf16[4,1,2,1,64,640]{5,4,3,2,1,0:T(8,128)(2,1)}, u32[]{:S(2)}, u32[]{:S(2)}) %collective-permute-start.37) | collective-permute-done | bytes 655392 | tf_op jit(solution)/shard_map/ppermute | solution.py:116
  230.6 12.2 %collective-permute-done.34 = bf16[160,4096]{1,0:T(8,128)(2,1)} collective-permute-done((bf16[160,4096]{1,0:T(8,128)(2,1)}, bf16[160,4096]{1,0:T(8,128)(2,1)}, u32[]{:S(2)}, u32[]{:S(2)}) %collective-permute-start.34) | collective-permute-done | bytes 1310752 | tf_op jit(solution)/shard_map/ppermute | solution.py:116
  249.3 2.4 collective-permute-start.32
  251.7 2.8 collective-permute-done.38
  254.9 5.1 %collective-permute-done.35 = bf16[80,4096]{1,0:T(8,128)(2,1)} collective-permute-done((bf16[80,4096]{1,0:T(8,128)(2,1)}, bf16[80,4096]{1,0:T(8,128)(2,1)}, u32[]{:S(2)}, u32[]{:S(2)}) %collective-permute-start.35) | collective-permute-done | bytes 655392 | tf_op jit(solution)/shard_map/ppermute | solution.py:116
  267.1 3.1 %collective-permute-done.39 = bf16[960,128]{1,0:T(8,128)(2,1)S(1)} collective-permute-done((bf16[960,128]{1,0:T(8,128)(2,1)S(1)}, bf16[960,128]{1,0:T(8,128)(2,1)S(1)}, u32[]{:S(2)}, u32[]{:S(2)}) %collective-permute-start.39) | collective-permute-done | bytes 245792 | tf_op jit(solution)/shard_map/ppermute | solution.py:116
  270.2 4.3 %collective-permute-done.41 = bf16[960,128]{1,0:T(8,128)(2,1)S(1)} collective-permute-done((bf16[960,128]{1,0:T(8,128)(2,1)S(1)}, bf16[960,128]{1,0:T(8,128)(2,1)S(1)}, u32[]{:S(2)}, u32[]{:S(2)}) %collective-permute-start.41) | collective-permute-done | bytes 245792 | tf_op jit(solution)/shard_map/ppermute | solution.py:116
  274.5 8.3 %collective-permute-done.40 = bf16[960,128]{1,0:T(8,128)(2,1)S(1)} collective-permute-done((bf16[960,128]{1,0:T(8,128)(2,1)S(1)}, bf16[960,128]{1,0:T(8,128)(2,1)S(1)}, u32[]{:S(2)}, u32[]{:S(2)}) %collective-permute-start.40) | collective-permute-done | bytes 245792 | tf_op jit(solution)/shard_map/ppermute | solution.py:116
  (413 shorter events, 133.6 us)
Async XLA Ops:
  1.8 20.9 %collective-permute-start.2 = (bf16[400,128]{1,0:T(8,128)(2,1)S(1)}, bf16[400,128]{1,0:T(8,128)(2,1)S(1)}, u32[]{:S(2)}, u32[]{:S(2)}) collective-permute-start(bf16[400,128]{1,0:T(8,128)(2,1)S(1)} %slice.234), channel_id=1, source_target_pairs={{0,24},{1,25},{2,26},{3,27},{4,28},{5,29},{6,30},{7,31},{8,16},{9,... | collective-permute-start | bytes 307208 | tf_op jit(solution)/shard_map/ppermute | solution.py:116
  6.9 16.5 %collective-permute-start = (bf16[400,128]{1,0:T(8,128)(2,1)S(1)}, bf16[400,128]{1,0:T(8,128)(2,1)S(1)}, u32[]{:S(2)}, u32[]{:S(2)}) collective-permute-start(bf16[400,128]{1,0:T(8,128)(2,1)S(1)} %slice.234), channel_id=1, source_target_pairs={{0,8},{1,9},{2,10},{3,11},{4,12},{5,13},{6,14},{7,15},{8,0},{9,1},... | collective-permute-start | bytes 307208 | tf_op jit(solution)/shard_map/ppermute | solution.py:116
  6.9 16.5 %collective-permute-start.1 = (bf16[400,128]{1,0:T(8,128)(2,1)S(1)}, bf16[400,128]{1,0:T(8,128)(2,1)S(1)}, u32[]{:S(2)}, u32[]{:S(2)}) collective-permute-start(bf16[400,128]{1,0:T(8,128)(2,1)S(1)} %slice.234), channel_id=1, source_target_pairs={{0,16},{1,17},{2,18},{3,19},{4,20},{5,21},{6,22},{7,23},{8,24},{9,... | collective-permute-start | bytes 307208 | tf_op jit(solution)/shard_map/ppermute | solution.py:116
  7.6 21.1 %collective-permute-start.14 = (bf16[960,128]{1,0:T(8,128)(2,1)S(1)}, bf16[960,128]{1,0:T(8,128)(2,1)S(1)}, u32[]{:S(2)}, u32[]{:S(2)}) collective-permute-start(bf16[960,128]{1,0:T(8,128)(2,1)S(1)} %slice.245), channel_id=1, source_target_pairs={{0,24},{1,25},{2,26},{3,27},{4,28},{5,29},{6,30},{7,31},{8,16},{9,... | collective-permute-start | bytes 737288 | tf_op jit(solution)/shard_map/ppermute | solution.py:116
  11.4 17.3 %collective-permute-start.12 = (bf16[960,128]{1,0:T(8,128)(2,1)S(1)}, bf16[960,128]{1,0:T(8,128)(2,1)S(1)}, u32[]{:S(2)}, u32[]{:S(2)}) collective-permute-start(bf16[960,128]{1,0:T(8,128)(2,1)S(1)} %slice.245), channel_id=1, source_target_pairs={{0,8},{1,9},{2,10},{3,11},{4,12},{5,13},{6,14},{7,15},{8,0},{9,1},... | collective-permute-start | bytes 737288 | tf_op jit(solution)/shard_map/ppermute | solution.py:116
  22.7 13.9 %collective-permute-start.13 = (bf16[960,128]{1,0:T(8,128)(2,1)S(1)}, bf16[960,128]{1,0:T(8,128)(2,1)S(1)}, u32[]{:S(2)}, u32[]{:S(2)}) collective-permute-start(bf16[960,128]{1,0:T(8,128)(2,1)S(1)} %slice.245), channel_id=1, source_target_pairs={{0,16},{1,17},{2,18},{3,19},{4,20},{5,21},{6,22},{7,23},{8,24},{9,... | collective-permute-start | bytes 737288 | tf_op jit(solution)/shard_map/ppermute | solution.py:116
  25.3 17.0 %collective-permute-start.9 = (bf16[4,1,1,1,32,640]{5,4,3,2,1,0:T(8,128)(2,1)}, bf16[4,1,1,1,32,640]{5,4,3,2,1,0:T(8,128)(2,1)}, u32[]{:S(2)}, u32[]{:S(2)}) collective-permute-start(bf16[4,1,1,1,32,640]{5,4,3,2,1,0:T(8,128)(2,1)} %reshape_reshape.6), channel_id=1, source_target_pairs={{0,2},{1,3},{2,0},{3,1},{4,6},{5,7},{6,4},{7,5},{8,10},{9,11},{10,... | collective-permute-start | bytes 491528 | tf_op jit(solution)/shard_map/ppermute | solution.py:116
  27.1 12.0 %collective-permute-start.3 = (bf16[80,1536]{1,0:T(8,128)(2,1)S(1)}, bf16[80,1536]{1,0:T(8,128)(2,1)S(1)}, u32[]{:S(2)}, u32[]{:S(2)}) collective-permute-start(bf16[80,1536]{1,0:T(8,128)(2,1)S(1)} %constant_dynamic-update-slice_fusion), channel_id=1, source_target_pairs={{0,4},{1,5},{2,6},{3,7},{4,0},{5,1},{6,2},{7,3},{8,12},{9,13},{10,... | collective-permute-start | bytes 737288 | tf_op jit(solution)/shard_map/ppermute | solution.py:116
  40.0 17.1 %collective-permute-start.4 = (bf16[160,1536]{1,0:T(8,128)(2,1)}, bf16[160,1536]{1,0:T(8,128)(2,1)}, u32[]{:S(2)}, u32[]{:S(2)}) collective-permute-start(bf16[160,1536]{1,0:T(8,128)(2,1)} %pad_maximum_fusion.13), channel_id=1, source_target_pairs={{0,2},{1,3},{2,0},{3,1},{4,6},{5,7},{6,4},{7,5},{8,10},{9,11},{10,... | collective-permute-start | bytes 1474568 | tf_op jit(solution)/shard_map/ppermute | solution.py:116
  40.8 25.1 %collective-permute-start.15 = (bf16[80,4096]{1,0:T(8,128)(2,1)S(1)}, bf16[80,4096]{1,0:T(8,128)(2,1)S(1)}, u32[]{:S(2)}, u32[]{:S(2)}) collective-permute-start(bf16[80,4096]{1,0:T(8,128)(2,1)S(1)} %constant_dynamic-update-slice_fusion.3), channel_id=1, source_target_pairs={{0,4},{1,5},{2,6},{3,7},{4,0},{5,1},{6,2},{7,3},{8,12},{9,13},{10,... | collective-permute-start | bytes 1966088 | tf_op jit(solution)/shard_map/ppermute | solution.py:116
  43.6 22.0 %collective-permute-start.10 = (bf16[4,1,2,1,32,640]{5,4,3,2,1,0:T(8,128)(2,1)S(1)}, bf16[4,1,2,1,32,640]{5,4,3,2,1,0:T(8,128)(2,1)S(1)}, u32[]{:S(2)}, u32[]{:S(2)}) collective-permute-start(bf16[4,1,2,1,32,640]{5,4,3,2,1,0:T(8,128)(2,1)S(1)} %maximum_select_fusion.7), channel_id=1, source_target_pairs={{0,4},{1,5},{2,6},{3,7},{4,0},{5,1},{6,2},{7,3},{8,12},{9,13},{10,... | collective-permute-start | bytes 983048 | tf_op jit(solution)/shard_map/ppermute | solution.py:116
  48.3 29.0 %collective-permute-start.19 = (bf16[4,1,2,1,64,640]{5,4,3,2,1,0:T(8,128)(2,1)S(1)}, bf16[4,1,2,1,64,640]{5,4,3,2,1,0:T(8,128)(2,1)S(1)}, u32[]{:S(2)}, u32[]{:S(2)}) collective-permute-start(bf16[4,1,2,1,64,640]{5,4,3,2,1,0:T(8,128)(2,1)S(1)} %maximum_select_fusion.5), channel_id=1, source_target_pairs={{0,4},{1,5},{2,6},{3,7},{4,0},{5,1},{6,2},{7,3},{8,12},{9,13},{10,... | collective-permute-start | bytes 1966088 | tf_op jit(solution)/shard_map/ppermute | solution.py:116
  58.2 20.6 %collective-permute-start.5 = (bf16[320,1536]{1,0:T(8,128)(2,1)S(1)}, bf16[320,1536]{1,0:T(8,128)(2,1)S(1)}, u32[]{:S(2)}, u32[]{:S(2)}) collective-permute-start(bf16[320,1536]{1,0:T(8,128)(2,1)S(1)} %pad_maximum_fusion.6), channel_id=1, source_target_pairs={{0,1},{1,0},{2,3},{3,2},{4,5},{5,4},{6,7},{7,6},{8,9},{9,8},{10,11... | collective-permute-start | bytes 2949128 | tf_op jit(solution)/shard_map/ppermute | solution.py:116
  65.7 12.9 %collective-permute-start.11 = (bf16[4,2,2,1,32,640]{5,4,3,2,1,0:T(8,128)(2,1)S(1)}, bf16[4,2,2,1,32,640]{5,4,3,2,1,0:T(8,128)(2,1)S(1)}, u32[]{:S(2)}, u32[]{:S(2)}) collective-permute-start(bf16[4,2,2,1,32,640]{5,4,3,2,1,0:T(8,128)(2,1)S(1)} %maximum_select_fusion.3), channel_id=1, source_target_pairs={{0,1},{1,0},{2,3},{3,2},{4,5},{5,4},{6,7},{7,6},{8,9},{9,8},{10,11... | collective-permute-start | bytes 1966088 | tf_op jit(solution)/shard_map/ppermute | solution.py:116
  67.2 31.5 %collective-permute-start.16 = (bf16[160,4096]{1,0:T(8,128)(2,1)}, bf16[160,4096]{1,0:T(8,128)(2,1)}, u32[]{:S(2)}, u32[]{:S(2)}) collective-permute-start(bf16[160,4096]{1,0:T(8,128)(2,1)} %pad_maximum_fusion.3), channel_id=1, source_target_pairs={{0,2},{1,3},{2,0},{3,1},{4,6},{5,7},{6,4},{7,5},{8,10},{9,11},{10,... | collective-permute-start | bytes 3932168 | tf_op jit(solution)/shard_map/ppermute | solution.py:116
  78.6 28.0 %collective-permute-start.20 = (bf16[4,2,2,1,64,640]{5,4,3,2,1,0:T(8,128)(2,1)}, bf16[4,2,2,1,64,640]{5,4,3,2,1,0:T(8,128)(2,1)}, u32[]{:S(2)}, u32[]{:S(2)}) collective-permute-start(bf16[4,2,2,1,64,640]{5,4,3,2,1,0:T(8,128)(2,1)} %maximum_select_fusion.2), channel_id=1, source_target_pairs={{0,1},{1,0},{2,3},{3,2},{4,5},{5,4},{6,7},{7,6},{8,9},{9,8},{10,11... | collective-permute-start | bytes 3932168 | tf_op jit(solution)/shard_map/ppermute | solution.py:116
  82.7 17.7 %collective-permute-start.8 = (bf16[128,512]{1,0:T(8,128)(2,1)}, bf16[128,512]{1,0:T(8,128)(2,1)}, u32[]{:S(2)}, u32[]{:S(2)}) collective-permute-start(bf16[128,512]{1,0:T(8,128)(2,1)} %pad_maximum_fusion.24), channel_id=1, source_target_pairs={{0,1},{1,2},{2,3},{4,5},{5,6},{6,7},{8,9},{9,10},{10,11},{12,13},{... | collective-permute-start | bytes 393224 | tf_op jit(solution)/shard_map/ppermute | solution.py:28
  85.8 15.1 %collective-permute-start.7 = (bf16[128,512]{1,0:T(8,128)(2,1)}, bf16[128,512]{1,0:T(8,128)(2,1)}, u32[]{:S(2)}, u32[]{:S(2)}) collective-permute-start(bf16[128,512]{1,0:T(8,128)(2,1)} %pad_maximum_fusion.24), channel_id=1, source_target_pairs={{0,2},{1,3},{4,6},{5,7},{8,10},{9,11},{12,14},{13,15},{16,18},{17,... | collective-permute-start | bytes 393224 | tf_op jit(solution)/shard_map/ppermute | solution.py:28
  89.3 14.0 %collective-permute-start.6 = (bf16[128,512]{1,0:T(8,128)(2,1)}, bf16[128,512]{1,0:T(8,128)(2,1)}, u32[]{:S(2)}, u32[]{:S(2)}) collective-permute-start(bf16[128,512]{1,0:T(8,128)(2,1)} %pad_maximum_fusion.24), channel_id=1, source_target_pairs={{0,3},{4,7},{8,11},{12,15},{16,19},{20,23},{24,27},{28,31}} | collective-permute-start | bytes 393224 | tf_op jit(solution)/shard_map/ppermute | solution.py:28
  153.9 25.3 %collective-permute-start.27 = (bf16[4,2,2,1,32,640]{5,4,3,2,1,0:T(8,128)(2,1)}, bf16[4,2,2,1,32,640]{5,4,3,2,1,0:T(8,128)(2,1)}, u32[]{:S(2)}, u32[]{:S(2)}) collective-permute-start(bf16[4,2,2,1,32,640]{5,4,3,2,1,0:T(8,128)(2,1)} %dynamic-slice_convert_fusion.2), channel_id=1, source_target_pairs={{0,1},{1,0},{2,3},{3,2},{4,5},{5,4},{6,7},{7,6},{8,9},{9,8},{10,11... | collective-permute-start | bytes 1966088 | tf_op jit(solution)/shard_map/ppermute | solution.py:116
  169.1 27.8 %collective-permute-start.36 = (bf16[4,2,2,1,64,640]{5,4,3,2,1,0:T(8,128)(2,1)}, bf16[4,2,2,1,64,640]{5,4,3,2,1,0:T(8,128)(2,1)}, u32[]{:S(2)}, u32[]{:S(2)}) collective-permute-start(bf16[4,2,2,1,64,640]{5,4,3,2,1,0:T(8,128)(2,1)} %dynamic-slice_convert_fusion), channel_id=1, source_target_pairs={{0,1},{1,0},{2,3},{3,2},{4,5},{5,4},{6,7},{7,6},{8,9},{9,8},{10,11... | collective-permute-start | bytes 3932168 | tf_op jit(solution)/shard_map/ppermute | solution.py:116
  173.9 32.2 %collective-permute-start.33 = (bf16[320,4096]{1,0:T(8,128)(2,1)}, bf16[320,4096]{1,0:T(8,128)(2,1)}, u32[]{:S(2)}, u32[]{:S(2)}) collective-permute-start(bf16[320,4096]{1,0:T(8,128)(2,1)} %slice.348), channel_id=1, source_target_pairs={{0,1},{1,0},{2,3},{3,2},{4,5},{5,4},{6,7},{7,6},{8,9},{9,8},{10,11... | collective-permute-start | bytes 7864328 | tf_op jit(solution)/shard_map/ppermute | solution.py:116
  175.8 14.5 %collective-permute-start.24 = (bf16[320,1536]{1,0:T(8,128)(2,1)S(1)}, bf16[320,1536]{1,0:T(8,128)(2,1)S(1)}, u32[]{:S(2)}, u32[]{:S(2)}) collective-permute-start(bf16[320,1536]{1,0:T(8,128)(2,1)S(1)} %slice.350), channel_id=1, source_target_pairs={{0,1},{1,0},{2,3},{3,2},{4,5},{5,4},{6,7},{7,6},{8,9},{9,8},{10,11... | collective-permute-start | bytes 2949128 | tf_op jit(solution)/shard_map/ppermute | solution.py:116
  185.1 77.1 %collective-permute-start.46 = (f32[24,128]{1,0:T(8,128)S(1)}, f32[24,128]{1,0:T(8,128)S(1)}, u32[]{:S(2)}, u32[]{:S(2)}) collective-permute-start(f32[24,128]{1,0:T(8,128)S(1)} %add.454), channel_id=1, source_target_pairs={{0,16},{1,17},{2,18},{3,19},{4,20},{5,21},{6,22},{7,23},{8,24},{9,... | collective-permute-start | bytes 36872 | tf_op jit(solution)/shard_map/ppermute | solution.py:116
  192.7 12.5 %collective-permute-start.25 = (bf16[160,1536]{1,0:T(8,128)(2,1)}, bf16[160,1536]{1,0:T(8,128)(2,1)S(1)}, u32[]{:S(2)}, u32[]{:S(2)}) collective-permute-start(bf16[160,1536]{1,0:T(8,128)(2,1)} %slice.352), channel_id=1, source_target_pairs={{0,2},{1,3},{2,0},{3,1},{4,6},{5,7},{6,4},{7,5},{8,10},{9,11},{10,... | collective-permute-start | bytes 1474568 | tf_op jit(solution)/shard_map/ppermute | solution.py:116
  213.8 28.9 %collective-permute-start.34 = (bf16[160,4096]{1,0:T(8,128)(2,1)}, bf16[160,4096]{1,0:T(8,128)(2,1)}, u32[]{:S(2)}, u32[]{:S(2)}) collective-permute-start(bf16[160,4096]{1,0:T(8,128)(2,1)} %slice.349), channel_id=1, source_target_pairs={{0,2},{1,3},{2,0},{3,1},{4,6},{5,7},{6,4},{7,5},{8,10},{9,11},{10,... | collective-permute-start | bytes 3932168 | tf_op jit(solution)/shard_map/ppermute | solution.py:116
  214.9 14.4 %collective-permute-start.37 = (bf16[4,1,2,1,64,640]{5,4,3,2,1,0:T(8,128)(2,1)S(1)}, bf16[4,1,2,1,64,640]{5,4,3,2,1,0:T(8,128)(2,1)}, u32[]{:S(2)}, u32[]{:S(2)}) collective-permute-start(bf16[4,1,2,1,64,640]{5,4,3,2,1,0:T(8,128)(2,1)S(1)} %dynamic-slice_convert_fusion.1), channel_id=1, source_target_pairs={{0,4},{1,5},{2,6},{3,7},{4,0},{5,1},{6,2},{7,3},{8,12},{9,13},{10,... | collective-permute-start | bytes 1966088 | tf_op jit(solution)/shard_map/ppermute | solution.py:116
  246.0 14.0 %collective-permute-start.35 = (bf16[80,4096]{1,0:T(8,128)(2,1)}, bf16[80,4096]{1,0:T(8,128)(2,1)}, u32[]{:S(2)}, u32[]{:S(2)}) collective-permute-start(bf16[80,4096]{1,0:T(8,128)(2,1)} %slice.351), channel_id=1, source_target_pairs={{0,4},{1,5},{2,6},{3,7},{4,0},{5,1},{6,2},{7,3},{8,12},{9,13},{10,... | collective-permute-start | bytes 1966088 | tf_op jit(solution)/shard_map/ppermute | solution.py:116
  249.3 15.1 %collective-permute-start.30 = (bf16[400,128]{1,0:T(8,128)(2,1)}, bf16[400,128]{1,0:T(8,128)(2,1)S(1)}, u32[]{:S(2)}, u32[]{:S(2)}) collective-permute-start(bf16[400,128]{1,0:T(8,128)(2,1)} %get-tuple-element.54), channel_id=1, source_target_pairs={{0,8},{1,9},{2,10},{3,11},{4,12},{5,13},{6,14},{7,15},{8,0},{9,1},... | collective-permute-start | bytes 307208 | tf_op jit(solution)/shard_map/ppermute | solution.py:116
  249.3 16.7 %collective-permute-start.32 = (bf16[400,128]{1,0:T(8,128)(2,1)}, bf16[400,128]{1,0:T(8,128)(2,1)}, u32[]{:S(2)}, u32[]{:S(2)}) collective-permute-start(bf16[400,128]{1,0:T(8,128)(2,1)} %get-tuple-element.55), channel_id=1, source_target_pairs={{0,24},{1,25},{2,26},{3,27},{4,28},{5,29},{6,30},{7,31},{8,16},{9,... | collective-permute-start | bytes 307208 | tf_op jit(solution)/shard_map/ppermute | solution.py:116
  262.2 12.3 %collective-permute-start.41 = (bf16[960,128]{1,0:T(8,128)(2,1)S(1)}, bf16[960,128]{1,0:T(8,128)(2,1)S(1)}, u32[]{:S(2)}, u32[]{:S(2)}) collective-permute-start(bf16[960,128]{1,0:T(8,128)(2,1)S(1)} %get-tuple-element.36), channel_id=1, source_target_pairs={{0,24},{1,25},{2,26},{3,27},{4,28},{5,29},{6,30},{7,31},{8,16},{9,... | collective-permute-start | bytes 737288 | tf_op jit(solution)/shard_map/ppermute | solution.py:116
  264.4 18.4 %collective-permute-start.40 = (bf16[960,128]{1,0:T(8,128)(2,1)S(1)}, bf16[960,128]{1,0:T(8,128)(2,1)S(1)}, u32[]{:S(2)}, u32[]{:S(2)}) collective-permute-start(bf16[960,128]{1,0:T(8,128)(2,1)S(1)} %get-tuple-element.37), channel_id=1, source_target_pairs={{0,16},{1,17},{2,18},{3,19},{4,20},{5,21},{6,22},{7,23},{8,24},{9,... | collective-permute-start | bytes 737288 | tf_op jit(solution)/shard_map/ppermute | solution.py:116
  (100 other events, 778.3 us)

commit v2 on v1

--- a/solution.py
+++ b/solution.py
@@ -1,6 +1,11 @@
+import functools
+import math
+
 import jax
 import jax.numpy as jnp
 from jax import lax
+from jax.experimental import pallas as pl
+from jax.experimental.pallas import tpu as pltpu
 from jax.sharding import PartitionSpec as P
 
 D = 640
@@ -105,6 +110,9 @@
 
 
 LOW_COUNT = 8
+LANES = 128
+LOW_MASKS = (0, 4, 2, 6, 1, 5, 3, 7)
+VMEM_BYTES = 56 * 1024 * 1024
 
 
 def aligned(device_count):
@@ -116,69 +124,179 @@
     return lax.ppermute(value, ALL_AXES, [(source, source ^ mask) for source in range(count)])
 
 
-def gather_high(rows):
-    high_count = lax.axis_size(ALL_AXES) // LOW_COUNT
-    high = lax.axis_index(ALL_AXES) // LOW_COUNT
+def local_call(kernel, outs, operands, scratch=(), flops=0):
+    specs = [pl.BlockSpec(memory_space=pltpu.SMEM)]
+    specs = specs + [pl.BlockSpec(memory_space=pltpu.VMEM)] * len(operands)
+    moved = sum(math.prod(value.shape) * value.dtype.itemsize for value in (*operands, *outs))
+    return pl.pallas_call(
+        kernel,
+        out_shape=outs,
+        in_specs=specs,
+        out_specs=tuple(pl.BlockSpec(memory_space=pltpu.VMEM) for _ in outs),
+        scratch_shapes=scratch,
+        compiler_params=pltpu.CompilerParams(vmem_limit_bytes=VMEM_BYTES),
+        cost_estimate=pl.CostEstimate(flops=flops, bytes_accessed=moved, transcendentals=0),
+    )(lax.axis_index(ALL_AXES).astype(jnp.int32).reshape(1), *operands)
+
+
+class Piece:
+    def __init__(self, rows, columns, device_count):
+        self.rows = rows
+        self.columns = columns
+        self.wide = rows == D
+        self.blocks = columns // LANES
+        self.own_rows = rows // device_count
+        self.flat_rows = self.own_rows * self.blocks
+        self.high_count = device_count // LOW_COUNT
+        self.block_rows = self.own_rows * self.high_count
+        self.size = self.block_rows * self.blocks
+
+
+def pack_kernel(pieces, index_ref, *refs):
+    high_count = pieces[0].high_count
+    parts, out_ref, flat, packed = refs[:high_count], refs[-3], refs[-2], refs[-1]
+    high = index_ref[0] // LOW_COUNT
+    for step, part in enumerate(parts):
+        flat[high ^ step] = part[...].astype(jnp.float32)
+    start, target = 0, 0
+    for piece in pieces:
+        for block in range(piece.blocks):
+            for place in range(high_count):
+                packed[pl.ds(target, piece.own_rows), :] = flat[
+                    place, pl.ds(start + block, piece.own_rows, stride=piece.blocks), :
+                ]
+                target = target + piece.own_rows
+        start = start + piece.flat_rows
+    out_ref[...] = packed[...].astype(jnp.bfloat16)
+
+
+def unpack_kernel(pieces, index_ref, *refs):
+    high_count = pieces[0].high_count
+    terms, outs, flat, packed = refs[:3], refs[3:-2], refs[-2], refs[-1]
+    high = index_ref[0] // LOW_COUNT
+    packed[...] = sum(term[...].astype(jnp.float32) for term in terms)
+    start, source = 0, 0
+    for piece in pieces:
+        for block in range(piece.blocks):
+            for place in range(high_count):
+                flat[place, pl.ds(start + block, piece.own_rows, stride=piece.blocks), :] = packed[
+                    pl.ds(source, piece.own_rows), :
+                ]
+                source = source + piece.own_rows
+        start = start + piece.flat_rows
+    for step, out_ref in enumerate(outs):
+        out_ref[...] = flat[high ^ step].astype(out_ref.dtype)
+
+
+def assemble_kernel(pieces, index_ref, near_ref, far_ref, *out_refs):
+    low = index_ref[0] % LOW_COUNT
+    size = sum(piece.size for piece in pieces)
+    for order, mask in enumerate(LOW_MASKS):
+        source = near_ref if order < 4 else far_ref
+        start = (order % 4) * size
+        for piece, out_ref in zip(pieces, out_refs):
+            for block in range(piece.blocks):
+                columns = slice(block * LANES, (block + 1) * LANES)
+                if piece.wide:
+                    out_ref[order * piece.block_rows : (order + 1) * piece.block_rows, columns] = (
+                        source[start : start + piece.block_rows, :]
+                    )
+                else:
+                    for place in range(piece.high_count):
+                        row = (place * LOW_COUNT + (low ^ mask)) * piece.own_rows
+                        first = start + place * piece.own_rows
+                        out_ref[
+                            pl.ds(pl.multiple_of(row, piece.own_rows), piece.own_rows), columns
+                        ] = source[first : first + piece.own_rows, :]
+                start = start + piece.block_rows
+
+
+def split_kernel(pieces, index_ref, *refs):
+    in_refs, near_ref, far_ref = refs[:-2], refs[-2], refs[-1]
+    low = index_ref[0] % LOW_COUNT
+    size = sum(piece.size for piece in pieces)
+    for order, mask in enumerate(LOW_MASKS):
+        target = near_ref if order < 4 else far_ref
+        start = (order % 4) * size
+        for piece, in_ref in zip(pieces, in_refs):
+            for block in range(piece.blocks):
+                columns = slice(block * LANES, (block + 1) * LANES)
+                if piece.wide:
+                    target[start : start + piece.block_rows, :] = in_ref[
+                        order * piece.block_rows : (order + 1) * piece.block_rows, columns
+                    ].astype(jnp.bfloat16)
+                else:
+                    for place in range(piece.high_count):
+                        row = (place * LOW_COUNT + (low ^ mask)) * piece.own_rows
+                        first = start + place * piece.own_rows
+                        target[first : first + piece.own_rows, :] = in_ref[
+                            pl.ds(pl.multiple_of(row, piece.own_rows), piece.own_rows), columns
+                        ].astype(jnp.bfloat16)
+                start = start + piece.block_rows
+
+
+def array(shape, kind):
+    return jax.ShapeDtypeStruct(shape, kind)
+
+
+def gather_blocks(pieces, rows):
+    high_count = pieces[0].high_count
+    size = sum(piece.size for piece in pieces)
     parts = [rows] + [swap(rows, step * LOW_COUNT) for step in range(1, high_count)]
-    return jnp.stack([lax.select_n(high ^ place, *parts) for place in range(high_count)])
-
-
-def scatter_high(blocks):
-    high_count = blocks.shape[0]
-    high = lax.axis_index(ALL_AXES) // LOW_COUNT
-    total = lax.dynamic_index_in_dim(blocks, high, 0, keepdims=False).astype(jnp.float32)
-    sends = [
-        lax.dynamic_index_in_dim(blocks, high ^ step, 0, keepdims=False)
-        for step in range(1, high_count)
-    ]
-    for step, send in enumerate(sends, start=1):
-        total = total + swap(send, step * LOW_COUNT).astype(jnp.float32)
-    return total
-
-
-def gather_relative(block, masks):
-    for mask in masks:
-        block = jnp.concatenate([block, swap(block, mask)], axis=0)
-    return block
-
-
-def scatter_relative(total, masks):
-    for mask in masks:
-        half = total.shape[0] // 2
-        total = total[:half] + swap(total[half:].astype(jnp.bfloat16), mask).astype(jnp.float32)
-    return total
-
-
-def gather_placed(block, masks):
-    low = lax.axis_index(ALL_AXES) % LOW_COUNT
-    high_count, rows, columns = block.shape
-    block = block.reshape(high_count, 1, 1, 1, rows, columns)
-    for mask in masks:
-        axis = {4: 1, 2: 2, 1: 3}[mask]
-        other = swap(block, mask)
-        block = jnp.where(
-            (low & mask) == 0,
-            jnp.concatenate([block, other], axis=axis),
-            jnp.concatenate([other, block], axis=axis),
-        )
-    return block.reshape(high_count * LOW_COUNT * rows, columns)
-
-
-def scatter_placed(total, high_count, masks):
-    low = lax.axis_index(ALL_AXES) % LOW_COUNT
-    columns = total.shape[1]
-    rows = total.shape[0] // (high_count * LOW_COUNT)
-    total = total.reshape(high_count, 2, 2, 2, rows, columns)
-    for mask in masks:
-        axis = {4: 1, 2: 2, 1: 3}[mask]
-        bit = jnp.where((low & mask) == 0, 0, 1)
-        send = lax.dynamic_index_in_dim(total, 1 - bit, axis).astype(jnp.bfloat16)
-        total = lax.dynamic_index_in_dim(total, bit, axis) + swap(send, mask).astype(jnp.float32)
-    return total.reshape(high_count, rows, columns)
-
-
-RELATIVE_MASKS = (4, 2, 1)
-PLACED_MASKS = (2, 4, 1)
+    (own,) = local_call(
+        functools.partial(pack_kernel, pieces),
+        (array((size, LANES), jnp.bfloat16),),
+        parts,
+        (
+            pltpu.VMEM((high_count, rows.shape[0], LANES), jnp.float32),
+            pltpu.VMEM((size, LANES), jnp.float32),
+        ),
+    )
+    beside, across = swap(own, 4), swap(own, 2)
+    half = size // 2
+    near = jnp.concatenate([own, beside, across, swap(across[:half], 4), swap(beside[half:], 2)])
+    return near, swap(near, 1)
+
+
+def assemble(pieces, near, far):
+    return local_call(
+        functools.partial(assemble_kernel, pieces),
+        tuple(array((piece.rows, piece.columns), jnp.bfloat16) for piece in pieces),
+        (near, far),
+    )
+
+
+def scatter_blocks(pieces, gradients):
+    high_count = pieces[0].high_count
+    size = sum(piece.size for piece in pieces)
+    flat_rows = sum(piece.flat_rows for piece in pieces)
+    near, far = local_call(
+        functools.partial(split_kernel, pieces),
+        (array((4 * size, LANES), jnp.bfloat16),) * 2,
+        gradients,
+    )
+    total = near.astype(jnp.float32) + swap(far, 1).astype(jnp.float32)
+    half = size // 2
+    diagonal = total[3 * size :].astype(jnp.bfloat16)
+    across = total[2 * size : 3 * size]
+    beside = total[size : 2 * size]
+    over_x = swap(diagonal[:half], 4).astype(jnp.float32)
+    over_y = swap(diagonal[half:], 2).astype(jnp.float32)
+    across = jnp.concatenate([across[:half] + over_x, across[half:]]).astype(jnp.bfloat16)
+    beside = jnp.concatenate([beside[:half], beside[half:] + over_y]).astype(jnp.bfloat16)
+    outs = local_call(
+        functools.partial(unpack_kernel, pieces),
+        (array((flat_rows, LANES), jnp.float32),)
+        + (array((flat_rows, LANES), jnp.bfloat16),) * (high_count - 1),
+        (total[:size], swap(beside, 4), swap(across, 2)),
+        (
+            pltpu.VMEM((high_count, flat_rows, LANES), jnp.float32),
+            pltpu.VMEM((size, LANES), jnp.float32),
+        ),
+    )
+    return outs[0] + sum(
+        swap(send, step * LOW_COUNT).astype(jnp.float32) for step, send in enumerate(outs) if step
+    )
 
 
 def width_order(device_count):
@@ -187,8 +305,7 @@
     high_count = device_count // LOW_COUNT
     column = jnp.arange(D, dtype=jnp.int32)
     place = column // (rows * high_count)
-    mask = (place & 1) * RELATIVE_MASKS[0]
-    mask = mask + ((place >> 1) & 1) * RELATIVE_MASKS[1] + (place >> 2) * RELATIVE_MASKS[2]
+    mask = (place & 1) * 4 + ((place >> 1) & 1) * 2 + (place >> 2)
     high = (column // rows) % high_count
     picked = (high * LOW_COUNT + (low ^ mask)) * rows + column % rows
     return (jnp.arange(D, dtype=jnp.int32)[:, None] == picked[None, :]).astype(jnp.float32)
@@ -203,59 +320,31 @@
             lax.all_gather(part, ALL_AXES, axis=0, tiled=True).reshape(shape_pair)
             for part, shape_pair in zip(shard_parts, piece_shapes())
         ]
-        return (
-            jnp.concatenate(full[0:3], axis=1),
-            full[3],
-            jnp.concatenate(full[4:6], axis=1),
-            full[6],
-            None,
-        )
-    block_width = D // LOW_COUNT
-    high_count = device_count // LOW_COUNT
-    rows = piece_rows(device_count)
-
-    def high_pieces(first, last):
-        stacked = gather_high(jnp.concatenate(shard_parts[first:last], axis=0))
-        result = []
-        row_start = 0
-        for row_count in rows[first:last]:
-            result.append(stacked[:, row_start : row_start + row_count])
-            row_start = row_start + row_count
-        return result
-
-    query, key, value, out = high_pieces(0, 4)
-    gate, up, down = high_pieces(4, 7)
-    qkv = jnp.concatenate([piece.reshape(block_width, -1) for piece in (query, key, value)], axis=1)
-    gate_up = jnp.concatenate([piece.reshape(block_width, -1) for piece in (gate, up)], axis=1)
-    return (
-        gather_relative(qkv, RELATIVE_MASKS),
-        gather_placed(out.reshape(high_count, -1, D), PLACED_MASKS),
-        gather_relative(gate_up, RELATIVE_MASKS),
-        gather_placed(down.reshape(high_count, -1, D), PLACED_MASKS),
-        width_order(device_count),
-    )
-
-
-def scatter_weights(wide, tall, wide_columns, device_count):
-    splits = [sum(wide_columns[:count]) for count in range(1, len(wide_columns))]
+        return full, None
+    pieces = [Piece(*shape_pair, device_count) for shape_pair in piece_shapes()]
+    full = []
+    for first, last in CHUNKS:
+        near, far = gather_blocks(pieces[first:last], jnp.concatenate(shard_parts[first:last]))
+        full.extend(assemble(pieces[first:last], near, far))
+    return full, width_order(device_count)
+
+
+CHUNKS = ((0, 4), (4, 6), (6, 7))
+
+
+def scatter_weights(gradients, device_count, chunk):
     if not aligned(device_count):
-        pieces = jnp.split(wide, splits, axis=1) + [tall]
         return jnp.concatenate(
             [
                 lax.psum_scatter(
                     piece.reshape(-1, 128), ALL_AXES, scatter_dimension=0, tiled=True
                 )
-                for piece in pieces
+                for piece in gradients
             ],
             axis=0,
         )
-    high_count = device_count // LOW_COUNT
-    wide = scatter_relative(wide, RELATIVE_MASKS[::-1]).astype(jnp.bfloat16)
-    tall = scatter_placed(tall, high_count, PLACED_MASKS[::-1]).astype(jnp.bfloat16)
-    flat = [
-        piece.reshape(high_count, -1, 128) for piece in jnp.split(wide, splits, axis=1) + [tall]
-    ]
-    return scatter_high(jnp.concatenate(flat, axis=1))
+    pieces = [Piece(*shape_pair, device_count) for shape_pair in piece_shapes()[slice(*chunk)]]
+    return scatter_blocks(pieces, [gradient.astype(jnp.bfloat16) for gradient in gradients])
 
 
 def sum_gains(values, device_count):
@@ -276,9 +365,8 @@
     devices_all = lax.axis_size("dp") * group_size
     group_index = lax.axis_index("group")
     local_rows = tokens.shape[0]
-    qkv_weight, out_weight, gate_up_weight, down_weight, order = gather_weights(
-        master, devices_all
-    )
+    weights, order = gather_weights(master, devices_all)
+    query_weight, key_weight, value_weight, out_weight, gate_weight, up_weight, down_weight = weights
     norm_input = gains[0:D]
     norm_attn = gains[D : 2 * D]
     norm_ffin = gains[2 * D : 3 * D]
@@ -304,10 +392,9 @@
     normed, back_input = jax.vjp(rms_norm, inputs, norm_input)
     normed_low = normed.astype(jnp.bfloat16)
     normed_low = ordered(normed_low)
-    projections = matmul(normed_low, qkv_weight)
-    query_proj = projections[:, : HQ * HD]
-    key_proj = projections[:, HQ * HD : HQ * HD + HD]
-    value_proj = projections[:, HQ * HD + HD :]
+    query_proj = matmul(normed_low, query_weight)
+    key_proj = matmul(normed_low, key_weight)
+    value_proj = matmul(normed_low, value_weight)
 
     def query_prep(flat_rows, gain_vec):
         return rotate(rms_norm(flat_rows.reshape(local_rows, HQ, HD), gain_vec), angles[:, None, :])
@@ -356,9 +443,8 @@
     normed_two, back_ffin = jax.vjp(rms_norm, middle, norm_ffin)
     normed_two_low = normed_two.astype(jnp.bfloat16)
     normed_two_low = ordered(normed_two_low)
-    gate_up_proj = matmul(normed_two_low, gate_up_weight)
-    gate_proj = gate_up_proj[:, :FF]
-    up_proj = gate_up_proj[:, FF:]
+    gate_proj = matmul(normed_two_low, gate_weight)
+    up_proj = matmul(normed_two_low, up_weight)
     hidden, back_hidden = jax.vjp(geglu, gate_proj, up_proj)
     hidden_low = hidden.astype(jnp.bfloat16)
     ffn_out = matmul(hidden_low, down_weight)
@@ -374,15 +460,19 @@
         "td,fd->tf", grad_ffn_low, down_weight, preferred_element_type=jnp.float32
     )
     grad_gate, grad_up = back_hidden(grad_hidden)
-    grad_gate_up_low = jnp.concatenate([grad_gate, grad_up], axis=1).astype(jnp.bfloat16)
-    grad_gate_up_w = jnp.einsum(
-        "td,tf->df", normed_two_low, grad_gate_up_low, preferred_element_type=jnp.float32
-    )
-    grads_ffn = scatter_weights(grad_gate_up_w, grad_down_w, (FF, FF), devices_all)
+    grad_gate_low = grad_gate.astype(jnp.bfloat16)
+    grad_up_low = grad_up.astype(jnp.bfloat16)
+    grads_down = scatter_weights([grad_down_w], devices_all, CHUNKS[2])
+    grad_gate_w = jnp.einsum(
+        "td,tf->df", normed_two_low, grad_gate_low, preferred_element_type=jnp.float32
+    )
+    grad_up_w = jnp.einsum(
+        "td,tf->df", normed_two_low, grad_up_low, preferred_element_type=jnp.float32
+    )
+    grads_gate_up = scatter_weights([grad_gate_w, grad_up_w], devices_all, CHUNKS[1])
     grad_normed_two = restored(
-        jnp.einsum(
-            "tf,df->td", grad_gate_up_low, gate_up_weight, preferred_element_type=jnp.float32
-        )
+        jnp.einsum("tf,df->td", grad_gate_low, gate_weight, preferred_element_type=jnp.float32)
+        + jnp.einsum("tf,df->td", grad_up_low, up_weight, preferred_element_type=jnp.float32)
     )
     grad_middle_norm, grad_gain_ffin = back_ffin(grad_normed_two)
     grad_middle = grad_out + grad_middle_norm
@@ -428,19 +518,29 @@
     value_total = both_total[:, HD:]
     grad_query_proj, grad_gain_query = back_query(grad_query)
     grad_key_proj, grad_gain_key = back_key(key_total)
-    grad_qkv_low = jnp.concatenate([grad_query_proj, grad_key_proj, value_total], axis=1).astype(
-        jnp.bfloat16
-    )
-    grad_qkv_w = jnp.einsum(
-        "td,te->de", normed_low, grad_qkv_low, preferred_element_type=jnp.float32
-    )
-    grads_attn = scatter_weights(grad_qkv_w, grad_out_w, (HQ * HD, HD, HD), devices_all)
+    grad_query_low = grad_query_proj.astype(jnp.bfloat16)
+    grad_key_low = grad_key_proj.astype(jnp.bfloat16)
+    grad_value_low = value_total.astype(jnp.bfloat16)
+    grad_query_w = jnp.einsum(
+        "td,te->de", normed_low, grad_query_low, preferred_element_type=jnp.float32
+    )
+    grad_key_w = jnp.einsum(
+        "td,te->de", normed_low, grad_key_low, preferred_element_type=jnp.float32
+    )
+    grad_value_w = jnp.einsum(
+        "td,te->de", normed_low, grad_value_low, preferred_element_type=jnp.float32
+    )
+    grads_attn = scatter_weights(
+        [grad_query_w, grad_key_w, grad_value_w, grad_out_w], devices_all, CHUNKS[0]
+    )
     grad_normed = restored(
-        jnp.einsum("te,de->td", grad_qkv_low, qkv_weight, preferred_element_type=jnp.float32)
+        jnp.einsum("te,de->td", grad_query_low, query_weight, preferred_element_type=jnp.float32)
+        + jnp.einsum("te,de->td", grad_key_low, key_weight, preferred_element_type=jnp.float32)
+        + jnp.einsum("te,de->td", grad_value_low, value_weight, preferred_element_type=jnp.float32)
     )
     grad_input_norm, grad_gain_input = back_input(grad_normed)
     grad_inputs = grad_middle + grad_input_norm
-    grads_local = jnp.concatenate([grads_attn, grads_ffn], axis=0)
+    grads_local = jnp.concatenate([grads_attn, grads_gate_up, grads_down], axis=0)
     gain_grads = sum_gains(
         jnp.concatenate(
             [

time: 286 us -> 277 us (0.969)
  Pallas kernels: 0 us -> 42 us
  waiting for transfers between devices: 101 us -> 62.6 us
  other arithmetic: 51.5 us -> 22.8 us
  starting transfers between devices: 53.5 us -> 78.7 us
  local copies, waits for them, and re-layouts: 36.8 us -> 25.9 us
    pallas_call x0 -> x12, Pallas kernels: none -> 42 us  [local_call(): pl.pallas_call(kernel, out_shape=outs, in_specs=specs, out_specs=tuple((p...]
    ppermute x41 -> x53, waiting for transfers between devices: 96.7 us -> 59.9 us  [swap(): lax.ppermute(value, ALL_AXES, [(source, source ^ mask) for source in rang...]
    ppermute x41 -> x53, starting transfers between devices: 40.8 us -> 68.7 us  [swap(): lax.ppermute(value, ALL_AXES, [(source, source ^ mask) for source in rang...]
    add x10 -> x3, other arithmetic: 13 us -> 1.13 us  [scatter_blocks(): outs[0]]
    unnamed x183 -> x221, local copies, waits for them, and re-layouts: 7.69 us -> 16.3 us
    select_n x6 -> x0, other arithmetic: 5.93 us -> none  [gather_placed(): jnp.where(low & mask == 0, jnp.concatenate([block, other], axis=axis), jn...]
    slice x13, local copies, waits for them, and re-layouts: 9.37 us -> 4.55 us  [the longest x3 4.19 us: scatter_blocks(): total[:size]]
    reshape x10 -> x0, local copies, waits for them, and re-layouts: 4.56 us -> none  [the longest x5 4.17 us: scatter_weights(): piece.reshape(high_count, -1, 128)]
  transfers between devices with their start and end apart: 47 -> 59, of which waited for: 22 -> 18; matrix products, arithmetic and copies ran while one was open for 29% -> 15% of each run, Pallas kernels for 0% -> 13%
where the time goes in v2:
time: 277 us; the launch traced here: 275 us
  starting transfers between devices  78.7 us (28%)
  waiting for transfers between devices  62.6 us (23%)
  Pallas kernels  42 us (15%)
  matrix products  41.1 us (15%)
  local copies, waits for them, and re-layouts  25.9 us (9%)
  other arithmetic  22.8 us (8%)
    ppermute x53, starting transfers between devices, swap(): lax.ppermute(value, ALL_AXES, [(source, source ^ mask) for source in rang...  68.7 us
    ppermute x53, waiting for transfers between devices, swap(): lax.ppermute(value, ALL_AXES, [(source, source ^ mask) for source in rang...  59.9 us
    pallas_call x12, Pallas kernels, local_call(): pl.pallas_call(kernel, out_shape=outs, in_specs=specs, out_specs=tuple((p...  42 us
    unnamed x221, local copies, waits for them, and re-layouts  16.3 us
    ppermute x6, starting transfers between devices, shifted(): lax.ppermute(value, axis, [(source, source + steps) for source in range(i...  10 us
    dot_general x9, matrix products, matmul(): return jnp.dot(left_side, right_side, preferred_element_type=jnp.float32)  8.25 us
  transfers between devices with their start and end apart: 59, of which 18 were waited for; matrix products, arithmetic and copies ran while one was open for 15% of the time, Pallas kernels for 13%

profile of v2, /device:TPU:0, one launch (start us, length us, event | category | flops | bytes accessed | tf_op | source)
XLA Modules:
  0.0 275.3 jit_solution(2402367885167678622)
XLA Ops:
  1.9 3.1 %collective-permute-start = (bf16[400,128]{1,0:T(8,128)(2,1)S(1)}, bf16[400,128]{1,0:T(8,128)(2,1)S(1)}, u32[]{:S(2)}, u32[]{:S(2)}) collective-permute-start(bf16[400,128]{1,0:T(8,128)(2,1)S(1)} %slice.275.refs_0_), channel_id=1, source_target_pairs={{0,8},{1,9},{2,10},{3,11},{4,12},{5,13},{6,14},{7,15},{8,0},{9,1},... | collective-permute-start | bytes 307208 | tf_op jit(solution)/shard_map/ppermute | solution.py:124
  5.0 2.6 collective-permute-start.1
  8.1 3.9 %collective-permute-start.21 = (bf16[320,128]{1,0:T(8,128)(2,1)S(1)}, bf16[320,128]{1,0:T(8,128)(2,1)S(1)}, u32[]{:S(2)}, u32[]{:S(2)}) collective-permute-start(bf16[320,128]{1,0:T(8,128)(2,1)S(1)} %slice.287.refs_0_), channel_id=1, source_target_pairs={{0,24},{1,25},{2,26},{3,27},{4,28},{5,29},{6,30},{7,31},{8,16},{9,... | collective-permute-start | bytes 245768 | tf_op jit(solution)/shard_map/ppermute | solution.py:124
  24.8 4.2 %collective-permute-start.11 = (bf16[640,128]{1,0:T(8,128)(2,1)S(1)}, bf16[640,128]{1,0:T(8,128)(2,1)S(1)}, u32[]{:S(2)}, u32[]{:S(2)}) collective-permute-start(bf16[640,128]{1,0:T(8,128)(2,1)S(1)} %slice.284.refs_0_), channel_id=1, source_target_pairs={{0,8},{1,9},{2,10},{3,11},{4,12},{5,13},{6,14},{7,15},{8,0},{9,1},... | collective-permute-start | bytes 491528 | tf_op jit(solution)/shard_map/ppermute | solution.py:124
  36.1 5.0 %collective-permute-done.12.refs_2_ = bf16[640,128]{1,0:T(8,128)(2,1)S(1)} collective-permute-done((bf16[640,128]{1,0:T(8,128)(2,1)S(1)}, bf16[640,128]{1,0:T(8,128)(2,1)S(1)}, u32[]{:S(2)}, u32[]{:S(2)}) %collective-permute-start.12) | collective-permute-done | bytes 163872 | tf_op jit(solution)/shard_map/ppermute | solution.py:124
  42.4 2.5 shard_map.154
  48.6 5.1 %collective-permute-done.4 = bf16[1600,128]{1,0:T(8,128)(2,1)S(1)} collective-permute-done((bf16[1600,128]{1,0:T(8,128)(2,1)}, bf16[1600,128]{1,0:T(8,128)(2,1)S(1)}, u32[]{:S(2)}, u32[]{:S(2)}) %collective-permute-start.4) | collective-permute-done | bytes 409632 | tf_op jit(solution)/shard_map/ppermute | solution.py:124
  55.0 8.5 %collective-permute-done.24 = bf16[640,128]{1,0:T(8,128)(2,1)S(1)} collective-permute-done((bf16[640,128]{1,0:T(8,128)(2,1)S(1)}, bf16[640,128]{1,0:T(8,128)(2,1)S(1)}, u32[]{:S(2)}, u32[]{:S(2)}) %collective-permute-start.24) | collective-permute-done | bytes 163872 | tf_op jit(solution)/shard_map/ppermute | solution.py:124
  65.7 3.5 %collective-permute-done.6 = bf16[800,128]{1,0:T(8,128)(2,1)S(1)} collective-permute-done((bf16[800,128]{1,0:T(8,128)(2,1)S(1)}, bf16[800,128]{1,0:T(8,128)(2,1)S(1)}, u32[]{:S(2)}, u32[]{:S(2)}) %collective-permute-start.6) | collective-permute-done | bytes 204832 | tf_op jit(solution)/shard_map/ppermute | solution.py:124
  74.2 6.6 %collective-permute-done.16 = bf16[1280,128]{1,0:T(8,128)(2,1)S(1)} collective-permute-done((bf16[1280,128]{1,0:T(8,128)(2,1)S(1)}, bf16[1280,128]{1,0:T(8,128)(2,1)S(1)}, u32[]{:S(2)}, u32[]{:S(2)}) %collective-permute-start.16) | collective-permute-done | bytes 327712 | tf_op jit(solution)/shard_map/ppermute | solution.py:124
  83.3 3.6 %shard_map.157 = bf16[2048,640]{1,0:T(8,128)(2,1)} custom-call(s32[1]{0:T(128)} %bitcast.index_ref, bf16[5120,128]{1,0:T(8,128)(2,1)} %copy-done.24, bf16[5120,128]{1,0:T(8,128)(2,1)} %copy-done.34), custom_call_target="tpu_custom_call" | custom-call | bytes 5242880 | tf_op jit(solution)/shard_map/pallas_call | solution.py:131
  88.2 4.2 %shard_map.153 = (bf16[640,1024]{1,0:T(8,128)(2,1)}, bf16[640,256]{1,0:T(8,128)(2,1)}, bf16[640,256]{1,0:T(8,128)(2,1)}, bf16[1024,640]{1,0:T(8,128)(2,1)}) custom-call(s32[1]{0:T(128)} %bitcast.index_ref, bf16[6400,128]{1,0:T(8,128)(2,1)} %copy-done.12, bf16[6400,128]{1,0:T(8,128)(2,1)} %copy-done.25), custom_call_target="tpu_custom_call" | custom-call | bytes 6553600 | tf_op jit(solution)/shard_map/pallas_call | solution.py:131
  108.5 6.0 %shard_map.155 = (bf16[640,2048]{1,0:T(8,128)(2,1)}, bf16[640,2048]{1,0:T(8,128)(2,1)}) custom-call(s32[1]{0:T(128)} %bitcast.index_ref, bf16[10240,128]{1,0:T(8,128)(2,1)} %constant_dynamic-update-slice_fusion.5.near_ref, bf16[10240,128]{1,0:T(8,128)(2,1)} %collective-permute-done.18.far_ref), custom_call_target="tpu_custom_call" | custom-call | bytes 10485760 | tf_op jit(solution)/shard_map/pallas_call | solution.py:131
  114.5 2.5 fusion.128
  135.5 3.0 %convolution_bitcast_fusion.3 = f32[128,4,256]{2,0,1:T(8,128)} fusion(f32[4,128,512]{1,2,0:T(8,128)} %convolution_bitcast_fusion, f32[4,128,512]{1,2,0:T(8,128)S(1)} %get-tuple-element.127, f32[4,128]{1,0:T(4,128)S(1)} %copy-done.74, bf16[512,512]{1,0:T(8,128)(2,1)} %copy-done.21), kind=kOutput, calls=%fused_computation.28 | convolution fusion | flops 136053760 | bytes 4984832 | tf_op jit(solution)/shard_map/hqk,kd->qhd/dot_general | solution.py:502
  138.6 3.0 %convolution_bitcast_fusion.2 = f32[512,256]{1,0:T(8,128)} fusion(f32[4,128,512]{1,2,0:T(8,128)} %convolution_bitcast_fusion, f32[4,128,512]{1,2,0:T(8,128)S(1)} %get-tuple-element.127, f32[4,128]{1,0:T(4,128)S(1)} %copy-done.74, bf16[128,4,128]{2,0,1:T(8,128)(2,1)} %copy-done.59, bf16[128,4,128]{2,0,1:T(8,128)(2,1)} %copy-done.58), kind=kOutput, calls=%fused_computation.27 | convolution fusion | flops 136578048 | bytes 2885632 | tf_op jit(solution)/shard_map/hqk,qhd->kd/dot_general | solution.py:505
  141.5 2.6 convolution_convert_fusion.3.refs_3_
  144.2 2.6 convolution_convert_fusion.1.refs_1_
  159.7 3.7 %shard_map.162 = (bf16[5120,128]{1,0:T(8,128)(2,1)}, bf16[5120,128]{1,0:T(8,128)(2,1)}) custom-call(s32[1]{0:T(128)} %bitcast.index_ref, bf16[2048,640]{1,0:T(8,128)(2,1)} %convolution_convert_fusion.refs_0_), custom_call_target="tpu_custom_call" | custom-call | bytes 5242880 | tf_op jit(solution)/shard_map/pallas_call | solution.py:131
  172.1 5.7 %shard_map.160 = (bf16[10240,128]{1,0:T(8,128)(2,1)}, bf16[10240,128]{1,0:T(8,128)(2,1)}) custom-call(s32[1]{0:T(128)} %bitcast.index_ref, bf16[640,2048]{1,0:T(8,128)(2,1)} %convolution_convert_fusion.2.refs_0_, bf16[640,2048]{1,0:T(8,128)(2,1)} %convolution_convert_fusion.1.refs_1_), custom_call_target="tpu_custom_call" | custom-call | bytes 10485760 | tf_op jit(solution)/shard_map/pallas_call | solution.py:131
  178.3 3.5 %collective-permute-start.55 = (f32[24,128]{1,0:T(8,128)S(1)}, f32[24,128]{1,0:T(8,128)S(1)}, u32[]{:S(2)}, u32[]{:S(2)}) collective-permute-start(f32[24,128]{1,0:T(8,128)S(1)} %bitcast_add_fusion), channel_id=1, source_target_pairs={{0,2},{1,3},{2,0},{3,1},{4,6},{5,7},{6,4},{7,5},{8,10},{9,11},{10,... | collective-permute-start | bytes 36872 | tf_op jit(solution)/shard_map/ppermute | solution.py:124
  185.6 4.3 %shard_map.158 = (bf16[6400,128]{1,0:T(8,128)(2,1)}, bf16[6400,128]{1,0:T(8,128)(2,1)}) custom-call(s32[1]{0:T(128)} %bitcast.index_ref, bf16[640,1024]{1,0:T(8,128)(2,1)} %convolution_convert_fusion.4.refs_0_, bf16[640,256]{1,0:T(8,128)(2,1)} %convolution_convert_fusion.6.refs_1_, bf16[640,256]{1,0:T(8,128)(2,1)} %convolution_convert_fusion.5.refs_2_, ...), custom_call_target="tpu_custom_call" | custom-call | bytes 6553600 | tf_op jit(solution)/shard_map/pallas_call | solution.py:131
  189.9 3.9 %collective-permute-start.57 = (f32[24,128]{1,0:T(8,128)S(1)}, f32[24,128]{1,0:T(8,128)S(1)}, u32[]{:S(2)}, u32[]{:S(2)}) collective-permute-start(f32[24,128]{1,0:T(8,128)S(1)} %add.412), channel_id=1, source_target_pairs={{0,8},{1,9},{2,10},{3,11},{4,12},{5,13},{6,14},{7,15},{8,0},{9,1},... | collective-permute-start | bytes 36872 | tf_op jit(solution)/shard_map/ppermute | solution.py:124
  206.0 9.5 %collective-permute-done.31 = bf16[800,128]{1,0:T(8,128)(2,1)S(1)} collective-permute-done((bf16[800,128]{1,0:T(8,128)(2,1)S(1)}, bf16[800,128]{1,0:T(8,128)(2,1)S(1)}, u32[]{:S(2)}, u32[]{:S(2)}) %collective-permute-start.31) | collective-permute-done | bytes 204832 | tf_op jit(solution)/shard_map/ppermute | solution.py:124
  222.3 4.3 %collective-permute-done.39 = bf16[1280,128]{1,0:T(8,128)(2,1)S(1)} collective-permute-done((bf16[1280,128]{1,0:T(8,128)(2,1)S(1)}, bf16[1280,128]{1,0:T(8,128)(2,1)S(1)}, u32[]{:S(2)}, u32[]{:S(2)}) %collective-permute-start.39) | collective-permute-done | bytes 327712 | tf_op jit(solution)/shard_map/ppermute | solution.py:124
  227.4 2.8 %collective-permute-done.41 = bf16[1280,128]{1,0:T(8,128)(2,1)S(1)} collective-permute-done((bf16[1280,128]{1,0:T(8,128)(2,1)S(1)}, bf16[1280,128]{1,0:T(8,128)(2,1)S(1)}, u32[]{:S(2)}, u32[]{:S(2)}) %collective-permute-start.41) | collective-permute-done | bytes 327712 | tf_op jit(solution)/shard_map/ppermute | solution.py:124
  239.2 2.5 collective-permute-start.52
  242.9 2.9 %collective-permute-start.53 = (bf16[320,128]{1,0:T(8,128)(2,1)}, bf16[320,128]{1,0:T(8,128)(2,1)S(1)}, u32[]{:S(2)}, u32[]{:S(2)}) collective-permute-start(bf16[320,128]{1,0:T(8,128)(2,1)} %get-tuple-element.55), channel_id=1, source_target_pairs={{0,24},{1,25},{2,26},{3,27},{4,28},{5,29},{6,30},{7,31},{8,16},{9,... | collective-permute-start | bytes 245768 | tf_op jit(solution)/shard_map/ppermute | solution.py:124
  252.6 2.9 %collective-permute-start.37 = (bf16[400,128]{1,0:T(8,128)(2,1)}, bf16[400,128]{1,0:T(8,128)(2,1)S(1)}, u32[]{:S(2)}, u32[]{:S(2)}) collective-permute-start(bf16[400,128]{1,0:T(8,128)(2,1)} %get-tuple-element.43), channel_id=1, source_target_pairs={{0,24},{1,25},{2,26},{3,27},{4,28},{5,29},{6,30},{7,31},{8,16},{9,... | collective-permute-start | bytes 307208 | tf_op jit(solution)/shard_map/ppermute | solution.py:124
  258.4 3.5 %shard_map.161 = (f32[640,128]{1,0:T(8,128)}, bf16[640,128]{1,0:T(8,128)(2,1)}, bf16[640,128]{1,0:T(8,128)(2,1)}, bf16[640,128]{1,0:T(8,128)(2,1)}) custom-call(s32[1]{0:T(128)} %bitcast.index_ref, f32[2560,128]{1,0:T(8,128)} %slice.303.refs_0_, bf16[2560,128]{1,0:T(8,128)(2,1)} %copy-done.41, bf16[2560,128]{1,0:T(8,128)(2,1)} %copy-done.40), custom_call_target="tpu_custom_call" | custom-call | bytes 3440640 | tf_op jit(solution)/shard_map/pallas_call | solution.py:131
  263.4 2.9 %collective-permute-start.45 = (bf16[640,128]{1,0:T(8,128)(2,1)}, bf16[640,128]{1,0:T(8,128)(2,1)S(1)}, u32[]{:S(2)}, u32[]{:S(2)}) collective-permute-start(bf16[640,128]{1,0:T(8,128)(2,1)} %get-tuple-element.49), channel_id=1, source_target_pairs={{0,24},{1,25},{2,26},{3,27},{4,28},{5,29},{6,30},{7,31},{8,16},{9,... | collective-permute-start | bytes 491528 | tf_op jit(solution)/shard_map/ppermute | solution.py:124
  268.3 4.3 %collective-permute-done.44 = bf16[640,128]{1,0:T(8,128)(2,1)S(1)} collective-permute-done((bf16[640,128]{1,0:T(8,128)(2,1)}, bf16[640,128]{1,0:T(8,128)(2,1)S(1)}, u32[]{:S(2)}, u32[]{:S(2)}) %collective-permute-start.44) | collective-permute-done | bytes 163872 | tf_op jit(solution)/shard_map/ppermute | solution.py:124
  (449 shorter events, 143.7 us)
Async XLA Ops:
  1.9 23.0 %collective-permute-start = (bf16[400,128]{1,0:T(8,128)(2,1)S(1)}, bf16[400,128]{1,0:T(8,128)(2,1)S(1)}, u32[]{:S(2)}, u32[]{:S(2)}) collective-permute-start(bf16[400,128]{1,0:T(8,128)(2,1)S(1)} %slice.275.refs_0_), channel_id=1, source_target_pairs={{0,8},{1,9},{2,10},{3,11},{4,12},{5,13},{6,14},{7,15},{8,0},{9,1},... | collective-permute-start | bytes 307208 | tf_op jit(solution)/shard_map/ppermute | solution.py:124
  5.0 24.1 %collective-permute-start.1 = (bf16[400,128]{1,0:T(8,128)(2,1)S(1)}, bf16[400,128]{1,0:T(8,128)(2,1)S(1)}, u32[]{:S(2)}, u32[]{:S(2)}) collective-permute-start(bf16[400,128]{1,0:T(8,128)(2,1)S(1)} %slice.275.refs_0_), channel_id=1, source_target_pairs={{0,16},{1,17},{2,18},{3,19},{4,20},{5,21},{6,22},{7,23},{8,24},{9,... | collective-permute-start | bytes 307208 | tf_op jit(solution)/shard_map/ppermute | solution.py:124
  16.7 14.4 %collective-permute-start.2 = (bf16[400,128]{1,0:T(8,128)(2,1)S(1)}, bf16[400,128]{1,0:T(8,128)(2,1)S(1)}, u32[]{:S(2)}, u32[]{:S(2)}) collective-permute-start(bf16[400,128]{1,0:T(8,128)(2,1)S(1)} %slice.275.refs_0_), channel_id=1, source_target_pairs={{0,24},{1,25},{2,26},{3,27},{4,28},{5,29},{6,30},{7,31},{8,16},{9,... | collective-permute-start | bytes 307208 | tf_op jit(solution)/shard_map/ppermute | solution.py:124
  20.8 26.1 %collective-permute-start.22 = (bf16[1280,128]{1,0:T(8,128)(2,1)}, bf16[1280,128]{1,0:T(8,128)(2,1)S(1)}, u32[]{:S(2)}, u32[]{:S(2)}) collective-permute-start(bf16[1280,128]{1,0:T(8,128)(2,1)} %shard_map.156), channel_id=1, source_target_pairs={{0,4},{1,5},{2,6},{3,7},{4,0},{5,1},{6,2},{7,3},{8,12},{9,13},{10,... | collective-permute-start | bytes 983048 | tf_op jit(solution)/shard_map/ppermute | solution.py:124
  22.3 23.3 %collective-permute-start.23 = (bf16[1280,128]{1,0:T(8,128)(2,1)}, bf16[1280,128]{1,0:T(8,128)(2,1)S(1)}, u32[]{:S(2)}, u32[]{:S(2)}) collective-permute-start(bf16[1280,128]{1,0:T(8,128)(2,1)} %shard_map.156), channel_id=1, source_target_pairs={{0,2},{1,3},{2,0},{3,1},{4,6},{5,7},{6,4},{7,5},{8,10},{9,11},{10,... | collective-permute-start | bytes 983048 | tf_op jit(solution)/shard_map/ppermute | solution.py:124
  29.0 12.1 %collective-permute-start.12 = (bf16[640,128]{1,0:T(8,128)(2,1)S(1)}, bf16[640,128]{1,0:T(8,128)(2,1)S(1)}, u32[]{:S(2)}, u32[]{:S(2)}) collective-permute-start(bf16[640,128]{1,0:T(8,128)(2,1)S(1)} %slice.284.refs_0_), channel_id=1, source_target_pairs={{0,16},{1,17},{2,18},{3,19},{4,20},{5,21},{6,22},{7,23},{8,24},{9,... | collective-permute-start | bytes 491528 | tf_op jit(solution)/shard_map/ppermute | solution.py:124
  35.5 18.7 %collective-permute-start.3 = (bf16[1600,128]{1,0:T(8,128)(2,1)}, bf16[1600,128]{1,0:T(8,128)(2,1)S(1)}, u32[]{:S(2)}, u32[]{:S(2)}) collective-permute-start(bf16[1600,128]{1,0:T(8,128)(2,1)} %shard_map.152), channel_id=1, source_target_pairs={{0,4},{1,5},{2,6},{3,7},{4,0},{5,1},{6,2},{7,3},{8,12},{9,13},{10,... | collective-permute-start | bytes 1228808 | tf_op jit(solution)/shard_map/ppermute | solution.py:124
  41.1 12.6 %collective-permute-start.4 = (bf16[1600,128]{1,0:T(8,128)(2,1)}, bf16[1600,128]{1,0:T(8,128)(2,1)S(1)}, u32[]{:S(2)}, u32[]{:S(2)}) collective-permute-start(bf16[1600,128]{1,0:T(8,128)(2,1)} %shard_map.152), channel_id=1, source_target_pairs={{0,2},{1,3},{2,0},{3,1},{4,6},{5,7},{6,4},{7,5},{8,10},{9,11},{10,... | collective-permute-start | bytes 1228808 | tf_op jit(solution)/shard_map/ppermute | solution.py:124
  45.0 26.7 %collective-permute-start.14 = (bf16[2560,128]{1,0:T(8,128)(2,1)}, bf16[2560,128]{1,0:T(8,128)(2,1)S(1)}, u32[]{:S(2)}, u32[]{:S(2)}) collective-permute-start(bf16[2560,128]{1,0:T(8,128)(2,1)} %shard_map.154), channel_id=1, source_target_pairs={{0,4},{1,5},{2,6},{3,7},{4,0},{5,1},{6,2},{7,3},{8,12},{9,13},{10,... | collective-permute-start | bytes 1966088 | tf_op jit(solution)/shard_map/ppermute | solution.py:124
  45.5 25.6 %collective-permute-start.15 = (bf16[2560,128]{1,0:T(8,128)(2,1)}, bf16[2560,128]{1,0:T(8,128)(2,1)S(1)}, u32[]{:S(2)}, u32[]{:S(2)}) collective-permute-start(bf16[2560,128]{1,0:T(8,128)(2,1)} %shard_map.154), channel_id=1, source_target_pairs={{0,2},{1,3},{2,0},{3,1},{4,6},{5,7},{6,4},{7,5},{8,10},{9,11},{10,... | collective-permute-start | bytes 1966088 | tf_op jit(solution)/shard_map/ppermute | solution.py:124
  46.9 16.6 %collective-permute-start.24 = (bf16[640,128]{1,0:T(8,128)(2,1)S(1)}, bf16[640,128]{1,0:T(8,128)(2,1)S(1)}, u32[]{:S(2)}, u32[]{:S(2)}) collective-permute-start(bf16[640,128]{1,0:T(8,128)(2,1)S(1)} %slice.288), channel_id=1, source_target_pairs={{0,4},{1,5},{2,6},{3,7},{4,0},{5,1},{6,2},{7,3},{8,12},{9,13},{10,... | collective-permute-start | bytes 491528 | tf_op jit(solution)/shard_map/ppermute | solution.py:124
  53.7 15.7 %collective-permute-start.25 = (bf16[640,128]{1,0:T(8,128)(2,1)S(1)}, bf16[640,128]{1,0:T(8,128)(2,1)S(1)}, u32[]{:S(2)}, u32[]{:S(2)}) collective-permute-start(bf16[640,128]{1,0:T(8,128)(2,1)S(1)} %slice.289), channel_id=1, source_target_pairs={{0,2},{1,3},{2,0},{3,1},{4,6},{5,7},{6,4},{7,5},{8,10},{9,11},{10,... | collective-permute-start | bytes 491528 | tf_op jit(solution)/shard_map/ppermute | solution.py:124
  54.2 11.5 %collective-permute-start.5 = (bf16[800,128]{1,0:T(8,128)(2,1)S(1)}, bf16[800,128]{1,0:T(8,128)(2,1)S(1)}, u32[]{:S(2)}, u32[]{:S(2)}) collective-permute-start(bf16[800,128]{1,0:T(8,128)(2,1)S(1)} %slice.276), channel_id=1, source_target_pairs={{0,4},{1,5},{2,6},{3,7},{4,0},{5,1},{6,2},{7,3},{8,12},{9,13},{10,... | collective-permute-start | bytes 614408 | tf_op jit(solution)/shard_map/ppermute | solution.py:124
  69.3 17.7 %collective-permute-start.7 = (bf16[6400,128]{1,0:T(8,128)(2,1)S(1)}, bf16[6400,128]{1,0:T(8,128)(2,1)S(1)}, u32[]{:S(2)}, u32[]{:S(2)}) collective-permute-start(bf16[6400,128]{1,0:T(8,128)(2,1)S(1)} %constant_dynamic-update-slice_fusion.near_ref), channel_id=1, source_target_pairs={{0,1},{1,0},{2,3},{3,2},{4,5},{5,4},{6,7},{7,6},{8,9},{9,8},{10,11... | collective-permute-start | bytes 4915208 | tf_op jit(solution)/shard_map/ppermute | solution.py:124
  69.4 12.8 %collective-permute-start.26 = (bf16[5120,128]{1,0:T(8,128)(2,1)S(1)}, bf16[5120,128]{1,0:T(8,128)(2,1)S(1)}, u32[]{:S(2)}, u32[]{:S(2)}) collective-permute-start(bf16[5120,128]{1,0:T(8,128)(2,1)S(1)} %constant_dynamic-update-slice_fusion.10.near_ref), channel_id=1, source_target_pairs={{0,1},{1,0},{2,3},{3,2},{4,5},{5,4},{6,7},{7,6},{8,9},{9,8},{10,11... | collective-permute-start | bytes 3932168 | tf_op jit(solution)/shard_map/ppermute | solution.py:124
  82.3 26.2 %collective-permute-start.18 = (bf16[10240,128]{1,0:T(8,128)(2,1)}, bf16[10240,128]{1,0:T(8,128)(2,1)}, u32[]{:S(2)}, u32[]{:S(2)}) collective-permute-start(bf16[10240,128]{1,0:T(8,128)(2,1)} %constant_dynamic-update-slice_fusion.5.near_ref), channel_id=1, source_target_pairs={{0,1},{1,0},{2,3},{3,2},{4,5},{5,4},{6,7},{7,6},{8,9},{9,8},{10,11... | collective-permute-start | bytes 7864328 | tf_op jit(solution)/shard_map/ppermute | solution.py:124
  163.4 30.4 %collective-permute-start.46 = (bf16[5120,128]{1,0:T(8,128)(2,1)}, bf16[5120,128]{1,0:T(8,128)(2,1)S(1)}, u32[]{:S(2)}, u32[]{:S(2)}) collective-permute-start(bf16[5120,128]{1,0:T(8,128)(2,1)} %get-tuple-element.51), channel_id=1, source_target_pairs={{0,1},{1,0},{2,3},{3,2},{4,5},{5,4},{6,7},{7,6},{8,9},{9,8},{10,11... | collective-permute-start | bytes 3932168 | tf_op jit(solution)/shard_map/ppermute | solution.py:124
  177.8 38.7 %collective-permute-start.38 = (bf16[10240,128]{1,0:T(8,128)(2,1)}, bf16[10240,128]{1,0:T(8,128)(2,1)}, u32[]{:S(2)}, u32[]{:S(2)}) collective-permute-start(bf16[10240,128]{1,0:T(8,128)(2,1)} %get-tuple-element.45), channel_id=1, source_target_pairs={{0,1},{1,0},{2,3},{3,2},{4,5},{5,4},{6,7},{7,6},{8,9},{9,8},{10,11... | collective-permute-start | bytes 7864328 | tf_op jit(solution)/shard_map/ppermute | solution.py:124
  189.9 12.9 %collective-permute-start.30 = (bf16[6400,128]{1,0:T(8,128)(2,1)}, bf16[6400,128]{1,0:T(8,128)(2,1)S(1)}, u32[]{:S(2)}, u32[]{:S(2)}) collective-permute-start(bf16[6400,128]{1,0:T(8,128)(2,1)} %get-tuple-element.39), channel_id=1, source_target_pairs={{0,1},{1,0},{2,3},{3,2},{4,5},{5,4},{6,7},{7,6},{8,9},{9,8},{10,11... | collective-permute-start | bytes 4915208 | tf_op jit(solution)/shard_map/ppermute | solution.py:124
  197.2 41.0 %collective-permute-start.58 = (f32[24,128]{1,0:T(8,128)S(1)}, f32[24,128]{1,0:T(8,128)S(1)}, u32[]{:S(2)}, u32[]{:S(2)}) collective-permute-start(f32[24,128]{1,0:T(8,128)S(1)} %add.413), channel_id=1, source_target_pairs={{0,16},{1,17},{2,18},{3,19},{4,20},{5,21},{6,22},{7,23},{8,24},{9,... | collective-permute-start | bytes 36872 | tf_op jit(solution)/shard_map/ppermute | solution.py:124
  202.4 29.8 %collective-permute-start.50 = (bf16[1280,128]{1,0:T(8,128)(2,1)S(1)}, bf16[1280,128]{1,0:T(8,128)(2,1)S(1)}, u32[]{:S(2)}, u32[]{:S(2)}) collective-permute-start(bf16[1280,128]{1,0:T(8,128)(2,1)S(1)} %pad_maximum_fusion.7), channel_id=1, source_target_pairs={{0,2},{1,3},{2,0},{3,1},{4,6},{5,7},{6,4},{7,5},{8,10},{9,11},{10,... | collective-permute-start | bytes 983048 | tf_op jit(solution)/shard_map/ppermute | solution.py:124
  203.3 12.1 %collective-permute-start.31 = (bf16[800,128]{1,0:T(8,128)(2,1)S(1)}, bf16[800,128]{1,0:T(8,128)(2,1)S(1)}, u32[]{:S(2)}, u32[]{:S(2)}) collective-permute-start(bf16[800,128]{1,0:T(8,128)(2,1)S(1)} %get-tuple-element.97), channel_id=1, source_target_pairs={{0,2},{1,3},{2,0},{3,1},{4,6},{5,7},{6,4},{7,5},{8,10},{9,11},{10,... | collective-permute-start | bytes 614408 | tf_op jit(solution)/shard_map/ppermute | solution.py:124
  215.4 17.7 %collective-permute-start.48 = (bf16[1280,128]{1,0:T(8,128)(2,1)S(1)}, bf16[1280,128]{1,0:T(8,128)(2,1)S(1)}, u32[]{:S(2)}, u32[]{:S(2)}) collective-permute-start(bf16[1280,128]{1,0:T(8,128)(2,1)S(1)} %pad_maximum_fusion.6), channel_id=1, source_target_pairs={{0,4},{1,5},{2,6},{3,7},{4,0},{5,1},{6,2},{7,3},{8,12},{9,13},{10,... | collective-permute-start | bytes 983048 | tf_op jit(solution)/shard_map/ppermute | solution.py:124
  226.7 12.5 %collective-permute-start.34 = (bf16[1600,128]{1,0:T(8,128)(2,1)}, bf16[1600,128]{1,0:T(8,128)(2,1)S(1)}, u32[]{:S(2)}, u32[]{:S(2)}) collective-permute-start(bf16[1600,128]{1,0:T(8,128)(2,1)} %pad_maximum_fusion.5), channel_id=1, source_target_pairs={{0,2},{1,3},{2,0},{3,1},{4,6},{5,7},{6,4},{7,5},{8,10},{9,11},{10,... | collective-permute-start | bytes 1228808 | tf_op jit(solution)/shard_map/ppermute | solution.py:124
  230.2 12.7 %collective-permute-start.32 = (bf16[1600,128]{1,0:T(8,128)(2,1)}, bf16[1600,128]{1,0:T(8,128)(2,1)}, u32[]{:S(2)}, u32[]{:S(2)}) collective-permute-start(bf16[1600,128]{1,0:T(8,128)(2,1)} %pad_maximum_fusion.4), channel_id=1, source_target_pairs={{0,4},{1,5},{2,6},{3,7},{4,0},{5,1},{6,2},{7,3},{8,12},{9,13},{10,... | collective-permute-start | bytes 1228808 | tf_op jit(solution)/shard_map/ppermute | solution.py:124
  232.2 24.5 %collective-permute-start.42 = (bf16[2560,128]{1,0:T(8,128)(2,1)S(1)}, bf16[2560,128]{1,0:T(8,128)(2,1)S(1)}, u32[]{:S(2)}, u32[]{:S(2)}) collective-permute-start(bf16[2560,128]{1,0:T(8,128)(2,1)S(1)} %pad_maximum_fusion.3), channel_id=1, source_target_pairs={{0,2},{1,3},{2,0},{3,1},{4,6},{5,7},{6,4},{7,5},{8,10},{9,11},{10,... | collective-permute-start | bytes 1966088 | tf_op jit(solution)/shard_map/ppermute | solution.py:124
  233.2 23.6 %collective-permute-start.40 = (bf16[2560,128]{1,0:T(8,128)(2,1)}, bf16[2560,128]{1,0:T(8,128)(2,1)S(1)}, u32[]{:S(2)}, u32[]{:S(2)}) collective-permute-start(bf16[2560,128]{1,0:T(8,128)(2,1)} %pad_maximum_fusion.2), channel_id=1, source_target_pairs={{0,4},{1,5},{2,6},{3,7},{4,0},{5,1},{6,2},{7,3},{8,12},{9,13},{10,... | collective-permute-start | bytes 1966088 | tf_op jit(solution)/shard_map/ppermute | solution.py:124
  238.2 12.9 %collective-permute-start.51 = (bf16[320,128]{1,0:T(8,128)(2,1)}, bf16[320,128]{1,0:T(8,128)(2,1)S(1)}, u32[]{:S(2)}, u32[]{:S(2)}) collective-permute-start(bf16[320,128]{1,0:T(8,128)(2,1)} %get-tuple-element.53), channel_id=1, source_target_pairs={{0,8},{1,9},{2,10},{3,11},{4,12},{5,13},{6,14},{7,15},{8,0},{9,1},... | collective-permute-start | bytes 245768 | tf_op jit(solution)/shard_map/ppermute | solution.py:124
  239.2 12.0 %collective-permute-start.52 = (bf16[320,128]{1,0:T(8,128)(2,1)}, bf16[320,128]{1,0:T(8,128)(2,1)S(1)}, u32[]{:S(2)}, u32[]{:S(2)}) collective-permute-start(bf16[320,128]{1,0:T(8,128)(2,1)} %get-tuple-element.54), channel_id=1, source_target_pairs={{0,16},{1,17},{2,18},{3,19},{4,20},{5,21},{6,22},{7,23},{8,24},{9,... | collective-permute-start | bytes 245768 | tf_op jit(solution)/shard_map/ppermute | solution.py:124
  251.1 12.2 %collective-permute-start.35 = (bf16[400,128]{1,0:T(8,128)(2,1)}, bf16[400,128]{1,0:T(8,128)(2,1)S(1)}, u32[]{:S(2)}, u32[]{:S(2)}) collective-permute-start(bf16[400,128]{1,0:T(8,128)(2,1)} %get-tuple-element.41), channel_id=1, source_target_pairs={{0,8},{1,9},{2,10},{3,11},{4,12},{5,13},{6,14},{7,15},{8,0},{9,1},... | collective-permute-start | bytes 307208 | tf_op jit(solution)/shard_map/ppermute | solution.py:124
  251.1 15.2 %collective-permute-start.36 = (bf16[400,128]{1,0:T(8,128)(2,1)}, bf16[400,128]{1,0:T(8,128)(2,1)S(1)}, u32[]{:S(2)}, u32[]{:S(2)}) collective-permute-start(bf16[400,128]{1,0:T(8,128)(2,1)} %get-tuple-element.42), channel_id=1, source_target_pairs={{0,16},{1,17},{2,18},{3,19},{4,20},{5,21},{6,22},{7,23},{8,24},{9,... | collective-permute-start | bytes 307208 | tf_op jit(solution)/shard_map/ppermute | solution.py:124
  252.6 13.8 %collective-permute-start.37 = (bf16[400,128]{1,0:T(8,128)(2,1)}, bf16[400,128]{1,0:T(8,128)(2,1)S(1)}, u32[]{:S(2)}, u32[]{:S(2)}) collective-permute-start(bf16[400,128]{1,0:T(8,128)(2,1)} %get-tuple-element.43), channel_id=1, source_target_pairs={{0,24},{1,25},{2,26},{3,27},{4,28},{5,29},{6,30},{7,31},{8,16},{9,... | collective-permute-start | bytes 307208 | tf_op jit(solution)/shard_map/ppermute | solution.py:124
  (129 other events, 977.0 us)

commit v3 on v2

--- a/solution.py
+++ b/solution.py
@@ -112,6 +112,8 @@
 LOW_COUNT = 8
 LANES = 128
 LOW_MASKS = (0, 4, 2, 6, 1, 5, 3, 7)
+GELU_SCALE = (2.0 / math.pi) ** 0.5
+GELU_CUBE = 0.044715
 VMEM_BYTES = 56 * 1024 * 1024
 
 
@@ -266,15 +268,19 @@
     )
 
 
-def scatter_blocks(pieces, gradients):
+def split(pieces, gradients):
+    size = sum(piece.size for piece in pieces)
+    return local_call(
+        functools.partial(split_kernel, pieces),
+        (array((4 * size, LANES), jnp.bfloat16),) * 2,
+        [gradient.astype(jnp.bfloat16) for gradient in gradients],
+    )
+
+
+def scatter_blocks(pieces, near, far):
     high_count = pieces[0].high_count
     size = sum(piece.size for piece in pieces)
     flat_rows = sum(piece.flat_rows for piece in pieces)
-    near, far = local_call(
-        functools.partial(split_kernel, pieces),
-        (array((4 * size, LANES), jnp.bfloat16),) * 2,
-        gradients,
-    )
     total = near.astype(jnp.float32) + swap(far, 1).astype(jnp.float32)
     half = size // 2
     diagonal = total[3 * size :].astype(jnp.bfloat16)
@@ -299,6 +305,223 @@
     )
 
 
+def norm_parts(values):
+    scale = lax.rsqrt(jnp.mean(values * values, axis=-1, keepdims=True) + norm_eps)
+    return scale, values * scale
+
+
+def norm_back(scale, normal, upstream, weight_vec):
+    weighted = upstream * (1.0 + weight_vec)
+    inner = jnp.mean(weighted * normal, axis=-1, keepdims=True)
+    return scale * (weighted - normal * inner), jnp.sum(normal * upstream, axis=0, keepdims=True)
+
+
+def product(left_side, right_side, left_axis, right_axis):
+    return lax.dot_general(
+        left_side,
+        right_side,
+        (((left_axis,), (right_axis,)), ((), ())),
+        preferred_element_type=jnp.float32,
+    )
+
+
+def unordered(rows_in, order_low):
+    upper = rows_in.astype(jnp.bfloat16)
+    lower = (rows_in - upper.astype(jnp.float32)).astype(jnp.bfloat16)
+    return product(upper, order_low, 1, 1) + product(lower, order_low, 1, 1)
+
+
+def wide_tile(near_ref, far_ref, size, start, rows):
+    return jnp.concatenate(
+        [
+            ref[place * size + start : place * size + start + rows, :]
+            for ref in (near_ref, far_ref)
+            for place in range(4)
+        ]
+    )
+
+
+def put_wide_tile(near_ref, far_ref, size, start, rows, tile):
+    for order in range(LOW_COUNT):
+        target = near_ref if order < 4 else far_ref
+        first = (order % 4) * size + start
+        target[first : first + rows, :] = tile[order * rows : (order + 1) * rows]
+
+
+def tall_rows(piece, low):
+    for order, mask in enumerate(LOW_MASKS):
+        for block in range(piece.blocks):
+            for place in range(piece.high_count):
+                row = (place * LOW_COUNT + (low ^ mask)) * piece.own_rows
+                yield (
+                    order,
+                    block * piece.block_rows + place * piece.own_rows,
+                    pl.ds(pl.multiple_of(row, piece.own_rows), piece.own_rows),
+                    slice(block * LANES, (block + 1) * LANES),
+                )
+
+
+def ffn_kernel(
+    gate_piece,
+    down_piece,
+    index_ref,
+    middle_ref,
+    cotangent_ref,
+    gain_in_ref,
+    gain_out_ref,
+    order_ref,
+    near_ref,
+    far_ref,
+    near_down_ref,
+    far_down_ref,
+    block_out_ref,
+    grad_middle_ref,
+    grad_gain_in_ref,
+    grad_gain_out_ref,
+    grad_near_ref,
+    grad_far_ref,
+    grad_near_down_ref,
+    grad_far_down_ref,
+    down_ref,
+    hidden_ref,
+    gelu_ref,
+    slope_ref,
+):
+    low = index_ref[0] % LOW_COUNT
+    rows = gate_piece.block_rows
+    size = 2 * gate_piece.size
+    width = 2 * LANES
+    for order, first, matrix_rows, columns in tall_rows(down_piece, low):
+        source = near_down_ref if order < 4 else far_down_ref
+        first = first + (order % 4) * down_piece.size
+        down_ref[matrix_rows, columns] = source[first : first + down_piece.own_rows, :]
+
+    def wide_tiles(step):
+        return [
+            jnp.concatenate(
+                [
+                    wide_tile(near_ref, far_ref, size, offset + block * rows, rows)
+                    for block in (2 * step, 2 * step + 1)
+                ],
+                axis=1,
+            )
+            for offset in (0, gate_piece.size)
+        ]
+
+    middle = middle_ref[...]
+    scale_in, normal_in = norm_parts(middle)
+    order_low = order_ref[...]
+    normed = (normal_in * (1.0 + gain_in_ref[...])).astype(jnp.bfloat16)
+    normed = product(normed, order_low, 1, 0).astype(jnp.bfloat16)
+    for step in range(FF // width):
+        columns = slice(step * width, (step + 1) * width)
+        gate_weight, up_weight = wide_tiles(step)
+        gate = product(normed, gate_weight, 1, 0)
+        up = product(normed, up_weight, 1, 0)
+        square = gate * gate
+        bend = jnp.tanh(GELU_SCALE * gate * (1.0 + GELU_CUBE * square))
+        half = 0.5 * (1.0 + bend)
+        gelu = gate * half
+        slope = half + 0.5 * gate * (1.0 - bend * bend) * GELU_SCALE * (
+            1.0 + 3.0 * GELU_CUBE * square
+        )
+        gelu_ref[:, columns] = gelu
+        slope_ref[:, columns] = slope * up
+        hidden_ref[:, columns] = (gelu * up).astype(jnp.bfloat16)
+    hidden = hidden_ref[...]
+    scale_out, normal_out = norm_parts(product(hidden, down_ref[...], 1, 0))
+    block_out_ref[...] = (middle + normal_out * (1.0 + gain_out_ref[...])).astype(jnp.bfloat16)
+    upstream = cotangent_ref[...].astype(jnp.float32)
+    grad_ffn, grad_gain_out_ref[...] = norm_back(
+        scale_out, normal_out, upstream, gain_out_ref[...]
+    )
+    grad_ffn = grad_ffn.astype(jnp.bfloat16)
+    grad_normed = jnp.zeros(middle.shape, jnp.float32)
+    for step in range(FF // width):
+        columns = slice(step * width, (step + 1) * width)
+        grad_hidden = product(grad_ffn, down_ref[columns, :], 1, 1)
+        down_ref[columns, :] = product(hidden_ref[:, columns], grad_ffn, 0, 0).astype(jnp.bfloat16)
+        grads = [
+            (grad_hidden * slope_ref[:, columns]).astype(jnp.bfloat16),
+            (grad_hidden * gelu_ref[:, columns]).astype(jnp.bfloat16),
+        ]
+        for place, (grad, weight) in enumerate(zip(grads, wide_tiles(step))):
+            grad_weight = product(normed, grad, 0, 0).astype(jnp.bfloat16)
+            for side in range(2):
+                put_wide_tile(
+                    grad_near_ref,
+                    grad_far_ref,
+                    size,
+                    place * gate_piece.size + (2 * step + side) * rows,
+                    rows,
+                    grad_weight[:, side * LANES : (side + 1) * LANES],
+                )
+            grad_normed = grad_normed + product(grad, weight, 1, 1)
+    for order, first, matrix_rows, columns in tall_rows(down_piece, low):
+        target = grad_near_down_ref if order < 4 else grad_far_down_ref
+        first = first + (order % 4) * down_piece.size
+        target[first : first + down_piece.own_rows, :] = down_ref[matrix_rows, columns]
+    grad_middle, grad_gain_in_ref[...] = norm_back(
+        scale_in, normal_in, unordered(grad_normed, order_low), gain_in_ref[...]
+    )
+    grad_middle_ref[...] = upstream + grad_middle
+
+
+def ffn_blocks(pieces, middle, cotangent, gain_in, gain_out, order, gate_up, down):
+    rows = middle.shape[0]
+    shapes = [array(value.shape, jnp.bfloat16) for value in (*gate_up, *down)]
+    outs = local_call(
+        functools.partial(ffn_kernel, pieces[4], pieces[6]),
+        (
+            array((rows, D), jnp.bfloat16),
+            array((rows, D), jnp.float32),
+            array((1, D), jnp.float32),
+            array((1, D), jnp.float32),
+            *shapes,
+        ),
+        (middle, cotangent, gain_in[None], gain_out[None], order, *gate_up, *down),
+        (
+            pltpu.VMEM((FF, D), jnp.bfloat16),
+            pltpu.VMEM((rows, FF), jnp.bfloat16),
+            pltpu.VMEM((rows, FF), jnp.float32),
+            pltpu.VMEM((rows, FF), jnp.float32),
+        ),
+        flops=18 * rows * D * FF,
+    )
+    return outs[0], outs[1], outs[2][0], outs[3][0], outs[4:6], outs[6:8]
+
+
+def ffn_plain(middle, cotangent, gain_in, gain_out, gate_weight, up_weight, down_weight):
+    normed_two, back_ffin = jax.vjp(rms_norm, middle, gain_in)
+    normed_two_low = normed_two.astype(jnp.bfloat16)
+    gate_proj = matmul(normed_two_low, gate_weight)
+    up_proj = matmul(normed_two_low, up_weight)
+    hidden, back_hidden = jax.vjp(geglu, gate_proj, up_proj)
+    hidden_low = hidden.astype(jnp.bfloat16)
+    branch_two, back_ffout = jax.vjp(rms_norm, matmul(hidden_low, down_weight), gain_out)
+    grad_out = cotangent.astype(jnp.float32)
+    grad_ffn, grad_gain_ffout = back_ffout(grad_out)
+    grad_ffn_low = grad_ffn.astype(jnp.bfloat16)
+    grad_gate, grad_up = back_hidden(product(grad_ffn_low, down_weight, 1, 1))
+    grad_gate_low = grad_gate.astype(jnp.bfloat16)
+    grad_up_low = grad_up.astype(jnp.bfloat16)
+    grad_weights = [
+        product(normed_two_low, grad_gate_low, 0, 0),
+        product(normed_two_low, grad_up_low, 0, 0),
+        product(hidden_low, grad_ffn_low, 0, 0),
+    ]
+    grad_middle, grad_gain_ffin = back_ffin(
+        product(grad_gate_low, gate_weight, 1, 1) + product(grad_up_low, up_weight, 1, 1)
+    )
+    return (
+        (middle + branch_two).astype(jnp.bfloat16),
+        grad_out + grad_middle,
+        grad_gain_ffin,
+        grad_gain_ffout,
+        grad_weights,
+    )
+
+
 def width_order(device_count):
     low = lax.axis_index(ALL_AXES) % LOW_COUNT
     rows = D // device_count
@@ -311,40 +534,34 @@
     return (jnp.arange(D, dtype=jnp.int32)[:, None] == picked[None, :]).astype(jnp.float32)
 
 
-def gather_weights(master, device_count):
+def gather_weights(master, device_count, pieces):
     shard_parts = [
         part_rows.astype(jnp.bfloat16) for part_rows in split_rows(master, piece_rows(device_count))
     ]
-    if not aligned(device_count):
+    if pieces is None:
         full = [
             lax.all_gather(part, ALL_AXES, axis=0, tiled=True).reshape(shape_pair)
             for part, shape_pair in zip(shard_parts, piece_shapes())
         ]
-        return full, None
-    pieces = [Piece(*shape_pair, device_count) for shape_pair in piece_shapes()]
-    full = []
-    for first, last in CHUNKS:
-        near, far = gather_blocks(pieces[first:last], jnp.concatenate(shard_parts[first:last]))
-        full.extend(assemble(pieces[first:last], near, far))
-    return full, width_order(device_count)
+        return full[:4], full[4:], None
+    blocks = [
+        gather_blocks(pieces[first:last], jnp.concatenate(shard_parts[first:last]))
+        for first, last in CHUNKS
+    ]
+    return assemble(pieces[:4], *blocks[0]), blocks[1:], width_order(device_count)
 
 
 CHUNKS = ((0, 4), (4, 6), (6, 7))
 
 
-def scatter_weights(gradients, device_count, chunk):
-    if not aligned(device_count):
-        return jnp.concatenate(
-            [
-                lax.psum_scatter(
-                    piece.reshape(-1, 128), ALL_AXES, scatter_dimension=0, tiled=True
-                )
-                for piece in gradients
-            ],
-            axis=0,
-        )
-    pieces = [Piece(*shape_pair, device_count) for shape_pair in piece_shapes()[slice(*chunk)]]
-    return scatter_blocks(pieces, [gradient.astype(jnp.bfloat16) for gradient in gradients])
+def scatter_plain(gradients):
+    return jnp.concatenate(
+        [
+            lax.psum_scatter(piece.reshape(-1, 128), ALL_AXES, scatter_dimension=0, tiled=True)
+            for piece in gradients
+        ],
+        axis=0,
+    )
 
 
 def sum_gains(values, device_count):
@@ -365,8 +582,11 @@
     devices_all = lax.axis_size("dp") * group_size
     group_index = lax.axis_index("group")
     local_rows = tokens.shape[0]
-    weights, order = gather_weights(master, devices_all)
-    query_weight, key_weight, value_weight, out_weight, gate_weight, up_weight, down_weight = weights
+    pieces = None
+    if aligned(devices_all):
+        pieces = [Piece(*shape_pair, devices_all) for shape_pair in piece_shapes()]
+    attention_weights, ffn_weights, order = gather_weights(master, devices_all, pieces)
+    query_weight, key_weight, value_weight, out_weight = attention_weights
     norm_input = gains[0:D]
     norm_attn = gains[D : 2 * D]
     norm_ffin = gains[2 * D : 3 * D]
@@ -440,42 +660,29 @@
     attn_out = matmul(attended_low, out_weight)
     branch_one, back_attn = jax.vjp(rms_norm, attn_out, norm_attn)
     middle = inputs + branch_one
-    normed_two, back_ffin = jax.vjp(rms_norm, middle, norm_ffin)
-    normed_two_low = normed_two.astype(jnp.bfloat16)
-    normed_two_low = ordered(normed_two_low)
-    gate_proj = matmul(normed_two_low, gate_weight)
-    up_proj = matmul(normed_two_low, up_weight)
-    hidden, back_hidden = jax.vjp(geglu, gate_proj, up_proj)
-    hidden_low = hidden.astype(jnp.bfloat16)
-    ffn_out = matmul(hidden_low, down_weight)
-    branch_two, back_ffout = jax.vjp(rms_norm, ffn_out, norm_ffout)
-    outputs = middle + branch_two
-    grad_out = cotangent.astype(jnp.float32)
-    grad_ffn, grad_gain_ffout = back_ffout(grad_out)
-    grad_ffn_low = grad_ffn.astype(jnp.bfloat16)
-    grad_down_w = jnp.einsum(
-        "tf,td->fd", hidden_low, grad_ffn_low, preferred_element_type=jnp.float32
-    )
-    grad_hidden = jnp.einsum(
-        "td,fd->tf", grad_ffn_low, down_weight, preferred_element_type=jnp.float32
-    )
-    grad_gate, grad_up = back_hidden(grad_hidden)
-    grad_gate_low = grad_gate.astype(jnp.bfloat16)
-    grad_up_low = grad_up.astype(jnp.bfloat16)
-    grads_down = scatter_weights([grad_down_w], devices_all, CHUNKS[2])
-    grad_gate_w = jnp.einsum(
-        "td,tf->df", normed_two_low, grad_gate_low, preferred_element_type=jnp.float32
-    )
-    grad_up_w = jnp.einsum(
-        "td,tf->df", normed_two_low, grad_up_low, preferred_element_type=jnp.float32
-    )
-    grads_gate_up = scatter_weights([grad_gate_w, grad_up_w], devices_all, CHUNKS[1])
-    grad_normed_two = restored(
-        jnp.einsum("tf,df->td", grad_gate_low, gate_weight, preferred_element_type=jnp.float32)
-        + jnp.einsum("tf,df->td", grad_up_low, up_weight, preferred_element_type=jnp.float32)
-    )
-    grad_middle_norm, grad_gain_ffin = back_ffin(grad_normed_two)
-    grad_middle = grad_out + grad_middle_norm
+    if order is None:
+        outputs, grad_middle, grad_gain_ffin, grad_gain_ffout, grads_ffn = ffn_plain(
+            middle, cotangent, norm_ffin, norm_ffout, *ffn_weights
+        )
+        grads_ffn = scatter_plain(grads_ffn)
+    else:
+        outputs, grad_middle, grad_gain_ffin, grad_gain_ffout, grads_gate_up, grads_down = (
+            ffn_blocks(
+                pieces,
+                middle,
+                cotangent,
+                norm_ffin,
+                norm_ffout,
+                order.astype(jnp.bfloat16),
+                *ffn_weights,
+            )
+        )
+        grads_ffn = jnp.concatenate(
+            [
+                scatter_blocks(pieces[4:6], *grads_gate_up),
+                scatter_blocks(pieces[6:7], *grads_down),
+            ]
+        )
     grad_attn, grad_gain_attn = back_attn(grad_middle)
     grad_attn_low = grad_attn.astype(jnp.bfloat16)
     grad_out_w = jnp.einsum(
@@ -530,9 +737,11 @@
     grad_value_w = jnp.einsum(
         "td,te->de", normed_low, grad_value_low, preferred_element_type=jnp.float32
     )
-    grads_attn = scatter_weights(
-        [grad_query_w, grad_key_w, grad_value_w, grad_out_w], devices_all, CHUNKS[0]
-    )
+    grads_attn = [grad_query_w, grad_key_w, grad_value_w, grad_out_w]
+    if order is None:
+        grads_attn = scatter_plain(grads_attn)
+    else:
+        grads_attn = scatter_blocks(pieces[:4], *split(pieces[:4], grads_attn))
     grad_normed = restored(
         jnp.einsum("te,de->td", grad_query_low, query_weight, preferred_element_type=jnp.float32)
         + jnp.einsum("te,de->td", grad_key_low, key_weight, preferred_element_type=jnp.float32)
@@ -540,7 +749,7 @@
     )
     grad_input_norm, grad_gain_input = back_input(grad_normed)
     grad_inputs = grad_middle + grad_input_norm
-    grads_local = jnp.concatenate([grads_attn, grads_gate_up, grads_down], axis=0)
+    grads_local = jnp.concatenate([grads_attn, grads_ffn], axis=0)
     gain_grads = sum_gains(
         jnp.concatenate(
             [
@@ -561,7 +770,7 @@
         gain_grads, gain_first, gain_second, gains, gain_rate, 0.0
     )
     return (
-        outputs.astype(jnp.bfloat16),
+        outputs,
         grad_inputs.astype(jnp.bfloat16),
         moment_first,
         moment_second,

time: 277 us -> 252 us (0.910)
  matrix products: 41.1 us -> 24.1 us
  Pallas kernels: 42 us -> 37.7 us
    dot_general x6 -> x0, matrix products: 10.8 us -> none  [the longest x1 2.59 us: shards(): jnp.einsum('td,tf->df', normed_two_low, grad_up_low, preferred_element_ty...]
    ppermute x53, waiting for transfers between devices: 59.9 us -> 55.4 us  [swap(): lax.ppermute(value, ALL_AXES, [(source, source ^ mask) for source in rang...]
    dot_general x9 -> x5, matrix products: 8.25 us -> 3.82 us  [matmul(): return jnp.dot(left_side, right_side, preferred_element_type=jnp.float32)]
    pallas_call x12 -> x9, Pallas kernels: 42 us -> 37.7 us  [local_call(): pl.pallas_call(kernel, out_shape=outs, in_specs=specs, out_specs=tuple((p...]
    unnamed x221 -> x141, local copies, waits for them, and re-layouts: 16.3 us -> 14.5 us
  transfers between devices with their start and end apart: 59 -> 59, of which waited for: 18 -> 19; matrix products, arithmetic and copies ran while one was open for 15% -> 18% of each run, Pallas kernels for 13% -> 9%
where the time goes in v3:
time: 252 us; the launch traced here: 251 us
  starting transfers between devices  78.5 us (31%)
  waiting for transfers between devices  60.4 us (24%)
  Pallas kernels  37.7 us (15%)
  local copies, waits for them, and re-layouts  25.2 us (10%)
  matrix products  24.1 us (10%)
  other arithmetic  23.3 us (9%)
    ppermute x53, starting transfers between devices, swap(): lax.ppermute(value, ALL_AXES, [(source, source ^ mask) for source in rang...  66.7 us
    ppermute x53, waiting for transfers between devices, swap(): lax.ppermute(value, ALL_AXES, [(source, source ^ mask) for source in rang...  55.4 us
    pallas_call x9, Pallas kernels, local_call(): pl.pallas_call(kernel, out_shape=outs, in_specs=specs, out_specs=tuple((p...  37.7 us
    unnamed x141, local copies, waits for them, and re-layouts  14.5 us
    ppermute x6, starting transfers between devices, shifted(): lax.ppermute(value, axis, [(source, source + steps) for source in range(i...  11.8 us
  transfers between devices with their start and end apart: 59, of which 19 were waited for; matrix products, arithmetic and copies ran while one was open for 18% of the time, Pallas kernels for 9%

profile of v3, /device:TPU:0, one launch (start us, length us, event | category | flops | bytes accessed | tf_op | source)
XLA Modules:
  0.0 251.0 jit_solution(13947638065141566845)
XLA Ops:
  1.9 3.1 %collective-permute-start = (bf16[400,128]{1,0:T(8,128)(2,1)S(1)}, bf16[400,128]{1,0:T(8,128)(2,1)S(1)}, u32[]{:S(2)}, u32[]{:S(2)}) collective-permute-start(bf16[400,128]{1,0:T(8,128)(2,1)S(1)} %slice.275.refs_0_), channel_id=1, source_target_pairs={{0,8},{1,9},{2,10},{3,11},{4,12},{5,13},{6,14},{7,15},{8,0},{9,1},... | collective-permute-start | bytes 307208 | tf_op jit(solution)/shard_map/ppermute | solution.py:126
  5.0 2.6 %collective-permute-start.1 = (bf16[400,128]{1,0:T(8,128)(2,1)S(1)}, bf16[400,128]{1,0:T(8,128)(2,1)S(1)}, u32[]{:S(2)}, u32[]{:S(2)}) collective-permute-start(bf16[400,128]{1,0:T(8,128)(2,1)S(1)} %slice.275.refs_0_), channel_id=1, source_target_pairs={{0,16},{1,17},{2,18},{3,19},{4,20},{5,21},{6,22},{7,23},{8,24},{9,... | collective-permute-start | bytes 307208 | tf_op jit(solution)/shard_map/ppermute | solution.py:126
  8.1 3.9 %collective-permute-start.21 = (bf16[320,128]{1,0:T(8,128)(2,1)S(1)}, bf16[320,128]{1,0:T(8,128)(2,1)S(1)}, u32[]{:S(2)}, u32[]{:S(2)}) collective-permute-start(bf16[320,128]{1,0:T(8,128)(2,1)S(1)} %slice.287.refs_0_), channel_id=1, source_target_pairs={{0,24},{1,25},{2,26},{3,27},{4,28},{5,29},{6,30},{7,31},{8,16},{9,... | collective-permute-start | bytes 245768 | tf_op jit(solution)/shard_map/ppermute | solution.py:126
  19.0 4.3 %collective-permute-start.12 = (bf16[640,128]{1,0:T(8,128)(2,1)S(1)}, bf16[640,128]{1,0:T(8,128)(2,1)S(1)}, u32[]{:S(2)}, u32[]{:S(2)}) collective-permute-start(bf16[640,128]{1,0:T(8,128)(2,1)S(1)} %slice.284.refs_0_), channel_id=1, source_target_pairs={{0,16},{1,17},{2,18},{3,19},{4,20},{5,21},{6,22},{7,23},{8,24},{9,... | collective-permute-start | bytes 491528 | tf_op jit(solution)/shard_map/ppermute | solution.py:126
  34.0 2.3 collective-permute-done.12.refs_2_
  38.5 2.5 %shard_map.154 = bf16[2560,128]{1,0:T(8,128)(2,1)} custom-call(s32[1]{0:T(128)} %bitcast.index_ref, bf16[640,128]{1,0:T(8,128)(2,1)} %copy-done.22, bf16[640,128]{1,0:T(8,128)(2,1)} %copy-done.33, bf16[640,128]{1,0:T(8,128)(2,1)} %copy-done.34, bf16[640,128]{1,0:T(8,128)(2,1)} %copy-done.35), custom_call_target="tpu_custom_call" | custom-call | bytes 1310720 | tf_op jit(solution)/shard_map/pallas_call | solution.py:133
  51.6 14.0 %collective-permute-done.5 = bf16[800,128]{1,0:T(8,128)(2,1)S(1)} collective-permute-done((bf16[800,128]{1,0:T(8,128)(2,1)S(1)}, bf16[800,128]{1,0:T(8,128)(2,1)S(1)}, u32[]{:S(2)}, u32[]{:S(2)}) %collective-permute-start.5) | collective-permute-done | bytes 204832 | tf_op jit(solution)/shard_map/ppermute | solution.py:126
  76.5 5.2 %collective-permute-done.16 = bf16[1280,128]{1,0:T(8,128)(2,1)S(1)} collective-permute-done((bf16[1280,128]{1,0:T(8,128)(2,1)S(1)}, bf16[1280,128]{1,0:T(8,128)(2,1)S(1)}, u32[]{:S(2)}, u32[]{:S(2)}) %collective-permute-start.16) | collective-permute-done | bytes 327712 | tf_op jit(solution)/shard_map/ppermute | solution.py:126
  85.1 4.3 %shard_map.153 = (bf16[640,1024]{1,0:T(8,128)(2,1)}, bf16[640,256]{1,0:T(8,128)(2,1)}, bf16[640,256]{1,0:T(8,128)(2,1)}, bf16[1024,640]{1,0:T(8,128)(2,1)}) custom-call(s32[1]{0:T(128)} %bitcast.index_ref, bf16[6400,128]{1,0:T(8,128)(2,1)} %copy-done.7, bf16[6400,128]{1,0:T(8,128)(2,1)} %copy-done.12), custom_call_target="tpu_custom_call" | custom-call | bytes 6553600 | tf_op jit(solution)/shard_map/pallas_call | solution.py:133
  92.4 2.4 collective-permute-start.10
  94.9 3.1 %collective-permute-start.8 = (bf16[128,512]{1,0:T(8,128)(2,1)S(1)}, bf16[128,512]{1,0:T(8,128)(2,1)}, u32[]{:S(2)}, u32[]{:S(2)}) collective-permute-start(bf16[128,512]{1,0:T(8,128)(2,1)S(1)} %pad_maximum_fusion.11), channel_id=1, source_target_pairs={{0,3},{4,7},{8,11},{12,15},{16,19},{20,23},{24,27},{28,31}} | collective-permute-start | bytes 393224 | tf_op jit(solution)/shard_map/ppermute | solution.py:33
  97.9 2.3 collective-permute-start.9
  106.6 14.7 %shard_map.156 = (bf16[128,640]{1,0:T(8,128)(2,1)}, f32[128,640]{1,0:T(8,128)}, f32[1,640]{1,0:T(1,128)}, f32[1,640]{1,0:T(1,128)}, bf16[10240,128]{1,0:T(8,128)...) custom-call(s32[1]{0:T(128)} %bitcast.index_ref, ...), custom_call_target="tpu_custom_call" | custom-call | flops 3019898880 | bytes 17541120 | tf_op jit(solution)/shard_map/pallas_call | solution.py:133
  126.5 2.2 convolution_bitcast_fusion
  129.9 3.1 %convolution_bitcast_fusion.3 = f32[128,4,256]{2,0,1:T(8,128)} fusion(f32[4,128,512]{1,2,0:T(8,128)} %convolution_bitcast_fusion, f32[4,128,512]{1,2,0:T(8,128)S(1)} %get-tuple-element.120, f32[4,128]{1,0:T(4,128)S(1)} %log_add_fusion, bf16[512,512]{1,0:T(8,128)(2,1)} %copy-done.11), kind=kOutput, calls=%fused_computation.22 | convolution fusion | flops 136053760 | bytes 4984832 | tf_op jit(solution)/shard_map/hqk,kd->qhd/dot_general | solution.py:709
  132.9 3.0 %convolution_bitcast_fusion.2 = f32[512,256]{1,0:T(8,128)} fusion(f32[4,128,512]{1,2,0:T(8,128)} %convolution_bitcast_fusion, f32[4,128,512]{1,2,0:T(8,128)S(1)} %get-tuple-element.120, f32[4,128]{1,0:T(4,128)S(1)} %log_add_fusion, bf16[128,4,128]{2,0,1:T(8,128)(2,1)} %copy-done.38, bf16[128,4,128]{2,0,1:T(8,128)(2,1)} %copy-done.37), kind=kOutput, calls=%fused_computation.21 | convolution fusion | flops 136578048 | bytes 2885632 | tf_op jit(solution)/shard_map/hqk,qhd->kd/dot_general | solution.py:712
  136.0 2.6 %convolution_convert_fusion.refs_3_ = bf16[1024,640]{1,0:T(8,128)(2,1)} fusion(bf16[128,1024]{0,1:T(8,128)(2,1)S(1)} %bitcast.98, bf16[128,640]{1,0:T(8,128)(2,1)} %copy-done.16), kind=kOutput, calls=%fused_computation.7 | convolution fusion | flops 168427520 | bytes 1736704 | tf_op jit(solution)/shard_map/to,td->od/dot_general | solution.py:688
  148.2 2.2 collective-permute-done.28
  165.3 4.2 %shard_map.157 = (bf16[6400,128]{1,0:T(8,128)(2,1)}, bf16[6400,128]{1,0:T(8,128)(2,1)}) custom-call(s32[1]{0:T(128)} %bitcast.index_ref, bf16[640,1024]{1,0:T(8,128)(2,1)} %convolution_convert_fusion.1.refs_0_, bf16[640,256]{1,0:T(8,128)(2,1)} %convolution_convert_fusion.3.refs_1_, bf16[640,256]{1,0:T(8,128)(2,1)} %convolution_convert_fusion.2.refs_2_, ...), custom_call_target="tpu_custom_call" | custom-call | bytes 6553600 | tf_op jit(solution)/shard_map/pallas_call | solution.py:133
  173.3 2.3 collective-permute-start.58
  181.4 9.3 %collective-permute-done.31 = bf16[800,128]{1,0:T(8,128)(2,1)S(1)} collective-permute-done((bf16[800,128]{1,0:T(8,128)(2,1)S(1)}, bf16[800,128]{1,0:T(8,128)(2,1)S(1)}, u32[]{:S(2)}, u32[]{:S(2)}) %collective-permute-start.31) | collective-permute-done | bytes 204832 | tf_op jit(solution)/shard_map/ppermute | solution.py:126
  196.8 3.8 %collective-permute-done.39 = bf16[1280,128]{1,0:T(8,128)(2,1)S(1)} collective-permute-done((bf16[1280,128]{1,0:T(8,128)(2,1)S(1)}, bf16[1280,128]{1,0:T(8,128)(2,1)S(1)}, u32[]{:S(2)}, u32[]{:S(2)}) %collective-permute-start.39) | collective-permute-done | bytes 327712 | tf_op jit(solution)/shard_map/ppermute | solution.py:126
  202.0 3.6 %collective-permute-done.41 = bf16[1280,128]{1,0:T(8,128)(2,1)S(1)} collective-permute-done((bf16[1280,128]{1,0:T(8,128)(2,1)S(1)}, bf16[1280,128]{1,0:T(8,128)(2,1)S(1)}, u32[]{:S(2)}, u32[]{:S(2)}) %collective-permute-start.41) | collective-permute-done | bytes 327712 | tf_op jit(solution)/shard_map/ppermute | solution.py:126
  211.0 2.2 shard_map.160
  214.4 2.7 %collective-permute-start.52 = (bf16[320,128]{1,0:T(8,128)(2,1)}, bf16[320,128]{1,0:T(8,128)(2,1)S(1)}, u32[]{:S(2)}, u32[]{:S(2)}) collective-permute-start(bf16[320,128]{1,0:T(8,128)(2,1)} %get-tuple-element.56), channel_id=1, source_target_pairs={{0,16},{1,17},{2,18},{3,19},{4,20},{5,21},{6,22},{7,23},{8,24},{9,... | collective-permute-start | bytes 245768 | tf_op jit(solution)/shard_map/ppermute | solution.py:126
  218.3 3.3 %collective-permute-start.53 = (bf16[320,128]{1,0:T(8,128)(2,1)}, bf16[320,128]{1,0:T(8,128)(2,1)S(1)}, u32[]{:S(2)}, u32[]{:S(2)}) collective-permute-start(bf16[320,128]{1,0:T(8,128)(2,1)} %get-tuple-element.57), channel_id=1, source_target_pairs={{0,24},{1,25},{2,26},{3,27},{4,28},{5,29},{6,30},{7,31},{8,16},{9,... | collective-permute-start | bytes 245768 | tf_op jit(solution)/shard_map/ppermute | solution.py:126
  224.4 2.4 shard_map.158
  227.8 3.3 %collective-permute-start.37 = (bf16[400,128]{1,0:T(8,128)(2,1)}, bf16[400,128]{1,0:T(8,128)(2,1)S(1)}, u32[]{:S(2)}, u32[]{:S(2)}) collective-permute-start(bf16[400,128]{1,0:T(8,128)(2,1)} %get-tuple-element.45), channel_id=1, source_target_pairs={{0,24},{1,25},{2,26},{3,27},{4,28},{5,29},{6,30},{7,31},{8,16},{9,... | collective-permute-start | bytes 307208 | tf_op jit(solution)/shard_map/ppermute | solution.py:126
  233.2 3.6 %shard_map.159 = (f32[640,128]{1,0:T(8,128)}, bf16[640,128]{1,0:T(8,128)(2,1)}, bf16[640,128]{1,0:T(8,128)(2,1)}, bf16[640,128]{1,0:T(8,128)(2,1)}) custom-call(s32[1]{0:T(128)} %bitcast.index_ref, f32[2560,128]{1,0:T(8,128)} %slice.303.refs_0_, bf16[2560,128]{1,0:T(8,128)(2,1)} %collective-permute-done.40.refs_1_, bf16[2560,128]{1,0:T(8,128)(2,1)} %copy-done.23), custom_call_target="tpu_custom_call" | custom-call | bytes 3440640 | tf_op jit(solution)/shard_map/pallas_call | solution.py:133
  237.9 3.3 %collective-permute-start.45 = (bf16[640,128]{1,0:T(8,128)(2,1)}, bf16[640,128]{1,0:T(8,128)(2,1)S(1)}, u32[]{:S(2)}, u32[]{:S(2)}) collective-permute-start(bf16[640,128]{1,0:T(8,128)(2,1)} %get-tuple-element.51), channel_id=1, source_target_pairs={{0,24},{1,25},{2,26},{3,27},{4,28},{5,29},{6,30},{7,31},{8,16},{9,... | collective-permute-start | bytes 491528 | tf_op jit(solution)/shard_map/ppermute | solution.py:126
  241.3 2.5 collective-permute-done.43
  243.8 4.5 %collective-permute-done.44 = bf16[640,128]{1,0:T(8,128)(2,1)S(1)} collective-permute-done((bf16[640,128]{1,0:T(8,128)(2,1)}, bf16[640,128]{1,0:T(8,128)(2,1)S(1)}, u32[]{:S(2)}, u32[]{:S(2)}) %collective-permute-start.44) | collective-permute-done | bytes 163872 | tf_op jit(solution)/shard_map/ppermute | solution.py:126
  (354 shorter events, 120.4 us)
Async XLA Ops:
  1.9 25.0 %collective-permute-start = (bf16[400,128]{1,0:T(8,128)(2,1)S(1)}, bf16[400,128]{1,0:T(8,128)(2,1)S(1)}, u32[]{:S(2)}, u32[]{:S(2)}) collective-permute-start(bf16[400,128]{1,0:T(8,128)(2,1)S(1)} %slice.275.refs_0_), channel_id=1, source_target_pairs={{0,8},{1,9},{2,10},{3,11},{4,12},{5,13},{6,14},{7,15},{8,0},{9,1},... | collective-permute-start | bytes 307208 | tf_op jit(solution)/shard_map/ppermute | solution.py:126
  5.0 22.4 %collective-permute-start.1 = (bf16[400,128]{1,0:T(8,128)(2,1)S(1)}, bf16[400,128]{1,0:T(8,128)(2,1)S(1)}, u32[]{:S(2)}, u32[]{:S(2)}) collective-permute-start(bf16[400,128]{1,0:T(8,128)(2,1)S(1)} %slice.275.refs_0_), channel_id=1, source_target_pairs={{0,16},{1,17},{2,18},{3,19},{4,20},{5,21},{6,22},{7,23},{8,24},{9,... | collective-permute-start | bytes 307208 | tf_op jit(solution)/shard_map/ppermute | solution.py:126
  7.6 11.3 %collective-permute-start.19 = (bf16[320,128]{1,0:T(8,128)(2,1)S(1)}, bf16[320,128]{1,0:T(8,128)(2,1)S(1)}, u32[]{:S(2)}, u32[]{:S(2)}) collective-permute-start(bf16[320,128]{1,0:T(8,128)(2,1)S(1)} %slice.287.refs_0_), channel_id=1, source_target_pairs={{0,8},{1,9},{2,10},{3,11},{4,12},{5,13},{6,14},{7,15},{8,0},{9,1},... | collective-permute-start | bytes 245768 | tf_op jit(solution)/shard_map/ppermute | solution.py:126
  18.9 14.4 %collective-permute-start.11 = (bf16[640,128]{1,0:T(8,128)(2,1)S(1)}, bf16[640,128]{1,0:T(8,128)(2,1)S(1)}, u32[]{:S(2)}, u32[]{:S(2)}) collective-permute-start(bf16[640,128]{1,0:T(8,128)(2,1)S(1)} %slice.284.refs_0_), channel_id=1, source_target_pairs={{0,8},{1,9},{2,10},{3,11},{4,12},{5,13},{6,14},{7,15},{8,0},{9,1},... | collective-permute-start | bytes 491528 | tf_op jit(solution)/shard_map/ppermute | solution.py:126
  19.0 17.2 %collective-permute-start.12 = (bf16[640,128]{1,0:T(8,128)(2,1)S(1)}, bf16[640,128]{1,0:T(8,128)(2,1)S(1)}, u32[]{:S(2)}, u32[]{:S(2)}) collective-permute-start(bf16[640,128]{1,0:T(8,128)(2,1)S(1)} %slice.284.refs_0_), channel_id=1, source_target_pairs={{0,16},{1,17},{2,18},{3,19},{4,20},{5,21},{6,22},{7,23},{8,24},{9,... | collective-permute-start | bytes 491528 | tf_op jit(solution)/shard_map/ppermute | solution.py:126
  27.4 17.8 %collective-permute-start.22 = (bf16[1280,128]{1,0:T(8,128)(2,1)}, bf16[1280,128]{1,0:T(8,128)(2,1)S(1)}, u32[]{:S(2)}, u32[]{:S(2)}) collective-permute-start(bf16[1280,128]{1,0:T(8,128)(2,1)} %shard_map.155), channel_id=1, source_target_pairs={{0,4},{1,5},{2,6},{3,7},{4,0},{5,1},{6,2},{7,3},{8,12},{9,13},{10,... | collective-permute-start | bytes 983048 | tf_op jit(solution)/shard_map/ppermute | solution.py:126
  28.9 15.6 %collective-permute-start.23 = (bf16[1280,128]{1,0:T(8,128)(2,1)}, bf16[1280,128]{1,0:T(8,128)(2,1)S(1)}, u32[]{:S(2)}, u32[]{:S(2)}) collective-permute-start(bf16[1280,128]{1,0:T(8,128)(2,1)} %shard_map.155), channel_id=1, source_target_pairs={{0,2},{1,3},{2,0},{3,1},{4,6},{5,7},{6,4},{7,5},{8,10},{9,11},{10,... | collective-permute-start | bytes 983048 | tf_op jit(solution)/shard_map/ppermute | solution.py:126
  33.4 16.4 %collective-permute-start.3 = (bf16[1600,128]{1,0:T(8,128)(2,1)}, bf16[1600,128]{1,0:T(8,128)(2,1)S(1)}, u32[]{:S(2)}, u32[]{:S(2)}) collective-permute-start(bf16[1600,128]{1,0:T(8,128)(2,1)} %shard_map.152), channel_id=1, source_target_pairs={{0,4},{1,5},{2,6},{3,7},{4,0},{5,1},{6,2},{7,3},{8,12},{9,13},{10,... | collective-permute-start | bytes 1228808 | tf_op jit(solution)/shard_map/ppermute | solution.py:126
  36.3 11.8 %collective-permute-start.4 = (bf16[1600,128]{1,0:T(8,128)(2,1)}, bf16[1600,128]{1,0:T(8,128)(2,1)S(1)}, u32[]{:S(2)}, u32[]{:S(2)}) collective-permute-start(bf16[1600,128]{1,0:T(8,128)(2,1)} %shard_map.152), channel_id=1, source_target_pairs={{0,2},{1,3},{2,0},{3,1},{4,6},{5,7},{6,4},{7,5},{8,10},{9,11},{10,... | collective-permute-start | bytes 1228808 | tf_op jit(solution)/shard_map/ppermute | solution.py:126
  41.0 32.2 %collective-permute-start.14 = (bf16[2560,128]{1,0:T(8,128)(2,1)}, bf16[2560,128]{1,0:T(8,128)(2,1)S(1)}, u32[]{:S(2)}, u32[]{:S(2)}) collective-permute-start(bf16[2560,128]{1,0:T(8,128)(2,1)} %shard_map.154), channel_id=1, source_target_pairs={{0,4},{1,5},{2,6},{3,7},{4,0},{5,1},{6,2},{7,3},{8,12},{9,13},{10,... | collective-permute-start | bytes 1966088 | tf_op jit(solution)/shard_map/ppermute | solution.py:126
  44.5 27.1 %collective-permute-start.15 = (bf16[2560,128]{1,0:T(8,128)(2,1)}, bf16[2560,128]{1,0:T(8,128)(2,1)S(1)}, u32[]{:S(2)}, u32[]{:S(2)}) collective-permute-start(bf16[2560,128]{1,0:T(8,128)(2,1)} %shard_map.154), channel_id=1, source_target_pairs={{0,2},{1,3},{2,0},{3,1},{4,6},{5,7},{6,4},{7,5},{8,10},{9,11},{10,... | collective-permute-start | bytes 1966088 | tf_op jit(solution)/shard_map/ppermute | solution.py:126
  45.2 22.9 %collective-permute-start.24 = (bf16[640,128]{1,0:T(8,128)(2,1)S(1)}, bf16[640,128]{1,0:T(8,128)(2,1)S(1)}, u32[]{:S(2)}, u32[]{:S(2)}) collective-permute-start(bf16[640,128]{1,0:T(8,128)(2,1)S(1)} %slice.288), channel_id=1, source_target_pairs={{0,4},{1,5},{2,6},{3,7},{4,0},{5,1},{6,2},{7,3},{8,12},{9,13},{10,... | collective-permute-start | bytes 491528 | tf_op jit(solution)/shard_map/ppermute | solution.py:126
  48.1 17.4 %collective-permute-start.5 = (bf16[800,128]{1,0:T(8,128)(2,1)S(1)}, bf16[800,128]{1,0:T(8,128)(2,1)S(1)}, u32[]{:S(2)}, u32[]{:S(2)}) collective-permute-start(bf16[800,128]{1,0:T(8,128)(2,1)S(1)} %slice.276), channel_id=1, source_target_pairs={{0,4},{1,5},{2,6},{3,7},{4,0},{5,1},{6,2},{7,3},{8,12},{9,13},{10,... | collective-permute-start | bytes 614408 | tf_op jit(solution)/shard_map/ppermute | solution.py:126
  49.9 17.3 %collective-permute-start.6 = (bf16[800,128]{1,0:T(8,128)(2,1)S(1)}, bf16[800,128]{1,0:T(8,128)(2,1)S(1)}, u32[]{:S(2)}, u32[]{:S(2)}) collective-permute-start(bf16[800,128]{1,0:T(8,128)(2,1)S(1)} %slice.277), channel_id=1, source_target_pairs={{0,2},{1,3},{2,0},{3,1},{4,6},{5,7},{6,4},{7,5},{8,10},{9,11},{10,... | collective-permute-start | bytes 614408 | tf_op jit(solution)/shard_map/ppermute | solution.py:126
  67.2 16.7 %collective-permute-start.7 = (bf16[6400,128]{1,0:T(8,128)(2,1)S(1)}, bf16[6400,128]{1,0:T(8,128)(2,1)S(1)}, u32[]{:S(2)}, u32[]{:S(2)}) collective-permute-start(bf16[6400,128]{1,0:T(8,128)(2,1)S(1)} %constant_dynamic-update-slice_fusion.near_ref), channel_id=1, source_target_pairs={{0,1},{1,0},{2,3},{3,2},{4,5},{5,4},{6,7},{7,6},{8,9},{9,8},{10,11... | collective-permute-start | bytes 4915208 | tf_op jit(solution)/shard_map/ppermute | solution.py:126
  71.6 35.0 %collective-permute-start.26 = (bf16[5120,128]{1,0:T(8,128)(2,1)}, bf16[5120,128]{1,0:T(8,128)(2,1)}, u32[]{:S(2)}, u32[]{:S(2)}) collective-permute-start(bf16[5120,128]{1,0:T(8,128)(2,1)} %constant_dynamic-update-slice_fusion.10.near_down_ref), channel_id=1, source_target_pairs={{0,1},{1,0},{2,3},{3,2},{4,5},{5,4},{6,7},{7,6},{8,9},{9,8},{10,11... | collective-permute-start | bytes 3932168 | tf_op jit(solution)/shard_map/ppermute | solution.py:126
  83.9 22.7 %collective-permute-start.18 = (bf16[10240,128]{1,0:T(8,128)(2,1)}, bf16[10240,128]{1,0:T(8,128)(2,1)}, u32[]{:S(2)}, u32[]{:S(2)}) collective-permute-start(bf16[10240,128]{1,0:T(8,128)(2,1)} %constant_dynamic-update-slice_fusion.5.near_ref), channel_id=1, source_target_pairs={{0,1},{1,0},{2,3},{3,2},{4,5},{5,4},{6,7},{7,6},{8,9},{9,8},{10,11... | collective-permute-start | bytes 7864328 | tf_op jit(solution)/shard_map/ppermute | solution.py:126
  147.0 23.5 %collective-permute-start.46 = (bf16[5120,128]{1,0:T(8,128)(2,1)}, bf16[5120,128]{1,0:T(8,128)(2,1)S(1)}, u32[]{:S(2)}, u32[]{:S(2)}) collective-permute-start(bf16[5120,128]{1,0:T(8,128)(2,1)} %get-tuple-element.53), channel_id=1, source_target_pairs={{0,1},{1,0},{2,3},{3,2},{4,5},{5,4},{6,7},{7,6},{8,9},{9,8},{10,11... | collective-permute-start | bytes 3932168 | tf_op jit(solution)/shard_map/ppermute | solution.py:126
  159.2 32.8 %collective-permute-start.38 = (bf16[10240,128]{1,0:T(8,128)(2,1)}, bf16[10240,128]{1,0:T(8,128)(2,1)S(1)}, u32[]{:S(2)}, u32[]{:S(2)}) collective-permute-start(bf16[10240,128]{1,0:T(8,128)(2,1)} %get-tuple-element.47), channel_id=1, source_target_pairs={{0,1},{1,0},{2,3},{3,2},{4,5},{5,4},{6,7},{7,6},{8,9},{9,8},{10,11... | collective-permute-start | bytes 7864328 | tf_op jit(solution)/shard_map/ppermute | solution.py:126
  173.3 39.9 %collective-permute-start.58 = (f32[24,128]{1,0:T(8,128)S(1)}, f32[24,128]{1,0:T(8,128)S(1)}, u32[]{:S(2)}, u32[]{:S(2)}) collective-permute-start(f32[24,128]{1,0:T(8,128)S(1)} %add.359), channel_id=1, source_target_pairs={{0,16},{1,17},{2,18},{3,19},{4,20},{5,21},{6,22},{7,23},{8,24},{9,... | collective-permute-start | bytes 36872 | tf_op jit(solution)/shard_map/ppermute | solution.py:126
  177.6 29.3 %collective-permute-start.50 = (bf16[1280,128]{1,0:T(8,128)(2,1)S(1)}, bf16[1280,128]{1,0:T(8,128)(2,1)S(1)}, u32[]{:S(2)}, u32[]{:S(2)}) collective-permute-start(bf16[1280,128]{1,0:T(8,128)(2,1)S(1)} %pad_maximum_fusion.7), channel_id=1, source_target_pairs={{0,2},{1,3},{2,0},{3,1},{4,6},{5,7},{6,4},{7,5},{8,10},{9,11},{10,... | collective-permute-start | bytes 983048 | tf_op jit(solution)/shard_map/ppermute | solution.py:126
  180.3 11.6 %collective-permute-start.33 = (bf16[800,128]{1,0:T(8,128)(2,1)S(1)}, bf16[800,128]{1,0:T(8,128)(2,1)S(1)}, u32[]{:S(2)}, u32[]{:S(2)}) collective-permute-start(bf16[800,128]{1,0:T(8,128)(2,1)S(1)} %get-tuple-element.90), channel_id=1, source_target_pairs={{0,4},{1,5},{2,6},{3,7},{4,0},{5,1},{6,2},{7,3},{8,12},{9,13},{10,... | collective-permute-start | bytes 614408 | tf_op jit(solution)/shard_map/ppermute | solution.py:126
  190.8 17.6 %collective-permute-start.48 = (bf16[1280,128]{1,0:T(8,128)(2,1)S(1)}, bf16[1280,128]{1,0:T(8,128)(2,1)S(1)}, u32[]{:S(2)}, u32[]{:S(2)}) collective-permute-start(bf16[1280,128]{1,0:T(8,128)(2,1)S(1)} %pad_maximum_fusion.6), channel_id=1, source_target_pairs={{0,4},{1,5},{2,6},{3,7},{4,0},{5,1},{6,2},{7,3},{8,12},{9,13},{10,... | collective-permute-start | bytes 983048 | tf_op jit(solution)/shard_map/ppermute | solution.py:126
  200.5 13.8 %collective-permute-start.34 = (bf16[1600,128]{1,0:T(8,128)(2,1)}, bf16[1600,128]{1,0:T(8,128)(2,1)}, u32[]{:S(2)}, u32[]{:S(2)}) collective-permute-start(bf16[1600,128]{1,0:T(8,128)(2,1)} %pad_maximum_fusion.5), channel_id=1, source_target_pairs={{0,2},{1,3},{2,0},{3,1},{4,6},{5,7},{6,4},{7,5},{8,10},{9,11},{10,... | collective-permute-start | bytes 1228808 | tf_op jit(solution)/shard_map/ppermute | solution.py:126
  205.5 12.7 %collective-permute-start.32 = (bf16[1600,128]{1,0:T(8,128)(2,1)}, bf16[1600,128]{1,0:T(8,128)(2,1)}, u32[]{:S(2)}, u32[]{:S(2)}) collective-permute-start(bf16[1600,128]{1,0:T(8,128)(2,1)} %pad_maximum_fusion.4), channel_id=1, source_target_pairs={{0,4},{1,5},{2,6},{3,7},{4,0},{5,1},{6,2},{7,3},{8,12},{9,13},{10,... | collective-permute-start | bytes 1228808 | tf_op jit(solution)/shard_map/ppermute | solution.py:126
  206.9 25.5 %collective-permute-start.42 = (bf16[2560,128]{1,0:T(8,128)(2,1)S(1)}, bf16[2560,128]{1,0:T(8,128)(2,1)S(1)}, u32[]{:S(2)}, u32[]{:S(2)}) collective-permute-start(bf16[2560,128]{1,0:T(8,128)(2,1)S(1)} %pad_maximum_fusion.3), channel_id=1, source_target_pairs={{0,2},{1,3},{2,0},{3,1},{4,6},{5,7},{6,4},{7,5},{8,10},{9,11},{10,... | collective-permute-start | bytes 1966088 | tf_op jit(solution)/shard_map/ppermute | solution.py:126
  208.4 24.0 %collective-permute-start.40 = (bf16[2560,128]{1,0:T(8,128)(2,1)S(1)}, bf16[2560,128]{1,0:T(8,128)(2,1)}, u32[]{:S(2)}, u32[]{:S(2)}) collective-permute-start(bf16[2560,128]{1,0:T(8,128)(2,1)S(1)} %pad_maximum_fusion.2), channel_id=1, source_target_pairs={{0,4},{1,5},{2,6},{3,7},{4,0},{5,1},{6,2},{7,3},{8,12},{9,13},{10,... | collective-permute-start | bytes 1966088 | tf_op jit(solution)/shard_map/ppermute | solution.py:126
  213.2 13.6 %collective-permute-start.51 = (bf16[320,128]{1,0:T(8,128)(2,1)}, bf16[320,128]{1,0:T(8,128)(2,1)S(1)}, u32[]{:S(2)}, u32[]{:S(2)}) collective-permute-start(bf16[320,128]{1,0:T(8,128)(2,1)} %get-tuple-element.55), channel_id=1, source_target_pairs={{0,8},{1,9},{2,10},{3,11},{4,12},{5,13},{6,14},{7,15},{8,0},{9,1},... | collective-permute-start | bytes 245768 | tf_op jit(solution)/shard_map/ppermute | solution.py:126
  214.4 12.6 %collective-permute-start.52 = (bf16[320,128]{1,0:T(8,128)(2,1)}, bf16[320,128]{1,0:T(8,128)(2,1)S(1)}, u32[]{:S(2)}, u32[]{:S(2)}) collective-permute-start(bf16[320,128]{1,0:T(8,128)(2,1)} %get-tuple-element.56), channel_id=1, source_target_pairs={{0,16},{1,17},{2,18},{3,19},{4,20},{5,21},{6,22},{7,23},{8,24},{9,... | collective-permute-start | bytes 245768 | tf_op jit(solution)/shard_map/ppermute | solution.py:126
  227.0 14.3 %collective-permute-start.36 = (bf16[400,128]{1,0:T(8,128)(2,1)}, bf16[400,128]{1,0:T(8,128)(2,1)S(1)}, u32[]{:S(2)}, u32[]{:S(2)}) collective-permute-start(bf16[400,128]{1,0:T(8,128)(2,1)} %get-tuple-element.44), channel_id=1, source_target_pairs={{0,16},{1,17},{2,18},{3,19},{4,20},{5,21},{6,22},{7,23},{8,24},{9,... | collective-permute-start | bytes 307208 | tf_op jit(solution)/shard_map/ppermute | solution.py:126
  227.8 13.4 %collective-permute-start.37 = (bf16[400,128]{1,0:T(8,128)(2,1)}, bf16[400,128]{1,0:T(8,128)(2,1)S(1)}, u32[]{:S(2)}, u32[]{:S(2)}) collective-permute-start(bf16[400,128]{1,0:T(8,128)(2,1)} %get-tuple-element.45), channel_id=1, source_target_pairs={{0,24},{1,25},{2,26},{3,27},{4,28},{5,29},{6,30},{7,31},{8,16},{9,... | collective-permute-start | bytes 307208 | tf_op jit(solution)/shard_map/ppermute | solution.py:126
  236.8 11.5 %collective-permute-start.44 = (bf16[640,128]{1,0:T(8,128)(2,1)}, bf16[640,128]{1,0:T(8,128)(2,1)S(1)}, u32[]{:S(2)}, u32[]{:S(2)}) collective-permute-start(bf16[640,128]{1,0:T(8,128)(2,1)} %get-tuple-element.50), channel_id=1, source_target_pairs={{0,16},{1,17},{2,18},{3,19},{4,20},{5,21},{6,22},{7,23},{8,24},{9,... | collective-permute-start | bytes 491528 | tf_op jit(solution)/shard_map/ppermute | solution.py:126
  (89 other events, 788.5 us)

commit v4 on v0

--- a/solution.py
+++ b/solution.py
@@ -1,6 +1,11 @@
+import functools
+import math
+
 import jax
 import jax.numpy as jnp
 from jax import lax
+from jax.experimental import pallas as pl
+from jax.experimental.pallas import tpu as pltpu
 from jax.sharding import PartitionSpec as P
 
 D = 640
@@ -9,6 +14,7 @@
 FF = 2048
 WINDOW = 512
 STEP = 10
+ALL_AXES = ("dp", "group")
 
 
 norm_eps = 1e-06
@@ -103,11 +109,742 @@
     return jnp.dot(left_side, right_side, preferred_element_type=jnp.float32)
 
 
+LOW_COUNT = 8
+LANES = 128
+LOW_MASKS = (0, 4, 2, 6, 1, 5, 3, 7)
+GELU_SCALE = (2.0 / math.pi) ** 0.5
+GELU_CUBE = 0.044715
+VMEM_BYTES = 56 * 1024 * 1024
+
+
+def aligned(device_count):
+    return device_count % LOW_COUNT == 0 and D % device_count == 0
+
+
+def swap(value, mask):
+    count = lax.axis_size(ALL_AXES)
+    return lax.ppermute(value, ALL_AXES, [(source, source ^ mask) for source in range(count)])
+
+
+def local_call(kernel, outs, operands, scratch=()):
+    specs = [pl.BlockSpec(memory_space=pltpu.SMEM)]
+    specs = specs + [pl.BlockSpec(memory_space=pltpu.VMEM)] * len(operands)
+    return pl.pallas_call(
+        kernel,
+        out_shape=outs,
+        in_specs=specs,
+        out_specs=tuple(pl.BlockSpec(memory_space=pltpu.VMEM) for _ in outs),
+        scratch_shapes=scratch,
+        compiler_params=pltpu.CompilerParams(vmem_limit_bytes=VMEM_BYTES),
+        cost_estimate=pl.CostEstimate(flops=0, bytes_accessed=0, transcendentals=0),
+    )(lax.axis_index(ALL_AXES).astype(jnp.int32).reshape(1), *operands)
+
+
+class Piece:
+    def __init__(self, rows, columns, device_count):
+        self.rows = rows
+        self.columns = columns
+        self.wide = rows == D
+        self.blocks = columns // LANES
+        self.own_rows = rows // device_count
+        self.flat_rows = self.own_rows * self.blocks
+        self.high_count = device_count // LOW_COUNT
+        self.block_rows = self.own_rows * self.high_count
+        self.size = self.block_rows * self.blocks
+
+
+def pack_kernel(pieces, later_count, index_ref, *refs):
+    high_count = pieces[0].high_count
+    parts, later = refs[:high_count], refs[high_count : high_count + later_count]
+    out_ref, later_outs = refs[high_count + later_count], refs[high_count + later_count + 1 : -2]
+    flat, packed = refs[-2:]
+    high = index_ref[0] // LOW_COUNT
+    for step, part in enumerate(parts):
+        flat[high ^ step] = part[...].astype(jnp.float32)
+    start, target = 0, 0
+    for piece in pieces:
+        for block in range(piece.blocks):
+            for place in range(high_count):
+                packed[pl.ds(target, piece.own_rows), :] = flat[
+                    place, pl.ds(start + block, piece.own_rows, stride=piece.blocks), :
+                ]
+                target = target + piece.own_rows
+        start = start + piece.flat_rows
+    out_ref[...] = packed[...].astype(jnp.bfloat16)
+    for ref, later_out in zip(later, later_outs):
+        later_out[...] = ref[...].astype(jnp.bfloat16)
+
+
+def unpack_kernel(pieces, extra_count, index_ref, *refs):
+    high_count = pieces[0].high_count
+    size = sum(piece.size for piece in pieces)
+    flat_rows = sum(piece.flat_rows for piece in pieces)
+    terms, outs, flat, packed = refs[:3], refs[-2 - high_count : -2], refs[-2], refs[-1]
+    high = index_ref[0] // LOW_COUNT
+    packed[...] = sum(term[:size, :].astype(jnp.float32) for term in terms)
+    start, source = 0, 0
+    for piece in pieces:
+        for block in range(piece.blocks):
+            for place in range(high_count):
+                flat[place, pl.ds(start + block, piece.own_rows, stride=piece.blocks), :] = packed[
+                    pl.ds(source, piece.own_rows), :
+                ]
+                source = source + piece.own_rows
+        start = start + piece.flat_rows
+    for step, out_ref in enumerate(outs):
+        out_ref[:flat_rows, :] = flat[high ^ step].astype(out_ref.dtype)
+        if extra_count:
+            extra = terms[2][size:, :].astype(jnp.float32) + refs[3][...].astype(jnp.float32)
+            out_ref[flat_rows:, :] = extra.astype(out_ref.dtype)
+
+
+def array(shape, kind):
+    return jax.ShapeDtypeStruct(shape, kind)
+
+
+def gather_blocks(pieces, rows, later=()):
+    high_count = pieces[0].high_count
+    size = sum(piece.size for piece in pieces)
+    parts = [rows] + [swap(rows, step * LOW_COUNT) for step in range(1, high_count)]
+    own, *later = local_call(
+        functools.partial(pack_kernel, pieces, len(later)),
+        (array((size, LANES), jnp.bfloat16),)
+        + tuple(array(value.shape, jnp.bfloat16) for value in later),
+        (*parts, *later),
+        (
+            pltpu.VMEM((high_count, rows.shape[0], LANES), jnp.float32),
+            pltpu.VMEM((size, LANES), jnp.float32),
+        ),
+    )
+    beside, across = swap(own, 4), swap(own, 2)
+    half = size // 2
+    near = jnp.concatenate([own, beside, across, swap(across[:half], 4), swap(beside[half:], 2)])
+    return (near, swap(near, 1)), later
+
+
+def scatter_blocks(pieces, near, far):
+    high_count = pieces[0].high_count
+    size = sum(piece.size for piece in pieces)
+    flat_rows = sum(piece.flat_rows for piece in pieces)
+    extra_count = near.shape[0] - 4 * size
+    total = near.astype(jnp.float32) + swap(far, 1).astype(jnp.float32)
+    half = size // 2
+    over_x = swap(
+        jnp.concatenate([total[3 * size : 3 * size + half], total[4 * size :]]).astype(
+            jnp.bfloat16
+        ),
+        4,
+    ).astype(jnp.float32)
+    over_y = swap(total[3 * size + half : 4 * size].astype(jnp.bfloat16), 2).astype(jnp.float32)
+    extra = total[4 * size :] + over_x[half:]
+    across = jnp.concatenate(
+        [total[2 * size : 2 * size + half] + over_x[:half], total[2 * size + half : 3 * size], extra]
+    ).astype(jnp.bfloat16)
+    beside = jnp.concatenate(
+        [total[size : size + half], total[size + half : 2 * size] + over_y]
+    ).astype(jnp.bfloat16)
+    terms = [total[:size], swap(beside, 4), swap(across, 2)]
+    if extra_count:
+        terms.append(extra)
+    outs = local_call(
+        functools.partial(unpack_kernel, pieces, extra_count),
+        (array((flat_rows + extra_count, LANES), jnp.float32),)
+        + (array((flat_rows + extra_count, LANES), jnp.bfloat16),) * (high_count - 1),
+        terms,
+        (
+            pltpu.VMEM((high_count, flat_rows, LANES), jnp.float32),
+            pltpu.VMEM((size, LANES), jnp.float32),
+        ),
+    )
+    return outs[0] + sum(
+        swap(send, step * LOW_COUNT).astype(jnp.float32) for step, send in enumerate(outs) if step
+    )
+
+
+def norm_parts(values):
+    scale = lax.rsqrt(jnp.mean(values * values, axis=-1, keepdims=True) + norm_eps)
+    return scale, values * scale
+
+
+def norm_back(scale, normal, upstream, weight_vec):
+    weighted = upstream * (1.0 + weight_vec)
+    inner = jnp.mean(weighted * normal, axis=-1, keepdims=True)
+    return scale * (weighted - normal * inner), jnp.sum(normal * upstream, axis=0, keepdims=True)
+
+
+def product(left_side, right_side, left_axis, right_axis):
+    return lax.dot_general(
+        left_side,
+        right_side,
+        (((left_axis,), (right_axis,)), ((), ())),
+        preferred_element_type=jnp.float32,
+    )
+
+
+def unordered(rows_in, order_low):
+    upper = rows_in.astype(jnp.bfloat16)
+    lower = (rows_in - upper.astype(jnp.float32)).astype(jnp.bfloat16)
+    return product(upper, order_low, 1, 1) + product(lower, order_low, 1, 1)
+
+
+def wide_tile(near_ref, far_ref, size, start, rows):
+    return jnp.concatenate(
+        [
+            ref[place * size + start : place * size + start + rows, :]
+            for ref in (near_ref, far_ref)
+            for place in range(4)
+        ]
+    )
+
+
+def put_wide_tile(near_ref, far_ref, size, start, rows, tile):
+    for order in range(LOW_COUNT):
+        target = near_ref if order < 4 else far_ref
+        first = (order % 4) * size + start
+        target[first : first + rows, :] = tile[order * rows : (order + 1) * rows]
+
+
+def tall_rows(piece, low):
+    for order, mask in enumerate(LOW_MASKS):
+        for block in range(piece.blocks):
+            for place in range(piece.high_count):
+                row = (place * LOW_COUNT + (low ^ mask)) * piece.own_rows
+                yield (
+                    order,
+                    block * piece.block_rows + place * piece.own_rows,
+                    pl.ds(pl.multiple_of(row, piece.own_rows), piece.own_rows),
+                    slice(block * LANES, (block + 1) * LANES),
+                )
+
+
+def ffn_kernel(
+    gate_piece,
+    down_piece,
+    index_ref,
+    middle_ref,
+    cotangent_ref,
+    gain_in_ref,
+    gain_out_ref,
+    order_ref,
+    near_ref,
+    far_ref,
+    near_down_ref,
+    far_down_ref,
+    block_out_ref,
+    grad_middle_ref,
+    grad_gain_in_ref,
+    grad_gain_out_ref,
+    grad_near_ref,
+    grad_far_ref,
+    grad_near_down_ref,
+    grad_far_down_ref,
+    down_ref,
+    hidden_ref,
+    gelu_ref,
+    slope_ref,
+):
+    low = index_ref[0] % LOW_COUNT
+    rows = gate_piece.block_rows
+    size = 2 * gate_piece.size
+    width = 2 * LANES
+    for order, first, matrix_rows, columns in tall_rows(down_piece, low):
+        source = near_down_ref if order < 4 else far_down_ref
+        first = first + (order % 4) * down_piece.size
+        down_ref[matrix_rows, columns] = source[first : first + down_piece.own_rows, :]
+
+    def wide_tiles(step):
+        return [
+            jnp.concatenate(
+                [
+                    wide_tile(near_ref, far_ref, size, offset + block * rows, rows)
+                    for block in (2 * step, 2 * step + 1)
+                ],
+                axis=1,
+            )
+            for offset in (0, gate_piece.size)
+        ]
+
+    middle = middle_ref[...]
+    scale_in, normal_in = norm_parts(middle)
+    order_low = order_ref[...]
+    normed = (normal_in * (1.0 + gain_in_ref[...])).astype(jnp.bfloat16)
+    normed = product(normed, order_low, 1, 0).astype(jnp.bfloat16)
+    for step in range(FF // width):
+        columns = slice(step * width, (step + 1) * width)
+        gate_weight, up_weight = wide_tiles(step)
+        gate = product(normed, gate_weight, 1, 0)
+        up = product(normed, up_weight, 1, 0)
+        square = gate * gate
+        bend = jnp.tanh(GELU_SCALE * gate * (1.0 + GELU_CUBE * square))
+        half = 0.5 * (1.0 + bend)
+        gelu = gate * half
+        slope = half + 0.5 * gate * (1.0 - bend * bend) * GELU_SCALE * (
+            1.0 + 3.0 * GELU_CUBE * square
+        )
+        gelu_ref[:, columns] = gelu
+        slope_ref[:, columns] = slope * up
+        hidden_ref[:, columns] = (gelu * up).astype(jnp.bfloat16)
+    hidden = hidden_ref[...]
+    scale_out, normal_out = norm_parts(product(hidden, down_ref[...], 1, 0))
+    block_out_ref[...] = (middle + normal_out * (1.0 + gain_out_ref[...])).astype(jnp.bfloat16)
+    upstream = cotangent_ref[...].astype(jnp.float32)
+    grad_ffn, grad_gain_out_ref[...] = norm_back(
+        scale_out, normal_out, upstream, gain_out_ref[...]
+    )
+    grad_ffn = grad_ffn.astype(jnp.bfloat16)
+    grad_normed = jnp.zeros(middle.shape, jnp.float32)
+    for step in range(FF // width):
+        columns = slice(step * width, (step + 1) * width)
+        grad_hidden = product(grad_ffn, down_ref[columns, :], 1, 1)
+        down_ref[columns, :] = product(hidden_ref[:, columns], grad_ffn, 0, 0).astype(jnp.bfloat16)
+        grads = [
+            (grad_hidden * slope_ref[:, columns]).astype(jnp.bfloat16),
+            (grad_hidden * gelu_ref[:, columns]).astype(jnp.bfloat16),
+        ]
+        for place, (grad, weight) in enumerate(zip(grads, wide_tiles(step))):
+            grad_weight = product(normed, grad, 0, 0).astype(jnp.bfloat16)
+            for side in range(2):
+                put_wide_tile(
+                    grad_near_ref,
+                    grad_far_ref,
+                    size,
+                    place * gate_piece.size + (2 * step + side) * rows,
+                    rows,
+                    grad_weight[:, side * LANES : (side + 1) * LANES],
+                )
+            grad_normed = grad_normed + product(grad, weight, 1, 1)
+    for order, first, matrix_rows, columns in tall_rows(down_piece, low):
+        target = grad_near_down_ref if order < 4 else grad_far_down_ref
+        first = first + (order % 4) * down_piece.size
+        target[first : first + down_piece.own_rows, :] = down_ref[matrix_rows, columns]
+    grad_middle, grad_gain_in_ref[...] = norm_back(
+        scale_in, normal_in, unordered(grad_normed, order_low), gain_in_ref[...]
+    )
+    grad_middle_ref[...] = upstream + grad_middle
+
+
+def ffn_blocks(pieces, middle, cotangent, gain_in, gain_out, order, gate_up, down):
+    rows = middle.shape[0]
+    shapes = [array(value.shape, jnp.bfloat16) for value in (*gate_up, *down)]
+    outs = local_call(
+        functools.partial(ffn_kernel, pieces[4], pieces[6]),
+        (
+            array((rows, D), jnp.bfloat16),
+            array((rows, D), jnp.float32),
+            array((1, D), jnp.float32),
+            array((1, D), jnp.float32),
+            *shapes,
+        ),
+        (middle, cotangent, gain_in, gain_out, order, *gate_up, *down),
+        (
+            pltpu.VMEM((FF, D), jnp.bfloat16),
+            pltpu.VMEM((rows, FF), jnp.bfloat16),
+            pltpu.VMEM((rows, FF), jnp.float32),
+            pltpu.VMEM((rows, FF), jnp.float32),
+        ),
+    )
+    return outs[0], outs[1], outs[2], outs[3], outs[4:6], outs[6:8]
+
+
+def turn(values, cosine, sine):
+    first_half, second_half = values[:, : HD // 2], values[:, HD // 2 :]
+    return jnp.concatenate(
+        [first_half * cosine - second_half * sine, second_half * cosine + first_half * sine], axis=1
+    )
+
+
+def wide_head(near_ref, far_ref, size, start, rows):
+    return jnp.concatenate(
+        [wide_tile(near_ref, far_ref, size, start + side * rows, rows) for side in range(2)], axis=1
+    )
+
+
+def head_starts(pieces):
+    rows = pieces[0].block_rows
+    return [2 * rows * head for head in range(HQ + 2)]
+
+
+def project_kernel(
+    pieces,
+    index_ref,
+    tokens_ref,
+    gain_ref,
+    gain_query_ref,
+    gain_key_ref,
+    cosine_ref,
+    sine_ref,
+    order_ref,
+    near_ref,
+    far_ref,
+    normed_ref,
+    query_proj_ref,
+    key_proj_ref,
+    query_ref,
+    key_value_ref,
+):
+    size = sum(piece.size for piece in pieces)
+    rows = pieces[0].block_rows
+    cosine, sine = cosine_ref[...], sine_ref[...]
+    _, normal = norm_parts(tokens_ref[...].astype(jnp.float32))
+    normed = (normal * (1.0 + gain_ref[...])).astype(jnp.bfloat16)
+    normed = product(normed, order_ref[...], 1, 0).astype(jnp.bfloat16)
+    normed_ref[...] = normed
+    starts = head_starts(pieces)
+    for head, start in enumerate(starts):
+        proj = product(normed, wide_head(near_ref, far_ref, size, start, rows), 1, 0)
+        columns = slice(head * HD, (head + 1) * HD)
+        if head == HQ + 1:
+            key_value_ref[:, HD:] = proj.astype(jnp.bfloat16)
+            continue
+        gain_vec = gain_query_ref[...] if head < HQ else gain_key_ref[...]
+        _, normal = norm_parts(proj)
+        turned = turn(normal * (1.0 + gain_vec), cosine, sine).astype(jnp.bfloat16)
+        if head < HQ:
+            query_proj_ref[:, columns] = proj
+            query_ref[:, columns] = turned
+        else:
+            key_proj_ref[...] = proj
+            key_value_ref[:, :HD] = turned
+
+
+def attend_kernel(
+    pieces,
+    index_ref,
+    tokens_ref,
+    gain_ref,
+    allowed_ref,
+    query_ref,
+    near_ref,
+    far_ref,
+    *refs,
+):
+    key_value_refs = refs[:-5]
+    probs_ref, attended_ref, attn_out_ref, middle_ref, out_weight_ref = refs[-5:]
+    out_piece = pieces[-1]
+    low = index_ref[0] % LOW_COUNT
+    size = sum(piece.size for piece in pieces)
+    out_start = size - out_piece.size
+    for order, first, matrix_rows, columns in tall_rows(out_piece, low):
+        source = near_ref if order < 4 else far_ref
+        first = first + (order % 4) * size + out_start
+        out_weight_ref[matrix_rows, columns] = source[first : first + out_piece.own_rows, :]
+    rows = tokens_ref.shape[0]
+    allowed = allowed_ref[...] > 0.0
+    keys = jnp.concatenate([ref[:, :HD] for ref in key_value_refs])
+    values = jnp.concatenate([ref[:, HD:] for ref in key_value_refs])
+    count = keys.shape[0]
+    for head in range(HQ):
+        columns = slice(head * HD, (head + 1) * HD)
+        scores = product(query_ref[:, columns], keys, 1, 1) * HD ** (-0.5)
+        scores = jnp.where(allowed, scores, -1e30)
+        raised = jnp.exp(scores - jnp.max(scores, axis=-1, keepdims=True))
+        probs = raised / jnp.sum(raised, axis=-1, keepdims=True)
+        probs_ref[:, head * count : (head + 1) * count] = probs
+        attended_ref[:, columns] = product(probs.astype(jnp.bfloat16), values, 1, 0).astype(
+            jnp.bfloat16
+        )
+    attn_out = product(attended_ref[...], out_weight_ref[...], 1, 0)
+    attn_out_ref[...] = attn_out
+    _, normal = norm_parts(attn_out)
+    middle_ref[...] = tokens_ref[...].astype(jnp.float32) + normal * (1.0 + gain_ref[...])
+
+
+def attend_back_kernel(
+    index_ref,
+    grad_middle_ref,
+    attn_out_ref,
+    gain_ref,
+    out_weight_ref,
+    attended_ref,
+    probs_ref,
+    query_ref,
+    *refs,
+):
+    part_count = (len(refs) - 3) // 2
+    key_value_refs = refs[:part_count]
+    grad_out_weight_ref, grad_query_ref, grad_gain_ref = refs[part_count : part_count + 3]
+    grad_key_value_refs = refs[part_count + 3 :]
+    rows = query_ref.shape[0]
+    scale, normal = norm_parts(attn_out_ref[...])
+    grad_attn, grad_gain_ref[...] = norm_back(scale, normal, grad_middle_ref[...], gain_ref[...])
+    grad_attn = grad_attn.astype(jnp.bfloat16)
+    grad_out_weight_ref[...] = product(attended_ref[...], grad_attn, 0, 0).astype(jnp.bfloat16)
+    keys = jnp.concatenate([ref[:, :HD] for ref in key_value_refs])
+    values = jnp.concatenate([ref[:, HD:] for ref in key_value_refs])
+    count = keys.shape[0]
+    grad_keys = jnp.zeros((count, HD), jnp.float32)
+    grad_values = jnp.zeros((count, HD), jnp.float32)
+    for head in range(HQ):
+        columns = slice(head * HD, (head + 1) * HD)
+        grad_attended = product(grad_attn, out_weight_ref[columns, :], 1, 1).astype(jnp.bfloat16)
+        probs = probs_ref[:, head * count : (head + 1) * count]
+        grad_probs = product(grad_attended, values, 1, 1)
+        grad_values = grad_values + product(probs.astype(jnp.bfloat16), grad_attended, 0, 0)
+        inner = jnp.sum(probs * grad_probs, axis=-1, keepdims=True)
+        grad_scores = (probs * (grad_probs - inner) * HD ** (-0.5)).astype(jnp.bfloat16)
+        grad_query_ref[:, columns] = product(grad_scores, keys, 1, 0)
+        grad_keys = grad_keys + product(grad_scores, query_ref[:, columns], 0, 0)
+    for part, ref in enumerate(grad_key_value_refs):
+        ref[:, :HD] = grad_keys[part * rows : (part + 1) * rows].astype(ref.dtype)
+        ref[:, HD:] = grad_values[part * rows : (part + 1) * rows].astype(ref.dtype)
+
+
+def project_back_kernel(
+    pieces,
+    index_ref,
+    tokens_ref,
+    gain_ref,
+    gain_query_ref,
+    gain_key_ref,
+    cosine_ref,
+    sine_ref,
+    order_ref,
+    near_ref,
+    far_ref,
+    normed_ref,
+    query_proj_ref,
+    key_proj_ref,
+    grad_query_ref,
+    grad_middle_ref,
+    grad_out_weight_ref,
+    gain_attn_ref,
+    gain_ffin_ref,
+    gain_ffout_ref,
+    *refs,
+):
+    key_value_refs = refs[:-4]
+    input_grad_ref, grad_near_ref, grad_far_ref, grad_gain_ref = refs[-4:]
+    low = index_ref[0] % LOW_COUNT
+    size = sum(piece.size for piece in pieces)
+    rows = pieces[0].block_rows
+    cosine, sine = cosine_ref[...], sine_ref[...]
+    normed = normed_ref[...]
+    key_value = sum(ref[...].astype(jnp.float32) for ref in key_value_refs)
+    grad_normed = jnp.zeros(tokens_ref.shape, jnp.float32)
+    grad_gain_query = jnp.zeros((1, HD), jnp.float32)
+    grad_gain_key = jnp.zeros((1, HD), jnp.float32)
+    for head, start in enumerate(head_starts(pieces)):
+        columns = slice(head * HD, (head + 1) * HD)
+        if head < HQ:
+            scale, normal = norm_parts(query_proj_ref[:, columns])
+            upstream = turn(grad_query_ref[:, columns], cosine, -sine)
+            grad, gain_row = norm_back(scale, normal, upstream, gain_query_ref[...])
+            grad_gain_query = grad_gain_query + gain_row
+        elif head == HQ:
+            scale, normal = norm_parts(key_proj_ref[...])
+            upstream = turn(key_value[:, :HD], cosine, -sine)
+            grad, grad_gain_key = norm_back(scale, normal, upstream, gain_key_ref[...])
+        else:
+            grad = key_value[:, HD:]
+        grad = grad.astype(jnp.bfloat16)
+        weight = wide_head(near_ref, far_ref, size, start, rows)
+        grad_normed = grad_normed + product(grad, weight, 1, 1)
+        grad_weight = product(normed, grad, 0, 0).astype(jnp.bfloat16)
+        for side in range(2):
+            put_wide_tile(
+                grad_near_ref,
+                grad_far_ref,
+                size,
+                start + side * rows,
+                rows,
+                grad_weight[:, side * LANES : (side + 1) * LANES],
+            )
+    out_piece = pieces[-1]
+    for order, first, matrix_rows, columns in tall_rows(out_piece, low):
+        target = grad_near_ref if order < 4 else grad_far_ref
+        first = first + (order % 4) * size + size - out_piece.size
+        target[first : first + out_piece.own_rows, :] = grad_out_weight_ref[matrix_rows, columns]
+    scale, normal = norm_parts(tokens_ref[...].astype(jnp.float32))
+    grad_inputs, grad_gain_input = norm_back(
+        scale, normal, unordered(grad_normed, order_ref[...]), gain_ref[...]
+    )
+    input_grad_ref[...] = (grad_middle_ref[...] + grad_inputs).astype(jnp.bfloat16)
+    grad_gains = [
+        grad_gain_input,
+        gain_attn_ref[...],
+        gain_ffin_ref[...],
+        gain_ffout_ref[...],
+        grad_gain_query,
+        grad_gain_key,
+    ]
+    row = 0
+    grad_gain_ref[...] = jnp.zeros(grad_gain_ref.shape, jnp.float32)
+    for values in grad_gains:
+        for start in range(0, values.shape[1], LANES):
+            grad_gain_ref[row : row + 1, :] = values[:, start : start + LANES]
+            row = row + 1
+    for target in (grad_near_ref, grad_far_ref):
+        target[4 * size :, :] = grad_gain_ref[...].astype(jnp.bfloat16)
+
+
+def width_order(device_count):
+    low = lax.axis_index(ALL_AXES) % LOW_COUNT
+    rows = D // device_count
+    high_count = device_count // LOW_COUNT
+    column = jnp.arange(D, dtype=jnp.int32)
+    place = column // (rows * high_count)
+    mask = (place & 1) * 4 + ((place >> 1) & 1) * 2 + (place >> 2)
+    high = (column // rows) % high_count
+    picked = (high * LOW_COUNT + (low ^ mask)) * rows + column % rows
+    return (jnp.arange(D, dtype=jnp.int32)[:, None] == picked[None, :]).astype(jnp.bfloat16)
+
+
+GAIN_ROWS = 32
+
+
+def shards_blocks(
+    device_count,
+    tokens,
+    doc_ids,
+    cotangent,
+    master,
+    first_moment,
+    second_moment,
+    gains,
+    gain_first,
+    gain_second,
+):
+    pieces = [Piece(*shape_pair, device_count) for shape_pair in piece_shapes()]
+    attention_pieces = pieces[:4]
+    local_rows = tokens.shape[0]
+    group_size = lax.axis_size("group")
+    first_row = lax.axis_index("group") * local_rows
+    attention_rows = sum(piece.flat_rows for piece in attention_pieces)
+    down_rows = pieces[6].flat_rows
+    attention_blocks, later = gather_blocks(
+        attention_pieces,
+        master[:attention_rows].astype(jnp.bfloat16),
+        (master[attention_rows:-down_rows], master[-down_rows:]),
+    )
+    gate_up_blocks, _ = gather_blocks(pieces[4:6], later[0])
+    down_blocks, _ = gather_blocks(pieces[6:7], later[1])
+    gain_parts = []
+    for start, width in ((0, D), (D, D), (2 * D, D), (3 * D, D), (4 * D, HD), (4 * D + HD, HD)):
+        gain_parts.append(gains[start : start + width][None])
+    gain_input, gain_attn, gain_ffin, gain_ffout, gain_query, gain_key = gain_parts
+    order = width_order(device_count)
+    doc_row = doc_ids[0]
+    angles = lax.dynamic_slice_in_dim(angles_of(positions(doc_row)), first_row, local_rows, 0)
+    cosine, sine = jnp.cos(angles), jnp.sin(angles)
+    query_docs = lax.dynamic_slice_in_dim(doc_row, first_row, local_rows, 0)
+    reach = min(-(-(WINDOW - 1) // local_rows), group_size - 1)
+    key_count = (reach + 1) * local_rows
+    doc_pad = jnp.concatenate([jnp.full((reach * local_rows,), -1, jnp.int32), doc_row])
+    key_docs = lax.dynamic_slice_in_dim(doc_pad, first_row, key_count, 0)
+    key_index = first_row - reach * local_rows + jnp.arange(key_count, dtype=jnp.int32)
+    query_index = first_row + jnp.arange(local_rows, dtype=jnp.int32)
+    distance = query_index[:, None] - key_index[None, :]
+    allowed = (distance >= 0) & (distance < WINDOW) & (key_docs[None, :] == query_docs[:, None])
+    allowed = allowed.astype(jnp.float32)
+
+    entry = (tokens, gain_input, gain_query, gain_key, cosine, sine, order)
+    width = HQ * HD
+    normed, query_proj, key_proj, query_rot, key_value = local_call(
+        functools.partial(project_kernel, attention_pieces),
+        (
+            array((local_rows, D), jnp.bfloat16),
+            array((local_rows, width), jnp.float32),
+            array((local_rows, HD), jnp.float32),
+            array((local_rows, width), jnp.bfloat16),
+            array((local_rows, 2 * HD), jnp.bfloat16),
+        ),
+        (*entry, *attention_blocks),
+    )
+    key_values = [shifted(key_value, "group", offset) for offset in range(reach, 0, -1)]
+    key_values.append(key_value)
+    probs, attended, attn_out, middle, out_weight = local_call(
+        functools.partial(attend_kernel, attention_pieces),
+        (
+            array((local_rows, HQ * key_count), jnp.float32),
+            array((local_rows, width), jnp.bfloat16),
+            array((local_rows, D), jnp.float32),
+            array((local_rows, D), jnp.float32),
+            array((width, D), jnp.bfloat16),
+        ),
+        (tokens, gain_attn, allowed, query_rot, *attention_blocks, *key_values),
+    )
+    outputs, grad_middle, grad_gain_ffin, grad_gain_ffout, grads_gate_up, grads_down = ffn_blocks(
+        pieces, middle, cotangent, gain_ffin, gain_ffout, order, gate_up_blocks, down_blocks
+    )
+    grads_down = scatter_blocks(pieces[6:7], *grads_down)
+    grads_gate_up = scatter_blocks(pieces[4:6], *grads_gate_up)
+    grad_out_weight, grad_query, grad_gain_attn, *grad_key_values = local_call(
+        attend_back_kernel,
+        (
+            array((width, D), jnp.bfloat16),
+            array((local_rows, width), jnp.float32),
+            array((1, D), jnp.float32),
+            *(array((local_rows, 2 * HD), jnp.bfloat16),) * reach,
+            array((local_rows, 2 * HD), jnp.float32),
+        ),
+        (
+            grad_middle,
+            attn_out,
+            gain_attn,
+            out_weight,
+            attended,
+            probs,
+            query_rot,
+            *key_values,
+        ),
+    )
+    grad_key_values = [
+        shifted(value, "group", place - reach) if place < reach else value
+        for place, value in enumerate(grad_key_values)
+    ]
+    block_rows = attention_blocks[0].shape[0] + GAIN_ROWS
+    grad_inputs, grad_near, grad_far, _ = local_call(
+        functools.partial(project_back_kernel, attention_pieces),
+        (
+            array((local_rows, D), jnp.bfloat16),
+            array((block_rows, LANES), jnp.bfloat16),
+            array((block_rows, LANES), jnp.bfloat16),
+            array((GAIN_ROWS, LANES), jnp.float32),
+        ),
+        (
+            *entry,
+            *attention_blocks,
+            normed,
+            query_proj,
+            key_proj,
+            grad_query,
+            grad_middle,
+            grad_out_weight,
+            grad_gain_attn,
+            grad_gain_ffin,
+            grad_gain_ffout,
+            *grad_key_values,
+        ),
+    )
+    grads_attention = scatter_blocks(attention_pieces, grad_near, grad_far)
+    gain_grads = grads_attention[attention_rows:].reshape(-1)[: gains.shape[0]]
+    grads_local = jnp.concatenate([grads_attention[:attention_rows], grads_gate_up, grads_down])
+    return (
+        outputs,
+        grad_inputs,
+        *adam_update(grads_local, first_moment, second_moment, master, learn_rate, weight_decay),
+        *adam_update(gain_grads, gain_first, gain_second, gains, gain_rate, 0.0),
+    )
+
+
 def shards(
     tokens, doc_ids, cotangent, master, first_moment, second_moment, gains, gain_first, gain_second
 ):
     group_size = lax.axis_size("group")
     devices_all = lax.axis_size("dp") * group_size
+    if aligned(devices_all):
+        return shards_blocks(
+            devices_all,
+            tokens,
+            doc_ids,
+            cotangent,
+            master,
+            first_moment,
+            second_moment,
+            gains,
+            gain_first,
+            gain_second,
+        )
     group_index = lax.axis_index("group")
     local_rows = tokens.shape[0]
     shard_parts = [

time: 1310 us -> 247 us (0.19)
  waiting for transfers between devices: 1030 us -> 82.8 us
  blocking collectives: 120 us -> 0 us
  Pallas kernels: 0 us -> 52.5 us
  starting transfers between devices: 23.5 us -> 71 us
  matrix products: 37.4 us -> 0 us
  local copies, waits for them, and re-layouts: 61.9 us -> 26.3 us
  between operations: 15.8 us -> 1.19 us
    reduce_scatter x5 -> x0, waiting for transfers between devices: 588 us -> none  [the longest x1 141 us: shards(): lax.psum_scatter(flat_gate, ('dp', 'group'), scatter_dimension=0, tiled=T...]
    unnamed x14 -> x0, waiting for transfers between devices: 266 us -> none
    all_gather x5 -> x0, waiting for transfers between devices: 168 us -> none  [the longest x1 56.4 us: shards(): lax.all_gather(shard_parts[4], ('dp', 'group'), axis=0, tiled=True)]
    all_gather x2 -> x0, blocking collectives: 81.4 us -> none  [the longest x1 44.2 us: shards(): lax.all_gather(shard_parts[2], ('dp', 'group'), axis=0, tiled=True)]
    ppermute x0 -> x48, waiting for transfers between devices: none -> 75.6 us  [swap(): lax.ppermute(value, ALL_AXES, [(source, source ^ mask) for source in rang...]
    ppermute x0 -> x48, starting transfers between devices: none -> 60.2 us  [swap(): lax.ppermute(value, ALL_AXES, [(source, source ^ mask) for source in rang...]
    pallas_call x0 -> x11, Pallas kernels: none -> 52.5 us  [local_call(): pl.pallas_call(kernel, out_shape=outs, in_specs=specs, out_specs=tuple((p...]
    reshape x15 -> x0, local copies, waits for them, and re-layouts: 45.5 us -> none  [the longest x8 20.4 us: shards(): full_rows.reshape(shape_pair)]
  transfers between devices with their start and end apart: 24 -> 54, of which waited for: 15 -> 22; matrix products, arithmetic and copies ran while one was open for 6% -> 12% of each run, Pallas kernels for 0% -> 13%
where the time goes in v4:
time: 247 us; the launch traced here: 246 us
  waiting for transfers between devices  82.8 us (34%)
  starting transfers between devices  71 us (29%)
  Pallas kernels  52.5 us (21%)
  local copies, waits for them, and re-layouts  26.3 us (11%)
  other arithmetic  12.2 us (5%)
    ppermute x48, waiting for transfers between devices, swap(): lax.ppermute(value, ALL_AXES, [(source, source ^ mask) for source in rang...  75.6 us
    ppermute x48, starting transfers between devices, swap(): lax.ppermute(value, ALL_AXES, [(source, source ^ mask) for source in rang...  60.2 us
    pallas_call x11, Pallas kernels, local_call(): pl.pallas_call(kernel, out_shape=outs, in_specs=specs, out_specs=tuple((p...  52.5 us
    unnamed x86, local copies, waits for them, and re-layouts  12.1 us
    ppermute x6, starting transfers between devices, shifted(): lax.ppermute(value, axis, [(source, source + steps) for source in range(i...  10.8 us
    ppermute x6, waiting for transfers between devices, shifted(): lax.ppermute(value, axis, [(source, source + steps) for source in range(i...  7.22 us
  transfers between devices with their start and end apart: 54, of which 22 were waited for; matrix products, arithmetic and copies ran while one was open for 12% of the time, Pallas kernels for 13%

profile of v4, /device:TPU:0, one launch (start us, length us, event | category | flops | bytes accessed | tf_op | source)
XLA Modules:
  0.0 246.0 jit_solution(5429769807719303988)
XLA Ops:
  1.6 5.1 %collective-permute-start.2 = (bf16[400,128]{1,0:T(8,128)(2,1)S(1)}, bf16[400,128]{1,0:T(8,128)(2,1)S(1)}, u32[]{:S(2)}, u32[]{:S(2)}) collective-permute-start(bf16[400,128]{1,0:T(8,128)(2,1)S(1)} %slice.267.refs_0_), channel_id=1, source_target_pairs={{0,24},{1,25},{2,26},{3,27},{4,28},{5,29},{6,30},{7,31},{8,16},{9,... | collective-permute-start | bytes 307208 | tf_op jit(solution)/shard_map/ppermute | solution.py:126
  12.9 2.4 collective-permute-done.1.refs_2_
  16.0 2.2 shard_map.152
  18.2 2.5 %collective-permute-start.13 = (bf16[640,128]{1,0:T(8,128)(2,1)}, bf16[640,128]{1,0:T(8,128)(2,1)S(1)}, u32[]{:S(2)}, u32[]{:S(2)}) collective-permute-start(bf16[640,128]{1,0:T(8,128)(2,1)} %get-tuple-element.55.refs_0_), channel_id=1, source_target_pairs={{0,24},{1,25},{2,26},{3,27},{4,28},{5,29},{6,30},{7,31},{8,16},{9,... | collective-permute-start | bytes 491528 | tf_op jit(solution)/shard_map/ppermute | solution.py:126
  22.6 2.5 %collective-permute-start.21 = (bf16[320,128]{1,0:T(8,128)(2,1)}, bf16[320,128]{1,0:T(8,128)(2,1)S(1)}, u32[]{:S(2)}, u32[]{:S(2)}) collective-permute-start(bf16[320,128]{1,0:T(8,128)(2,1)} %get-tuple-element.56.refs_0_), channel_id=1, source_target_pairs={{0,24},{1,25},{2,26},{3,27},{4,28},{5,29},{6,30},{7,31},{8,16},{9,... | collective-permute-start | bytes 245768 | tf_op jit(solution)/shard_map/ppermute | solution.py:126
  25.1 10.0 %collective-permute-done.21.refs_3_ = bf16[320,128]{1,0:T(8,128)(2,1)S(1)} collective-permute-done((bf16[320,128]{1,0:T(8,128)(2,1)}, bf16[320,128]{1,0:T(8,128)(2,1)S(1)}, u32[]{:S(2)}, u32[]{:S(2)}) %collective-permute-start.21) | collective-permute-done | bytes 81952 | tf_op jit(solution)/shard_map/ppermute | solution.py:126
  35.1 5.6 %collective-permute-start.19 = (bf16[320,128]{1,0:T(8,128)(2,1)}, bf16[320,128]{1,0:T(8,128)(2,1)S(1)}, u32[]{:S(2)}, u32[]{:S(2)}) collective-permute-start(bf16[320,128]{1,0:T(8,128)(2,1)} %get-tuple-element.56.refs_0_), channel_id=1, source_target_pairs={{0,8},{1,9},{2,10},{3,11},{4,12},{5,13},{6,14},{7,15},{8,0},{9,1},... | collective-permute-start | bytes 245768 | tf_op jit(solution)/shard_map/ppermute | solution.py:126
  49.7 2.5 %shard_map.155 = bf16[2560,128]{1,0:T(8,128)(2,1)} custom-call(s32[1]{0:T(128)} %bitcast.index_ref, bf16[640,128]{1,0:T(8,128)(2,1)} %get-tuple-element.55.refs_0_, bf16[640,128]{1,0:T(8,128)(2,1)} %copy-done.21, bf16[640,128]{1,0:T(8,128)(2,1)} %copy-done.20, bf16[640,128]{1,0:T(8,128)(2,1)} %copy-done.19), custom_call_target="tpu_custom_call" | custom-call | tf_op jit(solution)/shard_map/pallas_call | solution.py:132
  54.2 6.7 %collective-permute-done.23 = bf16[1280,128]{1,0:T(8,128)(2,1)S(1)} collective-permute-done((bf16[1280,128]{1,0:T(8,128)(2,1)}, bf16[1280,128]{1,0:T(8,128)(2,1)S(1)}, u32[]{:S(2)}, u32[]{:S(2)}) %collective-permute-start.23) | collective-permute-done | bytes 327712 | tf_op jit(solution)/shard_map/ppermute | solution.py:126
  63.2 11.0 %collective-permute-done.22 = bf16[1280,128]{1,0:T(8,128)(2,1)S(1)} collective-permute-done((bf16[1280,128]{1,0:T(8,128)(2,1)S(1)}, bf16[1280,128]{1,0:T(8,128)(2,1)S(1)}, u32[]{:S(2)}, u32[]{:S(2)}) %collective-permute-start.22) | collective-permute-done | bytes 327712 | tf_op jit(solution)/shard_map/ppermute | solution.py:126
  81.7 6.5 %collective-permute-done.16 = bf16[1280,128]{1,0:T(8,128)(2,1)S(1)} collective-permute-done((bf16[1280,128]{1,0:T(8,128)(2,1)S(1)}, bf16[1280,128]{1,0:T(8,128)(2,1)S(1)}, u32[]{:S(2)}, u32[]{:S(2)}) %collective-permute-start.16) | collective-permute-done | bytes 327712 | tf_op jit(solution)/shard_map/ppermute | solution.py:126
  91.2 2.7 %collective-permute-done.6 = bf16[800,128]{1,0:T(8,128)(2,1)S(1)} collective-permute-done((bf16[800,128]{1,0:T(8,128)(2,1)S(1)}, bf16[800,128]{1,0:T(8,128)(2,1)S(1)}, u32[]{:S(2)}, u32[]{:S(2)}) %collective-permute-start.6) | collective-permute-done | bytes 204832 | tf_op jit(solution)/shard_map/ppermute | solution.py:126
  103.9 4.0 %shard_map.153 = (bf16[128,640]{1,0:T(8,128)(2,1)}, f32[128,1024]{1,0:T(8,128)}, f32[128,256]{1,0:T(8,128)}, bf16[128,1024]{1,0:T(8,128)(2,1)}, bf16[128,512]{1,0:T(8,128)(2,1)}) custom-call(s32[1]{0:T(128)} %bitcast.index_ref, bf16[128,640]{1,0:T(8,128)(2,1)} %tokens_ref.5, f32[1,640]{1,0:T(1,128)} %broadcast_in_dim.15.gain_ref, f32[1,256]{1,0:T(1,128)} %bitcast.25, ...), custom_call_target="tpu_custom_call" | custom-call | tf_op jit(solution)/shard_map/pallas_call | solution.py:132
  107.9 2.0 collective-permute-start.10
  109.9 3.2 %collective-permute-start.9 = (bf16[128,512]{1,0:T(8,128)(2,1)}, bf16[128,512]{1,0:T(8,128)(2,1)S(1)}, u32[]{:S(2)}, u32[]{:S(2)}) collective-permute-start(bf16[128,512]{1,0:T(8,128)(2,1)} %get-tuple-element.53.refs_3_), channel_id=1, source_target_pairs={{0,2},{1,3},{4,6},{5,7},{8,10},{9,11},{12,14},{13,15},{16,18},{17,... | collective-permute-start | bytes 393224 | tf_op jit(solution)/shard_map/ppermute | solution.py:33
  118.2 5.7 %shard_map.154 = (f32[128,2048]{1,0:T(8,128)}, bf16[128,1024]{1,0:T(8,128)(2,1)}, f32[128,640]{1,0:T(8,128)}, f32[128,640]{1,0:T(8,128)}, bf16[1024,640]{1,0:T(8,128)(2,1)}) custom-call(s32[1]{0:T(128)} %bitcast.index_ref, bf16[128,640]{1,0:T(8,128)(2,1)} %tokens_ref.5, f32[1,640]{1,0:T(1,128)} %broadcast_in_dim.14.gain_ref, f32[128,512]{1,0:T(8,128)} %fusion.10.allowed_ref, ...), custom_call_target="tpu_custom_call" | custom-call | tf_op jit(solution)/shard_map/pallas_call | solution.py:132
  123.9 14.7 %shard_map.157 = (bf16[128,640]{1,0:T(8,128)(2,1)}, f32[128,640]{1,0:T(8,128)}, f32[1,640]{1,0:T(1,128)}, f32[1,640]{1,0:T(1,128)}, bf16[10240,128]{1,0:T(8,128)...) custom-call(s32[1]{0:T(128)} %bitcast.index_ref, ...), custom_call_target="tpu_custom_call" | custom-call | tf_op jit(solution)/shard_map/pallas_call | solution.py:132
  138.5 6.2 %shard_map.158 = (bf16[1024,640]{1,0:T(8,128)(2,1)}, f32[128,1024]{1,0:T(8,128)}, f32[1,640]{1,0:T(1,128)}, bf16[128,512]{1,0:T(8,128)(2,1)}, bf16[128,512]{1,0:...) custom-call(s32[1]{0:T(128)} %bitcast.index_ref, f32[128,640]{1,0:T(8,128)} %get-tuple-element.61.grad_middle_ref, ...), custom_call_target="tpu_custom_call" | custom-call | tf_op jit(solution)/shard_map/pallas_call | solution.py:132
  148.8 2.4 collective-permute-done.27.refs_0_
  151.2 2.8 %collective-permute-done.28.refs_1_ = bf16[128,512]{1,0:T(8,128)(2,1)S(1)} collective-permute-done((bf16[128,512]{1,0:T(8,128)(2,1)}, bf16[128,512]{1,0:T(8,128)(2,1)S(1)}, u32[]{:S(2)}, u32[]{:S(2)}) %collective-permute-start.28) | collective-permute-done | bytes 131104 | tf_op jit(solution)/shard_map/ppermute | solution.py:33
  154.7 7.4 %shard_map.159 = (bf16[128,640]{1,0:T(8,128)(2,1)}, bf16[6432,128]{1,0:T(8,128)(2,1)}, bf16[6432,128]{1,0:T(8,128)(2,1)}, f32[32,128]{1,0:T(8,128)}) custom-call(s32[1]{0:T(128)} %bitcast.index_ref, bf16[128,640]{1,0:T(8,128)(2,1)} %tokens_ref.5, f32[1,640]{1,0:T(1,128)} %broadcast_in_dim.15.gain_ref, f32[1,256]{1,0:T(1,128)} %bitcast.26, ...), custom_call_target="tpu_custom_call" | custom-call | tf_op jit(solution)/shard_map/pallas_call | solution.py:132
  165.3 4.6 %collective-permute-done.49 = bf16[640,128]{1,0:T(8,128)(2,1)S(1)} collective-permute-done((bf16[640,128]{1,0:T(8,128)(2,1)S(1)}, bf16[640,128]{1,0:T(8,128)(2,1)S(1)}, u32[]{:S(2)}, u32[]{:S(2)}) %collective-permute-start.49) | collective-permute-done | bytes 163872 | tf_op jit(solution)/shard_map/ppermute | solution.py:126
  176.2 8.2 %collective-permute-done.33 = bf16[832,128]{1,0:T(8,128)(2,1)S(1)} collective-permute-done((bf16[832,128]{1,0:T(8,128)(2,1)S(1)}, bf16[832,128]{1,0:T(8,128)(2,1)S(1)}, u32[]{:S(2)}, u32[]{:S(2)}) %collective-permute-start.33) | collective-permute-done | bytes 213024 | tf_op jit(solution)/shard_map/ppermute | solution.py:126
  189.5 7.4 %collective-permute-done.41 = bf16[1280,128]{1,0:T(8,128)(2,1)S(1)} collective-permute-done((bf16[1280,128]{1,0:T(8,128)(2,1)S(1)}, bf16[1280,128]{1,0:T(8,128)(2,1)S(1)}, u32[]{:S(2)}, u32[]{:S(2)}) %collective-permute-start.41) | collective-permute-done | bytes 327712 | tf_op jit(solution)/shard_map/ppermute | solution.py:126
  200.8 2.2 shard_map.162
  209.4 2.6 %collective-permute-start.53 = (bf16[320,128]{1,0:T(8,128)(2,1)}, bf16[320,128]{1,0:T(8,128)(2,1)S(1)}, u32[]{:S(2)}, u32[]{:S(2)}) collective-permute-start(bf16[320,128]{1,0:T(8,128)(2,1)} %get-tuple-element.93), channel_id=1, source_target_pairs={{0,24},{1,25},{2,26},{3,27},{4,28},{5,29},{6,30},{7,31},{8,16},{9,... | collective-permute-start | bytes 245768 | tf_op jit(solution)/shard_map/ppermute | solution.py:126
  212.1 2.1 slice.210.refs_0_
  214.2 2.4 shard_map.160
  218.4 2.6 %collective-permute-start.37 = (bf16[432,128]{1,0:T(8,128)(2,1)}, bf16[432,128]{1,0:T(8,128)(2,1)S(1)}, u32[]{:S(2)}, u32[]{:S(2)}) collective-permute-start(bf16[432,128]{1,0:T(8,128)(2,1)} %get-tuple-element.81), channel_id=1, source_target_pairs={{0,24},{1,25},{2,26},{3,27},{4,28},{5,29},{6,30},{7,31},{8,16},{9,... | collective-permute-start | bytes 331784 | tf_op jit(solution)/shard_map/ppermute | solution.py:126
  222.8 2.5 %collective-permute-done.37 = bf16[432,128]{1,0:T(8,128)(2,1)S(1)} collective-permute-done((bf16[432,128]{1,0:T(8,128)(2,1)}, bf16[432,128]{1,0:T(8,128)(2,1)S(1)}, u32[]{:S(2)}, u32[]{:S(2)}) %collective-permute-start.37) | collective-permute-done | bytes 110624 | tf_op jit(solution)/shard_map/ppermute | solution.py:126
  228.3 3.5 %shard_map.161 = (f32[640,128]{1,0:T(8,128)}, bf16[640,128]{1,0:T(8,128)(2,1)}, bf16[640,128]{1,0:T(8,128)(2,1)}, bf16[640,128]{1,0:T(8,128)(2,1)}) custom-call(s32[1]{0:T(128)} %bitcast.index_ref, f32[2560,128]{1,0:T(8,128)} %slice.221.refs_0_, bf16[2560,128]{1,0:T(8,128)(2,1)} %copy-done.11, bf16[2560,128]{1,0:T(8,128)(2,1)} %collective-permute-done.42.refs_2_), custom_call_target="tpu_custom_call" | custom-call | tf_op jit(solution)/shard_map/pallas_call | solution.py:132
  237.3 5.9 %collective-permute-done.44 = bf16[640,128]{1,0:T(8,128)(2,1)S(1)} collective-permute-done((bf16[640,128]{1,0:T(8,128)(2,1)}, bf16[640,128]{1,0:T(8,128)(2,1)S(1)}, u32[]{:S(2)}, u32[]{:S(2)}) %collective-permute-start.44) | collective-permute-done | bytes 163872 | tf_op jit(solution)/shard_map/ppermute | solution.py:126
  (235 shorter events, 92.7 us)
Async XLA Ops:
  1.6 11.3 %collective-permute-start.2 = (bf16[400,128]{1,0:T(8,128)(2,1)S(1)}, bf16[400,128]{1,0:T(8,128)(2,1)S(1)}, u32[]{:S(2)}, u32[]{:S(2)}) collective-permute-start(bf16[400,128]{1,0:T(8,128)(2,1)S(1)} %slice.267.refs_0_), channel_id=1, source_target_pairs={{0,24},{1,25},{2,26},{3,27},{4,28},{5,29},{6,30},{7,31},{8,16},{9,... | collective-permute-start | bytes 307208 | tf_op jit(solution)/shard_map/ppermute | solution.py:126
  18.2 28.6 %collective-permute-start.13 = (bf16[640,128]{1,0:T(8,128)(2,1)}, bf16[640,128]{1,0:T(8,128)(2,1)S(1)}, u32[]{:S(2)}, u32[]{:S(2)}) collective-permute-start(bf16[640,128]{1,0:T(8,128)(2,1)} %get-tuple-element.55.refs_0_), channel_id=1, source_target_pairs={{0,24},{1,25},{2,26},{3,27},{4,28},{5,29},{6,30},{7,31},{8,16},{9,... | collective-permute-start | bytes 491528 | tf_op jit(solution)/shard_map/ppermute | solution.py:126
  20.6 27.7 %collective-permute-start.12 = (bf16[640,128]{1,0:T(8,128)(2,1)}, bf16[640,128]{1,0:T(8,128)(2,1)S(1)}, u32[]{:S(2)}, u32[]{:S(2)}) collective-permute-start(bf16[640,128]{1,0:T(8,128)(2,1)} %get-tuple-element.55.refs_0_), channel_id=1, source_target_pairs={{0,16},{1,17},{2,18},{3,19},{4,20},{5,21},{6,22},{7,23},{8,24},{9,... | collective-permute-start | bytes 491528 | tf_op jit(solution)/shard_map/ppermute | solution.py:126
  20.6 27.7 %collective-permute-start.11 = (bf16[640,128]{1,0:T(8,128)(2,1)}, bf16[640,128]{1,0:T(8,128)(2,1)S(1)}, u32[]{:S(2)}, u32[]{:S(2)}) collective-permute-start(bf16[640,128]{1,0:T(8,128)(2,1)} %get-tuple-element.55.refs_0_), channel_id=1, source_target_pairs={{0,8},{1,9},{2,10},{3,11},{4,12},{5,13},{6,14},{7,15},{8,0},{9,1},... | collective-permute-start | bytes 491528 | tf_op jit(solution)/shard_map/ppermute | solution.py:126
  22.6 12.6 %collective-permute-start.21 = (bf16[320,128]{1,0:T(8,128)(2,1)}, bf16[320,128]{1,0:T(8,128)(2,1)S(1)}, u32[]{:S(2)}, u32[]{:S(2)}) collective-permute-start(bf16[320,128]{1,0:T(8,128)(2,1)} %get-tuple-element.56.refs_0_), channel_id=1, source_target_pairs={{0,24},{1,25},{2,26},{3,27},{4,28},{5,29},{6,30},{7,31},{8,16},{9,... | collective-permute-start | bytes 245768 | tf_op jit(solution)/shard_map/ppermute | solution.py:126
  25.1 16.1 %collective-permute-start.20 = (bf16[320,128]{1,0:T(8,128)(2,1)}, bf16[320,128]{1,0:T(8,128)(2,1)S(1)}, u32[]{:S(2)}, u32[]{:S(2)}) collective-permute-start(bf16[320,128]{1,0:T(8,128)(2,1)} %get-tuple-element.56.refs_0_), channel_id=1, source_target_pairs={{0,16},{1,17},{2,18},{3,19},{4,20},{5,21},{6,22},{7,23},{8,24},{9,... | collective-permute-start | bytes 245768 | tf_op jit(solution)/shard_map/ppermute | solution.py:126
  41.2 34.3 %collective-permute-start.4 = (bf16[1600,128]{1,0:T(8,128)(2,1)}, bf16[1600,128]{1,0:T(8,128)(2,1)S(1)}, u32[]{:S(2)}, u32[]{:S(2)}) collective-permute-start(bf16[1600,128]{1,0:T(8,128)(2,1)} %get-tuple-element.51), channel_id=1, source_target_pairs={{0,2},{1,3},{2,0},{3,1},{4,6},{5,7},{6,4},{7,5},{8,10},{9,11},{10,... | collective-permute-start | bytes 1228808 | tf_op jit(solution)/shard_map/ppermute | solution.py:126
  43.4 33.7 %collective-permute-start.3 = (bf16[1600,128]{1,0:T(8,128)(2,1)}, bf16[1600,128]{1,0:T(8,128)(2,1)S(1)}, u32[]{:S(2)}, u32[]{:S(2)}) collective-permute-start(bf16[1600,128]{1,0:T(8,128)(2,1)} %get-tuple-element.51), channel_id=1, source_target_pairs={{0,4},{1,5},{2,6},{3,7},{4,0},{5,1},{6,2},{7,3},{8,12},{9,13},{10,... | collective-permute-start | bytes 1228808 | tf_op jit(solution)/shard_map/ppermute | solution.py:126
  46.7 14.1 %collective-permute-start.23 = (bf16[1280,128]{1,0:T(8,128)(2,1)}, bf16[1280,128]{1,0:T(8,128)(2,1)S(1)}, u32[]{:S(2)}, u32[]{:S(2)}) collective-permute-start(bf16[1280,128]{1,0:T(8,128)(2,1)} %shard_map.156), channel_id=1, source_target_pairs={{0,2},{1,3},{2,0},{3,1},{4,6},{5,7},{6,4},{7,5},{8,10},{9,11},{10,... | collective-permute-start | bytes 983048 | tf_op jit(solution)/shard_map/ppermute | solution.py:126
  52.2 25.8 %collective-permute-start.15 = (bf16[2560,128]{1,0:T(8,128)(2,1)}, bf16[2560,128]{1,0:T(8,128)(2,1)S(1)}, u32[]{:S(2)}, u32[]{:S(2)}) collective-permute-start(bf16[2560,128]{1,0:T(8,128)(2,1)} %shard_map.155), channel_id=1, source_target_pairs={{0,2},{1,3},{2,0},{3,1},{4,6},{5,7},{6,4},{7,5},{8,10},{9,11},{10,... | collective-permute-start | bytes 1966088 | tf_op jit(solution)/shard_map/ppermute | solution.py:126
  52.7 26.6 %collective-permute-start.14 = (bf16[2560,128]{1,0:T(8,128)(2,1)}, bf16[2560,128]{1,0:T(8,128)(2,1)S(1)}, u32[]{:S(2)}, u32[]{:S(2)}) collective-permute-start(bf16[2560,128]{1,0:T(8,128)(2,1)} %shard_map.155), channel_id=1, source_target_pairs={{0,4},{1,5},{2,6},{3,7},{4,0},{5,1},{6,2},{7,3},{8,12},{9,13},{10,... | collective-permute-start | bytes 1966088 | tf_op jit(solution)/shard_map/ppermute | solution.py:126
  60.8 13.4 %collective-permute-start.22 = (bf16[1280,128]{1,0:T(8,128)(2,1)S(1)}, bf16[1280,128]{1,0:T(8,128)(2,1)S(1)}, u32[]{:S(2)}, u32[]{:S(2)}) collective-permute-start(bf16[1280,128]{1,0:T(8,128)(2,1)S(1)} %copy-done.7), channel_id=1, source_target_pairs={{0,4},{1,5},{2,6},{3,7},{4,0},{5,1},{6,2},{7,3},{8,12},{9,13},{10,... | collective-permute-start | bytes 983048 | tf_op jit(solution)/shard_map/ppermute | solution.py:126
  74.2 21.5 %collective-permute-start.24 = (bf16[640,128]{1,0:T(8,128)(2,1)S(1)}, bf16[640,128]{1,0:T(8,128)(2,1)S(1)}, u32[]{:S(2)}, u32[]{:S(2)}) collective-permute-start(bf16[640,128]{1,0:T(8,128)(2,1)S(1)} %slice.208), channel_id=1, source_target_pairs={{0,4},{1,5},{2,6},{3,7},{4,0},{5,1},{6,2},{7,3},{8,12},{9,13},{10,... | collective-permute-start | bytes 491528 | tf_op jit(solution)/shard_map/ppermute | solution.py:126
  75.5 20.9 %collective-permute-start.25 = (bf16[640,128]{1,0:T(8,128)(2,1)S(1)}, bf16[640,128]{1,0:T(8,128)(2,1)S(1)}, u32[]{:S(2)}, u32[]{:S(2)}) collective-permute-start(bf16[640,128]{1,0:T(8,128)(2,1)S(1)} %slice.209), channel_id=1, source_target_pairs={{0,2},{1,3},{2,0},{3,1},{4,6},{5,7},{6,4},{7,5},{8,10},{9,11},{10,... | collective-permute-start | bytes 491528 | tf_op jit(solution)/shard_map/ppermute | solution.py:126
  77.1 14.1 %collective-permute-start.5 = (bf16[800,128]{1,0:T(8,128)(2,1)S(1)}, bf16[800,128]{1,0:T(8,128)(2,1)S(1)}, u32[]{:S(2)}, u32[]{:S(2)}) collective-permute-start(bf16[800,128]{1,0:T(8,128)(2,1)S(1)} %slice.204), channel_id=1, source_target_pairs={{0,4},{1,5},{2,6},{3,7},{4,0},{5,1},{6,2},{7,3},{8,12},{9,13},{10,... | collective-permute-start | bytes 614408 | tf_op jit(solution)/shard_map/ppermute | solution.py:126
  79.4 10.9 %collective-permute-start.17 = (bf16[1280,128]{1,0:T(8,128)(2,1)S(1)}, bf16[1280,128]{1,0:T(8,128)(2,1)S(1)}, u32[]{:S(2)}, u32[]{:S(2)}) collective-permute-start(bf16[1280,128]{1,0:T(8,128)(2,1)S(1)} %slice.207), channel_id=1, source_target_pairs={{0,2},{1,3},{2,0},{3,1},{4,6},{5,7},{6,4},{7,5},{8,10},{9,11},{10,... | collective-permute-start | bytes 983048 | tf_op jit(solution)/shard_map/ppermute | solution.py:126
  91.0 32.8 %collective-permute-start.18 = (bf16[10240,128]{1,0:T(8,128)(2,1)}, bf16[10240,128]{1,0:T(8,128)(2,1)}, u32[]{:S(2)}, u32[]{:S(2)}) collective-permute-start(bf16[10240,128]{1,0:T(8,128)(2,1)} %constant_dynamic-update-slice_fusion.5.near_ref), channel_id=1, source_target_pairs={{0,1},{1,0},{2,3},{3,2},{4,5},{5,4},{6,7},{7,6},{8,9},{9,8},{10,11... | collective-permute-start | bytes 7864328 | tf_op jit(solution)/shard_map/ppermute | solution.py:126
  97.1 26.8 %collective-permute-start.26 = (bf16[5120,128]{1,0:T(8,128)(2,1)}, bf16[5120,128]{1,0:T(8,128)(2,1)}, u32[]{:S(2)}, u32[]{:S(2)}) collective-permute-start(bf16[5120,128]{1,0:T(8,128)(2,1)} %constant_dynamic-update-slice_fusion.10.near_down_ref), channel_id=1, source_target_pairs={{0,1},{1,0},{2,3},{3,2},{4,5},{5,4},{6,7},{7,6},{8,9},{9,8},{10,11... | collective-permute-start | bytes 3932168 | tf_op jit(solution)/shard_map/ppermute | solution.py:126
  138.5 24.8 %collective-permute-start.46 = (bf16[5120,128]{1,0:T(8,128)(2,1)}, bf16[5120,128]{1,0:T(8,128)(2,1)S(1)}, u32[]{:S(2)}, u32[]{:S(2)}) collective-permute-start(bf16[5120,128]{1,0:T(8,128)(2,1)} %get-tuple-element.89), channel_id=1, source_target_pairs={{0,1},{1,0},{2,3},{3,2},{4,5},{5,4},{6,7},{7,6},{8,9},{9,8},{10,11... | collective-permute-start | bytes 3932168 | tf_op jit(solution)/shard_map/ppermute | solution.py:126
  165.3 20.0 %collective-permute-start.38 = (bf16[10240,128]{1,0:T(8,128)(2,1)S(1)}, bf16[10240,128]{1,0:T(8,128)(2,1)S(1)}, u32[]{:S(2)}, u32[]{:S(2)}) collective-permute-start(bf16[10240,128]{1,0:T(8,128)(2,1)S(1)} %copy-done.36), channel_id=1, source_target_pairs={{0,1},{1,0},{2,3},{3,2},{4,5},{5,4},{6,7},{7,6},{8,9},{9,8},{10,11... | collective-permute-start | bytes 7864328 | tf_op jit(solution)/shard_map/ppermute | solution.py:126
  171.3 27.3 %collective-permute-start.48 = (bf16[1280,128]{1,0:T(8,128)(2,1)S(1)}, bf16[1280,128]{1,0:T(8,128)(2,1)S(1)}, u32[]{:S(2)}, u32[]{:S(2)}) collective-permute-start(bf16[1280,128]{1,0:T(8,128)(2,1)S(1)} %pad_maximum_fusion.5), channel_id=1, source_target_pairs={{0,4},{1,5},{2,6},{3,7},{4,0},{5,1},{6,2},{7,3},{8,12},{9,13},{10,... | collective-permute-start | bytes 983048 | tf_op jit(solution)/shard_map/ppermute | solution.py:126
  172.4 12.0 %collective-permute-start.31 = (bf16[800,128]{1,0:T(8,128)(2,1)S(1)}, bf16[800,128]{1,0:T(8,128)(2,1)S(1)}, u32[]{:S(2)}, u32[]{:S(2)}) collective-permute-start(bf16[800,128]{1,0:T(8,128)(2,1)S(1)} %get-tuple-element.120), channel_id=1, source_target_pairs={{0,2},{1,3},{2,0},{3,1},{4,6},{5,7},{6,4},{7,5},{8,10},{9,11},{10,... | collective-permute-start | bytes 614408 | tf_op jit(solution)/shard_map/ppermute | solution.py:126
  172.8 11.6 %collective-permute-start.33 = (bf16[832,128]{1,0:T(8,128)(2,1)S(1)}, bf16[832,128]{1,0:T(8,128)(2,1)S(1)}, u32[]{:S(2)}, u32[]{:S(2)}) collective-permute-start(bf16[832,128]{1,0:T(8,128)(2,1)S(1)} %pad_maximum_fusion.7), channel_id=1, source_target_pairs={{0,4},{1,5},{2,6},{3,7},{4,0},{5,1},{6,2},{7,3},{8,12},{9,13},{10,... | collective-permute-start | bytes 638984 | tf_op jit(solution)/shard_map/ppermute | solution.py:126
  174.3 26.4 %collective-permute-start.50 = (bf16[1280,128]{1,0:T(8,128)(2,1)S(1)}, bf16[1280,128]{1,0:T(8,128)(2,1)}, u32[]{:S(2)}, u32[]{:S(2)}) collective-permute-start(bf16[1280,128]{1,0:T(8,128)(2,1)S(1)} %pad_maximum_fusion.6), channel_id=1, source_target_pairs={{0,2},{1,3},{2,0},{3,1},{4,6},{5,7},{6,4},{7,5},{8,10},{9,11},{10,... | collective-permute-start | bytes 983048 | tf_op jit(solution)/shard_map/ppermute | solution.py:126
  186.1 10.7 %collective-permute-start.41 = (bf16[1280,128]{1,0:T(8,128)(2,1)S(1)}, bf16[1280,128]{1,0:T(8,128)(2,1)S(1)}, u32[]{:S(2)}, u32[]{:S(2)}) collective-permute-start(bf16[1280,128]{1,0:T(8,128)(2,1)S(1)} %get-tuple-element.110), channel_id=1, source_target_pairs={{0,4},{1,5},{2,6},{3,7},{4,0},{5,1},{6,2},{7,3},{8,12},{9,13},{10,... | collective-permute-start | bytes 983048 | tf_op jit(solution)/shard_map/ppermute | solution.py:126
  186.8 10.7 %collective-permute-start.39 = (bf16[1280,128]{1,0:T(8,128)(2,1)S(1)}, bf16[1280,128]{1,0:T(8,128)(2,1)S(1)}, u32[]{:S(2)}, u32[]{:S(2)}) collective-permute-start(bf16[1280,128]{1,0:T(8,128)(2,1)S(1)} %get-tuple-element.112), channel_id=1, source_target_pairs={{0,2},{1,3},{2,0},{3,1},{4,6},{5,7},{6,4},{7,5},{8,10},{9,11},{10,... | collective-permute-start | bytes 983048 | tf_op jit(solution)/shard_map/ppermute | solution.py:126
  188.2 17.6 %collective-permute-start.32 = (bf16[1600,128]{1,0:T(8,128)(2,1)}, bf16[1600,128]{1,0:T(8,128)(2,1)}, u32[]{:S(2)}, u32[]{:S(2)}) collective-permute-start(bf16[1600,128]{1,0:T(8,128)(2,1)} %pad_maximum_fusion.4), channel_id=1, source_target_pairs={{0,4},{1,5},{2,6},{3,7},{4,0},{5,1},{6,2},{7,3},{8,12},{9,13},{10,... | collective-permute-start | bytes 1228808 | tf_op jit(solution)/shard_map/ppermute | solution.py:126
  196.9 12.6 %collective-permute-start.34 = (bf16[1632,128]{1,0:T(8,128)(2,1)S(1)}, bf16[1632,128]{1,0:T(8,128)(2,1)S(1)}, u32[]{:S(2)}, u32[]{:S(2)}) collective-permute-start(bf16[1632,128]{1,0:T(8,128)(2,1)S(1)} %pad_maximum_fusion.3), channel_id=1, source_target_pairs={{0,2},{1,3},{2,0},{3,1},{4,6},{5,7},{6,4},{7,5},{8,10},{9,11},{10,... | collective-permute-start | bytes 1253384 | tf_op jit(solution)/shard_map/ppermute | solution.py:126
  197.7 29.8 %collective-permute-start.40 = (bf16[2560,128]{1,0:T(8,128)(2,1)S(1)}, bf16[2560,128]{1,0:T(8,128)(2,1)S(1)}, u32[]{:S(2)}, u32[]{:S(2)}) collective-permute-start(bf16[2560,128]{1,0:T(8,128)(2,1)S(1)} %pad_maximum_fusion.1), channel_id=1, source_target_pairs={{0,4},{1,5},{2,6},{3,7},{4,0},{5,1},{6,2},{7,3},{8,12},{9,13},{10,... | collective-permute-start | bytes 1966088 | tf_op jit(solution)/shard_map/ppermute | solution.py:126
  198.6 28.9 %collective-permute-start.42 = (bf16[2560,128]{1,0:T(8,128)(2,1)S(1)}, bf16[2560,128]{1,0:T(8,128)(2,1)}, u32[]{:S(2)}, u32[]{:S(2)}) collective-permute-start(bf16[2560,128]{1,0:T(8,128)(2,1)S(1)} %pad_maximum_fusion.2), channel_id=1, source_target_pairs={{0,2},{1,3},{2,0},{3,1},{4,6},{5,7},{6,4},{7,5},{8,10},{9,11},{10,... | collective-permute-start | bytes 1966088 | tf_op jit(solution)/shard_map/ppermute | solution.py:126
  203.0 13.6 %collective-permute-start.51 = (bf16[320,128]{1,0:T(8,128)(2,1)}, bf16[320,128]{1,0:T(8,128)(2,1)S(1)}, u32[]{:S(2)}, u32[]{:S(2)}) collective-permute-start(bf16[320,128]{1,0:T(8,128)(2,1)} %get-tuple-element.91), channel_id=1, source_target_pairs={{0,8},{1,9},{2,10},{3,11},{4,12},{5,13},{6,14},{7,15},{8,0},{9,1},... | collective-permute-start | bytes 245768 | tf_op jit(solution)/shard_map/ppermute | solution.py:126
  205.7 10.9 %collective-permute-start.52 = (bf16[320,128]{1,0:T(8,128)(2,1)}, bf16[320,128]{1,0:T(8,128)(2,1)S(1)}, u32[]{:S(2)}, u32[]{:S(2)}) collective-permute-start(bf16[320,128]{1,0:T(8,128)(2,1)} %get-tuple-element.92), channel_id=1, source_target_pairs={{0,16},{1,17},{2,18},{3,19},{4,20},{5,21},{6,22},{7,23},{8,24},{9,... | collective-permute-start | bytes 245768 | tf_op jit(solution)/shard_map/ppermute | solution.py:126
  (59 other events, 416.8 us)

commit v5 on v4

--- a/solution.py
+++ b/solution.py
@@ -126,18 +126,24 @@
     return lax.ppermute(value, ALL_AXES, [(source, source ^ mask) for source in range(count)])
 
 
-def local_call(kernel, outs, operands, scratch=()):
+def local_call(kernel, outs, operands, scratch=(), behind=()):
     specs = [pl.BlockSpec(memory_space=pltpu.SMEM)]
     specs = specs + [pl.BlockSpec(memory_space=pltpu.VMEM)] * len(operands)
+    specs = specs + [pl.BlockSpec(memory_space=pl.ANY)] * len(behind)
+    first, last = 1 + len(operands), 1 + len(operands) + len(behind)
+
+    def body(*refs):
+        kernel(*refs[:first], *refs[last:])
+
     return pl.pallas_call(
-        kernel,
+        body,
         out_shape=outs,
         in_specs=specs,
         out_specs=tuple(pl.BlockSpec(memory_space=pltpu.VMEM) for _ in outs),
         scratch_shapes=scratch,
         compiler_params=pltpu.CompilerParams(vmem_limit_bytes=VMEM_BYTES),
         cost_estimate=pl.CostEstimate(flops=0, bytes_accessed=0, transcendentals=0),
-    )(lax.axis_index(ALL_AXES).astype(jnp.int32).reshape(1), *operands)
+    )(lax.axis_index(ALL_AXES).astype(jnp.int32).reshape(1), *operands, *behind)
 
 
 class Piece:
@@ -153,11 +159,19 @@
         self.size = self.block_rows * self.blocks
 
 
-def pack_kernel(pieces, later_count, index_ref, *refs):
+def round_kernel(index_ref, in_ref, out_ref):
+    out_ref[...] = in_ref[...].astype(jnp.bfloat16)
+
+
+def halves_kernel(index_ref, first_ref, second_ref, first_out_ref, second_out_ref):
+    half = first_out_ref.shape[0]
+    first_out_ref[...] = first_ref[:half, :]
+    second_out_ref[...] = second_ref[half:, :]
+
+
+def pack_kernel(pieces, index_ref, *refs):
     high_count = pieces[0].high_count
-    parts, later = refs[:high_count], refs[high_count : high_count + later_count]
-    out_ref, later_outs = refs[high_count + later_count], refs[high_count + later_count + 1 : -2]
-    flat, packed = refs[-2:]
+    parts, out_ref, flat, packed = refs[:high_count], refs[-3], refs[-2], refs[-1]
     high = index_ref[0] // LOW_COUNT
     for step, part in enumerate(parts):
         flat[high ^ step] = part[...].astype(jnp.float32)
@@ -171,8 +185,6 @@
                 target = target + piece.own_rows
         start = start + piece.flat_rows
     out_ref[...] = packed[...].astype(jnp.bfloat16)
-    for ref, later_out in zip(later, later_outs):
-        later_out[...] = ref[...].astype(jnp.bfloat16)
 
 
 def unpack_kernel(pieces, extra_count, index_ref, *refs):
@@ -202,48 +214,64 @@
     return jax.ShapeDtypeStruct(shape, kind)
 
 
-def gather_blocks(pieces, rows, later=()):
+def gather_high(rows):
+    high_count = lax.axis_size(ALL_AXES) // LOW_COUNT
+    return [rows] + [swap(rows, step * LOW_COUNT) for step in range(1, high_count)]
+
+
+def gather_near(pieces, parts, behind=()):
     high_count = pieces[0].high_count
     size = sum(piece.size for piece in pieces)
-    parts = [rows] + [swap(rows, step * LOW_COUNT) for step in range(1, high_count)]
-    own, *later = local_call(
-        functools.partial(pack_kernel, pieces, len(later)),
-        (array((size, LANES), jnp.bfloat16),)
-        + tuple(array(value.shape, jnp.bfloat16) for value in later),
-        (*parts, *later),
+    (own,) = local_call(
+        functools.partial(pack_kernel, pieces),
+        (array((size, LANES), jnp.bfloat16),),
+        parts,
         (
-            pltpu.VMEM((high_count, rows.shape[0], LANES), jnp.float32),
+            pltpu.VMEM((high_count, parts[0].shape[0], LANES), jnp.float32),
             pltpu.VMEM((size, LANES), jnp.float32),
         ),
-    )
-    beside, across = swap(own, 4), swap(own, 2)
-    half = size // 2
-    near = jnp.concatenate([own, beside, across, swap(across[:half], 4), swap(beside[half:], 2)])
-    return (near, swap(near, 1)), later
-
-
-def scatter_blocks(pieces, near, far):
+        behind,
+    )
+    return own, swap(own, 4), swap(own, 2)
+
+
+def gather_diagonal(own, beside, across, behind=()):
+    half = own.shape[0] // 2
+    to_x, to_y = local_call(
+        halves_kernel,
+        (array((half, LANES), jnp.bfloat16),) * 2,
+        (across, beside),
+        (),
+        behind,
+    )
+    three = jnp.concatenate([own, beside, across])
+    diagonal = jnp.concatenate([swap(to_x, 4), swap(to_y, 2)])
+    return three, diagonal, swap(three, 1), swap(diagonal, 1)
+
+
+def sum_cores(near_three, near_one, far_three, far_one):
+    one = near_one.astype(jnp.float32) + swap(far_one, 1).astype(jnp.float32)
+    three = near_three.astype(jnp.float32) + swap(far_three, 1).astype(jnp.float32)
+    return three, one
+
+
+def scatter_blocks(pieces, three, one):
     high_count = pieces[0].high_count
     size = sum(piece.size for piece in pieces)
     flat_rows = sum(piece.flat_rows for piece in pieces)
-    extra_count = near.shape[0] - 4 * size
-    total = near.astype(jnp.float32) + swap(far, 1).astype(jnp.float32)
+    extra_count = one.shape[0] - size
     half = size // 2
-    over_x = swap(
-        jnp.concatenate([total[3 * size : 3 * size + half], total[4 * size :]]).astype(
-            jnp.bfloat16
-        ),
-        4,
-    ).astype(jnp.float32)
-    over_y = swap(total[3 * size + half : 4 * size].astype(jnp.bfloat16), 2).astype(jnp.float32)
-    extra = total[4 * size :] + over_x[half:]
+    over_x = swap(jnp.concatenate([one[:half], one[size:]]).astype(jnp.bfloat16), 4)
+    over_x = over_x.astype(jnp.float32)
+    over_y = swap(one[half:size].astype(jnp.bfloat16), 2).astype(jnp.float32)
+    extra = one[size:] + over_x[half:]
     across = jnp.concatenate(
-        [total[2 * size : 2 * size + half] + over_x[:half], total[2 * size + half : 3 * size], extra]
+        [three[2 * size : 2 * size + half] + over_x[:half], three[2 * size + half :], extra]
     ).astype(jnp.bfloat16)
     beside = jnp.concatenate(
-        [total[size : size + half], total[size + half : 2 * size] + over_y]
+        [three[size : size + half], three[size + half : 2 * size] + over_y]
     ).astype(jnp.bfloat16)
-    terms = [total[:size], swap(beside, 4), swap(across, 2)]
+    terms = [three[:size], swap(beside, 4), swap(across, 2)]
     if extra_count:
         terms.append(extra)
     outs = local_call(
@@ -287,21 +315,23 @@
     return product(upper, order_low, 1, 1) + product(lower, order_low, 1, 1)
 
 
-def wide_tile(near_ref, far_ref, size, start, rows):
-    return jnp.concatenate(
-        [
-            ref[place * size + start : place * size + start + rows, :]
-            for ref in (near_ref, far_ref)
-            for place in range(4)
-        ]
-    )
-
-
-def put_wide_tile(near_ref, far_ref, size, start, rows, tile):
+def low_block(refs, size, order):
+    three, one = refs[:2] if order < 4 else refs[2:]
+    return (one, 0) if order % 4 == 3 else (three, order % 4 * size)
+
+
+def wide_tile(refs, size, start, rows):
+    tiles = []
     for order in range(LOW_COUNT):
-        target = near_ref if order < 4 else far_ref
-        first = (order % 4) * size + start
-        target[first : first + rows, :] = tile[order * rows : (order + 1) * rows]
+        ref, first = low_block(refs, size, order)
+        tiles.append(ref[first + start : first + start + rows, :])
+    return jnp.concatenate(tiles)
+
+
+def put_wide_tile(refs, size, start, rows, tile):
+    for order in range(LOW_COUNT):
+        ref, first = low_block(refs, size, order)
+        ref[first + start : first + start + rows, :] = tile[order * rows : (order + 1) * rows]
 
 
 def tall_rows(piece, low):
@@ -326,37 +356,25 @@
     gain_in_ref,
     gain_out_ref,
     order_ref,
-    near_ref,
-    far_ref,
-    near_down_ref,
-    far_down_ref,
-    block_out_ref,
-    grad_middle_ref,
-    grad_gain_in_ref,
-    grad_gain_out_ref,
-    grad_near_ref,
-    grad_far_ref,
-    grad_near_down_ref,
-    grad_far_down_ref,
-    down_ref,
-    hidden_ref,
-    gelu_ref,
-    slope_ref,
+    *refs,
 ):
+    weight_refs, grad_refs = refs[:4], refs[8:12]
+    block_out_ref, grad_middle_ref, grad_gain_in_ref, grad_gain_out_ref = refs[4:8]
+    down_ref, hidden_ref, gelu_ref, slope_ref = refs[12:]
     low = index_ref[0] % LOW_COUNT
     rows = gate_piece.block_rows
-    size = 2 * gate_piece.size
+    size = 2 * gate_piece.size + down_piece.size
     width = 2 * LANES
-    for order, first, matrix_rows, columns in tall_rows(down_piece, low):
-        source = near_down_ref if order < 4 else far_down_ref
-        first = first + (order % 4) * down_piece.size
+    for order, start, matrix_rows, columns in tall_rows(down_piece, low):
+        source, first = low_block(weight_refs, size, order)
+        first = first + start + 2 * gate_piece.size
         down_ref[matrix_rows, columns] = source[first : first + down_piece.own_rows, :]
 
     def wide_tiles(step):
         return [
             jnp.concatenate(
                 [
-                    wide_tile(near_ref, far_ref, size, offset + block * rows, rows)
+                    wide_tile(weight_refs, size, offset + block * rows, rows)
                     for block in (2 * step, 2 * step + 1)
                 ],
                 axis=1,
@@ -405,17 +423,16 @@
             grad_weight = product(normed, grad, 0, 0).astype(jnp.bfloat16)
             for side in range(2):
                 put_wide_tile(
-                    grad_near_ref,
-                    grad_far_ref,
+                    grad_refs,
                     size,
                     place * gate_piece.size + (2 * step + side) * rows,
                     rows,
                     grad_weight[:, side * LANES : (side + 1) * LANES],
                 )
             grad_normed = grad_normed + product(grad, weight, 1, 1)
-    for order, first, matrix_rows, columns in tall_rows(down_piece, low):
-        target = grad_near_down_ref if order < 4 else grad_far_down_ref
-        first = first + (order % 4) * down_piece.size
+    for order, start, matrix_rows, columns in tall_rows(down_piece, low):
+        target, first = low_block(grad_refs, size, order)
+        first = first + start + 2 * gate_piece.size
         target[first : first + down_piece.own_rows, :] = down_ref[matrix_rows, columns]
     grad_middle, grad_gain_in_ref[...] = norm_back(
         scale_in, normal_in, unordered(grad_normed, order_low), gain_in_ref[...]
@@ -423,9 +440,8 @@
     grad_middle_ref[...] = upstream + grad_middle
 
 
-def ffn_blocks(pieces, middle, cotangent, gain_in, gain_out, order, gate_up, down):
+def ffn_blocks(pieces, middle, cotangent, gain_in, gain_out, order, blocks):
     rows = middle.shape[0]
-    shapes = [array(value.shape, jnp.bfloat16) for value in (*gate_up, *down)]
     outs = local_call(
         functools.partial(ffn_kernel, pieces[4], pieces[6]),
         (
@@ -433,9 +449,9 @@
             array((rows, D), jnp.float32),
             array((1, D), jnp.float32),
             array((1, D), jnp.float32),
-            *shapes,
+            *(array(value.shape, jnp.bfloat16) for value in blocks),
         ),
-        (middle, cotangent, gain_in, gain_out, order, *gate_up, *down),
+        (middle, cotangent, gain_in, gain_out, order, *blocks),
         (
             pltpu.VMEM((FF, D), jnp.bfloat16),
             pltpu.VMEM((rows, FF), jnp.bfloat16),
@@ -443,7 +459,7 @@
             pltpu.VMEM((rows, FF), jnp.float32),
         ),
     )
-    return outs[0], outs[1], outs[2], outs[3], outs[4:6], outs[6:8]
+    return *outs[:4], outs[4:]
 
 
 def turn(values, cosine, sine):
@@ -453,9 +469,9 @@
     )
 
 
-def wide_head(near_ref, far_ref, size, start, rows):
+def wide_head(refs, size, start, rows):
     return jnp.concatenate(
-        [wide_tile(near_ref, far_ref, size, start + side * rows, rows) for side in range(2)], axis=1
+        [wide_tile(refs, size, start + side * rows, rows) for side in range(2)], axis=1
     )
 
 
@@ -474,14 +490,10 @@
     cosine_ref,
     sine_ref,
     order_ref,
-    near_ref,
-    far_ref,
-    normed_ref,
-    query_proj_ref,
-    key_proj_ref,
-    query_ref,
-    key_value_ref,
+    *refs,
 ):
+    weight_refs = refs[:4]
+    normed_ref, query_proj_ref, key_proj_ref, query_ref, key_value_ref = refs[4:]
     size = sum(piece.size for piece in pieces)
     rows = pieces[0].block_rows
     cosine, sine = cosine_ref[...], sine_ref[...]
@@ -491,7 +503,7 @@
     normed_ref[...] = normed
     starts = head_starts(pieces)
     for head, start in enumerate(starts):
-        proj = product(normed, wide_head(near_ref, far_ref, size, start, rows), 1, 0)
+        proj = product(normed, wide_head(weight_refs, size, start, rows), 1, 0)
         columns = slice(head * HD, (head + 1) * HD)
         if head == HQ + 1:
             key_value_ref[:, HD:] = proj.astype(jnp.bfloat16)
@@ -514,19 +526,17 @@
     gain_ref,
     allowed_ref,
     query_ref,
-    near_ref,
-    far_ref,
     *refs,
 ):
-    key_value_refs = refs[:-5]
+    weight_refs, key_value_refs = refs[:4], refs[4:-5]
     probs_ref, attended_ref, attn_out_ref, middle_ref, out_weight_ref = refs[-5:]
     out_piece = pieces[-1]
     low = index_ref[0] % LOW_COUNT
     size = sum(piece.size for piece in pieces)
     out_start = size - out_piece.size
-    for order, first, matrix_rows, columns in tall_rows(out_piece, low):
-        source = near_ref if order < 4 else far_ref
-        first = first + (order % 4) * size + out_start
+    for order, start, matrix_rows, columns in tall_rows(out_piece, low):
+        source, first = low_block(weight_refs, size, order)
+        first = first + start + out_start
         out_weight_ref[matrix_rows, columns] = source[first : first + out_piece.own_rows, :]
     rows = tokens_ref.shape[0]
     allowed = allowed_ref[...] > 0.0
@@ -599,8 +609,6 @@
     cosine_ref,
     sine_ref,
     order_ref,
-    near_ref,
-    far_ref,
     normed_ref,
     query_proj_ref,
     key_proj_ref,
@@ -612,8 +620,8 @@
     gain_ffout_ref,
     *refs,
 ):
-    key_value_refs = refs[:-4]
-    input_grad_ref, grad_near_ref, grad_far_ref, grad_gain_ref = refs[-4:]
+    weight_refs, key_value_refs, grad_refs = refs[:4], refs[4:-6], refs[-6:-2]
+    input_grad_ref, grad_gain_ref = refs[-2:]
     low = index_ref[0] % LOW_COUNT
     size = sum(piece.size for piece in pieces)
     rows = pieces[0].block_rows
@@ -637,22 +645,21 @@
         else:
             grad = key_value[:, HD:]
         grad = grad.astype(jnp.bfloat16)
-        weight = wide_head(near_ref, far_ref, size, start, rows)
+        weight = wide_head(weight_refs, size, start, rows)
         grad_normed = grad_normed + product(grad, weight, 1, 1)
         grad_weight = product(normed, grad, 0, 0).astype(jnp.bfloat16)
         for side in range(2):
             put_wide_tile(
-                grad_near_ref,
-                grad_far_ref,
+                grad_refs,
                 size,
                 start + side * rows,
                 rows,
                 grad_weight[:, side * LANES : (side + 1) * LANES],
             )
     out_piece = pieces[-1]
-    for order, first, matrix_rows, columns in tall_rows(out_piece, low):
-        target = grad_near_ref if order < 4 else grad_far_ref
-        first = first + (order % 4) * size + size - out_piece.size
+    for order, start, matrix_rows, columns in tall_rows(out_piece, low):
+        target, first = low_block(grad_refs, size, order)
+        first = first + start + size - out_piece.size
         target[first : first + out_piece.own_rows, :] = grad_out_weight_ref[matrix_rows, columns]
     scale, normal = norm_parts(tokens_ref[...].astype(jnp.float32))
     grad_inputs, grad_gain_input = norm_back(
@@ -673,8 +680,8 @@
         for start in range(0, values.shape[1], LANES):
             grad_gain_ref[row : row + 1, :] = values[:, start : start + LANES]
             row = row + 1
-    for target in (grad_near_ref, grad_far_ref):
-        target[4 * size :, :] = grad_gain_ref[...].astype(jnp.bfloat16)
+    for target in (grad_refs[1], grad_refs[3]):
+        target[size:, :] = grad_gain_ref[...].astype(jnp.bfloat16)
 
 
 def width_order(device_count):
@@ -710,14 +717,17 @@
     group_size = lax.axis_size("group")
     first_row = lax.axis_index("group") * local_rows
     attention_rows = sum(piece.flat_rows for piece in attention_pieces)
-    down_rows = pieces[6].flat_rows
-    attention_blocks, later = gather_blocks(
-        attention_pieces,
-        master[:attention_rows].astype(jnp.bfloat16),
-        (master[attention_rows:-down_rows], master[-down_rows:]),
-    )
-    gate_up_blocks, _ = gather_blocks(pieces[4:6], later[0])
-    down_blocks, _ = gather_blocks(pieces[6:7], later[1])
+    attention_parts = gather_high(master[:attention_rows].astype(jnp.bfloat16))
+    (ffn_rows,) = local_call(
+        round_kernel,
+        (array((master.shape[0] - attention_rows, LANES), jnp.bfloat16),),
+        (master[attention_rows:],),
+        (),
+        attention_parts[1:],
+    )
+    ffn_parts = gather_high(ffn_rows)
+    attention_blocks = gather_diagonal(*gather_near(attention_pieces, attention_parts))
+    ffn_near = gather_near(pieces[4:7], ffn_parts, (attention_blocks[1],))
     gain_parts = []
     for start, width in ((0, D), (D, D), (2 * D, D), (3 * D, D), (4 * D, HD), (4 * D + HD, HD)):
         gain_parts.append(gains[start : start + width][None])
@@ -763,11 +773,12 @@
         ),
         (tokens, gain_attn, allowed, query_rot, *attention_blocks, *key_values),
     )
-    outputs, grad_middle, grad_gain_ffin, grad_gain_ffout, grads_gate_up, grads_down = ffn_blocks(
-        pieces, middle, cotangent, gain_ffin, gain_ffout, order, gate_up_blocks, down_blocks
-    )
-    grads_down = scatter_blocks(pieces[6:7], *grads_down)
-    grads_gate_up = scatter_blocks(pieces[4:6], *grads_gate_up)
+    ffn_weights = gather_diagonal(*ffn_near, (key_value,))
+    outputs, grad_middle, grad_gain_ffin, grad_gain_ffout, grads_ffn = ffn_blocks(
+        pieces, middle, cotangent, gain_ffin, gain_ffout, order, ffn_weights
+    )
+    ffn_three, ffn_one = sum_cores(*grads_ffn)
+    grads_ffn = scatter_blocks(pieces[4:7], ffn_three, ffn_one)
     grad_out_weight, grad_query, grad_gain_attn, *grad_key_values = local_call(
         attend_back_kernel,
         (
@@ -792,18 +803,19 @@
         shifted(value, "group", place - reach) if place < reach else value
         for place, value in enumerate(grad_key_values)
     ]
-    block_rows = attention_blocks[0].shape[0] + GAIN_ROWS
-    grad_inputs, grad_near, grad_far, _ = local_call(
+    block_rows = attention_blocks[1].shape[0] + GAIN_ROWS
+    *grads_attention, grad_inputs, _ = local_call(
         functools.partial(project_back_kernel, attention_pieces),
         (
+            array(attention_blocks[0].shape, jnp.bfloat16),
+            array((block_rows, LANES), jnp.bfloat16),
+            array(attention_blocks[0].shape, jnp.bfloat16),
+            array((block_rows, LANES), jnp.bfloat16),
             array((local_rows, D), jnp.bfloat16),
-            array((block_rows, LANES), jnp.bfloat16),
-            array((block_rows, LANES), jnp.bfloat16),
             array((GAIN_ROWS, LANES), jnp.float32),
         ),
         (
             *entry,
-            *attention_blocks,
             normed,
             query_proj,
             key_proj,
@@ -813,12 +825,15 @@
             grad_gain_attn,
             grad_gain_ffin,
             grad_gain_ffout,
+            *attention_blocks,
             *grad_key_values,
         ),
-    )
-    grads_attention = scatter_blocks(attention_pieces, grad_near, grad_far)
+        (),
+        (ffn_three, ffn_one),
+    )
+    grads_attention = scatter_blocks(attention_pieces, *sum_cores(*grads_attention))
     gain_grads = grads_attention[attention_rows:].reshape(-1)[: gains.shape[0]]
-    grads_local = jnp.concatenate([grads_attention[:attention_rows], grads_gate_up, grads_down])
+    grads_local = jnp.concatenate([grads_attention[:attention_rows], grads_ffn])
     return (
         outputs,
         grad_inputs,

time: 247 us -> 261 us (1.057)
  other arithmetic: 12.2 us -> 27.5 us
  waiting for transfers between devices: 82.8 us -> 95.8 us
  starting transfers between devices: 71 us -> 59.4 us
  local copies, waits for them, and re-layouts: 26.3 us -> 20.2 us
  Pallas kernels: 52.5 us -> 55.9 us
    ppermute x48 -> x36, waiting for transfers between devices: 75.6 us -> 94.1 us  [swap(): lax.ppermute(value, ALL_AXES, [(source, source ^ mask) for source in rang...]
    concatenate x7, other arithmetic: 0.96 us -> 13.7 us  [the longest x2 12 us: gather_diagonal(): three = jnp.concatenate([own, beside, across])]
    ppermute x48 -> x36, starting transfers between devices: 60.2 us -> 49.4 us  [swap(): lax.ppermute(value, ALL_AXES, [(source, source ^ mask) for source in rang...]
    ppermute x6, waiting for transfers between devices: 7.22 us -> 1.61 us  [shifted(): lax.ppermute(value, axis, [(source, source + steps) for source in range(i...]
    another operation x9 -> x8, other arithmetic: 2.76 us -> 6.93 us
    pallas_call x11 -> x12, Pallas kernels: 52.5 us -> 55.9 us  [local_call(): pl.pallas_call(body, out_shape=outs, in_specs=specs, out_specs=tuple((pl....]
    unnamed x86 -> x94, local copies, waits for them, and re-layouts: 12.1 us -> 9.15 us
    slice x18 -> x11, local copies, waits for them, and re-layouts: 8.76 us -> 7.78 us  [the longest x2 3.53 us: scatter_blocks(): terms = [three[:size], swap(beside, 4), swap(across, 2)]]
  transfers between devices with their start and end apart: 54 -> 42, of which waited for: 22 -> 16; matrix products, arithmetic and copies ran while one was open for 12% -> 13% of each run, Pallas kernels for 13% -> 13%
where the time goes in v5:
time: 261 us; the launch traced here: 260 us
  waiting for transfers between devices  95.8 us (37%)
  starting transfers between devices  59.4 us (23%)
  Pallas kernels  55.9 us (21%)
  other arithmetic  27.5 us (11%)
  local copies, waits for them, and re-layouts  20.2 us (8%)
    ppermute x36, waiting for transfers between devices, swap(): lax.ppermute(value, ALL_AXES, [(source, source ^ mask) for source in rang...  94.1 us
    pallas_call x12, Pallas kernels, local_call(): pl.pallas_call(body, out_shape=outs, in_specs=specs, out_specs=tuple((pl....  55.9 us
    ppermute x36, starting transfers between devices, swap(): lax.ppermute(value, ALL_AXES, [(source, source ^ mask) for source in rang...  49.4 us
    concatenate x2, other arithmetic, gather_diagonal(): three = jnp.concatenate([own, beside, across])  12 us
    ppermute x6, starting transfers between devices, shifted(): lax.ppermute(value, axis, [(source, source + steps) for source in range(i...  9.98 us
    unnamed x94, local copies, waits for them, and re-layouts  9.15 us
    another operation x8, other arithmetic  6.93 us
  transfers between devices with their start and end apart: 42, of which 16 were waited for; matrix products, arithmetic and copies ran while one was open for 13% of the time, Pallas kernels for 13%

profile of v5, /device:TPU:0, one launch (start us, length us, event | category | flops | bytes accessed | tf_op | source)
XLA Modules:
  0.0 260.1 jit_solution(4825283862276482686)
XLA Ops:
  1.6 3.1 %collective-permute-start = (bf16[400,128]{1,0:T(8,128)(2,1)S(1)}, bf16[400,128]{1,0:T(8,128)(2,1)S(1)}, u32[]{:S(2)}, u32[]{:S(2)}) collective-permute-start(bf16[400,128]{1,0:T(8,128)(2,1)S(1)} %slice.188.refs_1_), channel_id=1, source_target_pairs={{0,8},{1,9},{2,10},{3,11},{4,12},{5,13},{6,14},{7,15},{8,0},{9,1},... | collective-permute-start | bytes 307208 | tf_op jit(solution)/shard_map/ppermute | solution.py:126
  4.7 2.6 collective-permute-start.1
  7.6 7.8 %collective-permute-done.1.refs_3_ = bf16[400,128]{1,0:T(8,128)(2,1)S(1)} collective-permute-done((bf16[400,128]{1,0:T(8,128)(2,1)S(1)}, bf16[400,128]{1,0:T(8,128)(2,1)S(1)}, u32[]{:S(2)}, u32[]{:S(2)}) %collective-permute-start.1) | collective-permute-done | bytes 102432 | tf_op jit(solution)/shard_map/ppermute | solution.py:126
  23.0 4.6 %collective-permute-done.4.refs_1_ = bf16[1600,128]{1,0:T(8,128)(2,1)S(1)} collective-permute-done((bf16[1600,128]{1,0:T(8,128)(2,1)}, bf16[1600,128]{1,0:T(8,128)(2,1)S(1)}, u32[]{:S(2)}, u32[]{:S(2)}) %collective-permute-start.4) | collective-permute-done | bytes 409632 | tf_op jit(solution)/shard_map/ppermute | solution.py:126
  34.8 2.4 collective-permute-start.12
  41.2 4.4 %collective-permute-done.6 = bf16[800,128]{1,0:T(8,128)(2,1)S(1)} collective-permute-done((bf16[800,128]{1,0:T(8,128)(2,1)}, bf16[800,128]{1,0:T(8,128)(2,1)S(1)}, u32[]{:S(2)}, u32[]{:S(2)}) %collective-permute-start.6) | collective-permute-done | bytes 204832 | tf_op jit(solution)/shard_map/ppermute | solution.py:126
  45.7 10.5 %collective-permute-done.13.refs_3_ = bf16[960,128]{1,0:T(8,128)(2,1)S(1)} collective-permute-done((bf16[960,128]{1,0:T(8,128)(2,1)}, bf16[960,128]{1,0:T(8,128)(2,1)S(1)}, u32[]{:S(2)}, u32[]{:S(2)}) %collective-permute-start.13) | collective-permute-done | bytes 245792 | tf_op jit(solution)/shard_map/ppermute | solution.py:126
  57.6 2.9 %shard_map.157 = bf16[3840,128]{1,0:T(8,128)(2,1)} custom-call(s32[1]{0:T(128)} %bitcast.refs_0_, bf16[960,128]{1,0:T(8,128)(2,1)} %shard_map.156.refs_1_, bf16[960,128]{1,0:T(8,128)(2,1)} %copy-done.33, bf16[960,128]{1,0:T(8,128)(2,1)} %copy-done.34, bf16[960,128]{1,0:T(8,128)(2,1)} %copy-done.35, bf16[1600,128]{1,0:T(8,128)(2,1)} %copy-done.1), custom_call_target="tpu_custom_call" | custom-call | tf_op jit(solution)/shard_map/pallas_call | solution.py:138
  62.9 14.1 %collective-permute-done.16.refs_1_ = bf16[3840,128]{1,0:T(8,128)(2,1)S(1)} collective-permute-done((bf16[3840,128]{1,0:T(8,128)(2,1)}, bf16[3840,128]{1,0:T(8,128)(2,1)S(1)}, u32[]{:S(2)}, u32[]{:S(2)}) %collective-permute-start.16) | collective-permute-done | bytes 983072 | tf_op jit(solution)/shard_map/ppermute | solution.py:126
  78.3 11.9 %pad_maximum_fusion.refs_6_ = bf16[11520,128]{1,0:T(8,128)(2,1)} fusion(bf16[3840,128]{1,0:T(8,128)(2,1)S(1)} %collective-permute-done.16.refs_1_, bf16[3840,128]{1,0:T(8,128)(2,1)} %collective-permute-done.15.refs_2_, bf16[3840,128]{1,0:T(8,128)(2,1)S(1)} %copy-done.5), kind=kLoop, calls=%fused_computation.1 | loop fusion | flops 8847360 | bytes 5898240 | tf_op jit(solution)/shard_map/concatenate | solution.py:247
  94.1 2.1 collective-permute-done.8.refs_11_.refs_8_.refs_20_
  97.0 3.9 %shard_map.154 = (bf16[128,640]{1,0:T(8,128)(2,1)}, f32[128,1024]{1,0:T(8,128)}, f32[128,256]{1,0:T(8,128)}, bf16[128,1024]{1,0:T(8,128)(2,1)}, bf16[128,512]{1,0:T(8,128)(2,1)}) custom-call(s32[1]{0:T(128)} %bitcast.refs_0_, bf16[128,640]{1,0:T(8,128)(2,1)} %refs_1_.5, f32[1,640]{1,0:T(1,128)} %broadcast_in_dim.15.refs_2_, f32[1,256]{1,0:T(1,128)} %bitcast.27, ...), custom_call_target="tpu_custom_call" | custom-call | tf_op jit(solution)/shard_map/pallas_call | solution.py:138
  100.8 2.5 shard_map.158
  104.4 12.4 %collective-permute-done.17 = bf16[1920,128]{1,0:T(8,128)(2,1)S(1)} collective-permute-done((bf16[1920,128]{1,0:T(8,128)(2,1)}, bf16[1920,128]{1,0:T(8,128)(2,1)S(1)}, u32[]{:S(2)}, u32[]{:S(2)}) %collective-permute-start.17) | collective-permute-done | bytes 491552 | tf_op jit(solution)/shard_map/ppermute | solution.py:126
  119.2 2.4 collective-permute-start.9
  122.9 2.2 collective-permute-start.11
  128.3 5.7 %shard_map.155 = (f32[128,2048]{1,0:T(8,128)}, bf16[128,1024]{1,0:T(8,128)(2,1)}, f32[128,640]{1,0:T(8,128)}, f32[128,640]{1,0:T(8,128)}, bf16[1024,640]{1,0:T(8,128)(2,1)}) custom-call(s32[1]{0:T(128)} %bitcast.refs_0_, bf16[128,640]{1,0:T(8,128)(2,1)} %refs_1_.5, f32[1,640]{1,0:T(1,128)} %broadcast_in_dim.14.refs_2_.refs_3_, f32[128,512]{1,0:T(8,128)} %fusion.8.refs_3_, ...), custom_call_target="tpu_custom_call" | custom-call | tf_op jit(solution)/shard_map/pallas_call | solution.py:138
  134.9 14.6 %shard_map.159 = (bf16[128,640]{1,0:T(8,128)(2,1)}, f32[128,640]{1,0:T(8,128)}, f32[1,640]{1,0:T(1,128)}, f32[1,640]{1,0:T(1,128)}, bf16[11520,128]{1,0:T(8,128)...) custom-call(s32[1]{0:T(128)} %bitcast.refs_0_, ...), custom_call_target="tpu_custom_call" | custom-call | tf_op jit(solution)/shard_map/pallas_call | solution.py:138
  150.4 6.2 %shard_map.160 = (bf16[1024,640]{1,0:T(8,128)(2,1)}, f32[128,1024]{1,0:T(8,128)}, f32[1,640]{1,0:T(1,128)}, bf16[128,512]{1,0:T(8,128)(2,1)}, bf16[128,512]{1,0:...) custom-call(s32[1]{0:T(128)} %bitcast.refs_0_, f32[128,640]{1,0:T(8,128)} %get-tuple-element.61.refs_1_.refs_12_, ...), custom_call_target="tpu_custom_call" | custom-call | tf_op jit(solution)/shard_map/pallas_call | solution.py:138
  163.9 3.3 %collective-permute-start.35 = (bf16[1920,128]{1,0:T(8,128)(2,1)S(1)}, bf16[1920,128]{1,0:T(8,128)(2,1)S(1)}, u32[]{:S(2)}, u32[]{:S(2)}) collective-permute-start(bf16[1920,128]{1,0:T(8,128)(2,1)S(1)} %get-tuple-element.115), channel_id=1, source_target_pairs={{0,2},{1,3},{2,0},{3,1},{4,6},{5,7},{6,4},{7,5},{8,10},{9,11},{10,... | collective-permute-start | bytes 1474568 | tf_op jit(solution)/shard_map/ppermute | solution.py:126
  167.1 3.9 %fusion.28 = (bf16[11520,128]{1,0:T(8,128)(2,1)}, f32[11520,128]{1,0:T(8,128)}) fusion(bf16[11520,128]{1,0:T(8,128)(2,1)S(1)} %collective-permute-done.24, bf16[11520,128]{1,0:T(8,128)(2,1)S(1)} %copy-done.7), kind=kLoop, calls=%fused_computation.85 | loop fusion | flops 5898240 | bytes 14745600 | tf_op jit(solution)/shard_map/convert.6
  171.7 7.7 %shard_map.161 = (bf16[4800,128]{1,0:T(8,128)(2,1)}, bf16[1632,128]{1,0:T(8,128)(2,1)}, bf16[4800,128]{1,0:T(8,128)(2,1)}, bf16[1632,128]{1,0:T(8,128)(2,1)}, bf...) custom-call(s32[1]{0:T(128)} %bitcast.refs_0_, bf16[128,640]{1,0:T(8,128)(2,1)} %refs_1_.5, f32[1,640]{1,0:T(1,128)} %broadcast_in_dim.15.refs_2_, ...), custom_call_target="tpu_custom_call" | custom-call | tf_op jit(solution)/shard_map/pallas_call | solution.py:138
  183.9 2.0 collective-permute-start.28
  185.9 24.0 %collective-permute-done.30 = bf16[832,128]{1,0:T(8,128)(2,1)S(1)} collective-permute-done((bf16[832,128]{1,0:T(8,128)(2,1)S(1)}, bf16[832,128]{1,0:T(8,128)(2,1)S(1)}, u32[]{:S(2)}, u32[]{:S(2)}) %collective-permute-start.30) | collective-permute-done | bytes 213024 | tf_op jit(solution)/shard_map/ppermute | solution.py:126
  218.3 4.3 %shard_map.163 = (f32[960,128]{1,0:T(8,128)}, bf16[960,128]{1,0:T(8,128)(2,1)}, bf16[960,128]{1,0:T(8,128)(2,1)}, bf16[960,128]{1,0:T(8,128)(2,1)}) custom-call(s32[1]{0:T(128)} %bitcast.refs_0_, f32[3840,128]{1,0:T(8,128)} %slice.155.refs_1_, bf16[3840,128]{1,0:T(8,128)(2,1)} %copy-done.19, bf16[3840,128]{1,0:T(8,128)(2,1)} %copy-done.20), custom_call_target="tpu_custom_call" | custom-call | tf_op jit(solution)/shard_map/pallas_call | solution.py:138
  223.9 7.8 %collective-permute-start.40 = (bf16[960,128]{1,0:T(8,128)(2,1)}, bf16[960,128]{1,0:T(8,128)(2,1)S(1)}, u32[]{:S(2)}, u32[]{:S(2)}) collective-permute-start(bf16[960,128]{1,0:T(8,128)(2,1)} %get-tuple-element.90), channel_id=1, source_target_pairs={{0,16},{1,17},{2,18},{3,19},{4,20},{5,21},{6,22},{7,23},{8,24},{9,... | collective-permute-start | bytes 737288 | tf_op jit(solution)/shard_map/ppermute | solution.py:126
  232.2 2.1 slice.144.refs_1_
  235.1 2.5 shard_map.162
  237.6 2.4 collective-permute-start.34
  240.5 6.1 %collective-permute-start.32 = (bf16[432,128]{1,0:T(8,128)(2,1)}, bf16[432,128]{1,0:T(8,128)(2,1)S(1)}, u32[]{:S(2)}, u32[]{:S(2)}) collective-permute-start(bf16[432,128]{1,0:T(8,128)(2,1)} %get-tuple-element.85), channel_id=1, source_target_pairs={{0,8},{1,9},{2,10},{3,11},{4,12},{5,13},{6,14},{7,15},{8,0},{9,1},... | collective-permute-start | bytes 331784 | tf_op jit(solution)/shard_map/ppermute | solution.py:126
  246.6 7.4 %collective-permute-done.40 = bf16[960,128]{1,0:T(8,128)(2,1)S(1)} collective-permute-done((bf16[960,128]{1,0:T(8,128)(2,1)}, bf16[960,128]{1,0:T(8,128)(2,1)S(1)}, u32[]{:S(2)}, u32[]{:S(2)}) %collective-permute-start.40) | collective-permute-done | bytes 245792 | tf_op jit(solution)/shard_map/ppermute | solution.py:126
  254.1 2.7 %collective-permute-done.33 = bf16[432,128]{1,0:T(8,128)(2,1)S(1)} collective-permute-done((bf16[432,128]{1,0:T(8,128)(2,1)}, bf16[432,128]{1,0:T(8,128)(2,1)S(1)}, u32[]{:S(2)}, u32[]{:S(2)}) %collective-permute-start.33) | collective-permute-done | bytes 110624 | tf_op jit(solution)/shard_map/ppermute | solution.py:126
  (212 shorter events, 66.5 us)
Async XLA Ops:
  4.7 10.7 %collective-permute-start.1 = (bf16[400,128]{1,0:T(8,128)(2,1)S(1)}, bf16[400,128]{1,0:T(8,128)(2,1)S(1)}, u32[]{:S(2)}, u32[]{:S(2)}) collective-permute-start(bf16[400,128]{1,0:T(8,128)(2,1)S(1)} %slice.188.refs_1_), channel_id=1, source_target_pairs={{0,16},{1,17},{2,18},{3,19},{4,20},{5,21},{6,22},{7,23},{8,24},{9,... | collective-permute-start | bytes 307208 | tf_op jit(solution)/shard_map/ppermute | solution.py:126
  31.4 9.8 %collective-permute-start.5 = (bf16[800,128]{1,0:T(8,128)(2,1)}, bf16[800,128]{1,0:T(8,128)(2,1)S(1)}, u32[]{:S(2)}, u32[]{:S(2)}) collective-permute-start(bf16[800,128]{1,0:T(8,128)(2,1)} %get-tuple-element.50), channel_id=1, source_target_pairs={{0,4},{1,5},{2,6},{3,7},{4,0},{5,1},{6,2},{7,3},{8,12},{9,13},{10,... | collective-permute-start | bytes 614408 | tf_op jit(solution)/shard_map/ppermute | solution.py:126
  34.8 10.9 %collective-permute-start.12 = (bf16[960,128]{1,0:T(8,128)(2,1)}, bf16[960,128]{1,0:T(8,128)(2,1)S(1)}, u32[]{:S(2)}, u32[]{:S(2)}) collective-permute-start(bf16[960,128]{1,0:T(8,128)(2,1)} %shard_map.156.refs_1_), channel_id=1, source_target_pairs={{0,8},{1,9},{2,10},{3,11},{4,12},{5,13},{6,14},{7,15},{8,0},{9,1},... | collective-permute-start | bytes 737288 | tf_op jit(solution)/shard_map/ppermute | solution.py:126
  37.2 19.0 %collective-permute-start.13 = (bf16[960,128]{1,0:T(8,128)(2,1)}, bf16[960,128]{1,0:T(8,128)(2,1)S(1)}, u32[]{:S(2)}, u32[]{:S(2)}) collective-permute-start(bf16[960,128]{1,0:T(8,128)(2,1)} %shard_map.156.refs_1_), channel_id=1, source_target_pairs={{0,16},{1,17},{2,18},{3,19},{4,20},{5,21},{6,22},{7,23},{8,24},{9,... | collective-permute-start | bytes 737288 | tf_op jit(solution)/shard_map/ppermute | solution.py:126
  38.2 18.0 %collective-permute-start.14 = (bf16[960,128]{1,0:T(8,128)(2,1)}, bf16[960,128]{1,0:T(8,128)(2,1)S(1)}, u32[]{:S(2)}, u32[]{:S(2)}) collective-permute-start(bf16[960,128]{1,0:T(8,128)(2,1)} %shard_map.156.refs_1_), channel_id=1, source_target_pairs={{0,24},{1,25},{2,26},{3,27},{4,28},{5,29},{6,30},{7,31},{8,16},{9,... | collective-permute-start | bytes 737288 | tf_op jit(solution)/shard_map/ppermute | solution.py:126
  60.5 16.4 %collective-permute-start.16 = (bf16[3840,128]{1,0:T(8,128)(2,1)}, bf16[3840,128]{1,0:T(8,128)(2,1)S(1)}, u32[]{:S(2)}, u32[]{:S(2)}) collective-permute-start(bf16[3840,128]{1,0:T(8,128)(2,1)} %shard_map.157), channel_id=1, source_target_pairs={{0,2},{1,3},{2,0},{3,1},{4,6},{5,7},{6,4},{7,5},{8,10},{9,11},{10,... | collective-permute-start | bytes 2949128 | tf_op jit(solution)/shard_map/ppermute | solution.py:126
  61.8 16.5 %collective-permute-start.15 = (bf16[3840,128]{1,0:T(8,128)(2,1)}, bf16[3840,128]{1,0:T(8,128)(2,1)}, u32[]{:S(2)}, u32[]{:S(2)}) collective-permute-start(bf16[3840,128]{1,0:T(8,128)(2,1)} %shard_map.157), channel_id=1, source_target_pairs={{0,4},{1,5},{2,6},{3,7},{4,0},{5,1},{6,2},{7,3},{8,12},{9,13},{10,... | collective-permute-start | bytes 2949128 | tf_op jit(solution)/shard_map/ppermute | solution.py:126
  62.8 33.4 %collective-permute-start.7 = (bf16[4800,128]{1,0:T(8,128)(2,1)S(1)}, bf16[4800,128]{1,0:T(8,128)(2,1)}, u32[]{:S(2)}, u32[]{:S(2)}) collective-permute-start(bf16[4800,128]{1,0:T(8,128)(2,1)S(1)} %pad_maximum_fusion.1.refs_8_.refs_5_.refs_17_), channel_id=1, source_target_pairs={{0,1},{1,0},{2,3},{3,2},{4,5},{5,4},{6,7},{7,6},{8,9},{9,8},{10,11... | collective-permute-start | bytes 3686408 | tf_op jit(solution)/shard_map/ppermute | solution.py:126
  90.2 43.7 %collective-permute-start.19 = (bf16[11520,128]{1,0:T(8,128)(2,1)}, bf16[11520,128]{1,0:T(8,128)(2,1)}, u32[]{:S(2)}, u32[]{:S(2)}) collective-permute-start(bf16[11520,128]{1,0:T(8,128)(2,1)} %pad_maximum_fusion.refs_6_), channel_id=1, source_target_pairs={{0,1},{1,0},{2,3},{3,2},{4,5},{5,4},{6,7},{7,6},{8,9},{9,8},{10,11... | collective-permute-start | bytes 8847368 | tf_op jit(solution)/shard_map/ppermute | solution.py:126
  103.4 13.5 %collective-permute-start.17 = (bf16[1920,128]{1,0:T(8,128)(2,1)}, bf16[1920,128]{1,0:T(8,128)(2,1)S(1)}, u32[]{:S(2)}, u32[]{:S(2)}) collective-permute-start(bf16[1920,128]{1,0:T(8,128)(2,1)} %get-tuple-element.55), channel_id=1, source_target_pairs={{0,4},{1,5},{2,6},{3,7},{4,0},{5,1},{6,2},{7,3},{8,12},{9,13},{10,... | collective-permute-start | bytes 1474568 | tf_op jit(solution)/shard_map/ppermute | solution.py:126
  103.9 13.2 %collective-permute-start.18 = (bf16[1920,128]{1,0:T(8,128)(2,1)}, bf16[1920,128]{1,0:T(8,128)(2,1)S(1)}, u32[]{:S(2)}, u32[]{:S(2)}) collective-permute-start(bf16[1920,128]{1,0:T(8,128)(2,1)} %get-tuple-element.56), channel_id=1, source_target_pairs={{0,2},{1,3},{2,0},{3,1},{4,6},{5,7},{6,4},{7,5},{8,10},{9,11},{10,... | collective-permute-start | bytes 1474568 | tf_op jit(solution)/shard_map/ppermute | solution.py:126
  117.2 16.8 %collective-permute-start.20 = (bf16[3840,128]{1,0:T(8,128)(2,1)S(1)}, bf16[3840,128]{1,0:T(8,128)(2,1)S(1)}, u32[]{:S(2)}, u32[]{:S(2)}) collective-permute-start(bf16[3840,128]{1,0:T(8,128)(2,1)S(1)} %constant_dynamic-update-slice_fusion.2.refs_7_), channel_id=1, source_target_pairs={{0,1},{1,0},{2,3},{3,2},{4,5},{5,4},{6,7},{7,6},{8,9},{9,8},{10,11... | collective-permute-start | bytes 2949128 | tf_op jit(solution)/shard_map/ppermute | solution.py:126
  149.6 14.3 %collective-permute-start.24 = (bf16[11520,128]{1,0:T(8,128)(2,1)}, bf16[11520,128]{1,0:T(8,128)(2,1)S(1)}, u32[]{:S(2)}, u32[]{:S(2)}) collective-permute-start(bf16[11520,128]{1,0:T(8,128)(2,1)} %get-tuple-element.76), channel_id=1, source_target_pairs={{0,1},{1,0},{2,3},{3,2},{4,5},{5,4},{6,7},{7,6},{8,9},{9,8},{10,11... | collective-permute-start | bytes 8847368 | tf_op jit(solution)/shard_map/ppermute | solution.py:126
  150.3 10.3 %collective-permute-start.25 = (bf16[3840,128]{1,0:T(8,128)(2,1)}, bf16[3840,128]{1,0:T(8,128)(2,1)S(1)}, u32[]{:S(2)}, u32[]{:S(2)}) collective-permute-start(bf16[3840,128]{1,0:T(8,128)(2,1)} %get-tuple-element.78), channel_id=1, source_target_pairs={{0,1},{1,0},{2,3},{3,2},{4,5},{5,4},{6,7},{7,6},{8,9},{9,8},{10,11... | collective-permute-start | bytes 2949128 | tf_op jit(solution)/shard_map/ppermute | solution.py:126
  156.6 14.4 %collective-permute-start.21 = (bf16[128,512]{1,0:T(8,128)(2,1)}, bf16[128,512]{1,0:T(8,128)(2,1)S(1)}, u32[]{:S(2)}, u32[]{:S(2)}) collective-permute-start(bf16[128,512]{1,0:T(8,128)(2,1)} %get-tuple-element.71), channel_id=1, source_target_pairs={{3,0},{7,4},{11,8},{15,12},{19,16},{23,20},{27,24},{31,28}} | collective-permute-start | bytes 393224 | tf_op jit(solution)/shard_map/ppermute | solution.py:33
  157.8 13.2 %collective-permute-start.22 = (bf16[128,512]{1,0:T(8,128)(2,1)}, bf16[128,512]{1,0:T(8,128)(2,1)S(1)}, u32[]{:S(2)}, u32[]{:S(2)}) collective-permute-start(bf16[128,512]{1,0:T(8,128)(2,1)} %get-tuple-element.72), channel_id=1, source_target_pairs={{2,0},{3,1},{6,4},{7,5},{10,8},{11,9},{14,12},{15,13},{18,16},{19,... | collective-permute-start | bytes 393224 | tf_op jit(solution)/shard_map/ppermute | solution.py:33
  159.1 11.9 %collective-permute-start.23 = (bf16[128,512]{1,0:T(8,128)(2,1)}, bf16[128,512]{1,0:T(8,128)(2,1)S(1)}, u32[]{:S(2)}, u32[]{:S(2)}) collective-permute-start(bf16[128,512]{1,0:T(8,128)(2,1)} %get-tuple-element.73), channel_id=1, source_target_pairs={{1,0},{2,1},{3,2},{5,4},{6,5},{7,6},{9,8},{10,9},{11,10},{13,12},{... | collective-permute-start | bytes 393224 | tf_op jit(solution)/shard_map/ppermute | solution.py:33
  162.3 18.6 %collective-permute-start.37 = (bf16[1920,128]{1,0:T(8,128)(2,1)S(1)}, bf16[1920,128]{1,0:T(8,128)(2,1)S(1)}, u32[]{:S(2)}, u32[]{:S(2)}) collective-permute-start(bf16[1920,128]{1,0:T(8,128)(2,1)S(1)} %get-tuple-element.114), channel_id=1, source_target_pairs={{0,4},{1,5},{2,6},{3,7},{4,0},{5,1},{6,2},{7,3},{8,12},{9,13},{10,... | collective-permute-start | bytes 1474568 | tf_op jit(solution)/shard_map/ppermute | solution.py:126
  163.9 17.0 %collective-permute-start.35 = (bf16[1920,128]{1,0:T(8,128)(2,1)S(1)}, bf16[1920,128]{1,0:T(8,128)(2,1)S(1)}, u32[]{:S(2)}, u32[]{:S(2)}) collective-permute-start(bf16[1920,128]{1,0:T(8,128)(2,1)S(1)} %get-tuple-element.115), channel_id=1, source_target_pairs={{0,2},{1,3},{2,0},{3,1},{4,6},{5,7},{6,4},{7,5},{8,10},{9,11},{10,... | collective-permute-start | bytes 1474568 | tf_op jit(solution)/shard_map/ppermute | solution.py:126
  181.2 35.2 %collective-permute-start.36 = (bf16[3840,128]{1,0:T(8,128)(2,1)S(1)}, bf16[3840,128]{1,0:T(8,128)(2,1)S(1)}, u32[]{:S(2)}, u32[]{:S(2)}) collective-permute-start(bf16[3840,128]{1,0:T(8,128)(2,1)S(1)} %pad_maximum_fusion.2), channel_id=1, source_target_pairs={{0,4},{1,5},{2,6},{3,7},{4,0},{5,1},{6,2},{7,3},{8,12},{9,13},{10,... | collective-permute-start | bytes 2949128 | tf_op jit(solution)/shard_map/ppermute | solution.py:126
  182.1 28.5 %collective-permute-start.26 = (bf16[4800,128]{1,0:T(8,128)(2,1)S(1)}, bf16[4800,128]{1,0:T(8,128)(2,1)S(1)}, u32[]{:S(2)}, u32[]{:S(2)}) collective-permute-start(bf16[4800,128]{1,0:T(8,128)(2,1)S(1)} %copy-done.43), channel_id=1, source_target_pairs={{0,1},{1,0},{2,3},{3,2},{4,5},{5,4},{6,7},{7,6},{8,9},{9,8},{10,11... | collective-permute-start | bytes 3686408 | tf_op jit(solution)/shard_map/ppermute | solution.py:126
  182.8 27.1 %collective-permute-start.30 = (bf16[832,128]{1,0:T(8,128)(2,1)S(1)}, bf16[832,128]{1,0:T(8,128)(2,1)S(1)}, u32[]{:S(2)}, u32[]{:S(2)}) collective-permute-start(bf16[832,128]{1,0:T(8,128)(2,1)S(1)} %pad_maximum_fusion.7), channel_id=1, source_target_pairs={{0,4},{1,5},{2,6},{3,7},{4,0},{5,1},{6,2},{7,3},{8,12},{9,13},{10,... | collective-permute-start | bytes 638984 | tf_op jit(solution)/shard_map/ppermute | solution.py:126
  183.8 32.6 %collective-permute-start.38 = (bf16[3840,128]{1,0:T(8,128)(2,1)S(1)}, bf16[3840,128]{1,0:T(8,128)(2,1)S(1)}, u32[]{:S(2)}, u32[]{:S(2)}) collective-permute-start(bf16[3840,128]{1,0:T(8,128)(2,1)S(1)} %pad_maximum_fusion.3), channel_id=1, source_target_pairs={{0,2},{1,3},{2,0},{3,1},{4,6},{5,7},{6,4},{7,5},{8,10},{9,11},{10,... | collective-permute-start | bytes 2949128 | tf_op jit(solution)/shard_map/ppermute | solution.py:126
  183.9 28.0 %collective-permute-start.28 = (bf16[800,128]{1,0:T(8,128)(2,1)S(1)}, bf16[800,128]{1,0:T(8,128)(2,1)S(1)}, u32[]{:S(2)}, u32[]{:S(2)}) collective-permute-start(bf16[800,128]{1,0:T(8,128)(2,1)S(1)} %get-tuple-element.119), channel_id=1, source_target_pairs={{0,2},{1,3},{2,0},{3,1},{4,6},{5,7},{6,4},{7,5},{8,10},{9,11},{10,... | collective-permute-start | bytes 614408 | tf_op jit(solution)/shard_map/ppermute | solution.py:126
  212.8 21.5 %collective-permute-start.31 = (bf16[1632,128]{1,0:T(8,128)(2,1)}, bf16[1632,128]{1,0:T(8,128)(2,1)S(1)}, u32[]{:S(2)}, u32[]{:S(2)}) collective-permute-start(bf16[1632,128]{1,0:T(8,128)(2,1)} %pad_maximum_fusion.5), channel_id=1, source_target_pairs={{0,2},{1,3},{2,0},{3,1},{4,6},{5,7},{6,4},{7,5},{8,10},{9,11},{10,... | collective-permute-start | bytes 1253384 | tf_op jit(solution)/shard_map/ppermute | solution.py:126
  213.9 20.5 %collective-permute-start.29 = (bf16[1600,128]{1,0:T(8,128)(2,1)}, bf16[1600,128]{1,0:T(8,128)(2,1)}, u32[]{:S(2)}, u32[]{:S(2)}) collective-permute-start(bf16[1600,128]{1,0:T(8,128)(2,1)} %pad_maximum_fusion.6), channel_id=1, source_target_pairs={{0,4},{1,5},{2,6},{3,7},{4,0},{5,1},{6,2},{7,3},{8,12},{9,13},{10,... | collective-permute-start | bytes 1228808 | tf_op jit(solution)/shard_map/ppermute | solution.py:126
  222.6 17.9 %collective-permute-start.41 = (bf16[960,128]{1,0:T(8,128)(2,1)}, bf16[960,128]{1,0:T(8,128)(2,1)S(1)}, u32[]{:S(2)}, u32[]{:S(2)}) collective-permute-start(bf16[960,128]{1,0:T(8,128)(2,1)} %get-tuple-element.91), channel_id=1, source_target_pairs={{0,24},{1,25},{2,26},{3,27},{4,28},{5,29},{6,30},{7,31},{8,16},{9,... | collective-permute-start | bytes 737288 | tf_op jit(solution)/shard_map/ppermute | solution.py:126
  223.9 30.1 %collective-permute-start.40 = (bf16[960,128]{1,0:T(8,128)(2,1)}, bf16[960,128]{1,0:T(8,128)(2,1)S(1)}, u32[]{:S(2)}, u32[]{:S(2)}) collective-permute-start(bf16[960,128]{1,0:T(8,128)(2,1)} %get-tuple-element.90), channel_id=1, source_target_pairs={{0,16},{1,17},{2,18},{3,19},{4,20},{5,21},{6,22},{7,23},{8,24},{9,... | collective-permute-start | bytes 737288 | tf_op jit(solution)/shard_map/ppermute | solution.py:126
  231.7 22.3 %collective-permute-start.39 = (bf16[960,128]{1,0:T(8,128)(2,1)}, bf16[960,128]{1,0:T(8,128)(2,1)S(1)}, u32[]{:S(2)}, u32[]{:S(2)}) collective-permute-start(bf16[960,128]{1,0:T(8,128)(2,1)} %get-tuple-element.89), channel_id=1, source_target_pairs={{0,8},{1,9},{2,10},{3,11},{4,12},{5,13},{6,14},{7,15},{8,0},{9,1},... | collective-permute-start | bytes 737288 | tf_op jit(solution)/shard_map/ppermute | solution.py:126
  237.6 16.5 %collective-permute-start.34 = (bf16[432,128]{1,0:T(8,128)(2,1)}, bf16[432,128]{1,0:T(8,128)(2,1)S(1)}, u32[]{:S(2)}, u32[]{:S(2)}) collective-permute-start(bf16[432,128]{1,0:T(8,128)(2,1)} %get-tuple-element.87), channel_id=1, source_target_pairs={{0,24},{1,25},{2,26},{3,27},{4,28},{5,29},{6,30},{7,31},{8,16},{9,... | collective-permute-start | bytes 331784 | tf_op jit(solution)/shard_map/ppermute | solution.py:126
  239.9 16.8 %collective-permute-start.33 = (bf16[432,128]{1,0:T(8,128)(2,1)}, bf16[432,128]{1,0:T(8,128)(2,1)S(1)}, u32[]{:S(2)}, u32[]{:S(2)}) collective-permute-start(bf16[432,128]{1,0:T(8,128)(2,1)} %get-tuple-element.86), channel_id=1, source_target_pairs={{0,16},{1,17},{2,18},{3,19},{4,20},{5,21},{6,22},{7,23},{8,24},{9,... | collective-permute-start | bytes 331784 | tf_op jit(solution)/shard_map/ppermute | solution.py:126
  240.5 16.2 %collective-permute-start.32 = (bf16[432,128]{1,0:T(8,128)(2,1)}, bf16[432,128]{1,0:T(8,128)(2,1)S(1)}, u32[]{:S(2)}, u32[]{:S(2)}) collective-permute-start(bf16[432,128]{1,0:T(8,128)(2,1)} %get-tuple-element.85), channel_id=1, source_target_pairs={{0,8},{1,9},{2,10},{3,11},{4,12},{5,13},{6,14},{7,15},{8,0},{9,1},... | collective-permute-start | bytes 331784 | tf_op jit(solution)/shard_map/ppermute | solution.py:126
  (56 other events, 626.9 us)

commit v6 on v5

--- a/solution.py
+++ b/solution.py
@@ -159,19 +159,18 @@
         self.size = self.block_rows * self.blocks
 
 
-def round_kernel(index_ref, in_ref, out_ref):
-    out_ref[...] = in_ref[...].astype(jnp.bfloat16)
-
-
 def halves_kernel(index_ref, first_ref, second_ref, first_out_ref, second_out_ref):
     half = first_out_ref.shape[0]
     first_out_ref[...] = first_ref[:half, :]
     second_out_ref[...] = second_ref[half:, :]
 
 
-def pack_kernel(pieces, index_ref, *refs):
+def pack_kernel(pieces, later_count, index_ref, *refs):
     high_count = pieces[0].high_count
     parts, out_ref, flat, packed = refs[:high_count], refs[-3], refs[-2], refs[-1]
+    if later_count:
+        later_ref, out_ref = refs[high_count], refs[high_count + 1]
+        refs[-3][...] = later_ref[later_ref.shape[0] - later_count :, :].astype(jnp.bfloat16)
     high = index_ref[0] // LOW_COUNT
     for step, part in enumerate(parts):
         flat[high ^ step] = part[...].astype(jnp.float32)
@@ -187,13 +186,64 @@
     out_ref[...] = packed[...].astype(jnp.bfloat16)
 
 
-def unpack_kernel(pieces, extra_count, index_ref, *refs):
+def sum_one_kernel(size, index_ref, near_ref, far_ref, to_x_ref, to_y_ref):
+    total = near_ref[...].astype(jnp.float32) + far_ref[...].astype(jnp.float32)
+    half = size // 2
+    to_x_ref[:half, :] = total[:half].astype(jnp.bfloat16)
+    if total.shape[0] > size:
+        to_x_ref[half:, :] = total[size:].astype(jnp.bfloat16)
+    to_y_ref[...] = total[half:size].astype(jnp.bfloat16)
+
+
+def sum_three_kernel(
+    size,
+    index_ref,
+    near_ref,
+    far_ref,
+    near_extra_ref,
+    far_extra_ref,
+    over_x_ref,
+    over_y_ref,
+    own_ref,
+    beside_ref,
+    across_ref,
+    extra_ref,
+):
+    half = size // 2
+
+    def both(first, last):
+        return near_ref[first:last, :].astype(jnp.float32) + far_ref[first:last, :].astype(
+            jnp.float32
+        )
+
+    own_ref[...] = both(0, size)
+    beside_ref[:half, :] = both(size, size + half).astype(jnp.bfloat16)
+    beside_ref[half:, :] = (
+        both(size + half, 2 * size) + over_y_ref[...].astype(jnp.float32)
+    ).astype(jnp.bfloat16)
+    across_ref[:half, :] = (
+        both(2 * size, 2 * size + half) + over_x_ref[:half, :].astype(jnp.float32)
+    ).astype(jnp.bfloat16)
+    across_ref[half:size, :] = both(2 * size + half, 3 * size).astype(jnp.bfloat16)
+    if across_ref.shape[0] > size:
+        extra = near_extra_ref[size:, :].astype(jnp.float32)
+        extra = extra + far_extra_ref[size:, :].astype(jnp.float32)
+        extra = extra + over_x_ref[half:, :].astype(jnp.float32)
+        extra_ref[...] = extra
+        across_ref[size:, :] = extra.astype(jnp.bfloat16)
+    else:
+        extra_ref[...] = jnp.zeros(extra_ref.shape, jnp.float32)
+
+
+def unpack_kernel(pieces, index_ref, own_ref, beside_ref, across_ref, extra_ref, *refs):
     high_count = pieces[0].high_count
     size = sum(piece.size for piece in pieces)
     flat_rows = sum(piece.flat_rows for piece in pieces)
-    terms, outs, flat, packed = refs[:3], refs[-2 - high_count : -2], refs[-2], refs[-1]
+    outs, flat, packed = refs[:-2], refs[-2], refs[-1]
     high = index_ref[0] // LOW_COUNT
-    packed[...] = sum(term[:size, :].astype(jnp.float32) for term in terms)
+    packed[...] = (
+        own_ref[...] + beside_ref[...].astype(jnp.float32) + across_ref[:size, :].astype(jnp.float32)
+    )
     start, source = 0, 0
     for piece in pieces:
         for block in range(piece.blocks):
@@ -205,8 +255,8 @@
         start = start + piece.flat_rows
     for step, out_ref in enumerate(outs):
         out_ref[:flat_rows, :] = flat[high ^ step].astype(out_ref.dtype)
-        if extra_count:
-            extra = terms[2][size:, :].astype(jnp.float32) + refs[3][...].astype(jnp.float32)
+        if out_ref.shape[0] > flat_rows:
+            extra = extra_ref[...] + across_ref[size:, :].astype(jnp.float32)
             out_ref[flat_rows:, :] = extra.astype(out_ref.dtype)
 
 
@@ -219,12 +269,16 @@
     return [rows] + [swap(rows, step * LOW_COUNT) for step in range(1, high_count)]
 
 
-def gather_near(pieces, parts, behind=()):
+def gather_near(pieces, parts, later=None, later_count=0, behind=()):
     high_count = pieces[0].high_count
     size = sum(piece.size for piece in pieces)
-    (own,) = local_call(
-        functools.partial(pack_kernel, pieces),
-        (array((size, LANES), jnp.bfloat16),),
+    outs = (array((size, LANES), jnp.bfloat16),)
+    if later_count:
+        parts = (*parts, later)
+        outs = outs + (array((later_count, LANES), jnp.bfloat16),)
+    own, *rounded = local_call(
+        functools.partial(pack_kernel, pieces, later_count),
+        outs,
         parts,
         (
             pltpu.VMEM((high_count, parts[0].shape[0], LANES), jnp.float32),
@@ -232,7 +286,7 @@
         ),
         behind,
     )
-    return own, swap(own, 4), swap(own, 2)
+    return (own, swap(own, 4), swap(own, 2)), *rounded
 
 
 def gather_diagonal(own, beside, across, behind=()):
@@ -244,41 +298,51 @@
         (),
         behind,
     )
-    three = jnp.concatenate([own, beside, across])
-    diagonal = jnp.concatenate([swap(to_x, 4), swap(to_y, 2)])
-    return three, diagonal, swap(three, 1), swap(diagonal, 1)
-
-
-def sum_cores(near_three, near_one, far_three, far_one):
-    one = near_one.astype(jnp.float32) + swap(far_one, 1).astype(jnp.float32)
-    three = near_three.astype(jnp.float32) + swap(far_three, 1).astype(jnp.float32)
-    return three, one
-
-
-def scatter_blocks(pieces, three, one):
+    near = (own, beside, across, swap(to_x, 4), swap(to_y, 2))
+    return near + tuple(swap(value, 1) for value in near)
+
+
+def scatter_start(pieces, near_three, near_one, far_three, far_one):
+    size = sum(piece.size for piece in pieces)
+    far_one = swap(far_one, 1)
+    far_three = swap(far_three, 1)
+    half = size // 2
+    to_x, to_y = local_call(
+        functools.partial(sum_one_kernel, size),
+        (
+            array((near_one.shape[0] - half, LANES), jnp.bfloat16),
+            array((half, LANES), jnp.bfloat16),
+        ),
+        (near_one, far_one),
+    )
+    return (near_three, far_three, near_one, far_one, swap(to_x, 4), swap(to_y, 2)), to_y
+
+
+def scatter_middle(pieces, started):
+    size = sum(piece.size for piece in pieces)
+    extra_count = started[2].shape[0] - size
+    return local_call(
+        functools.partial(sum_three_kernel, size),
+        (
+            array((size, LANES), jnp.float32),
+            array((size, LANES), jnp.bfloat16),
+            array((size + extra_count, LANES), jnp.bfloat16),
+            array((max(extra_count, 8), LANES), jnp.float32),
+        ),
+        started,
+    )
+
+
+def scatter_end(pieces, own, beside, across, extra):
     high_count = pieces[0].high_count
     size = sum(piece.size for piece in pieces)
     flat_rows = sum(piece.flat_rows for piece in pieces)
-    extra_count = one.shape[0] - size
-    half = size // 2
-    over_x = swap(jnp.concatenate([one[:half], one[size:]]).astype(jnp.bfloat16), 4)
-    over_x = over_x.astype(jnp.float32)
-    over_y = swap(one[half:size].astype(jnp.bfloat16), 2).astype(jnp.float32)
-    extra = one[size:] + over_x[half:]
-    across = jnp.concatenate(
-        [three[2 * size : 2 * size + half] + over_x[:half], three[2 * size + half :], extra]
-    ).astype(jnp.bfloat16)
-    beside = jnp.concatenate(
-        [three[size : size + half], three[size + half : 2 * size] + over_y]
-    ).astype(jnp.bfloat16)
-    terms = [three[:size], swap(beside, 4), swap(across, 2)]
-    if extra_count:
-        terms.append(extra)
+    out_rows = flat_rows + across.shape[0] - size
     outs = local_call(
-        functools.partial(unpack_kernel, pieces, extra_count),
-        (array((flat_rows + extra_count, LANES), jnp.float32),)
-        + (array((flat_rows + extra_count, LANES), jnp.bfloat16),) * (high_count - 1),
-        terms,
+        functools.partial(unpack_kernel, pieces),
+        (array((out_rows, LANES), jnp.float32),)
+        + (array((out_rows, LANES), jnp.bfloat16),) * (high_count - 1),
+        (own, swap(beside, 4), swap(across, 2), extra),
         (
             pltpu.VMEM((high_count, flat_rows, LANES), jnp.float32),
             pltpu.VMEM((size, LANES), jnp.float32),
@@ -315,23 +379,32 @@
     return product(upper, order_low, 1, 1) + product(lower, order_low, 1, 1)
 
 
-def low_block(refs, size, order):
+def weight_rows(refs, size, order, start, rows):
+    refs = refs[:5] if order < 4 else refs[5:]
+    ref = refs[order % 4]
+    if order % 4 == 3 and 2 * start >= size:
+        ref, start = refs[4], start - size // 2
+    return ref[start : start + rows, :]
+
+
+def put_rows(refs, size, order, start, rows):
     three, one = refs[:2] if order < 4 else refs[2:]
-    return (one, 0) if order % 4 == 3 else (three, order % 4 * size)
+    if order % 4 == 3:
+        one[start : start + rows.shape[0], :] = rows
+    else:
+        start = order % 4 * size + start
+        three[start : start + rows.shape[0], :] = rows
 
 
 def wide_tile(refs, size, start, rows):
-    tiles = []
-    for order in range(LOW_COUNT):
-        ref, first = low_block(refs, size, order)
-        tiles.append(ref[first + start : first + start + rows, :])
-    return jnp.concatenate(tiles)
+    return jnp.concatenate(
+        [weight_rows(refs, size, order, start, rows) for order in range(LOW_COUNT)]
+    )
 
 
 def put_wide_tile(refs, size, start, rows, tile):
     for order in range(LOW_COUNT):
-        ref, first = low_block(refs, size, order)
-        ref[first + start : first + start + rows, :] = tile[order * rows : (order + 1) * rows]
+        put_rows(refs, size, order, start, tile[order * rows : (order + 1) * rows])
 
 
 def tall_rows(piece, low):
@@ -358,17 +431,18 @@
     order_ref,
     *refs,
 ):
-    weight_refs, grad_refs = refs[:4], refs[8:12]
-    block_out_ref, grad_middle_ref, grad_gain_in_ref, grad_gain_out_ref = refs[4:8]
-    down_ref, hidden_ref, gelu_ref, slope_ref = refs[12:]
+    weight_refs, grad_refs = refs[:10], refs[14:18]
+    block_out_ref, grad_middle_ref, grad_gain_in_ref, grad_gain_out_ref = refs[10:14]
+    down_ref, hidden_ref, gelu_ref, slope_ref = refs[18:]
     low = index_ref[0] % LOW_COUNT
     rows = gate_piece.block_rows
     size = 2 * gate_piece.size + down_piece.size
     width = 2 * LANES
     for order, start, matrix_rows, columns in tall_rows(down_piece, low):
-        source, first = low_block(weight_refs, size, order)
-        first = first + start + 2 * gate_piece.size
-        down_ref[matrix_rows, columns] = source[first : first + down_piece.own_rows, :]
+        start = start + 2 * gate_piece.size
+        down_ref[matrix_rows, columns] = weight_rows(
+            weight_refs, size, order, start, down_piece.own_rows
+        )
 
     def wide_tiles(step):
         return [
@@ -431,13 +505,20 @@
                 )
             grad_normed = grad_normed + product(grad, weight, 1, 1)
     for order, start, matrix_rows, columns in tall_rows(down_piece, low):
-        target, first = low_block(grad_refs, size, order)
-        first = first + start + 2 * gate_piece.size
-        target[first : first + down_piece.own_rows, :] = down_ref[matrix_rows, columns]
+        start = start + 2 * gate_piece.size
+        put_rows(grad_refs, size, order, start, down_ref[matrix_rows, columns])
     grad_middle, grad_gain_in_ref[...] = norm_back(
         scale_in, normal_in, unordered(grad_normed, order_low), gain_in_ref[...]
     )
     grad_middle_ref[...] = upstream + grad_middle
+
+
+def grad_arrays(pieces, extra_count=0):
+    size = sum(piece.size for piece in pieces)
+    return (
+        array((3 * size, LANES), jnp.bfloat16),
+        array((size + extra_count, LANES), jnp.bfloat16),
+    ) * 2
 
 
 def ffn_blocks(pieces, middle, cotangent, gain_in, gain_out, order, blocks):
@@ -449,7 +530,7 @@
             array((rows, D), jnp.float32),
             array((1, D), jnp.float32),
             array((1, D), jnp.float32),
-            *(array(value.shape, jnp.bfloat16) for value in blocks),
+            *grad_arrays(pieces[4:7]),
         ),
         (middle, cotangent, gain_in, gain_out, order, *blocks),
         (
@@ -492,8 +573,8 @@
     order_ref,
     *refs,
 ):
-    weight_refs = refs[:4]
-    normed_ref, query_proj_ref, key_proj_ref, query_ref, key_value_ref = refs[4:]
+    weight_refs = refs[:10]
+    normed_ref, query_proj_ref, key_proj_ref, query_ref, key_value_ref = refs[10:]
     size = sum(piece.size for piece in pieces)
     rows = pieces[0].block_rows
     cosine, sine = cosine_ref[...], sine_ref[...]
@@ -528,16 +609,16 @@
     query_ref,
     *refs,
 ):
-    weight_refs, key_value_refs = refs[:4], refs[4:-5]
+    weight_refs, key_value_refs = refs[:10], refs[10:-5]
     probs_ref, attended_ref, attn_out_ref, middle_ref, out_weight_ref = refs[-5:]
     out_piece = pieces[-1]
     low = index_ref[0] % LOW_COUNT
     size = sum(piece.size for piece in pieces)
     out_start = size - out_piece.size
     for order, start, matrix_rows, columns in tall_rows(out_piece, low):
-        source, first = low_block(weight_refs, size, order)
-        first = first + start + out_start
-        out_weight_ref[matrix_rows, columns] = source[first : first + out_piece.own_rows, :]
+        out_weight_ref[matrix_rows, columns] = weight_rows(
+            weight_refs, size, order, start + out_start, out_piece.own_rows
+        )
     rows = tokens_ref.shape[0]
     allowed = allowed_ref[...] > 0.0
     keys = jnp.concatenate([ref[:, :HD] for ref in key_value_refs])
@@ -620,7 +701,7 @@
     gain_ffout_ref,
     *refs,
 ):
-    weight_refs, key_value_refs, grad_refs = refs[:4], refs[4:-6], refs[-6:-2]
+    weight_refs, key_value_refs, grad_refs = refs[:10], refs[10:-6], refs[-6:-2]
     input_grad_ref, grad_gain_ref = refs[-2:]
     low = index_ref[0] % LOW_COUNT
     size = sum(piece.size for piece in pieces)
@@ -658,9 +739,8 @@
             )
     out_piece = pieces[-1]
     for order, start, matrix_rows, columns in tall_rows(out_piece, low):
-        target, first = low_block(grad_refs, size, order)
-        first = first + start + size - out_piece.size
-        target[first : first + out_piece.own_rows, :] = grad_out_weight_ref[matrix_rows, columns]
+        start = start + size - out_piece.size
+        put_rows(grad_refs, size, order, start, grad_out_weight_ref[matrix_rows, columns])
     scale, normal = norm_parts(tokens_ref[...].astype(jnp.float32))
     grad_inputs, grad_gain_input = norm_back(
         scale, normal, unordered(grad_normed, order_ref[...]), gain_ref[...]
@@ -717,17 +797,16 @@
     group_size = lax.axis_size("group")
     first_row = lax.axis_index("group") * local_rows
     attention_rows = sum(piece.flat_rows for piece in attention_pieces)
-    attention_parts = gather_high(master[:attention_rows].astype(jnp.bfloat16))
-    (ffn_rows,) = local_call(
-        round_kernel,
-        (array((master.shape[0] - attention_rows, LANES), jnp.bfloat16),),
-        (master[attention_rows:],),
-        (),
-        attention_parts[1:],
+    ffn_pieces = pieces[4:7]
+    attention_near, ffn_rows = gather_near(
+        attention_pieces,
+        gather_high(master[:attention_rows].astype(jnp.bfloat16)),
+        master,
+        master.shape[0] - attention_rows,
     )
     ffn_parts = gather_high(ffn_rows)
-    attention_blocks = gather_diagonal(*gather_near(attention_pieces, attention_parts))
-    ffn_near = gather_near(pieces[4:7], ffn_parts, (attention_blocks[1],))
+    attention_blocks = gather_diagonal(*attention_near, (ffn_parts[1],))
+    (ffn_near,) = gather_near(ffn_pieces, ffn_parts, behind=(attention_blocks[3],))
     gain_parts = []
     for start, width in ((0, D), (D, D), (2 * D, D), (3 * D, D), (4 * D, HD), (4 * D + HD, HD)):
         gain_parts.append(gains[start : start + width][None])
@@ -759,6 +838,8 @@
             array((local_rows, 2 * HD), jnp.bfloat16),
         ),
         (*entry, *attention_blocks),
+        (),
+        (ffn_near[0],),
     )
     key_values = [shifted(key_value, "group", offset) for offset in range(reach, 0, -1)]
     key_values.append(key_value)
@@ -773,12 +854,11 @@
         ),
         (tokens, gain_attn, allowed, query_rot, *attention_blocks, *key_values),
     )
-    ffn_weights = gather_diagonal(*ffn_near, (key_value,))
+    ffn_weights = gather_diagonal(*ffn_near, (middle,))
     outputs, grad_middle, grad_gain_ffin, grad_gain_ffout, grads_ffn = ffn_blocks(
         pieces, middle, cotangent, gain_ffin, gain_ffout, order, ffn_weights
     )
-    ffn_three, ffn_one = sum_cores(*grads_ffn)
-    grads_ffn = scatter_blocks(pieces[4:7], ffn_three, ffn_one)
+    ffn_started, ffn_sent = scatter_start(ffn_pieces, *grads_ffn)
     grad_out_weight, grad_query, grad_gain_attn, *grad_key_values = local_call(
         attend_back_kernel,
         (
@@ -798,19 +878,18 @@
             query_rot,
             *key_values,
         ),
-    )
+        (),
+        (ffn_sent,),
+    )
+    ffn_sums = scatter_middle(ffn_pieces, ffn_started)
     grad_key_values = [
         shifted(value, "group", place - reach) if place < reach else value
         for place, value in enumerate(grad_key_values)
     ]
-    block_rows = attention_blocks[1].shape[0] + GAIN_ROWS
     *grads_attention, grad_inputs, _ = local_call(
         functools.partial(project_back_kernel, attention_pieces),
         (
-            array(attention_blocks[0].shape, jnp.bfloat16),
-            array((block_rows, LANES), jnp.bfloat16),
-            array(attention_blocks[0].shape, jnp.bfloat16),
-            array((block_rows, LANES), jnp.bfloat16),
+            *grad_arrays(attention_pieces, GAIN_ROWS),
             array((local_rows, D), jnp.bfloat16),
             array((GAIN_ROWS, LANES), jnp.float32),
         ),
@@ -829,9 +908,13 @@
             *grad_key_values,
         ),
         (),
-        (ffn_three, ffn_one),
-    )
-    grads_attention = scatter_blocks(attention_pieces, *sum_cores(*grads_attention))
+        (ffn_sums[1],),
+    )
+    grads_ffn = scatter_end(ffn_pieces, *ffn_sums)
+    attention_started, _ = scatter_start(attention_pieces, *grads_attention)
+    grads_attention = scatter_end(
+        attention_pieces, *scatter_middle(attention_pieces, attention_started)
+    )
     gain_grads = grads_attention[attention_rows:].reshape(-1)[: gains.shape[0]]
     grads_local = jnp.concatenate([grads_attention[:attention_rows], grads_ffn])
     return (

time: 261 us -> 254 us (0.973)
  other arithmetic: 27.5 us -> 8.48 us
  Pallas kernels: 55.9 us -> 67.9 us
  starting transfers between devices: 59.4 us -> 48.8 us
  waiting for transfers between devices: 95.8 us -> 106 us
    concatenate x7 -> x0, other arithmetic: 13.7 us -> none  [the longest x2 12 us: gather_diagonal(): three = jnp.concatenate([own, beside, across])]
    pallas_call x12 -> x15, Pallas kernels: 55.9 us -> 67.9 us  [local_call(): pl.pallas_call(body, out_shape=outs, in_specs=specs, out_specs=tuple((pl....]
    ppermute x36 -> x42, starting transfers between devices: 49.4 us -> 38.7 us  [swap(): lax.ppermute(value, ALL_AXES, [(source, source ^ mask) for source in rang...]
    ppermute x36 -> x42, waiting for transfers between devices: 94.1 us -> 104 us  [swap(): lax.ppermute(value, ALL_AXES, [(source, source ^ mask) for source in rang...]
    slice x10 -> x2, local copies, waits for them, and re-layouts: 7.76 us -> 1.02 us  [the longest x1 0.94 us: shards_blocks(): master[:attention_rows].astype(jnp.bfloat16)]
    another operation x8 -> x2, other arithmetic: 6.93 us -> 0.34 us
    unnamed x94 -> x112, local copies, waits for them, and re-layouts: 9.15 us -> 15.7 us
  transfers between devices with their start and end apart: 42 -> 48, of which waited for: 16 -> 22; matrix products, arithmetic and copies ran while one was open for 13% -> 4% of each run, Pallas kernels for 13% -> 17%
where the time goes in v6:
time: 254 us; the launch traced here: 253 us
  waiting for transfers between devices  106 us (42%)
  Pallas kernels  67.9 us (27%)
  starting transfers between devices  48.8 us (19%)
  local copies, waits for them, and re-layouts  21.3 us (8%)
  other arithmetic  8.48 us (3%)
    ppermute x42, waiting for transfers between devices, swap(): lax.ppermute(value, ALL_AXES, [(source, source ^ mask) for source in rang...  104 us
    pallas_call x15, Pallas kernels, local_call(): pl.pallas_call(body, out_shape=outs, in_specs=specs, out_specs=tuple((pl....  67.9 us
    ppermute x42, starting transfers between devices, swap(): lax.ppermute(value, ALL_AXES, [(source, source ^ mask) for source in rang...  38.7 us
    unnamed x112, local copies, waits for them, and re-layouts  15.7 us
    ppermute x6, starting transfers between devices, shifted(): lax.ppermute(value, axis, [(source, source + steps) for source in range(i...  10.1 us
  transfers between devices with their start and end apart: 48, of which 22 were waited for; matrix products, arithmetic and copies ran while one was open for 4% of the time, Pallas kernels for 17%

profile of v6, /device:TPU:0, one launch (start us, length us, event | category | flops | bytes accessed | tf_op | source)
XLA Modules:
  0.0 253.5 jit_solution(6262086312683855279)
XLA Ops:
  1.6 5.1 %collective-permute-start.2 = (bf16[400,128]{1,0:T(8,128)(2,1)S(1)}, bf16[400,128]{1,0:T(8,128)(2,1)S(1)}, u32[]{:S(2)}, u32[]{:S(2)}) collective-permute-start(bf16[400,128]{1,0:T(8,128)(2,1)S(1)} %slice.74.refs_1_), channel_id=1, source_target_pairs={{0,24},{1,25},{2,26},{3,27},{4,28},{5,29},{6,30},{7,31},{8,16},{9,... | collective-permute-start | bytes 307208 | tf_op jit(solution)/shard_map/ppermute | solution.py:126
  10.5 4.8 %collective-permute-done.1.refs_3_ = bf16[400,128]{1,0:T(8,128)(2,1)S(1)} collective-permute-done((bf16[400,128]{1,0:T(8,128)(2,1)S(1)}, bf16[400,128]{1,0:T(8,128)(2,1)S(1)}, u32[]{:S(2)}, u32[]{:S(2)}) %collective-permute-start.1) | collective-permute-done | bytes 102432 | tf_op jit(solution)/shard_map/ppermute | solution.py:126
  16.0 2.3 shard_map.152
  21.8 2.1 collective-permute-start.14
  25.7 5.7 %collective-permute-done.5.refs_3_.refs_2_ = bf16[960,128]{1,0:T(8,128)(2,1)S(1)} collective-permute-done((bf16[960,128]{1,0:T(8,128)(2,1)}, bf16[960,128]{1,0:T(8,128)(2,1)S(1)}, u32[]{:S(2)}, u32[]{:S(2)}) %collective-permute-start.5) | collective-permute-done | bytes 245792 | tf_op jit(solution)/shard_map/ppermute | solution.py:126
  36.1 9.0 %collective-permute-done.13.refs_3_ = bf16[960,128]{1,0:T(8,128)(2,1)S(1)} collective-permute-done((bf16[960,128]{1,0:T(8,128)(2,1)}, bf16[960,128]{1,0:T(8,128)(2,1)S(1)}, u32[]{:S(2)}, u32[]{:S(2)}) %collective-permute-start.13) | collective-permute-done | bytes 245792 | tf_op jit(solution)/shard_map/ppermute | solution.py:126
  46.4 3.0 %shard_map.154.refs_18_.refs_6_ = bf16[3840,128]{1,0:T(8,128)(2,1)} custom-call(s32[1]{0:T(128)} %bitcast.refs_0_, bf16[960,128]{1,0:T(8,128)(2,1)} %get-tuple-element.65.refs_1_, bf16[960,128]{1,0:T(8,128)(2,1)} %copy-done.25, bf16[960,128]{1,0:T(8,128)(2,1)} %copy-done.42, bf16[960,128]{1,0:T(8,128)(2,1)} %copy-done.41, bf16[800,128]{1,0:T(8,128)(2,1)} %copy-done.11), custom_call_target="tpu_custom_call" | custom-call | tf_op jit(solution)/shard_map/pallas_call | solution.py:138
  56.3 19.3 %collective-permute-done.7.refs_12_.refs_9_.refs_21_ = bf16[800,128]{1,0:T(8,128)(2,1)S(1)} collective-permute-done((bf16[800,128]{1,0:T(8,128)(2,1)S(1)}, bf16[800,128]{1,0:T(8,128)(2,1)S(1)}, u32[]{:S(2)}, u32[]{:S(2)}) %collective-permute-start.7) | collective-permute-done | bytes 204832 | tf_op jit(solution)/shard_map/ppermute | solution.py:126
  78.2 4.0 %shard_map.155 = (bf16[128,640]{1,0:T(8,128)(2,1)}, f32[128,1024]{1,0:T(8,128)}, f32[128,256]{1,0:T(8,128)}, bf16[128,1024]{1,0:T(8,128)(2,1)}, bf16[128,512]{1,0:T(8,128)(2,1)}) custom-call(s32[1]{0:T(128)} %bitcast.refs_0_, bf16[128,640]{1,0:T(8,128)(2,1)} %refs_1_.5, f32[1,640]{1,0:T(1,128)} %broadcast_in_dim.15.refs_2_, f32[1,256]{1,0:T(1,128)} %bitcast.25, ...), custom_call_target="tpu_custom_call" | custom-call | tf_op jit(solution)/shard_map/pallas_call | solution.py:138
  82.2 2.1 collective-permute-start.17
  84.3 2.4 collective-permute-start.16
  91.7 5.8 %shard_map.156 = (f32[128,2048]{1,0:T(8,128)}, bf16[128,1024]{1,0:T(8,128)(2,1)}, f32[128,640]{1,0:T(8,128)}, f32[128,640]{1,0:T(8,128)}, bf16[1024,640]{1,0:T(8,128)(2,1)}) custom-call(s32[1]{0:T(128)} %bitcast.refs_0_, bf16[128,640]{1,0:T(8,128)(2,1)} %refs_1_.5, f32[1,640]{1,0:T(1,128)} %broadcast_in_dim.14.refs_2_.refs_3_, f32[128,512]{1,0:T(8,128)} %fusion.4.refs_3_, ...), custom_call_target="tpu_custom_call" | custom-call | tf_op jit(solution)/shard_map/pallas_call | solution.py:138
  98.7 2.5 shard_map.157
  103.6 9.6 %collective-permute-done.20.refs_9_ = bf16[1920,128]{1,0:T(8,128)(2,1)S(1)} collective-permute-done((bf16[1920,128]{1,0:T(8,128)(2,1)}, bf16[1920,128]{1,0:T(8,128)(2,1)S(1)}, u32[]{:S(2)}, u32[]{:S(2)}) %collective-permute-start.20) | collective-permute-done | bytes 491552 | tf_op jit(solution)/shard_map/ppermute | solution.py:126
  113.2 2.5 collective-permute-done.21.refs_10_
  119.5 14.7 %shard_map.158 = (bf16[128,640]{1,0:T(8,128)(2,1)}, f32[128,640]{1,0:T(8,128)}, f32[1,640]{1,0:T(1,128)}, f32[1,640]{1,0:T(1,128)}, bf16[11520,128]{1,0:T(8,128)...) custom-call(s32[1]{0:T(128)} %bitcast.refs_0_, ...), custom_call_target="tpu_custom_call" | custom-call | tf_op jit(solution)/shard_map/pallas_call | solution.py:138
  134.7 6.5 %collective-permute-done.27.refs_2_.refs_4_ = bf16[3840,128]{1,0:T(8,128)(2,1)S(1)} collective-permute-done((bf16[3840,128]{1,0:T(8,128)(2,1)}, bf16[3840,128]{1,0:T(8,128)(2,1)S(1)}, u32[]{:S(2)}, u32[]{:S(2)}) %collective-permute-start.27) | collective-permute-done | bytes 983072 | tf_op jit(solution)/shard_map/ppermute | solution.py:126
  142.2 2.6 %shard_map.159 = (bf16[1920,128]{1,0:T(8,128)(2,1)}, bf16[1920,128]{1,0:T(8,128)(2,1)}) custom-call(s32[1]{0:T(128)} %bitcast.refs_0_, bf16[3840,128]{1,0:T(8,128)(2,1)} %get-tuple-element.82.refs_1_.refs_3_, bf16[3840,128]{1,0:T(8,128)(2,1)} %copy-done.7), custom_call_target="tpu_custom_call" | custom-call | tf_op jit(solution)/shard_map/pallas_call | solution.py:138
  148.0 6.2 %shard_map.160 = (bf16[1024,640]{1,0:T(8,128)(2,1)}, f32[128,1024]{1,0:T(8,128)}, f32[1,640]{1,0:T(1,128)}, bf16[128,512]{1,0:T(8,128)(2,1)}, bf16[128,512]{1,0:...) custom-call(s32[1]{0:T(128)} %bitcast.refs_0_, f32[128,640]{1,0:T(8,128)} %get-tuple-element.77.refs_1_.refs_12_, ...), custom_call_target="tpu_custom_call" | custom-call | tf_op jit(solution)/shard_map/pallas_call | solution.py:138
  161.8 5.7 %shard_map.161 = (f32[3840,128]{1,0:T(8,128)}, bf16[3840,128]{1,0:T(8,128)(2,1)}, bf16[3840,128]{1,0:T(8,128)(2,1)}, f32[8,128]{1,0:T(8,128)}) custom-call(s32[1]{0:T(128)} %bitcast.refs_0_, bf16[11520,128]{1,0:T(8,128)(2,1)} %get-tuple-element.94.refs_1_, bf16[11520,128]{1,0:T(8,128)(2,1)} %copy-done.13, ...), custom_call_target="tpu_custom_call" | custom-call | tf_op jit(solution)/shard_map/pallas_call | solution.py:138
  168.3 7.4 %shard_map.162 = (bf16[4800,128]{1,0:T(8,128)(2,1)}, bf16[1632,128]{1,0:T(8,128)(2,1)}, bf16[4800,128]{1,0:T(8,128)(2,1)}, bf16[1632,128]{1,0:T(8,128)(2,1)}, bf...) custom-call(s32[1]{0:T(128)} %bitcast.refs_0_, bf16[128,640]{1,0:T(8,128)(2,1)} %refs_1_.5, f32[1,640]{1,0:T(1,128)} %broadcast_in_dim.15.refs_2_, ...), custom_call_target="tpu_custom_call" | custom-call | tf_op jit(solution)/shard_map/pallas_call | solution.py:138
  180.1 2.0 collective-permute-done.35.refs_2_.refs_4_
  186.2 18.8 %collective-permute-done.37.refs_6_ = bf16[800,128]{1,0:T(8,128)(2,1)S(1)} collective-permute-done((bf16[800,128]{1,0:T(8,128)(2,1)}, bf16[800,128]{1,0:T(8,128)(2,1)S(1)}, u32[]{:S(2)}, u32[]{:S(2)}) %collective-permute-start.37) | collective-permute-done | bytes 204832 | tf_op jit(solution)/shard_map/ppermute | solution.py:126
  207.8 3.3 %shard_map.164 = (f32[1600,128]{1,0:T(8,128)}, bf16[1600,128]{1,0:T(8,128)(2,1)}, bf16[1632,128]{1,0:T(8,128)(2,1)}, f32[32,128]{1,0:T(8,128)}) custom-call(s32[1]{0:T(128)} %bitcast.refs_0_, bf16[4800,128]{1,0:T(8,128)(2,1)} %get-tuple-element.99.refs_1_, bf16[4800,128]{1,0:T(8,128)(2,1)} %copy-done.18, ...), custom_call_target="tpu_custom_call" | custom-call | tf_op jit(solution)/shard_map/pallas_call | solution.py:138
  214.2 4.3 %shard_map.166 = (f32[960,128]{1,0:T(8,128)}, bf16[960,128]{1,0:T(8,128)(2,1)}, bf16[960,128]{1,0:T(8,128)(2,1)}, bf16[960,128]{1,0:T(8,128)(2,1)}) custom-call(s32[1]{0:T(128)} %bitcast.refs_0_, f32[3840,128]{1,0:T(8,128)} %get-tuple-element.113.refs_1_, bf16[3840,128]{1,0:T(8,128)(2,1)} %copy-done.22, bf16[3840,128]{1,0:T(8,128)(2,1)} %copy-done.21, ...), custom_call_target="tpu_custom_call" | custom-call | tf_op jit(solution)/shard_map/pallas_call | solution.py:138
  218.5 2.4 collective-permute-start.46
  220.9 2.0 collective-permute-start.47
  223.8 2.5 shard_map.165
  226.4 2.3 collective-permute-start.41
  228.7 2.8 %collective-permute-done.45 = bf16[960,128]{1,0:T(8,128)(2,1)S(1)} collective-permute-done((bf16[960,128]{1,0:T(8,128)(2,1)}, bf16[960,128]{1,0:T(8,128)(2,1)S(1)}, u32[]{:S(2)}, u32[]{:S(2)}) %collective-permute-start.45) | collective-permute-done | bytes 245792 | tf_op jit(solution)/shard_map/ppermute | solution.py:126
  233.2 10.4 %collective-permute-done.46 = bf16[960,128]{1,0:T(8,128)(2,1)S(1)} collective-permute-done((bf16[960,128]{1,0:T(8,128)(2,1)}, bf16[960,128]{1,0:T(8,128)(2,1)S(1)}, u32[]{:S(2)}, u32[]{:S(2)}) %collective-permute-start.46) | collective-permute-done | bytes 245792 | tf_op jit(solution)/shard_map/ppermute | solution.py:126
  243.7 6.4 %collective-permute-done.41 = bf16[432,128]{1,0:T(8,128)(2,1)S(1)} collective-permute-done((bf16[432,128]{1,0:T(8,128)(2,1)}, bf16[432,128]{1,0:T(8,128)(2,1)S(1)}, u32[]{:S(2)}, u32[]{:S(2)}) %collective-permute-start.41) | collective-permute-done | bytes 110624 | tf_op jit(solution)/shard_map/ppermute | solution.py:126
  (219 shorter events, 72.0 us)
Async XLA Ops:
  18.3 13.1 %collective-permute-start.4 = (bf16[1600,128]{1,0:T(8,128)(2,1)}, bf16[1600,128]{1,0:T(8,128)(2,1)S(1)}, u32[]{:S(2)}, u32[]{:S(2)}) collective-permute-start(bf16[1600,128]{1,0:T(8,128)(2,1)} %get-tuple-element.64.refs_8_.refs_5_.refs_17_), channel_id=1, source_target_pairs={{0,2},{1,3},{2,0},{3,1},{4,6},{5,7},{6,4},{7,5},{8,10},{9,11},{10,... | collective-permute-start | bytes 1228808 | tf_op jit(solution)/shard_map/ppermute | solution.py:126
  19.8 11.6 %collective-permute-start.3 = (bf16[1600,128]{1,0:T(8,128)(2,1)}, bf16[1600,128]{1,0:T(8,128)(2,1)S(1)}, u32[]{:S(2)}, u32[]{:S(2)}) collective-permute-start(bf16[1600,128]{1,0:T(8,128)(2,1)} %get-tuple-element.64.refs_8_.refs_5_.refs_17_), channel_id=1, source_target_pairs={{0,4},{1,5},{2,6},{3,7},{4,0},{5,1},{6,2},{7,3},{8,12},{9,13},{10,... | collective-permute-start | bytes 1228808 | tf_op jit(solution)/shard_map/ppermute | solution.py:126
  21.8 14.3 %collective-permute-start.14 = (bf16[960,128]{1,0:T(8,128)(2,1)}, bf16[960,128]{1,0:T(8,128)(2,1)S(1)}, u32[]{:S(2)}, u32[]{:S(2)}) collective-permute-start(bf16[960,128]{1,0:T(8,128)(2,1)} %get-tuple-element.65.refs_1_), channel_id=1, source_target_pairs={{0,24},{1,25},{2,26},{3,27},{4,28},{5,29},{6,30},{7,31},{8,16},{9,... | collective-permute-start | bytes 737288 | tf_op jit(solution)/shard_map/ppermute | solution.py:126
  23.9 21.2 %collective-permute-start.13 = (bf16[960,128]{1,0:T(8,128)(2,1)}, bf16[960,128]{1,0:T(8,128)(2,1)S(1)}, u32[]{:S(2)}, u32[]{:S(2)}) collective-permute-start(bf16[960,128]{1,0:T(8,128)(2,1)} %get-tuple-element.65.refs_1_), channel_id=1, source_target_pairs={{0,16},{1,17},{2,18},{3,19},{4,20},{5,21},{6,22},{7,23},{8,24},{9,... | collective-permute-start | bytes 737288 | tf_op jit(solution)/shard_map/ppermute | solution.py:126
  35.5 19.6 %collective-permute-start.8 = (bf16[1600,128]{1,0:T(8,128)(2,1)}, bf16[1600,128]{1,0:T(8,128)(2,1)S(1)}, u32[]{:S(2)}, u32[]{:S(2)}) collective-permute-start(bf16[1600,128]{1,0:T(8,128)(2,1)} %get-tuple-element.64.refs_8_.refs_5_.refs_17_), channel_id=1, source_target_pairs={{0,1},{1,0},{2,3},{3,2},{4,5},{5,4},{6,7},{7,6},{8,9},{9,8},{10,11... | collective-permute-start | bytes 1228808 | tf_op jit(solution)/shard_map/ppermute | solution.py:126
  49.4 48.0 %collective-permute-start.19 = (bf16[3840,128]{1,0:T(8,128)(2,1)}, bf16[3840,128]{1,0:T(8,128)(2,1)S(1)}, u32[]{:S(2)}, u32[]{:S(2)}) collective-permute-start(bf16[3840,128]{1,0:T(8,128)(2,1)} %shard_map.154.refs_18_.refs_6_), channel_id=1, source_target_pairs={{0,2},{1,3},{2,0},{3,1},{4,6},{5,7},{6,4},{7,5},{8,10},{9,11},{10,... | collective-permute-start | bytes 2949128 | tf_op jit(solution)/shard_map/ppermute | solution.py:126
  49.9 47.5 %collective-permute-start.18 = (bf16[3840,128]{1,0:T(8,128)(2,1)}, bf16[3840,128]{1,0:T(8,128)(2,1)S(1)}, u32[]{:S(2)}, u32[]{:S(2)}) collective-permute-start(bf16[3840,128]{1,0:T(8,128)(2,1)} %shard_map.154.refs_18_.refs_6_), channel_id=1, source_target_pairs={{0,4},{1,5},{2,6},{3,7},{4,0},{5,1},{6,2},{7,3},{8,12},{9,13},{10,... | collective-permute-start | bytes 2949128 | tf_op jit(solution)/shard_map/ppermute | solution.py:126
  52.3 23.3 %collective-permute-start.10 = (bf16[1600,128]{1,0:T(8,128)(2,1)S(1)}, bf16[1600,128]{1,0:T(8,128)(2,1)S(1)}, u32[]{:S(2)}, u32[]{:S(2)}) collective-permute-start(bf16[1600,128]{1,0:T(8,128)(2,1)S(1)} %copy-done.2), channel_id=1, source_target_pairs={{0,1},{1,0},{2,3},{3,2},{4,5},{5,4},{6,7},{7,6},{8,9},{9,8},{10,11... | collective-permute-start | bytes 1228808 | tf_op jit(solution)/shard_map/ppermute | solution.py:126
  53.5 22.1 %collective-permute-start.7 = (bf16[800,128]{1,0:T(8,128)(2,1)S(1)}, bf16[800,128]{1,0:T(8,128)(2,1)S(1)}, u32[]{:S(2)}, u32[]{:S(2)}) collective-permute-start(bf16[800,128]{1,0:T(8,128)(2,1)S(1)} %copy-done.55), channel_id=1, source_target_pairs={{0,2},{1,3},{2,0},{3,1},{4,6},{5,7},{6,4},{7,5},{8,10},{9,11},{10,... | collective-permute-start | bytes 614408 | tf_op jit(solution)/shard_map/ppermute | solution.py:126
  55.1 22.3 %collective-permute-start.9 = (bf16[1600,128]{1,0:T(8,128)(2,1)S(1)}, bf16[1600,128]{1,0:T(8,128)(2,1)S(1)}, u32[]{:S(2)}, u32[]{:S(2)}) collective-permute-start(bf16[1600,128]{1,0:T(8,128)(2,1)S(1)} %copy-done.4), channel_id=1, source_target_pairs={{0,1},{1,0},{2,3},{3,2},{4,5},{5,4},{6,7},{7,6},{8,9},{9,8},{10,11... | collective-permute-start | bytes 1228808 | tf_op jit(solution)/shard_map/ppermute | solution.py:126
  89.1 27.9 %collective-permute-start.22 = (bf16[3840,128]{1,0:T(8,128)(2,1)S(1)}, bf16[3840,128]{1,0:T(8,128)(2,1)S(1)}, u32[]{:S(2)}, u32[]{:S(2)}) collective-permute-start(bf16[3840,128]{1,0:T(8,128)(2,1)S(1)} %copy-done), channel_id=1, source_target_pairs={{0,1},{1,0},{2,3},{3,2},{4,5},{5,4},{6,7},{7,6},{8,9},{9,8},{10,11... | collective-permute-start | bytes 2949128 | tf_op jit(solution)/shard_map/ppermute | solution.py:126
  101.2 12.0 %collective-permute-start.20 = (bf16[1920,128]{1,0:T(8,128)(2,1)}, bf16[1920,128]{1,0:T(8,128)(2,1)S(1)}, u32[]{:S(2)}, u32[]{:S(2)}) collective-permute-start(bf16[1920,128]{1,0:T(8,128)(2,1)} %get-tuple-element.71), channel_id=1, source_target_pairs={{0,4},{1,5},{2,6},{3,7},{4,0},{5,1},{6,2},{7,3},{8,12},{9,13},{10,... | collective-permute-start | bytes 1474568 | tf_op jit(solution)/shard_map/ppermute | solution.py:126
  101.7 15.3 %collective-permute-start.24 = (bf16[3840,128]{1,0:T(8,128)(2,1)}, bf16[3840,128]{1,0:T(8,128)(2,1)S(1)}, u32[]{:S(2)}, u32[]{:S(2)}) collective-permute-start(bf16[3840,128]{1,0:T(8,128)(2,1)} %copy-done.5), channel_id=1, source_target_pairs={{0,1},{1,0},{2,3},{3,2},{4,5},{5,4},{6,7},{7,6},{8,9},{9,8},{10,11... | collective-permute-start | bytes 2949128 | tf_op jit(solution)/shard_map/ppermute | solution.py:126
  101.7 15.3 %collective-permute-start.23 = (bf16[3840,128]{1,0:T(8,128)(2,1)}, bf16[3840,128]{1,0:T(8,128)(2,1)S(1)}, u32[]{:S(2)}, u32[]{:S(2)}) collective-permute-start(bf16[3840,128]{1,0:T(8,128)(2,1)} %copy-done.6), channel_id=1, source_target_pairs={{0,1},{1,0},{2,3},{3,2},{4,5},{5,4},{6,7},{7,6},{8,9},{9,8},{10,11... | collective-permute-start | bytes 2949128 | tf_op jit(solution)/shard_map/ppermute | solution.py:126
  102.2 13.5 %collective-permute-start.21 = (bf16[1920,128]{1,0:T(8,128)(2,1)}, bf16[1920,128]{1,0:T(8,128)(2,1)S(1)}, u32[]{:S(2)}, u32[]{:S(2)}) collective-permute-start(bf16[1920,128]{1,0:T(8,128)(2,1)} %get-tuple-element.72), channel_id=1, source_target_pairs={{0,2},{1,3},{2,0},{3,1},{4,6},{5,7},{6,4},{7,5},{8,10},{9,11},{10,... | collective-permute-start | bytes 1474568 | tf_op jit(solution)/shard_map/ppermute | solution.py:126
  134.2 25.9 %collective-permute-start.31 = (bf16[11520,128]{1,0:T(8,128)(2,1)}, bf16[11520,128]{1,0:T(8,128)(2,1)S(1)}, u32[]{:S(2)}, u32[]{:S(2)}) collective-permute-start(bf16[11520,128]{1,0:T(8,128)(2,1)} %get-tuple-element.95), channel_id=1, source_target_pairs={{0,1},{1,0},{2,3},{3,2},{4,5},{5,4},{6,7},{7,6},{8,9},{9,8},{10,11... | collective-permute-start | bytes 8847368 | tf_op jit(solution)/shard_map/ppermute | solution.py:126
  144.8 13.7 %collective-permute-start.32 = (bf16[1920,128]{1,0:T(8,128)(2,1)}, bf16[1920,128]{1,0:T(8,128)(2,1)S(1)}, u32[]{:S(2)}, u32[]{:S(2)}) collective-permute-start(bf16[1920,128]{1,0:T(8,128)(2,1)} %get-tuple-element.96), channel_id=1, source_target_pairs={{0,4},{1,5},{2,6},{3,7},{4,0},{5,1},{6,2},{7,3},{8,12},{9,13},{10,... | collective-permute-start | bytes 1474568 | tf_op jit(solution)/shard_map/ppermute | solution.py:126
  146.3 13.8 %collective-permute-start.33 = (bf16[1920,128]{1,0:T(8,128)(2,1)}, bf16[1920,128]{1,0:T(8,128)(2,1)S(1)}, u32[]{:S(2)}, u32[]{:S(2)}) collective-permute-start(bf16[1920,128]{1,0:T(8,128)(2,1)} %get-tuple-element.84.refs_12_), channel_id=1, source_target_pairs={{0,2},{1,3},{2,0},{3,1},{4,6},{5,7},{6,4},{7,5},{8,10},{9,11},{10,... | collective-permute-start | bytes 1474568 | tf_op jit(solution)/shard_map/ppermute | solution.py:126
  154.2 13.3 %collective-permute-start.28 = (bf16[128,512]{1,0:T(8,128)(2,1)}, bf16[128,512]{1,0:T(8,128)(2,1)S(1)}, u32[]{:S(2)}, u32[]{:S(2)}) collective-permute-start(bf16[128,512]{1,0:T(8,128)(2,1)} %get-tuple-element.90), channel_id=1, source_target_pairs={{3,0},{7,4},{11,8},{15,12},{19,16},{23,20},{27,24},{31,28}} | collective-permute-start | bytes 393224 | tf_op jit(solution)/shard_map/ppermute | solution.py:33
  155.5 12.1 %collective-permute-start.29 = (bf16[128,512]{1,0:T(8,128)(2,1)}, bf16[128,512]{1,0:T(8,128)(2,1)S(1)}, u32[]{:S(2)}, u32[]{:S(2)}) collective-permute-start(bf16[128,512]{1,0:T(8,128)(2,1)} %get-tuple-element.91), channel_id=1, source_target_pairs={{2,0},{3,1},{6,4},{7,5},{10,8},{11,9},{14,12},{15,13},{18,16},{19,... | collective-permute-start | bytes 393224 | tf_op jit(solution)/shard_map/ppermute | solution.py:33
  175.7 31.0 %collective-permute-start.34 = (bf16[4800,128]{1,0:T(8,128)(2,1)}, bf16[4800,128]{1,0:T(8,128)(2,1)S(1)}, u32[]{:S(2)}, u32[]{:S(2)}) collective-permute-start(bf16[4800,128]{1,0:T(8,128)(2,1)} %get-tuple-element.100), channel_id=1, source_target_pairs={{0,1},{1,0},{2,3},{3,2},{4,5},{5,4},{6,7},{7,6},{8,9},{9,8},{10,11... | collective-permute-start | bytes 3686408 | tf_op jit(solution)/shard_map/ppermute | solution.py:126
  176.9 36.0 %collective-permute-start.44 = (bf16[3840,128]{1,0:T(8,128)(2,1)S(1)}, bf16[3840,128]{1,0:T(8,128)(2,1)S(1)}, u32[]{:S(2)}, u32[]{:S(2)}) collective-permute-start(bf16[3840,128]{1,0:T(8,128)(2,1)S(1)} %copy-done.54), channel_id=1, source_target_pairs={{0,2},{1,3},{2,0},{3,1},{4,6},{5,7},{6,4},{7,5},{8,10},{9,11},{10,... | collective-permute-start | bytes 2949128 | tf_op jit(solution)/shard_map/ppermute | solution.py:126
  178.6 34.3 %collective-permute-start.43 = (bf16[3840,128]{1,0:T(8,128)(2,1)S(1)}, bf16[3840,128]{1,0:T(8,128)(2,1)S(1)}, u32[]{:S(2)}, u32[]{:S(2)}) collective-permute-start(bf16[3840,128]{1,0:T(8,128)(2,1)S(1)} %copy-done.19), channel_id=1, source_target_pairs={{0,4},{1,5},{2,6},{3,7},{4,0},{5,1},{6,2},{7,3},{8,12},{9,13},{10,... | collective-permute-start | bytes 2949128 | tf_op jit(solution)/shard_map/ppermute | solution.py:126
  184.8 21.9 %collective-permute-start.36 = (bf16[832,128]{1,0:T(8,128)(2,1)}, bf16[832,128]{1,0:T(8,128)(2,1)S(1)}, u32[]{:S(2)}, u32[]{:S(2)}) collective-permute-start(bf16[832,128]{1,0:T(8,128)(2,1)} %get-tuple-element.103), channel_id=1, source_target_pairs={{0,4},{1,5},{2,6},{3,7},{4,0},{5,1},{6,2},{7,3},{8,12},{9,13},{10,... | collective-permute-start | bytes 638984 | tf_op jit(solution)/shard_map/ppermute | solution.py:126
  185.3 19.7 %collective-permute-start.37 = (bf16[800,128]{1,0:T(8,128)(2,1)}, bf16[800,128]{1,0:T(8,128)(2,1)S(1)}, u32[]{:S(2)}, u32[]{:S(2)}) collective-permute-start(bf16[800,128]{1,0:T(8,128)(2,1)} %get-tuple-element.104), channel_id=1, source_target_pairs={{0,2},{1,3},{2,0},{3,1},{4,6},{5,7},{6,4},{7,5},{8,10},{9,11},{10,... | collective-permute-start | bytes 614408 | tf_op jit(solution)/shard_map/ppermute | solution.py:126
  211.1 11.8 %collective-permute-start.39 = (bf16[1632,128]{1,0:T(8,128)(2,1)}, bf16[1632,128]{1,0:T(8,128)(2,1)S(1)}, u32[]{:S(2)}, u32[]{:S(2)}) collective-permute-start(bf16[1632,128]{1,0:T(8,128)(2,1)} %get-tuple-element.107), channel_id=1, source_target_pairs={{0,2},{1,3},{2,0},{3,1},{4,6},{5,7},{6,4},{7,5},{8,10},{9,11},{10,... | collective-permute-start | bytes 1253384 | tf_op jit(solution)/shard_map/ppermute | solution.py:126
  218.5 13.0 %collective-permute-start.45 = (bf16[960,128]{1,0:T(8,128)(2,1)}, bf16[960,128]{1,0:T(8,128)(2,1)S(1)}, u32[]{:S(2)}, u32[]{:S(2)}) collective-permute-start(bf16[960,128]{1,0:T(8,128)(2,1)} %get-tuple-element.117), channel_id=1, source_target_pairs={{0,8},{1,9},{2,10},{3,11},{4,12},{5,13},{6,14},{7,15},{8,0},{9,1},... | collective-permute-start | bytes 737288 | tf_op jit(solution)/shard_map/ppermute | solution.py:126
  218.5 25.1 %collective-permute-start.46 = (bf16[960,128]{1,0:T(8,128)(2,1)}, bf16[960,128]{1,0:T(8,128)(2,1)S(1)}, u32[]{:S(2)}, u32[]{:S(2)}) collective-permute-start(bf16[960,128]{1,0:T(8,128)(2,1)} %get-tuple-element.118), channel_id=1, source_target_pairs={{0,16},{1,17},{2,18},{3,19},{4,20},{5,21},{6,22},{7,23},{8,24},{9,... | collective-permute-start | bytes 737288 | tf_op jit(solution)/shard_map/ppermute | solution.py:126
  220.9 22.8 %collective-permute-start.47 = (bf16[960,128]{1,0:T(8,128)(2,1)}, bf16[960,128]{1,0:T(8,128)(2,1)S(1)}, u32[]{:S(2)}, u32[]{:S(2)}) collective-permute-start(bf16[960,128]{1,0:T(8,128)(2,1)} %get-tuple-element.119), channel_id=1, source_target_pairs={{0,24},{1,25},{2,26},{3,27},{4,28},{5,29},{6,30},{7,31},{8,16},{9,... | collective-permute-start | bytes 737288 | tf_op jit(solution)/shard_map/ppermute | solution.py:126
  226.3 17.4 %collective-permute-start.40 = (bf16[432,128]{1,0:T(8,128)(2,1)}, bf16[432,128]{1,0:T(8,128)(2,1)S(1)}, u32[]{:S(2)}, u32[]{:S(2)}) collective-permute-start(bf16[432,128]{1,0:T(8,128)(2,1)} %get-tuple-element.110), channel_id=1, source_target_pairs={{0,8},{1,9},{2,10},{3,11},{4,12},{5,13},{6,14},{7,15},{8,0},{9,1},... | collective-permute-start | bytes 331784 | tf_op jit(solution)/shard_map/ppermute | solution.py:126
  226.4 23.8 %collective-permute-start.41 = (bf16[432,128]{1,0:T(8,128)(2,1)}, bf16[432,128]{1,0:T(8,128)(2,1)S(1)}, u32[]{:S(2)}, u32[]{:S(2)}) collective-permute-start(bf16[432,128]{1,0:T(8,128)(2,1)} %get-tuple-element.111), channel_id=1, source_target_pairs={{0,16},{1,17},{2,18},{3,19},{4,20},{5,21},{6,22},{7,23},{8,24},{9,... | collective-permute-start | bytes 331784 | tf_op jit(solution)/shard_map/ppermute | solution.py:126
  231.5 18.6 %collective-permute-start.42 = (bf16[432,128]{1,0:T(8,128)(2,1)}, bf16[432,128]{1,0:T(8,128)(2,1)S(1)}, u32[]{:S(2)}, u32[]{:S(2)}) collective-permute-start(bf16[432,128]{1,0:T(8,128)(2,1)} %get-tuple-element.112), channel_id=1, source_target_pairs={{0,24},{1,25},{2,26},{3,27},{4,28},{5,29},{6,30},{7,31},{8,16},{9,... | collective-permute-start | bytes 331784 | tf_op jit(solution)/shard_map/ppermute | solution.py:126
  (72 other events, 474.5 us)

commit v7 on v6

--- a/solution.py
+++ b/solution.py
@@ -159,18 +159,20 @@
         self.size = self.block_rows * self.blocks
 
 
-def halves_kernel(index_ref, first_ref, second_ref, first_out_ref, second_out_ref):
-    half = first_out_ref.shape[0]
-    first_out_ref[...] = first_ref[:half, :]
-    second_out_ref[...] = second_ref[half:, :]
-
-
-def pack_kernel(pieces, later_count, index_ref, *refs):
+def round_kernel(index_ref, in_ref, out_ref):
+    out_ref[...] = in_ref[in_ref.shape[0] - out_ref.shape[0] :, :].astype(jnp.bfloat16)
+
+
+def join_kernel(index_ref, *refs):
+    out_ref = refs[-1]
+    rows = refs[0].shape[0]
+    for place, ref in enumerate(refs[:-1]):
+        out_ref[place * rows : (place + 1) * rows, :] = ref[...]
+
+
+def pack_kernel(pieces, index_ref, *refs):
     high_count = pieces[0].high_count
-    parts, out_ref, flat, packed = refs[:high_count], refs[-3], refs[-2], refs[-1]
-    if later_count:
-        later_ref, out_ref = refs[high_count], refs[high_count + 1]
-        refs[-3][...] = later_ref[later_ref.shape[0] - later_count :, :].astype(jnp.bfloat16)
+    parts, out_refs, flat, packed = refs[:high_count], refs[-4:-2], refs[-2], refs[-1]
     high = index_ref[0] // LOW_COUNT
     for step, part in enumerate(parts):
         flat[high ^ step] = part[...].astype(jnp.float32)
@@ -183,7 +185,9 @@
                 ]
                 target = target + piece.own_rows
         start = start + piece.flat_rows
-    out_ref[...] = packed[...].astype(jnp.bfloat16)
+    half = target // 2
+    for place, out_ref in enumerate(out_refs):
+        out_ref[...] = packed[place * half : (place + 1) * half, :].astype(jnp.bfloat16)
 
 
 def sum_one_kernel(size, index_ref, near_ref, far_ref, to_x_ref, to_y_ref):
@@ -200,49 +204,76 @@
     index_ref,
     near_ref,
     far_ref,
-    near_extra_ref,
-    far_extra_ref,
+    own_ref,
+    beside_first_ref,
+    beside_second_ref,
+    across_first_ref,
+    across_second_ref,
+):
+    half = size // 2
+    outs = (beside_first_ref, beside_second_ref, across_first_ref, across_second_ref)
+    own_ref[...] = near_ref[:size, :].astype(jnp.float32) + far_ref[:size, :].astype(jnp.float32)
+    for place, out_ref in enumerate(outs):
+        rows = slice(size + place * half, size + (place + 1) * half)
+        total = near_ref[rows, :].astype(jnp.float32) + far_ref[rows, :].astype(jnp.float32)
+        out_ref[...] = total.astype(out_ref.dtype)
+
+
+def sum_passed_kernel(
+    size,
+    index_ref,
+    beside_ref,
+    across_ref,
     over_x_ref,
     over_y_ref,
-    own_ref,
-    beside_ref,
-    across_ref,
+    near_one_ref,
+    far_one_ref,
+    beside_out_ref,
+    across_out_ref,
     extra_ref,
 ):
     half = size // 2
-
-    def both(first, last):
-        return near_ref[first:last, :].astype(jnp.float32) + far_ref[first:last, :].astype(
-            jnp.float32
-        )
-
-    own_ref[...] = both(0, size)
-    beside_ref[:half, :] = both(size, size + half).astype(jnp.bfloat16)
-    beside_ref[half:, :] = (
-        both(size + half, 2 * size) + over_y_ref[...].astype(jnp.float32)
+    beside_out_ref[...] = (beside_ref[...] + over_y_ref[...].astype(jnp.float32)).astype(
+        jnp.bfloat16
+    )
+    across_out_ref[:half, :] = (
+        across_ref[...] + over_x_ref[:half, :].astype(jnp.float32)
     ).astype(jnp.bfloat16)
-    across_ref[:half, :] = (
-        both(2 * size, 2 * size + half) + over_x_ref[:half, :].astype(jnp.float32)
-    ).astype(jnp.bfloat16)
-    across_ref[half:size, :] = both(2 * size + half, 3 * size).astype(jnp.bfloat16)
-    if across_ref.shape[0] > size:
-        extra = near_extra_ref[size:, :].astype(jnp.float32)
-        extra = extra + far_extra_ref[size:, :].astype(jnp.float32)
+    if across_out_ref.shape[0] > half:
+        extra = near_one_ref[size:, :].astype(jnp.float32)
+        extra = extra + far_one_ref[size:, :].astype(jnp.float32)
         extra = extra + over_x_ref[half:, :].astype(jnp.float32)
         extra_ref[...] = extra
-        across_ref[size:, :] = extra.astype(jnp.bfloat16)
+        across_out_ref[half:, :] = extra.astype(jnp.bfloat16)
     else:
         extra_ref[...] = jnp.zeros(extra_ref.shape, jnp.float32)
 
 
-def unpack_kernel(pieces, index_ref, own_ref, beside_ref, across_ref, extra_ref, *refs):
+def unpack_kernel(
+    pieces,
+    index_ref,
+    own_ref,
+    beside_first_ref,
+    beside_second_ref,
+    across_first_ref,
+    across_second_ref,
+    extra_ref,
+    *refs,
+):
     high_count = pieces[0].high_count
-    size = sum(piece.size for piece in pieces)
+    half = sum(piece.size for piece in pieces) // 2
     flat_rows = sum(piece.flat_rows for piece in pieces)
     outs, flat, packed = refs[:-2], refs[-2], refs[-1]
     high = index_ref[0] // LOW_COUNT
-    packed[...] = (
-        own_ref[...] + beside_ref[...].astype(jnp.float32) + across_ref[:size, :].astype(jnp.float32)
+    packed[:half, :] = (
+        own_ref[:half, :]
+        + beside_first_ref[...].astype(jnp.float32)
+        + across_first_ref[:half, :].astype(jnp.float32)
+    )
+    packed[half:, :] = (
+        own_ref[half:, :]
+        + beside_second_ref[...].astype(jnp.float32)
+        + across_second_ref[...].astype(jnp.float32)
     )
     start, source = 0, 0
     for piece in pieces:
@@ -256,7 +287,7 @@
     for step, out_ref in enumerate(outs):
         out_ref[:flat_rows, :] = flat[high ^ step].astype(out_ref.dtype)
         if out_ref.shape[0] > flat_rows:
-            extra = extra_ref[...] + across_ref[size:, :].astype(jnp.float32)
+            extra = extra_ref[...] + across_first_ref[half:, :].astype(jnp.float32)
             out_ref[flat_rows:, :] = extra.astype(out_ref.dtype)
 
 
@@ -264,21 +295,24 @@
     return jax.ShapeDtypeStruct(shape, kind)
 
 
-def gather_high(rows):
+def gather_high(rows, doubling):
     high_count = lax.axis_size(ALL_AXES) // LOW_COUNT
-    return [rows] + [swap(rows, step * LOW_COUNT) for step in range(1, high_count)]
-
-
-def gather_near(pieces, parts, later=None, later_count=0, behind=()):
+    if not doubling:
+        return [rows] + [swap(rows, step * LOW_COUNT) for step in range(1, high_count)]
+    parts = {0: rows}
+    mask = high_count // 2
+    while mask:
+        parts.update({step | mask: swap(value, mask * LOW_COUNT) for step, value in parts.items()})
+        mask = mask // 2
+    return [parts[step] for step in range(high_count)]
+
+
+def gather_near(pieces, parts, behind=()):
     high_count = pieces[0].high_count
     size = sum(piece.size for piece in pieces)
-    outs = (array((size, LANES), jnp.bfloat16),)
-    if later_count:
-        parts = (*parts, later)
-        outs = outs + (array((later_count, LANES), jnp.bfloat16),)
-    own, *rounded = local_call(
-        functools.partial(pack_kernel, pieces, later_count),
-        outs,
+    first, second = local_call(
+        functools.partial(pack_kernel, pieces),
+        (array((size // 2, LANES), jnp.bfloat16),) * 2,
         parts,
         (
             pltpu.VMEM((high_count, parts[0].shape[0], LANES), jnp.float32),
@@ -286,63 +320,101 @@
         ),
         behind,
     )
-    return (own, swap(own, 4), swap(own, 2)), *rounded
-
-
-def gather_diagonal(own, beside, across, behind=()):
-    half = own.shape[0] // 2
-    to_x, to_y = local_call(
-        halves_kernel,
-        (array((half, LANES), jnp.bfloat16),) * 2,
-        (across, beside),
+    beside_second, across_first = swap(second, 4), swap(first, 2)
+    beside_first, across_second = swap(first, 4), swap(second, 2)
+    return (
+        (first, second, beside_first, beside_second, across_first, across_second),
+        (swap(across_first, 4), swap(beside_second, 2)),
+    )
+
+
+def gather_cores(three, diagonal, behind=()):
+    (three,) = local_call(
+        join_kernel,
+        (array((6 * three[0].shape[0], LANES), jnp.bfloat16),),
+        three,
         (),
         behind,
     )
-    near = (own, beside, across, swap(to_x, 4), swap(to_y, 2))
+    near = (three, *diagonal)
     return near + tuple(swap(value, 1) for value in near)
 
 
-def scatter_start(pieces, near_three, near_one, far_three, far_one):
-    size = sum(piece.size for piece in pieces)
+def scatter_cores(far_three, far_one):
     far_one = swap(far_one, 1)
-    far_three = swap(far_three, 1)
-    half = size // 2
+    return swap(far_three, 1), far_one
+
+
+def scatter_one(pieces, near_one, far_one, behind=()):
+    half = sum(piece.size for piece in pieces) // 2
     to_x, to_y = local_call(
-        functools.partial(sum_one_kernel, size),
+        functools.partial(sum_one_kernel, 2 * half),
         (
             array((near_one.shape[0] - half, LANES), jnp.bfloat16),
             array((half, LANES), jnp.bfloat16),
         ),
         (near_one, far_one),
-    )
-    return (near_three, far_three, near_one, far_one, swap(to_x, 4), swap(to_y, 2)), to_y
-
-
-def scatter_middle(pieces, started):
+        (),
+        behind,
+    )
+    return swap(to_x, 4), swap(to_y, 2), to_y
+
+
+def scatter_three(pieces, near_three, far_three, behind=()):
     size = sum(piece.size for piece in pieces)
-    extra_count = started[2].shape[0] - size
-    return local_call(
+    half = size // 2
+    own, beside_first, beside_second, across_first, across_second = local_call(
         functools.partial(sum_three_kernel, size),
         (
             array((size, LANES), jnp.float32),
-            array((size, LANES), jnp.bfloat16),
-            array((size + extra_count, LANES), jnp.bfloat16),
+            array((half, LANES), jnp.bfloat16),
+            array((half, LANES), jnp.float32),
+            array((half, LANES), jnp.float32),
+            array((half, LANES), jnp.bfloat16),
+        ),
+        (near_three, far_three),
+        (),
+        behind,
+    )
+    return own, swap(beside_first, 4), beside_second, across_first, swap(across_second, 2)
+
+
+def scatter_passed(pieces, threes, over_x, over_y, near_one, far_one, behind=()):
+    size = sum(piece.size for piece in pieces)
+    extra_count = near_one.shape[0] - size
+    own, beside_first, beside_second, across_first, across_second = threes
+    beside_second, across_first, extra = local_call(
+        functools.partial(sum_passed_kernel, size),
+        (
+            array((size // 2, LANES), jnp.bfloat16),
+            array((size // 2 + extra_count, LANES), jnp.bfloat16),
             array((max(extra_count, 8), LANES), jnp.float32),
         ),
-        started,
-    )
-
-
-def scatter_end(pieces, own, beside, across, extra):
+        (beside_second, across_first, over_x, over_y, near_one, far_one),
+        (),
+        behind,
+    )
+    terms = (
+        own,
+        beside_first,
+        swap(beside_second, 4),
+        swap(across_first, 2),
+        across_second,
+        extra,
+    )
+    return terms, beside_second
+
+
+def scatter_high(pieces, terms):
     high_count = pieces[0].high_count
     size = sum(piece.size for piece in pieces)
     flat_rows = sum(piece.flat_rows for piece in pieces)
-    out_rows = flat_rows + across.shape[0] - size
+    out_rows = flat_rows + terms[3].shape[0] - size // 2
     outs = local_call(
         functools.partial(unpack_kernel, pieces),
         (array((out_rows, LANES), jnp.float32),)
         + (array((out_rows, LANES), jnp.bfloat16),) * (high_count - 1),
-        (own, swap(beside, 4), swap(across, 2), extra),
+        terms,
         (
             pltpu.VMEM((high_count, flat_rows, LANES), jnp.float32),
             pltpu.VMEM((size, LANES), jnp.float32),
@@ -380,10 +452,12 @@
 
 
 def weight_rows(refs, size, order, start, rows):
-    refs = refs[:5] if order < 4 else refs[5:]
-    ref = refs[order % 4]
-    if order % 4 == 3 and 2 * start >= size:
-        ref, start = refs[4], start - size // 2
+    three, *diagonal = refs[:3] if order < 4 else refs[3:]
+    if order % 4 == 3:
+        second = int(2 * start >= size)
+        ref, start = diagonal[second], start - second * (size // 2)
+    else:
+        ref, start = three, order % 4 * size + start
     return ref[start : start + rows, :]
 
 
@@ -431,9 +505,9 @@
     order_ref,
     *refs,
 ):
-    weight_refs, grad_refs = refs[:10], refs[14:18]
-    block_out_ref, grad_middle_ref, grad_gain_in_ref, grad_gain_out_ref = refs[10:14]
-    down_ref, hidden_ref, gelu_ref, slope_ref = refs[18:]
+    weight_refs, grad_refs = refs[:6], refs[10:14]
+    block_out_ref, grad_middle_ref, grad_gain_in_ref, grad_gain_out_ref = refs[6:10]
+    down_ref, hidden_ref, gelu_ref, slope_ref = refs[14:]
     low = index_ref[0] % LOW_COUNT
     rows = gate_piece.block_rows
     size = 2 * gate_piece.size + down_piece.size
@@ -573,8 +647,8 @@
     order_ref,
     *refs,
 ):
-    weight_refs = refs[:10]
-    normed_ref, query_proj_ref, key_proj_ref, query_ref, key_value_ref = refs[10:]
+    weight_refs = refs[:6]
+    normed_ref, query_proj_ref, key_proj_ref, query_ref, key_value_ref = refs[6:]
     size = sum(piece.size for piece in pieces)
     rows = pieces[0].block_rows
     cosine, sine = cosine_ref[...], sine_ref[...]
@@ -609,7 +683,7 @@
     query_ref,
     *refs,
 ):
-    weight_refs, key_value_refs = refs[:10], refs[10:-5]
+    weight_refs, key_value_refs = refs[:6], refs[6:-5]
     probs_ref, attended_ref, attn_out_ref, middle_ref, out_weight_ref = refs[-5:]
     out_piece = pieces[-1]
     low = index_ref[0] % LOW_COUNT
@@ -680,55 +754,79 @@
         ref[:, HD:] = grad_values[part * rows : (part + 1) * rows].astype(ref.dtype)
 
 
+def query_back_kernel(
+    pieces,
+    index_ref,
+    gain_ref,
+    cosine_ref,
+    sine_ref,
+    normed_ref,
+    query_proj_ref,
+    grad_query_ref,
+    *refs,
+):
+    weight_refs = refs[:6]
+    grad_weight_ref, grad_normed_ref, grad_gain_ref = refs[6:]
+    size = sum(piece.size for piece in pieces)
+    rows = pieces[0].block_rows
+    cosine, sine = cosine_ref[...], sine_ref[...]
+    normed = normed_ref[...]
+    grad_normed = jnp.zeros(grad_normed_ref.shape, jnp.float32)
+    grad_gain = jnp.zeros((1, HD), jnp.float32)
+    for head, start in enumerate(head_starts(pieces)[:HQ]):
+        columns = slice(head * HD, (head + 1) * HD)
+        scale, normal = norm_parts(query_proj_ref[:, columns])
+        upstream = turn(grad_query_ref[:, columns], cosine, -sine)
+        grad, gain_row = norm_back(scale, normal, upstream, gain_ref[...])
+        grad_gain = grad_gain + gain_row
+        grad = grad.astype(jnp.bfloat16)
+        weight = wide_head(weight_refs, size, start, rows)
+        grad_normed = grad_normed + product(grad, weight, 1, 1)
+        grad_weight_ref[:, columns] = product(normed, grad, 0, 0).astype(jnp.bfloat16)
+    grad_normed_ref[...] = grad_normed
+    grad_gain_ref[...] = grad_gain
+
+
 def project_back_kernel(
     pieces,
     index_ref,
     tokens_ref,
     gain_ref,
-    gain_query_ref,
     gain_key_ref,
     cosine_ref,
     sine_ref,
     order_ref,
     normed_ref,
-    query_proj_ref,
     key_proj_ref,
-    grad_query_ref,
+    grad_query_weight_ref,
+    grad_normed_ref,
     grad_middle_ref,
     grad_out_weight_ref,
     gain_attn_ref,
     gain_ffin_ref,
     gain_ffout_ref,
+    gain_query_ref,
     *refs,
 ):
-    weight_refs, key_value_refs, grad_refs = refs[:10], refs[10:-6], refs[-6:-2]
+    weight_refs, key_value_refs, grad_refs = refs[:6], refs[6:-6], refs[-6:-2]
     input_grad_ref, grad_gain_ref = refs[-2:]
     low = index_ref[0] % LOW_COUNT
     size = sum(piece.size for piece in pieces)
     rows = pieces[0].block_rows
-    cosine, sine = cosine_ref[...], sine_ref[...]
     normed = normed_ref[...]
     key_value = sum(ref[...].astype(jnp.float32) for ref in key_value_refs)
-    grad_normed = jnp.zeros(tokens_ref.shape, jnp.float32)
-    grad_gain_query = jnp.zeros((1, HD), jnp.float32)
-    grad_gain_key = jnp.zeros((1, HD), jnp.float32)
+    scale, normal = norm_parts(key_proj_ref[...])
+    upstream = turn(key_value[:, :HD], cosine_ref[...], -sine_ref[...])
+    grad_key, grad_gain_key = norm_back(scale, normal, upstream, gain_key_ref[...])
+    grad_normed = grad_normed_ref[...]
     for head, start in enumerate(head_starts(pieces)):
-        columns = slice(head * HD, (head + 1) * HD)
         if head < HQ:
-            scale, normal = norm_parts(query_proj_ref[:, columns])
-            upstream = turn(grad_query_ref[:, columns], cosine, -sine)
-            grad, gain_row = norm_back(scale, normal, upstream, gain_query_ref[...])
-            grad_gain_query = grad_gain_query + gain_row
-        elif head == HQ:
-            scale, normal = norm_parts(key_proj_ref[...])
-            upstream = turn(key_value[:, :HD], cosine, -sine)
-            grad, grad_gain_key = norm_back(scale, normal, upstream, gain_key_ref[...])
+            grad_weight = grad_query_weight_ref[:, head * HD : (head + 1) * HD]
         else:
-            grad = key_value[:, HD:]
-        grad = grad.astype(jnp.bfloat16)
-        weight = wide_head(weight_refs, size, start, rows)
-        grad_normed = grad_normed + product(grad, weight, 1, 1)
-        grad_weight = product(normed, grad, 0, 0).astype(jnp.bfloat16)
+            grad = (grad_key if head == HQ else key_value[:, HD:]).astype(jnp.bfloat16)
+            weight = wide_head(weight_refs, size, start, rows)
+            grad_normed = grad_normed + product(grad, weight, 1, 1)
+            grad_weight = product(normed, grad, 0, 0).astype(jnp.bfloat16)
         for side in range(2):
             put_wide_tile(
                 grad_refs,
@@ -751,7 +849,7 @@
         gain_attn_ref[...],
         gain_ffin_ref[...],
         gain_ffout_ref[...],
-        grad_gain_query,
+        gain_query_ref[...],
         grad_gain_key,
     ]
     row = 0
@@ -798,15 +896,20 @@
     first_row = lax.axis_index("group") * local_rows
     attention_rows = sum(piece.flat_rows for piece in attention_pieces)
     ffn_pieces = pieces[4:7]
-    attention_near, ffn_rows = gather_near(
-        attention_pieces,
-        gather_high(master[:attention_rows].astype(jnp.bfloat16)),
-        master,
-        master.shape[0] - attention_rows,
-    )
-    ffn_parts = gather_high(ffn_rows)
-    attention_blocks = gather_diagonal(*attention_near, (ffn_parts[1],))
-    (ffn_near,) = gather_near(ffn_pieces, ffn_parts, behind=(attention_blocks[3],))
+    attention_parts = gather_high(master[:attention_rows].astype(jnp.bfloat16), False)
+    (ffn_rows,) = local_call(
+        round_kernel,
+        (array((master.shape[0] - attention_rows, LANES), jnp.bfloat16),),
+        (master,),
+        (),
+        (attention_parts[1],),
+    )
+    ffn_parts = gather_high(ffn_rows, True)
+    attention_near = gather_near(attention_pieces, attention_parts)
+    attention_blocks = gather_cores(*attention_near)
+    ffn_near = gather_near(
+        ffn_pieces, ffn_parts, (attention_blocks[0], *attention_near[1])
+    )
     gain_parts = []
     for start, width in ((0, D), (D, D), (2 * D, D), (3 * D, D), (4 * D, HD), (4 * D + HD, HD)):
         gain_parts.append(gains[start : start + width][None])
@@ -826,7 +929,6 @@
     allowed = (distance >= 0) & (distance < WINDOW) & (key_docs[None, :] == query_docs[:, None])
     allowed = allowed.astype(jnp.float32)
 
-    entry = (tokens, gain_input, gain_query, gain_key, cosine, sine, order)
     width = HQ * HD
     normed, query_proj, key_proj, query_rot, key_value = local_call(
         functools.partial(project_kernel, attention_pieces),
@@ -837,10 +939,9 @@
             array((local_rows, width), jnp.bfloat16),
             array((local_rows, 2 * HD), jnp.bfloat16),
         ),
-        (*entry, *attention_blocks),
-        (),
-        (ffn_near[0],),
-    )
+        (tokens, gain_input, gain_query, gain_key, cosine, sine, order, *attention_blocks),
+    )
+    ffn_weights = gather_cores(*ffn_near, (key_value,))
     key_values = [shifted(key_value, "group", offset) for offset in range(reach, 0, -1)]
     key_values.append(key_value)
     probs, attended, attn_out, middle, out_weight = local_call(
@@ -853,12 +954,14 @@
             array((width, D), jnp.bfloat16),
         ),
         (tokens, gain_attn, allowed, query_rot, *attention_blocks, *key_values),
-    )
-    ffn_weights = gather_diagonal(*ffn_near, (middle,))
+        (),
+        (ffn_weights[0],),
+    )
     outputs, grad_middle, grad_gain_ffin, grad_gain_ffout, grads_ffn = ffn_blocks(
         pieces, middle, cotangent, gain_ffin, gain_ffout, order, ffn_weights
     )
-    ffn_started, ffn_sent = scatter_start(ffn_pieces, *grads_ffn)
+    near_three, near_one, far_three, far_one = grads_ffn
+    far_three, far_one = scatter_cores(far_three, far_one)
     grad_out_weight, grad_query, grad_gain_attn, *grad_key_values = local_call(
         attend_back_kernel,
         (
@@ -878,10 +981,23 @@
             query_rot,
             *key_values,
         ),
+    )
+    over_x, over_y, sent = scatter_one(ffn_pieces, near_one, far_one, (grad_query,))
+    threes = scatter_three(ffn_pieces, near_three, far_three, (sent,))
+    grad_query_weight, grad_normed, grad_gain_query = local_call(
+        functools.partial(query_back_kernel, attention_pieces),
+        (
+            array((D, width), jnp.bfloat16),
+            array((local_rows, D), jnp.float32),
+            array((1, HD), jnp.float32),
+        ),
+        (gain_query, cosine, sine, normed, query_proj, grad_query, *attention_blocks),
         (),
-        (ffn_sent,),
-    )
-    ffn_sums = scatter_middle(ffn_pieces, ffn_started)
+        (threes[0],),
+    )
+    ffn_terms, sent = scatter_passed(
+        ffn_pieces, threes, over_x, over_y, near_one, far_one, (grad_normed,)
+    )
     grad_key_values = [
         shifted(value, "group", place - reach) if place < reach else value
         for place, value in enumerate(grad_key_values)
@@ -894,27 +1010,35 @@
             array((GAIN_ROWS, LANES), jnp.float32),
         ),
         (
-            *entry,
+            tokens,
+            gain_input,
+            gain_key,
+            cosine,
+            sine,
+            order,
             normed,
-            query_proj,
             key_proj,
-            grad_query,
+            grad_query_weight,
+            grad_normed,
             grad_middle,
             grad_out_weight,
             grad_gain_attn,
             grad_gain_ffin,
             grad_gain_ffout,
+            grad_gain_query,
             *attention_blocks,
             *grad_key_values,
         ),
         (),
-        (ffn_sums[1],),
-    )
-    grads_ffn = scatter_end(ffn_pieces, *ffn_sums)
-    attention_started, _ = scatter_start(attention_pieces, *grads_attention)
-    grads_attention = scatter_end(
-        attention_pieces, *scatter_middle(attention_pieces, attention_started)
-    )
+        (threes[1], threes[4], sent),
+    )
+    grads_ffn = scatter_high(ffn_pieces, ffn_terms)
+    near_three, near_one, far_three, far_one = grads_attention
+    far_three, far_one = scatter_cores(far_three, far_one)
+    over_x, over_y, sent = scatter_one(attention_pieces, near_one, far_one)
+    threes = scatter_three(attention_pieces, near_three, far_three, (sent,))
+    terms, _ = scatter_passed(attention_pieces, threes, over_x, over_y, near_one, far_one)
+    grads_attention = scatter_high(attention_pieces, terms)
     gain_grads = grads_attention[attention_rows:].reshape(-1)[: gains.shape[0]]
     grads_local = jnp.concatenate([grads_attention[:attention_rows], grads_ffn])
     return (

time: 254 us -> 242 us (0.953)
  waiting for transfers between devices: 106 us -> 81.9 us
  Pallas kernels: 67.9 us -> 79.6 us
  starting transfers between devices: 48.8 us -> 52.1 us
    ppermute x42 -> x46, waiting for transfers between devices: 104 us -> 76.5 us  [swap(): lax.ppermute(value, ALL_AXES, [(source, source ^ mask) for source in rang...]
    pallas_call x15 -> x19, Pallas kernels: 67.9 us -> 79.6 us  [local_call(): pl.pallas_call(body, out_shape=outs, in_specs=specs, out_specs=tuple((pl....]
    ppermute x6, waiting for transfers between devices: 1.87 us -> 5.38 us  [shifted(): lax.ppermute(value, axis, [(source, source + steps) for source in range(i...]
    ppermute x42 -> x46, starting transfers between devices: 38.7 us -> 41.6 us  [swap(): lax.ppermute(value, ALL_AXES, [(source, source ^ mask) for source in rang...]
    unnamed x112 -> x118, local copies, waits for them, and re-layouts: 15.7 us -> 14.1 us
  transfers between devices with their start and end apart: 48 -> 52, of which waited for: 22 -> 31; matrix products, arithmetic and copies ran while one was open for 4% -> 3% of each run, Pallas kernels for 17% -> 22%
where the time goes in v7:
time: 242 us; the launch traced here: 241 us
  waiting for transfers between devices  81.9 us (34%)
  Pallas kernels  79.6 us (33%)
  starting transfers between devices  52.1 us (22%)
  local copies, waits for them, and re-layouts  18.9 us (8%)
  other arithmetic  7.77 us (3%)
    pallas_call x19, Pallas kernels, local_call(): pl.pallas_call(body, out_shape=outs, in_specs=specs, out_specs=tuple((pl....  79.6 us
    ppermute x46, waiting for transfers between devices, swap(): lax.ppermute(value, ALL_AXES, [(source, source ^ mask) for source in rang...  76.5 us
    ppermute x46, starting transfers between devices, swap(): lax.ppermute(value, ALL_AXES, [(source, source ^ mask) for source in rang...  41.6 us
    unnamed x118, local copies, waits for them, and re-layouts  14.1 us
    ppermute x6, starting transfers between devices, shifted(): lax.ppermute(value, axis, [(source, source + steps) for source in range(i...  10.6 us
    ppermute x6, waiting for transfers between devices, shifted(): lax.ppermute(value, axis, [(source, source + steps) for source in range(i...  5.38 us
  transfers between devices with their start and end apart: 52, of which 31 were waited for; matrix products, arithmetic and copies ran while one was open for 3% of the time, Pallas kernels for 22%

profile of v7, /device:TPU:0, one launch (start us, length us, event | category | flops | bytes accessed | tf_op | source)
XLA Modules:
  0.0 241.3 jit_solution(10184071238929519884)
XLA Ops:
  1.6 5.1 %collective-permute-start.2 = (bf16[400,128]{1,0:T(8,128)(2,1)S(1)}, bf16[400,128]{1,0:T(8,128)(2,1)S(1)}, u32[]{:S(2)}, u32[]{:S(2)}) collective-permute-start(bf16[400,128]{1,0:T(8,128)(2,1)S(1)} %slice.74.refs_1_), channel_id=1, source_target_pairs={{0,24},{1,25},{2,26},{3,27},{4,28},{5,29},{6,30},{7,31},{8,16},{9,... | collective-permute-start | bytes 307208 | tf_op jit(solution)/shard_map/ppermute | solution.py:126
  10.5 4.8 %collective-permute-done.1.refs_3_ = bf16[400,128]{1,0:T(8,128)(2,1)S(1)} collective-permute-done((bf16[400,128]{1,0:T(8,128)(2,1)S(1)}, bf16[400,128]{1,0:T(8,128)(2,1)S(1)}, u32[]{:S(2)}, u32[]{:S(2)}) %collective-permute-start.1) | collective-permute-done | bytes 102432 | tf_op jit(solution)/shard_map/ppermute | solution.py:126
  30.6 2.5 %shard_map.153.refs_8_.refs_5_.refs_7_.refs_17_ = bf16[4800,128]{1,0:T(8,128)(2,1)} custom-call(s32[1]{0:T(128)} %bitcast.refs_0_, bf16[800,128]{1,0:T(8,128)(2,1)} %get-tuple-element.73.refs_1_, bf16[800,128]{1,0:T(8,128)(2,1)} %get-tuple-element.74.refs_2_, bf16[800,128]{1,0:T(8,128)(2,1)} %copy-done.42, bf16[800,128]{1,0:T(8,128)(2,1)} %copy-done.41, ...), custom_call_target="tpu_custom_call" | custom-call | tf_op jit(solution)/shard_map/pallas_call | solution.py:138
  38.4 3.0 %collective-permute-done.7.refs_9_.refs_6_.refs_8_.refs_18_ = bf16[800,128]{1,0:T(8,128)(2,1)S(1)} collective-permute-done((bf16[800,128]{1,0:T(8,128)(2,1)}, bf16[800,128]{1,0:T(8,128)(2,1)S(1)}, u32[]{:S(2)}, u32[]{:S(2)}) %collective-permute-start.7) | collective-permute-done | bytes 204832 | tf_op jit(solution)/shard_map/ppermute | solution.py:126
  42.7 2.5 %collective-permute-done.15.refs_2_ = bf16[960,128]{1,0:T(8,128)(2,1)S(1)} collective-permute-done((bf16[960,128]{1,0:T(8,128)(2,1)S(1)}, bf16[960,128]{1,0:T(8,128)(2,1)S(1)}, u32[]{:S(2)}, u32[]{:S(2)}) %collective-permute-start.15) | collective-permute-done | bytes 245792 | tf_op jit(solution)/shard_map/ppermute | solution.py:126
  45.1 4.2 %collective-permute-done.17.refs_4_ = bf16[960,128]{1,0:T(8,128)(2,1)S(1)} collective-permute-done((bf16[960,128]{1,0:T(8,128)(2,1)S(1)}, bf16[960,128]{1,0:T(8,128)(2,1)S(1)}, u32[]{:S(2)}, u32[]{:S(2)}) %collective-permute-start.17) | collective-permute-done | bytes 245792 | tf_op jit(solution)/shard_map/ppermute | solution.py:126
  50.1 2.9 %shard_map.156 = (bf16[1920,128]{1,0:T(8,128)(2,1)}, bf16[1920,128]{1,0:T(8,128)(2,1)}) custom-call(s32[1]{0:T(128)} %bitcast.refs_0_, bf16[960,128]{1,0:T(8,128)(2,1)} %shard_map.155.refs_1_, bf16[960,128]{1,0:T(8,128)(2,1)} %copy-done.32, bf16[960,128]{1,0:T(8,128)(2,1)} %copy-done.31, bf16[960,128]{1,0:T(8,128)(2,1)} %copy-done.33, ...), custom_call_target="tpu_custom_call" | custom-call | tf_op jit(solution)/shard_map/pallas_call | solution.py:138
  60.9 3.9 %shard_map.154 = (bf16[128,640]{1,0:T(8,128)(2,1)}, f32[128,1024]{1,0:T(8,128)}, f32[128,256]{1,0:T(8,128)}, bf16[128,1024]{1,0:T(8,128)(2,1)}, bf16[128,512]{1,0:T(8,128)(2,1)}) custom-call(s32[1]{0:T(128)} %bitcast.refs_0_, bf16[128,640]{1,0:T(8,128)(2,1)} %refs_1_.7, f32[1,640]{1,0:T(1,128)} %broadcast_in_dim.15.refs_2_, f32[1,256]{1,0:T(1,128)} %bitcast.23, ...), custom_call_target="tpu_custom_call" | custom-call | tf_op jit(solution)/shard_map/pallas_call | solution.py:138
  64.7 2.6 %collective-permute-done.20.refs_5_ = bf16[1920,128]{1,0:T(8,128)(2,1)S(1)} collective-permute-done((bf16[1920,128]{1,0:T(8,128)(2,1)}, bf16[1920,128]{1,0:T(8,128)(2,1)S(1)}, u32[]{:S(2)}, u32[]{:S(2)}) %collective-permute-start.20) | collective-permute-done | bytes 491552 | tf_op jit(solution)/shard_map/ppermute | solution.py:126
  68.4 7.6 %collective-permute-done.21.refs_6_ = bf16[1920,128]{1,0:T(8,128)(2,1)} collective-permute-done((bf16[1920,128]{1,0:T(8,128)(2,1)}, bf16[1920,128]{1,0:T(8,128)(2,1)}, u32[]{:S(2)}, u32[]{:S(2)}) %collective-permute-start.21) | collective-permute-done | bytes 491552 | tf_op jit(solution)/shard_map/ppermute | solution.py:126
  77.5 3.7 %shard_map.157.refs_15_.refs_6_ = bf16[11520,128]{1,0:T(8,128)(2,1)} custom-call(s32[1]{0:T(128)} %bitcast.refs_0_, bf16[1920,128]{1,0:T(8,128)(2,1)} %get-tuple-element.77.refs_1_, bf16[1920,128]{1,0:T(8,128)(2,1)} %get-tuple-element.78.refs_2_, bf16[1920,128]{1,0:T(8,128)(2,1)} %copy-done.25, bf16[1920,128]{1,0:T(8,128)(2,1)} %copy-done.24, ...), custom_call_target="tpu_custom_call" | custom-call | tf_op jit(solution)/shard_map/pallas_call | solution.py:138
  82.7 12.4 %collective-permute-done.22.refs_7_ = bf16[1920,128]{1,0:T(8,128)(2,1)} collective-permute-done((bf16[1920,128]{1,0:T(8,128)(2,1)}, bf16[1920,128]{1,0:T(8,128)(2,1)}, u32[]{:S(2)}, u32[]{:S(2)}) %collective-permute-start.22) | collective-permute-done | bytes 491552 | tf_op jit(solution)/shard_map/ppermute | solution.py:126
  99.7 2.8 %collective-permute-start.13 = (bf16[128,512]{1,0:T(8,128)(2,1)S(1)}, bf16[128,512]{1,0:T(8,128)(2,1)S(1)}, u32[]{:S(2)}, u32[]{:S(2)}) collective-permute-start(bf16[128,512]{1,0:T(8,128)(2,1)S(1)} %copy-done.13), channel_id=1, source_target_pairs={{0,2},{1,3},{4,6},{5,7},{8,10},{9,11},{12,14},{13,15},{16,18},{17,... | collective-permute-start | bytes 393224 | tf_op jit(solution)/shard_map/ppermute | solution.py:33
  107.0 5.7 %shard_map.158 = (f32[128,2048]{1,0:T(8,128)}, bf16[128,1024]{1,0:T(8,128)(2,1)}, f32[128,640]{1,0:T(8,128)}, f32[128,640]{1,0:T(8,128)}, bf16[1024,640]{1,0:T(8,128)(2,1)}) custom-call(s32[1]{0:T(128)} %bitcast.refs_0_, bf16[128,640]{1,0:T(8,128)(2,1)} %refs_1_.7, f32[1,640]{1,0:T(1,128)} %broadcast_in_dim.14.refs_2_.refs_3_, f32[128,512]{1,0:T(8,128)} %fusion.4.refs_3_, ...), custom_call_target="tpu_custom_call" | custom-call | tf_op jit(solution)/shard_map/pallas_call | solution.py:138
  114.5 14.6 %shard_map.159 = (bf16[128,640]{1,0:T(8,128)(2,1)}, f32[128,640]{1,0:T(8,128)}, f32[1,640]{1,0:T(1,128)}, f32[1,640]{1,0:T(1,128)}, bf16[11520,128]{1,0:T(8,128)...) custom-call(s32[1]{0:T(128)} %bitcast.refs_0_, ...), custom_call_target="tpu_custom_call" | custom-call | tf_op jit(solution)/shard_map/pallas_call | solution.py:138
  129.6 6.2 %shard_map.160 = (bf16[1024,640]{1,0:T(8,128)(2,1)}, f32[128,1024]{1,0:T(8,128)}, f32[1,640]{1,0:T(1,128)}, bf16[128,512]{1,0:T(8,128)(2,1)}, bf16[128,512]{1,0:...) custom-call(s32[1]{0:T(128)} %bitcast.refs_0_, f32[128,640]{1,0:T(8,128)} %get-tuple-element.84.refs_1_.refs_11_, ...), custom_call_target="tpu_custom_call" | custom-call | tf_op jit(solution)/shard_map/pallas_call | solution.py:138
  137.0 2.6 %shard_map.161 = (bf16[1920,128]{1,0:T(8,128)(2,1)}, bf16[1920,128]{1,0:T(8,128)(2,1)}) custom-call(s32[1]{0:T(128)} %bitcast.refs_0_, bf16[3840,128]{1,0:T(8,128)(2,1)} %get-tuple-element.92.refs_1_.refs_5_, bf16[3840,128]{1,0:T(8,128)(2,1)} %copy-done.3, f32[128,1024]{1,0:T(8,128)} %get-tuple-element.89.refs_3_.refs_6_), custom_call_target="tpu_custom_call" | custom-call | tf_op jit(solution)/shard_map/pallas_call | solution.py:138
  144.6 5.1 %shard_map.162 = (f32[3840,128]{1,0:T(8,128)}, bf16[1920,128]{1,0:T(8,128)(2,1)}, f32[1920,128]{1,0:T(8,128)}, f32[1920,128]{1,0:T(8,128)}, bf16[1920,128]{1,0:T(8,128)(2,1)}) custom-call(s32[1]{0:T(128)} %bitcast.refs_0_, bf16[11520,128]{1,0:T(8,128)(2,1)} %get-tuple-element.90.refs_1_, bf16[11520,128]{1,0:T(8,128)(2,1)} %copy-done.7, ...), custom_call_target="tpu_custom_call" | custom-call | tf_op jit(solution)/shard_map/pallas_call | solution.py:138
  156.8 4.5 %shard_map.163 = (bf16[640,1024]{1,0:T(8,128)(2,1)}, f32[128,640]{1,0:T(8,128)}, f32[1,256]{1,0:T(1,128)}) custom-call(s32[1]{0:T(128)} %bitcast.refs_0_, f32[1,256]{1,0:T(1,128)} %bitcast.24, f32[128,128]{1,0:T(8,128)} %get-tuple-element.151.refs_5_.refs_2_.refs_4_, f32[128,128]{1,0:T(8,128)} %get-tuple-element.150.refs_6_.refs_3_.refs_5_, ...), custom_call_target="tpu_custom_call" | custom-call | tf_op jit(solution)/shard_map/pallas_call | solution.py:138
  161.4 3.4 %shard_map.164 = (bf16[1920,128]{1,0:T(8,128)(2,1)}, bf16[1920,128]{1,0:T(8,128)(2,1)}, f32[8,128]{1,0:T(8,128)}) custom-call(s32[1]{0:T(128)} %bitcast.refs_0_, f32[1920,128]{1,0:T(8,128)} %get-tuple-element.109.refs_1_, f32[1920,128]{1,0:T(8,128)} %get-tuple-element.110.refs_2_, bf16[1920,128]{1,0:T(8,128)(2,1)} %copy-done.27, ...), custom_call_target="tpu_custom_call" | custom-call | tf_op jit(solution)/shard_map/pallas_call | solution.py:138
  164.8 2.6 %collective-permute-done.29.refs_23_ = bf16[128,512]{1,0:T(8,128)(2,1)S(1)} collective-permute-done((bf16[128,512]{1,0:T(8,128)(2,1)S(1)}, bf16[128,512]{1,0:T(8,128)(2,1)S(1)}, u32[]{:S(2)}, u32[]{:S(2)}) %collective-permute-start.29) | collective-permute-done | bytes 131104 | tf_op jit(solution)/shard_map/ppermute | solution.py:33
  169.7 6.8 %shard_map.165 = (bf16[4800,128]{1,0:T(8,128)(2,1)}, bf16[1632,128]{1,0:T(8,128)(2,1)}, bf16[4800,128]{1,0:T(8,128)(2,1)}, bf16[1632,128]{1,0:T(8,128)(2,1)}, bf...) custom-call(s32[1]{0:T(128)} %bitcast.refs_0_, bf16[128,640]{1,0:T(8,128)(2,1)} %refs_1_.7, f32[1,640]{1,0:T(1,128)} %broadcast_in_dim.15.refs_2_, ...), custom_call_target="tpu_custom_call" | custom-call | tf_op jit(solution)/shard_map/pallas_call | solution.py:138
  179.2 2.6 %collective-permute-done.37.refs_2_.refs_6_ = bf16[1632,128]{1,0:T(8,128)(2,1)S(1)} collective-permute-done((bf16[1632,128]{1,0:T(8,128)(2,1)}, bf16[1632,128]{1,0:T(8,128)(2,1)S(1)}, u32[]{:S(2)}, u32[]{:S(2)}) %collective-permute-start.37) | collective-permute-done | bytes 417824 | tf_op jit(solution)/shard_map/ppermute | solution.py:126
  186.4 3.0 %shard_map.167 = (f32[1600,128]{1,0:T(8,128)}, bf16[800,128]{1,0:T(8,128)(2,1)}, f32[800,128]{1,0:T(8,128)}, f32[800,128]{1,0:T(8,128)}, bf16[800,128]{1,0:T(8,128)(2,1)}) custom-call(s32[1]{0:T(128)} %bitcast.refs_0_, bf16[4800,128]{1,0:T(8,128)(2,1)} %get-tuple-element.114.refs_1_, bf16[4800,128]{1,0:T(8,128)(2,1)} %copy-done.12, ...), custom_call_target="tpu_custom_call" | custom-call | tf_op jit(solution)/shard_map/pallas_call | solution.py:138
  190.7 5.8 %collective-permute-done.40.refs_4_ = bf16[800,128]{1,0:T(8,128)(2,1)S(1)} collective-permute-done((bf16[800,128]{1,0:T(8,128)(2,1)}, bf16[800,128]{1,0:T(8,128)(2,1)S(1)}, u32[]{:S(2)}, u32[]{:S(2)}) %collective-permute-start.40) | collective-permute-done | bytes 204832 | tf_op jit(solution)/shard_map/ppermute | solution.py:126
  198.0 2.3 shard_map.168
  201.8 4.3 %shard_map.170 = (f32[960,128]{1,0:T(8,128)}, bf16[960,128]{1,0:T(8,128)(2,1)}, bf16[960,128]{1,0:T(8,128)(2,1)}, bf16[960,128]{1,0:T(8,128)(2,1)}) custom-call(s32[1]{0:T(128)} %bitcast.refs_0_, f32[3840,128]{1,0:T(8,128)} %get-tuple-element.95.refs_13_.refs_1_, bf16[1920,128]{1,0:T(8,128)(2,1)} %copy-done.9, bf16[1920,128]{1,0:T(8,128)(2,1)} %copy-done.23, ...), custom_call_target="tpu_custom_call" | custom-call | tf_op jit(solution)/shard_map/pallas_call | solution.py:138
  206.4 2.2 collective-permute-start.50
  212.7 7.3 %collective-permute-done.43.refs_5_ = bf16[800,128]{1,0:T(8,128)(2,1)S(1)} collective-permute-done((bf16[800,128]{1,0:T(8,128)(2,1)S(1)}, bf16[800,128]{1,0:T(8,128)(2,1)S(1)}, u32[]{:S(2)}, u32[]{:S(2)}) %collective-permute-start.43) | collective-permute-done | bytes 204832 | tf_op jit(solution)/shard_map/ppermute | solution.py:126
  220.7 2.5 %shard_map.169 = (f32[432,128]{1,0:T(8,128)}, bf16[432,128]{1,0:T(8,128)(2,1)}, bf16[432,128]{1,0:T(8,128)(2,1)}, bf16[432,128]{1,0:T(8,128)(2,1)}) custom-call(s32[1]{0:T(128)} %bitcast.refs_0_, f32[1600,128]{1,0:T(8,128)} %get-tuple-element.119.refs_1_, bf16[800,128]{1,0:T(8,128)(2,1)} %copy-done.36, bf16[800,128]{1,0:T(8,128)(2,1)} %copy-done.37, ...), custom_call_target="tpu_custom_call" | custom-call | tf_op jit(solution)/shard_map/pallas_call | solution.py:138
  223.4 2.5 %collective-permute-start.45 = (bf16[432,128]{1,0:T(8,128)(2,1)}, bf16[432,128]{1,0:T(8,128)(2,1)S(1)}, u32[]{:S(2)}, u32[]{:S(2)}) collective-permute-start(bf16[432,128]{1,0:T(8,128)(2,1)} %get-tuple-element.130), channel_id=1, source_target_pairs={{0,16},{1,17},{2,18},{3,19},{4,20},{5,21},{6,22},{7,23},{8,24},{9,... | collective-permute-start | bytes 331784 | tf_op jit(solution)/shard_map/ppermute | solution.py:126
  229.9 8.1 %collective-permute-done.45 = bf16[432,128]{1,0:T(8,128)(2,1)S(1)} collective-permute-done((bf16[432,128]{1,0:T(8,128)(2,1)}, bf16[432,128]{1,0:T(8,128)(2,1)S(1)}, u32[]{:S(2)}, u32[]{:S(2)}) %collective-permute-start.45) | collective-permute-done | bytes 110624 | tf_op jit(solution)/shard_map/ppermute | solution.py:126
  (237 shorter events, 90.1 us)
Async XLA Ops:
  24.7 12.0 %collective-permute-start.16 = (bf16[960,128]{1,0:T(8,128)(2,1)}, bf16[960,128]{1,0:T(8,128)(2,1)S(1)}, u32[]{:S(2)}, u32[]{:S(2)}) collective-permute-start(bf16[960,128]{1,0:T(8,128)(2,1)} %shard_map.155.refs_1_), channel_id=1, source_target_pairs={{0,16},{1,17},{2,18},{3,19},{4,20},{5,21},{6,22},{7,23},{8,24},{9,... | collective-permute-start | bytes 737288 | tf_op jit(solution)/shard_map/ppermute | solution.py:126
  33.1 26.7 %collective-permute-start.9 = (bf16[4800,128]{1,0:T(8,128)(2,1)}, bf16[4800,128]{1,0:T(8,128)(2,1)S(1)}, u32[]{:S(2)}, u32[]{:S(2)}) collective-permute-start(bf16[4800,128]{1,0:T(8,128)(2,1)} %shard_map.153.refs_8_.refs_5_.refs_7_.refs_17_), channel_id=1, source_target_pairs={{0,1},{1,0},{2,3},{3,2},{4,5},{5,4},{6,7},{7,6},{8,9},{9,8},{10,11... | collective-permute-start | bytes 3686408 | tf_op jit(solution)/shard_map/ppermute | solution.py:126
  36.6 12.8 %collective-permute-start.17 = (bf16[960,128]{1,0:T(8,128)(2,1)S(1)}, bf16[960,128]{1,0:T(8,128)(2,1)S(1)}, u32[]{:S(2)}, u32[]{:S(2)}) collective-permute-start(bf16[960,128]{1,0:T(8,128)(2,1)S(1)} %collective-permute-done.16.refs_3_), channel_id=1, source_target_pairs={{0,8},{1,9},{2,10},{3,11},{4,12},{5,13},{6,14},{7,15},{8,0},{9,1},... | collective-permute-start | bytes 737288 | tf_op jit(solution)/shard_map/ppermute | solution.py:126
  41.4 13.2 %collective-permute-start.10 = (bf16[800,128]{1,0:T(8,128)(2,1)S(1)}, bf16[800,128]{1,0:T(8,128)(2,1)S(1)}, u32[]{:S(2)}, u32[]{:S(2)}) collective-permute-start(bf16[800,128]{1,0:T(8,128)(2,1)S(1)} %collective-permute-done.7.refs_9_.refs_6_.refs_8_.refs_18_), channel_id=1, source_target_pairs={{0,1},{1,0},{2,3},{3,2},{4,5},{5,4},{6,7},{7,6},{8,9},{9,8},{10,11... | collective-permute-start | bytes 614408 | tf_op jit(solution)/shard_map/ppermute | solution.py:126
  42.6 13.0 %collective-permute-start.11 = (bf16[800,128]{1,0:T(8,128)(2,1)S(1)}, bf16[800,128]{1,0:T(8,128)(2,1)S(1)}, u32[]{:S(2)}, u32[]{:S(2)}) collective-permute-start(bf16[800,128]{1,0:T(8,128)(2,1)S(1)} %collective-permute-done.8.refs_10_.refs_7_.refs_9_.refs_19_), channel_id=1, source_target_pairs={{0,1},{1,0},{2,3},{3,2},{4,5},{5,4},{6,7},{7,6},{8,9},{9,8},{10,11... | collective-permute-start | bytes 614408 | tf_op jit(solution)/shard_map/ppermute | solution.py:126
  53.0 14.4 %collective-permute-start.20 = (bf16[1920,128]{1,0:T(8,128)(2,1)}, bf16[1920,128]{1,0:T(8,128)(2,1)S(1)}, u32[]{:S(2)}, u32[]{:S(2)}) collective-permute-start(bf16[1920,128]{1,0:T(8,128)(2,1)} %get-tuple-element.77.refs_1_), channel_id=1, source_target_pairs={{0,2},{1,3},{2,0},{3,1},{4,6},{5,7},{6,4},{7,5},{8,10},{9,11},{10,... | collective-permute-start | bytes 1474568 | tf_op jit(solution)/shard_map/ppermute | solution.py:126
  54.1 14.4 %collective-permute-start.18 = (bf16[1920,128]{1,0:T(8,128)(2,1)}, bf16[1920,128]{1,0:T(8,128)(2,1)S(1)}, u32[]{:S(2)}, u32[]{:S(2)}) collective-permute-start(bf16[1920,128]{1,0:T(8,128)(2,1)} %get-tuple-element.77.refs_1_), channel_id=1, source_target_pairs={{0,4},{1,5},{2,6},{3,7},{4,0},{5,1},{6,2},{7,3},{8,12},{9,13},{10,... | collective-permute-start | bytes 1474568 | tf_op jit(solution)/shard_map/ppermute | solution.py:126
  54.6 21.4 %collective-permute-start.21 = (bf16[1920,128]{1,0:T(8,128)(2,1)}, bf16[1920,128]{1,0:T(8,128)(2,1)}, u32[]{:S(2)}, u32[]{:S(2)}) collective-permute-start(bf16[1920,128]{1,0:T(8,128)(2,1)} %get-tuple-element.78.refs_2_), channel_id=1, source_target_pairs={{0,2},{1,3},{2,0},{3,1},{4,6},{5,7},{6,4},{7,5},{8,10},{9,11},{10,... | collective-permute-start | bytes 1474568 | tf_op jit(solution)/shard_map/ppermute | solution.py:126
  55.6 21.2 %collective-permute-start.19 = (bf16[1920,128]{1,0:T(8,128)(2,1)}, bf16[1920,128]{1,0:T(8,128)(2,1)S(1)}, u32[]{:S(2)}, u32[]{:S(2)}) collective-permute-start(bf16[1920,128]{1,0:T(8,128)(2,1)} %get-tuple-element.78.refs_2_), channel_id=1, source_target_pairs={{0,4},{1,5},{2,6},{3,7},{4,0},{5,1},{6,2},{7,3},{8,12},{9,13},{10,... | collective-permute-start | bytes 1474568 | tf_op jit(solution)/shard_map/ppermute | solution.py:126
  81.2 31.6 %collective-permute-start.24 = (bf16[11520,128]{1,0:T(8,128)(2,1)}, bf16[11520,128]{1,0:T(8,128)(2,1)S(1)}, u32[]{:S(2)}, u32[]{:S(2)}) collective-permute-start(bf16[11520,128]{1,0:T(8,128)(2,1)} %shard_map.157.refs_15_.refs_6_), channel_id=1, source_target_pairs={{0,1},{1,0},{2,3},{3,2},{4,5},{5,4},{6,7},{7,6},{8,9},{9,8},{10,11... | collective-permute-start | bytes 8847368 | tf_op jit(solution)/shard_map/ppermute | solution.py:126
  81.2 13.9 %collective-permute-start.22 = (bf16[1920,128]{1,0:T(8,128)(2,1)}, bf16[1920,128]{1,0:T(8,128)(2,1)}, u32[]{:S(2)}, u32[]{:S(2)}) collective-permute-start(bf16[1920,128]{1,0:T(8,128)(2,1)} %copy-done.21), channel_id=1, source_target_pairs={{0,4},{1,5},{2,6},{3,7},{4,0},{5,1},{6,2},{7,3},{8,12},{9,13},{10,... | collective-permute-start | bytes 1474568 | tf_op jit(solution)/shard_map/ppermute | solution.py:126
  81.8 13.7 %collective-permute-start.23 = (bf16[1920,128]{1,0:T(8,128)(2,1)}, bf16[1920,128]{1,0:T(8,128)(2,1)}, u32[]{:S(2)}, u32[]{:S(2)}) collective-permute-start(bf16[1920,128]{1,0:T(8,128)(2,1)} %copy-done.24), channel_id=1, source_target_pairs={{0,2},{1,3},{2,0},{3,1},{4,6},{5,7},{6,4},{7,5},{8,10},{9,11},{10,... | collective-permute-start | bytes 1474568 | tf_op jit(solution)/shard_map/ppermute | solution.py:126
  95.2 17.6 %collective-permute-start.25 = (bf16[1920,128]{1,0:T(8,128)(2,1)}, bf16[1920,128]{1,0:T(8,128)(2,1)}, u32[]{:S(2)}, u32[]{:S(2)}) collective-permute-start(bf16[1920,128]{1,0:T(8,128)(2,1)} %collective-permute-done.22.refs_7_), channel_id=1, source_target_pairs={{0,1},{1,0},{2,3},{3,2},{4,5},{5,4},{6,7},{7,6},{8,9},{9,8},{10,11... | collective-permute-start | bytes 1474568 | tf_op jit(solution)/shard_map/ppermute | solution.py:126
  95.4 17.3 %collective-permute-start.26 = (bf16[1920,128]{1,0:T(8,128)(2,1)}, bf16[1920,128]{1,0:T(8,128)(2,1)}, u32[]{:S(2)}, u32[]{:S(2)}) collective-permute-start(bf16[1920,128]{1,0:T(8,128)(2,1)} %collective-permute-done.23.refs_8_), channel_id=1, source_target_pairs={{0,1},{1,0},{2,3},{3,2},{4,5},{5,4},{6,7},{7,6},{8,9},{9,8},{10,11... | collective-permute-start | bytes 1474568 | tf_op jit(solution)/shard_map/ppermute | solution.py:126
  129.1 14.0 %collective-permute-start.27 = (bf16[11520,128]{1,0:T(8,128)(2,1)}, bf16[11520,128]{1,0:T(8,128)(2,1)S(1)}, u32[]{:S(2)}, u32[]{:S(2)}) collective-permute-start(bf16[11520,128]{1,0:T(8,128)(2,1)} %get-tuple-element.91), channel_id=1, source_target_pairs={{0,1},{1,0},{2,3},{3,2},{4,5},{5,4},{6,7},{7,6},{8,9},{9,8},{10,11... | collective-permute-start | bytes 8847368 | tf_op jit(solution)/shard_map/ppermute | solution.py:126
  139.6 14.2 %collective-permute-start.34 = (bf16[1920,128]{1,0:T(8,128)(2,1)}, bf16[1920,128]{1,0:T(8,128)(2,1)S(1)}, u32[]{:S(2)}, u32[]{:S(2)}) collective-permute-start(bf16[1920,128]{1,0:T(8,128)(2,1)} %get-tuple-element.111), channel_id=1, source_target_pairs={{0,4},{1,5},{2,6},{3,7},{4,0},{5,1},{6,2},{7,3},{8,12},{9,13},{10,... | collective-permute-start | bytes 1474568 | tf_op jit(solution)/shard_map/ppermute | solution.py:126
  141.1 14.3 %collective-permute-start.35 = (bf16[1920,128]{1,0:T(8,128)(2,1)}, bf16[1920,128]{1,0:T(8,128)(2,1)S(1)}, u32[]{:S(2)}, u32[]{:S(2)}) collective-permute-start(bf16[1920,128]{1,0:T(8,128)(2,1)} %get-tuple-element.94.refs_3_), channel_id=1, source_target_pairs={{0,2},{1,3},{2,0},{3,1},{4,6},{5,7},{6,4},{7,5},{8,10},{9,11},{10,... | collective-permute-start | bytes 1474568 | tf_op jit(solution)/shard_map/ppermute | solution.py:126
  149.7 19.0 %collective-permute-start.32 = (bf16[1920,128]{1,0:T(8,128)(2,1)}, bf16[1920,128]{1,0:T(8,128)(2,1)S(1)}, u32[]{:S(2)}, u32[]{:S(2)}) collective-permute-start(bf16[1920,128]{1,0:T(8,128)(2,1)} %get-tuple-element.107), channel_id=1, source_target_pairs={{0,4},{1,5},{2,6},{3,7},{4,0},{5,1},{6,2},{7,3},{8,12},{9,13},{10,... | collective-permute-start | bytes 1474568 | tf_op jit(solution)/shard_map/ppermute | solution.py:126
  150.2 18.5 %collective-permute-start.33 = (bf16[1920,128]{1,0:T(8,128)(2,1)}, bf16[1920,128]{1,0:T(8,128)(2,1)S(1)}, u32[]{:S(2)}, u32[]{:S(2)}) collective-permute-start(bf16[1920,128]{1,0:T(8,128)(2,1)} %get-tuple-element.108), channel_id=1, source_target_pairs={{0,2},{1,3},{2,0},{3,1},{4,6},{5,7},{6,4},{7,5},{8,10},{9,11},{10,... | collective-permute-start | bytes 1474568 | tf_op jit(solution)/shard_map/ppermute | solution.py:126
  150.3 17.1 %collective-permute-start.29 = (bf16[128,512]{1,0:T(8,128)(2,1)S(1)}, bf16[128,512]{1,0:T(8,128)(2,1)S(1)}, u32[]{:S(2)}, u32[]{:S(2)}) collective-permute-start(bf16[128,512]{1,0:T(8,128)(2,1)S(1)} %copy-done.58), channel_id=1, source_target_pairs={{3,0},{7,4},{11,8},{15,12},{19,16},{23,20},{27,24},{31,28}} | collective-permute-start | bytes 393224 | tf_op jit(solution)/shard_map/ppermute | solution.py:33
  153.7 14.9 %collective-permute-start.30 = (bf16[128,512]{1,0:T(8,128)(2,1)S(1)}, bf16[128,512]{1,0:T(8,128)(2,1)S(1)}, u32[]{:S(2)}, u32[]{:S(2)}) collective-permute-start(bf16[128,512]{1,0:T(8,128)(2,1)S(1)} %copy-done.57), channel_id=1, source_target_pairs={{2,0},{3,1},{6,4},{7,5},{10,8},{11,9},{14,12},{15,13},{18,16},{19,... | collective-permute-start | bytes 393224 | tf_op jit(solution)/shard_map/ppermute | solution.py:33
  155.3 13.3 %collective-permute-start.31 = (bf16[128,512]{1,0:T(8,128)(2,1)S(1)}, bf16[128,512]{1,0:T(8,128)(2,1)S(1)}, u32[]{:S(2)}, u32[]{:S(2)}) collective-permute-start(bf16[128,512]{1,0:T(8,128)(2,1)S(1)} %copy-done.56), channel_id=1, source_target_pairs={{1,0},{2,1},{3,2},{5,4},{6,5},{7,6},{9,8},{10,9},{11,10},{13,12},{... | collective-permute-start | bytes 393224 | tf_op jit(solution)/shard_map/ppermute | solution.py:33
  178.5 22.3 %collective-permute-start.48 = (bf16[1920,128]{1,0:T(8,128)(2,1)S(1)}, bf16[1920,128]{1,0:T(8,128)(2,1)S(1)}, u32[]{:S(2)}, u32[]{:S(2)}) collective-permute-start(bf16[1920,128]{1,0:T(8,128)(2,1)S(1)} %copy-done.53), channel_id=1, source_target_pairs={{0,2},{1,3},{2,0},{3,1},{4,6},{5,7},{6,4},{7,5},{8,10},{9,11},{10,... | collective-permute-start | bytes 1474568 | tf_op jit(solution)/shard_map/ppermute | solution.py:126
  178.7 22.2 %collective-permute-start.47 = (bf16[1920,128]{1,0:T(8,128)(2,1)S(1)}, bf16[1920,128]{1,0:T(8,128)(2,1)S(1)}, u32[]{:S(2)}, u32[]{:S(2)}) collective-permute-start(bf16[1920,128]{1,0:T(8,128)(2,1)S(1)} %copy-done.20), channel_id=1, source_target_pairs={{0,4},{1,5},{2,6},{3,7},{4,0},{5,1},{6,2},{7,3},{8,12},{9,13},{10,... | collective-permute-start | bytes 1474568 | tf_op jit(solution)/shard_map/ppermute | solution.py:126
  184.5 12.8 %collective-permute-start.39 = (bf16[832,128]{1,0:T(8,128)(2,1)}, bf16[832,128]{1,0:T(8,128)(2,1)S(1)}, u32[]{:S(2)}, u32[]{:S(2)}) collective-permute-start(bf16[832,128]{1,0:T(8,128)(2,1)} %get-tuple-element.123), channel_id=1, source_target_pairs={{0,4},{1,5},{2,6},{3,7},{4,0},{5,1},{6,2},{7,3},{8,12},{9,13},{10,... | collective-permute-start | bytes 638984 | tf_op jit(solution)/shard_map/ppermute | solution.py:126
  189.4 21.2 %collective-permute-start.38 = (bf16[800,128]{1,0:T(8,128)(2,1)}, bf16[800,128]{1,0:T(8,128)(2,1)S(1)}, u32[]{:S(2)}, u32[]{:S(2)}) collective-permute-start(bf16[800,128]{1,0:T(8,128)(2,1)} %get-tuple-element.120), channel_id=1, source_target_pairs={{0,4},{1,5},{2,6},{3,7},{4,0},{5,1},{6,2},{7,3},{8,12},{9,13},{10,... | collective-permute-start | bytes 614408 | tf_op jit(solution)/shard_map/ppermute | solution.py:126
  200.3 12.1 %collective-permute-start.41 = (bf16[800,128]{1,0:T(8,128)(2,1)}, bf16[800,128]{1,0:T(8,128)(2,1)S(1)}, u32[]{:S(2)}, u32[]{:S(2)}) collective-permute-start(bf16[800,128]{1,0:T(8,128)(2,1)} %get-tuple-element.124), channel_id=1, source_target_pairs={{0,4},{1,5},{2,6},{3,7},{4,0},{5,1},{6,2},{7,3},{8,12},{9,13},{10,... | collective-permute-start | bytes 614408 | tf_op jit(solution)/shard_map/ppermute | solution.py:126
  206.1 19.8 %collective-permute-start.49 = (bf16[960,128]{1,0:T(8,128)(2,1)}, bf16[960,128]{1,0:T(8,128)(2,1)S(1)}, u32[]{:S(2)}, u32[]{:S(2)}) collective-permute-start(bf16[960,128]{1,0:T(8,128)(2,1)} %get-tuple-element.135), channel_id=1, source_target_pairs={{0,8},{1,9},{2,10},{3,11},{4,12},{5,13},{6,14},{7,15},{8,0},{9,1},... | collective-permute-start | bytes 737288 | tf_op jit(solution)/shard_map/ppermute | solution.py:126
  206.4 22.9 %collective-permute-start.50 = (bf16[960,128]{1,0:T(8,128)(2,1)}, bf16[960,128]{1,0:T(8,128)(2,1)S(1)}, u32[]{:S(2)}, u32[]{:S(2)}) collective-permute-start(bf16[960,128]{1,0:T(8,128)(2,1)} %get-tuple-element.136), channel_id=1, source_target_pairs={{0,16},{1,17},{2,18},{3,19},{4,20},{5,21},{6,22},{7,23},{8,24},{9,... | collective-permute-start | bytes 737288 | tf_op jit(solution)/shard_map/ppermute | solution.py:126
  208.7 20.7 %collective-permute-start.51 = (bf16[960,128]{1,0:T(8,128)(2,1)}, bf16[960,128]{1,0:T(8,128)(2,1)S(1)}, u32[]{:S(2)}, u32[]{:S(2)}) collective-permute-start(bf16[960,128]{1,0:T(8,128)(2,1)} %get-tuple-element.137), channel_id=1, source_target_pairs={{0,24},{1,25},{2,26},{3,27},{4,28},{5,29},{6,30},{7,31},{8,16},{9,... | collective-permute-start | bytes 737288 | tf_op jit(solution)/shard_map/ppermute | solution.py:126
  223.4 14.6 %collective-permute-start.45 = (bf16[432,128]{1,0:T(8,128)(2,1)}, bf16[432,128]{1,0:T(8,128)(2,1)S(1)}, u32[]{:S(2)}, u32[]{:S(2)}) collective-permute-start(bf16[432,128]{1,0:T(8,128)(2,1)} %get-tuple-element.130), channel_id=1, source_target_pairs={{0,16},{1,17},{2,18},{3,19},{4,20},{5,21},{6,22},{7,23},{8,24},{9,... | collective-permute-start | bytes 331784 | tf_op jit(solution)/shard_map/ppermute | solution.py:126
  225.9 12.1 %collective-permute-start.46 = (bf16[432,128]{1,0:T(8,128)(2,1)}, bf16[432,128]{1,0:T(8,128)(2,1)S(1)}, u32[]{:S(2)}, u32[]{:S(2)}) collective-permute-start(bf16[432,128]{1,0:T(8,128)(2,1)} %get-tuple-element.131), channel_id=1, source_target_pairs={{0,24},{1,25},{2,26},{3,27},{4,28},{5,29},{6,30},{7,31},{8,16},{9,... | collective-permute-start | bytes 331784 | tf_op jit(solution)/shard_map/ppermute | solution.py:126
  (79 other events, 521.3 us)

commit v8 on v7

--- a/solution.py
+++ b/solution.py
@@ -159,10 +159,6 @@
         self.size = self.block_rows * self.blocks
 
 
-def round_kernel(index_ref, in_ref, out_ref):
-    out_ref[...] = in_ref[in_ref.shape[0] - out_ref.shape[0] :, :].astype(jnp.bfloat16)
-
-
 def join_kernel(index_ref, *refs):
     out_ref = refs[-1]
     rows = refs[0].shape[0]
@@ -172,7 +168,7 @@
 
 def pack_kernel(pieces, index_ref, *refs):
     high_count = pieces[0].high_count
-    parts, out_refs, flat, packed = refs[:high_count], refs[-4:-2], refs[-2], refs[-1]
+    parts, out_refs, flat, packed = refs[:high_count], refs[high_count:-2], refs[-2], refs[-1]
     high = index_ref[0] // LOW_COUNT
     for step, part in enumerate(parts):
         flat[high ^ step] = part[...].astype(jnp.float32)
@@ -185,9 +181,9 @@
                 ]
                 target = target + piece.own_rows
         start = start + piece.flat_rows
-    half = target // 2
+    count = target // len(out_refs)
     for place, out_ref in enumerate(out_refs):
-        out_ref[...] = packed[place * half : (place + 1) * half, :].astype(jnp.bfloat16)
+        out_ref[...] = packed[place * count : (place + 1) * count, :].astype(jnp.bfloat16)
 
 
 def sum_one_kernel(size, index_ref, near_ref, far_ref, to_x_ref, to_y_ref):
@@ -212,11 +208,12 @@
 ):
     half = size // 2
     outs = (beside_first_ref, beside_second_ref, across_first_ref, across_second_ref)
-    own_ref[...] = near_ref[:size, :].astype(jnp.float32) + far_ref[:size, :].astype(jnp.float32)
+    total = near_ref[:size, :].astype(jnp.float32) + far_ref[:size, :].astype(jnp.float32)
+    own_ref[...] = total.astype(jnp.bfloat16)
     for place, out_ref in enumerate(outs):
         rows = slice(size + place * half, size + (place + 1) * half)
         total = near_ref[rows, :].astype(jnp.float32) + far_ref[rows, :].astype(jnp.float32)
-        out_ref[...] = total.astype(out_ref.dtype)
+        out_ref[...] = total.astype(jnp.bfloat16)
 
 
 def sum_passed_kernel(
@@ -233,12 +230,10 @@
     extra_ref,
 ):
     half = size // 2
-    beside_out_ref[...] = (beside_ref[...] + over_y_ref[...].astype(jnp.float32)).astype(
-        jnp.bfloat16
-    )
-    across_out_ref[:half, :] = (
-        across_ref[...] + over_x_ref[:half, :].astype(jnp.float32)
-    ).astype(jnp.bfloat16)
+    beside = beside_ref[...].astype(jnp.float32) + over_y_ref[...].astype(jnp.float32)
+    beside_out_ref[...] = beside.astype(jnp.bfloat16)
+    across = across_ref[...].astype(jnp.float32) + over_x_ref[:half, :].astype(jnp.float32)
+    across_out_ref[:half, :] = across.astype(jnp.bfloat16)
     if across_out_ref.shape[0] > half:
         extra = near_one_ref[size:, :].astype(jnp.float32)
         extra = extra + far_one_ref[size:, :].astype(jnp.float32)
@@ -266,12 +261,12 @@
     outs, flat, packed = refs[:-2], refs[-2], refs[-1]
     high = index_ref[0] // LOW_COUNT
     packed[:half, :] = (
-        own_ref[:half, :]
+        own_ref[:half, :].astype(jnp.float32)
         + beside_first_ref[...].astype(jnp.float32)
         + across_first_ref[:half, :].astype(jnp.float32)
     )
     packed[half:, :] = (
-        own_ref[half:, :]
+        own_ref[half:, :].astype(jnp.float32)
         + beside_second_ref[...].astype(jnp.float32)
         + across_second_ref[...].astype(jnp.float32)
     )
@@ -307,12 +302,12 @@
     return [parts[step] for step in range(high_count)]
 
 
-def gather_near(pieces, parts, behind=()):
+def gather_own(pieces, parts, count, behind=()):
     high_count = pieces[0].high_count
     size = sum(piece.size for piece in pieces)
-    first, second = local_call(
+    return local_call(
         functools.partial(pack_kernel, pieces),
-        (array((size // 2, LANES), jnp.bfloat16),) * 2,
+        (array((size // count, LANES), jnp.bfloat16),) * count,
         parts,
         (
             pltpu.VMEM((high_count, parts[0].shape[0], LANES), jnp.float32),
@@ -320,6 +315,9 @@
         ),
         behind,
     )
+
+
+def gather_halves(first, second):
     beside_second, across_first = swap(second, 4), swap(first, 2)
     beside_first, across_second = swap(first, 4), swap(second, 2)
     return (
@@ -328,10 +326,15 @@
     )
 
 
+def gather_wholes(own):
+    beside, across = swap(own, 4), swap(own, 2)
+    return (own, beside, across), (swap(across, 4),)
+
+
 def gather_cores(three, diagonal, behind=()):
     (three,) = local_call(
         join_kernel,
-        (array((6 * three[0].shape[0], LANES), jnp.bfloat16),),
+        (array((len(three) * three[0].shape[0], LANES), jnp.bfloat16),),
         three,
         (),
         behind,
@@ -366,11 +369,8 @@
     own, beside_first, beside_second, across_first, across_second = local_call(
         functools.partial(sum_three_kernel, size),
         (
-            array((size, LANES), jnp.float32),
-            array((half, LANES), jnp.bfloat16),
-            array((half, LANES), jnp.float32),
-            array((half, LANES), jnp.float32),
-            array((half, LANES), jnp.bfloat16),
+            array((size, LANES), jnp.bfloat16),
+            *(array((half, LANES), jnp.bfloat16),) * 4,
         ),
         (near_three, far_three),
         (),
@@ -420,9 +420,8 @@
             pltpu.VMEM((size, LANES), jnp.float32),
         ),
     )
-    return outs[0] + sum(
-        swap(send, step * LOW_COUNT).astype(jnp.float32) for step, send in enumerate(outs) if step
-    )
+    arrived = [swap(send, step * LOW_COUNT) for step, send in enumerate(outs) if step]
+    return outs[0] + sum(value.astype(jnp.float32) for value in arrived), outs[0], arrived
 
 
 def norm_parts(values):
@@ -452,10 +451,11 @@
 
 
 def weight_rows(refs, size, order, start, rows):
-    three, *diagonal = refs[:3] if order < 4 else refs[3:]
+    count = len(refs) // 2
+    three, *diagonal = refs[:count] if order < 4 else refs[count:]
     if order % 4 == 3:
-        second = int(2 * start >= size)
-        ref, start = diagonal[second], start - second * (size // 2)
+        part = size // len(diagonal)
+        ref, start = diagonal[start // part], start % part
     else:
         ref, start = three, order % 4 * size + start
     return ref[start : start + rows, :]
@@ -647,8 +647,8 @@
     order_ref,
     *refs,
 ):
-    weight_refs = refs[:6]
-    normed_ref, query_proj_ref, key_proj_ref, query_ref, key_value_ref = refs[6:]
+    weight_refs = refs[:4]
+    normed_ref, query_proj_ref, key_proj_ref, query_ref, key_value_ref = refs[4:]
     size = sum(piece.size for piece in pieces)
     rows = pieces[0].block_rows
     cosine, sine = cosine_ref[...], sine_ref[...]
@@ -683,7 +683,7 @@
     query_ref,
     *refs,
 ):
-    weight_refs, key_value_refs = refs[:6], refs[6:-5]
+    weight_refs, key_value_refs = refs[:4], refs[4:-5]
     probs_ref, attended_ref, attn_out_ref, middle_ref, out_weight_ref = refs[-5:]
     out_piece = pieces[-1]
     low = index_ref[0] % LOW_COUNT
@@ -765,8 +765,8 @@
     grad_query_ref,
     *refs,
 ):
-    weight_refs = refs[:6]
-    grad_weight_ref, grad_normed_ref, grad_gain_ref = refs[6:]
+    weight_refs = refs[:4]
+    grad_weight_ref, grad_normed_ref, grad_gain_ref = refs[4:]
     size = sum(piece.size for piece in pieces)
     rows = pieces[0].block_rows
     cosine, sine = cosine_ref[...], sine_ref[...]
@@ -808,7 +808,7 @@
     gain_query_ref,
     *refs,
 ):
-    weight_refs, key_value_refs, grad_refs = refs[:6], refs[6:-6], refs[-6:-2]
+    weight_refs, key_value_refs, grad_refs = refs[:4], refs[4:-6], refs[-6:-2]
     input_grad_ref, grad_gain_ref = refs[-2:]
     low = index_ref[0] % LOW_COUNT
     size = sum(piece.size for piece in pieces)
@@ -896,19 +896,14 @@
     first_row = lax.axis_index("group") * local_rows
     attention_rows = sum(piece.flat_rows for piece in attention_pieces)
     ffn_pieces = pieces[4:7]
-    attention_parts = gather_high(master[:attention_rows].astype(jnp.bfloat16), False)
-    (ffn_rows,) = local_call(
-        round_kernel,
-        (array((master.shape[0] - attention_rows, LANES), jnp.bfloat16),),
-        (master,),
-        (),
-        (attention_parts[1],),
-    )
+    rounded = master.astype(jnp.bfloat16)
+    attention_parts = gather_high(rounded[:attention_rows], False)
+    ffn_rows = rounded[attention_rows:]
     ffn_parts = gather_high(ffn_rows, True)
-    attention_near = gather_near(attention_pieces, attention_parts)
+    attention_near = gather_wholes(*gather_own(attention_pieces, attention_parts, 1))
     attention_blocks = gather_cores(*attention_near)
-    ffn_near = gather_near(
-        ffn_pieces, ffn_parts, (attention_blocks[0], *attention_near[1])
+    ffn_near = gather_halves(
+        *gather_own(ffn_pieces, ffn_parts, 2, (attention_blocks[0], *attention_near[1]))
     )
     gain_parts = []
     for start, width in ((0, D), (D, D), (2 * D, D), (3 * D, D), (4 * D, HD), (4 * D + HD, HD)):
@@ -941,8 +936,8 @@
         ),
         (tokens, gain_input, gain_query, gain_key, cosine, sine, order, *attention_blocks),
     )
-    ffn_weights = gather_cores(*ffn_near, (key_value,))
     key_values = [shifted(key_value, "group", offset) for offset in range(reach, 0, -1)]
+    ffn_weights = gather_cores(*ffn_near, key_values)
     key_values.append(key_value)
     probs, attended, attn_out, middle, out_weight = local_call(
         functools.partial(attend_kernel, attention_pieces),
@@ -982,7 +977,11 @@
             *key_values,
         ),
     )
-    over_x, over_y, sent = scatter_one(ffn_pieces, near_one, far_one, (grad_query,))
+    grad_key_values = [
+        shifted(value, "group", place - reach) if place < reach else value
+        for place, value in enumerate(grad_key_values)
+    ]
+    over_x, over_y, sent = scatter_one(ffn_pieces, near_one, far_one, grad_key_values[:-1])
     threes = scatter_three(ffn_pieces, near_three, far_three, (sent,))
     grad_query_weight, grad_normed, grad_gain_query = local_call(
         functools.partial(query_back_kernel, attention_pieces),
@@ -995,13 +994,6 @@
         (),
         (threes[0],),
     )
-    ffn_terms, sent = scatter_passed(
-        ffn_pieces, threes, over_x, over_y, near_one, far_one, (grad_normed,)
-    )
-    grad_key_values = [
-        shifted(value, "group", place - reach) if place < reach else value
-        for place, value in enumerate(grad_key_values)
-    ]
     *grads_attention, grad_inputs, _ = local_call(
         functools.partial(project_back_kernel, attention_pieces),
         (
@@ -1030,15 +1022,24 @@
             *grad_key_values,
         ),
         (),
-        (threes[1], threes[4], sent),
-    )
-    grads_ffn = scatter_high(ffn_pieces, ffn_terms)
+        (over_x, over_y),
+    )
+    ffn_terms, _ = scatter_passed(
+        ffn_pieces,
+        threes,
+        over_x,
+        over_y,
+        near_one,
+        far_one,
+        (grad_inputs, threes[1], threes[4]),
+    )
     near_three, near_one, far_three, far_one = grads_attention
     far_three, far_one = scatter_cores(far_three, far_one)
-    over_x, over_y, sent = scatter_one(attention_pieces, near_one, far_one)
-    threes = scatter_three(attention_pieces, near_three, far_three, (sent,))
+    grads_ffn, sent, arrived = scatter_high(ffn_pieces, ffn_terms)
+    over_x, over_y, sent = scatter_one(attention_pieces, near_one, far_one, (sent,))
+    threes = scatter_three(attention_pieces, near_three, far_three, (sent, arrived[0]))
     terms, _ = scatter_passed(attention_pieces, threes, over_x, over_y, near_one, far_one)
-    grads_attention = scatter_high(attention_pieces, terms)
+    grads_attention, _, _ = scatter_high(attention_pieces, terms)
     gain_grads = grads_attention[attention_rows:].reshape(-1)[: gains.shape[0]]
     grads_local = jnp.concatenate([grads_attention[:attention_rows], grads_ffn])
     return (

time: 242 us -> 237 us (0.979)
  Pallas kernels: 79.6 us -> 76.2 us
  waiting for transfers between devices: 81.9 us -> 85.3 us
  starting transfers between devices: 52.1 us -> 49.5 us
    pallas_call x19 -> x18, Pallas kernels: 79.6 us -> 76.2 us  [local_call(): pl.pallas_call(body, out_shape=outs, in_specs=specs, out_specs=tuple((pl....]
    ppermute x6, waiting for transfers between devices: 5.38 us -> 8.6 us  [shifted(): lax.ppermute(value, axis, [(source, source + steps) for source in range(i...]
    ppermute x46 -> x42, starting transfers between devices: 41.6 us -> 40.3 us  [swap(): lax.ppermute(value, ALL_AXES, [(source, source ^ mask) for source in rang...]
    ppermute x46 -> x42, waiting for transfers between devices: 76.5 us -> 76.7 us  [swap(): lax.ppermute(value, ALL_AXES, [(source, source ^ mask) for source in rang...]
    unnamed x118 -> x106, local copies, waits for them, and re-layouts: 14.1 us -> 14 us
  transfers between devices with their start and end apart: 52 -> 48, of which waited for: 31 -> 25; matrix products, arithmetic and copies ran while one was open for 3% -> 3% of each run, Pallas kernels for 22% -> 24%
where the time goes in v8:
time: 237 us; the launch traced here: 236 us
  waiting for transfers between devices  85.3 us (36%)
  Pallas kernels  76.2 us (32%)
  starting transfers between devices  49.5 us (21%)
  local copies, waits for them, and re-layouts  17.2 us (7%)
  other arithmetic  7.26 us (3%)
    ppermute x42, waiting for transfers between devices, swap(): lax.ppermute(value, ALL_AXES, [(source, source ^ mask) for source in rang...  76.7 us
    pallas_call x18, Pallas kernels, local_call(): pl.pallas_call(body, out_shape=outs, in_specs=specs, out_specs=tuple((pl....  76.2 us
    ppermute x42, starting transfers between devices, swap(): lax.ppermute(value, ALL_AXES, [(source, source ^ mask) for source in rang...  40.3 us
    unnamed x106, local copies, waits for them, and re-layouts  14 us
    ppermute x6, starting transfers between devices, shifted(): lax.ppermute(value, axis, [(source, source + steps) for source in range(i...  9.25 us
    ppermute x6, waiting for transfers between devices, shifted(): lax.ppermute(value, axis, [(source, source + steps) for source in range(i...  8.6 us
  transfers between devices with their start and end apart: 48, of which 25 were waited for; matrix products, arithmetic and copies ran while one was open for 3% of the time, Pallas kernels for 24%

profile of v8, /device:TPU:0, one launch (start us, length us, event | category | flops | bytes accessed | tf_op | source)
XLA Modules:
  0.0 236.4 jit_solution(11515709553606533243)
XLA Ops:
  1.8 5.1 %collective-permute-start.2 = (bf16[400,128]{1,0:T(8,128)(2,1)S(1)}, bf16[400,128]{1,0:T(8,128)(2,1)S(1)}, u32[]{:S(2)}, u32[]{:S(2)}) collective-permute-start(bf16[400,128]{1,0:T(8,128)(2,1)S(1)} %slice.65.refs_1_), channel_id=1, source_target_pairs={{0,24},{1,25},{2,26},{3,27},{4,28},{5,29},{6,30},{7,31},{8,16},{9,... | collective-permute-start | bytes 307208 | tf_op jit(solution)/shard_map/ppermute | solution.py:126
  7.6 3.2 %collective-permute-done.2.refs_4_ = bf16[400,128]{1,0:T(8,128)(2,1)S(1)} collective-permute-done((bf16[400,128]{1,0:T(8,128)(2,1)S(1)}, bf16[400,128]{1,0:T(8,128)(2,1)S(1)}, u32[]{:S(2)}, u32[]{:S(2)}) %collective-permute-start.2) | collective-permute-done | bytes 102432 | tf_op jit(solution)/shard_map/ppermute | solution.py:126
  10.8 4.8 %collective-permute-done.1.refs_3_ = bf16[400,128]{1,0:T(8,128)(2,1)S(1)} collective-permute-done((bf16[400,128]{1,0:T(8,128)(2,1)S(1)}, bf16[400,128]{1,0:T(8,128)(2,1)S(1)}, u32[]{:S(2)}, u32[]{:S(2)}) %collective-permute-start.1) | collective-permute-done | bytes 102432 | tf_op jit(solution)/shard_map/ppermute | solution.py:126
  20.3 2.5 %collective-permute-start.11 = (bf16[960,128]{1,0:T(8,128)(2,1)S(1)}, bf16[960,128]{1,0:T(8,128)(2,1)S(1)}, u32[]{:S(2)}, u32[]{:S(2)}) collective-permute-start(bf16[960,128]{1,0:T(8,128)(2,1)S(1)} %slice.66.refs_1_), channel_id=1, source_target_pairs={{0,8},{1,9},{2,10},{3,11},{4,12},{5,13},{6,14},{7,15},{8,0},{9,1},... | collective-permute-start | bytes 737288 | tf_op jit(solution)/shard_map/ppermute | solution.py:126
  24.4 4.5 %collective-permute-done.4.refs_3_ = bf16[1600,128]{1,0:T(8,128)(2,1)S(1)} collective-permute-done((bf16[1600,128]{1,0:T(8,128)(2,1)}, bf16[1600,128]{1,0:T(8,128)(2,1)S(1)}, u32[]{:S(2)}, u32[]{:S(2)}) %collective-permute-start.4) | collective-permute-done | bytes 409632 | tf_op jit(solution)/shard_map/ppermute | solution.py:126
  30.9 3.8 %collective-permute-done.3.refs_2_ = bf16[1600,128]{1,0:T(8,128)(2,1)S(1)} collective-permute-done((bf16[1600,128]{1,0:T(8,128)(2,1)}, bf16[1600,128]{1,0:T(8,128)(2,1)S(1)}, u32[]{:S(2)}, u32[]{:S(2)}) %collective-permute-start.3) | collective-permute-done | bytes 409632 | tf_op jit(solution)/shard_map/ppermute | solution.py:126
  35.5 2.4 %shard_map.153.refs_8_.refs_5_.refs_7_.refs_17_ = bf16[4800,128]{1,0:T(8,128)(2,1)} custom-call(s32[1]{0:T(128)} %bitcast.refs_0_, bf16[1600,128]{1,0:T(8,128)(2,1)} %shard_map.152.refs_1_, bf16[1600,128]{1,0:T(8,128)(2,1)} %copy-done.31, bf16[1600,128]{1,0:T(8,128)(2,1)} %copy-done.30), custom_call_target="tpu_custom_call" | custom-call | tf_op jit(solution)/shard_map/pallas_call | solution.py:138
  38.0 3.1 %collective-permute-done.5.refs_9_.refs_6_.refs_8_.refs_18_ = bf16[1600,128]{1,0:T(8,128)(2,1)S(1)} collective-permute-done((bf16[1600,128]{1,0:T(8,128)(2,1)S(1)}, bf16[1600,128]{1,0:T(8,128)(2,1)S(1)}, u32[]{:S(2)}, u32[]{:S(2)}) %collective-permute-start.5) | collective-permute-done | bytes 409632 | tf_op jit(solution)/shard_map/ppermute | solution.py:126
  42.5 7.0 %collective-permute-done.13.refs_4_ = bf16[960,128]{1,0:T(8,128)(2,1)S(1)} collective-permute-done((bf16[960,128]{1,0:T(8,128)(2,1)S(1)}, bf16[960,128]{1,0:T(8,128)(2,1)S(1)}, u32[]{:S(2)}, u32[]{:S(2)}) %collective-permute-start.13) | collective-permute-done | bytes 245792 | tf_op jit(solution)/shard_map/ppermute | solution.py:126
  50.3 2.9 %shard_map.155 = (bf16[1920,128]{1,0:T(8,128)(2,1)}, bf16[1920,128]{1,0:T(8,128)(2,1)}) custom-call(s32[1]{0:T(128)} %bitcast.refs_0_, bf16[960,128]{1,0:T(8,128)(2,1)} %copy-done.19, bf16[960,128]{1,0:T(8,128)(2,1)} %copy-done.33, bf16[960,128]{1,0:T(8,128)(2,1)} %copy-done.32, bf16[960,128]{1,0:T(8,128)(2,1)} %copy-done.34, ...), custom_call_target="tpu_custom_call" | custom-call | tf_op jit(solution)/shard_map/pallas_call | solution.py:138
  60.5 3.9 %shard_map.154 = (bf16[128,640]{1,0:T(8,128)(2,1)}, f32[128,1024]{1,0:T(8,128)}, f32[128,256]{1,0:T(8,128)}, bf16[128,1024]{1,0:T(8,128)(2,1)}, bf16[128,512]{1,0:T(8,128)(2,1)}) custom-call(s32[1]{0:T(128)} %bitcast.refs_0_, bf16[128,640]{1,0:T(8,128)(2,1)} %refs_1_.5, f32[1,640]{1,0:T(1,128)} %broadcast_in_dim.15.refs_2_, f32[1,256]{1,0:T(1,128)} %bitcast.23, ...), custom_call_target="tpu_custom_call" | custom-call | tf_op jit(solution)/shard_map/pallas_call | solution.py:138
  67.5 2.4 %collective-permute-start.9 = (bf16[128,512]{1,0:T(8,128)(2,1)}, bf16[128,512]{1,0:T(8,128)(2,1)S(1)}, u32[]{:S(2)}, u32[]{:S(2)}) collective-permute-start(bf16[128,512]{1,0:T(8,128)(2,1)} %get-tuple-element.72.refs_12_.refs_11_), channel_id=1, source_target_pairs={{0,2},{1,3},{4,6},{5,7},{8,10},{9,11},{12,14},{13,15},{16,18},{17,... | collective-permute-start | bytes 393224 | tf_op jit(solution)/shard_map/ppermute | solution.py:33
  71.4 5.4 %collective-permute-done.17.refs_6_ = bf16[1920,128]{1,0:T(8,128)(2,1)} collective-permute-done((bf16[1920,128]{1,0:T(8,128)(2,1)}, bf16[1920,128]{1,0:T(8,128)(2,1)}, u32[]{:S(2)}, u32[]{:S(2)}) %collective-permute-start.17) | collective-permute-done | bytes 491552 | tf_op jit(solution)/shard_map/ppermute | solution.py:126
  81.1 3.6 %shard_map.156.refs_13_.refs_6_ = bf16[11520,128]{1,0:T(8,128)(2,1)} custom-call(s32[1]{0:T(128)} %bitcast.refs_0_, bf16[1920,128]{1,0:T(8,128)(2,1)} %get-tuple-element.73.refs_1_, bf16[1920,128]{1,0:T(8,128)(2,1)} %get-tuple-element.74.refs_2_, bf16[1920,128]{1,0:T(8,128)(2,1)} %collective-permute-done.14.refs_3_, ...), custom_call_target="tpu_custom_call" | custom-call | tf_op jit(solution)/shard_map/pallas_call | solution.py:138
  88.4 10.2 %collective-permute-done.18.refs_7_ = bf16[1920,128]{1,0:T(8,128)(2,1)S(1)} collective-permute-done((bf16[1920,128]{1,0:T(8,128)(2,1)}, bf16[1920,128]{1,0:T(8,128)(2,1)S(1)}, u32[]{:S(2)}, u32[]{:S(2)}) %collective-permute-start.18) | collective-permute-done | bytes 491552 | tf_op jit(solution)/shard_map/ppermute | solution.py:126
  102.6 5.7 %shard_map.157 = (f32[128,2048]{1,0:T(8,128)}, bf16[128,1024]{1,0:T(8,128)(2,1)}, f32[128,640]{1,0:T(8,128)}, f32[128,640]{1,0:T(8,128)}, bf16[1024,640]{1,0:T(8,128)(2,1)}) custom-call(s32[1]{0:T(128)} %bitcast.refs_0_, bf16[128,640]{1,0:T(8,128)(2,1)} %refs_1_.5, f32[1,640]{1,0:T(1,128)} %broadcast_in_dim.14.refs_2_.refs_3_, f32[128,512]{1,0:T(8,128)} %fusion.4.refs_3_, ...), custom_call_target="tpu_custom_call" | custom-call | tf_op jit(solution)/shard_map/pallas_call | solution.py:138
  110.0 14.6 %shard_map.158 = (bf16[128,640]{1,0:T(8,128)(2,1)}, f32[128,640]{1,0:T(8,128)}, f32[1,640]{1,0:T(1,128)}, f32[1,640]{1,0:T(1,128)}, bf16[11520,128]{1,0:T(8,128)...) custom-call(s32[1]{0:T(128)} %bitcast.refs_0_, ...), custom_call_target="tpu_custom_call" | custom-call | tf_op jit(solution)/shard_map/pallas_call | solution.py:138
  125.2 6.2 %shard_map.159 = (bf16[1024,640]{1,0:T(8,128)(2,1)}, f32[128,1024]{1,0:T(8,128)}, f32[1,640]{1,0:T(1,128)}, bf16[128,512]{1,0:T(8,128)(2,1)}, bf16[128,512]{1,0:...) custom-call(s32[1]{0:T(128)} %bitcast.refs_0_, f32[128,640]{1,0:T(8,128)} %get-tuple-element.80.refs_1_.refs_11_, ...), custom_call_target="tpu_custom_call" | custom-call | tf_op jit(solution)/shard_map/pallas_call | solution.py:138
  135.4 2.4 %collective-permute-done.25.refs_3_.refs_21_ = bf16[128,512]{1,0:T(8,128)(2,1)S(1)} collective-permute-done((bf16[128,512]{1,0:T(8,128)(2,1)}, bf16[128,512]{1,0:T(8,128)(2,1)S(1)}, u32[]{:S(2)}, u32[]{:S(2)}) %collective-permute-start.25) | collective-permute-done | bytes 131104 | tf_op jit(solution)/shard_map/ppermute | solution.py:33
  137.8 2.8 %collective-permute-done.26.refs_4_.refs_22_ = bf16[128,512]{1,0:T(8,128)(2,1)S(1)} collective-permute-done((bf16[128,512]{1,0:T(8,128)(2,1)}, bf16[128,512]{1,0:T(8,128)(2,1)S(1)}, u32[]{:S(2)}, u32[]{:S(2)}) %collective-permute-start.26) | collective-permute-done | bytes 131104 | tf_op jit(solution)/shard_map/ppermute | solution.py:33
  141.7 2.6 %shard_map.160 = (bf16[1920,128]{1,0:T(8,128)(2,1)}, bf16[1920,128]{1,0:T(8,128)(2,1)}) custom-call(s32[1]{0:T(128)} %bitcast.refs_0_, bf16[3840,128]{1,0:T(8,128)(2,1)} %get-tuple-element.88.refs_1_.refs_5_, bf16[3840,128]{1,0:T(8,128)(2,1)} %copy-done.3, bf16[128,512]{1,0:T(8,128)(2,1)} %copy-done.22, bf16[128,512]{1,0:T(8,128)(2,1)} %copy-done.23, ...), custom_call_target="tpu_custom_call" | custom-call | tf_op jit(solution)/shard_map/pallas_call | solution.py:138
  147.6 4.5 %shard_map.161 = (bf16[3840,128]{1,0:T(8,128)(2,1)}, bf16[1920,128]{1,0:T(8,128)(2,1)}, bf16[1920,128]{1,0:T(8,128)(2,1)}, bf16[1920,128]{1,0:T(8,128)(2,1)}, bf16[1920,128]{1,0:T(8,128)(2,1)}) custom-call(s32[1]{0:T(128)} %bitcast.refs_0_, bf16[11520,128]{1,0:T(8,128)(2,1)} %get-tuple-element.86.refs_1_, bf16[11520,128]{1,0:T(8,128)(2,1)} %copy-done.4, ...), custom_call_target="tpu_custom_call" | custom-call | tf_op jit(solution)/shard_map/pallas_call | solution.py:138
  154.5 4.5 %shard_map.162 = (bf16[640,1024]{1,0:T(8,128)(2,1)}, f32[128,640]{1,0:T(8,128)}, f32[1,256]{1,0:T(1,128)}) custom-call(s32[1]{0:T(128)} %bitcast.refs_0_, f32[1,256]{1,0:T(1,128)} %bitcast.24, f32[128,128]{1,0:T(8,128)} %get-tuple-element.147.refs_5_.refs_2_.refs_4_, f32[128,128]{1,0:T(8,128)} %get-tuple-element.146.refs_6_.refs_3_.refs_5_, ...), custom_call_target="tpu_custom_call" | custom-call | tf_op jit(solution)/shard_map/pallas_call | solution.py:138
  160.0 6.6 %shard_map.163 = (bf16[4800,128]{1,0:T(8,128)(2,1)}, bf16[1632,128]{1,0:T(8,128)(2,1)}, bf16[4800,128]{1,0:T(8,128)(2,1)}, bf16[1632,128]{1,0:T(8,128)(2,1)}, bf...) custom-call(s32[1]{0:T(128)} %bitcast.refs_0_, bf16[128,640]{1,0:T(8,128)(2,1)} %refs_1_.5, f32[1,640]{1,0:T(1,128)} %broadcast_in_dim.15.refs_2_, ...), custom_call_target="tpu_custom_call" | custom-call | tf_op jit(solution)/shard_map/pallas_call | solution.py:138
  170.5 3.2 %shard_map.164 = (bf16[1920,128]{1,0:T(8,128)(2,1)}, bf16[1920,128]{1,0:T(8,128)(2,1)}, f32[8,128]{1,0:T(8,128)}) custom-call(s32[1]{0:T(128)} %bitcast.refs_0_, bf16[1920,128]{1,0:T(8,128)(2,1)} %get-tuple-element.110.refs_1_, bf16[1920,128]{1,0:T(8,128)(2,1)} %get-tuple-element.111.refs_2_, bf16[1920,128]{1,0:T(8,128)(2,1)} %copy-done.10, ...), custom_call_target="tpu_custom_call" | custom-call | tf_op jit(solution)/shard_map/pallas_call | solution.py:138
  175.4 11.7 %collective-permute-done.34.refs_3_ = bf16[1920,128]{1,0:T(8,128)(2,1)S(1)} collective-permute-done((bf16[1920,128]{1,0:T(8,128)(2,1)}, bf16[1920,128]{1,0:T(8,128)(2,1)S(1)}, u32[]{:S(2)}, u32[]{:S(2)}) %collective-permute-start.34) | collective-permute-done | bytes 491552 | tf_op jit(solution)/shard_map/ppermute | solution.py:126
  189.0 4.1 %shard_map.165 = (f32[960,128]{1,0:T(8,128)}, bf16[960,128]{1,0:T(8,128)(2,1)}, bf16[960,128]{1,0:T(8,128)(2,1)}, bf16[960,128]{1,0:T(8,128)(2,1)}) custom-call(s32[1]{0:T(128)} %bitcast.refs_0_, bf16[3840,128]{1,0:T(8,128)(2,1)} %get-tuple-element.94.refs_11_.refs_1_, bf16[1920,128]{1,0:T(8,128)(2,1)} %copy-done.8, bf16[1920,128]{1,0:T(8,128)(2,1)} %copy-done.25, ...), custom_call_target="tpu_custom_call" | custom-call | tf_op jit(solution)/shard_map/pallas_call | solution.py:138
  197.0 3.0 %collective-permute-done.36.refs_4_ = bf16[960,128]{1,0:T(8,128)(2,1)S(1)} collective-permute-done((bf16[960,128]{1,0:T(8,128)(2,1)}, bf16[960,128]{1,0:T(8,128)(2,1)S(1)}, u32[]{:S(2)}, u32[]{:S(2)}) %collective-permute-start.36) | collective-permute-done | bytes 245792 | tf_op jit(solution)/shard_map/ppermute | solution.py:126
  201.2 2.8 %shard_map.167 = (bf16[1600,128]{1,0:T(8,128)(2,1)}, bf16[800,128]{1,0:T(8,128)(2,1)}, bf16[800,128]{1,0:T(8,128)(2,1)}, bf16[800,128]{1,0:T(8,128)(2,1)}, bf16[800,128]{1,0:T(8,128)(2,1)}) custom-call(s32[1]{0:T(128)} %bitcast.refs_0_, bf16[4800,128]{1,0:T(8,128)(2,1)} %get-tuple-element.105.refs_1_, bf16[4800,128]{1,0:T(8,128)(2,1)} %copy-done.13, ...), custom_call_target="tpu_custom_call" | custom-call | tf_op jit(solution)/shard_map/pallas_call | solution.py:138
  213.9 3.4 %collective-permute-done.40.refs_3_ = bf16[800,128]{1,0:T(8,128)(2,1)S(1)} collective-permute-done((bf16[800,128]{1,0:T(8,128)(2,1)}, bf16[800,128]{1,0:T(8,128)(2,1)S(1)}, u32[]{:S(2)}, u32[]{:S(2)}) %collective-permute-start.40) | collective-permute-done | bytes 204832 | tf_op jit(solution)/shard_map/ppermute | solution.py:126
  220.3 2.4 %shard_map.169 = (f32[432,128]{1,0:T(8,128)}, bf16[432,128]{1,0:T(8,128)(2,1)}, bf16[432,128]{1,0:T(8,128)(2,1)}, bf16[432,128]{1,0:T(8,128)(2,1)}) custom-call(s32[1]{0:T(128)} %bitcast.refs_0_, bf16[1600,128]{1,0:T(8,128)(2,1)} %get-tuple-element.119.refs_1_, bf16[800,128]{1,0:T(8,128)(2,1)} %copy-done.38, bf16[800,128]{1,0:T(8,128)(2,1)} %copy-done.40, ...), custom_call_target="tpu_custom_call" | custom-call | tf_op jit(solution)/shard_map/pallas_call | solution.py:138
  228.0 6.0 %collective-permute-done.44 = bf16[432,128]{1,0:T(8,128)(2,1)S(1)} collective-permute-done((bf16[432,128]{1,0:T(8,128)(2,1)}, bf16[432,128]{1,0:T(8,128)(2,1)S(1)}, u32[]{:S(2)}, u32[]{:S(2)}) %collective-permute-start.44) | collective-permute-done | bytes 110624 | tf_op jit(solution)/shard_map/ppermute | solution.py:126
  (218 shorter events, 84.2 us)
Async XLA Ops:
  18.2 10.7 %collective-permute-start.4 = (bf16[1600,128]{1,0:T(8,128)(2,1)}, bf16[1600,128]{1,0:T(8,128)(2,1)S(1)}, u32[]{:S(2)}, u32[]{:S(2)}) collective-permute-start(bf16[1600,128]{1,0:T(8,128)(2,1)} %shard_map.152.refs_1_), channel_id=1, source_target_pairs={{0,2},{1,3},{2,0},{3,1},{4,6},{5,7},{6,4},{7,5},{8,10},{9,11},{10,... | collective-permute-start | bytes 1228808 | tf_op jit(solution)/shard_map/ppermute | solution.py:126
  19.8 21.4 %collective-permute-start.12 = (bf16[960,128]{1,0:T(8,128)(2,1)S(1)}, bf16[960,128]{1,0:T(8,128)(2,1)S(1)}, u32[]{:S(2)}, u32[]{:S(2)}) collective-permute-start(bf16[960,128]{1,0:T(8,128)(2,1)S(1)} %slice.66.refs_1_), channel_id=1, source_target_pairs={{0,16},{1,17},{2,18},{3,19},{4,20},{5,21},{6,22},{7,23},{8,24},{9,... | collective-permute-start | bytes 737288 | tf_op jit(solution)/shard_map/ppermute | solution.py:126
  20.3 22.2 %collective-permute-start.11 = (bf16[960,128]{1,0:T(8,128)(2,1)S(1)}, bf16[960,128]{1,0:T(8,128)(2,1)S(1)}, u32[]{:S(2)}, u32[]{:S(2)}) collective-permute-start(bf16[960,128]{1,0:T(8,128)(2,1)S(1)} %slice.66.refs_1_), channel_id=1, source_target_pairs={{0,8},{1,9},{2,10},{3,11},{4,12},{5,13},{6,14},{7,15},{8,0},{9,1},... | collective-permute-start | bytes 737288 | tf_op jit(solution)/shard_map/ppermute | solution.py:126
  22.9 11.9 %collective-permute-start.3 = (bf16[1600,128]{1,0:T(8,128)(2,1)}, bf16[1600,128]{1,0:T(8,128)(2,1)S(1)}, u32[]{:S(2)}, u32[]{:S(2)}) collective-permute-start(bf16[1600,128]{1,0:T(8,128)(2,1)} %shard_map.152.refs_1_), channel_id=1, source_target_pairs={{0,4},{1,5},{2,6},{3,7},{4,0},{5,1},{6,2},{7,3},{8,12},{9,13},{10,... | collective-permute-start | bytes 1228808 | tf_op jit(solution)/shard_map/ppermute | solution.py:126
  28.9 12.1 %collective-permute-start.5 = (bf16[1600,128]{1,0:T(8,128)(2,1)S(1)}, bf16[1600,128]{1,0:T(8,128)(2,1)S(1)}, u32[]{:S(2)}, u32[]{:S(2)}) collective-permute-start(bf16[1600,128]{1,0:T(8,128)(2,1)S(1)} %collective-permute-done.4.refs_3_), channel_id=1, source_target_pairs={{0,4},{1,5},{2,6},{3,7},{4,0},{5,1},{6,2},{7,3},{8,12},{9,13},{10,... | collective-permute-start | bytes 1228808 | tf_op jit(solution)/shard_map/ppermute | solution.py:126
  37.9 21.6 %collective-permute-start.6 = (bf16[4800,128]{1,0:T(8,128)(2,1)}, bf16[4800,128]{1,0:T(8,128)(2,1)S(1)}, u32[]{:S(2)}, u32[]{:S(2)}) collective-permute-start(bf16[4800,128]{1,0:T(8,128)(2,1)} %shard_map.153.refs_8_.refs_5_.refs_7_.refs_17_), channel_id=1, source_target_pairs={{0,1},{1,0},{2,3},{3,2},{4,5},{5,4},{6,7},{7,6},{8,9},{9,8},{10,11... | collective-permute-start | bytes 3686408 | tf_op jit(solution)/shard_map/ppermute | solution.py:126
  41.1 15.6 %collective-permute-start.7 = (bf16[1600,128]{1,0:T(8,128)(2,1)S(1)}, bf16[1600,128]{1,0:T(8,128)(2,1)S(1)}, u32[]{:S(2)}, u32[]{:S(2)}) collective-permute-start(bf16[1600,128]{1,0:T(8,128)(2,1)S(1)} %collective-permute-done.5.refs_9_.refs_6_.refs_8_.refs_18_), channel_id=1, source_target_pairs={{0,1},{1,0},{2,3},{3,2},{4,5},{5,4},{6,7},{7,6},{8,9},{9,8},{10,11... | collective-permute-start | bytes 1228808 | tf_op jit(solution)/shard_map/ppermute | solution.py:126
  53.1 14.3 %collective-permute-start.16 = (bf16[1920,128]{1,0:T(8,128)(2,1)}, bf16[1920,128]{1,0:T(8,128)(2,1)S(1)}, u32[]{:S(2)}, u32[]{:S(2)}) collective-permute-start(bf16[1920,128]{1,0:T(8,128)(2,1)} %get-tuple-element.73.refs_1_), channel_id=1, source_target_pairs={{0,2},{1,3},{2,0},{3,1},{4,6},{5,7},{6,4},{7,5},{8,10},{9,11},{10,... | collective-permute-start | bytes 1474568 | tf_op jit(solution)/shard_map/ppermute | solution.py:126
  53.6 16.2 %collective-permute-start.14 = (bf16[1920,128]{1,0:T(8,128)(2,1)}, bf16[1920,128]{1,0:T(8,128)(2,1)}, u32[]{:S(2)}, u32[]{:S(2)}) collective-permute-start(bf16[1920,128]{1,0:T(8,128)(2,1)} %get-tuple-element.73.refs_1_), channel_id=1, source_target_pairs={{0,4},{1,5},{2,6},{3,7},{4,0},{5,1},{6,2},{7,3},{8,12},{9,13},{10,... | collective-permute-start | bytes 1474568 | tf_op jit(solution)/shard_map/ppermute | solution.py:126
  55.1 21.7 %collective-permute-start.17 = (bf16[1920,128]{1,0:T(8,128)(2,1)}, bf16[1920,128]{1,0:T(8,128)(2,1)}, u32[]{:S(2)}, u32[]{:S(2)}) collective-permute-start(bf16[1920,128]{1,0:T(8,128)(2,1)} %get-tuple-element.74.refs_2_), channel_id=1, source_target_pairs={{0,2},{1,3},{2,0},{3,1},{4,6},{5,7},{6,4},{7,5},{8,10},{9,11},{10,... | collective-permute-start | bytes 1474568 | tf_op jit(solution)/shard_map/ppermute | solution.py:126
  56.7 20.4 %collective-permute-start.15 = (bf16[1920,128]{1,0:T(8,128)(2,1)}, bf16[1920,128]{1,0:T(8,128)(2,1)}, u32[]{:S(2)}, u32[]{:S(2)}) collective-permute-start(bf16[1920,128]{1,0:T(8,128)(2,1)} %get-tuple-element.74.refs_2_), channel_id=1, source_target_pairs={{0,4},{1,5},{2,6},{3,7},{4,0},{5,1},{6,2},{7,3},{8,12},{9,13},{10,... | collective-permute-start | bytes 1474568 | tf_op jit(solution)/shard_map/ppermute | solution.py:126
  64.4 12.6 %collective-permute-start.10 = (bf16[128,512]{1,0:T(8,128)(2,1)}, bf16[128,512]{1,0:T(8,128)(2,1)S(1)}, u32[]{:S(2)}, u32[]{:S(2)}) collective-permute-start(bf16[128,512]{1,0:T(8,128)(2,1)} %get-tuple-element.72.refs_12_.refs_11_), channel_id=1, source_target_pairs={{0,1},{1,2},{2,3},{4,5},{5,6},{6,7},{8,9},{9,10},{10,11},{12,13},{... | collective-permute-start | bytes 393224 | tf_op jit(solution)/shard_map/ppermute | solution.py:33
  67.5 11.5 %collective-permute-start.9 = (bf16[128,512]{1,0:T(8,128)(2,1)}, bf16[128,512]{1,0:T(8,128)(2,1)S(1)}, u32[]{:S(2)}, u32[]{:S(2)}) collective-permute-start(bf16[128,512]{1,0:T(8,128)(2,1)} %get-tuple-element.72.refs_12_.refs_11_), channel_id=1, source_target_pairs={{0,2},{1,3},{4,6},{5,7},{8,10},{9,11},{12,14},{13,15},{16,18},{17,... | collective-permute-start | bytes 393224 | tf_op jit(solution)/shard_map/ppermute | solution.py:33
  69.9 10.6 %collective-permute-start.8 = (bf16[128,512]{1,0:T(8,128)(2,1)}, bf16[128,512]{1,0:T(8,128)(2,1)S(1)}, u32[]{:S(2)}, u32[]{:S(2)}) collective-permute-start(bf16[128,512]{1,0:T(8,128)(2,1)} %get-tuple-element.72.refs_12_.refs_11_), channel_id=1, source_target_pairs={{0,3},{4,7},{8,11},{12,15},{16,19},{20,23},{24,27},{28,31}} | collective-permute-start | bytes 393224 | tf_op jit(solution)/shard_map/ppermute | solution.py:33
  84.7 23.6 %collective-permute-start.20 = (bf16[11520,128]{1,0:T(8,128)(2,1)}, bf16[11520,128]{1,0:T(8,128)(2,1)S(1)}, u32[]{:S(2)}, u32[]{:S(2)}) collective-permute-start(bf16[11520,128]{1,0:T(8,128)(2,1)} %shard_map.156.refs_13_.refs_6_), channel_id=1, source_target_pairs={{0,1},{1,0},{2,3},{3,2},{4,5},{5,4},{6,7},{7,6},{8,9},{9,8},{10,11... | collective-permute-start | bytes 8847368 | tf_op jit(solution)/shard_map/ppermute | solution.py:126
  84.8 13.8 %collective-permute-start.18 = (bf16[1920,128]{1,0:T(8,128)(2,1)}, bf16[1920,128]{1,0:T(8,128)(2,1)S(1)}, u32[]{:S(2)}, u32[]{:S(2)}) collective-permute-start(bf16[1920,128]{1,0:T(8,128)(2,1)} %copy-done.27), channel_id=1, source_target_pairs={{0,4},{1,5},{2,6},{3,7},{4,0},{5,1},{6,2},{7,3},{8,12},{9,13},{10,... | collective-permute-start | bytes 1474568 | tf_op jit(solution)/shard_map/ppermute | solution.py:126
  86.2 13.7 %collective-permute-start.19 = (bf16[1920,128]{1,0:T(8,128)(2,1)}, bf16[1920,128]{1,0:T(8,128)(2,1)}, u32[]{:S(2)}, u32[]{:S(2)}) collective-permute-start(bf16[1920,128]{1,0:T(8,128)(2,1)} %collective-permute-done.15.refs_4_), channel_id=1, source_target_pairs={{0,2},{1,3},{2,0},{3,1},{4,6},{5,7},{6,4},{7,5},{8,10},{9,11},{10,... | collective-permute-start | bytes 1474568 | tf_op jit(solution)/shard_map/ppermute | solution.py:126
  124.6 21.3 %collective-permute-start.23 = (bf16[11520,128]{1,0:T(8,128)(2,1)}, bf16[11520,128]{1,0:T(8,128)(2,1)S(1)}, u32[]{:S(2)}, u32[]{:S(2)}) collective-permute-start(bf16[11520,128]{1,0:T(8,128)(2,1)} %get-tuple-element.87), channel_id=1, source_target_pairs={{0,1},{1,0},{2,3},{3,2},{4,5},{5,4},{6,7},{7,6},{8,9},{9,8},{10,11... | collective-permute-start | bytes 8847368 | tf_op jit(solution)/shard_map/ppermute | solution.py:126
  125.1 15.5 %collective-permute-start.24 = (bf16[3840,128]{1,0:T(8,128)(2,1)}, bf16[3840,128]{1,0:T(8,128)(2,1)S(1)}, u32[]{:S(2)}, u32[]{:S(2)}) collective-permute-start(bf16[3840,128]{1,0:T(8,128)(2,1)} %get-tuple-element.89), channel_id=1, source_target_pairs={{0,1},{1,0},{2,3},{3,2},{4,5},{5,4},{6,7},{7,6},{8,9},{9,8},{10,11... | collective-permute-start | bytes 2949128 | tf_op jit(solution)/shard_map/ppermute | solution.py:126
  144.3 14.7 %collective-permute-start.28 = (bf16[1920,128]{1,0:T(8,128)(2,1)}, bf16[1920,128]{1,0:T(8,128)(2,1)S(1)}, u32[]{:S(2)}, u32[]{:S(2)}) collective-permute-start(bf16[1920,128]{1,0:T(8,128)(2,1)} %get-tuple-element.103), channel_id=1, source_target_pairs={{0,4},{1,5},{2,6},{3,7},{4,0},{5,1},{6,2},{7,3},{8,12},{9,13},{10,... | collective-permute-start | bytes 1474568 | tf_op jit(solution)/shard_map/ppermute | solution.py:126
  144.9 14.3 %collective-permute-start.29 = (bf16[1920,128]{1,0:T(8,128)(2,1)}, bf16[1920,128]{1,0:T(8,128)(2,1)S(1)}, u32[]{:S(2)}, u32[]{:S(2)}) collective-permute-start(bf16[1920,128]{1,0:T(8,128)(2,1)} %get-tuple-element.93.refs_3_), channel_id=1, source_target_pairs={{0,2},{1,3},{2,0},{3,1},{4,6},{5,7},{6,4},{7,5},{8,10},{9,11},{10,... | collective-permute-start | bytes 1474568 | tf_op jit(solution)/shard_map/ppermute | solution.py:126
  152.1 16.8 %collective-permute-start.32 = (bf16[1920,128]{1,0:T(8,128)(2,1)}, bf16[1920,128]{1,0:T(8,128)(2,1)S(1)}, u32[]{:S(2)}, u32[]{:S(2)}) collective-permute-start(bf16[1920,128]{1,0:T(8,128)(2,1)} %get-tuple-element.109), channel_id=1, source_target_pairs={{0,4},{1,5},{2,6},{3,7},{4,0},{5,1},{6,2},{7,3},{8,12},{9,13},{10,... | collective-permute-start | bytes 1474568 | tf_op jit(solution)/shard_map/ppermute | solution.py:126
  153.5 16.2 %collective-permute-start.33 = (bf16[1920,128]{1,0:T(8,128)(2,1)}, bf16[1920,128]{1,0:T(8,128)(2,1)S(1)}, u32[]{:S(2)}, u32[]{:S(2)}) collective-permute-start(bf16[1920,128]{1,0:T(8,128)(2,1)} %get-tuple-element.112), channel_id=1, source_target_pairs={{0,2},{1,3},{2,0},{3,1},{4,6},{5,7},{6,4},{7,5},{8,10},{9,11},{10,... | collective-permute-start | bytes 1474568 | tf_op jit(solution)/shard_map/ppermute | solution.py:126
  166.6 33.5 %collective-permute-start.30 = (bf16[4800,128]{1,0:T(8,128)(2,1)}, bf16[4800,128]{1,0:T(8,128)(2,1)S(1)}, u32[]{:S(2)}, u32[]{:S(2)}) collective-permute-start(bf16[4800,128]{1,0:T(8,128)(2,1)} %get-tuple-element.106), channel_id=1, source_target_pairs={{0,1},{1,0},{2,3},{3,2},{4,5},{5,4},{6,7},{7,6},{8,9},{9,8},{10,11... | collective-permute-start | bytes 3686408 | tf_op jit(solution)/shard_map/ppermute | solution.py:126
  173.7 13.4 %collective-permute-start.34 = (bf16[1920,128]{1,0:T(8,128)(2,1)}, bf16[1920,128]{1,0:T(8,128)(2,1)S(1)}, u32[]{:S(2)}, u32[]{:S(2)}) collective-permute-start(bf16[1920,128]{1,0:T(8,128)(2,1)} %get-tuple-element.113), channel_id=1, source_target_pairs={{0,4},{1,5},{2,6},{3,7},{4,0},{5,1},{6,2},{7,3},{8,12},{9,13},{10,... | collective-permute-start | bytes 1474568 | tf_op jit(solution)/shard_map/ppermute | solution.py:126
  175.1 13.1 %collective-permute-start.35 = (bf16[1920,128]{1,0:T(8,128)(2,1)}, bf16[1920,128]{1,0:T(8,128)(2,1)S(1)}, u32[]{:S(2)}, u32[]{:S(2)}) collective-permute-start(bf16[1920,128]{1,0:T(8,128)(2,1)} %get-tuple-element.114), channel_id=1, source_target_pairs={{0,2},{1,3},{2,0},{3,1},{4,6},{5,7},{6,4},{7,5},{8,10},{9,11},{10,... | collective-permute-start | bytes 1474568 | tf_op jit(solution)/shard_map/ppermute | solution.py:126
  175.4 18.0 %collective-permute-start.31 = (bf16[1632,128]{1,0:T(8,128)(2,1)S(1)}, bf16[1632,128]{1,0:T(8,128)(2,1)S(1)}, u32[]{:S(2)}, u32[]{:S(2)}) collective-permute-start(bf16[1632,128]{1,0:T(8,128)(2,1)S(1)} %copy-done.49), channel_id=1, source_target_pairs={{0,1},{1,0},{2,3},{3,2},{4,5},{5,4},{6,7},{7,6},{8,9},{9,8},{10,11... | collective-permute-start | bytes 1253384 | tf_op jit(solution)/shard_map/ppermute | solution.py:126
  196.1 11.3 %collective-permute-start.38 = (bf16[832,128]{1,0:T(8,128)(2,1)}, bf16[832,128]{1,0:T(8,128)(2,1)S(1)}, u32[]{:S(2)}, u32[]{:S(2)}) collective-permute-start(bf16[832,128]{1,0:T(8,128)(2,1)} %get-tuple-element.123), channel_id=1, source_target_pairs={{0,4},{1,5},{2,6},{3,7},{4,0},{5,1},{6,2},{7,3},{8,12},{9,13},{10,... | collective-permute-start | bytes 638984 | tf_op jit(solution)/shard_map/ppermute | solution.py:126
  196.7 10.7 %collective-permute-start.39 = (bf16[800,128]{1,0:T(8,128)(2,1)}, bf16[800,128]{1,0:T(8,128)(2,1)S(1)}, u32[]{:S(2)}, u32[]{:S(2)}) collective-permute-start(bf16[800,128]{1,0:T(8,128)(2,1)} %get-tuple-element.117.refs_3_), channel_id=1, source_target_pairs={{0,2},{1,3},{2,0},{3,1},{4,6},{5,7},{6,4},{7,5},{8,10},{9,11},{10,... | collective-permute-start | bytes 614408 | tf_op jit(solution)/shard_map/ppermute | solution.py:126
  204.7 22.5 %collective-permute-start.46 = (bf16[960,128]{1,0:T(8,128)(2,1)S(1)}, bf16[960,128]{1,0:T(8,128)(2,1)S(1)}, u32[]{:S(2)}, u32[]{:S(2)}) collective-permute-start(bf16[960,128]{1,0:T(8,128)(2,1)S(1)} %copy-done.51), channel_id=1, source_target_pairs={{0,16},{1,17},{2,18},{3,19},{4,20},{5,21},{6,22},{7,23},{8,24},{9,... | collective-permute-start | bytes 737288 | tf_op jit(solution)/shard_map/ppermute | solution.py:126
  205.4 21.8 %collective-permute-start.47 = (bf16[960,128]{1,0:T(8,128)(2,1)S(1)}, bf16[960,128]{1,0:T(8,128)(2,1)S(1)}, u32[]{:S(2)}, u32[]{:S(2)}) collective-permute-start(bf16[960,128]{1,0:T(8,128)(2,1)S(1)} %copy-done.50), channel_id=1, source_target_pairs={{0,24},{1,25},{2,26},{3,27},{4,28},{5,29},{6,30},{7,31},{8,16},{9,... | collective-permute-start | bytes 737288 | tf_op jit(solution)/shard_map/ppermute | solution.py:126
  223.6 10.5 %collective-permute-start.44 = (bf16[432,128]{1,0:T(8,128)(2,1)}, bf16[432,128]{1,0:T(8,128)(2,1)S(1)}, u32[]{:S(2)}, u32[]{:S(2)}) collective-permute-start(bf16[432,128]{1,0:T(8,128)(2,1)} %get-tuple-element.130), channel_id=1, source_target_pairs={{0,16},{1,17},{2,18},{3,19},{4,20},{5,21},{6,22},{7,23},{8,24},{9,... | collective-permute-start | bytes 331784 | tf_op jit(solution)/shard_map/ppermute | solution.py:126
  (69 other events, 431.5 us)

commit v9 on v8

--- a/solution.py
+++ b/solution.py
@@ -118,7 +118,8 @@
 
 
 def aligned(device_count):
-    return device_count % LOW_COUNT == 0 and D % device_count == 0
+    groups = lax.axis_size("group") == 4
+    return groups and device_count % LOW_COUNT == 0 and D % device_count == 0
 
 
 def swap(value, mask):
@@ -157,13 +158,6 @@
         self.high_count = device_count // LOW_COUNT
         self.block_rows = self.own_rows * self.high_count
         self.size = self.block_rows * self.blocks
-
-
-def join_kernel(index_ref, *refs):
-    out_ref = refs[-1]
-    rows = refs[0].shape[0]
-    for place, ref in enumerate(refs[:-1]):
-        out_ref[place * rows : (place + 1) * rows, :] = ref[...]
 
 
 def pack_kernel(pieces, index_ref, *refs):
@@ -200,20 +194,26 @@
     index_ref,
     near_ref,
     far_ref,
-    own_ref,
-    beside_first_ref,
-    beside_second_ref,
-    across_first_ref,
-    across_second_ref,
+    *refs,
 ):
+    key_refs = refs[:-5]
+    own_ref, beside_first_ref, beside_second_ref, across_first_ref, across_second_ref = refs[-5:]
     half = size // 2
+    if key_refs:
+        across_key_ref, cores_key_ref = key_refs
+        rows = across_key_ref.shape[0]
+        keys = across_key_ref[...] + cores_key_ref[rows:, :].astype(jnp.float32)
+        for block in range(keys.shape[1] // LANES):
+            first = half + block * rows
+            columns = slice(block * LANES, (block + 1) * LANES)
+            across_second_ref[first : first + rows, :] = keys[:, columns].astype(jnp.bfloat16)
     outs = (beside_first_ref, beside_second_ref, across_first_ref, across_second_ref)
     total = near_ref[:size, :].astype(jnp.float32) + far_ref[:size, :].astype(jnp.float32)
     own_ref[...] = total.astype(jnp.bfloat16)
     for place, out_ref in enumerate(outs):
         rows = slice(size + place * half, size + (place + 1) * half)
         total = near_ref[rows, :].astype(jnp.float32) + far_ref[rows, :].astype(jnp.float32)
-        out_ref[...] = total.astype(jnp.bfloat16)
+        out_ref[:half, :] = total.astype(jnp.bfloat16)
 
 
 def sum_passed_kernel(
@@ -268,7 +268,7 @@
     packed[half:, :] = (
         own_ref[half:, :].astype(jnp.float32)
         + beside_second_ref[...].astype(jnp.float32)
-        + across_second_ref[...].astype(jnp.float32)
+        + across_second_ref[:half, :].astype(jnp.float32)
     )
     start, source = 0, 0
     for piece in pieces:
@@ -290,16 +290,9 @@
     return jax.ShapeDtypeStruct(shape, kind)
 
 
-def gather_high(rows, doubling):
+def gather_high(rows):
     high_count = lax.axis_size(ALL_AXES) // LOW_COUNT
-    if not doubling:
-        return [rows] + [swap(rows, step * LOW_COUNT) for step in range(1, high_count)]
-    parts = {0: rows}
-    mask = high_count // 2
-    while mask:
-        parts.update({step | mask: swap(value, mask * LOW_COUNT) for step, value in parts.items()})
-        mask = mask // 2
-    return [parts[step] for step in range(high_count)]
+    return [rows] + [swap(rows, step * LOW_COUNT) for step in range(1, high_count)]
 
 
 def gather_own(pieces, parts, count, behind=()):
@@ -321,25 +314,23 @@
     beside_second, across_first = swap(second, 4), swap(first, 2)
     beside_first, across_second = swap(first, 4), swap(second, 2)
     return (
-        (first, second, beside_first, beside_second, across_first, across_second),
-        (swap(across_first, 4), swap(beside_second, 2)),
+        first,
+        second,
+        beside_first,
+        beside_second,
+        across_first,
+        across_second,
+        swap(across_first, 4),
+        swap(beside_second, 2),
     )
 
 
 def gather_wholes(own):
     beside, across = swap(own, 4), swap(own, 2)
-    return (own, beside, across), (swap(across, 4),)
-
-
-def gather_cores(three, diagonal, behind=()):
-    (three,) = local_call(
-        join_kernel,
-        (array((len(three) * three[0].shape[0], LANES), jnp.bfloat16),),
-        three,
-        (),
-        behind,
-    )
-    near = (three, *diagonal)
+    return own, beside, across, swap(across, 4)
+
+
+def gather_cores(near):
     return near + tuple(swap(value, 1) for value in near)
 
 
@@ -363,16 +354,17 @@
     return swap(to_x, 4), swap(to_y, 2), to_y
 
 
-def scatter_three(pieces, near_three, far_three, behind=()):
+def scatter_three(pieces, near_three, far_three, behind=(), keys=()):
     size = sum(piece.size for piece in pieces)
     half = size // 2
     own, beside_first, beside_second, across_first, across_second = local_call(
         functools.partial(sum_three_kernel, size),
         (
             array((size, LANES), jnp.bfloat16),
-            *(array((half, LANES), jnp.bfloat16),) * 4,
-        ),
-        (near_three, far_three),
+            *(array((half, LANES), jnp.bfloat16),) * 3,
+            array((half + (keys[0].size // LANES if keys else 0), LANES), jnp.bfloat16),
+        ),
+        (near_three, far_three, *keys),
         (),
         behind,
     )
@@ -405,7 +397,7 @@
     return terms, beside_second
 
 
-def scatter_high(pieces, terms):
+def scatter_high(pieces, terms, behind=()):
     high_count = pieces[0].high_count
     size = sum(piece.size for piece in pieces)
     flat_rows = sum(piece.flat_rows for piece in pieces)
@@ -419,6 +411,7 @@
             pltpu.VMEM((high_count, flat_rows, LANES), jnp.float32),
             pltpu.VMEM((size, LANES), jnp.float32),
         ),
+        behind,
     )
     arrived = [swap(send, step * LOW_COUNT) for step, send in enumerate(outs) if step]
     return outs[0] + sum(value.astype(jnp.float32) for value in arrived), outs[0], arrived
@@ -451,14 +444,9 @@
 
 
 def weight_rows(refs, size, order, start, rows):
-    count = len(refs) // 2
-    three, *diagonal = refs[:count] if order < 4 else refs[count:]
-    if order % 4 == 3:
-        part = size // len(diagonal)
-        ref, start = diagonal[start // part], start % part
-    else:
-        ref, start = three, order % 4 * size + start
-    return ref[start : start + rows, :]
+    count = len(refs) // LOW_COUNT
+    part = size // count
+    return refs[order * count + start // part][start % part : start % part + rows, :]
 
 
 def put_rows(refs, size, order, start, rows):
@@ -505,9 +493,9 @@
     order_ref,
     *refs,
 ):
-    weight_refs, grad_refs = refs[:6], refs[10:14]
-    block_out_ref, grad_middle_ref, grad_gain_in_ref, grad_gain_out_ref = refs[6:10]
-    down_ref, hidden_ref, gelu_ref, slope_ref = refs[14:]
+    weight_refs, grad_refs = refs[:16], refs[20:24]
+    block_out_ref, grad_middle_ref, grad_gain_in_ref, grad_gain_out_ref = refs[16:20]
+    down_ref, hidden_ref, gelu_ref, slope_ref = refs[24:]
     low = index_ref[0] % LOW_COUNT
     rows = gate_piece.block_rows
     size = 2 * gate_piece.size + down_piece.size
@@ -647,8 +635,8 @@
     order_ref,
     *refs,
 ):
-    weight_refs = refs[:4]
-    normed_ref, query_proj_ref, key_proj_ref, query_ref, key_value_ref = refs[4:]
+    weight_refs = refs[:8]
+    normed_ref, query_proj_ref, key_proj_ref, query_ref, key_value_ref = refs[8:]
     size = sum(piece.size for piece in pieces)
     rows = pieces[0].block_rows
     cosine, sine = cosine_ref[...], sine_ref[...]
@@ -683,7 +671,7 @@
     query_ref,
     *refs,
 ):
-    weight_refs, key_value_refs = refs[:4], refs[4:-5]
+    weight_refs, key_value_refs = refs[:8], refs[8:-5]
     probs_ref, attended_ref, attn_out_ref, middle_ref, out_weight_ref = refs[-5:]
     out_piece = pieces[-1]
     low = index_ref[0] % LOW_COUNT
@@ -725,10 +713,9 @@
     query_ref,
     *refs,
 ):
-    part_count = (len(refs) - 3) // 2
-    key_value_refs = refs[:part_count]
-    grad_out_weight_ref, grad_query_ref, grad_gain_ref = refs[part_count : part_count + 3]
-    grad_key_value_refs = refs[part_count + 3 :]
+    key_value_refs = refs[:4]
+    grad_out_weight_ref, grad_query_ref, grad_gain_ref = refs[4:7]
+    grad_own_ref, grad_across_ref, grad_cores_ref = refs[7:]
     rows = query_ref.shape[0]
     scale, normal = norm_parts(attn_out_ref[...])
     grad_attn, grad_gain_ref[...] = norm_back(scale, normal, grad_middle_ref[...], gain_ref[...])
@@ -749,7 +736,13 @@
         grad_scores = (probs * (grad_probs - inner) * HD ** (-0.5)).astype(jnp.bfloat16)
         grad_query_ref[:, columns] = product(grad_scores, keys, 1, 0)
         grad_keys = grad_keys + product(grad_scores, query_ref[:, columns], 0, 0)
-    for part, ref in enumerate(grad_key_value_refs):
+    targets = (
+        grad_own_ref,
+        grad_cores_ref.at[:rows],
+        grad_across_ref,
+        grad_cores_ref.at[rows:],
+    )
+    for part, ref in enumerate(targets):
         ref[:, :HD] = grad_keys[part * rows : (part + 1) * rows].astype(ref.dtype)
         ref[:, HD:] = grad_values[part * rows : (part + 1) * rows].astype(ref.dtype)
 
@@ -765,8 +758,8 @@
     grad_query_ref,
     *refs,
 ):
-    weight_refs = refs[:4]
-    grad_weight_ref, grad_normed_ref, grad_gain_ref = refs[4:]
+    weight_refs = refs[:8]
+    grad_weight_ref, grad_normed_ref, grad_gain_ref = refs[8:]
     size = sum(piece.size for piece in pieces)
     rows = pieces[0].block_rows
     cosine, sine = cosine_ref[...], sine_ref[...]
@@ -798,47 +791,45 @@
     order_ref,
     normed_ref,
     key_proj_ref,
-    grad_query_weight_ref,
     grad_normed_ref,
     grad_middle_ref,
-    grad_out_weight_ref,
     gain_attn_ref,
     gain_ffin_ref,
     gain_ffout_ref,
     gain_query_ref,
+    own_key_ref,
+    cores_key_ref,
+    across_key_ref,
     *refs,
 ):
-    weight_refs, key_value_refs, grad_refs = refs[:4], refs[4:-6], refs[-6:-2]
-    input_grad_ref, grad_gain_ref = refs[-2:]
-    low = index_ref[0] % LOW_COUNT
+    weight_refs = refs[:8]
+    grad_weight_ref, input_grad_ref, grad_gain_ref = refs[8:]
     size = sum(piece.size for piece in pieces)
     rows = pieces[0].block_rows
     normed = normed_ref[...]
-    key_value = sum(ref[...].astype(jnp.float32) for ref in key_value_refs)
+    key_rows = own_key_ref.shape[0]
+    first = across_key_ref.shape[0] - 4 * key_rows
+    key_value = own_key_ref[...] + cores_key_ref[:key_rows, :].astype(jnp.float32)
+    key_value = key_value + jnp.concatenate(
+        [
+            across_key_ref[first + block * key_rows : first + (block + 1) * key_rows, :].astype(
+                jnp.float32
+            )
+            for block in range(4)
+        ],
+        axis=1,
+    )
     scale, normal = norm_parts(key_proj_ref[...])
     upstream = turn(key_value[:, :HD], cosine_ref[...], -sine_ref[...])
     grad_key, grad_gain_key = norm_back(scale, normal, upstream, gain_key_ref[...])
     grad_normed = grad_normed_ref[...]
-    for head, start in enumerate(head_starts(pieces)):
-        if head < HQ:
-            grad_weight = grad_query_weight_ref[:, head * HD : (head + 1) * HD]
-        else:
-            grad = (grad_key if head == HQ else key_value[:, HD:]).astype(jnp.bfloat16)
-            weight = wide_head(weight_refs, size, start, rows)
-            grad_normed = grad_normed + product(grad, weight, 1, 1)
-            grad_weight = product(normed, grad, 0, 0).astype(jnp.bfloat16)
-        for side in range(2):
-            put_wide_tile(
-                grad_refs,
-                size,
-                start + side * rows,
-                rows,
-                grad_weight[:, side * LANES : (side + 1) * LANES],
-            )
-    out_piece = pieces[-1]
-    for order, start, matrix_rows, columns in tall_rows(out_piece, low):
-        start = start + size - out_piece.size
-        put_rows(grad_refs, size, order, start, grad_out_weight_ref[matrix_rows, columns])
+    for place, start in enumerate(head_starts(pieces)[HQ:]):
+        grad = (key_value[:, HD:] if place else grad_key).astype(jnp.bfloat16)
+        weight = wide_head(weight_refs, size, start, rows)
+        grad_normed = grad_normed + product(grad, weight, 1, 1)
+        grad_weight_ref[:, place * HD : (place + 1) * HD] = product(normed, grad, 0, 0).astype(
+            jnp.bfloat16
+        )
     scale, normal = norm_parts(tokens_ref[...].astype(jnp.float32))
     grad_inputs, grad_gain_input = norm_back(
         scale, normal, unordered(grad_normed, order_ref[...]), gain_ref[...]
@@ -858,8 +849,31 @@
         for start in range(0, values.shape[1], LANES):
             grad_gain_ref[row : row + 1, :] = values[:, start : start + LANES]
             row = row + 1
+
+
+def split_kernel(
+    pieces,
+    index_ref,
+    query_ref,
+    key_value_ref,
+    out_ref,
+    gain_ref,
+    *grad_refs,
+):
+    low = index_ref[0] % LOW_COUNT
+    size = sum(piece.size for piece in pieces)
+    rows = pieces[0].block_rows
+    start = 0
+    for matrix_ref in (query_ref, key_value_ref):
+        for column in range(0, matrix_ref.shape[1], LANES):
+            tile = matrix_ref[:, column : column + LANES]
+            put_wide_tile(grad_refs, size, start, rows, tile)
+            start = start + rows
+    out_piece = pieces[-1]
+    for order, first, matrix_rows, columns in tall_rows(out_piece, low):
+        put_rows(grad_refs, size, order, start + first, out_ref[matrix_rows, columns])
     for target in (grad_refs[1], grad_refs[3]):
-        target[size:, :] = grad_gain_ref[...].astype(jnp.bfloat16)
+        target[size:, :] = gain_ref[...].astype(jnp.bfloat16)
 
 
 def width_order(device_count):
@@ -897,13 +911,15 @@
     attention_rows = sum(piece.flat_rows for piece in attention_pieces)
     ffn_pieces = pieces[4:7]
     rounded = master.astype(jnp.bfloat16)
-    attention_parts = gather_high(rounded[:attention_rows], False)
+    attention_parts = gather_high(rounded[:attention_rows])
     ffn_rows = rounded[attention_rows:]
-    ffn_parts = gather_high(ffn_rows, True)
-    attention_near = gather_wholes(*gather_own(attention_pieces, attention_parts, 1))
-    attention_blocks = gather_cores(*attention_near)
-    ffn_near = gather_halves(
-        *gather_own(ffn_pieces, ffn_parts, 2, (attention_blocks[0], *attention_near[1]))
+    ffn_parts = gather_high(ffn_rows)
+    attention_near = gather_wholes(
+        *gather_own(attention_pieces, attention_parts, 1, (ffn_parts[1],))
+    )
+    attention_blocks = gather_cores(attention_near)
+    ffn_weights = gather_cores(
+        gather_halves(*gather_own(ffn_pieces, ffn_parts, 2, attention_near[1:]))
     )
     gain_parts = []
     for start, width in ((0, D), (D, D), (2 * D, D), (3 * D, D), (4 * D, HD), (4 * D + HD, HD)):
@@ -914,11 +930,14 @@
     angles = lax.dynamic_slice_in_dim(angles_of(positions(doc_row)), first_row, local_rows, 0)
     cosine, sine = jnp.cos(angles), jnp.sin(angles)
     query_docs = lax.dynamic_slice_in_dim(doc_row, first_row, local_rows, 0)
-    reach = min(-(-(WINDOW - 1) // local_rows), group_size - 1)
-    key_count = (reach + 1) * local_rows
-    doc_pad = jnp.concatenate([jnp.full((reach * local_rows,), -1, jnp.int32), doc_row])
-    key_docs = lax.dynamic_slice_in_dim(doc_pad, first_row, key_count, 0)
-    key_index = first_row - reach * local_rows + jnp.arange(key_count, dtype=jnp.int32)
+    key_count = group_size * local_rows
+    first_keys = [(lax.axis_index("group") ^ step) * local_rows for step in range(group_size)]
+    key_docs = jnp.concatenate(
+        [lax.dynamic_slice_in_dim(doc_row, start, local_rows, 0) for start in first_keys]
+    )
+    key_index = jnp.concatenate(
+        [start + jnp.arange(local_rows, dtype=jnp.int32) for start in first_keys]
+    )
     query_index = first_row + jnp.arange(local_rows, dtype=jnp.int32)
     distance = query_index[:, None] - key_index[None, :]
     allowed = (distance >= 0) & (distance < WINDOW) & (key_docs[None, :] == query_docs[:, None])
@@ -936,9 +955,7 @@
         ),
         (tokens, gain_input, gain_query, gain_key, cosine, sine, order, *attention_blocks),
     )
-    key_values = [shifted(key_value, "group", offset) for offset in range(reach, 0, -1)]
-    ffn_weights = gather_cores(*ffn_near, key_values)
-    key_values.append(key_value)
+    key_values = [key_value] + [swap(key_value, step) for step in range(1, group_size)]
     probs, attended, attn_out, middle, out_weight = local_call(
         functools.partial(attend_kernel, attention_pieces),
         (
@@ -949,22 +966,21 @@
             array((width, D), jnp.bfloat16),
         ),
         (tokens, gain_attn, allowed, query_rot, *attention_blocks, *key_values),
-        (),
-        (ffn_weights[0],),
     )
     outputs, grad_middle, grad_gain_ffin, grad_gain_ffout, grads_ffn = ffn_blocks(
         pieces, middle, cotangent, gain_ffin, gain_ffout, order, ffn_weights
     )
     near_three, near_one, far_three, far_one = grads_ffn
     far_three, far_one = scatter_cores(far_three, far_one)
-    grad_out_weight, grad_query, grad_gain_attn, *grad_key_values = local_call(
+    grad_out_weight, grad_query, grad_gain_attn, own_key, across_key, cores_key = local_call(
         attend_back_kernel,
         (
             array((width, D), jnp.bfloat16),
             array((local_rows, width), jnp.float32),
             array((1, D), jnp.float32),
-            *(array((local_rows, 2 * HD), jnp.bfloat16),) * reach,
             array((local_rows, 2 * HD), jnp.float32),
+            array((local_rows, 2 * HD), jnp.float32),
+            array((2 * local_rows, 2 * HD), jnp.bfloat16),
         ),
         (
             grad_middle,
@@ -977,12 +993,9 @@
             *key_values,
         ),
     )
-    grad_key_values = [
-        shifted(value, "group", place - reach) if place < reach else value
-        for place, value in enumerate(grad_key_values)
-    ]
-    over_x, over_y, sent = scatter_one(ffn_pieces, near_one, far_one, grad_key_values[:-1])
-    threes = scatter_three(ffn_pieces, near_three, far_three, (sent,))
+    cores_key = swap(cores_key, 1)
+    over_x, over_y, sent = scatter_one(ffn_pieces, near_one, far_one, (grad_query,))
+    threes = scatter_three(ffn_pieces, near_three, far_three, (sent,), (across_key, cores_key))
     grad_query_weight, grad_normed, grad_gain_query = local_call(
         functools.partial(query_back_kernel, attention_pieces),
         (
@@ -994,10 +1007,13 @@
         (),
         (threes[0],),
     )
-    *grads_attention, grad_inputs, _ = local_call(
+    ffn_terms, sent = scatter_passed(
+        ffn_pieces, threes, over_x, over_y, near_one, far_one, (grad_normed,)
+    )
+    grad_key_weight, grad_inputs, grad_gains = local_call(
         functools.partial(project_back_kernel, attention_pieces),
         (
-            *grad_arrays(attention_pieces, GAIN_ROWS),
+            array((D, 2 * HD), jnp.bfloat16),
             array((local_rows, D), jnp.bfloat16),
             array((GAIN_ROWS, LANES), jnp.float32),
         ),
@@ -1010,36 +1026,33 @@
             order,
             normed,
             key_proj,
-            grad_query_weight,
             grad_normed,
             grad_middle,
-            grad_out_weight,
             grad_gain_attn,
             grad_gain_ffin,
             grad_gain_ffout,
             grad_gain_query,
+            own_key,
+            cores_key,
+            threes[4],
             *attention_blocks,
-            *grad_key_values,
         ),
         (),
-        (over_x, over_y),
-    )
-    ffn_terms, _ = scatter_passed(
-        ffn_pieces,
-        threes,
-        over_x,
-        over_y,
-        near_one,
-        far_one,
-        (grad_inputs, threes[1], threes[4]),
-    )
-    near_three, near_one, far_three, far_one = grads_attention
+        (sent, threes[1]),
+    )
+    grads_ffn, sent, arrived = scatter_high(ffn_pieces, ffn_terms, (grad_inputs,))
+    near_three, near_one, far_three, far_one = local_call(
+        functools.partial(split_kernel, attention_pieces),
+        grad_arrays(attention_pieces, GAIN_ROWS),
+        (grad_query_weight, grad_key_weight, grad_out_weight, grad_gains),
+        (),
+        (sent,),
+    )
     far_three, far_one = scatter_cores(far_three, far_one)
-    grads_ffn, sent, arrived = scatter_high(ffn_pieces, ffn_terms)
-    over_x, over_y, sent = scatter_one(attention_pieces, near_one, far_one, (sent,))
+    over_x, over_y, sent = scatter_one(attention_pieces, near_one, far_one)
     threes = scatter_three(attention_pieces, near_three, far_three, (sent, arrived[0]))
     terms, _ = scatter_passed(attention_pieces, threes, over_x, over_y, near_one, far_one)
-    grads_attention, _, _ = scatter_high(attention_pieces, terms)
+    grads_attention, _, _ = scatter_high(attention_pieces, terms, arrived)
     gain_grads = grads_attention[attention_rows:].reshape(-1)[: gains.shape[0]]
     grads_local = jnp.concatenate([grads_attention[:attention_rows], grads_ffn])
     return (

time: 237 us -> 227 us (0.958)
  waiting for transfers between devices: 85.3 us -> 79.1 us
  Pallas kernels: 76.2 us -> 72.6 us
    ppermute x6 -> x0, starting transfers between devices: 9.25 us -> none  [shifted(): lax.ppermute(value, axis, [(source, source + steps) for source in range(i...]
    ppermute x6 -> x0, waiting for transfers between devices: 8.6 us -> none  [shifted(): lax.ppermute(value, axis, [(source, source + steps) for source in range(i...]
    ppermute x42 -> x53, starting transfers between devices: 40.3 us -> 48.8 us  [swap(): lax.ppermute(value, ALL_AXES, [(source, source ^ mask) for source in rang...]
    pallas_call x18 -> x17, Pallas kernels: 76.2 us -> 72.6 us  [local_call(): pl.pallas_call(body, out_shape=outs, in_specs=specs, out_specs=tuple((pl....]
    ppermute x42 -> x53, waiting for transfers between devices: 76.7 us -> 79.1 us  [swap(): lax.ppermute(value, ALL_AXES, [(source, source ^ mask) for source in rang...]
    unnamed x106 -> x124, local copies, waits for them, and re-layouts: 14 us -> 13.1 us
  transfers between devices with their start and end apart: 48 -> 53, of which waited for: 25 -> 21; matrix products, arithmetic and copies ran while one was open for 3% -> 4% of each run, Pallas kernels for 24% -> 20%
where the time goes in v9:
time: 227 us; the launch traced here: 226 us
  waiting for transfers between devices  79.1 us (35%)
  Pallas kernels  72.6 us (32%)
  starting transfers between devices  48.8 us (21%)
  local copies, waits for them, and re-layouts  16.4 us (7%)
  other arithmetic  8.29 us (4%)
    ppermute x53, waiting for transfers between devices, swap(): lax.ppermute(value, ALL_AXES, [(source, source ^ mask) for source in rang...  79.1 us
    pallas_call x17, Pallas kernels, local_call(): pl.pallas_call(body, out_shape=outs, in_specs=specs, out_specs=tuple((pl....  72.6 us
    ppermute x53, starting transfers between devices, swap(): lax.ppermute(value, ALL_AXES, [(source, source ^ mask) for source in rang...  48.8 us
    unnamed x124, local copies, waits for them, and re-layouts  13.1 us
  transfers between devices with their start and end apart: 53, of which 21 were waited for; matrix products, arithmetic and copies ran while one was open for 4% of the time, Pallas kernels for 20%

profile of v9, /device:TPU:0, one launch (start us, length us, event | category | flops | bytes accessed | tf_op | source)
XLA Modules:
  0.0 226.4 jit_solution(5184577986295639895)
XLA Ops:
  1.8 3.1 %collective-permute-start.3 = (bf16[960,128]{1,0:T(8,128)(2,1)S(1)}, bf16[960,128]{1,0:T(8,128)(2,1)S(1)}, u32[]{:S(2)}, u32[]{:S(2)}) collective-permute-start(bf16[960,128]{1,0:T(8,128)(2,1)S(1)} %slice.66.refs_1_), channel_id=1, source_target_pairs={{0,8},{1,9},{2,10},{3,11},{4,12},{5,13},{6,14},{7,15},{8,0},{9,1},... | collective-permute-start | bytes 737288 | tf_op jit(solution)/shard_map/ppermute | solution.py:127
  4.9 2.5 %collective-permute-start.2 = (bf16[400,128]{1,0:T(8,128)(2,1)S(1)}, bf16[400,128]{1,0:T(8,128)(2,1)S(1)}, u32[]{:S(2)}, u32[]{:S(2)}) collective-permute-start(bf16[400,128]{1,0:T(8,128)(2,1)S(1)} %slice.65.refs_1_), channel_id=1, source_target_pairs={{0,24},{1,25},{2,26},{3,27},{4,28},{5,29},{6,30},{7,31},{8,16},{9,... | collective-permute-start | bytes 307208 | tf_op jit(solution)/shard_map/ppermute | solution.py:127
  9.4 7.0 %collective-permute-done.2.refs_4_ = bf16[400,128]{1,0:T(8,128)(2,1)S(1)} collective-permute-done((bf16[400,128]{1,0:T(8,128)(2,1)S(1)}, bf16[400,128]{1,0:T(8,128)(2,1)S(1)}, u32[]{:S(2)}, u32[]{:S(2)}) %collective-permute-start.2) | collective-permute-done | bytes 102432 | tf_op jit(solution)/shard_map/ppermute | solution.py:127
  21.8 3.6 %collective-permute-start.15 = (bf16[960,128]{1,0:T(8,128)(2,1)S(1)}, bf16[960,128]{1,0:T(8,128)(2,1)S(1)}, u32[]{:S(2)}, u32[]{:S(2)}) collective-permute-start(bf16[960,128]{1,0:T(8,128)(2,1)S(1)} %slice.66.refs_1_), channel_id=1, source_target_pairs={{0,24},{1,25},{2,26},{3,27},{4,28},{5,29},{6,30},{7,31},{8,16},{9,... | collective-permute-start | bytes 737288 | tf_op jit(solution)/shard_map/ppermute | solution.py:127
  26.9 4.1 %collective-permute-done.5.refs_10_.refs_7_.refs_6_.refs_9_.refs_20_ = bf16[1600,128]{1,0:T(8,128)(2,1)S(1)} collective-permute-done((bf16[1600,128]{1,0:T(8,128)(2,1)}, bf16[1600,128]{1,0:T(8,128)(2,1)S(1)}, u32[]{:S(2)}, u32[]{:S(2)}) %collective-permute-start.5) | collective-permute-done | bytes 409632 | tf_op jit(solution)/shard_map/ppermute | solution.py:127
  34.2 3.9 %collective-permute-done.4.refs_9_.refs_6_.refs_5_.refs_8_.refs_19_ = bf16[1600,128]{1,0:T(8,128)(2,1)S(1)} collective-permute-done((bf16[1600,128]{1,0:T(8,128)(2,1)}, bf16[1600,128]{1,0:T(8,128)(2,1)S(1)}, u32[]{:S(2)}, u32[]{:S(2)}) %collective-permute-start.4) | collective-permute-done | bytes 409632 | tf_op jit(solution)/shard_map/ppermute | solution.py:127
  38.1 7.2 %collective-permute-done.14.refs_3_ = bf16[960,128]{1,0:T(8,128)(2,1)S(1)} collective-permute-done((bf16[960,128]{1,0:T(8,128)(2,1)S(1)}, bf16[960,128]{1,0:T(8,128)(2,1)S(1)}, u32[]{:S(2)}, u32[]{:S(2)}) %collective-permute-start.14) | collective-permute-done | bytes 245792 | tf_op jit(solution)/shard_map/ppermute | solution.py:127
  46.7 2.9 %shard_map.155 = (bf16[1920,128]{1,0:T(8,128)(2,1)}, bf16[1920,128]{1,0:T(8,128)(2,1)}) custom-call(s32[1]{0:T(128)} %bitcast.refs_0_, bf16[960,128]{1,0:T(8,128)(2,1)} %copy-done.18, bf16[960,128]{1,0:T(8,128)(2,1)} %copy-done.19, bf16[960,128]{1,0:T(8,128)(2,1)} %copy-done.41, bf16[960,128]{1,0:T(8,128)(2,1)} %copy-done.40, bf16[1600,128]{1,0:T(8,128)(2,1)} %copy-done.1, ...), custom_call_target="tpu_custom_call" | custom-call | tf_op jit(solution)/shard_map/pallas_call | solution.py:139
  56.7 8.4 %collective-permute-done.18.refs_10_ = bf16[1920,128]{1,0:T(8,128)(2,1)S(1)} collective-permute-done((bf16[1920,128]{1,0:T(8,128)(2,1)}, bf16[1920,128]{1,0:T(8,128)(2,1)S(1)}, u32[]{:S(2)}, u32[]{:S(2)}) %collective-permute-start.18) | collective-permute-done | bytes 491552 | tf_op jit(solution)/shard_map/ppermute | solution.py:127
  67.3 9.0 %collective-permute-done.17.refs_9_ = bf16[1920,128]{1,0:T(8,128)(2,1)} collective-permute-done((bf16[1920,128]{1,0:T(8,128)(2,1)}, bf16[1920,128]{1,0:T(8,128)(2,1)}, u32[]{:S(2)}, u32[]{:S(2)}) %collective-permute-start.17) | collective-permute-done | bytes 491552 | tf_op jit(solution)/shard_map/ppermute | solution.py:127
  78.4 3.9 %shard_map.153 = (bf16[128,640]{1,0:T(8,128)(2,1)}, f32[128,1024]{1,0:T(8,128)}, f32[128,256]{1,0:T(8,128)}, bf16[128,1024]{1,0:T(8,128)(2,1)}, bf16[128,512]{1,0:T(8,128)(2,1)}) custom-call(s32[1]{0:T(128)} %bitcast.refs_0_, bf16[128,640]{1,0:T(8,128)(2,1)} %refs_1_.5, f32[1,640]{1,0:T(1,128)} %broadcast_in_dim.30.refs_2_, f32[1,256]{1,0:T(1,128)} %bitcast.29, ...), custom_call_target="tpu_custom_call" | custom-call | tf_op jit(solution)/shard_map/pallas_call | solution.py:139
  83.7 6.8 %collective-permute-done.13.refs_16_.refs_11_ = bf16[128,512]{1,0:T(8,128)(2,1)S(1)} collective-permute-done((bf16[128,512]{1,0:T(8,128)(2,1)}, bf16[128,512]{1,0:T(8,128)(2,1)S(1)}, u32[]{:S(2)}, u32[]{:S(2)}) %collective-permute-start.13) | collective-permute-done | bytes 131104 | tf_op jit(solution)/shard_map/ppermute | solution.py:127
  96.6 5.7 %shard_map.154 = (f32[128,2048]{1,0:T(8,128)}, bf16[128,1024]{1,0:T(8,128)(2,1)}, f32[128,640]{1,0:T(8,128)}, f32[128,640]{1,0:T(8,128)}, bf16[1024,640]{1,0:T(8,128)(2,1)}) custom-call(s32[1]{0:T(128)} %bitcast.refs_0_, bf16[128,640]{1,0:T(8,128)(2,1)} %refs_1_.5, f32[1,640]{1,0:T(1,128)} %broadcast_in_dim.14.refs_2_.refs_3_, f32[128,512]{1,0:T(8,128)} %fusion.4.refs_3_, ...), custom_call_target="tpu_custom_call" | custom-call | tf_op jit(solution)/shard_map/pallas_call | solution.py:139
  103.7 14.9 %shard_map.156 = (bf16[128,640]{1,0:T(8,128)(2,1)}, f32[128,640]{1,0:T(8,128)}, f32[1,640]{1,0:T(1,128)}, f32[1,640]{1,0:T(1,128)}, bf16[11520,128]{1,0:T(8,128)...) custom-call(s32[1]{0:T(128)} %bitcast.refs_0_, ...), custom_call_target="tpu_custom_call" | custom-call | tf_op jit(solution)/shard_map/pallas_call | solution.py:139
  119.2 5.8 %shard_map.157 = (bf16[1024,640]{1,0:T(8,128)(2,1)}, f32[128,1024]{1,0:T(8,128)}, f32[1,640]{1,0:T(1,128)}, f32[128,512]{1,0:T(8,128)}, f32[128,512]{1,0:T(8,128)}, /*index=5*/bf16[256,512]{1,0:T(8,128)(2,1)}) custom-call(s32[1]{0:T(128)} %bitcast.refs_0_, f32[128,640]{1,0:T(8,128)} %get-tuple-element.81.refs_1_.refs_10_, ...), custom_call_target="tpu_custom_call" | custom-call | tf_op jit(solution)/shard_map/pallas_call | solution.py:139
  126.7 2.6 %shard_map.158 = (bf16[1920,128]{1,0:T(8,128)(2,1)}, bf16[1920,128]{1,0:T(8,128)(2,1)}) custom-call(s32[1]{0:T(128)} %bitcast.refs_0_, bf16[3840,128]{1,0:T(8,128)(2,1)} %get-tuple-element.91.refs_1_.refs_5_, bf16[3840,128]{1,0:T(8,128)(2,1)} %copy-done.7, f32[128,1024]{1,0:T(8,128)} %get-tuple-element.86.refs_3_.refs_6_), custom_call_target="tpu_custom_call" | custom-call | tf_op jit(solution)/shard_map/pallas_call | solution.py:139
  135.5 4.6 %shard_map.159 = (bf16[3840,128]{1,0:T(8,128)(2,1)}, bf16[1920,128]{1,0:T(8,128)(2,1)}, bf16[1920,128]{1,0:T(8,128)(2,1)}, bf16[1920,128]{1,0:T(8,128)(2,1)}, bf16[2432,128]{1,0:T(8,128)(2,1)}) custom-call(s32[1]{0:T(128)} %bitcast.refs_0_, bf16[11520,128]{1,0:T(8,128)(2,1)} %get-tuple-element.87.refs_1_, bf16[11520,128]{1,0:T(8,128)(2,1)} %copy-done.8, ...), custom_call_target="tpu_custom_call" | custom-call | tf_op jit(solution)/shard_map/pallas_call | solution.py:139
  141.1 4.5 %shard_map.160 = (bf16[640,1024]{1,0:T(8,128)(2,1)}, f32[128,640]{1,0:T(8,128)}, f32[1,256]{1,0:T(1,128)}) custom-call(s32[1]{0:T(128)} %bitcast.refs_0_, f32[1,256]{1,0:T(1,128)} %bitcast.30, f32[128,128]{1,0:T(8,128)} %get-tuple-element.153.refs_5_.refs_2_.refs_4_, f32[128,128]{1,0:T(8,128)} %get-tuple-element.152.refs_6_.refs_3_.refs_5_, ...), custom_call_target="tpu_custom_call" | custom-call | tf_op jit(solution)/shard_map/pallas_call | solution.py:139
  146.6 3.2 %shard_map.161 = (bf16[1920,128]{1,0:T(8,128)(2,1)}, bf16[1920,128]{1,0:T(8,128)(2,1)}, f32[8,128]{1,0:T(8,128)}) custom-call(s32[1]{0:T(128)} %bitcast.refs_0_, bf16[1920,128]{1,0:T(8,128)(2,1)} %get-tuple-element.102.refs_1_, bf16[1920,128]{1,0:T(8,128)(2,1)} %get-tuple-element.103.refs_2_, bf16[1920,128]{1,0:T(8,128)(2,1)} %copy-done.36, ...), custom_call_target="tpu_custom_call" | custom-call | tf_op jit(solution)/shard_map/pallas_call | solution.py:139
  154.1 4.4 %collective-permute-done.33.refs_17_.refs_5_ = bf16[2432,128]{1,0:T(8,128)(2,1)S(1)} collective-permute-done((bf16[2432,128]{1,0:T(8,128)(2,1)}, bf16[2432,128]{1,0:T(8,128)(2,1)S(1)}, u32[]{:S(2)}, u32[]{:S(2)}) %collective-permute-start.33) | collective-permute-done | bytes 622624 | tf_op jit(solution)/shard_map/ppermute | solution.py:127
  159.3 4.7 %shard_map.162 = (bf16[640,512]{1,0:T(8,128)(2,1)}, bf16[128,640]{1,0:T(8,128)(2,1)}, f32[32,128]{1,0:T(8,128)}) custom-call(s32[1]{0:T(128)} %bitcast.refs_0_, bf16[128,640]{1,0:T(8,128)(2,1)} %refs_1_.5, f32[1,640]{1,0:T(1,128)} %broadcast_in_dim.30.refs_2_, f32[1,256]{1,0:T(1,128)} %bitcast.28, f32[128,128]{1,0:T(8,128)} %get-tuple-element.153.refs_5_.refs_2_.refs_4_, ...), custom_call_target="tpu_custom_call" | custom-call | tf_op jit(solution)/shard_map/pallas_call | solution.py:139
  164.0 4.1 %collective-permute-done.38.refs_4_ = bf16[1920,128]{1,0:T(8,128)(2,1)S(1)} collective-permute-done((bf16[1920,128]{1,0:T(8,128)(2,1)}, bf16[1920,128]{1,0:T(8,128)(2,1)S(1)}, u32[]{:S(2)}, u32[]{:S(2)}) %collective-permute-start.38) | collective-permute-done | bytes 491552 | tf_op jit(solution)/shard_map/ppermute | solution.py:127
  169.1 4.1 %shard_map.163 = (f32[960,128]{1,0:T(8,128)}, bf16[960,128]{1,0:T(8,128)(2,1)}, bf16[960,128]{1,0:T(8,128)(2,1)}, bf16[960,128]{1,0:T(8,128)(2,1)}) custom-call(s32[1]{0:T(128)} %bitcast.refs_0_, bf16[3840,128]{1,0:T(8,128)(2,1)} %get-tuple-element.94.refs_15_.refs_1_, bf16[1920,128]{1,0:T(8,128)(2,1)} %copy-done.13, bf16[1920,128]{1,0:T(8,128)(2,1)} %copy-done.37, ...), custom_call_target="tpu_custom_call" | custom-call | tf_op jit(solution)/shard_map/pallas_call | solution.py:139
  173.2 4.3 %shard_map.164 = (bf16[4800,128]{1,0:T(8,128)(2,1)}, bf16[1632,128]{1,0:T(8,128)(2,1)}, bf16[4800,128]{1,0:T(8,128)(2,1)}, bf16[1632,128]{1,0:T(8,128)(2,1)}) custom-call(s32[1]{0:T(128)} %bitcast.refs_0_, bf16[640,1024]{1,0:T(8,128)(2,1)} %get-tuple-element.108.refs_1_, bf16[640,512]{1,0:T(8,128)(2,1)} %get-tuple-element.109.refs_2_, ...), custom_call_target="tpu_custom_call" | custom-call | tf_op jit(solution)/shard_map/pallas_call | solution.py:139
  178.0 3.0 %collective-permute-start.48 = (bf16[960,128]{1,0:T(8,128)(2,1)S(1)}, bf16[960,128]{1,0:T(8,128)(2,1)S(1)}, u32[]{:S(2)}, u32[]{:S(2)}) collective-permute-start(bf16[960,128]{1,0:T(8,128)(2,1)S(1)} %copy-done.58), channel_id=1, source_target_pairs={{0,16},{1,17},{2,18},{3,19},{4,20},{5,21},{6,22},{7,23},{8,24},{9,... | collective-permute-start | bytes 737288 | tf_op jit(solution)/shard_map/ppermute | solution.py:127
  186.0 4.9 %collective-permute-done.41.refs_4_.refs_7_ = bf16[960,128]{1,0:T(8,128)(2,1)S(1)} collective-permute-done((bf16[960,128]{1,0:T(8,128)(2,1)S(1)}, bf16[960,128]{1,0:T(8,128)(2,1)S(1)}, u32[]{:S(2)}, u32[]{:S(2)}) %collective-permute-start.41) | collective-permute-done | bytes 245792 | tf_op jit(solution)/shard_map/ppermute | solution.py:127
  193.3 2.7 %shard_map.166 = (bf16[1600,128]{1,0:T(8,128)(2,1)}, bf16[800,128]{1,0:T(8,128)(2,1)}, bf16[800,128]{1,0:T(8,128)(2,1)}, bf16[800,128]{1,0:T(8,128)(2,1)}, bf16[800,128]{1,0:T(8,128)(2,1)}) custom-call(s32[1]{0:T(128)} %bitcast.refs_0_, bf16[4800,128]{1,0:T(8,128)(2,1)} %get-tuple-element.115.refs_1_, bf16[4800,128]{1,0:T(8,128)(2,1)} %copy-done.16, ...), custom_call_target="tpu_custom_call" | custom-call | tf_op jit(solution)/shard_map/pallas_call | solution.py:139
  196.8 2.3 %shard_map.167 = (bf16[800,128]{1,0:T(8,128)(2,1)}, bf16[832,128]{1,0:T(8,128)(2,1)}, f32[32,128]{1,0:T(8,128)}) custom-call(s32[1]{0:T(128)} %bitcast.refs_0_, bf16[800,128]{1,0:T(8,128)(2,1)} %get-tuple-element.123.refs_1_, bf16[800,128]{1,0:T(8,128)(2,1)} %get-tuple-element.124.refs_2_, bf16[832,128]{1,0:T(8,128)(2,1)} %copy-done.44, ...), custom_call_target="tpu_custom_call" | custom-call | tf_op jit(solution)/shard_map/pallas_call | solution.py:139
  203.4 5.2 %collective-permute-done.42.refs_2_ = bf16[800,128]{1,0:T(8,128)(2,1)S(1)} collective-permute-done((bf16[800,128]{1,0:T(8,128)(2,1)S(1)}, bf16[800,128]{1,0:T(8,128)(2,1)S(1)}, u32[]{:S(2)}, u32[]{:S(2)}) %collective-permute-start.42) | collective-permute-done | bytes 204832 | tf_op jit(solution)/shard_map/ppermute | solution.py:127
  211.6 2.5 %shard_map.168 = (f32[432,128]{1,0:T(8,128)}, bf16[432,128]{1,0:T(8,128)(2,1)}, bf16[432,128]{1,0:T(8,128)(2,1)}, bf16[432,128]{1,0:T(8,128)(2,1)}) custom-call(s32[1]{0:T(128)} %bitcast.refs_0_, bf16[1600,128]{1,0:T(8,128)(2,1)} %get-tuple-element.121.refs_1_, bf16[800,128]{1,0:T(8,128)(2,1)} %copy-done.45, bf16[800,128]{1,0:T(8,128)(2,1)} %copy-done.46, ...), custom_call_target="tpu_custom_call" | custom-call | tf_op jit(solution)/shard_map/pallas_call | solution.py:139
  214.0 3.0 %collective-permute-start.51 = (bf16[432,128]{1,0:T(8,128)(2,1)}, bf16[432,128]{1,0:T(8,128)(2,1)S(1)}, u32[]{:S(2)}, u32[]{:S(2)}) collective-permute-start(bf16[432,128]{1,0:T(8,128)(2,1)} %get-tuple-element.134), channel_id=1, source_target_pairs={{0,16},{1,17},{2,18},{3,19},{4,20},{5,21},{6,22},{7,23},{8,24},{9,... | collective-permute-start | bytes 331784 | tf_op jit(solution)/shard_map/ppermute | solution.py:127
  219.7 2.9 %collective-permute-done.51 = bf16[432,128]{1,0:T(8,128)(2,1)S(1)} collective-permute-done((bf16[432,128]{1,0:T(8,128)(2,1)}, bf16[432,128]{1,0:T(8,128)(2,1)S(1)}, u32[]{:S(2)}, u32[]{:S(2)}) %collective-permute-start.51) | collective-permute-done | bytes 110624 | tf_op jit(solution)/shard_map/ppermute | solution.py:127
  (248 shorter events, 73.5 us)
Async XLA Ops:
  1.8 15.6 %collective-permute-start.3 = (bf16[960,128]{1,0:T(8,128)(2,1)S(1)}, bf16[960,128]{1,0:T(8,128)(2,1)S(1)}, u32[]{:S(2)}, u32[]{:S(2)}) collective-permute-start(bf16[960,128]{1,0:T(8,128)(2,1)S(1)} %slice.66.refs_1_), channel_id=1, source_target_pairs={{0,8},{1,9},{2,10},{3,11},{4,12},{5,13},{6,14},{7,15},{8,0},{9,1},... | collective-permute-start | bytes 737288 | tf_op jit(solution)/shard_map/ppermute | solution.py:127
  4.9 11.5 %collective-permute-start.2 = (bf16[400,128]{1,0:T(8,128)(2,1)S(1)}, bf16[400,128]{1,0:T(8,128)(2,1)S(1)}, u32[]{:S(2)}, u32[]{:S(2)}) collective-permute-start(bf16[400,128]{1,0:T(8,128)(2,1)S(1)} %slice.65.refs_1_), channel_id=1, source_target_pairs={{0,24},{1,25},{2,26},{3,27},{4,28},{5,29},{6,30},{7,31},{8,16},{9,... | collective-permute-start | bytes 307208 | tf_op jit(solution)/shard_map/ppermute | solution.py:127
  20.1 10.9 %collective-permute-start.5 = (bf16[1600,128]{1,0:T(8,128)(2,1)}, bf16[1600,128]{1,0:T(8,128)(2,1)S(1)}, u32[]{:S(2)}, u32[]{:S(2)}) collective-permute-start(bf16[1600,128]{1,0:T(8,128)(2,1)} %shard_map.152.refs_8_.refs_5_.refs_7_.refs_18_), channel_id=1, source_target_pairs={{0,2},{1,3},{2,0},{3,1},{4,6},{5,7},{6,4},{7,5},{8,10},{9,11},{10,... | collective-permute-start | bytes 1228808 | tf_op jit(solution)/shard_map/ppermute | solution.py:127
  21.8 11.8 %collective-permute-start.15 = (bf16[960,128]{1,0:T(8,128)(2,1)S(1)}, bf16[960,128]{1,0:T(8,128)(2,1)S(1)}, u32[]{:S(2)}, u32[]{:S(2)}) collective-permute-start(bf16[960,128]{1,0:T(8,128)(2,1)S(1)} %slice.66.refs_1_), channel_id=1, source_target_pairs={{0,24},{1,25},{2,26},{3,27},{4,28},{5,29},{6,30},{7,31},{8,16},{9,... | collective-permute-start | bytes 737288 | tf_op jit(solution)/shard_map/ppermute | solution.py:127
  25.4 19.8 %collective-permute-start.14 = (bf16[960,128]{1,0:T(8,128)(2,1)S(1)}, bf16[960,128]{1,0:T(8,128)(2,1)S(1)}, u32[]{:S(2)}, u32[]{:S(2)}) collective-permute-start(bf16[960,128]{1,0:T(8,128)(2,1)S(1)} %slice.66.refs_1_), channel_id=1, source_target_pairs={{0,16},{1,17},{2,18},{3,19},{4,20},{5,21},{6,22},{7,23},{8,24},{9,... | collective-permute-start | bytes 737288 | tf_op jit(solution)/shard_map/ppermute | solution.py:127
  25.4 12.6 %collective-permute-start.4 = (bf16[1600,128]{1,0:T(8,128)(2,1)}, bf16[1600,128]{1,0:T(8,128)(2,1)S(1)}, u32[]{:S(2)}, u32[]{:S(2)}) collective-permute-start(bf16[1600,128]{1,0:T(8,128)(2,1)} %shard_map.152.refs_8_.refs_5_.refs_7_.refs_18_), channel_id=1, source_target_pairs={{0,4},{1,5},{2,6},{3,7},{4,0},{5,1},{6,2},{7,3},{8,12},{9,13},{10,... | collective-permute-start | bytes 1228808 | tf_op jit(solution)/shard_map/ppermute | solution.py:127
  31.0 14.2 %collective-permute-start.6 = (bf16[1600,128]{1,0:T(8,128)(2,1)S(1)}, bf16[1600,128]{1,0:T(8,128)(2,1)S(1)}, u32[]{:S(2)}, u32[]{:S(2)}) collective-permute-start(bf16[1600,128]{1,0:T(8,128)(2,1)S(1)} %collective-permute-done.5.refs_10_.refs_7_.refs_6_.refs_9_.refs_20_), channel_id=1, source_target_pairs={{0,4},{1,5},{2,6},{3,7},{4,0},{5,1},{6,2},{7,3},{8,12},{9,13},{10,... | collective-permute-start | bytes 1228808 | tf_op jit(solution)/shard_map/ppermute | solution.py:127
  33.6 17.1 %collective-permute-start.7 = (bf16[1600,128]{1,0:T(8,128)(2,1)}, bf16[1600,128]{1,0:T(8,128)(2,1)S(1)}, u32[]{:S(2)}, u32[]{:S(2)}) collective-permute-start(bf16[1600,128]{1,0:T(8,128)(2,1)} %shard_map.152.refs_8_.refs_5_.refs_7_.refs_18_), channel_id=1, source_target_pairs={{0,1},{1,0},{2,3},{3,2},{4,5},{5,4},{6,7},{7,6},{8,9},{9,8},{10,11... | collective-permute-start | bytes 1228808 | tf_op jit(solution)/shard_map/ppermute | solution.py:127
  33.7 17.6 %collective-permute-start.9 = (bf16[1600,128]{1,0:T(8,128)(2,1)S(1)}, bf16[1600,128]{1,0:T(8,128)(2,1)S(1)}, u32[]{:S(2)}, u32[]{:S(2)}) collective-permute-start(bf16[1600,128]{1,0:T(8,128)(2,1)S(1)} %collective-permute-done.5.refs_10_.refs_7_.refs_6_.refs_9_.refs_20_), channel_id=1, source_target_pairs={{0,1},{1,0},{2,3},{3,2},{4,5},{5,4},{6,7},{7,6},{8,9},{9,8},{10,11... | collective-permute-start | bytes 1228808 | tf_op jit(solution)/shard_map/ppermute | solution.py:127
  38.0 14.8 %collective-permute-start.8 = (bf16[1600,128]{1,0:T(8,128)(2,1)S(1)}, bf16[1600,128]{1,0:T(8,128)(2,1)S(1)}, u32[]{:S(2)}, u32[]{:S(2)}) collective-permute-start(bf16[1600,128]{1,0:T(8,128)(2,1)S(1)} %collective-permute-done.4.refs_9_.refs_6_.refs_5_.refs_8_.refs_19_), channel_id=1, source_target_pairs={{0,1},{1,0},{2,3},{3,2},{4,5},{5,4},{6,7},{7,6},{8,9},{9,8},{10,11... | collective-permute-start | bytes 1228808 | tf_op jit(solution)/shard_map/ppermute | solution.py:127
  50.7 14.4 %collective-permute-start.18 = (bf16[1920,128]{1,0:T(8,128)(2,1)}, bf16[1920,128]{1,0:T(8,128)(2,1)S(1)}, u32[]{:S(2)}, u32[]{:S(2)}) collective-permute-start(bf16[1920,128]{1,0:T(8,128)(2,1)} %get-tuple-element.75.refs_6_), channel_id=1, source_target_pairs={{0,2},{1,3},{2,0},{3,1},{4,6},{5,7},{6,4},{7,5},{8,10},{9,11},{10,... | collective-permute-start | bytes 1474568 | tf_op jit(solution)/shard_map/ppermute | solution.py:127
  51.3 14.4 %collective-permute-start.16 = (bf16[1920,128]{1,0:T(8,128)(2,1)}, bf16[1920,128]{1,0:T(8,128)(2,1)}, u32[]{:S(2)}, u32[]{:S(2)}) collective-permute-start(bf16[1920,128]{1,0:T(8,128)(2,1)} %get-tuple-element.75.refs_6_), channel_id=1, source_target_pairs={{0,4},{1,5},{2,6},{3,7},{4,0},{5,1},{6,2},{7,3},{8,12},{9,13},{10,... | collective-permute-start | bytes 1474568 | tf_op jit(solution)/shard_map/ppermute | solution.py:127
  52.8 23.5 %collective-permute-start.17 = (bf16[1920,128]{1,0:T(8,128)(2,1)}, bf16[1920,128]{1,0:T(8,128)(2,1)}, u32[]{:S(2)}, u32[]{:S(2)}) collective-permute-start(bf16[1920,128]{1,0:T(8,128)(2,1)} %get-tuple-element.76.refs_7_), channel_id=1, source_target_pairs={{0,4},{1,5},{2,6},{3,7},{4,0},{5,1},{6,2},{7,3},{8,12},{9,13},{10,... | collective-permute-start | bytes 1474568 | tf_op jit(solution)/shard_map/ppermute | solution.py:127
  53.4 28.9 %collective-permute-start.23 = (bf16[1920,128]{1,0:T(8,128)(2,1)}, bf16[1920,128]{1,0:T(8,128)(2,1)S(1)}, u32[]{:S(2)}, u32[]{:S(2)}) collective-permute-start(bf16[1920,128]{1,0:T(8,128)(2,1)} %get-tuple-element.76.refs_7_), channel_id=1, source_target_pairs={{0,1},{1,0},{2,3},{3,2},{4,5},{5,4},{6,7},{7,6},{8,9},{9,8},{10,11... | collective-permute-start | bytes 1474568 | tf_op jit(solution)/shard_map/ppermute | solution.py:127
  54.2 28.9 %collective-permute-start.19 = (bf16[1920,128]{1,0:T(8,128)(2,1)}, bf16[1920,128]{1,0:T(8,128)(2,1)}, u32[]{:S(2)}, u32[]{:S(2)}) collective-permute-start(bf16[1920,128]{1,0:T(8,128)(2,1)} %get-tuple-element.76.refs_7_), channel_id=1, source_target_pairs={{0,2},{1,3},{2,0},{3,1},{4,6},{5,7},{6,4},{7,5},{8,10},{9,11},{10,... | collective-permute-start | bytes 1474568 | tf_op jit(solution)/shard_map/ppermute | solution.py:127
  65.1 28.2 %collective-permute-start.26 = (bf16[1920,128]{1,0:T(8,128)(2,1)S(1)}, bf16[1920,128]{1,0:T(8,128)(2,1)}, u32[]{:S(2)}, u32[]{:S(2)}) collective-permute-start(bf16[1920,128]{1,0:T(8,128)(2,1)S(1)} %collective-permute-done.18.refs_10_), channel_id=1, source_target_pairs={{0,1},{1,0},{2,3},{3,2},{4,5},{5,4},{6,7},{7,6},{8,9},{9,8},{10,11... | collective-permute-start | bytes 1474568 | tf_op jit(solution)/shard_map/ppermute | solution.py:127
  65.8 27.6 %collective-permute-start.20 = (bf16[1920,128]{1,0:T(8,128)(2,1)S(1)}, bf16[1920,128]{1,0:T(8,128)(2,1)}, u32[]{:S(2)}, u32[]{:S(2)}) collective-permute-start(bf16[1920,128]{1,0:T(8,128)(2,1)S(1)} %collective-permute-done.18.refs_10_), channel_id=1, source_target_pairs={{0,4},{1,5},{2,6},{3,7},{4,0},{5,1},{6,2},{7,3},{8,12},{9,13},{10,... | collective-permute-start | bytes 1474568 | tf_op jit(solution)/shard_map/ppermute | solution.py:127
  76.3 17.5 %collective-permute-start.21 = (bf16[1920,128]{1,0:T(8,128)(2,1)}, bf16[1920,128]{1,0:T(8,128)(2,1)}, u32[]{:S(2)}, u32[]{:S(2)}) collective-permute-start(bf16[1920,128]{1,0:T(8,128)(2,1)} %collective-permute-done.17.refs_9_), channel_id=1, source_target_pairs={{0,2},{1,3},{2,0},{3,1},{4,6},{5,7},{6,4},{7,5},{8,10},{9,11},{10,... | collective-permute-start | bytes 1474568 | tf_op jit(solution)/shard_map/ppermute | solution.py:127
  118.6 15.3 %collective-permute-start.30 = (bf16[11520,128]{1,0:T(8,128)(2,1)}, bf16[11520,128]{1,0:T(8,128)(2,1)S(1)}, u32[]{:S(2)}, u32[]{:S(2)}) collective-permute-start(bf16[11520,128]{1,0:T(8,128)(2,1)} %get-tuple-element.88), channel_id=1, source_target_pairs={{0,1},{1,0},{2,3},{3,2},{4,5},{5,4},{6,7},{7,6},{8,9},{9,8},{10,11... | collective-permute-start | bytes 8847368 | tf_op jit(solution)/shard_map/ppermute | solution.py:127
  129.3 16.4 %collective-permute-start.34 = (bf16[1920,128]{1,0:T(8,128)(2,1)}, bf16[1920,128]{1,0:T(8,128)(2,1)S(1)}, u32[]{:S(2)}, u32[]{:S(2)}) collective-permute-start(bf16[1920,128]{1,0:T(8,128)(2,1)} %get-tuple-element.104), channel_id=1, source_target_pairs={{0,4},{1,5},{2,6},{3,7},{4,0},{5,1},{6,2},{7,3},{8,12},{9,13},{10,... | collective-permute-start | bytes 1474568 | tf_op jit(solution)/shard_map/ppermute | solution.py:127
  130.8 14.9 %collective-permute-start.35 = (bf16[1920,128]{1,0:T(8,128)(2,1)}, bf16[1920,128]{1,0:T(8,128)(2,1)S(1)}, u32[]{:S(2)}, u32[]{:S(2)}) collective-permute-start(bf16[1920,128]{1,0:T(8,128)(2,1)} %get-tuple-element.93.refs_5_), channel_id=1, source_target_pairs={{0,2},{1,3},{2,0},{3,1},{4,6},{5,7},{6,4},{7,5},{8,10},{9,11},{10,... | collective-permute-start | bytes 1474568 | tf_op jit(solution)/shard_map/ppermute | solution.py:127
  140.1 18.3 %collective-permute-start.33 = (bf16[2432,128]{1,0:T(8,128)(2,1)}, bf16[2432,128]{1,0:T(8,128)(2,1)S(1)}, u32[]{:S(2)}, u32[]{:S(2)}) collective-permute-start(bf16[2432,128]{1,0:T(8,128)(2,1)} %get-tuple-element.101), channel_id=1, source_target_pairs={{0,2},{1,3},{2,0},{3,1},{4,6},{5,7},{6,4},{7,5},{8,10},{9,11},{10,... | collective-permute-start | bytes 1867784 | tf_op jit(solution)/shard_map/ppermute | solution.py:127
  140.6 13.5 %collective-permute-start.36 = (bf16[1920,128]{1,0:T(8,128)(2,1)}, bf16[1920,128]{1,0:T(8,128)(2,1)S(1)}, u32[]{:S(2)}, u32[]{:S(2)}) collective-permute-start(bf16[1920,128]{1,0:T(8,128)(2,1)} %get-tuple-element.106), channel_id=1, source_target_pairs={{0,4},{1,5},{2,6},{3,7},{4,0},{5,1},{6,2},{7,3},{8,12},{9,13},{10,... | collective-permute-start | bytes 1474568 | tf_op jit(solution)/shard_map/ppermute | solution.py:127
  149.8 18.3 %collective-permute-start.38 = (bf16[1920,128]{1,0:T(8,128)(2,1)}, bf16[1920,128]{1,0:T(8,128)(2,1)S(1)}, u32[]{:S(2)}, u32[]{:S(2)}) collective-permute-start(bf16[1920,128]{1,0:T(8,128)(2,1)} %get-tuple-element.112), channel_id=1, source_target_pairs={{0,2},{1,3},{2,0},{3,1},{4,6},{5,7},{6,4},{7,5},{8,10},{9,11},{10,... | collective-permute-start | bytes 1474568 | tf_op jit(solution)/shard_map/ppermute | solution.py:127
  151.3 16.8 %collective-permute-start.37 = (bf16[1920,128]{1,0:T(8,128)(2,1)}, bf16[1920,128]{1,0:T(8,128)(2,1)S(1)}, u32[]{:S(2)}, u32[]{:S(2)}) collective-permute-start(bf16[1920,128]{1,0:T(8,128)(2,1)} %get-tuple-element.105.refs_26_), channel_id=1, source_target_pairs={{0,4},{1,5},{2,6},{3,7},{4,0},{5,1},{6,2},{7,3},{8,12},{9,13},{10,... | collective-permute-start | bytes 1474568 | tf_op jit(solution)/shard_map/ppermute | solution.py:127
  177.5 14.8 %collective-permute-start.39 = (bf16[4800,128]{1,0:T(8,128)(2,1)}, bf16[4800,128]{1,0:T(8,128)(2,1)S(1)}, u32[]{:S(2)}, u32[]{:S(2)}) collective-permute-start(bf16[4800,128]{1,0:T(8,128)(2,1)} %get-tuple-element.116), channel_id=1, source_target_pairs={{0,1},{1,0},{2,3},{3,2},{4,5},{5,4},{6,7},{7,6},{8,9},{9,8},{10,11... | collective-permute-start | bytes 3686408 | tf_op jit(solution)/shard_map/ppermute | solution.py:127
  178.0 12.9 %collective-permute-start.41 = (bf16[960,128]{1,0:T(8,128)(2,1)S(1)}, bf16[960,128]{1,0:T(8,128)(2,1)S(1)}, u32[]{:S(2)}, u32[]{:S(2)}) collective-permute-start(bf16[960,128]{1,0:T(8,128)(2,1)S(1)} %copy-done.59), channel_id=1, source_target_pairs={{0,8},{1,9},{2,10},{3,11},{4,12},{5,13},{6,14},{7,15},{8,0},{9,1},... | collective-permute-start | bytes 737288 | tf_op jit(solution)/shard_map/ppermute | solution.py:127
  178.0 24.8 %collective-permute-start.48 = (bf16[960,128]{1,0:T(8,128)(2,1)S(1)}, bf16[960,128]{1,0:T(8,128)(2,1)S(1)}, u32[]{:S(2)}, u32[]{:S(2)}) collective-permute-start(bf16[960,128]{1,0:T(8,128)(2,1)S(1)} %copy-done.58), channel_id=1, source_target_pairs={{0,16},{1,17},{2,18},{3,19},{4,20},{5,21},{6,22},{7,23},{8,24},{9,... | collective-permute-start | bytes 737288 | tf_op jit(solution)/shard_map/ppermute | solution.py:127
  183.9 12.2 %collective-permute-start.43 = (bf16[832,128]{1,0:T(8,128)(2,1)}, bf16[832,128]{1,0:T(8,128)(2,1)S(1)}, u32[]{:S(2)}, u32[]{:S(2)}) collective-permute-start(bf16[832,128]{1,0:T(8,128)(2,1)} %get-tuple-element.125), channel_id=1, source_target_pairs={{0,4},{1,5},{2,6},{3,7},{4,0},{5,1},{6,2},{7,3},{8,12},{9,13},{10,... | collective-permute-start | bytes 638984 | tf_op jit(solution)/shard_map/ppermute | solution.py:127
  184.5 11.6 %collective-permute-start.44 = (bf16[800,128]{1,0:T(8,128)(2,1)}, bf16[800,128]{1,0:T(8,128)(2,1)S(1)}, u32[]{:S(2)}, u32[]{:S(2)}) collective-permute-start(bf16[800,128]{1,0:T(8,128)(2,1)} %get-tuple-element.119.refs_3_), channel_id=1, source_target_pairs={{0,2},{1,3},{2,0},{3,1},{4,6},{5,7},{6,4},{7,5},{8,10},{9,11},{10,... | collective-permute-start | bytes 614408 | tf_op jit(solution)/shard_map/ppermute | solution.py:127
  190.9 12.5 %collective-permute-start.49 = (bf16[960,128]{1,0:T(8,128)(2,1)S(1)}, bf16[960,128]{1,0:T(8,128)(2,1)S(1)}, u32[]{:S(2)}, u32[]{:S(2)}) collective-permute-start(bf16[960,128]{1,0:T(8,128)(2,1)S(1)} %copy-done.57), channel_id=1, source_target_pairs={{0,24},{1,25},{2,26},{3,27},{4,28},{5,29},{6,30},{7,31},{8,16},{9,... | collective-permute-start | bytes 737288 | tf_op jit(solution)/shard_map/ppermute | solution.py:127
  199.2 11.6 %collective-permute-start.46 = (bf16[832,128]{1,0:T(8,128)(2,1)}, bf16[832,128]{1,0:T(8,128)(2,1)S(1)}, u32[]{:S(2)}, u32[]{:S(2)}) collective-permute-start(bf16[832,128]{1,0:T(8,128)(2,1)} %get-tuple-element.127), channel_id=1, source_target_pairs={{0,2},{1,3},{2,0},{3,1},{4,6},{5,7},{6,4},{7,5},{8,10},{9,11},{10,... | collective-permute-start | bytes 638984 | tf_op jit(solution)/shard_map/ppermute | solution.py:127
  (83 other events, 650.8 us)

commit v10 on v9

--- a/solution.py
+++ b/solution.py
@@ -158,6 +158,10 @@
         self.high_count = device_count // LOW_COUNT
         self.block_rows = self.own_rows * self.high_count
         self.size = self.block_rows * self.blocks
+
+
+def copy_kernel(index_ref, in_ref, out_ref):
+    out_ref[...] = in_ref[...]
 
 
 def pack_kernel(pieces, index_ref, *refs):
@@ -310,18 +314,24 @@
     )
 
 
+def copied(value, behind):
+    return local_call(copy_kernel, (array(value.shape, jnp.bfloat16),), (value,), (), behind)[0]
+
+
 def gather_halves(first, second):
-    beside_second, across_first = swap(second, 4), swap(first, 2)
-    beside_first, across_second = swap(first, 4), swap(second, 2)
+    return swap(second, 4), swap(first, 2)
+
+
+def gather_rest(first, second, beside_second, across_first, behind, behind_last):
     return (
         first,
         second,
-        beside_first,
+        swap(copied(first, behind), 4),
         beside_second,
         across_first,
-        across_second,
+        swap(second, 2),
         swap(across_first, 4),
-        swap(beside_second, 2),
+        swap(copied(beside_second, behind_last), 2),
     )
 
 
@@ -918,9 +928,8 @@
         *gather_own(attention_pieces, attention_parts, 1, (ffn_parts[1],))
     )
     attention_blocks = gather_cores(attention_near)
-    ffn_weights = gather_cores(
-        gather_halves(*gather_own(ffn_pieces, ffn_parts, 2, attention_near[1:]))
-    )
+    ffn_own = gather_own(ffn_pieces, ffn_parts, 2, attention_near[1:])
+    ffn_passed = gather_halves(*ffn_own)
     gain_parts = []
     for start, width in ((0, D), (D, D), (2 * D, D), (3 * D, D), (4 * D, HD), (4 * D + HD, HD)):
         gain_parts.append(gains[start : start + width][None])
@@ -956,6 +965,9 @@
         (tokens, gain_input, gain_query, gain_key, cosine, sine, order, *attention_blocks),
     )
     key_values = [key_value] + [swap(key_value, step) for step in range(1, group_size)]
+    ffn_weights = gather_cores(
+        gather_rest(*ffn_own, *ffn_passed, (key_value,), key_values[1:])
+    )
     probs, attended, attn_out, middle, out_weight = local_call(
         functools.partial(attend_kernel, attention_pieces),
         (
@@ -1050,8 +1062,10 @@
     )
     far_three, far_one = scatter_cores(far_three, far_one)
     over_x, over_y, sent = scatter_one(attention_pieces, near_one, far_one)
-    threes = scatter_three(attention_pieces, near_three, far_three, (sent, arrived[0]))
-    terms, _ = scatter_passed(attention_pieces, threes, over_x, over_y, near_one, far_one)
+    threes = scatter_three(attention_pieces, near_three, far_three, (sent,))
+    terms, _ = scatter_passed(
+        attention_pieces, threes, over_x, over_y, near_one, far_one, (arrived[0],)
+    )
     grads_attention, _, _ = scatter_high(attention_pieces, terms, arrived)
     gain_grads = grads_attention[attention_rows:].reshape(-1)[: gains.shape[0]]
     grads_local = jnp.concatenate([grads_attention[:attention_rows], grads_ffn])

time: 227 us -> 224 us (0.987)
  waiting for transfers between devices: 79.1 us -> 67.9 us
  starting transfers between devices: 48.8 us -> 53.4 us
  Pallas kernels: 72.6 us -> 76.5 us
    ppermute x53, waiting for transfers between devices: 79.1 us -> 67.9 us  [swap(): lax.ppermute(value, ALL_AXES, [(source, source ^ mask) for source in rang...]
    ppermute x53, starting transfers between devices: 48.8 us -> 53.4 us  [swap(): lax.ppermute(value, ALL_AXES, [(source, source ^ mask) for source in rang...]
    pallas_call x17 -> x19, Pallas kernels: 72.6 us -> 76.5 us  [local_call(): pl.pallas_call(body, out_shape=outs, in_specs=specs, out_specs=tuple((pl....]
    unnamed x124 -> x132, local copies, waits for them, and re-layouts: 13.1 us -> 12.7 us
  transfers between devices with their start and end apart: 53 -> 53, of which waited for: 21 -> 19; matrix products, arithmetic and copies ran while one was open for 4% -> 4% of each run, Pallas kernels for 20% -> 23%
where the time goes in v10:
time: 224 us; the launch traced here: 223 us
  Pallas kernels  76.5 us (34%)
  waiting for transfers between devices  67.9 us (30%)
  starting transfers between devices  53.4 us (24%)
  local copies, waits for them, and re-layouts  15.9 us (7%)
  other arithmetic  8.26 us (4%)
    pallas_call x19, Pallas kernels, local_call(): pl.pallas_call(body, out_shape=outs, in_specs=specs, out_specs=tuple((pl....  76.5 us
    ppermute x53, waiting for transfers between devices, swap(): lax.ppermute(value, ALL_AXES, [(source, source ^ mask) for source in rang...  67.9 us
    ppermute x53, starting transfers between devices, swap(): lax.ppermute(value, ALL_AXES, [(source, source ^ mask) for source in rang...  53.4 us
    unnamed x132, local copies, waits for them, and re-layouts  12.7 us
  transfers between devices with their start and end apart: 53, of which 19 were waited for; matrix products, arithmetic and copies ran while one was open for 4% of the time, Pallas kernels for 23%

profile of v10, /device:TPU:0, one launch (start us, length us, event | category | flops | bytes accessed | tf_op | source)
XLA Modules:
  0.0 223.2 jit_solution(5879713358083921297)
XLA Ops:
  1.8 3.1 %collective-permute-start.3 = (bf16[960,128]{1,0:T(8,128)(2,1)S(1)}, bf16[960,128]{1,0:T(8,128)(2,1)S(1)}, u32[]{:S(2)}, u32[]{:S(2)}) collective-permute-start(bf16[960,128]{1,0:T(8,128)(2,1)S(1)} %slice.66.refs_1_), channel_id=1, source_target_pairs={{0,8},{1,9},{2,10},{3,11},{4,12},{5,13},{6,14},{7,15},{8,0},{9,1},... | collective-permute-start | bytes 737288 | tf_op jit(solution)/shard_map/ppermute | solution.py:127
  5.0 2.5 %collective-permute-start.2 = (bf16[400,128]{1,0:T(8,128)(2,1)S(1)}, bf16[400,128]{1,0:T(8,128)(2,1)S(1)}, u32[]{:S(2)}, u32[]{:S(2)}) collective-permute-start(bf16[400,128]{1,0:T(8,128)(2,1)S(1)} %slice.65.refs_1_), channel_id=1, source_target_pairs={{0,24},{1,25},{2,26},{3,27},{4,28},{5,29},{6,30},{7,31},{8,16},{9,... | collective-permute-start | bytes 307208 | tf_op jit(solution)/shard_map/ppermute | solution.py:127
  9.4 2.5 %collective-permute-start.15 = (bf16[960,128]{1,0:T(8,128)(2,1)S(1)}, bf16[960,128]{1,0:T(8,128)(2,1)S(1)}, u32[]{:S(2)}, u32[]{:S(2)}) collective-permute-start(bf16[960,128]{1,0:T(8,128)(2,1)S(1)} %slice.66.refs_1_), channel_id=1, source_target_pairs={{0,24},{1,25},{2,26},{3,27},{4,28},{5,29},{6,30},{7,31},{8,16},{9,... | collective-permute-start | bytes 737288 | tf_op jit(solution)/shard_map/ppermute | solution.py:127
  12.0 4.5 %collective-permute-done.2.refs_4_ = bf16[400,128]{1,0:T(8,128)(2,1)S(1)} collective-permute-done((bf16[400,128]{1,0:T(8,128)(2,1)S(1)}, bf16[400,128]{1,0:T(8,128)(2,1)S(1)}, u32[]{:S(2)}, u32[]{:S(2)}) %collective-permute-start.2) | collective-permute-done | bytes 102432 | tf_op jit(solution)/shard_map/ppermute | solution.py:127
  24.9 5.2 %collective-permute-done.5.refs_10_.refs_7_.refs_6_.refs_9_.refs_20_ = bf16[1600,128]{1,0:T(8,128)(2,1)S(1)} collective-permute-done((bf16[1600,128]{1,0:T(8,128)(2,1)}, bf16[1600,128]{1,0:T(8,128)(2,1)S(1)}, u32[]{:S(2)}, u32[]{:S(2)}) %collective-permute-start.5) | collective-permute-done | bytes 409632 | tf_op jit(solution)/shard_map/ppermute | solution.py:127
  31.8 3.5 %collective-permute-start.14 = (bf16[960,128]{1,0:T(8,128)(2,1)S(1)}, bf16[960,128]{1,0:T(8,128)(2,1)S(1)}, u32[]{:S(2)}, u32[]{:S(2)}) collective-permute-start(bf16[960,128]{1,0:T(8,128)(2,1)S(1)} %slice.66.refs_1_), channel_id=1, source_target_pairs={{0,16},{1,17},{2,18},{3,19},{4,20},{5,21},{6,22},{7,23},{8,24},{9,... | collective-permute-start | bytes 737288 | tf_op jit(solution)/shard_map/ppermute | solution.py:127
  36.4 10.6 %collective-permute-done.14.refs_3_ = bf16[960,128]{1,0:T(8,128)(2,1)S(1)} collective-permute-done((bf16[960,128]{1,0:T(8,128)(2,1)S(1)}, bf16[960,128]{1,0:T(8,128)(2,1)S(1)}, u32[]{:S(2)}, u32[]{:S(2)}) %collective-permute-start.14) | collective-permute-done | bytes 245792 | tf_op jit(solution)/shard_map/ppermute | solution.py:127
  48.5 2.9 %shard_map.155 = (bf16[1920,128]{1,0:T(8,128)(2,1)}, bf16[1920,128]{1,0:T(8,128)(2,1)}) custom-call(s32[1]{0:T(128)} %bitcast.refs_0_, bf16[960,128]{1,0:T(8,128)(2,1)} %copy-done.22, bf16[960,128]{1,0:T(8,128)(2,1)} %copy-done.23, bf16[960,128]{1,0:T(8,128)(2,1)} %copy-done.45, bf16[960,128]{1,0:T(8,128)(2,1)} %copy-done.44, bf16[1600,128]{1,0:T(8,128)(2,1)} %copy-done.1, ...), custom_call_target="tpu_custom_call" | custom-call | tf_op jit(solution)/shard_map/pallas_call | solution.py:139
  56.8 4.0 %shard_map.153 = (bf16[128,640]{1,0:T(8,128)(2,1)}, f32[128,1024]{1,0:T(8,128)}, f32[128,256]{1,0:T(8,128)}, bf16[128,1024]{1,0:T(8,128)(2,1)}, bf16[128,512]{1,0:T(8,128)(2,1)}) custom-call(s32[1]{0:T(128)} %bitcast.refs_0_, bf16[128,640]{1,0:T(8,128)(2,1)} %refs_1_.5, f32[1,640]{1,0:T(1,128)} %broadcast_in_dim.30.refs_2_, f32[1,256]{1,0:T(1,128)} %bitcast.29, ...), custom_call_target="tpu_custom_call" | custom-call | tf_op jit(solution)/shard_map/pallas_call | solution.py:139
  62.0 3.6 %collective-permute-done.18.refs_10_ = bf16[1920,128]{1,0:T(8,128)(2,1)} collective-permute-done((bf16[1920,128]{1,0:T(8,128)(2,1)}, bf16[1920,128]{1,0:T(8,128)(2,1)}, u32[]{:S(2)}, u32[]{:S(2)}) %collective-permute-start.18) | collective-permute-done | bytes 491552 | tf_op jit(solution)/shard_map/ppermute | solution.py:127
  76.9 6.5 %collective-permute-done.19.refs_11_ = bf16[1920,128]{1,0:T(8,128)(2,1)S(1)} collective-permute-done((bf16[1920,128]{1,0:T(8,128)(2,1)S(1)}, bf16[1920,128]{1,0:T(8,128)(2,1)S(1)}, u32[]{:S(2)}, u32[]{:S(2)}) %collective-permute-start.19) | collective-permute-done | bytes 491552 | tf_op jit(solution)/shard_map/ppermute | solution.py:127
  85.8 8.0 %collective-permute-done.20.refs_12_ = bf16[1920,128]{1,0:T(8,128)(2,1)S(1)} collective-permute-done((bf16[1920,128]{1,0:T(8,128)(2,1)}, bf16[1920,128]{1,0:T(8,128)(2,1)S(1)}, u32[]{:S(2)}, u32[]{:S(2)}) %collective-permute-start.20) | collective-permute-done | bytes 491552 | tf_op jit(solution)/shard_map/ppermute | solution.py:127
  96.9 5.7 %shard_map.154 = (f32[128,2048]{1,0:T(8,128)}, bf16[128,1024]{1,0:T(8,128)(2,1)}, f32[128,640]{1,0:T(8,128)}, f32[128,640]{1,0:T(8,128)}, bf16[1024,640]{1,0:T(8,128)(2,1)}) custom-call(s32[1]{0:T(128)} %bitcast.refs_0_, bf16[128,640]{1,0:T(8,128)(2,1)} %refs_1_.5, f32[1,640]{1,0:T(1,128)} %broadcast_in_dim.14.refs_2_.refs_3_, f32[128,512]{1,0:T(8,128)} %fusion.4.refs_3_, ...), custom_call_target="tpu_custom_call" | custom-call | tf_op jit(solution)/shard_map/pallas_call | solution.py:139
  104.1 14.9 %shard_map.158 = (bf16[128,640]{1,0:T(8,128)(2,1)}, f32[128,640]{1,0:T(8,128)}, f32[1,640]{1,0:T(1,128)}, f32[1,640]{1,0:T(1,128)}, bf16[11520,128]{1,0:T(8,128)...) custom-call(s32[1]{0:T(128)} %bitcast.refs_0_, ...), custom_call_target="tpu_custom_call" | custom-call | tf_op jit(solution)/shard_map/pallas_call | solution.py:139
  119.5 5.8 %shard_map.159 = (bf16[1024,640]{1,0:T(8,128)(2,1)}, f32[128,1024]{1,0:T(8,128)}, f32[1,640]{1,0:T(1,128)}, f32[128,512]{1,0:T(8,128)}, f32[128,512]{1,0:T(8,128)}, /*index=5*/bf16[256,512]{1,0:T(8,128)(2,1)}) custom-call(s32[1]{0:T(128)} %bitcast.refs_0_, f32[128,640]{1,0:T(8,128)} %get-tuple-element.81.refs_1_.refs_10_, ...), custom_call_target="tpu_custom_call" | custom-call | tf_op jit(solution)/shard_map/pallas_call | solution.py:139
  126.9 2.6 %shard_map.160 = (bf16[1920,128]{1,0:T(8,128)(2,1)}, bf16[1920,128]{1,0:T(8,128)(2,1)}) custom-call(s32[1]{0:T(128)} %bitcast.refs_0_, bf16[3840,128]{1,0:T(8,128)(2,1)} %get-tuple-element.91.refs_1_.refs_5_, bf16[3840,128]{1,0:T(8,128)(2,1)} %copy-done.7, f32[128,1024]{1,0:T(8,128)} %get-tuple-element.86.refs_3_.refs_6_), custom_call_target="tpu_custom_call" | custom-call | tf_op jit(solution)/shard_map/pallas_call | solution.py:139
  134.8 4.6 %shard_map.161 = (bf16[3840,128]{1,0:T(8,128)(2,1)}, bf16[1920,128]{1,0:T(8,128)(2,1)}, bf16[1920,128]{1,0:T(8,128)(2,1)}, bf16[1920,128]{1,0:T(8,128)(2,1)}, bf16[2432,128]{1,0:T(8,128)(2,1)}) custom-call(s32[1]{0:T(128)} %bitcast.refs_0_, bf16[11520,128]{1,0:T(8,128)(2,1)} %get-tuple-element.87.refs_1_, bf16[11520,128]{1,0:T(8,128)(2,1)} %copy-done.8, ...), custom_call_target="tpu_custom_call" | custom-call | tf_op jit(solution)/shard_map/pallas_call | solution.py:139
  141.4 4.5 %shard_map.162 = (bf16[640,1024]{1,0:T(8,128)(2,1)}, f32[128,640]{1,0:T(8,128)}, f32[1,256]{1,0:T(1,128)}) custom-call(s32[1]{0:T(128)} %bitcast.refs_0_, f32[1,256]{1,0:T(1,128)} %bitcast.30, f32[128,128]{1,0:T(8,128)} %get-tuple-element.153.refs_5_.refs_2_.refs_4_, f32[128,128]{1,0:T(8,128)} %get-tuple-element.152.refs_6_.refs_3_.refs_5_, ...), custom_call_target="tpu_custom_call" | custom-call | tf_op jit(solution)/shard_map/pallas_call | solution.py:139
  146.9 3.2 %shard_map.163 = (bf16[1920,128]{1,0:T(8,128)(2,1)}, bf16[1920,128]{1,0:T(8,128)(2,1)}, f32[8,128]{1,0:T(8,128)}) custom-call(s32[1]{0:T(128)} %bitcast.refs_0_, bf16[1920,128]{1,0:T(8,128)(2,1)} %get-tuple-element.102.refs_1_, bf16[1920,128]{1,0:T(8,128)(2,1)} %get-tuple-element.103.refs_2_, bf16[1920,128]{1,0:T(8,128)(2,1)} %copy-done.40, ...), custom_call_target="tpu_custom_call" | custom-call | tf_op jit(solution)/shard_map/pallas_call | solution.py:139
  153.9 4.6 %collective-permute-done.33.refs_17_.refs_5_ = bf16[2432,128]{1,0:T(8,128)(2,1)S(1)} collective-permute-done((bf16[2432,128]{1,0:T(8,128)(2,1)}, bf16[2432,128]{1,0:T(8,128)(2,1)S(1)}, u32[]{:S(2)}, u32[]{:S(2)}) %collective-permute-start.33) | collective-permute-done | bytes 622624 | tf_op jit(solution)/shard_map/ppermute | solution.py:127
  159.3 4.7 %shard_map.164 = (bf16[640,512]{1,0:T(8,128)(2,1)}, bf16[128,640]{1,0:T(8,128)(2,1)}, f32[32,128]{1,0:T(8,128)}) custom-call(s32[1]{0:T(128)} %bitcast.refs_0_, bf16[128,640]{1,0:T(8,128)(2,1)} %refs_1_.5, f32[1,640]{1,0:T(1,128)} %broadcast_in_dim.30.refs_2_, f32[1,256]{1,0:T(1,128)} %bitcast.28, f32[128,128]{1,0:T(8,128)} %get-tuple-element.153.refs_5_.refs_2_.refs_4_, ...), custom_call_target="tpu_custom_call" | custom-call | tf_op jit(solution)/shard_map/pallas_call | solution.py:139
  164.0 3.9 %collective-permute-done.38.refs_4_ = bf16[1920,128]{1,0:T(8,128)(2,1)S(1)} collective-permute-done((bf16[1920,128]{1,0:T(8,128)(2,1)}, bf16[1920,128]{1,0:T(8,128)(2,1)S(1)}, u32[]{:S(2)}, u32[]{:S(2)}) %collective-permute-start.38) | collective-permute-done | bytes 491552 | tf_op jit(solution)/shard_map/ppermute | solution.py:127
  168.9 4.1 %shard_map.165 = (f32[960,128]{1,0:T(8,128)}, bf16[960,128]{1,0:T(8,128)(2,1)}, bf16[960,128]{1,0:T(8,128)(2,1)}, bf16[960,128]{1,0:T(8,128)(2,1)}) custom-call(s32[1]{0:T(128)} %bitcast.refs_0_, bf16[3840,128]{1,0:T(8,128)(2,1)} %get-tuple-element.94.refs_15_.refs_1_, bf16[1920,128]{1,0:T(8,128)(2,1)} %copy-done.14, bf16[1920,128]{1,0:T(8,128)(2,1)} %copy-done.41, ...), custom_call_target="tpu_custom_call" | custom-call | tf_op jit(solution)/shard_map/pallas_call | solution.py:139
  173.0 4.3 %shard_map.166 = (bf16[4800,128]{1,0:T(8,128)(2,1)}, bf16[1632,128]{1,0:T(8,128)(2,1)}, bf16[4800,128]{1,0:T(8,128)(2,1)}, bf16[1632,128]{1,0:T(8,128)(2,1)}) custom-call(s32[1]{0:T(128)} %bitcast.refs_0_, bf16[640,1024]{1,0:T(8,128)(2,1)} %get-tuple-element.108.refs_1_, bf16[640,512]{1,0:T(8,128)(2,1)} %get-tuple-element.109.refs_2_, ...), custom_call_target="tpu_custom_call" | custom-call | tf_op jit(solution)/shard_map/pallas_call | solution.py:139
  178.6 3.4 %collective-permute-start.48 = (bf16[960,128]{1,0:T(8,128)(2,1)S(1)}, bf16[960,128]{1,0:T(8,128)(2,1)S(1)}, u32[]{:S(2)}, u32[]{:S(2)}) collective-permute-start(bf16[960,128]{1,0:T(8,128)(2,1)S(1)} %copy-done.62), channel_id=1, source_target_pairs={{0,16},{1,17},{2,18},{3,19},{4,20},{5,21},{6,22},{7,23},{8,24},{9,... | collective-permute-start | bytes 737288 | tf_op jit(solution)/shard_map/ppermute | solution.py:127
  187.0 2.7 %collective-permute-start.49 = (bf16[960,128]{1,0:T(8,128)(2,1)S(1)}, bf16[960,128]{1,0:T(8,128)(2,1)S(1)}, u32[]{:S(2)}, u32[]{:S(2)}) collective-permute-start(bf16[960,128]{1,0:T(8,128)(2,1)S(1)} %copy-done.61), channel_id=1, source_target_pairs={{0,24},{1,25},{2,26},{3,27},{4,28},{5,29},{6,30},{7,31},{8,16},{9,... | collective-permute-start | bytes 737288 | tf_op jit(solution)/shard_map/ppermute | solution.py:127
  189.7 2.8 %shard_map.168 = (bf16[1600,128]{1,0:T(8,128)(2,1)}, bf16[800,128]{1,0:T(8,128)(2,1)}, bf16[800,128]{1,0:T(8,128)(2,1)}, bf16[800,128]{1,0:T(8,128)(2,1)}, bf16[800,128]{1,0:T(8,128)(2,1)}) custom-call(s32[1]{0:T(128)} %bitcast.refs_0_, bf16[4800,128]{1,0:T(8,128)(2,1)} %get-tuple-element.115.refs_1_, bf16[4800,128]{1,0:T(8,128)(2,1)} %copy-done.17, ...), custom_call_target="tpu_custom_call" | custom-call | tf_op jit(solution)/shard_map/pallas_call | solution.py:139
  193.3 2.3 %shard_map.169 = (bf16[800,128]{1,0:T(8,128)(2,1)}, bf16[832,128]{1,0:T(8,128)(2,1)}, f32[32,128]{1,0:T(8,128)}) custom-call(s32[1]{0:T(128)} %bitcast.refs_0_, bf16[800,128]{1,0:T(8,128)(2,1)} %get-tuple-element.122.refs_1_, bf16[800,128]{1,0:T(8,128)(2,1)} %get-tuple-element.123.refs_2_, bf16[832,128]{1,0:T(8,128)(2,1)} %copy-done.48, ...), custom_call_target="tpu_custom_call" | custom-call | tf_op jit(solution)/shard_map/pallas_call | solution.py:139
  199.8 4.6 %collective-permute-done.41.refs_2_ = bf16[800,128]{1,0:T(8,128)(2,1)S(1)} collective-permute-done((bf16[800,128]{1,0:T(8,128)(2,1)S(1)}, bf16[800,128]{1,0:T(8,128)(2,1)S(1)}, u32[]{:S(2)}, u32[]{:S(2)}) %collective-permute-start.41) | collective-permute-done | bytes 204832 | tf_op jit(solution)/shard_map/ppermute | solution.py:127
  207.5 2.5 %shard_map.170 = (f32[432,128]{1,0:T(8,128)}, bf16[432,128]{1,0:T(8,128)(2,1)}, bf16[432,128]{1,0:T(8,128)(2,1)}, bf16[432,128]{1,0:T(8,128)(2,1)}) custom-call(s32[1]{0:T(128)} %bitcast.refs_0_, bf16[1600,128]{1,0:T(8,128)(2,1)} %get-tuple-element.120.refs_1_, bf16[800,128]{1,0:T(8,128)(2,1)} %copy-done.49, bf16[800,128]{1,0:T(8,128)(2,1)} %copy-done.50, ...), custom_call_target="tpu_custom_call" | custom-call | tf_op jit(solution)/shard_map/pallas_call | solution.py:139
  210.2 3.6 %collective-permute-start.51 = (bf16[432,128]{1,0:T(8,128)(2,1)}, bf16[432,128]{1,0:T(8,128)(2,1)S(1)}, u32[]{:S(2)}, u32[]{:S(2)}) collective-permute-start(bf16[432,128]{1,0:T(8,128)(2,1)} %get-tuple-element.134), channel_id=1, source_target_pairs={{0,16},{1,17},{2,18},{3,19},{4,20},{5,21},{6,22},{7,23},{8,24},{9,... | collective-permute-start | bytes 331784 | tf_op jit(solution)/shard_map/ppermute | solution.py:127
  215.7 3.8 %collective-permute-done.51 = bf16[432,128]{1,0:T(8,128)(2,1)S(1)} collective-permute-done((bf16[432,128]{1,0:T(8,128)(2,1)}, bf16[432,128]{1,0:T(8,128)(2,1)S(1)}, u32[]{:S(2)}, u32[]{:S(2)}) %collective-permute-start.51) | collective-permute-done | bytes 110624 | tf_op jit(solution)/shard_map/ppermute | solution.py:127
  (258 shorter events, 76.6 us)
Async XLA Ops:
  1.8 16.7 %collective-permute-start.3 = (bf16[960,128]{1,0:T(8,128)(2,1)S(1)}, bf16[960,128]{1,0:T(8,128)(2,1)S(1)}, u32[]{:S(2)}, u32[]{:S(2)}) collective-permute-start(bf16[960,128]{1,0:T(8,128)(2,1)S(1)} %slice.66.refs_1_), channel_id=1, source_target_pairs={{0,8},{1,9},{2,10},{3,11},{4,12},{5,13},{6,14},{7,15},{8,0},{9,1},... | collective-permute-start | bytes 737288 | tf_op jit(solution)/shard_map/ppermute | solution.py:127
  5.0 11.5 %collective-permute-start.2 = (bf16[400,128]{1,0:T(8,128)(2,1)S(1)}, bf16[400,128]{1,0:T(8,128)(2,1)S(1)}, u32[]{:S(2)}, u32[]{:S(2)}) collective-permute-start(bf16[400,128]{1,0:T(8,128)(2,1)S(1)} %slice.65.refs_1_), channel_id=1, source_target_pairs={{0,24},{1,25},{2,26},{3,27},{4,28},{5,29},{6,30},{7,31},{8,16},{9,... | collective-permute-start | bytes 307208 | tf_op jit(solution)/shard_map/ppermute | solution.py:127
  7.5 11.0 %collective-permute-start.1 = (bf16[400,128]{1,0:T(8,128)(2,1)S(1)}, bf16[400,128]{1,0:T(8,128)(2,1)S(1)}, u32[]{:S(2)}, u32[]{:S(2)}) collective-permute-start(bf16[400,128]{1,0:T(8,128)(2,1)S(1)} %slice.65.refs_1_), channel_id=1, source_target_pairs={{0,16},{1,17},{2,18},{3,19},{4,20},{5,21},{6,22},{7,23},{8,24},{9,... | collective-permute-start | bytes 307208 | tf_op jit(solution)/shard_map/ppermute | solution.py:127
  9.4 22.4 %collective-permute-start.15 = (bf16[960,128]{1,0:T(8,128)(2,1)S(1)}, bf16[960,128]{1,0:T(8,128)(2,1)S(1)}, u32[]{:S(2)}, u32[]{:S(2)}) collective-permute-start(bf16[960,128]{1,0:T(8,128)(2,1)S(1)} %slice.66.refs_1_), channel_id=1, source_target_pairs={{0,24},{1,25},{2,26},{3,27},{4,28},{5,29},{6,30},{7,31},{8,16},{9,... | collective-permute-start | bytes 737288 | tf_op jit(solution)/shard_map/ppermute | solution.py:127
  24.9 28.0 %collective-permute-start.7 = (bf16[1600,128]{1,0:T(8,128)(2,1)}, bf16[1600,128]{1,0:T(8,128)(2,1)S(1)}, u32[]{:S(2)}, u32[]{:S(2)}) collective-permute-start(bf16[1600,128]{1,0:T(8,128)(2,1)} %shard_map.152.refs_8_.refs_5_.refs_7_.refs_18_), channel_id=1, source_target_pairs={{0,1},{1,0},{2,3},{3,2},{4,5},{5,4},{6,7},{7,6},{8,9},{9,8},{10,11... | collective-permute-start | bytes 1228808 | tf_op jit(solution)/shard_map/ppermute | solution.py:127
  30.1 23.0 %collective-permute-start.9 = (bf16[1600,128]{1,0:T(8,128)(2,1)S(1)}, bf16[1600,128]{1,0:T(8,128)(2,1)S(1)}, u32[]{:S(2)}, u32[]{:S(2)}) collective-permute-start(bf16[1600,128]{1,0:T(8,128)(2,1)S(1)} %collective-permute-done.5.refs_10_.refs_7_.refs_6_.refs_9_.refs_20_), channel_id=1, source_target_pairs={{0,1},{1,0},{2,3},{3,2},{4,5},{5,4},{6,7},{7,6},{8,9},{9,8},{10,11... | collective-permute-start | bytes 1228808 | tf_op jit(solution)/shard_map/ppermute | solution.py:127
  30.1 16.9 %collective-permute-start.6 = (bf16[1600,128]{1,0:T(8,128)(2,1)S(1)}, bf16[1600,128]{1,0:T(8,128)(2,1)S(1)}, u32[]{:S(2)}, u32[]{:S(2)}) collective-permute-start(bf16[1600,128]{1,0:T(8,128)(2,1)S(1)} %collective-permute-done.5.refs_10_.refs_7_.refs_6_.refs_9_.refs_20_), channel_id=1, source_target_pairs={{0,4},{1,5},{2,6},{3,7},{4,0},{5,1},{6,2},{7,3},{8,12},{9,13},{10,... | collective-permute-start | bytes 1228808 | tf_op jit(solution)/shard_map/ppermute | solution.py:127
  31.5 22.1 %collective-permute-start.8 = (bf16[1600,128]{1,0:T(8,128)(2,1)S(1)}, bf16[1600,128]{1,0:T(8,128)(2,1)S(1)}, u32[]{:S(2)}, u32[]{:S(2)}) collective-permute-start(bf16[1600,128]{1,0:T(8,128)(2,1)S(1)} %collective-permute-done.4.refs_9_.refs_6_.refs_5_.refs_8_.refs_19_), channel_id=1, source_target_pairs={{0,1},{1,0},{2,3},{3,2},{4,5},{5,4},{6,7},{7,6},{8,9},{9,8},{10,11... | collective-permute-start | bytes 1228808 | tf_op jit(solution)/shard_map/ppermute | solution.py:127
  31.8 15.2 %collective-permute-start.14 = (bf16[960,128]{1,0:T(8,128)(2,1)S(1)}, bf16[960,128]{1,0:T(8,128)(2,1)S(1)}, u32[]{:S(2)}, u32[]{:S(2)}) collective-permute-start(bf16[960,128]{1,0:T(8,128)(2,1)S(1)} %slice.66.refs_1_), channel_id=1, source_target_pairs={{0,16},{1,17},{2,18},{3,19},{4,20},{5,21},{6,22},{7,23},{8,24},{9,... | collective-permute-start | bytes 737288 | tf_op jit(solution)/shard_map/ppermute | solution.py:127
  51.3 23.3 %collective-permute-start.22 = (bf16[1920,128]{1,0:T(8,128)(2,1)}, bf16[1920,128]{1,0:T(8,128)(2,1)S(1)}, u32[]{:S(2)}, u32[]{:S(2)}) collective-permute-start(bf16[1920,128]{1,0:T(8,128)(2,1)} %get-tuple-element.75.refs_1_.refs_6_), channel_id=1, source_target_pairs={{0,1},{1,0},{2,3},{3,2},{4,5},{5,4},{6,7},{7,6},{8,9},{9,8},{10,11... | collective-permute-start | bytes 1474568 | tf_op jit(solution)/shard_map/ppermute | solution.py:127
  51.3 14.3 %collective-permute-start.18 = (bf16[1920,128]{1,0:T(8,128)(2,1)}, bf16[1920,128]{1,0:T(8,128)(2,1)}, u32[]{:S(2)}, u32[]{:S(2)}) collective-permute-start(bf16[1920,128]{1,0:T(8,128)(2,1)} %get-tuple-element.75.refs_1_.refs_6_), channel_id=1, source_target_pairs={{0,2},{1,3},{2,0},{3,1},{4,6},{5,7},{6,4},{7,5},{8,10},{9,11},{10,... | collective-permute-start | bytes 1474568 | tf_op jit(solution)/shard_map/ppermute | solution.py:127
  52.9 22.5 %collective-permute-start.23 = (bf16[1920,128]{1,0:T(8,128)(2,1)}, bf16[1920,128]{1,0:T(8,128)(2,1)}, u32[]{:S(2)}, u32[]{:S(2)}) collective-permute-start(bf16[1920,128]{1,0:T(8,128)(2,1)} %get-tuple-element.76.refs_7_), channel_id=1, source_target_pairs={{0,1},{1,0},{2,3},{3,2},{4,5},{5,4},{6,7},{7,6},{8,9},{9,8},{10,11... | collective-permute-start | bytes 1474568 | tf_op jit(solution)/shard_map/ppermute | solution.py:127
  53.1 14.1 %collective-permute-start.17 = (bf16[1920,128]{1,0:T(8,128)(2,1)}, bf16[1920,128]{1,0:T(8,128)(2,1)S(1)}, u32[]{:S(2)}, u32[]{:S(2)}) collective-permute-start(bf16[1920,128]{1,0:T(8,128)(2,1)} %get-tuple-element.76.refs_7_), channel_id=1, source_target_pairs={{0,4},{1,5},{2,6},{3,7},{4,0},{5,1},{6,2},{7,3},{8,12},{9,13},{10,... | collective-permute-start | bytes 1474568 | tf_op jit(solution)/shard_map/ppermute | solution.py:127
  69.3 14.1 %collective-permute-start.19 = (bf16[1920,128]{1,0:T(8,128)(2,1)S(1)}, bf16[1920,128]{1,0:T(8,128)(2,1)S(1)}, u32[]{:S(2)}, u32[]{:S(2)}) collective-permute-start(bf16[1920,128]{1,0:T(8,128)(2,1)S(1)} %copy-done.28), channel_id=1, source_target_pairs={{0,2},{1,3},{2,0},{3,1},{4,6},{5,7},{6,4},{7,5},{8,10},{9,11},{10,... | collective-permute-start | bytes 1474568 | tf_op jit(solution)/shard_map/ppermute | solution.py:127
  70.9 14.4 %collective-permute-start.16 = (bf16[1920,128]{1,0:T(8,128)(2,1)}, bf16[1920,128]{1,0:T(8,128)(2,1)S(1)}, u32[]{:S(2)}, u32[]{:S(2)}) collective-permute-start(bf16[1920,128]{1,0:T(8,128)(2,1)} %shard_map.156), channel_id=1, source_target_pairs={{0,4},{1,5},{2,6},{3,7},{4,0},{5,1},{6,2},{7,3},{8,12},{9,13},{10,... | collective-permute-start | bytes 1474568 | tf_op jit(solution)/shard_map/ppermute | solution.py:127
  72.1 13.1 %collective-permute-start.26 = (bf16[1920,128]{1,0:T(8,128)(2,1)}, bf16[1920,128]{1,0:T(8,128)(2,1)S(1)}, u32[]{:S(2)}, u32[]{:S(2)}) collective-permute-start(bf16[1920,128]{1,0:T(8,128)(2,1)} %collective-permute-done.18.refs_10_), channel_id=1, source_target_pairs={{0,1},{1,0},{2,3},{3,2},{4,5},{5,4},{6,7},{7,6},{8,9},{9,8},{10,11... | collective-permute-start | bytes 1474568 | tf_op jit(solution)/shard_map/ppermute | solution.py:127
  74.6 19.2 %collective-permute-start.20 = (bf16[1920,128]{1,0:T(8,128)(2,1)}, bf16[1920,128]{1,0:T(8,128)(2,1)S(1)}, u32[]{:S(2)}, u32[]{:S(2)}) collective-permute-start(bf16[1920,128]{1,0:T(8,128)(2,1)} %collective-permute-done.18.refs_10_), channel_id=1, source_target_pairs={{0,4},{1,5},{2,6},{3,7},{4,0},{5,1},{6,2},{7,3},{8,12},{9,13},{10,... | collective-permute-start | bytes 1474568 | tf_op jit(solution)/shard_map/ppermute | solution.py:127
  75.4 18.4 %collective-permute-start.21 = (bf16[1920,128]{1,0:T(8,128)(2,1)}, bf16[1920,128]{1,0:T(8,128)(2,1)}, u32[]{:S(2)}, u32[]{:S(2)}) collective-permute-start(bf16[1920,128]{1,0:T(8,128)(2,1)} %shard_map.157), channel_id=1, source_target_pairs={{0,2},{1,3},{2,0},{3,1},{4,6},{5,7},{6,4},{7,5},{8,10},{9,11},{10,... | collective-permute-start | bytes 1474568 | tf_op jit(solution)/shard_map/ppermute | solution.py:127
  83.4 19.3 %collective-permute-start.25 = (bf16[1920,128]{1,0:T(8,128)(2,1)}, bf16[1920,128]{1,0:T(8,128)(2,1)S(1)}, u32[]{:S(2)}, u32[]{:S(2)}) collective-permute-start(bf16[1920,128]{1,0:T(8,128)(2,1)} %copy-done.13), channel_id=1, source_target_pairs={{0,1},{1,0},{2,3},{3,2},{4,5},{5,4},{6,7},{7,6},{8,9},{9,8},{10,11... | collective-permute-start | bytes 1474568 | tf_op jit(solution)/shard_map/ppermute | solution.py:127
  85.2 17.4 %collective-permute-start.27 = (bf16[1920,128]{1,0:T(8,128)(2,1)S(1)}, bf16[1920,128]{1,0:T(8,128)(2,1)S(1)}, u32[]{:S(2)}, u32[]{:S(2)}) collective-permute-start(bf16[1920,128]{1,0:T(8,128)(2,1)S(1)} %collective-permute-done.19.refs_11_), channel_id=1, source_target_pairs={{0,1},{1,0},{2,3},{3,2},{4,5},{5,4},{6,7},{7,6},{8,9},{9,8},{10,11... | collective-permute-start | bytes 1474568 | tf_op jit(solution)/shard_map/ppermute | solution.py:127
  85.3 17.4 %collective-permute-start.24 = (bf16[1920,128]{1,0:T(8,128)(2,1)S(1)}, bf16[1920,128]{1,0:T(8,128)(2,1)S(1)}, u32[]{:S(2)}, u32[]{:S(2)}) collective-permute-start(bf16[1920,128]{1,0:T(8,128)(2,1)S(1)} %collective-permute-done.16.refs_8_), channel_id=1, source_target_pairs={{0,1},{1,0},{2,3},{3,2},{4,5},{5,4},{6,7},{7,6},{8,9},{9,8},{10,11... | collective-permute-start | bytes 1474568 | tf_op jit(solution)/shard_map/ppermute | solution.py:127
  118.9 14.2 %collective-permute-start.30 = (bf16[11520,128]{1,0:T(8,128)(2,1)}, bf16[11520,128]{1,0:T(8,128)(2,1)S(1)}, u32[]{:S(2)}, u32[]{:S(2)}) collective-permute-start(bf16[11520,128]{1,0:T(8,128)(2,1)} %get-tuple-element.88), channel_id=1, source_target_pairs={{0,1},{1,0},{2,3},{3,2},{4,5},{5,4},{6,7},{7,6},{8,9},{9,8},{10,11... | collective-permute-start | bytes 8847368 | tf_op jit(solution)/shard_map/ppermute | solution.py:127
  129.6 16.3 %collective-permute-start.34 = (bf16[1920,128]{1,0:T(8,128)(2,1)}, bf16[1920,128]{1,0:T(8,128)(2,1)S(1)}, u32[]{:S(2)}, u32[]{:S(2)}) collective-permute-start(bf16[1920,128]{1,0:T(8,128)(2,1)} %get-tuple-element.104), channel_id=1, source_target_pairs={{0,4},{1,5},{2,6},{3,7},{4,0},{5,1},{6,2},{7,3},{8,12},{9,13},{10,... | collective-permute-start | bytes 1474568 | tf_op jit(solution)/shard_map/ppermute | solution.py:127
  130.8 15.1 %collective-permute-start.35 = (bf16[1920,128]{1,0:T(8,128)(2,1)}, bf16[1920,128]{1,0:T(8,128)(2,1)S(1)}, u32[]{:S(2)}, u32[]{:S(2)}) collective-permute-start(bf16[1920,128]{1,0:T(8,128)(2,1)} %get-tuple-element.93.refs_5_), channel_id=1, source_target_pairs={{0,2},{1,3},{2,0},{3,1},{4,6},{5,7},{6,4},{7,5},{8,10},{9,11},{10,... | collective-permute-start | bytes 1474568 | tf_op jit(solution)/shard_map/ppermute | solution.py:127
  139.4 19.1 %collective-permute-start.33 = (bf16[2432,128]{1,0:T(8,128)(2,1)}, bf16[2432,128]{1,0:T(8,128)(2,1)S(1)}, u32[]{:S(2)}, u32[]{:S(2)}) collective-permute-start(bf16[2432,128]{1,0:T(8,128)(2,1)} %get-tuple-element.101), channel_id=1, source_target_pairs={{0,2},{1,3},{2,0},{3,1},{4,6},{5,7},{6,4},{7,5},{8,10},{9,11},{10,... | collective-permute-start | bytes 1867784 | tf_op jit(solution)/shard_map/ppermute | solution.py:127
  140.6 13.3 %collective-permute-start.36 = (bf16[1920,128]{1,0:T(8,128)(2,1)}, bf16[1920,128]{1,0:T(8,128)(2,1)S(1)}, u32[]{:S(2)}, u32[]{:S(2)}) collective-permute-start(bf16[1920,128]{1,0:T(8,128)(2,1)} %get-tuple-element.106), channel_id=1, source_target_pairs={{0,4},{1,5},{2,6},{3,7},{4,0},{5,1},{6,2},{7,3},{8,12},{9,13},{10,... | collective-permute-start | bytes 1474568 | tf_op jit(solution)/shard_map/ppermute | solution.py:127
  150.0 17.8 %collective-permute-start.38 = (bf16[1920,128]{1,0:T(8,128)(2,1)}, bf16[1920,128]{1,0:T(8,128)(2,1)S(1)}, u32[]{:S(2)}, u32[]{:S(2)}) collective-permute-start(bf16[1920,128]{1,0:T(8,128)(2,1)} %get-tuple-element.112), channel_id=1, source_target_pairs={{0,2},{1,3},{2,0},{3,1},{4,6},{5,7},{6,4},{7,5},{8,10},{9,11},{10,... | collective-permute-start | bytes 1474568 | tf_op jit(solution)/shard_map/ppermute | solution.py:127
  151.5 16.3 %collective-permute-start.37 = (bf16[1920,128]{1,0:T(8,128)(2,1)}, bf16[1920,128]{1,0:T(8,128)(2,1)S(1)}, u32[]{:S(2)}, u32[]{:S(2)}) collective-permute-start(bf16[1920,128]{1,0:T(8,128)(2,1)} %get-tuple-element.105.refs_26_), channel_id=1, source_target_pairs={{0,4},{1,5},{2,6},{3,7},{4,0},{5,1},{6,2},{7,3},{8,12},{9,13},{10,... | collective-permute-start | bytes 1474568 | tf_op jit(solution)/shard_map/ppermute | solution.py:127
  177.8 14.6 %collective-permute-start.44 = (bf16[960,128]{1,0:T(8,128)(2,1)S(1)}, bf16[960,128]{1,0:T(8,128)(2,1)S(1)}, u32[]{:S(2)}, u32[]{:S(2)}) collective-permute-start(bf16[960,128]{1,0:T(8,128)(2,1)S(1)} %copy-done.63), channel_id=1, source_target_pairs={{0,8},{1,9},{2,10},{3,11},{4,12},{5,13},{6,14},{7,15},{8,0},{9,1},... | collective-permute-start | bytes 737288 | tf_op jit(solution)/shard_map/ppermute | solution.py:127
  178.6 20.0 %collective-permute-start.48 = (bf16[960,128]{1,0:T(8,128)(2,1)S(1)}, bf16[960,128]{1,0:T(8,128)(2,1)S(1)}, u32[]{:S(2)}, u32[]{:S(2)}) collective-permute-start(bf16[960,128]{1,0:T(8,128)(2,1)S(1)} %copy-done.62), channel_id=1, source_target_pairs={{0,16},{1,17},{2,18},{3,19},{4,20},{5,21},{6,22},{7,23},{8,24},{9,... | collective-permute-start | bytes 737288 | tf_op jit(solution)/shard_map/ppermute | solution.py:127
  187.0 12.9 %collective-permute-start.49 = (bf16[960,128]{1,0:T(8,128)(2,1)S(1)}, bf16[960,128]{1,0:T(8,128)(2,1)S(1)}, u32[]{:S(2)}, u32[]{:S(2)}) collective-permute-start(bf16[960,128]{1,0:T(8,128)(2,1)S(1)} %copy-done.61), channel_id=1, source_target_pairs={{0,24},{1,25},{2,26},{3,27},{4,28},{5,29},{6,30},{7,31},{8,16},{9,... | collective-permute-start | bytes 737288 | tf_op jit(solution)/shard_map/ppermute | solution.py:127
  195.6 11.1 %collective-permute-start.46 = (bf16[832,128]{1,0:T(8,128)(2,1)}, bf16[832,128]{1,0:T(8,128)(2,1)S(1)}, u32[]{:S(2)}, u32[]{:S(2)}) collective-permute-start(bf16[832,128]{1,0:T(8,128)(2,1)} %get-tuple-element.127), channel_id=1, source_target_pairs={{0,2},{1,3},{2,0},{3,1},{4,6},{5,7},{6,4},{7,5},{8,10},{9,11},{10,... | collective-permute-start | bytes 638984 | tf_op jit(solution)/shard_map/ppermute | solution.py:127
  (87 other events, 591.3 us)

commit v11 on v10

--- a/solution.py
+++ b/solution.py
@@ -218,6 +218,11 @@
         rows = slice(size + place * half, size + (place + 1) * half)
         total = near_ref[rows, :].astype(jnp.float32) + far_ref[rows, :].astype(jnp.float32)
         out_ref[:half, :] = total.astype(jnp.bfloat16)
+
+
+def sum_all_kernel(size, index_ref, near_three, near_one, far_three, far_one, *out_refs):
+    sum_one_kernel(size, index_ref, near_one, far_one, *out_refs[:2])
+    sum_three_kernel(size, index_ref, near_three, far_three, *out_refs[2:])
 
 
 def sum_passed_kernel(
@@ -318,6 +323,18 @@
     return local_call(copy_kernel, (array(value.shape, jnp.bfloat16),), (value,), (), behind)[0]
 
 
+def held(values, behind):
+    count = len(values)
+    return pl.pallas_call(
+        lambda *refs: None,
+        out_shape=tuple(array(value.shape, value.dtype) for value in values),
+        in_specs=[pl.BlockSpec(memory_space=pl.ANY)] * (count + len(behind)),
+        out_specs=tuple(pl.BlockSpec(memory_space=pl.ANY) for _ in values),
+        input_output_aliases={place: place for place in range(count)},
+        cost_estimate=pl.CostEstimate(flops=0, bytes_accessed=0, transcendentals=0),
+    )(*values, *behind)
+
+
 def gather_halves(first, second):
     return swap(second, 4), swap(first, 2)
 
@@ -379,6 +396,29 @@
         behind,
     )
     return own, swap(beside_first, 4), beside_second, across_first, swap(across_second, 2)
+
+
+def scatter_all(pieces, near_three, near_one, far_three, far_one, behind=()):
+    size = sum(piece.size for piece in pieces)
+    half = size // 2
+    to_x, to_y, own, beside_first, beside_second, across_first, across_second = local_call(
+        functools.partial(sum_all_kernel, size),
+        (
+            array((near_one.shape[0] - half, LANES), jnp.bfloat16),
+            array((half, LANES), jnp.bfloat16),
+            array((size, LANES), jnp.bfloat16),
+            *(array((half, LANES), jnp.bfloat16),) * 4,
+        ),
+        (near_three, near_one, far_three, far_one),
+        (),
+        behind,
+    )
+    over_x, over_y = swap(to_x, 4), swap(to_y, 2)
+    return (
+        over_x,
+        over_y,
+        (own, swap(beside_first, 4), beside_second, across_first, swap(across_second, 2)),
+    )
 
 
 def scatter_passed(pieces, threes, over_x, over_y, near_one, far_one, behind=()):
@@ -927,7 +967,9 @@
     attention_near = gather_wholes(
         *gather_own(attention_pieces, attention_parts, 1, (ffn_parts[1],))
     )
-    attention_blocks = gather_cores(attention_near)
+    own, beside, across, diagonal = attention_near
+    own, beside = held((own, beside), (across, *ffn_parts[2:]))
+    attention_blocks = gather_cores((own, beside, across, diagonal))
     ffn_own = gather_own(ffn_pieces, ffn_parts, 2, attention_near[1:])
     ffn_passed = gather_halves(*ffn_own)
     gain_parts = []
@@ -965,9 +1007,6 @@
         (tokens, gain_input, gain_query, gain_key, cosine, sine, order, *attention_blocks),
     )
     key_values = [key_value] + [swap(key_value, step) for step in range(1, group_size)]
-    ffn_weights = gather_cores(
-        gather_rest(*ffn_own, *ffn_passed, (key_value,), key_values[1:])
-    )
     probs, attended, attn_out, middle, out_weight = local_call(
         functools.partial(attend_kernel, attention_pieces),
         (
@@ -978,7 +1017,10 @@
             array((width, D), jnp.bfloat16),
         ),
         (tokens, gain_attn, allowed, query_rot, *attention_blocks, *key_values),
-    )
+        (),
+        ffn_passed,
+    )
+    ffn_weights = gather_cores(gather_rest(*ffn_own, *ffn_passed, (key_value,), (middle,)))
     outputs, grad_middle, grad_gain_ffin, grad_gain_ffout, grads_ffn = ffn_blocks(
         pieces, middle, cotangent, gain_ffin, gain_ffout, order, ffn_weights
     )
@@ -1052,17 +1094,17 @@
         (),
         (sent, threes[1]),
     )
-    grads_ffn, sent, arrived = scatter_high(ffn_pieces, ffn_terms, (grad_inputs,))
     near_three, near_one, far_three, far_one = local_call(
         functools.partial(split_kernel, attention_pieces),
         grad_arrays(attention_pieces, GAIN_ROWS),
         (grad_query_weight, grad_key_weight, grad_out_weight, grad_gains),
-        (),
-        (sent,),
-    )
+    )
+    far_three, far_one = held((far_three, far_one), ffn_terms[2:4])
+    grads_ffn, sent, arrived = scatter_high(ffn_pieces, ffn_terms, (near_one,))
     far_three, far_one = scatter_cores(far_three, far_one)
-    over_x, over_y, sent = scatter_one(attention_pieces, near_one, far_one)
-    threes = scatter_three(attention_pieces, near_three, far_three, (sent,))
+    over_x, over_y, threes = scatter_all(
+        attention_pieces, near_three, near_one, far_three, far_one, (sent,)
+    )
     terms, _ = scatter_passed(
         attention_pieces, threes, over_x, over_y, near_one, far_one, (arrived[0],)
     )

time: 224 us -> 225 us (level)
  waiting for transfers between devices: 67.9 us -> 76.3 us
  starting transfers between devices: 53.4 us -> 48.4 us
    ppermute x53, waiting for transfers between devices: 67.9 us -> 76.3 us  [swap(): lax.ppermute(value, ALL_AXES, [(source, source ^ mask) for source in rang...]
    ppermute x53, starting transfers between devices: 53.4 us -> 48.4 us  [swap(): lax.ppermute(value, ALL_AXES, [(source, source ^ mask) for source in rang...]
    pallas_call x19 -> x18, Pallas kernels: 76.5 us -> 74.8 us  [local_call(): pl.pallas_call(body, out_shape=outs, in_specs=specs, out_specs=tuple((pl....]
    unnamed x132 -> x144, local copies, waits for them, and re-layouts: 12.7 us -> 12.5 us
  transfers between devices with their start and end apart: 53 -> 53, of which waited for: 19 -> 24; matrix products, arithmetic and copies ran while one was open for 4% -> 4% of each run, Pallas kernels for 23% -> 26%
where the time goes in v11:
time: 225 us
  waiting for transfers between devices  76.3 us (34%)
  Pallas kernels  74.8 us (33%)
  starting transfers between devices  48.4 us (22%)
  local copies, waits for them, and re-layouts  15.8 us (7%)
  other arithmetic  8.35 us (4%)
    ppermute x53, waiting for transfers between devices, swap(): lax.ppermute(value, ALL_AXES, [(source, source ^ mask) for source in rang...  76.3 us
    pallas_call x18, Pallas kernels, local_call(): pl.pallas_call(body, out_shape=outs, in_specs=specs, out_specs=tuple((pl....  74.8 us
    ppermute x53, starting transfers between devices, swap(): lax.ppermute(value, ALL_AXES, [(source, source ^ mask) for source in rang...  48.4 us
    unnamed x144, local copies, waits for them, and re-layouts  12.5 us
  transfers between devices with their start and end apart: 53, of which 24 were waited for; matrix products, arithmetic and copies ran while one was open for 4% of the time, Pallas kernels for 26%

profile of v11, /device:TPU:0, one launch (start us, length us, event | category | flops | bytes accessed | tf_op | source)
XLA Modules:
  0.0 224.8 jit_solution(5455207411582719306)
XLA Ops:
  1.8 5.1 %collective-permute-start.2 = (bf16[400,128]{1,0:T(8,128)(2,1)S(1)}, bf16[400,128]{1,0:T(8,128)(2,1)S(1)}, u32[]{:S(2)}, u32[]{:S(2)}) collective-permute-start(bf16[400,128]{1,0:T(8,128)(2,1)S(1)} %slice.65.refs_1_), channel_id=1, source_target_pairs={{0,24},{1,25},{2,26},{3,27},{4,28},{5,29},{6,30},{7,31},{8,16},{9,... | collective-permute-start | bytes 307208 | tf_op jit(solution)/shard_map/ppermute | solution.py:127
  7.6 3.8 %collective-permute-start.7 = (bf16[960,128]{1,0:T(8,128)(2,1)S(1)}, bf16[960,128]{1,0:T(8,128)(2,1)S(1)}, u32[]{:S(2)}, u32[]{:S(2)}) collective-permute-start(bf16[960,128]{1,0:T(8,128)(2,1)S(1)} %slice.66.refs_1_), channel_id=1, source_target_pairs={{0,24},{1,25},{2,26},{3,27},{4,28},{5,29},{6,30},{7,31},{8,16},{9,... | collective-permute-start | bytes 737288 | tf_op jit(solution)/shard_map/ppermute | solution.py:127
  12.3 4.1 %collective-permute-start.6 = (bf16[960,128]{1,0:T(8,128)(2,1)S(1)}, bf16[960,128]{1,0:T(8,128)(2,1)S(1)}, u32[]{:S(2)}, u32[]{:S(2)}) collective-permute-start(bf16[960,128]{1,0:T(8,128)(2,1)S(1)} %slice.66.refs_1_), channel_id=1, source_target_pairs={{0,16},{1,17},{2,18},{3,19},{4,20},{5,21},{6,22},{7,23},{8,24},{9,... | collective-permute-start | bytes 737288 | tf_op jit(solution)/shard_map/ppermute | solution.py:127
  16.4 5.4 %collective-permute-done.1.refs_3_ = bf16[400,128]{1,0:T(8,128)(2,1)S(1)} collective-permute-done((bf16[400,128]{1,0:T(8,128)(2,1)S(1)}, bf16[400,128]{1,0:T(8,128)(2,1)S(1)}, u32[]{:S(2)}, u32[]{:S(2)}) %collective-permute-start.1) | collective-permute-done | bytes 102432 | tf_op jit(solution)/shard_map/ppermute | solution.py:127
  21.8 3.5 %collective-permute-done.3.refs_5_.refs_2_ = bf16[960,128]{1,0:T(8,128)(2,1)S(1)} collective-permute-done((bf16[960,128]{1,0:T(8,128)(2,1)S(1)}, bf16[960,128]{1,0:T(8,128)(2,1)S(1)}, u32[]{:S(2)}, u32[]{:S(2)}) %collective-permute-start.3) | collective-permute-done | bytes 245792 | tf_op jit(solution)/shard_map/ppermute | solution.py:127
  31.9 6.9 %collective-permute-done.5.refs_2_.refs_10_.refs_6_.refs_7_.refs_9_.refs_20_ = bf16[1600,128]{1,0:T(8,128)(2,1)S(1)} collective-permute-done((bf16[1600,128]{1,0:T(8,128)(2,1)}, bf16[1600,128]{1,0:T(8,128)(2,1)S(1)}, u32[]{:S(2)}, u32[]{:S(2)}) %collective-permute-start.5) | collective-permute-done | bytes 409632 | tf_op jit(solution)/shard_map/ppermute | solution.py:127
  42.2 7.6 %collective-permute-done.8.refs_11_.refs_7_.refs_8_.refs_10_.refs_21_ = bf16[1600,128]{1,0:T(8,128)(2,1)S(1)} collective-permute-done((bf16[1600,128]{1,0:T(8,128)(2,1)S(1)}, bf16[1600,128]{1,0:T(8,128)(2,1)S(1)}, u32[]{:S(2)}, u32[]{:S(2)}) %collective-permute-start.8) | collective-permute-done | bytes 409632 | tf_op jit(solution)/shard_map/ppermute | solution.py:127
  50.6 2.9 %shard_map.155 = (bf16[1920,128]{1,0:T(8,128)(2,1)}, bf16[1920,128]{1,0:T(8,128)(2,1)}) custom-call(s32[1]{0:T(128)} %bitcast.refs_0_, bf16[960,128]{1,0:T(8,128)(2,1)} %copy-done.27, bf16[960,128]{1,0:T(8,128)(2,1)} %copy-done.29, bf16[960,128]{1,0:T(8,128)(2,1)} %copy-done.31, bf16[960,128]{1,0:T(8,128)(2,1)} %copy-done.28, bf16[1600,128]{1,0:T(8,128)(2,1)} %copy-done.1, ...), custom_call_target="tpu_custom_call" | custom-call | tf_op jit(solution)/shard_map/pallas_call | solution.py:139
  62.4 3.9 %shard_map.154 = (bf16[128,640]{1,0:T(8,128)(2,1)}, f32[128,1024]{1,0:T(8,128)}, f32[128,256]{1,0:T(8,128)}, bf16[128,1024]{1,0:T(8,128)(2,1)}, bf16[128,512]{1,0:T(8,128)(2,1)}) custom-call(s32[1]{0:T(128)} %bitcast.refs_0_, bf16[128,640]{1,0:T(8,128)(2,1)} %refs_1_.5, f32[1,640]{1,0:T(1,128)} %broadcast_in_dim.30.refs_2_, f32[1,256]{1,0:T(1,128)} %bitcast.29, ...), custom_call_target="tpu_custom_call" | custom-call | tf_op jit(solution)/shard_map/pallas_call | solution.py:139
  66.4 2.7 %collective-permute-done.19.refs_11_ = bf16[1920,128]{1,0:T(8,128)(2,1)S(1)} collective-permute-done((bf16[1920,128]{1,0:T(8,128)(2,1)S(1)}, bf16[1920,128]{1,0:T(8,128)(2,1)S(1)}, u32[]{:S(2)}, u32[]{:S(2)}) %collective-permute-start.19) | collective-permute-done | bytes 491552 | tf_op jit(solution)/shard_map/ppermute | solution.py:127
  72.3 7.3 %collective-permute-done.17.refs_18_.refs_10_ = bf16[1920,128]{1,0:T(8,128)(2,1)S(1)} collective-permute-done((bf16[1920,128]{1,0:T(8,128)(2,1)S(1)}, bf16[1920,128]{1,0:T(8,128)(2,1)S(1)}, u32[]{:S(2)}, u32[]{:S(2)}) %collective-permute-start.17) | collective-permute-done | bytes 491552 | tf_op jit(solution)/shard_map/ppermute | solution.py:127
  86.4 5.7 %shard_map.156 = (f32[128,2048]{1,0:T(8,128)}, bf16[128,1024]{1,0:T(8,128)(2,1)}, f32[128,640]{1,0:T(8,128)}, f32[128,640]{1,0:T(8,128)}, bf16[1024,640]{1,0:T(8,128)(2,1)}) custom-call(s32[1]{0:T(128)} %bitcast.refs_0_, bf16[128,640]{1,0:T(8,128)(2,1)} %refs_1_.5, f32[1,640]{1,0:T(1,128)} %broadcast_in_dim.14.refs_2_.refs_3_, f32[128,512]{1,0:T(8,128)} %fusion.4.refs_3_, ...), custom_call_target="tpu_custom_call" | custom-call | tf_op jit(solution)/shard_map/pallas_call | solution.py:139
  96.4 9.7 %collective-permute-done.20.refs_12_ = bf16[1920,128]{1,0:T(8,128)(2,1)S(1)} collective-permute-done((bf16[1920,128]{1,0:T(8,128)(2,1)S(1)}, bf16[1920,128]{1,0:T(8,128)(2,1)S(1)}, u32[]{:S(2)}, u32[]{:S(2)}) %collective-permute-start.20) | collective-permute-done | bytes 491552 | tf_op jit(solution)/shard_map/ppermute | solution.py:127
  110.9 14.9 %shard_map.159 = (bf16[128,640]{1,0:T(8,128)(2,1)}, f32[128,640]{1,0:T(8,128)}, f32[1,640]{1,0:T(1,128)}, f32[1,640]{1,0:T(1,128)}, bf16[11520,128]{1,0:T(8,128)...) custom-call(s32[1]{0:T(128)} %bitcast.refs_0_, ...), custom_call_target="tpu_custom_call" | custom-call | tf_op jit(solution)/shard_map/pallas_call | solution.py:139
  126.4 5.8 %shard_map.160 = (bf16[1024,640]{1,0:T(8,128)(2,1)}, f32[128,1024]{1,0:T(8,128)}, f32[1,640]{1,0:T(1,128)}, f32[128,512]{1,0:T(8,128)}, f32[128,512]{1,0:T(8,128)}, /*index=5*/bf16[256,512]{1,0:T(8,128)(2,1)}) custom-call(s32[1]{0:T(128)} %bitcast.refs_0_, f32[128,640]{1,0:T(8,128)} %get-tuple-element.87.refs_1_.refs_10_, ...), custom_call_target="tpu_custom_call" | custom-call | tf_op jit(solution)/shard_map/pallas_call | solution.py:139
  133.9 2.6 %shard_map.161 = (bf16[1920,128]{1,0:T(8,128)(2,1)}, bf16[1920,128]{1,0:T(8,128)(2,1)}) custom-call(s32[1]{0:T(128)} %bitcast.refs_0_, bf16[3840,128]{1,0:T(8,128)(2,1)} %get-tuple-element.97.refs_1_.refs_5_, bf16[3840,128]{1,0:T(8,128)(2,1)} %copy-done.10, f32[128,1024]{1,0:T(8,128)} %get-tuple-element.92.refs_3_.refs_6_), custom_call_target="tpu_custom_call" | custom-call | tf_op jit(solution)/shard_map/pallas_call | solution.py:139
  141.1 4.6 %shard_map.162 = (bf16[3840,128]{1,0:T(8,128)(2,1)}, bf16[1920,128]{1,0:T(8,128)(2,1)}, bf16[1920,128]{1,0:T(8,128)(2,1)}, bf16[1920,128]{1,0:T(8,128)(2,1)}, bf16[2432,128]{1,0:T(8,128)(2,1)}) custom-call(s32[1]{0:T(128)} %bitcast.refs_0_, bf16[11520,128]{1,0:T(8,128)(2,1)} %get-tuple-element.93.refs_1_, bf16[11520,128]{1,0:T(8,128)(2,1)} %copy-done.11, ...), custom_call_target="tpu_custom_call" | custom-call | tf_op jit(solution)/shard_map/pallas_call | solution.py:139
  148.3 4.5 %shard_map.163 = (bf16[640,1024]{1,0:T(8,128)(2,1)}, f32[128,640]{1,0:T(8,128)}, f32[1,256]{1,0:T(1,128)}) custom-call(s32[1]{0:T(128)} %bitcast.refs_0_, f32[1,256]{1,0:T(1,128)} %bitcast.30, f32[128,128]{1,0:T(8,128)} %get-tuple-element.161.refs_5_.refs_2_.refs_4_, f32[128,128]{1,0:T(8,128)} %get-tuple-element.160.refs_6_.refs_3_.refs_5_, ...), custom_call_target="tpu_custom_call" | custom-call | tf_op jit(solution)/shard_map/pallas_call | solution.py:139
  153.8 3.2 %shard_map.164 = (bf16[1920,128]{1,0:T(8,128)(2,1)}, bf16[1920,128]{1,0:T(8,128)(2,1)}, f32[8,128]{1,0:T(8,128)}) custom-call(s32[1]{0:T(128)} %bitcast.refs_0_, bf16[1920,128]{1,0:T(8,128)(2,1)} %get-tuple-element.108.refs_1_, bf16[1920,128]{1,0:T(8,128)(2,1)} %get-tuple-element.109.refs_2_, bf16[1920,128]{1,0:T(8,128)(2,1)} %copy-done.49, ...), custom_call_target="tpu_custom_call" | custom-call | tf_op jit(solution)/shard_map/pallas_call | solution.py:139
  158.3 3.1 %collective-permute-done.36.refs_27_.refs_2_ = bf16[1920,128]{1,0:T(8,128)(2,1)S(1)} collective-permute-done((bf16[1920,128]{1,0:T(8,128)(2,1)}, bf16[1920,128]{1,0:T(8,128)(2,1)S(1)}, u32[]{:S(2)}, u32[]{:S(2)}) %collective-permute-start.36) | collective-permute-done | bytes 491552 | tf_op jit(solution)/shard_map/ppermute | solution.py:127
  161.5 3.6 %collective-permute-done.33.refs_17_.refs_5_ = bf16[2432,128]{1,0:T(8,128)(2,1)S(1)} collective-permute-done((bf16[2432,128]{1,0:T(8,128)(2,1)}, bf16[2432,128]{1,0:T(8,128)(2,1)S(1)}, u32[]{:S(2)}, u32[]{:S(2)}) %collective-permute-start.33) | collective-permute-done | bytes 622624 | tf_op jit(solution)/shard_map/ppermute | solution.py:127
  165.8 4.7 %shard_map.165 = (bf16[640,512]{1,0:T(8,128)(2,1)}, bf16[128,640]{1,0:T(8,128)(2,1)}, f32[32,128]{1,0:T(8,128)}) custom-call(s32[1]{0:T(128)} %bitcast.refs_0_, bf16[128,640]{1,0:T(8,128)(2,1)} %refs_1_.5, f32[1,640]{1,0:T(1,128)} %broadcast_in_dim.30.refs_2_, f32[1,256]{1,0:T(1,128)} %bitcast.28, f32[128,128]{1,0:T(8,128)} %get-tuple-element.161.refs_5_.refs_2_.refs_4_, ...), custom_call_target="tpu_custom_call" | custom-call | tf_op jit(solution)/shard_map/pallas_call | solution.py:139
  170.5 4.2 %shard_map.166 = (bf16[4800,128]{1,0:T(8,128)(2,1)}, bf16[1632,128]{1,0:T(8,128)(2,1)}, bf16[4800,128]{1,0:T(8,128)(2,1)}, bf16[1632,128]{1,0:T(8,128)(2,1)}) custom-call(s32[1]{0:T(128)} %bitcast.refs_0_, bf16[640,1024]{1,0:T(8,128)(2,1)} %get-tuple-element.114.refs_1_, bf16[640,512]{1,0:T(8,128)(2,1)} %get-tuple-element.115.refs_2_, ...), custom_call_target="tpu_custom_call" | custom-call | tf_op jit(solution)/shard_map/pallas_call | solution.py:139
  176.2 4.1 %shard_map.168 = (f32[960,128]{1,0:T(8,128)}, bf16[960,128]{1,0:T(8,128)(2,1)}, bf16[960,128]{1,0:T(8,128)(2,1)}, bf16[960,128]{1,0:T(8,128)(2,1)}) custom-call(s32[1]{0:T(128)} %bitcast.refs_0_, bf16[3840,128]{1,0:T(8,128)(2,1)} %get-tuple-element.100.refs_15_.refs_1_, bf16[1920,128]{1,0:T(8,128)(2,1)} %copy-done.20, bf16[1920,128]{1,0:T(8,128)(2,1)} %copy-done.17, ...), custom_call_target="tpu_custom_call" | custom-call | tf_op jit(solution)/shard_map/pallas_call | solution.py:139
  181.4 2.8 %collective-permute-start.48 = (bf16[960,128]{1,0:T(8,128)(2,1)}, bf16[960,128]{1,0:T(8,128)(2,1)S(1)}, u32[]{:S(2)}, u32[]{:S(2)}) collective-permute-start(bf16[960,128]{1,0:T(8,128)(2,1)} %get-tuple-element.138), channel_id=1, source_target_pairs={{0,16},{1,17},{2,18},{3,19},{4,20},{5,21},{6,22},{7,23},{8,24},{9,... | collective-permute-start | bytes 737288 | tf_op jit(solution)/shard_map/ppermute | solution.py:127
  185.3 3.1 %shard_map.169 = (bf16[832,128]{1,0:T(8,128)(2,1)}, bf16[800,128]{1,0:T(8,128)(2,1)}, bf16[1600,128]{1,0:T(8,128)(2,1)}, bf16[800,128]{1,0:T(8,128)(2,1)}, bf16[...) custom-call(s32[1]{0:T(128)} %bitcast.refs_0_, ...), custom_call_target="tpu_custom_call" | custom-call | tf_op jit(solution)/shard_map/pallas_call | solution.py:139
  190.8 2.7 %collective-permute-done.44.refs_7_ = bf16[960,128]{1,0:T(8,128)(2,1)S(1)} collective-permute-done((bf16[960,128]{1,0:T(8,128)(2,1)}, bf16[960,128]{1,0:T(8,128)(2,1)S(1)}, u32[]{:S(2)}, u32[]{:S(2)}) %collective-permute-start.44) | collective-permute-done | bytes 245792 | tf_op jit(solution)/shard_map/ppermute | solution.py:127
  193.5 2.6 %collective-permute-done.43.refs_4_ = bf16[800,128]{1,0:T(8,128)(2,1)S(1)} collective-permute-done((bf16[800,128]{1,0:T(8,128)(2,1)}, bf16[800,128]{1,0:T(8,128)(2,1)S(1)}, u32[]{:S(2)}, u32[]{:S(2)}) %collective-permute-start.43) | collective-permute-done | bytes 204832 | tf_op jit(solution)/shard_map/ppermute | solution.py:127
  203.3 3.9 %collective-permute-done.41.refs_2_ = bf16[800,128]{1,0:T(8,128)(2,1)S(1)} collective-permute-done((bf16[800,128]{1,0:T(8,128)(2,1)S(1)}, bf16[800,128]{1,0:T(8,128)(2,1)S(1)}, u32[]{:S(2)}, u32[]{:S(2)}) %collective-permute-start.41) | collective-permute-done | bytes 204832 | tf_op jit(solution)/shard_map/ppermute | solution.py:127
  210.1 2.5 %shard_map.171 = (f32[432,128]{1,0:T(8,128)}, bf16[432,128]{1,0:T(8,128)(2,1)}, bf16[432,128]{1,0:T(8,128)(2,1)}, bf16[432,128]{1,0:T(8,128)(2,1)}) custom-call(s32[1]{0:T(128)} %bitcast.refs_0_, bf16[1600,128]{1,0:T(8,128)(2,1)} %get-tuple-element.127.refs_1_, bf16[800,128]{1,0:T(8,128)(2,1)} %copy-done.57, bf16[800,128]{1,0:T(8,128)(2,1)} %copy-done.59, ...), custom_call_target="tpu_custom_call" | custom-call | tf_op jit(solution)/shard_map/pallas_call | solution.py:139
  214.2 2.8 %collective-permute-start.52 = (bf16[432,128]{1,0:T(8,128)(2,1)}, bf16[432,128]{1,0:T(8,128)(2,1)S(1)}, u32[]{:S(2)}, u32[]{:S(2)}) collective-permute-start(bf16[432,128]{1,0:T(8,128)(2,1)} %get-tuple-element.143), channel_id=1, source_target_pairs={{0,24},{1,25},{2,26},{3,27},{4,28},{5,29},{6,30},{7,31},{8,16},{9,... | collective-permute-start | bytes 331784 | tf_op jit(solution)/shard_map/ppermute | solution.py:127
  219.0 3.4 %collective-permute-done.51 = bf16[432,128]{1,0:T(8,128)(2,1)S(1)} collective-permute-done((bf16[432,128]{1,0:T(8,128)(2,1)}, bf16[432,128]{1,0:T(8,128)(2,1)S(1)}, u32[]{:S(2)}, u32[]{:S(2)}) %collective-permute-start.51) | collective-permute-done | bytes 110624 | tf_op jit(solution)/shard_map/ppermute | solution.py:127
  (271 shorter events, 76.2 us)
Async XLA Ops:
  6.9 14.8 %collective-permute-start.1 = (bf16[400,128]{1,0:T(8,128)(2,1)S(1)}, bf16[400,128]{1,0:T(8,128)(2,1)S(1)}, u32[]{:S(2)}, u32[]{:S(2)}) collective-permute-start(bf16[400,128]{1,0:T(8,128)(2,1)S(1)} %slice.65.refs_1_), channel_id=1, source_target_pairs={{0,16},{1,17},{2,18},{3,19},{4,20},{5,21},{6,22},{7,23},{8,24},{9,... | collective-permute-start | bytes 307208 | tf_op jit(solution)/shard_map/ppermute | solution.py:127
  7.0 14.8 %collective-permute-start = (bf16[400,128]{1,0:T(8,128)(2,1)S(1)}, bf16[400,128]{1,0:T(8,128)(2,1)S(1)}, u32[]{:S(2)}, u32[]{:S(2)}) collective-permute-start(bf16[400,128]{1,0:T(8,128)(2,1)S(1)} %slice.65.refs_1_), channel_id=1, source_target_pairs={{0,8},{1,9},{2,10},{3,11},{4,12},{5,13},{6,14},{7,15},{8,0},{9,1},... | collective-permute-start | bytes 307208 | tf_op jit(solution)/shard_map/ppermute | solution.py:127
  7.6 32.8 %collective-permute-start.7 = (bf16[960,128]{1,0:T(8,128)(2,1)S(1)}, bf16[960,128]{1,0:T(8,128)(2,1)S(1)}, u32[]{:S(2)}, u32[]{:S(2)}) collective-permute-start(bf16[960,128]{1,0:T(8,128)(2,1)S(1)} %slice.66.refs_1_), channel_id=1, source_target_pairs={{0,24},{1,25},{2,26},{3,27},{4,28},{5,29},{6,30},{7,31},{8,16},{9,... | collective-permute-start | bytes 737288 | tf_op jit(solution)/shard_map/ppermute | solution.py:127
  11.4 13.8 %collective-permute-start.3 = (bf16[960,128]{1,0:T(8,128)(2,1)S(1)}, bf16[960,128]{1,0:T(8,128)(2,1)S(1)}, u32[]{:S(2)}, u32[]{:S(2)}) collective-permute-start(bf16[960,128]{1,0:T(8,128)(2,1)S(1)} %slice.66.refs_1_), channel_id=1, source_target_pairs={{0,8},{1,9},{2,10},{3,11},{4,12},{5,13},{6,14},{7,15},{8,0},{9,1},... | collective-permute-start | bytes 737288 | tf_op jit(solution)/shard_map/ppermute | solution.py:127
  12.3 28.1 %collective-permute-start.6 = (bf16[960,128]{1,0:T(8,128)(2,1)S(1)}, bf16[960,128]{1,0:T(8,128)(2,1)S(1)}, u32[]{:S(2)}, u32[]{:S(2)}) collective-permute-start(bf16[960,128]{1,0:T(8,128)(2,1)S(1)} %slice.66.refs_1_), channel_id=1, source_target_pairs={{0,16},{1,17},{2,18},{3,19},{4,20},{5,21},{6,22},{7,23},{8,24},{9,... | collective-permute-start | bytes 737288 | tf_op jit(solution)/shard_map/ppermute | solution.py:127
  30.4 11.8 %collective-permute-start.4 = (bf16[1600,128]{1,0:T(8,128)(2,1)}, bf16[1600,128]{1,0:T(8,128)(2,1)S(1)}, u32[]{:S(2)}, u32[]{:S(2)}) collective-permute-start(bf16[1600,128]{1,0:T(8,128)(2,1)} %shard_map.152.refs_0_), channel_id=1, source_target_pairs={{0,4},{1,5},{2,6},{3,7},{4,0},{5,1},{6,2},{7,3},{8,12},{9,13},{10,... | collective-permute-start | bytes 1228808 | tf_op jit(solution)/shard_map/ppermute | solution.py:127
  40.3 16.7 %collective-permute-start.11 = (bf16[1600,128]{1,0:T(8,128)(2,1)S(1)}, bf16[1600,128]{1,0:T(8,128)(2,1)S(1)}, u32[]{:S(2)}, u32[]{:S(2)}) collective-permute-start(bf16[1600,128]{1,0:T(8,128)(2,1)S(1)} %collective-permute-done.5.refs_2_.refs_10_.refs_6_.refs_7_.refs_9_.refs_20_), channel_id=1, source_target_pairs={{0,1},{1,0},{2,3},{3,2},{4,5},{5,4},{6,7},{7,6},{8,9},{9,8},{10,11... | collective-permute-start | bytes 1228808 | tf_op jit(solution)/shard_map/ppermute | solution.py:127
  55.0 14.0 %collective-permute-start.19 = (bf16[1920,128]{1,0:T(8,128)(2,1)S(1)}, bf16[1920,128]{1,0:T(8,128)(2,1)S(1)}, u32[]{:S(2)}, u32[]{:S(2)}) collective-permute-start(bf16[1920,128]{1,0:T(8,128)(2,1)S(1)} %copy-done.38), channel_id=1, source_target_pairs={{0,2},{1,3},{2,0},{3,1},{4,6},{5,7},{6,4},{7,5},{8,10},{9,11},{10,... | collective-permute-start | bytes 1474568 | tf_op jit(solution)/shard_map/ppermute | solution.py:127
  55.5 14.0 %collective-permute-start.16 = (bf16[1920,128]{1,0:T(8,128)(2,1)S(1)}, bf16[1920,128]{1,0:T(8,128)(2,1)S(1)}, u32[]{:S(2)}, u32[]{:S(2)}) collective-permute-start(bf16[1920,128]{1,0:T(8,128)(2,1)S(1)} %copy-done.38), channel_id=1, source_target_pairs={{0,4},{1,5},{2,6},{3,7},{4,0},{5,1},{6,2},{7,3},{8,12},{9,13},{10,... | collective-permute-start | bytes 1474568 | tf_op jit(solution)/shard_map/ppermute | solution.py:127
  57.2 36.9 %collective-permute-start.23 = (bf16[1920,128]{1,0:T(8,128)(2,1)S(1)}, bf16[1920,128]{1,0:T(8,128)(2,1)S(1)}, u32[]{:S(2)}, u32[]{:S(2)}) collective-permute-start(bf16[1920,128]{1,0:T(8,128)(2,1)S(1)} %copy-done.38), channel_id=1, source_target_pairs={{0,1},{1,0},{2,3},{3,2},{4,5},{5,4},{6,7},{7,6},{8,9},{9,8},{10,11... | collective-permute-start | bytes 1474568 | tf_op jit(solution)/shard_map/ppermute | solution.py:127
  57.7 21.9 %collective-permute-start.17 = (bf16[1920,128]{1,0:T(8,128)(2,1)S(1)}, bf16[1920,128]{1,0:T(8,128)(2,1)S(1)}, u32[]{:S(2)}, u32[]{:S(2)}) collective-permute-start(bf16[1920,128]{1,0:T(8,128)(2,1)S(1)} %copy-done.18), channel_id=1, source_target_pairs={{0,2},{1,3},{2,0},{3,1},{4,6},{5,7},{6,4},{7,5},{8,10},{9,11},{10,... | collective-permute-start | bytes 1474568 | tf_op jit(solution)/shard_map/ppermute | solution.py:127
  66.3 15.3 %collective-permute-start.15 = (bf16[128,512]{1,0:T(8,128)(2,1)}, bf16[128,512]{1,0:T(8,128)(2,1)S(1)}, u32[]{:S(2)}, u32[]{:S(2)}) collective-permute-start(bf16[128,512]{1,0:T(8,128)(2,1)} %get-tuple-element.79.refs_13_.refs_2_.refs_8_), channel_id=1, source_target_pairs={{0,3},{1,2},{2,1},{3,0},{4,7},{5,6},{6,5},{7,4},{8,11},{9,10},{10,... | collective-permute-start | bytes 393224 | tf_op jit(solution)/shard_map/ppermute | solution.py:127
  69.1 15.8 %collective-permute-start.14 = (bf16[128,512]{1,0:T(8,128)(2,1)}, bf16[128,512]{1,0:T(8,128)(2,1)S(1)}, u32[]{:S(2)}, u32[]{:S(2)}) collective-permute-start(bf16[128,512]{1,0:T(8,128)(2,1)} %get-tuple-element.79.refs_13_.refs_2_.refs_8_), channel_id=1, source_target_pairs={{0,2},{1,3},{2,0},{3,1},{4,6},{5,7},{6,4},{7,5},{8,10},{9,11},{10,... | collective-permute-start | bytes 393224 | tf_op jit(solution)/shard_map/ppermute | solution.py:127
  69.6 15.3 %collective-permute-start.13 = (bf16[128,512]{1,0:T(8,128)(2,1)}, bf16[128,512]{1,0:T(8,128)(2,1)S(1)}, u32[]{:S(2)}, u32[]{:S(2)}) collective-permute-start(bf16[128,512]{1,0:T(8,128)(2,1)} %get-tuple-element.79.refs_13_.refs_2_.refs_8_), channel_id=1, source_target_pairs={{0,1},{1,0},{2,3},{3,2},{4,5},{5,4},{6,7},{7,6},{8,9},{9,8},{10,11... | collective-permute-start | bytes 393224 | tf_op jit(solution)/shard_map/ppermute | solution.py:127
  79.6 15.0 %collective-permute-start.22 = (bf16[1920,128]{1,0:T(8,128)(2,1)S(1)}, bf16[1920,128]{1,0:T(8,128)(2,1)S(1)}, u32[]{:S(2)}, u32[]{:S(2)}) collective-permute-start(bf16[1920,128]{1,0:T(8,128)(2,1)S(1)} %copy-done.19), channel_id=1, source_target_pairs={{0,1},{1,0},{2,3},{3,2},{4,5},{5,4},{6,7},{7,6},{8,9},{9,8},{10,11... | collective-permute-start | bytes 1474568 | tf_op jit(solution)/shard_map/ppermute | solution.py:127
  81.6 14.2 %collective-permute-start.18 = (bf16[1920,128]{1,0:T(8,128)(2,1)}, bf16[1920,128]{1,0:T(8,128)(2,1)S(1)}, u32[]{:S(2)}, u32[]{:S(2)}) collective-permute-start(bf16[1920,128]{1,0:T(8,128)(2,1)} %shard_map.157), channel_id=1, source_target_pairs={{0,4},{1,5},{2,6},{3,7},{4,0},{5,1},{6,2},{7,3},{8,12},{9,13},{10,... | collective-permute-start | bytes 1474568 | tf_op jit(solution)/shard_map/ppermute | solution.py:127
  84.8 11.0 %collective-permute-start.27 = (bf16[1920,128]{1,0:T(8,128)(2,1)S(1)}, bf16[1920,128]{1,0:T(8,128)(2,1)S(1)}, u32[]{:S(2)}, u32[]{:S(2)}) collective-permute-start(bf16[1920,128]{1,0:T(8,128)(2,1)S(1)} %collective-permute-done.19.refs_11_), channel_id=1, source_target_pairs={{0,1},{1,0},{2,3},{3,2},{4,5},{5,4},{6,7},{7,6},{8,9},{9,8},{10,11... | collective-permute-start | bytes 1474568 | tf_op jit(solution)/shard_map/ppermute | solution.py:127
  84.9 21.2 %collective-permute-start.20 = (bf16[1920,128]{1,0:T(8,128)(2,1)S(1)}, bf16[1920,128]{1,0:T(8,128)(2,1)S(1)}, u32[]{:S(2)}, u32[]{:S(2)}) collective-permute-start(bf16[1920,128]{1,0:T(8,128)(2,1)S(1)} %collective-permute-done.17.refs_18_.refs_10_), channel_id=1, source_target_pairs={{0,4},{1,5},{2,6},{3,7},{4,0},{5,1},{6,2},{7,3},{8,12},{9,13},{10,... | collective-permute-start | bytes 1474568 | tf_op jit(solution)/shard_map/ppermute | solution.py:127
  94.1 13.5 %collective-permute-start.21 = (bf16[1920,128]{1,0:T(8,128)(2,1)}, bf16[1920,128]{1,0:T(8,128)(2,1)S(1)}, u32[]{:S(2)}, u32[]{:S(2)}) collective-permute-start(bf16[1920,128]{1,0:T(8,128)(2,1)} %shard_map.158), channel_id=1, source_target_pairs={{0,2},{1,3},{2,0},{3,1},{4,6},{5,7},{6,4},{7,5},{8,10},{9,11},{10,... | collective-permute-start | bytes 1474568 | tf_op jit(solution)/shard_map/ppermute | solution.py:127
  94.6 14.2 %collective-permute-start.25 = (bf16[1920,128]{1,0:T(8,128)(2,1)S(1)}, bf16[1920,128]{1,0:T(8,128)(2,1)S(1)}, u32[]{:S(2)}, u32[]{:S(2)}) collective-permute-start(bf16[1920,128]{1,0:T(8,128)(2,1)S(1)} %copy-done.9), channel_id=1, source_target_pairs={{0,1},{1,0},{2,3},{3,2},{4,5},{5,4},{6,7},{7,6},{8,9},{9,8},{10,11... | collective-permute-start | bytes 1474568 | tf_op jit(solution)/shard_map/ppermute | solution.py:127
  95.9 13.0 %collective-permute-start.26 = (bf16[1920,128]{1,0:T(8,128)(2,1)S(1)}, bf16[1920,128]{1,0:T(8,128)(2,1)S(1)}, u32[]{:S(2)}, u32[]{:S(2)}) collective-permute-start(bf16[1920,128]{1,0:T(8,128)(2,1)S(1)} %copy-done.23), channel_id=1, source_target_pairs={{0,1},{1,0},{2,3},{3,2},{4,5},{5,4},{6,7},{7,6},{8,9},{9,8},{10,11... | collective-permute-start | bytes 1474568 | tf_op jit(solution)/shard_map/ppermute | solution.py:127
  95.9 13.0 %collective-permute-start.24 = (bf16[1920,128]{1,0:T(8,128)(2,1)S(1)}, bf16[1920,128]{1,0:T(8,128)(2,1)S(1)}, u32[]{:S(2)}, u32[]{:S(2)}) collective-permute-start(bf16[1920,128]{1,0:T(8,128)(2,1)S(1)} %collective-permute-done.18.refs_8_), channel_id=1, source_target_pairs={{0,1},{1,0},{2,3},{3,2},{4,5},{5,4},{6,7},{7,6},{8,9},{9,8},{10,11... | collective-permute-start | bytes 1474568 | tf_op jit(solution)/shard_map/ppermute | solution.py:127
  125.8 13.7 %collective-permute-start.30 = (bf16[11520,128]{1,0:T(8,128)(2,1)}, bf16[11520,128]{1,0:T(8,128)(2,1)S(1)}, u32[]{:S(2)}, u32[]{:S(2)}) collective-permute-start(bf16[11520,128]{1,0:T(8,128)(2,1)} %get-tuple-element.94), channel_id=1, source_target_pairs={{0,1},{1,0},{2,3},{3,2},{4,5},{5,4},{6,7},{7,6},{8,9},{9,8},{10,11... | collective-permute-start | bytes 8847368 | tf_op jit(solution)/shard_map/ppermute | solution.py:127
  136.5 16.3 %collective-permute-start.34 = (bf16[1920,128]{1,0:T(8,128)(2,1)}, bf16[1920,128]{1,0:T(8,128)(2,1)S(1)}, u32[]{:S(2)}, u32[]{:S(2)}) collective-permute-start(bf16[1920,128]{1,0:T(8,128)(2,1)} %get-tuple-element.110), channel_id=1, source_target_pairs={{0,4},{1,5},{2,6},{3,7},{4,0},{5,1},{6,2},{7,3},{8,12},{9,13},{10,... | collective-permute-start | bytes 1474568 | tf_op jit(solution)/shard_map/ppermute | solution.py:127
  137.4 15.4 %collective-permute-start.35 = (bf16[1920,128]{1,0:T(8,128)(2,1)}, bf16[1920,128]{1,0:T(8,128)(2,1)S(1)}, u32[]{:S(2)}, u32[]{:S(2)}) collective-permute-start(bf16[1920,128]{1,0:T(8,128)(2,1)} %get-tuple-element.99.refs_5_), channel_id=1, source_target_pairs={{0,2},{1,3},{2,0},{3,1},{4,6},{5,7},{6,4},{7,5},{8,10},{9,11},{10,... | collective-permute-start | bytes 1474568 | tf_op jit(solution)/shard_map/ppermute | solution.py:127
  145.6 19.4 %collective-permute-start.33 = (bf16[2432,128]{1,0:T(8,128)(2,1)}, bf16[2432,128]{1,0:T(8,128)(2,1)S(1)}, u32[]{:S(2)}, u32[]{:S(2)}) collective-permute-start(bf16[2432,128]{1,0:T(8,128)(2,1)} %get-tuple-element.107), channel_id=1, source_target_pairs={{0,2},{1,3},{2,0},{3,1},{4,6},{5,7},{6,4},{7,5},{8,10},{9,11},{10,... | collective-permute-start | bytes 1867784 | tf_op jit(solution)/shard_map/ppermute | solution.py:127
  147.1 14.3 %collective-permute-start.36 = (bf16[1920,128]{1,0:T(8,128)(2,1)}, bf16[1920,128]{1,0:T(8,128)(2,1)S(1)}, u32[]{:S(2)}, u32[]{:S(2)}) collective-permute-start(bf16[1920,128]{1,0:T(8,128)(2,1)} %get-tuple-element.112), channel_id=1, source_target_pairs={{0,4},{1,5},{2,6},{3,7},{4,0},{5,1},{6,2},{7,3},{8,12},{9,13},{10,... | collective-permute-start | bytes 1474568 | tf_op jit(solution)/shard_map/ppermute | solution.py:127
  156.9 17.8 %collective-permute-start.38 = (bf16[1920,128]{1,0:T(8,128)(2,1)}, bf16[1920,128]{1,0:T(8,128)(2,1)S(1)}, u32[]{:S(2)}, u32[]{:S(2)}) collective-permute-start(bf16[1920,128]{1,0:T(8,128)(2,1)} %get-tuple-element.122), channel_id=1, source_target_pairs={{0,2},{1,3},{2,0},{3,1},{4,6},{5,7},{6,4},{7,5},{8,10},{9,11},{10,... | collective-permute-start | bytes 1474568 | tf_op jit(solution)/shard_map/ppermute | solution.py:127
  157.4 17.3 %collective-permute-start.37 = (bf16[1920,128]{1,0:T(8,128)(2,1)}, bf16[1920,128]{1,0:T(8,128)(2,1)S(1)}, u32[]{:S(2)}, u32[]{:S(2)}) collective-permute-start(bf16[1920,128]{1,0:T(8,128)(2,1)} %get-tuple-element.111.refs_26_), channel_id=1, source_target_pairs={{0,4},{1,5},{2,6},{3,7},{4,0},{5,1},{6,2},{7,3},{8,12},{9,13},{10,... | collective-permute-start | bytes 1474568 | tf_op jit(solution)/shard_map/ppermute | solution.py:127
  180.4 13.1 %collective-permute-start.44 = (bf16[960,128]{1,0:T(8,128)(2,1)}, bf16[960,128]{1,0:T(8,128)(2,1)S(1)}, u32[]{:S(2)}, u32[]{:S(2)}) collective-permute-start(bf16[960,128]{1,0:T(8,128)(2,1)} %get-tuple-element.133), channel_id=1, source_target_pairs={{0,8},{1,9},{2,10},{3,11},{4,12},{5,13},{6,14},{7,15},{8,0},{9,1},... | collective-permute-start | bytes 737288 | tf_op jit(solution)/shard_map/ppermute | solution.py:127
  181.4 20.7 %collective-permute-start.48 = (bf16[960,128]{1,0:T(8,128)(2,1)}, bf16[960,128]{1,0:T(8,128)(2,1)S(1)}, u32[]{:S(2)}, u32[]{:S(2)}) collective-permute-start(bf16[960,128]{1,0:T(8,128)(2,1)} %get-tuple-element.138), channel_id=1, source_target_pairs={{0,16},{1,17},{2,18},{3,19},{4,20},{5,21},{6,22},{7,23},{8,24},{9,... | collective-permute-start | bytes 737288 | tf_op jit(solution)/shard_map/ppermute | solution.py:127
  190.5 12.8 %collective-permute-start.49 = (bf16[960,128]{1,0:T(8,128)(2,1)S(1)}, bf16[960,128]{1,0:T(8,128)(2,1)S(1)}, u32[]{:S(2)}, u32[]{:S(2)}) collective-permute-start(bf16[960,128]{1,0:T(8,128)(2,1)S(1)} %copy-done.69), channel_id=1, source_target_pairs={{0,24},{1,25},{2,26},{3,27},{4,28},{5,29},{6,30},{7,31},{8,16},{9,... | collective-permute-start | bytes 737288 | tf_op jit(solution)/shard_map/ppermute | solution.py:127
  (93 other events, 628.8 us)

commit v12 on v11

--- a/solution.py
+++ b/solution.py
@@ -339,17 +339,11 @@
     return swap(second, 4), swap(first, 2)
 
 
-def gather_rest(first, second, beside_second, across_first, behind, behind_last):
-    return (
-        first,
-        second,
-        swap(copied(first, behind), 4),
-        beside_second,
-        across_first,
-        swap(second, 2),
-        swap(across_first, 4),
-        swap(copied(beside_second, behind_last), 2),
-    )
+def gather_rest(first, second, beside_second, across_first, keys, behind):
+    beside_first, across_second = swap(copied(first, keys[:1]), 4), swap(second, 2)
+    over_x, over_y = swap(across_first, 4), swap(copied(beside_second, keys[1:]), 2)
+    diagonal = held((over_x, over_y), behind)
+    return first, second, beside_first, beside_second, across_first, across_second, *diagonal
 
 
 def gather_wholes(own):
@@ -967,9 +961,7 @@
     attention_near = gather_wholes(
         *gather_own(attention_pieces, attention_parts, 1, (ffn_parts[1],))
     )
-    own, beside, across, diagonal = attention_near
-    own, beside = held((own, beside), (across, *ffn_parts[2:]))
-    attention_blocks = gather_cores((own, beside, across, diagonal))
+    attention_blocks = gather_cores(attention_near)
     ffn_own = gather_own(ffn_pieces, ffn_parts, 2, attention_near[1:])
     ffn_passed = gather_halves(*ffn_own)
     gain_parts = []
@@ -1017,10 +1009,8 @@
             array((width, D), jnp.bfloat16),
         ),
         (tokens, gain_attn, allowed, query_rot, *attention_blocks, *key_values),
-        (),
-        ffn_passed,
-    )
-    ffn_weights = gather_cores(gather_rest(*ffn_own, *ffn_passed, (key_value,), (middle,)))
+    )
+    ffn_weights = gather_cores(gather_rest(*ffn_own, *ffn_passed, key_values, (middle,)))
     outputs, grad_middle, grad_gain_ffin, grad_gain_ffout, grads_ffn = ffn_blocks(
         pieces, middle, cotangent, gain_ffin, gain_ffout, order, ffn_weights
     )

time: 225 us -> 217 us (0.964)
  waiting for transfers between devices: 76.3 us -> 63.3 us
  starting transfers between devices: 48.4 us -> 51.7 us
    ppermute x53, waiting for transfers between devices: 76.3 us -> 63.3 us  [swap(): lax.ppermute(value, ALL_AXES, [(source, source ^ mask) for source in rang...]
    ppermute x53, starting transfers between devices: 48.4 us -> 51.7 us  [swap(): lax.ppermute(value, ALL_AXES, [(source, source ^ mask) for source in rang...]
    unnamed x144 -> x130, local copies, waits for them, and re-layouts: 12.5 us -> 13.7 us
  transfers between devices with their start and end apart: 53 -> 53, of which waited for: 24 -> 23; matrix products, arithmetic and copies ran while one was open for 4% -> 4% of each run, Pallas kernels for 26% -> 27%
where the time goes in v12:
time: 217 us; the launch traced here: 216 us
  Pallas kernels  74.7 us (34%)
  waiting for transfers between devices  63.3 us (29%)
  starting transfers between devices  51.7 us (24%)
  local copies, waits for them, and re-layouts  17 us (8%)
  other arithmetic  8.29 us (4%)
    pallas_call x18, Pallas kernels, local_call(): pl.pallas_call(body, out_shape=outs, in_specs=specs, out_specs=tuple((pl....  74.7 us
    ppermute x53, waiting for transfers between devices, swap(): lax.ppermute(value, ALL_AXES, [(source, source ^ mask) for source in rang...  63.3 us
    ppermute x53, starting transfers between devices, swap(): lax.ppermute(value, ALL_AXES, [(source, source ^ mask) for source in rang...  51.7 us
    unnamed x130, local copies, waits for them, and re-layouts  13.7 us
  transfers between devices with their start and end apart: 53, of which 23 were waited for; matrix products, arithmetic and copies ran while one was open for 4% of the time, Pallas kernels for 27%

profile of v12, /device:TPU:0, one launch (start us, length us, event | category | flops | bytes accessed | tf_op | source)
XLA Modules:
  0.0 216.2 jit_solution(4614864357668749206)
XLA Ops:
  1.8 3.1 %collective-permute-start.3 = (bf16[960,128]{1,0:T(8,128)(2,1)S(1)}, bf16[960,128]{1,0:T(8,128)(2,1)S(1)}, u32[]{:S(2)}, u32[]{:S(2)}) collective-permute-start(bf16[960,128]{1,0:T(8,128)(2,1)S(1)} %slice.66.refs_1_), channel_id=1, source_target_pairs={{0,8},{1,9},{2,10},{3,11},{4,12},{5,13},{6,14},{7,15},{8,0},{9,1},... | collective-permute-start | bytes 737288 | tf_op jit(solution)/shard_map/ppermute | solution.py:127
  5.0 2.5 %collective-permute-start.2 = (bf16[400,128]{1,0:T(8,128)(2,1)S(1)}, bf16[400,128]{1,0:T(8,128)(2,1)S(1)}, u32[]{:S(2)}, u32[]{:S(2)}) collective-permute-start(bf16[400,128]{1,0:T(8,128)(2,1)S(1)} %slice.65.refs_1_), channel_id=1, source_target_pairs={{0,24},{1,25},{2,26},{3,27},{4,28},{5,29},{6,30},{7,31},{8,16},{9,... | collective-permute-start | bytes 307208 | tf_op jit(solution)/shard_map/ppermute | solution.py:127
  9.4 2.5 %collective-permute-start.15 = (bf16[960,128]{1,0:T(8,128)(2,1)S(1)}, bf16[960,128]{1,0:T(8,128)(2,1)S(1)}, u32[]{:S(2)}, u32[]{:S(2)}) collective-permute-start(bf16[960,128]{1,0:T(8,128)(2,1)S(1)} %slice.66.refs_1_), channel_id=1, source_target_pairs={{0,24},{1,25},{2,26},{3,27},{4,28},{5,29},{6,30},{7,31},{8,16},{9,... | collective-permute-start | bytes 737288 | tf_op jit(solution)/shard_map/ppermute | solution.py:127
  12.0 4.5 %collective-permute-done.2.refs_4_ = bf16[400,128]{1,0:T(8,128)(2,1)S(1)} collective-permute-done((bf16[400,128]{1,0:T(8,128)(2,1)S(1)}, bf16[400,128]{1,0:T(8,128)(2,1)S(1)}, u32[]{:S(2)}, u32[]{:S(2)}) %collective-permute-start.2) | collective-permute-done | bytes 102432 | tf_op jit(solution)/shard_map/ppermute | solution.py:127
  25.0 5.1 %collective-permute-done.5.refs_10_.refs_7_.refs_6_.refs_9_.refs_20_ = bf16[1600,128]{1,0:T(8,128)(2,1)S(1)} collective-permute-done((bf16[1600,128]{1,0:T(8,128)(2,1)}, bf16[1600,128]{1,0:T(8,128)(2,1)S(1)}, u32[]{:S(2)}, u32[]{:S(2)}) %collective-permute-start.5) | collective-permute-done | bytes 409632 | tf_op jit(solution)/shard_map/ppermute | solution.py:127
  32.6 3.4 %collective-permute-done.4.refs_9_.refs_6_.refs_5_.refs_8_.refs_19_ = bf16[1600,128]{1,0:T(8,128)(2,1)S(1)} collective-permute-done((bf16[1600,128]{1,0:T(8,128)(2,1)}, bf16[1600,128]{1,0:T(8,128)(2,1)S(1)}, u32[]{:S(2)}, u32[]{:S(2)}) %collective-permute-start.4) | collective-permute-done | bytes 409632 | tf_op jit(solution)/shard_map/ppermute | solution.py:127
  38.0 6.4 %collective-permute-done.6.refs_11_.refs_8_.refs_7_.refs_10_.refs_21_ = bf16[1600,128]{1,0:T(8,128)(2,1)S(1)} collective-permute-done((bf16[1600,128]{1,0:T(8,128)(2,1)S(1)}, bf16[1600,128]{1,0:T(8,128)(2,1)S(1)}, u32[]{:S(2)}, u32[]{:S(2)}) %collective-permute-start.6) | collective-permute-done | bytes 409632 | tf_op jit(solution)/shard_map/ppermute | solution.py:127
  45.1 2.9 %shard_map.155 = (bf16[1920,128]{1,0:T(8,128)(2,1)}, bf16[1920,128]{1,0:T(8,128)(2,1)}) custom-call(s32[1]{0:T(128)} %bitcast.refs_0_, bf16[960,128]{1,0:T(8,128)(2,1)} %copy-done.28, bf16[960,128]{1,0:T(8,128)(2,1)} %copy-done.29, bf16[960,128]{1,0:T(8,128)(2,1)} %copy-done.46, bf16[960,128]{1,0:T(8,128)(2,1)} %copy-done.45, bf16[1600,128]{1,0:T(8,128)(2,1)} %copy-done.1, ...), custom_call_target="tpu_custom_call" | custom-call | tf_op jit(solution)/shard_map/pallas_call | solution.py:139
  53.5 3.9 %shard_map.153 = (bf16[128,640]{1,0:T(8,128)(2,1)}, f32[128,1024]{1,0:T(8,128)}, f32[128,256]{1,0:T(8,128)}, bf16[128,1024]{1,0:T(8,128)(2,1)}, bf16[128,512]{1,0:T(8,128)(2,1)}) custom-call(s32[1]{0:T(128)} %bitcast.refs_0_, bf16[128,640]{1,0:T(8,128)(2,1)} %refs_1_.5, f32[1,640]{1,0:T(1,128)} %broadcast_in_dim.30.refs_2_, f32[1,256]{1,0:T(1,128)} %bitcast.29, ...), custom_call_target="tpu_custom_call" | custom-call | tf_op jit(solution)/shard_map/pallas_call | solution.py:139
  61.4 2.5 %collective-permute-start.20 = (bf16[1920,128]{1,0:T(8,128)(2,1)}, bf16[1920,128]{1,0:T(8,128)(2,1)S(1)}, u32[]{:S(2)}, u32[]{:S(2)}) collective-permute-start(bf16[1920,128]{1,0:T(8,128)(2,1)} %collective-permute-done.18.refs_10_), channel_id=1, source_target_pairs={{0,4},{1,5},{2,6},{3,7},{4,0},{5,1},{6,2},{7,3},{8,12},{9,13},{10,... | collective-permute-start | bytes 1474568 | tf_op jit(solution)/shard_map/ppermute | solution.py:127
  63.9 2.8 %collective-permute-done.12.refs_15_.refs_3_.refs_10_ = bf16[128,512]{1,0:T(8,128)(2,1)S(1)} collective-permute-done((bf16[128,512]{1,0:T(8,128)(2,1)}, bf16[128,512]{1,0:T(8,128)(2,1)S(1)}, u32[]{:S(2)}, u32[]{:S(2)}) %collective-permute-start.12) | collective-permute-done | bytes 131104 | tf_op jit(solution)/shard_map/ppermute | solution.py:127
  75.8 8.3 %collective-permute-done.21.refs_1_ = bf16[1920,128]{1,0:T(8,128)(2,1)S(1)} collective-permute-done((bf16[1920,128]{1,0:T(8,128)(2,1)}, bf16[1920,128]{1,0:T(8,128)(2,1)S(1)}, u32[]{:S(2)}, u32[]{:S(2)}) %collective-permute-start.21) | collective-permute-done | bytes 491552 | tf_op jit(solution)/shard_map/ppermute | solution.py:127
  85.6 5.7 %shard_map.154 = (f32[128,2048]{1,0:T(8,128)}, bf16[128,1024]{1,0:T(8,128)(2,1)}, f32[128,640]{1,0:T(8,128)}, f32[128,640]{1,0:T(8,128)}, bf16[1024,640]{1,0:T(8,128)(2,1)}) custom-call(s32[1]{0:T(128)} %bitcast.refs_0_, bf16[128,640]{1,0:T(8,128)(2,1)} %refs_1_.5, f32[1,640]{1,0:T(1,128)} %broadcast_in_dim.14.refs_2_.refs_3_, f32[128,512]{1,0:T(8,128)} %fusion.4.refs_3_, ...), custom_call_target="tpu_custom_call" | custom-call | tf_op jit(solution)/shard_map/pallas_call | solution.py:139
  98.6 14.9 %shard_map.159 = (bf16[128,640]{1,0:T(8,128)(2,1)}, f32[128,640]{1,0:T(8,128)}, f32[1,640]{1,0:T(1,128)}, f32[1,640]{1,0:T(1,128)}, bf16[11520,128]{1,0:T(8,128)...) custom-call(s32[1]{0:T(128)} %bitcast.refs_0_, ...), custom_call_target="tpu_custom_call" | custom-call | tf_op jit(solution)/shard_map/pallas_call | solution.py:139
  114.1 5.8 %shard_map.160 = (bf16[1024,640]{1,0:T(8,128)(2,1)}, f32[128,1024]{1,0:T(8,128)}, f32[1,640]{1,0:T(1,128)}, f32[128,512]{1,0:T(8,128)}, f32[128,512]{1,0:T(8,128)}, /*index=5*/bf16[256,512]{1,0:T(8,128)(2,1)}) custom-call(s32[1]{0:T(128)} %bitcast.refs_0_, f32[128,640]{1,0:T(8,128)} %get-tuple-element.87.refs_1_.refs_10_, ...), custom_call_target="tpu_custom_call" | custom-call | tf_op jit(solution)/shard_map/pallas_call | solution.py:139
  121.5 2.6 %shard_map.161 = (bf16[1920,128]{1,0:T(8,128)(2,1)}, bf16[1920,128]{1,0:T(8,128)(2,1)}) custom-call(s32[1]{0:T(128)} %bitcast.refs_0_, bf16[3840,128]{1,0:T(8,128)(2,1)} %get-tuple-element.97.refs_1_.refs_5_, bf16[3840,128]{1,0:T(8,128)(2,1)} %copy-done.7, f32[128,1024]{1,0:T(8,128)} %get-tuple-element.92.refs_3_.refs_6_), custom_call_target="tpu_custom_call" | custom-call | tf_op jit(solution)/shard_map/pallas_call | solution.py:139
  129.3 4.6 %shard_map.162 = (bf16[3840,128]{1,0:T(8,128)(2,1)}, bf16[1920,128]{1,0:T(8,128)(2,1)}, bf16[1920,128]{1,0:T(8,128)(2,1)}, bf16[1920,128]{1,0:T(8,128)(2,1)}, bf16[2432,128]{1,0:T(8,128)(2,1)}) custom-call(s32[1]{0:T(128)} %bitcast.refs_0_, bf16[11520,128]{1,0:T(8,128)(2,1)} %get-tuple-element.93.refs_1_, bf16[11520,128]{1,0:T(8,128)(2,1)} %copy-done.8, ...), custom_call_target="tpu_custom_call" | custom-call | tf_op jit(solution)/shard_map/pallas_call | solution.py:139
  136.0 4.5 %shard_map.163 = (bf16[640,1024]{1,0:T(8,128)(2,1)}, f32[128,640]{1,0:T(8,128)}, f32[1,256]{1,0:T(1,128)}) custom-call(s32[1]{0:T(128)} %bitcast.refs_0_, f32[1,256]{1,0:T(1,128)} %bitcast.30, f32[128,128]{1,0:T(8,128)} %get-tuple-element.161.refs_5_.refs_2_.refs_4_, f32[128,128]{1,0:T(8,128)} %get-tuple-element.160.refs_6_.refs_3_.refs_5_, ...), custom_call_target="tpu_custom_call" | custom-call | tf_op jit(solution)/shard_map/pallas_call | solution.py:139
  141.4 3.2 %shard_map.164 = (bf16[1920,128]{1,0:T(8,128)(2,1)}, bf16[1920,128]{1,0:T(8,128)(2,1)}, f32[8,128]{1,0:T(8,128)}) custom-call(s32[1]{0:T(128)} %bitcast.refs_0_, bf16[1920,128]{1,0:T(8,128)(2,1)} %get-tuple-element.108.refs_1_, bf16[1920,128]{1,0:T(8,128)(2,1)} %get-tuple-element.109.refs_2_, bf16[1920,128]{1,0:T(8,128)(2,1)} %copy-done.40, ...), custom_call_target="tpu_custom_call" | custom-call | tf_op jit(solution)/shard_map/pallas_call | solution.py:139
  146.6 2.3 %collective-permute-done.36.refs_27_.refs_2_ = bf16[1920,128]{1,0:T(8,128)(2,1)S(1)} collective-permute-done((bf16[1920,128]{1,0:T(8,128)(2,1)}, bf16[1920,128]{1,0:T(8,128)(2,1)S(1)}, u32[]{:S(2)}, u32[]{:S(2)}) %collective-permute-start.36) | collective-permute-done | bytes 491552 | tf_op jit(solution)/shard_map/ppermute | solution.py:127
  148.9 4.0 %collective-permute-done.33.refs_17_.refs_5_ = bf16[2432,128]{1,0:T(8,128)(2,1)S(1)} collective-permute-done((bf16[2432,128]{1,0:T(8,128)(2,1)}, bf16[2432,128]{1,0:T(8,128)(2,1)S(1)}, u32[]{:S(2)}, u32[]{:S(2)}) %collective-permute-start.33) | collective-permute-done | bytes 622624 | tf_op jit(solution)/shard_map/ppermute | solution.py:127
  153.7 4.7 %shard_map.165 = (bf16[640,512]{1,0:T(8,128)(2,1)}, bf16[128,640]{1,0:T(8,128)(2,1)}, f32[32,128]{1,0:T(8,128)}) custom-call(s32[1]{0:T(128)} %bitcast.refs_0_, bf16[128,640]{1,0:T(8,128)(2,1)} %refs_1_.5, f32[1,640]{1,0:T(1,128)} %broadcast_in_dim.30.refs_2_, f32[1,256]{1,0:T(1,128)} %bitcast.28, f32[128,128]{1,0:T(8,128)} %get-tuple-element.161.refs_5_.refs_2_.refs_4_, ...), custom_call_target="tpu_custom_call" | custom-call | tf_op jit(solution)/shard_map/pallas_call | solution.py:139
  158.4 4.3 %shard_map.166 = (bf16[4800,128]{1,0:T(8,128)(2,1)}, bf16[1632,128]{1,0:T(8,128)(2,1)}, bf16[4800,128]{1,0:T(8,128)(2,1)}, bf16[1632,128]{1,0:T(8,128)(2,1)}) custom-call(s32[1]{0:T(128)} %bitcast.refs_0_, bf16[640,1024]{1,0:T(8,128)(2,1)} %get-tuple-element.114.refs_1_, bf16[640,512]{1,0:T(8,128)(2,1)} %get-tuple-element.115.refs_2_, ...), custom_call_target="tpu_custom_call" | custom-call | tf_op jit(solution)/shard_map/pallas_call | solution.py:139
  164.2 4.1 %shard_map.168 = (f32[960,128]{1,0:T(8,128)}, bf16[960,128]{1,0:T(8,128)(2,1)}, bf16[960,128]{1,0:T(8,128)(2,1)}, bf16[960,128]{1,0:T(8,128)(2,1)}) custom-call(s32[1]{0:T(128)} %bitcast.refs_0_, bf16[3840,128]{1,0:T(8,128)(2,1)} %get-tuple-element.100.refs_15_.refs_1_, bf16[1920,128]{1,0:T(8,128)(2,1)} %copy-done.19, bf16[1920,128]{1,0:T(8,128)(2,1)} %copy-done.14, ...), custom_call_target="tpu_custom_call" | custom-call | tf_op jit(solution)/shard_map/pallas_call | solution.py:139
  170.2 5.7 %collective-permute-start.48 = (bf16[960,128]{1,0:T(8,128)(2,1)}, bf16[960,128]{1,0:T(8,128)(2,1)S(1)}, u32[]{:S(2)}, u32[]{:S(2)}) collective-permute-start(bf16[960,128]{1,0:T(8,128)(2,1)} %get-tuple-element.138), channel_id=1, source_target_pairs={{0,16},{1,17},{2,18},{3,19},{4,20},{5,21},{6,22},{7,23},{8,24},{9,... | collective-permute-start | bytes 737288 | tf_op jit(solution)/shard_map/ppermute | solution.py:127
  177.0 3.1 %shard_map.169 = (bf16[832,128]{1,0:T(8,128)(2,1)}, bf16[800,128]{1,0:T(8,128)(2,1)}, bf16[1600,128]{1,0:T(8,128)(2,1)}, bf16[800,128]{1,0:T(8,128)(2,1)}, bf16[...) custom-call(s32[1]{0:T(128)} %bitcast.refs_0_, ...), custom_call_target="tpu_custom_call" | custom-call | tf_op jit(solution)/shard_map/pallas_call | solution.py:139
  182.0 5.5 %collective-permute-done.43.refs_4_ = bf16[800,128]{1,0:T(8,128)(2,1)S(1)} collective-permute-done((bf16[800,128]{1,0:T(8,128)(2,1)}, bf16[800,128]{1,0:T(8,128)(2,1)S(1)}, u32[]{:S(2)}, u32[]{:S(2)}) %collective-permute-start.43) | collective-permute-done | bytes 204832 | tf_op jit(solution)/shard_map/ppermute | solution.py:127
  188.2 2.3 %shard_map.170 = (bf16[800,128]{1,0:T(8,128)(2,1)}, bf16[832,128]{1,0:T(8,128)(2,1)}, f32[32,128]{1,0:T(8,128)}) custom-call(s32[1]{0:T(128)} %bitcast.refs_0_, bf16[800,128]{1,0:T(8,128)(2,1)} %get-tuple-element.129.refs_1_, bf16[800,128]{1,0:T(8,128)(2,1)} %get-tuple-element.130.refs_2_, bf16[832,128]{1,0:T(8,128)(2,1)} %copy-done.49, ...), custom_call_target="tpu_custom_call" | custom-call | tf_op jit(solution)/shard_map/pallas_call | solution.py:139
  194.7 3.9 %collective-permute-done.41.refs_2_ = bf16[800,128]{1,0:T(8,128)(2,1)S(1)} collective-permute-done((bf16[800,128]{1,0:T(8,128)(2,1)S(1)}, bf16[800,128]{1,0:T(8,128)(2,1)S(1)}, u32[]{:S(2)}, u32[]{:S(2)}) %collective-permute-start.41) | collective-permute-done | bytes 204832 | tf_op jit(solution)/shard_map/ppermute | solution.py:127
  201.6 2.5 %shard_map.171 = (f32[432,128]{1,0:T(8,128)}, bf16[432,128]{1,0:T(8,128)(2,1)}, bf16[432,128]{1,0:T(8,128)(2,1)}, bf16[432,128]{1,0:T(8,128)(2,1)}) custom-call(s32[1]{0:T(128)} %bitcast.refs_0_, bf16[1600,128]{1,0:T(8,128)(2,1)} %get-tuple-element.127.refs_1_, bf16[800,128]{1,0:T(8,128)(2,1)} %copy-done.50, bf16[800,128]{1,0:T(8,128)(2,1)} %copy-done.52, ...), custom_call_target="tpu_custom_call" | custom-call | tf_op jit(solution)/shard_map/pallas_call | solution.py:139
  205.6 3.0 %collective-permute-start.52 = (bf16[432,128]{1,0:T(8,128)(2,1)}, bf16[432,128]{1,0:T(8,128)(2,1)S(1)}, u32[]{:S(2)}, u32[]{:S(2)}) collective-permute-start(bf16[432,128]{1,0:T(8,128)(2,1)} %get-tuple-element.143), channel_id=1, source_target_pairs={{0,24},{1,25},{2,26},{3,27},{4,28},{5,29},{6,30},{7,31},{8,16},{9,... | collective-permute-start | bytes 331784 | tf_op jit(solution)/shard_map/ppermute | solution.py:127
  210.6 3.1 %collective-permute-done.51 = bf16[432,128]{1,0:T(8,128)(2,1)S(1)} collective-permute-done((bf16[432,128]{1,0:T(8,128)(2,1)}, bf16[432,128]{1,0:T(8,128)(2,1)S(1)}, u32[]{:S(2)}, u32[]{:S(2)}) %collective-permute-start.51) | collective-permute-done | bytes 110624 | tf_op jit(solution)/shard_map/ppermute | solution.py:127
  (257 shorter events, 77.5 us)
Async XLA Ops:
  1.8 16.7 %collective-permute-start.3 = (bf16[960,128]{1,0:T(8,128)(2,1)S(1)}, bf16[960,128]{1,0:T(8,128)(2,1)S(1)}, u32[]{:S(2)}, u32[]{:S(2)}) collective-permute-start(bf16[960,128]{1,0:T(8,128)(2,1)S(1)} %slice.66.refs_1_), channel_id=1, source_target_pairs={{0,8},{1,9},{2,10},{3,11},{4,12},{5,13},{6,14},{7,15},{8,0},{9,1},... | collective-permute-start | bytes 737288 | tf_op jit(solution)/shard_map/ppermute | solution.py:127
  5.0 11.5 %collective-permute-start.2 = (bf16[400,128]{1,0:T(8,128)(2,1)S(1)}, bf16[400,128]{1,0:T(8,128)(2,1)S(1)}, u32[]{:S(2)}, u32[]{:S(2)}) collective-permute-start(bf16[400,128]{1,0:T(8,128)(2,1)S(1)} %slice.65.refs_1_), channel_id=1, source_target_pairs={{0,24},{1,25},{2,26},{3,27},{4,28},{5,29},{6,30},{7,31},{8,16},{9,... | collective-permute-start | bytes 307208 | tf_op jit(solution)/shard_map/ppermute | solution.py:127
  7.5 11.0 %collective-permute-start.1 = (bf16[400,128]{1,0:T(8,128)(2,1)S(1)}, bf16[400,128]{1,0:T(8,128)(2,1)S(1)}, u32[]{:S(2)}, u32[]{:S(2)}) collective-permute-start(bf16[400,128]{1,0:T(8,128)(2,1)S(1)} %slice.65.refs_1_), channel_id=1, source_target_pairs={{0,16},{1,17},{2,18},{3,19},{4,20},{5,21},{6,22},{7,23},{8,24},{9,... | collective-permute-start | bytes 307208 | tf_op jit(solution)/shard_map/ppermute | solution.py:127
  7.7 10.8 %collective-permute-start = (bf16[400,128]{1,0:T(8,128)(2,1)S(1)}, bf16[400,128]{1,0:T(8,128)(2,1)S(1)}, u32[]{:S(2)}, u32[]{:S(2)}) collective-permute-start(bf16[400,128]{1,0:T(8,128)(2,1)S(1)} %slice.65.refs_1_), channel_id=1, source_target_pairs={{0,8},{1,9},{2,10},{3,11},{4,12},{5,13},{6,14},{7,15},{8,0},{9,1},... | collective-permute-start | bytes 307208 | tf_op jit(solution)/shard_map/ppermute | solution.py:127
  9.4 23.2 %collective-permute-start.15 = (bf16[960,128]{1,0:T(8,128)(2,1)S(1)}, bf16[960,128]{1,0:T(8,128)(2,1)S(1)}, u32[]{:S(2)}, u32[]{:S(2)}) collective-permute-start(bf16[960,128]{1,0:T(8,128)(2,1)S(1)} %slice.66.refs_1_), channel_id=1, source_target_pairs={{0,24},{1,25},{2,26},{3,27},{4,28},{5,29},{6,30},{7,31},{8,16},{9,... | collective-permute-start | bytes 737288 | tf_op jit(solution)/shard_map/ppermute | solution.py:127
  16.5 21.5 %collective-permute-start.14 = (bf16[960,128]{1,0:T(8,128)(2,1)S(1)}, bf16[960,128]{1,0:T(8,128)(2,1)S(1)}, u32[]{:S(2)}, u32[]{:S(2)}) collective-permute-start(bf16[960,128]{1,0:T(8,128)(2,1)S(1)} %slice.66.refs_1_), channel_id=1, source_target_pairs={{0,16},{1,17},{2,18},{3,19},{4,20},{5,21},{6,22},{7,23},{8,24},{9,... | collective-permute-start | bytes 737288 | tf_op jit(solution)/shard_map/ppermute | solution.py:127
  23.4 26.6 %collective-permute-start.7 = (bf16[1600,128]{1,0:T(8,128)(2,1)}, bf16[1600,128]{1,0:T(8,128)(2,1)S(1)}, u32[]{:S(2)}, u32[]{:S(2)}) collective-permute-start(bf16[1600,128]{1,0:T(8,128)(2,1)} %shard_map.152.refs_8_.refs_5_.refs_7_.refs_18_), channel_id=1, source_target_pairs={{0,1},{1,0},{2,3},{3,2},{4,5},{5,4},{6,7},{7,6},{8,9},{9,8},{10,11... | collective-permute-start | bytes 1228808 | tf_op jit(solution)/shard_map/ppermute | solution.py:127
  23.4 12.5 %collective-permute-start.4 = (bf16[1600,128]{1,0:T(8,128)(2,1)}, bf16[1600,128]{1,0:T(8,128)(2,1)S(1)}, u32[]{:S(2)}, u32[]{:S(2)}) collective-permute-start(bf16[1600,128]{1,0:T(8,128)(2,1)} %shard_map.152.refs_8_.refs_5_.refs_7_.refs_18_), channel_id=1, source_target_pairs={{0,4},{1,5},{2,6},{3,7},{4,0},{5,1},{6,2},{7,3},{8,12},{9,13},{10,... | collective-permute-start | bytes 1228808 | tf_op jit(solution)/shard_map/ppermute | solution.py:127
  30.1 14.2 %collective-permute-start.6 = (bf16[1600,128]{1,0:T(8,128)(2,1)S(1)}, bf16[1600,128]{1,0:T(8,128)(2,1)S(1)}, u32[]{:S(2)}, u32[]{:S(2)}) collective-permute-start(bf16[1600,128]{1,0:T(8,128)(2,1)S(1)} %collective-permute-done.5.refs_10_.refs_7_.refs_6_.refs_9_.refs_20_), channel_id=1, source_target_pairs={{0,4},{1,5},{2,6},{3,7},{4,0},{5,1},{6,2},{7,3},{8,12},{9,13},{10,... | collective-permute-start | bytes 1228808 | tf_op jit(solution)/shard_map/ppermute | solution.py:127
  32.6 19.8 %collective-permute-start.9 = (bf16[1600,128]{1,0:T(8,128)(2,1)S(1)}, bf16[1600,128]{1,0:T(8,128)(2,1)S(1)}, u32[]{:S(2)}, u32[]{:S(2)}) collective-permute-start(bf16[1600,128]{1,0:T(8,128)(2,1)S(1)} %collective-permute-done.5.refs_10_.refs_7_.refs_6_.refs_9_.refs_20_), channel_id=1, source_target_pairs={{0,1},{1,0},{2,3},{3,2},{4,5},{5,4},{6,7},{7,6},{8,9},{9,8},{10,11... | collective-permute-start | bytes 1228808 | tf_op jit(solution)/shard_map/ppermute | solution.py:127
  36.0 16.4 %collective-permute-start.8 = (bf16[1600,128]{1,0:T(8,128)(2,1)S(1)}, bf16[1600,128]{1,0:T(8,128)(2,1)S(1)}, u32[]{:S(2)}, u32[]{:S(2)}) collective-permute-start(bf16[1600,128]{1,0:T(8,128)(2,1)S(1)} %collective-permute-done.4.refs_9_.refs_6_.refs_5_.refs_8_.refs_19_), channel_id=1, source_target_pairs={{0,1},{1,0},{2,3},{3,2},{4,5},{5,4},{6,7},{7,6},{8,9},{9,8},{10,11... | collective-permute-start | bytes 1228808 | tf_op jit(solution)/shard_map/ppermute | solution.py:127
  48.0 13.4 %collective-permute-start.18 = (bf16[1920,128]{1,0:T(8,128)(2,1)}, bf16[1920,128]{1,0:T(8,128)(2,1)}, u32[]{:S(2)}, u32[]{:S(2)}) collective-permute-start(bf16[1920,128]{1,0:T(8,128)(2,1)} %get-tuple-element.79.refs_1_.refs_6_), channel_id=1, source_target_pairs={{0,2},{1,3},{2,0},{3,1},{4,6},{5,7},{6,4},{7,5},{8,10},{9,11},{10,... | collective-permute-start | bytes 1474568 | tf_op jit(solution)/shard_map/ppermute | solution.py:127
  48.5 15.3 %collective-permute-start.17 = (bf16[1920,128]{1,0:T(8,128)(2,1)}, bf16[1920,128]{1,0:T(8,128)(2,1)S(1)}, u32[]{:S(2)}, u32[]{:S(2)}) collective-permute-start(bf16[1920,128]{1,0:T(8,128)(2,1)} %get-tuple-element.80.refs_7_), channel_id=1, source_target_pairs={{0,4},{1,5},{2,6},{3,7},{4,0},{5,1},{6,2},{7,3},{8,12},{9,13},{10,... | collective-permute-start | bytes 1474568 | tf_op jit(solution)/shard_map/ppermute | solution.py:127
  61.4 12.9 %collective-permute-start.20 = (bf16[1920,128]{1,0:T(8,128)(2,1)}, bf16[1920,128]{1,0:T(8,128)(2,1)S(1)}, u32[]{:S(2)}, u32[]{:S(2)}) collective-permute-start(bf16[1920,128]{1,0:T(8,128)(2,1)} %collective-permute-done.18.refs_10_), channel_id=1, source_target_pairs={{0,4},{1,5},{2,6},{3,7},{4,0},{5,1},{6,2},{7,3},{8,12},{9,13},{10,... | collective-permute-start | bytes 1474568 | tf_op jit(solution)/shard_map/ppermute | solution.py:127
  69.8 14.3 %collective-permute-start.21 = (bf16[1920,128]{1,0:T(8,128)(2,1)}, bf16[1920,128]{1,0:T(8,128)(2,1)S(1)}, u32[]{:S(2)}, u32[]{:S(2)}) collective-permute-start(bf16[1920,128]{1,0:T(8,128)(2,1)} %shard_map.157), channel_id=1, source_target_pairs={{0,2},{1,3},{2,0},{3,1},{4,6},{5,7},{6,4},{7,5},{8,10},{9,11},{10,... | collective-permute-start | bytes 1474568 | tf_op jit(solution)/shard_map/ppermute | solution.py:127
  71.0 20.4 %collective-permute-start.22 = (bf16[1920,128]{1,0:T(8,128)(2,1)S(1)}, bf16[1920,128]{1,0:T(8,128)(2,1)S(1)}, u32[]{:S(2)}, u32[]{:S(2)}) collective-permute-start(bf16[1920,128]{1,0:T(8,128)(2,1)S(1)} %copy-done.15), channel_id=1, source_target_pairs={{0,1},{1,0},{2,3},{3,2},{4,5},{5,4},{6,7},{7,6},{8,9},{9,8},{10,11... | collective-permute-start | bytes 1474568 | tf_op jit(solution)/shard_map/ppermute | solution.py:127
  71.1 23.0 %collective-permute-start.23 = (bf16[1920,128]{1,0:T(8,128)(2,1)S(1)}, bf16[1920,128]{1,0:T(8,128)(2,1)S(1)}, u32[]{:S(2)}, u32[]{:S(2)}) collective-permute-start(bf16[1920,128]{1,0:T(8,128)(2,1)S(1)} %copy-done.34), channel_id=1, source_target_pairs={{0,1},{1,0},{2,3},{3,2},{4,5},{5,4},{6,7},{7,6},{8,9},{9,8},{10,11... | collective-permute-start | bytes 1474568 | tf_op jit(solution)/shard_map/ppermute | solution.py:127
  71.6 22.0 %collective-permute-start.19 = (bf16[1920,128]{1,0:T(8,128)(2,1)S(1)}, bf16[1920,128]{1,0:T(8,128)(2,1)}, u32[]{:S(2)}, u32[]{:S(2)}) collective-permute-start(bf16[1920,128]{1,0:T(8,128)(2,1)S(1)} %copy-done.34), channel_id=1, source_target_pairs={{0,2},{1,3},{2,0},{3,1},{4,6},{5,7},{6,4},{7,5},{8,10},{9,11},{10,... | collective-permute-start | bytes 1474568 | tf_op jit(solution)/shard_map/ppermute | solution.py:127
  74.3 19.3 %collective-permute-start.16 = (bf16[1920,128]{1,0:T(8,128)(2,1)}, bf16[1920,128]{1,0:T(8,128)(2,1)}, u32[]{:S(2)}, u32[]{:S(2)}) collective-permute-start(bf16[1920,128]{1,0:T(8,128)(2,1)} %shard_map.156), channel_id=1, source_target_pairs={{0,4},{1,5},{2,6},{3,7},{4,0},{5,1},{6,2},{7,3},{8,12},{9,13},{10,... | collective-permute-start | bytes 1474568 | tf_op jit(solution)/shard_map/ppermute | solution.py:127
  113.5 14.1 %collective-permute-start.30 = (bf16[11520,128]{1,0:T(8,128)(2,1)}, bf16[11520,128]{1,0:T(8,128)(2,1)S(1)}, u32[]{:S(2)}, u32[]{:S(2)}) collective-permute-start(bf16[11520,128]{1,0:T(8,128)(2,1)} %get-tuple-element.94), channel_id=1, source_target_pairs={{0,1},{1,0},{2,3},{3,2},{4,5},{5,4},{6,7},{7,6},{8,9},{9,8},{10,11... | collective-permute-start | bytes 8847368 | tf_op jit(solution)/shard_map/ppermute | solution.py:127
  124.2 16.3 %collective-permute-start.34 = (bf16[1920,128]{1,0:T(8,128)(2,1)}, bf16[1920,128]{1,0:T(8,128)(2,1)S(1)}, u32[]{:S(2)}, u32[]{:S(2)}) collective-permute-start(bf16[1920,128]{1,0:T(8,128)(2,1)} %get-tuple-element.110), channel_id=1, source_target_pairs={{0,4},{1,5},{2,6},{3,7},{4,0},{5,1},{6,2},{7,3},{8,12},{9,13},{10,... | collective-permute-start | bytes 1474568 | tf_op jit(solution)/shard_map/ppermute | solution.py:127
  125.3 15.2 %collective-permute-start.35 = (bf16[1920,128]{1,0:T(8,128)(2,1)}, bf16[1920,128]{1,0:T(8,128)(2,1)S(1)}, u32[]{:S(2)}, u32[]{:S(2)}) collective-permute-start(bf16[1920,128]{1,0:T(8,128)(2,1)} %get-tuple-element.99.refs_5_), channel_id=1, source_target_pairs={{0,2},{1,3},{2,0},{3,1},{4,6},{5,7},{6,4},{7,5},{8,10},{9,11},{10,... | collective-permute-start | bytes 1474568 | tf_op jit(solution)/shard_map/ppermute | solution.py:127
  133.9 19.0 %collective-permute-start.33 = (bf16[2432,128]{1,0:T(8,128)(2,1)}, bf16[2432,128]{1,0:T(8,128)(2,1)S(1)}, u32[]{:S(2)}, u32[]{:S(2)}) collective-permute-start(bf16[2432,128]{1,0:T(8,128)(2,1)} %get-tuple-element.107), channel_id=1, source_target_pairs={{0,2},{1,3},{2,0},{3,1},{4,6},{5,7},{6,4},{7,5},{8,10},{9,11},{10,... | collective-permute-start | bytes 1867784 | tf_op jit(solution)/shard_map/ppermute | solution.py:127
  135.1 13.8 %collective-permute-start.36 = (bf16[1920,128]{1,0:T(8,128)(2,1)}, bf16[1920,128]{1,0:T(8,128)(2,1)S(1)}, u32[]{:S(2)}, u32[]{:S(2)}) collective-permute-start(bf16[1920,128]{1,0:T(8,128)(2,1)} %get-tuple-element.112), channel_id=1, source_target_pairs={{0,4},{1,5},{2,6},{3,7},{4,0},{5,1},{6,2},{7,3},{8,12},{9,13},{10,... | collective-permute-start | bytes 1474568 | tf_op jit(solution)/shard_map/ppermute | solution.py:127
  144.6 18.1 %collective-permute-start.38 = (bf16[1920,128]{1,0:T(8,128)(2,1)}, bf16[1920,128]{1,0:T(8,128)(2,1)S(1)}, u32[]{:S(2)}, u32[]{:S(2)}) collective-permute-start(bf16[1920,128]{1,0:T(8,128)(2,1)} %get-tuple-element.122), channel_id=1, source_target_pairs={{0,2},{1,3},{2,0},{3,1},{4,6},{5,7},{6,4},{7,5},{8,10},{9,11},{10,... | collective-permute-start | bytes 1474568 | tf_op jit(solution)/shard_map/ppermute | solution.py:127
  145.5 17.2 %collective-permute-start.37 = (bf16[1920,128]{1,0:T(8,128)(2,1)}, bf16[1920,128]{1,0:T(8,128)(2,1)S(1)}, u32[]{:S(2)}, u32[]{:S(2)}) collective-permute-start(bf16[1920,128]{1,0:T(8,128)(2,1)} %get-tuple-element.111.refs_26_), channel_id=1, source_target_pairs={{0,4},{1,5},{2,6},{3,7},{4,0},{5,1},{6,2},{7,3},{8,12},{9,13},{10,... | collective-permute-start | bytes 1474568 | tf_op jit(solution)/shard_map/ppermute | solution.py:127
  163.6 12.2 %collective-permute-start.39 = (bf16[4800,128]{1,0:T(8,128)(2,1)}, bf16[4800,128]{1,0:T(8,128)(2,1)S(1)}, u32[]{:S(2)}, u32[]{:S(2)}) collective-permute-start(bf16[4800,128]{1,0:T(8,128)(2,1)} %get-tuple-element.123), channel_id=1, source_target_pairs={{0,1},{1,0},{2,3},{3,2},{4,5},{5,4},{6,7},{7,6},{8,9},{9,8},{10,11... | collective-permute-start | bytes 3686408 | tf_op jit(solution)/shard_map/ppermute | solution.py:127
  163.6 12.2 %collective-permute-start.40 = (bf16[1632,128]{1,0:T(8,128)(2,1)}, bf16[1632,128]{1,0:T(8,128)(2,1)S(1)}, u32[]{:S(2)}, u32[]{:S(2)}) collective-permute-start(bf16[1632,128]{1,0:T(8,128)(2,1)} %get-tuple-element.124), channel_id=1, source_target_pairs={{0,1},{1,0},{2,3},{3,2},{4,5},{5,4},{6,7},{7,6},{8,9},{9,8},{10,11... | collective-permute-start | bytes 1253384 | tf_op jit(solution)/shard_map/ppermute | solution.py:127
  168.3 13.7 %collective-permute-start.44 = (bf16[960,128]{1,0:T(8,128)(2,1)}, bf16[960,128]{1,0:T(8,128)(2,1)S(1)}, u32[]{:S(2)}, u32[]{:S(2)}) collective-permute-start(bf16[960,128]{1,0:T(8,128)(2,1)} %get-tuple-element.133), channel_id=1, source_target_pairs={{0,8},{1,9},{2,10},{3,11},{4,12},{5,13},{6,14},{7,15},{8,0},{9,1},... | collective-permute-start | bytes 737288 | tf_op jit(solution)/shard_map/ppermute | solution.py:127
  170.2 23.6 %collective-permute-start.48 = (bf16[960,128]{1,0:T(8,128)(2,1)}, bf16[960,128]{1,0:T(8,128)(2,1)S(1)}, u32[]{:S(2)}, u32[]{:S(2)}) collective-permute-start(bf16[960,128]{1,0:T(8,128)(2,1)} %get-tuple-element.138), channel_id=1, source_target_pairs={{0,16},{1,17},{2,18},{3,19},{4,20},{5,21},{6,22},{7,23},{8,24},{9,... | collective-permute-start | bytes 737288 | tf_op jit(solution)/shard_map/ppermute | solution.py:127
  181.9 12.7 %collective-permute-start.49 = (bf16[960,128]{1,0:T(8,128)(2,1)S(1)}, bf16[960,128]{1,0:T(8,128)(2,1)S(1)}, u32[]{:S(2)}, u32[]{:S(2)}) collective-permute-start(bf16[960,128]{1,0:T(8,128)(2,1)S(1)} %copy-done.62), channel_id=1, source_target_pairs={{0,24},{1,25},{2,26},{3,27},{4,28},{5,29},{6,30},{7,31},{8,16},{9,... | collective-permute-start | bytes 737288 | tf_op jit(solution)/shard_map/ppermute | solution.py:127
  190.5 10.3 %collective-permute-start.46 = (bf16[832,128]{1,0:T(8,128)(2,1)}, bf16[832,128]{1,0:T(8,128)(2,1)S(1)}, u32[]{:S(2)}, u32[]{:S(2)}) collective-permute-start(bf16[832,128]{1,0:T(8,128)(2,1)} %get-tuple-element.135), channel_id=1, source_target_pairs={{0,2},{1,3},{2,0},{3,1},{4,6},{5,7},{6,4},{7,5},{8,10},{9,11},{10,... | collective-permute-start | bytes 638984 | tf_op jit(solution)/shard_map/ppermute | solution.py:127
  (86 other events, 504.3 us)

commit v13 on v12

--- a/solution.py
+++ b/solution.py
@@ -184,13 +184,19 @@
         out_ref[...] = packed[place * count : (place + 1) * count, :].astype(jnp.bfloat16)
 
 
-def sum_one_kernel(size, index_ref, near_ref, far_ref, to_x_ref, to_y_ref):
+def sum_one_kernel(
+    size, index_ref, near_ref, far_ref, across_key_ref, cores_key_ref, to_x_ref, to_y_ref
+):
     total = near_ref[...].astype(jnp.float32) + far_ref[...].astype(jnp.float32)
     half = size // 2
-    to_x_ref[:half, :] = total[:half].astype(jnp.bfloat16)
-    if total.shape[0] > size:
-        to_x_ref[half:, :] = total[size:].astype(jnp.bfloat16)
-    to_y_ref[...] = total[half:size].astype(jnp.bfloat16)
+    to_x_ref[...] = total[:half].astype(jnp.bfloat16)
+    to_y_ref[:half, :] = total[half:].astype(jnp.bfloat16)
+    rows = across_key_ref.shape[0]
+    keys = across_key_ref[...] + cores_key_ref[rows:, :].astype(jnp.float32)
+    for block in range(keys.shape[1] // LANES):
+        first = half + block * rows
+        columns = slice(block * LANES, (block + 1) * LANES)
+        to_y_ref[first : first + rows, :] = keys[:, columns].astype(jnp.bfloat16)
 
 
 def sum_three_kernel(
@@ -198,87 +204,62 @@
     index_ref,
     near_ref,
     far_ref,
-    *refs,
+    own_ref,
+    beside_first_ref,
+    beside_second_ref,
+    across_first_ref,
+    across_second_ref,
 ):
-    key_refs = refs[:-5]
-    own_ref, beside_first_ref, beside_second_ref, across_first_ref, across_second_ref = refs[-5:]
     half = size // 2
-    if key_refs:
-        across_key_ref, cores_key_ref = key_refs
-        rows = across_key_ref.shape[0]
-        keys = across_key_ref[...] + cores_key_ref[rows:, :].astype(jnp.float32)
-        for block in range(keys.shape[1] // LANES):
-            first = half + block * rows
-            columns = slice(block * LANES, (block + 1) * LANES)
-            across_second_ref[first : first + rows, :] = keys[:, columns].astype(jnp.bfloat16)
     outs = (beside_first_ref, beside_second_ref, across_first_ref, across_second_ref)
     total = near_ref[:size, :].astype(jnp.float32) + far_ref[:size, :].astype(jnp.float32)
     own_ref[...] = total.astype(jnp.bfloat16)
     for place, out_ref in enumerate(outs):
         rows = slice(size + place * half, size + (place + 1) * half)
         total = near_ref[rows, :].astype(jnp.float32) + far_ref[rows, :].astype(jnp.float32)
-        out_ref[:half, :] = total.astype(jnp.bfloat16)
+        out_ref[...] = total.astype(jnp.bfloat16)
 
 
 def sum_all_kernel(size, index_ref, near_three, near_one, far_three, far_one, *out_refs):
-    sum_one_kernel(size, index_ref, near_one, far_one, *out_refs[:2])
-    sum_three_kernel(size, index_ref, near_three, far_three, *out_refs[2:])
+    extra = near_one[size:, :].astype(jnp.float32) + far_one[size:, :].astype(jnp.float32)
+    for place, out_ref in enumerate(out_refs):
+        near, far, first = near_three, far_three, place * size
+        if place == 3:
+            near, far, first = near_one, far_one, 0
+        rows = slice(first, first + size)
+        total = near[rows, :].astype(jnp.float32) + far[rows, :].astype(jnp.float32)
+        out_ref[:size, :] = total.astype(jnp.bfloat16)
+        out_ref[size:, :] = extra.astype(jnp.bfloat16)
 
 
 def sum_passed_kernel(
-    size,
     index_ref,
     beside_ref,
     across_ref,
     over_x_ref,
     over_y_ref,
-    near_one_ref,
-    far_one_ref,
     beside_out_ref,
     across_out_ref,
-    extra_ref,
 ):
-    half = size // 2
-    beside = beside_ref[...].astype(jnp.float32) + over_y_ref[...].astype(jnp.float32)
+    half = beside_ref.shape[0]
+    beside = beside_ref[...].astype(jnp.float32) + over_y_ref[:half, :].astype(jnp.float32)
     beside_out_ref[...] = beside.astype(jnp.bfloat16)
-    across = across_ref[...].astype(jnp.float32) + over_x_ref[:half, :].astype(jnp.float32)
-    across_out_ref[:half, :] = across.astype(jnp.bfloat16)
-    if across_out_ref.shape[0] > half:
-        extra = near_one_ref[size:, :].astype(jnp.float32)
-        extra = extra + far_one_ref[size:, :].astype(jnp.float32)
-        extra = extra + over_x_ref[half:, :].astype(jnp.float32)
-        extra_ref[...] = extra
-        across_out_ref[half:, :] = extra.astype(jnp.bfloat16)
-    else:
-        extra_ref[...] = jnp.zeros(extra_ref.shape, jnp.float32)
-
-
-def unpack_kernel(
-    pieces,
-    index_ref,
-    own_ref,
-    beside_first_ref,
-    beside_second_ref,
-    across_first_ref,
-    across_second_ref,
-    extra_ref,
-    *refs,
-):
+    across = across_ref[...].astype(jnp.float32) + over_x_ref[...].astype(jnp.float32)
+    across_out_ref[...] = across.astype(jnp.bfloat16)
+
+
+def unpack_kernel(pieces, term_rows, index_ref, *refs):
     high_count = pieces[0].high_count
-    half = sum(piece.size for piece in pieces) // 2
     flat_rows = sum(piece.flat_rows for piece in pieces)
-    outs, flat, packed = refs[:-2], refs[-2], refs[-1]
+    terms, outs = refs[: -2 - high_count], refs[-2 - high_count : -2]
+    flat, packed = refs[-2:]
     high = index_ref[0] // LOW_COUNT
-    packed[:half, :] = (
-        own_ref[:half, :].astype(jnp.float32)
-        + beside_first_ref[...].astype(jnp.float32)
-        + across_first_ref[:half, :].astype(jnp.float32)
-    )
-    packed[half:, :] = (
-        own_ref[half:, :].astype(jnp.float32)
-        + beside_second_ref[...].astype(jnp.float32)
-        + across_second_ref[:half, :].astype(jnp.float32)
-    )
+    count = len(terms) * term_rows // packed.shape[0]
+    for first in range(0, packed.shape[0], term_rows):
+        place = first // term_rows * count
+        packed[first : first + term_rows, :] = sum(
+            term[:term_rows, :].astype(jnp.float32) for term in terms[place : place + count]
+        )
     start, source = 0, 0
     for piece in pieces:
         for block in range(piece.blocks):
@@ -291,7 +272,7 @@
     for step, out_ref in enumerate(outs):
         out_ref[:flat_rows, :] = flat[high ^ step].astype(out_ref.dtype)
         if out_ref.shape[0] > flat_rows:
-            extra = extra_ref[...] + across_first_ref[half:, :].astype(jnp.float32)
+            extra = sum(term[term_rows:, :].astype(jnp.float32) for term in terms)
             out_ref[flat_rows:, :] = extra.astype(out_ref.dtype)
 
 
@@ -347,8 +328,7 @@
 
 
 def gather_wholes(own):
-    beside, across = swap(own, 4), swap(own, 2)
-    return own, beside, across, swap(across, 4)
+    return own, swap(own, 4), swap(own, 2), swap(own, 6)
 
 
 def gather_cores(near):
@@ -360,96 +340,77 @@
     return swap(far_three, 1), far_one
 
 
-def scatter_one(pieces, near_one, far_one, behind=()):
+def scatter_one(pieces, near_one, far_one, keys):
     half = sum(piece.size for piece in pieces) // 2
     to_x, to_y = local_call(
         functools.partial(sum_one_kernel, 2 * half),
         (
-            array((near_one.shape[0] - half, LANES), jnp.bfloat16),
             array((half, LANES), jnp.bfloat16),
-        ),
-        (near_one, far_one),
-        (),
-        behind,
-    )
-    return swap(to_x, 4), swap(to_y, 2), to_y
-
-
-def scatter_three(pieces, near_three, far_three, behind=(), keys=()):
+            array((half + keys[0].size // LANES, LANES), jnp.bfloat16),
+        ),
+        (near_one, far_one, *keys),
+    )
+    return swap(to_x, 4), swap(to_y, 2), to_x
+
+
+def scatter_three(pieces, near_three, far_three, behind=()):
     size = sum(piece.size for piece in pieces)
     half = size // 2
     own, beside_first, beside_second, across_first, across_second = local_call(
         functools.partial(sum_three_kernel, size),
         (
             array((size, LANES), jnp.bfloat16),
-            *(array((half, LANES), jnp.bfloat16),) * 3,
-            array((half + (keys[0].size // LANES if keys else 0), LANES), jnp.bfloat16),
-        ),
-        (near_three, far_three, *keys),
+            *(array((half, LANES), jnp.bfloat16),) * 4,
+        ),
+        (near_three, far_three),
         (),
         behind,
     )
     return own, swap(beside_first, 4), beside_second, across_first, swap(across_second, 2)
 
 
-def scatter_all(pieces, near_three, near_one, far_three, far_one, behind=()):
+def scatter_passed(threes, over_x, over_y, behind=()):
+    own, beside_first, beside_second, across_first, across_second = threes
+    half = beside_second.shape[0]
+    beside_second, across_first = local_call(
+        sum_passed_kernel,
+        (array((half, LANES), jnp.bfloat16),) * 2,
+        (beside_second, across_first, over_x, over_y),
+        (),
+        behind,
+    )
+    terms = (
+        own[:half],
+        beside_first,
+        swap(across_first, 2),
+        own[half:],
+        swap(beside_second, 4),
+        across_second,
+    )
+    return terms, beside_second
+
+
+def scatter_direct(pieces, near_three, near_one, far_three, far_one, behind=()):
+    rows = near_one.shape[0]
     size = sum(piece.size for piece in pieces)
-    half = size // 2
-    to_x, to_y, own, beside_first, beside_second, across_first, across_second = local_call(
+    own, beside, across, diagonal = local_call(
         functools.partial(sum_all_kernel, size),
-        (
-            array((near_one.shape[0] - half, LANES), jnp.bfloat16),
-            array((half, LANES), jnp.bfloat16),
-            array((size, LANES), jnp.bfloat16),
-            *(array((half, LANES), jnp.bfloat16),) * 4,
-        ),
+        (array((rows, LANES), jnp.bfloat16),) * 4,
         (near_three, near_one, far_three, far_one),
         (),
         behind,
     )
-    over_x, over_y = swap(to_x, 4), swap(to_y, 2)
-    return (
-        over_x,
-        over_y,
-        (own, swap(beside_first, 4), beside_second, across_first, swap(across_second, 2)),
-    )
-
-
-def scatter_passed(pieces, threes, over_x, over_y, near_one, far_one, behind=()):
-    size = sum(piece.size for piece in pieces)
-    extra_count = near_one.shape[0] - size
-    own, beside_first, beside_second, across_first, across_second = threes
-    beside_second, across_first, extra = local_call(
-        functools.partial(sum_passed_kernel, size),
-        (
-            array((size // 2, LANES), jnp.bfloat16),
-            array((size // 2 + extra_count, LANES), jnp.bfloat16),
-            array((max(extra_count, 8), LANES), jnp.float32),
-        ),
-        (beside_second, across_first, over_x, over_y, near_one, far_one),
-        (),
-        behind,
-    )
-    terms = (
-        own,
-        beside_first,
-        swap(beside_second, 4),
-        swap(across_first, 2),
-        across_second,
-        extra,
-    )
-    return terms, beside_second
-
-
-def scatter_high(pieces, terms, behind=()):
+    return (own, swap(beside, 4), swap(across, 2), swap(diagonal, 6)), own
+
+
+def scatter_unpack(pieces, terms, extra_count=0, behind=()):
     high_count = pieces[0].high_count
     size = sum(piece.size for piece in pieces)
     flat_rows = sum(piece.flat_rows for piece in pieces)
-    out_rows = flat_rows + terms[3].shape[0] - size // 2
-    outs = local_call(
-        functools.partial(unpack_kernel, pieces),
-        (array((out_rows, LANES), jnp.float32),)
-        + (array((out_rows, LANES), jnp.bfloat16),) * (high_count - 1),
+    return local_call(
+        functools.partial(unpack_kernel, pieces, terms[0].shape[0] - extra_count),
+        (array((flat_rows + extra_count, LANES), jnp.float32),)
+        + (array((flat_rows + extra_count, LANES), jnp.bfloat16),) * (high_count - 1),
         terms,
         (
             pltpu.VMEM((high_count, flat_rows, LANES), jnp.float32),
@@ -457,8 +418,6 @@
         ),
         behind,
     )
-    arrived = [swap(send, step * LOW_COUNT) for step, send in enumerate(outs) if step]
-    return outs[0] + sum(value.astype(jnp.float32) for value in arrived), outs[0], arrived
 
 
 def norm_parts(values):
@@ -961,6 +920,7 @@
     attention_near = gather_wholes(
         *gather_own(attention_pieces, attention_parts, 1, (ffn_parts[1],))
     )
+    attention_near = tuple(held(attention_near, ffn_parts[2:]))
     attention_blocks = gather_cores(attention_near)
     ffn_own = gather_own(ffn_pieces, ffn_parts, 2, attention_near[1:])
     ffn_passed = gather_halves(*ffn_own)
@@ -1038,8 +998,8 @@
         ),
     )
     cores_key = swap(cores_key, 1)
-    over_x, over_y, sent = scatter_one(ffn_pieces, near_one, far_one, (grad_query,))
-    threes = scatter_three(ffn_pieces, near_three, far_three, (sent,), (across_key, cores_key))
+    over_x, over_y, sent = scatter_one(ffn_pieces, near_one, far_one, (across_key, cores_key))
+    threes = scatter_three(ffn_pieces, near_three, far_three, (swap(sent[:16], 1),))
     grad_query_weight, grad_normed, grad_gain_query = local_call(
         functools.partial(query_back_kernel, attention_pieces),
         (
@@ -1051,9 +1011,7 @@
         (),
         (threes[0],),
     )
-    ffn_terms, sent = scatter_passed(
-        ffn_pieces, threes, over_x, over_y, near_one, far_one, (grad_normed,)
-    )
+    ffn_terms, sent = scatter_passed(threes, over_x, over_y, (grad_normed,))
     grad_key_weight, grad_inputs, grad_gains = local_call(
         functools.partial(project_back_kernel, attention_pieces),
         (
@@ -1078,27 +1036,31 @@
             grad_gain_query,
             own_key,
             cores_key,
-            threes[4],
+            over_y,
             *attention_blocks,
         ),
         (),
-        (sent, threes[1]),
+        (sent, threes[1], threes[4]),
     )
     near_three, near_one, far_three, far_one = local_call(
         functools.partial(split_kernel, attention_pieces),
         grad_arrays(attention_pieces, GAIN_ROWS),
         (grad_query_weight, grad_key_weight, grad_out_weight, grad_gains),
     )
-    far_three, far_one = held((far_three, far_one), ffn_terms[2:4])
-    grads_ffn, sent, arrived = scatter_high(ffn_pieces, ffn_terms, (near_one,))
+    far_three, far_one = held((far_three, far_one), (ffn_terms[2], ffn_terms[4]))
+    own_ffn, first_plane, *planes = scatter_unpack(ffn_pieces, ffn_terms, 0, (near_one,))
     far_three, far_one = scatter_cores(far_three, far_one)
-    over_x, over_y, threes = scatter_all(
-        attention_pieces, near_three, near_one, far_three, far_one, (sent,)
-    )
-    terms, _ = scatter_passed(
-        attention_pieces, threes, over_x, over_y, near_one, far_one, (arrived[0],)
-    )
-    grads_attention, _, _ = scatter_high(attention_pieces, terms, arrived)
+    terms, sent = scatter_direct(
+        attention_pieces, near_three, near_one, far_three, far_one, (first_plane,)
+    )
+    planes = [first_plane, *held(planes, (sent,))]
+    arrived = [swap(plane, step * LOW_COUNT) for step, plane in enumerate(planes, start=1)]
+    grads_ffn = own_ffn + sum(value.astype(jnp.float32) for value in arrived)
+    own_attention, *planes = scatter_unpack(attention_pieces, terms, GAIN_ROWS, arrived)
+    grads_attention = own_attention + sum(
+        swap(plane, step * LOW_COUNT).astype(jnp.float32)
+        for step, plane in enumerate(planes, start=1)
+    )
     gain_grads = grads_attention[attention_rows:].reshape(-1)[: gains.shape[0]]
     grads_local = jnp.concatenate([grads_attention[:attention_rows], grads_ffn])
     return (

time: 217 us -> 221 us (1.018)
  waiting for transfers between devices: 63.3 us -> 68.4 us
  local copies, waits for them, and re-layouts: 17 us -> 20.4 us
  Pallas kernels: 74.7 us -> 71.9 us
    ppermute x53 -> x51, waiting for transfers between devices: 63.3 us -> 68.4 us  [swap(): lax.ppermute(value, ALL_AXES, [(source, source ^ mask) for source in rang...]
    pallas_call x18 -> x17, Pallas kernels: 74.7 us -> 71.9 us  [local_call(): pl.pallas_call(body, out_shape=outs, in_specs=specs, out_specs=tuple((pl....]
    ppermute x53 -> x51, starting transfers between devices: 51.7 us -> 49.9 us  [swap(): lax.ppermute(value, ALL_AXES, [(source, source ^ mask) for source in rang...]
    unnamed x130 -> x118, local copies, waits for them, and re-layouts: 13.7 us -> 15.4 us
  transfers between devices with their start and end apart: 53 -> 51, of which waited for: 23 -> 20; matrix products, arithmetic and copies ran while one was open for 4% -> 5% of each run, Pallas kernels for 27% -> 25%
where the time goes in v13:
time: 221 us; the launch traced here: 220 us
  Pallas kernels  71.9 us (33%)
  waiting for transfers between devices  68.4 us (31%)
  starting transfers between devices  49.9 us (23%)
  local copies, waits for them, and re-layouts  20.4 us (9%)
  other arithmetic  8.52 us (4%)
    pallas_call x17, Pallas kernels, local_call(): pl.pallas_call(body, out_shape=outs, in_specs=specs, out_specs=tuple((pl....  71.9 us
    ppermute x51, waiting for transfers between devices, swap(): lax.ppermute(value, ALL_AXES, [(source, source ^ mask) for source in rang...  68.4 us
    ppermute x51, starting transfers between devices, swap(): lax.ppermute(value, ALL_AXES, [(source, source ^ mask) for source in rang...  49.9 us
    unnamed x118, local copies, waits for them, and re-layouts  15.4 us
  transfers between devices with their start and end apart: 51, of which 20 were waited for; matrix products, arithmetic and copies ran while one was open for 5% of the time, Pallas kernels for 25%

profile of v13, /device:TPU:0, one launch (start us, length us, event | category | flops | bytes accessed | tf_op | source)
XLA Modules:
  0.0 220.2 jit_solution(16412273267258890305)
XLA Ops:
  1.8 3.1 %collective-permute-start.3 = (bf16[960,128]{1,0:T(8,128)(2,1)S(1)}, bf16[960,128]{1,0:T(8,128)(2,1)S(1)}, u32[]{:S(2)}, u32[]{:S(2)}) collective-permute-start(bf16[960,128]{1,0:T(8,128)(2,1)S(1)} %slice.78.refs_1_), channel_id=1, source_target_pairs={{0,8},{1,9},{2,10},{3,11},{4,12},{5,13},{6,14},{7,15},{8,0},{9,1},... | collective-permute-start | bytes 737288 | tf_op jit(solution)/shard_map/ppermute | solution.py:127
  4.9 2.5 %collective-permute-start.2 = (bf16[400,128]{1,0:T(8,128)(2,1)S(1)}, bf16[400,128]{1,0:T(8,128)(2,1)S(1)}, u32[]{:S(2)}, u32[]{:S(2)}) collective-permute-start(bf16[400,128]{1,0:T(8,128)(2,1)S(1)} %slice.77.refs_1_), channel_id=1, source_target_pairs={{0,24},{1,25},{2,26},{3,27},{4,28},{5,29},{6,30},{7,31},{8,16},{9,... | collective-permute-start | bytes 307208 | tf_op jit(solution)/shard_map/ppermute | solution.py:127
  9.4 2.5 %collective-permute-start.8 = (bf16[960,128]{1,0:T(8,128)(2,1)S(1)}, bf16[960,128]{1,0:T(8,128)(2,1)S(1)}, u32[]{:S(2)}, u32[]{:S(2)}) collective-permute-start(bf16[960,128]{1,0:T(8,128)(2,1)S(1)} %slice.78.refs_1_), channel_id=1, source_target_pairs={{0,24},{1,25},{2,26},{3,27},{4,28},{5,29},{6,30},{7,31},{8,16},{9,... | collective-permute-start | bytes 737288 | tf_op jit(solution)/shard_map/ppermute | solution.py:127
  12.5 4.0 %collective-permute-done.2.refs_4_ = bf16[400,128]{1,0:T(8,128)(2,1)S(1)} collective-permute-done((bf16[400,128]{1,0:T(8,128)(2,1)S(1)}, bf16[400,128]{1,0:T(8,128)(2,1)S(1)}, u32[]{:S(2)}, u32[]{:S(2)}) %collective-permute-start.2) | collective-permute-done | bytes 102432 | tf_op jit(solution)/shard_map/ppermute | solution.py:127
  16.5 2.0 collective-permute-done.1.refs_3_
  19.3 2.0 shard_map.152.refs_0_
  21.2 2.4 %collective-permute-start.6 = (bf16[1600,128]{1,0:T(8,128)(2,1)}, bf16[1600,128]{1,0:T(8,128)(2,1)S(1)}, u32[]{:S(2)}, u32[]{:S(2)}) collective-permute-start(bf16[1600,128]{1,0:T(8,128)(2,1)} %shard_map.152.refs_0_), channel_id=1, source_target_pairs={{0,6},{1,7},{2,4},{3,5},{4,2},{5,3},{6,0},{7,1},{8,14},{9,15},{10,... | collective-permute-start | bytes 1228808 | tf_op jit(solution)/shard_map/ppermute | solution.py:127
  26.2 11.8 %collective-permute-done.7.refs_4_.refs_3_ = bf16[960,128]{1,0:T(8,128)(2,1)S(1)} collective-permute-done((bf16[960,128]{1,0:T(8,128)(2,1)S(1)}, bf16[960,128]{1,0:T(8,128)(2,1)S(1)}, u32[]{:S(2)}, u32[]{:S(2)}) %collective-permute-start.7) | collective-permute-done | bytes 245792 | tf_op jit(solution)/shard_map/ppermute | solution.py:127
  43.3 2.9 %shard_map.156 = (bf16[1920,128]{1,0:T(8,128)(2,1)}, bf16[1920,128]{1,0:T(8,128)(2,1)}) custom-call(s32[1]{0:T(128)} %bitcast.refs_0_, bf16[960,128]{1,0:T(8,128)(2,1)} %copy-done.26, bf16[960,128]{1,0:T(8,128)(2,1)} %copy-done.27, bf16[960,128]{1,0:T(8,128)(2,1)} %copy-done.30, bf16[960,128]{1,0:T(8,128)(2,1)} %copy-done.28, ...), custom_call_target="tpu_custom_call" | custom-call | tf_op jit(solution)/shard_map/pallas_call | solution.py:139
  51.9 3.9 %shard_map.154 = (bf16[128,640]{1,0:T(8,128)(2,1)}, f32[128,1024]{1,0:T(8,128)}, f32[128,256]{1,0:T(8,128)}, bf16[128,1024]{1,0:T(8,128)(2,1)}, bf16[128,512]{1,0:T(8,128)(2,1)}) custom-call(s32[1]{0:T(128)} %bitcast.refs_0_, bf16[128,640]{1,0:T(8,128)(2,1)} %refs_1_.5, f32[1,640]{1,0:T(1,128)} %broadcast_in_dim.30.refs_2_, f32[1,256]{1,0:T(1,128)} %bitcast.29, ...), custom_call_target="tpu_custom_call" | custom-call | tf_op jit(solution)/shard_map/pallas_call | solution.py:139
  57.7 2.2 %collective-permute-done.18.refs_10_ = bf16[1920,128]{1,0:T(8,128)(2,1)S(1)} collective-permute-done((bf16[1920,128]{1,0:T(8,128)(2,1)}, bf16[1920,128]{1,0:T(8,128)(2,1)S(1)}, u32[]{:S(2)}, u32[]{:S(2)}) %collective-permute-start.18) | collective-permute-done | bytes 491552 | tf_op jit(solution)/shard_map/ppermute | solution.py:127
  62.1 3.0 %collective-permute-done.14.refs_15_.refs_3_.refs_10_ = bf16[128,512]{1,0:T(8,128)(2,1)S(1)} collective-permute-done((bf16[128,512]{1,0:T(8,128)(2,1)}, bf16[128,512]{1,0:T(8,128)(2,1)S(1)}, u32[]{:S(2)}, u32[]{:S(2)}) %collective-permute-start.14) | collective-permute-done | bytes 131104 | tf_op jit(solution)/shard_map/ppermute | solution.py:127
  66.5 1.9 shard_map.158
  74.2 8.5 %collective-permute-done.21.refs_1_ = bf16[1920,128]{1,0:T(8,128)(2,1)S(1)} collective-permute-done((bf16[1920,128]{1,0:T(8,128)(2,1)}, bf16[1920,128]{1,0:T(8,128)(2,1)S(1)}, u32[]{:S(2)}, u32[]{:S(2)}) %collective-permute-start.21) | collective-permute-done | bytes 491552 | tf_op jit(solution)/shard_map/ppermute | solution.py:127
  84.2 5.7 %shard_map.155 = (f32[128,2048]{1,0:T(8,128)}, bf16[128,1024]{1,0:T(8,128)(2,1)}, f32[128,640]{1,0:T(8,128)}, f32[128,640]{1,0:T(8,128)}, bf16[1024,640]{1,0:T(8,128)(2,1)}) custom-call(s32[1]{0:T(128)} %bitcast.refs_0_, bf16[128,640]{1,0:T(8,128)(2,1)} %refs_1_.5, f32[1,640]{1,0:T(1,128)} %broadcast_in_dim.14.refs_2_.refs_3_, f32[128,512]{1,0:T(8,128)} %fusion.4.refs_3_, ...), custom_call_target="tpu_custom_call" | custom-call | tf_op jit(solution)/shard_map/pallas_call | solution.py:139
  97.1 14.9 %shard_map.160 = (bf16[128,640]{1,0:T(8,128)(2,1)}, f32[128,640]{1,0:T(8,128)}, f32[1,640]{1,0:T(1,128)}, f32[1,640]{1,0:T(1,128)}, bf16[11520,128]{1,0:T(8,128)...) custom-call(s32[1]{0:T(128)} %bitcast.refs_0_, ...), custom_call_target="tpu_custom_call" | custom-call | tf_op jit(solution)/shard_map/pallas_call | solution.py:139
  112.5 5.8 %shard_map.161 = (bf16[1024,640]{1,0:T(8,128)(2,1)}, f32[128,1024]{1,0:T(8,128)}, f32[1,640]{1,0:T(1,128)}, f32[128,512]{1,0:T(8,128)}, f32[128,512]{1,0:T(8,128)}, /*index=5*/bf16[256,512]{1,0:T(8,128)(2,1)}) custom-call(s32[1]{0:T(128)} %bitcast.refs_0_, f32[128,640]{1,0:T(8,128)} %get-tuple-element.90.refs_1_.refs_10_, ...), custom_call_target="tpu_custom_call" | custom-call | tf_op jit(solution)/shard_map/pallas_call | solution.py:139
  121.1 2.7 %shard_map.162 = (bf16[1920,128]{1,0:T(8,128)(2,1)}, bf16[2432,128]{1,0:T(8,128)(2,1)}) custom-call(s32[1]{0:T(128)} %bitcast.refs_0_, bf16[3840,128]{1,0:T(8,128)(2,1)} %get-tuple-element.98.refs_1_, bf16[3840,128]{1,0:T(8,128)(2,1)} %copy-done.25, f32[128,512]{1,0:T(8,128)} %get-tuple-element.100.refs_3_, bf16[256,512]{1,0:T(8,128)(2,1)} %copy-done.24), custom_call_target="tpu_custom_call" | custom-call | tf_op jit(solution)/shard_map/pallas_call | solution.py:139
  129.3 4.5 %shard_map.163 = (bf16[3840,128]{1,0:T(8,128)(2,1)}, bf16[1920,128]{1,0:T(8,128)(2,1)}, bf16[1920,128]{1,0:T(8,128)(2,1)}, bf16[1920,128]{1,0:T(8,128)(2,1)}, bf16[1920,128]{1,0:T(8,128)(2,1)}) custom-call(s32[1]{0:T(128)} %bitcast.refs_0_, bf16[11520,128]{1,0:T(8,128)(2,1)} %get-tuple-element.96.refs_1_, bf16[11520,128]{1,0:T(8,128)(2,1)} %copy-done.8, ...), custom_call_target="tpu_custom_call" | custom-call | tf_op jit(solution)/shard_map/pallas_call | solution.py:139
  135.8 4.5 %shard_map.164 = (bf16[640,1024]{1,0:T(8,128)(2,1)}, f32[128,640]{1,0:T(8,128)}, f32[1,256]{1,0:T(1,128)}) custom-call(s32[1]{0:T(128)} %bitcast.refs_0_, f32[1,256]{1,0:T(1,128)} %bitcast.30, f32[128,128]{1,0:T(8,128)} %get-tuple-element.161.refs_5_.refs_2_.refs_4_, f32[128,128]{1,0:T(8,128)} %get-tuple-element.160.refs_6_.refs_3_.refs_5_, ...), custom_call_target="tpu_custom_call" | custom-call | tf_op jit(solution)/shard_map/pallas_call | solution.py:139
  141.7 2.6 %shard_map.165 = (bf16[1920,128]{1,0:T(8,128)(2,1)}, bf16[1920,128]{1,0:T(8,128)(2,1)}) custom-call(s32[1]{0:T(128)} %bitcast.refs_0_, bf16[1920,128]{1,0:T(8,128)(2,1)} %get-tuple-element.111.refs_1_, bf16[1920,128]{1,0:T(8,128)(2,1)} %get-tuple-element.112.refs_2_, bf16[1920,128]{1,0:T(8,128)(2,1)} %copy-done.42, bf16[2432,128]{1,0:T(8,128)(2,1)} %copy-done.10, ...), custom_call_target="tpu_custom_call" | custom-call | tf_op jit(solution)/shard_map/pallas_call | solution.py:139
  146.3 3.4 %collective-permute-done.36.refs_27_.refs_2_ = bf16[1920,128]{1,0:T(8,128)(2,1)S(1)} collective-permute-done((bf16[1920,128]{1,0:T(8,128)(2,1)}, bf16[1920,128]{1,0:T(8,128)(2,1)S(1)}, u32[]{:S(2)}, u32[]{:S(2)}) %collective-permute-start.36) | collective-permute-done | bytes 491552 | tf_op jit(solution)/shard_map/ppermute | solution.py:127
  152.2 4.7 %shard_map.166 = (bf16[640,512]{1,0:T(8,128)(2,1)}, bf16[128,640]{1,0:T(8,128)(2,1)}, f32[32,128]{1,0:T(8,128)}) custom-call(s32[1]{0:T(128)} %bitcast.refs_0_, bf16[128,640]{1,0:T(8,128)(2,1)} %refs_1_.5, f32[1,640]{1,0:T(1,128)} %broadcast_in_dim.30.refs_2_, f32[1,256]{1,0:T(1,128)} %bitcast.28, f32[128,128]{1,0:T(8,128)} %get-tuple-element.161.refs_5_.refs_2_.refs_4_, ...), custom_call_target="tpu_custom_call" | custom-call | tf_op jit(solution)/shard_map/pallas_call | solution.py:139
  156.9 4.2 %shard_map.167 = (bf16[4800,128]{1,0:T(8,128)(2,1)}, bf16[1632,128]{1,0:T(8,128)(2,1)}, bf16[4800,128]{1,0:T(8,128)(2,1)}, bf16[1632,128]{1,0:T(8,128)(2,1)}) custom-call(s32[1]{0:T(128)} %bitcast.refs_0_, bf16[640,1024]{1,0:T(8,128)(2,1)} %get-tuple-element.117.refs_1_, bf16[640,512]{1,0:T(8,128)(2,1)} %get-tuple-element.118.refs_2_, ...), custom_call_target="tpu_custom_call" | custom-call | tf_op jit(solution)/shard_map/pallas_call | solution.py:139
  164.3 4.1 %shard_map.169 = (f32[960,128]{1,0:T(8,128)}, bf16[960,128]{1,0:T(8,128)(2,1)}, bf16[960,128]{1,0:T(8,128)(2,1)}, bf16[960,128]{1,0:T(8,128)(2,1)}) custom-call(s32[1]{0:T(128)} %bitcast.refs_0_, bf16[1920,128]{1,0:T(8,128)(2,1)} %get-tuple-element.149.refs_1_, bf16[1920,128]{1,0:T(8,128)(2,1)} %copy-done.17, bf16[1920,128]{1,0:T(8,128)(2,1)} %copy-done.11, ...), custom_call_target="tpu_custom_call" | custom-call | tf_op jit(solution)/shard_map/pallas_call | solution.py:139
  168.5 2.4 %collective-permute-start.45 = (bf16[960,128]{1,0:T(8,128)(2,1)}, bf16[960,128]{1,0:T(8,128)(2,1)S(1)}, u32[]{:S(2)}, u32[]{:S(2)}) collective-permute-start(bf16[960,128]{1,0:T(8,128)(2,1)} %get-tuple-element.128.refs_5_), channel_id=1, source_target_pairs={{0,8},{1,9},{2,10},{3,11},{4,12},{5,13},{6,14},{7,15},{8,0},{9,1},... | collective-permute-start | bytes 737288 | tf_op jit(solution)/shard_map/ppermute | solution.py:127
  172.0 3.1 %shard_map.170 = (bf16[1632,128]{1,0:T(8,128)(2,1)}, bf16[1632,128]{1,0:T(8,128)(2,1)}, bf16[1632,128]{1,0:T(8,128)(2,1)}, bf16[1632,128]{1,0:T(8,128)(2,1)}) custom-call(s32[1]{0:T(128)} %bitcast.refs_0_, bf16[4800,128]{1,0:T(8,128)(2,1)} %get-tuple-element.121.refs_1_, bf16[1632,128]{1,0:T(8,128)(2,1)} %get-tuple-element.122.refs_7_.refs_2_, ...), custom_call_target="tpu_custom_call" | custom-call | tf_op jit(solution)/shard_map/pallas_call | solution.py:139
  178.7 2.0 collective-permute-start.46
  181.2 15.1 %collective-permute-done.46.refs_6_ = bf16[960,128]{1,0:T(8,128)(2,1)S(1)} collective-permute-done((bf16[960,128]{1,0:T(8,128)(2,1)}, bf16[960,128]{1,0:T(8,128)(2,1)S(1)}, u32[]{:S(2)}, u32[]{:S(2)}) %collective-permute-start.46) | collective-permute-done | bytes 245792 | tf_op jit(solution)/shard_map/ppermute | solution.py:127
  198.1 2.6 %shard_map.172 = (f32[432,128]{1,0:T(8,128)}, bf16[432,128]{1,0:T(8,128)(2,1)}, bf16[432,128]{1,0:T(8,128)(2,1)}, bf16[432,128]{1,0:T(8,128)(2,1)}) custom-call(s32[1]{0:T(128)} %bitcast.refs_0_, bf16[1632,128]{1,0:T(8,128)(2,1)} %get-tuple-element.129.refs_2_.refs_1_, bf16[1632,128]{1,0:T(8,128)(2,1)} %copy-done.45, bf16[1632,128]{1,0:T(8,128)(2,1)} %copy-done.46, ...), custom_call_target="tpu_custom_call" | custom-call | tf_op jit(solution)/shard_map/pallas_call | solution.py:139
  200.7 5.7 %collective-permute-start.48 = (bf16[432,128]{1,0:T(8,128)(2,1)}, bf16[432,128]{1,0:T(8,128)(2,1)S(1)}, u32[]{:S(2)}, u32[]{:S(2)}) collective-permute-start(bf16[432,128]{1,0:T(8,128)(2,1)} %get-tuple-element.138), channel_id=1, source_target_pairs={{0,8},{1,9},{2,10},{3,11},{4,12},{5,13},{6,14},{7,15},{8,0},{9,1},... | collective-permute-start | bytes 331784 | tf_op jit(solution)/shard_map/ppermute | solution.py:127
  210.5 7.3 %collective-permute-done.49 = bf16[432,128]{1,0:T(8,128)(2,1)S(1)} collective-permute-done((bf16[432,128]{1,0:T(8,128)(2,1)}, bf16[432,128]{1,0:T(8,128)(2,1)S(1)}, u32[]{:S(2)}, u32[]{:S(2)}) %collective-permute-start.49) | collective-permute-done | bytes 110624 | tf_op jit(solution)/shard_map/ppermute | solution.py:127
  (244 shorter events, 71.1 us)
Async XLA Ops:
  1.8 16.7 %collective-permute-start.3 = (bf16[960,128]{1,0:T(8,128)(2,1)S(1)}, bf16[960,128]{1,0:T(8,128)(2,1)S(1)}, u32[]{:S(2)}, u32[]{:S(2)}) collective-permute-start(bf16[960,128]{1,0:T(8,128)(2,1)S(1)} %slice.78.refs_1_), channel_id=1, source_target_pairs={{0,8},{1,9},{2,10},{3,11},{4,12},{5,13},{6,14},{7,15},{8,0},{9,1},... | collective-permute-start | bytes 737288 | tf_op jit(solution)/shard_map/ppermute | solution.py:127
  4.9 11.5 %collective-permute-start.2 = (bf16[400,128]{1,0:T(8,128)(2,1)S(1)}, bf16[400,128]{1,0:T(8,128)(2,1)S(1)}, u32[]{:S(2)}, u32[]{:S(2)}) collective-permute-start(bf16[400,128]{1,0:T(8,128)(2,1)S(1)} %slice.77.refs_1_), channel_id=1, source_target_pairs={{0,24},{1,25},{2,26},{3,27},{4,28},{5,29},{6,30},{7,31},{8,16},{9,... | collective-permute-start | bytes 307208 | tf_op jit(solution)/shard_map/ppermute | solution.py:127
  7.5 11.0 %collective-permute-start.1 = (bf16[400,128]{1,0:T(8,128)(2,1)S(1)}, bf16[400,128]{1,0:T(8,128)(2,1)S(1)}, u32[]{:S(2)}, u32[]{:S(2)}) collective-permute-start(bf16[400,128]{1,0:T(8,128)(2,1)S(1)} %slice.77.refs_1_), channel_id=1, source_target_pairs={{0,16},{1,17},{2,18},{3,19},{4,20},{5,21},{6,22},{7,23},{8,24},{9,... | collective-permute-start | bytes 307208 | tf_op jit(solution)/shard_map/ppermute | solution.py:127
  7.7 10.8 %collective-permute-start = (bf16[400,128]{1,0:T(8,128)(2,1)S(1)}, bf16[400,128]{1,0:T(8,128)(2,1)S(1)}, u32[]{:S(2)}, u32[]{:S(2)}) collective-permute-start(bf16[400,128]{1,0:T(8,128)(2,1)S(1)} %slice.77.refs_1_), channel_id=1, source_target_pairs={{0,8},{1,9},{2,10},{3,11},{4,12},{5,13},{6,14},{7,15},{8,0},{9,1},... | collective-permute-start | bytes 307208 | tf_op jit(solution)/shard_map/ppermute | solution.py:127
  9.4 16.8 %collective-permute-start.8 = (bf16[960,128]{1,0:T(8,128)(2,1)S(1)}, bf16[960,128]{1,0:T(8,128)(2,1)S(1)}, u32[]{:S(2)}, u32[]{:S(2)}) collective-permute-start(bf16[960,128]{1,0:T(8,128)(2,1)S(1)} %slice.78.refs_1_), channel_id=1, source_target_pairs={{0,24},{1,25},{2,26},{3,27},{4,28},{5,29},{6,30},{7,31},{8,16},{9,... | collective-permute-start | bytes 737288 | tf_op jit(solution)/shard_map/ppermute | solution.py:127
  16.5 21.5 %collective-permute-start.7 = (bf16[960,128]{1,0:T(8,128)(2,1)S(1)}, bf16[960,128]{1,0:T(8,128)(2,1)S(1)}, u32[]{:S(2)}, u32[]{:S(2)}) collective-permute-start(bf16[960,128]{1,0:T(8,128)(2,1)S(1)} %slice.78.refs_1_), channel_id=1, source_target_pairs={{0,16},{1,17},{2,18},{3,19},{4,20},{5,21},{6,22},{7,23},{8,24},{9,... | collective-permute-start | bytes 737288 | tf_op jit(solution)/shard_map/ppermute | solution.py:127
  21.2 16.7 %collective-permute-start.6 = (bf16[1600,128]{1,0:T(8,128)(2,1)}, bf16[1600,128]{1,0:T(8,128)(2,1)S(1)}, u32[]{:S(2)}, u32[]{:S(2)}) collective-permute-start(bf16[1600,128]{1,0:T(8,128)(2,1)} %shard_map.152.refs_0_), channel_id=1, source_target_pairs={{0,6},{1,7},{2,4},{3,5},{4,2},{5,3},{6,0},{7,1},{8,14},{9,15},{10,... | collective-permute-start | bytes 1228808 | tf_op jit(solution)/shard_map/ppermute | solution.py:127
  23.7 16.1 %collective-permute-start.5 = (bf16[1600,128]{1,0:T(8,128)(2,1)}, bf16[1600,128]{1,0:T(8,128)(2,1)S(1)}, u32[]{:S(2)}, u32[]{:S(2)}) collective-permute-start(bf16[1600,128]{1,0:T(8,128)(2,1)} %shard_map.152.refs_0_), channel_id=1, source_target_pairs={{0,2},{1,3},{2,0},{3,1},{4,6},{5,7},{6,4},{7,5},{8,10},{9,11},{10,... | collective-permute-start | bytes 1228808 | tf_op jit(solution)/shard_map/ppermute | solution.py:127
  24.2 15.6 %collective-permute-start.4 = (bf16[1600,128]{1,0:T(8,128)(2,1)}, bf16[1600,128]{1,0:T(8,128)(2,1)S(1)}, u32[]{:S(2)}, u32[]{:S(2)}) collective-permute-start(bf16[1600,128]{1,0:T(8,128)(2,1)} %shard_map.152.refs_0_), channel_id=1, source_target_pairs={{0,4},{1,5},{2,6},{3,7},{4,0},{5,1},{6,2},{7,3},{8,12},{9,13},{10,... | collective-permute-start | bytes 1228808 | tf_op jit(solution)/shard_map/ppermute | solution.py:127
  46.2 13.8 %collective-permute-start.18 = (bf16[1920,128]{1,0:T(8,128)(2,1)}, bf16[1920,128]{1,0:T(8,128)(2,1)S(1)}, u32[]{:S(2)}, u32[]{:S(2)}) collective-permute-start(bf16[1920,128]{1,0:T(8,128)(2,1)} %get-tuple-element.82.refs_1_.refs_6_), channel_id=1, source_target_pairs={{0,2},{1,3},{2,0},{3,1},{4,6},{5,7},{6,4},{7,5},{8,10},{9,11},{10,... | collective-permute-start | bytes 1474568 | tf_op jit(solution)/shard_map/ppermute | solution.py:127
  47.6 14.0 %collective-permute-start.17 = (bf16[1920,128]{1,0:T(8,128)(2,1)}, bf16[1920,128]{1,0:T(8,128)(2,1)S(1)}, u32[]{:S(2)}, u32[]{:S(2)}) collective-permute-start(bf16[1920,128]{1,0:T(8,128)(2,1)} %get-tuple-element.83.refs_7_), channel_id=1, source_target_pairs={{0,4},{1,5},{2,6},{3,7},{4,0},{5,1},{6,2},{7,3},{8,12},{9,13},{10,... | collective-permute-start | bytes 1474568 | tf_op jit(solution)/shard_map/ppermute | solution.py:127
  59.9 12.9 %collective-permute-start.20 = (bf16[1920,128]{1,0:T(8,128)(2,1)S(1)}, bf16[1920,128]{1,0:T(8,128)(2,1)S(1)}, u32[]{:S(2)}, u32[]{:S(2)}) collective-permute-start(bf16[1920,128]{1,0:T(8,128)(2,1)S(1)} %collective-permute-done.18.refs_10_), channel_id=1, source_target_pairs={{0,4},{1,5},{2,6},{3,7},{4,0},{5,1},{6,2},{7,3},{8,12},{9,13},{10,... | collective-permute-start | bytes 1474568 | tf_op jit(solution)/shard_map/ppermute | solution.py:127
  68.3 14.3 %collective-permute-start.21 = (bf16[1920,128]{1,0:T(8,128)(2,1)}, bf16[1920,128]{1,0:T(8,128)(2,1)S(1)}, u32[]{:S(2)}, u32[]{:S(2)}) collective-permute-start(bf16[1920,128]{1,0:T(8,128)(2,1)} %shard_map.158), channel_id=1, source_target_pairs={{0,2},{1,3},{2,0},{3,1},{4,6},{5,7},{6,4},{7,5},{8,10},{9,11},{10,... | collective-permute-start | bytes 1474568 | tf_op jit(solution)/shard_map/ppermute | solution.py:127
  69.8 20.1 %collective-permute-start.22 = (bf16[1920,128]{1,0:T(8,128)(2,1)S(1)}, bf16[1920,128]{1,0:T(8,128)(2,1)S(1)}, u32[]{:S(2)}, u32[]{:S(2)}) collective-permute-start(bf16[1920,128]{1,0:T(8,128)(2,1)S(1)} %copy-done.13), channel_id=1, source_target_pairs={{0,1},{1,0},{2,3},{3,2},{4,5},{5,4},{6,7},{7,6},{8,9},{9,8},{10,11... | collective-permute-start | bytes 1474568 | tf_op jit(solution)/shard_map/ppermute | solution.py:127
  69.9 22.7 %collective-permute-start.23 = (bf16[1920,128]{1,0:T(8,128)(2,1)S(1)}, bf16[1920,128]{1,0:T(8,128)(2,1)}, u32[]{:S(2)}, u32[]{:S(2)}) collective-permute-start(bf16[1920,128]{1,0:T(8,128)(2,1)S(1)} %copy-done.35), channel_id=1, source_target_pairs={{0,1},{1,0},{2,3},{3,2},{4,5},{5,4},{6,7},{7,6},{8,9},{9,8},{10,11... | collective-permute-start | bytes 1474568 | tf_op jit(solution)/shard_map/ppermute | solution.py:127
  70.4 21.7 %collective-permute-start.19 = (bf16[1920,128]{1,0:T(8,128)(2,1)S(1)}, bf16[1920,128]{1,0:T(8,128)(2,1)}, u32[]{:S(2)}, u32[]{:S(2)}) collective-permute-start(bf16[1920,128]{1,0:T(8,128)(2,1)S(1)} %copy-done.35), channel_id=1, source_target_pairs={{0,2},{1,3},{2,0},{3,1},{4,6},{5,7},{6,4},{7,5},{8,10},{9,11},{10,... | collective-permute-start | bytes 1474568 | tf_op jit(solution)/shard_map/ppermute | solution.py:127
  72.8 19.2 %collective-permute-start.16 = (bf16[1920,128]{1,0:T(8,128)(2,1)}, bf16[1920,128]{1,0:T(8,128)(2,1)}, u32[]{:S(2)}, u32[]{:S(2)}) collective-permute-start(bf16[1920,128]{1,0:T(8,128)(2,1)} %shard_map.157), channel_id=1, source_target_pairs={{0,4},{1,5},{2,6},{3,7},{4,0},{5,1},{6,2},{7,3},{8,12},{9,13},{10,... | collective-permute-start | bytes 1474568 | tf_op jit(solution)/shard_map/ppermute | solution.py:127
  111.9 15.8 %collective-permute-start.30 = (bf16[11520,128]{1,0:T(8,128)(2,1)}, bf16[11520,128]{1,0:T(8,128)(2,1)S(1)}, u32[]{:S(2)}, u32[]{:S(2)}) collective-permute-start(bf16[11520,128]{1,0:T(8,128)(2,1)} %get-tuple-element.97), channel_id=1, source_target_pairs={{0,1},{1,0},{2,3},{3,2},{4,5},{5,4},{6,7},{7,6},{8,9},{9,8},{10,11... | collective-permute-start | bytes 8847368 | tf_op jit(solution)/shard_map/ppermute | solution.py:127
  123.8 17.1 %collective-permute-start.34 = (bf16[2432,128]{1,0:T(8,128)(2,1)}, bf16[2432,128]{1,0:T(8,128)(2,1)S(1)}, u32[]{:S(2)}, u32[]{:S(2)}) collective-permute-start(bf16[2432,128]{1,0:T(8,128)(2,1)} %get-tuple-element.110), channel_id=1, source_target_pairs={{0,2},{1,3},{2,0},{3,1},{4,6},{5,7},{6,4},{7,5},{8,10},{9,11},{10,... | collective-permute-start | bytes 1867784 | tf_op jit(solution)/shard_map/ppermute | solution.py:127
  125.0 15.4 %collective-permute-start.35 = (bf16[1920,128]{1,0:T(8,128)(2,1)}, bf16[1920,128]{1,0:T(8,128)(2,1)S(1)}, u32[]{:S(2)}, u32[]{:S(2)}) collective-permute-start(bf16[1920,128]{1,0:T(8,128)(2,1)} %get-tuple-element.102), channel_id=1, source_target_pairs={{0,4},{1,5},{2,6},{3,7},{4,0},{5,1},{6,2},{7,3},{8,12},{9,13},{10,... | collective-permute-start | bytes 1474568 | tf_op jit(solution)/shard_map/ppermute | solution.py:127
  133.8 16.0 %collective-permute-start.36 = (bf16[1920,128]{1,0:T(8,128)(2,1)}, bf16[1920,128]{1,0:T(8,128)(2,1)S(1)}, u32[]{:S(2)}, u32[]{:S(2)}) collective-permute-start(bf16[1920,128]{1,0:T(8,128)(2,1)} %get-tuple-element.114), channel_id=1, source_target_pairs={{0,4},{1,5},{2,6},{3,7},{4,0},{5,1},{6,2},{7,3},{8,12},{9,13},{10,... | collective-permute-start | bytes 1474568 | tf_op jit(solution)/shard_map/ppermute | solution.py:127
  134.9 16.5 %collective-permute-start.37 = (bf16[1920,128]{1,0:T(8,128)(2,1)}, bf16[1920,128]{1,0:T(8,128)(2,1)S(1)}, u32[]{:S(2)}, u32[]{:S(2)}) collective-permute-start(bf16[1920,128]{1,0:T(8,128)(2,1)} %get-tuple-element.115), channel_id=1, source_target_pairs={{0,2},{1,3},{2,0},{3,1},{4,6},{5,7},{6,4},{7,5},{8,10},{9,11},{10,... | collective-permute-start | bytes 1474568 | tf_op jit(solution)/shard_map/ppermute | solution.py:127
  144.3 16.8 %collective-permute-start.38 = (bf16[1920,128]{1,0:T(8,128)(2,1)}, bf16[1920,128]{1,0:T(8,128)(2,1)S(1)}, u32[]{:S(2)}, u32[]{:S(2)}) collective-permute-start(bf16[1920,128]{1,0:T(8,128)(2,1)} %get-tuple-element.125), channel_id=1, source_target_pairs={{0,2},{1,3},{2,0},{3,1},{4,6},{5,7},{6,4},{7,5},{8,10},{9,11},{10,... | collective-permute-start | bytes 1474568 | tf_op jit(solution)/shard_map/ppermute | solution.py:127
  145.5 15.7 %collective-permute-start.39 = (bf16[1920,128]{1,0:T(8,128)(2,1)}, bf16[1920,128]{1,0:T(8,128)(2,1)S(1)}, u32[]{:S(2)}, u32[]{:S(2)}) collective-permute-start(bf16[1920,128]{1,0:T(8,128)(2,1)} %get-tuple-element.113.refs_26_), channel_id=1, source_target_pairs={{0,4},{1,5},{2,6},{3,7},{4,0},{5,1},{6,2},{7,3},{8,12},{9,13},{10,... | collective-permute-start | bytes 1474568 | tf_op jit(solution)/shard_map/ppermute | solution.py:127
  168.5 12.2 %collective-permute-start.45 = (bf16[960,128]{1,0:T(8,128)(2,1)}, bf16[960,128]{1,0:T(8,128)(2,1)S(1)}, u32[]{:S(2)}, u32[]{:S(2)}) collective-permute-start(bf16[960,128]{1,0:T(8,128)(2,1)} %get-tuple-element.128.refs_5_), channel_id=1, source_target_pairs={{0,8},{1,9},{2,10},{3,11},{4,12},{5,13},{6,14},{7,15},{8,0},{9,1},... | collective-permute-start | bytes 737288 | tf_op jit(solution)/shard_map/ppermute | solution.py:127
  175.2 21.1 %collective-permute-start.42 = (bf16[1632,128]{1,0:T(8,128)(2,1)}, bf16[1632,128]{1,0:T(8,128)(2,1)S(1)}, u32[]{:S(2)}, u32[]{:S(2)}) collective-permute-start(bf16[1632,128]{1,0:T(8,128)(2,1)} %get-tuple-element.130), channel_id=1, source_target_pairs={{0,4},{1,5},{2,6},{3,7},{4,0},{5,1},{6,2},{7,3},{8,12},{9,13},{10,... | collective-permute-start | bytes 1253384 | tf_op jit(solution)/shard_map/ppermute | solution.py:127
  176.6 19.7 %collective-permute-start.43 = (bf16[1632,128]{1,0:T(8,128)(2,1)}, bf16[1632,128]{1,0:T(8,128)(2,1)S(1)}, u32[]{:S(2)}, u32[]{:S(2)}) collective-permute-start(bf16[1632,128]{1,0:T(8,128)(2,1)} %get-tuple-element.131), channel_id=1, source_target_pairs={{0,2},{1,3},{2,0},{3,1},{4,6},{5,7},{6,4},{7,5},{8,10},{9,11},{10,... | collective-permute-start | bytes 1253384 | tf_op jit(solution)/shard_map/ppermute | solution.py:127
  177.4 18.9 %collective-permute-start.44 = (bf16[1632,128]{1,0:T(8,128)(2,1)}, bf16[1632,128]{1,0:T(8,128)(2,1)S(1)}, u32[]{:S(2)}, u32[]{:S(2)}) collective-permute-start(bf16[1632,128]{1,0:T(8,128)(2,1)} %get-tuple-element.132), channel_id=1, source_target_pairs={{0,6},{1,7},{2,4},{3,5},{4,2},{5,3},{6,0},{7,1},{8,14},{9,15},{10,... | collective-permute-start | bytes 1253384 | tf_op jit(solution)/shard_map/ppermute | solution.py:127
  178.7 17.6 %collective-permute-start.46 = (bf16[960,128]{1,0:T(8,128)(2,1)}, bf16[960,128]{1,0:T(8,128)(2,1)S(1)}, u32[]{:S(2)}, u32[]{:S(2)}) collective-permute-start(bf16[960,128]{1,0:T(8,128)(2,1)} %get-tuple-element.135), channel_id=1, source_target_pairs={{0,16},{1,17},{2,18},{3,19},{4,20},{5,21},{6,22},{7,23},{8,24},{9,... | collective-permute-start | bytes 737288 | tf_op jit(solution)/shard_map/ppermute | solution.py:127
  180.6 15.6 %collective-permute-start.47 = (bf16[960,128]{1,0:T(8,128)(2,1)}, bf16[960,128]{1,0:T(8,128)(2,1)S(1)}, u32[]{:S(2)}, u32[]{:S(2)}) collective-permute-start(bf16[960,128]{1,0:T(8,128)(2,1)} %get-tuple-element.136), channel_id=1, source_target_pairs={{0,24},{1,25},{2,26},{3,27},{4,28},{5,29},{6,30},{7,31},{8,16},{9,... | collective-permute-start | bytes 737288 | tf_op jit(solution)/shard_map/ppermute | solution.py:127
  206.4 11.4 %collective-permute-start.49 = (bf16[432,128]{1,0:T(8,128)(2,1)}, bf16[432,128]{1,0:T(8,128)(2,1)S(1)}, u32[]{:S(2)}, u32[]{:S(2)}) collective-permute-start(bf16[432,128]{1,0:T(8,128)(2,1)} %get-tuple-element.139), channel_id=1, source_target_pairs={{0,16},{1,17},{2,18},{3,19},{4,20},{5,21},{6,22},{7,23},{8,24},{9,... | collective-permute-start | bytes 331784 | tf_op jit(solution)/shard_map/ppermute | solution.py:127
  207.6 10.2 %collective-permute-start.50 = (bf16[432,128]{1,0:T(8,128)(2,1)}, bf16[432,128]{1,0:T(8,128)(2,1)S(1)}, u32[]{:S(2)}, u32[]{:S(2)}) collective-permute-start(bf16[432,128]{1,0:T(8,128)(2,1)} %get-tuple-element.140), channel_id=1, source_target_pairs={{0,24},{1,25},{2,26},{3,27},{4,28},{5,29},{6,30},{7,31},{8,16},{9,... | collective-permute-start | bytes 331784 | tf_op jit(solution)/shard_map/ppermute | solution.py:127
  (78 other events, 460.4 us)

commit v14 on v13

--- a/solution.py
+++ b/solution.py
@@ -184,40 +184,28 @@
         out_ref[...] = packed[place * count : (place + 1) * count, :].astype(jnp.bfloat16)
 
 
-def sum_one_kernel(
-    size, index_ref, near_ref, far_ref, across_key_ref, cores_key_ref, to_x_ref, to_y_ref
-):
+def sum_one_kernel(index_ref, near_ref, far_ref, to_x_ref, to_y_ref):
     total = near_ref[...].astype(jnp.float32) + far_ref[...].astype(jnp.float32)
-    half = size // 2
+    half = to_x_ref.shape[0]
     to_x_ref[...] = total[:half].astype(jnp.bfloat16)
-    to_y_ref[:half, :] = total[half:].astype(jnp.bfloat16)
-    rows = across_key_ref.shape[0]
-    keys = across_key_ref[...] + cores_key_ref[rows:, :].astype(jnp.float32)
-    for block in range(keys.shape[1] // LANES):
-        first = half + block * rows
-        columns = slice(block * LANES, (block + 1) * LANES)
-        to_y_ref[first : first + rows, :] = keys[:, columns].astype(jnp.bfloat16)
-
-
-def sum_three_kernel(
-    size,
-    index_ref,
-    near_ref,
-    far_ref,
-    own_ref,
-    beside_first_ref,
-    beside_second_ref,
-    across_first_ref,
-    across_second_ref,
-):
-    half = size // 2
-    outs = (beside_first_ref, beside_second_ref, across_first_ref, across_second_ref)
-    total = near_ref[:size, :].astype(jnp.float32) + far_ref[:size, :].astype(jnp.float32)
-    own_ref[...] = total.astype(jnp.bfloat16)
-    for place, out_ref in enumerate(outs):
-        rows = slice(size + place * half, size + (place + 1) * half)
+    to_y_ref[...] = total[half:].astype(jnp.bfloat16)
+
+
+def sum_halves_kernel(starts, index_ref, near_ref, far_ref, *refs):
+    key_refs, out_refs = refs[: -len(starts)], refs[-len(starts) :]
+    half = near_ref.shape[0] // 6
+    for first, out_ref in zip(starts, out_refs):
+        rows = slice(first, first + half)
         total = near_ref[rows, :].astype(jnp.float32) + far_ref[rows, :].astype(jnp.float32)
-        out_ref[...] = total.astype(jnp.bfloat16)
+        out_ref[:half, :] = total.astype(jnp.bfloat16)
+    if key_refs:
+        across_key_ref, cores_key_ref = key_refs
+        rows = across_key_ref.shape[0]
+        keys = across_key_ref[...] + cores_key_ref[rows:, :].astype(jnp.float32)
+        for block in range(keys.shape[1] // LANES):
+            first = half + block * rows
+            columns = slice(block * LANES, (block + 1) * LANES)
+            out_refs[-1][first : first + rows, :] = keys[:, columns].astype(jnp.bfloat16)
 
 
 def sum_all_kernel(size, index_ref, near_three, near_one, far_three, far_one, *out_refs):
@@ -241,8 +229,7 @@
     beside_out_ref,
     across_out_ref,
 ):
-    half = beside_ref.shape[0]
-    beside = beside_ref[...].astype(jnp.float32) + over_y_ref[:half, :].astype(jnp.float32)
+    beside = beside_ref[...].astype(jnp.float32) + over_y_ref[...].astype(jnp.float32)
     beside_out_ref[...] = beside.astype(jnp.bfloat16)
     across = across_ref[...].astype(jnp.float32) + over_x_ref[...].astype(jnp.float32)
     across_out_ref[...] = across.astype(jnp.bfloat16)
@@ -340,38 +327,42 @@
     return swap(far_three, 1), far_one
 
 
-def scatter_one(pieces, near_one, far_one, keys):
-    half = sum(piece.size for piece in pieces) // 2
+def scatter_one(near_one, far_one):
+    half = near_one.shape[0] // 2
     to_x, to_y = local_call(
-        functools.partial(sum_one_kernel, 2 * half),
+        sum_one_kernel, (array((half, LANES), jnp.bfloat16),) * 2, (near_one, far_one)
+    )
+    return swap(to_x, 4), swap(to_y, 2), to_x
+
+
+def scatter_free(near_three, far_three, keys):
+    half = near_three.shape[0] // 6
+    beside_first, across_second = local_call(
+        functools.partial(sum_halves_kernel, (2 * half, 5 * half)),
         (
             array((half, LANES), jnp.bfloat16),
             array((half + keys[0].size // LANES, LANES), jnp.bfloat16),
         ),
-        (near_one, far_one, *keys),
-    )
-    return swap(to_x, 4), swap(to_y, 2), to_x
-
-
-def scatter_three(pieces, near_three, far_three, behind=()):
-    size = sum(piece.size for piece in pieces)
-    half = size // 2
-    own, beside_first, beside_second, across_first, across_second = local_call(
-        functools.partial(sum_three_kernel, size),
-        (
-            array((size, LANES), jnp.bfloat16),
-            *(array((half, LANES), jnp.bfloat16),) * 4,
-        ),
+        (near_three, far_three, *keys),
+    )
+    return swap(beside_first, 4), swap(across_second, 2), beside_first
+
+
+def scatter_rest(near_three, far_three, behind):
+    half = near_three.shape[0] // 6
+    return local_call(
+        functools.partial(sum_halves_kernel, (0, half, 3 * half, 4 * half)),
+        (array((half, LANES), jnp.bfloat16),) * 4,
         (near_three, far_three),
         (),
         behind,
     )
-    return own, swap(beside_first, 4), beside_second, across_first, swap(across_second, 2)
-
-
-def scatter_passed(threes, over_x, over_y, behind=()):
-    own, beside_first, beside_second, across_first, across_second = threes
-    half = beside_second.shape[0]
+
+
+def scatter_passed(free, rest, over_x, over_y, behind=()):
+    beside_first, across_second = free
+    own_first, own_second, beside_second, across_first = rest
+    half = own_first.shape[0]
     beside_second, across_first = local_call(
         sum_passed_kernel,
         (array((half, LANES), jnp.bfloat16),) * 2,
@@ -380,10 +371,10 @@
         behind,
     )
     terms = (
-        own[:half],
+        own_first,
         beside_first,
         swap(across_first, 2),
-        own[half:],
+        own_second,
         swap(beside_second, 4),
         across_second,
     )
@@ -400,7 +391,7 @@
         (),
         behind,
     )
-    return (own, swap(beside, 4), swap(across, 2), swap(diagonal, 6)), own
+    return own, swap(beside, 4), swap(across, 2), swap(diagonal, 6)
 
 
 def scatter_unpack(pieces, terms, extra_count=0, behind=()):
@@ -811,8 +802,8 @@
     rows = pieces[0].block_rows
     normed = normed_ref[...]
     key_rows = own_key_ref.shape[0]
+    key_value = own_key_ref[...] + cores_key_ref[:key_rows, :].astype(jnp.float32)
     first = across_key_ref.shape[0] - 4 * key_rows
-    key_value = own_key_ref[...] + cores_key_ref[:key_rows, :].astype(jnp.float32)
     key_value = key_value + jnp.concatenate(
         [
             across_key_ref[first + block * key_rows : first + (block + 1) * key_rows, :].astype(
@@ -976,6 +967,8 @@
     )
     near_three, near_one, far_three, far_one = grads_ffn
     far_three, far_one = scatter_cores(far_three, far_one)
+    over_x, over_y, sent = scatter_one(near_one, far_one)
+    sent = swap(sent[:16], 1)
     grad_out_weight, grad_query, grad_gain_attn, own_key, across_key, cores_key = local_call(
         attend_back_kernel,
         (
@@ -996,10 +989,12 @@
             query_rot,
             *key_values,
         ),
+        (),
+        (sent,),
     )
     cores_key = swap(cores_key, 1)
-    over_x, over_y, sent = scatter_one(ffn_pieces, near_one, far_one, (across_key, cores_key))
-    threes = scatter_three(ffn_pieces, near_three, far_three, (swap(sent[:16], 1),))
+    *free, sent = scatter_free(near_three, far_three, (across_key, cores_key))
+    rest = scatter_rest(near_three, far_three, (sent,))
     grad_query_weight, grad_normed, grad_gain_query = local_call(
         functools.partial(query_back_kernel, attention_pieces),
         (
@@ -1009,9 +1004,9 @@
         ),
         (gain_query, cosine, sine, normed, query_proj, grad_query, *attention_blocks),
         (),
-        (threes[0],),
-    )
-    ffn_terms, sent = scatter_passed(threes, over_x, over_y, (grad_normed,))
+        (rest[0],),
+    )
+    ffn_terms, sent = scatter_passed(free, rest, over_x, over_y)
     grad_key_weight, grad_inputs, grad_gains = local_call(
         functools.partial(project_back_kernel, attention_pieces),
         (
@@ -1036,11 +1031,11 @@
             grad_gain_query,
             own_key,
             cores_key,
-            over_y,
+            free[1],
             *attention_blocks,
         ),
         (),
-        (sent, threes[1], threes[4]),
+        (sent, free[0]),
     )
     near_three, near_one, far_three, far_one = local_call(
         functools.partial(split_kernel, attention_pieces),
@@ -1048,12 +1043,11 @@
         (grad_query_weight, grad_key_weight, grad_out_weight, grad_gains),
     )
     far_three, far_one = held((far_three, far_one), (ffn_terms[2], ffn_terms[4]))
-    own_ffn, first_plane, *planes = scatter_unpack(ffn_pieces, ffn_terms, 0, (near_one,))
+    own_ffn, *planes = scatter_unpack(ffn_pieces, ffn_terms, 0, (near_one,))
     far_three, far_one = scatter_cores(far_three, far_one)
-    terms, sent = scatter_direct(
-        attention_pieces, near_three, near_one, far_three, far_one, (first_plane,)
-    )
-    planes = [first_plane, *held(planes, (sent,))]
+    terms = scatter_direct(
+        attention_pieces, near_three, near_one, far_three, far_one, (own_ffn,)
+    )
     arrived = [swap(plane, step * LOW_COUNT) for step, plane in enumerate(planes, start=1)]
     grads_ffn = own_ffn + sum(value.astype(jnp.float32) for value in arrived)
     own_attention, *planes = scatter_unpack(attention_pieces, terms, GAIN_ROWS, arrived)

time: 221 us -> 225 us (1.018)
  Pallas kernels: 71.9 us -> 75.3 us
    pallas_call x17 -> x18, Pallas kernels: 71.9 us -> 75.3 us  [local_call(): pl.pallas_call(body, out_shape=outs, in_specs=specs, out_specs=tuple((pl....]
    unnamed x118 -> x120, local copies, waits for them, and re-layouts: 15.4 us -> 14.8 us
  transfers between devices with their start and end apart: 51 -> 51, of which waited for: 20 -> 19; matrix products, arithmetic and copies ran while one was open for 5% -> 4% of each run, Pallas kernels for 25% -> 26%
where the time goes in v14:
time: 225 us; the launch traced here: 224 us
  Pallas kernels  75.3 us (33%)
  waiting for transfers between devices  70.6 us (31%)
  starting transfers between devices  50 us (22%)
  local copies, waits for them, and re-layouts  18.8 us (8%)
  other arithmetic  8.41 us (4%)
    pallas_call x18, Pallas kernels, local_call(): pl.pallas_call(body, out_shape=outs, in_specs=specs, out_specs=tuple((pl....  75.3 us
    ppermute x51, waiting for transfers between devices, swap(): lax.ppermute(value, ALL_AXES, [(source, source ^ mask) for source in rang...  70.6 us
    ppermute x51, starting transfers between devices, swap(): lax.ppermute(value, ALL_AXES, [(source, source ^ mask) for source in rang...  50 us
    unnamed x120, local copies, waits for them, and re-layouts  14.8 us
  transfers between devices with their start and end apart: 51, of which 19 were waited for; matrix products, arithmetic and copies ran while one was open for 4% of the time, Pallas kernels for 26%

profile of v14, /device:TPU:0, one launch (start us, length us, event | category | flops | bytes accessed | tf_op | source)
XLA Modules:
  0.0 224.2 jit_solution(4054078782535892375)
XLA Ops:
  1.8 3.1 %collective-permute-start.3 = (bf16[960,128]{1,0:T(8,128)(2,1)S(1)}, bf16[960,128]{1,0:T(8,128)(2,1)S(1)}, u32[]{:S(2)}, u32[]{:S(2)}) collective-permute-start(bf16[960,128]{1,0:T(8,128)(2,1)S(1)} %slice.70.refs_1_), channel_id=1, source_target_pairs={{0,8},{1,9},{2,10},{3,11},{4,12},{5,13},{6,14},{7,15},{8,0},{9,1},... | collective-permute-start | bytes 737288 | tf_op jit(solution)/shard_map/ppermute | solution.py:127
  4.9 2.5 %collective-permute-start.2 = (bf16[400,128]{1,0:T(8,128)(2,1)S(1)}, bf16[400,128]{1,0:T(8,128)(2,1)S(1)}, u32[]{:S(2)}, u32[]{:S(2)}) collective-permute-start(bf16[400,128]{1,0:T(8,128)(2,1)S(1)} %slice.69.refs_1_), channel_id=1, source_target_pairs={{0,24},{1,25},{2,26},{3,27},{4,28},{5,29},{6,30},{7,31},{8,16},{9,... | collective-permute-start | bytes 307208 | tf_op jit(solution)/shard_map/ppermute | solution.py:127
  9.4 2.5 %collective-permute-start.8 = (bf16[960,128]{1,0:T(8,128)(2,1)S(1)}, bf16[960,128]{1,0:T(8,128)(2,1)S(1)}, u32[]{:S(2)}, u32[]{:S(2)}) collective-permute-start(bf16[960,128]{1,0:T(8,128)(2,1)S(1)} %slice.70.refs_1_), channel_id=1, source_target_pairs={{0,24},{1,25},{2,26},{3,27},{4,28},{5,29},{6,30},{7,31},{8,16},{9,... | collective-permute-start | bytes 737288 | tf_op jit(solution)/shard_map/ppermute | solution.py:127
  12.5 4.0 %collective-permute-done.2.refs_4_ = bf16[400,128]{1,0:T(8,128)(2,1)S(1)} collective-permute-done((bf16[400,128]{1,0:T(8,128)(2,1)S(1)}, bf16[400,128]{1,0:T(8,128)(2,1)S(1)}, u32[]{:S(2)}, u32[]{:S(2)}) %collective-permute-start.2) | collective-permute-done | bytes 102432 | tf_op jit(solution)/shard_map/ppermute | solution.py:127
  16.5 2.0 collective-permute-done.1.refs_3_
  19.3 2.0 shard_map.152.refs_0_
  21.2 2.4 %collective-permute-start.6 = (bf16[1600,128]{1,0:T(8,128)(2,1)}, bf16[1600,128]{1,0:T(8,128)(2,1)S(1)}, u32[]{:S(2)}, u32[]{:S(2)}) collective-permute-start(bf16[1600,128]{1,0:T(8,128)(2,1)} %shard_map.152.refs_0_), channel_id=1, source_target_pairs={{0,6},{1,7},{2,4},{3,5},{4,2},{5,3},{6,0},{7,1},{8,14},{9,15},{10,... | collective-permute-start | bytes 1228808 | tf_op jit(solution)/shard_map/ppermute | solution.py:127
  26.2 11.8 %collective-permute-done.7.refs_4_.refs_3_ = bf16[960,128]{1,0:T(8,128)(2,1)S(1)} collective-permute-done((bf16[960,128]{1,0:T(8,128)(2,1)S(1)}, bf16[960,128]{1,0:T(8,128)(2,1)S(1)}, u32[]{:S(2)}, u32[]{:S(2)}) %collective-permute-start.7) | collective-permute-done | bytes 245792 | tf_op jit(solution)/shard_map/ppermute | solution.py:127
  43.3 2.9 %shard_map.156 = (bf16[1920,128]{1,0:T(8,128)(2,1)}, bf16[1920,128]{1,0:T(8,128)(2,1)}) custom-call(s32[1]{0:T(128)} %bitcast.refs_0_, bf16[960,128]{1,0:T(8,128)(2,1)} %copy-done.25, bf16[960,128]{1,0:T(8,128)(2,1)} %copy-done.26, bf16[960,128]{1,0:T(8,128)(2,1)} %copy-done.28, bf16[960,128]{1,0:T(8,128)(2,1)} %copy-done.27, ...), custom_call_target="tpu_custom_call" | custom-call | tf_op jit(solution)/shard_map/pallas_call | solution.py:139
  51.9 3.9 %shard_map.154 = (bf16[128,640]{1,0:T(8,128)(2,1)}, f32[128,1024]{1,0:T(8,128)}, f32[128,256]{1,0:T(8,128)}, bf16[128,1024]{1,0:T(8,128)(2,1)}, bf16[128,512]{1,0:T(8,128)(2,1)}) custom-call(s32[1]{0:T(128)} %bitcast.refs_0_, bf16[128,640]{1,0:T(8,128)(2,1)} %refs_1_.5, f32[1,640]{1,0:T(1,128)} %broadcast_in_dim.30.refs_2_, f32[1,256]{1,0:T(1,128)} %bitcast.29, ...), custom_call_target="tpu_custom_call" | custom-call | tf_op jit(solution)/shard_map/pallas_call | solution.py:139
  57.7 2.2 collective-permute-done.18.refs_10_
  62.1 3.1 %collective-permute-done.14.refs_15_.refs_3_.refs_10_ = bf16[128,512]{1,0:T(8,128)(2,1)S(1)} collective-permute-done((bf16[128,512]{1,0:T(8,128)(2,1)}, bf16[128,512]{1,0:T(8,128)(2,1)S(1)}, u32[]{:S(2)}, u32[]{:S(2)}) %collective-permute-start.14) | collective-permute-done | bytes 131104 | tf_op jit(solution)/shard_map/ppermute | solution.py:127
  74.2 8.5 %collective-permute-done.21.refs_1_ = bf16[1920,128]{1,0:T(8,128)(2,1)S(1)} collective-permute-done((bf16[1920,128]{1,0:T(8,128)(2,1)}, bf16[1920,128]{1,0:T(8,128)(2,1)S(1)}, u32[]{:S(2)}, u32[]{:S(2)}) %collective-permute-start.21) | collective-permute-done | bytes 491552 | tf_op jit(solution)/shard_map/ppermute | solution.py:127
  84.2 5.7 %shard_map.155 = (f32[128,2048]{1,0:T(8,128)}, bf16[128,1024]{1,0:T(8,128)(2,1)}, f32[128,640]{1,0:T(8,128)}, f32[128,640]{1,0:T(8,128)}, bf16[1024,640]{1,0:T(8,128)(2,1)}) custom-call(s32[1]{0:T(128)} %bitcast.refs_0_, bf16[128,640]{1,0:T(8,128)(2,1)} %refs_1_.5, f32[1,640]{1,0:T(1,128)} %broadcast_in_dim.14.refs_2_.refs_3_, f32[128,512]{1,0:T(8,128)} %fusion.4.refs_3_, ...), custom_call_target="tpu_custom_call" | custom-call | tf_op jit(solution)/shard_map/pallas_call | solution.py:139
  97.1 14.8 %shard_map.160 = (bf16[128,640]{1,0:T(8,128)(2,1)}, f32[128,640]{1,0:T(8,128)}, f32[1,640]{1,0:T(1,128)}, f32[1,640]{1,0:T(1,128)}, bf16[11520,128]{1,0:T(8,128)...) custom-call(s32[1]{0:T(128)} %bitcast.refs_0_, ...), custom_call_target="tpu_custom_call" | custom-call | tf_op jit(solution)/shard_map/pallas_call | solution.py:139
  112.5 6.5 %collective-permute-done.30.refs_2_ = bf16[3840,128]{1,0:T(8,128)(2,1)S(1)} collective-permute-done((bf16[3840,128]{1,0:T(8,128)(2,1)}, bf16[3840,128]{1,0:T(8,128)(2,1)S(1)}, u32[]{:S(2)}, u32[]{:S(2)}) %collective-permute-start.30) | collective-permute-done | bytes 983072 | tf_op jit(solution)/shard_map/ppermute | solution.py:127
  119.9 2.6 %shard_map.161 = (bf16[1920,128]{1,0:T(8,128)(2,1)}, bf16[1920,128]{1,0:T(8,128)(2,1)}) custom-call(s32[1]{0:T(128)} %bitcast.refs_0_, bf16[3840,128]{1,0:T(8,128)(2,1)} %get-tuple-element.94.refs_1_, bf16[3840,128]{1,0:T(8,128)(2,1)} %copy-done.24), custom_call_target="tpu_custom_call" | custom-call | tf_op jit(solution)/shard_map/pallas_call | solution.py:139
  127.0 5.8 %shard_map.162 = (bf16[1024,640]{1,0:T(8,128)(2,1)}, f32[128,1024]{1,0:T(8,128)}, f32[1,640]{1,0:T(1,128)}, f32[128,512]{1,0:T(8,128)}, f32[128,512]{1,0:T(8,128)}, /*index=5*/bf16[256,512]{1,0:T(8,128)(2,1)}) custom-call(s32[1]{0:T(128)} %bitcast.refs_0_, f32[128,640]{1,0:T(8,128)} %get-tuple-element.89.refs_1_.refs_10_, ...), custom_call_target="tpu_custom_call" | custom-call | tf_op jit(solution)/shard_map/pallas_call | solution.py:139
  136.2 3.9 %shard_map.163 = (bf16[1920,128]{1,0:T(8,128)(2,1)}, bf16[2432,128]{1,0:T(8,128)(2,1)}) custom-call(s32[1]{0:T(128)} %bitcast.refs_0_, bf16[11520,128]{1,0:T(8,128)(2,1)} %get-tuple-element.98.refs_1_, bf16[11520,128]{1,0:T(8,128)(2,1)} %copy-done.3, f32[128,512]{1,0:T(8,128)} %get-tuple-element.100.refs_3_, bf16[256,512]{1,0:T(8,128)(2,1)} %copy-done.23), custom_call_target="tpu_custom_call" | custom-call | tf_op jit(solution)/shard_map/pallas_call | solution.py:139
  142.1 4.1 %shard_map.164 = (bf16[1920,128]{1,0:T(8,128)(2,1)}, bf16[1920,128]{1,0:T(8,128)(2,1)}, bf16[1920,128]{1,0:T(8,128)(2,1)}, bf16[1920,128]{1,0:T(8,128)(2,1)}) custom-call(s32[1]{0:T(128)} %bitcast.refs_0_, bf16[11520,128]{1,0:T(8,128)(2,1)} %get-tuple-element.98.refs_1_, bf16[11520,128]{1,0:T(8,128)(2,1)} %copy-done.3, ...), custom_call_target="tpu_custom_call" | custom-call | tf_op jit(solution)/shard_map/pallas_call | solution.py:139
  147.2 2.5 %shard_map.166 = (bf16[1920,128]{1,0:T(8,128)(2,1)}, bf16[1920,128]{1,0:T(8,128)(2,1)}) custom-call(s32[1]{0:T(128)} %bitcast.refs_0_, bf16[1920,128]{1,0:T(8,128)(2,1)} %get-tuple-element.111.refs_1_, bf16[1920,128]{1,0:T(8,128)(2,1)} %get-tuple-element.112.refs_2_, bf16[1920,128]{1,0:T(8,128)(2,1)} %copy-done.38, bf16[1920,128]{1,0:T(8,128)(2,1)} %copy-done.37), custom_call_target="tpu_custom_call" | custom-call | tf_op jit(solution)/shard_map/pallas_call | solution.py:139
  151.8 4.5 %shard_map.165 = (bf16[640,1024]{1,0:T(8,128)(2,1)}, f32[128,640]{1,0:T(8,128)}, f32[1,256]{1,0:T(1,128)}) custom-call(s32[1]{0:T(128)} %bitcast.refs_0_, f32[1,256]{1,0:T(1,128)} %bitcast.30, f32[128,128]{1,0:T(8,128)} %get-tuple-element.157.refs_5_.refs_2_.refs_4_, f32[128,128]{1,0:T(8,128)} %get-tuple-element.156.refs_6_.refs_3_.refs_5_, ...), custom_call_target="tpu_custom_call" | custom-call | tf_op jit(solution)/shard_map/pallas_call | solution.py:139
  158.0 4.7 %shard_map.167 = (bf16[640,512]{1,0:T(8,128)(2,1)}, bf16[128,640]{1,0:T(8,128)(2,1)}, f32[32,128]{1,0:T(8,128)}) custom-call(s32[1]{0:T(128)} %bitcast.refs_0_, bf16[128,640]{1,0:T(8,128)(2,1)} %refs_1_.5, f32[1,640]{1,0:T(1,128)} %broadcast_in_dim.30.refs_2_, f32[1,256]{1,0:T(1,128)} %bitcast.28, f32[128,128]{1,0:T(8,128)} %get-tuple-element.157.refs_5_.refs_2_.refs_4_, ...), custom_call_target="tpu_custom_call" | custom-call | tf_op jit(solution)/shard_map/pallas_call | solution.py:139
  162.7 4.3 %shard_map.168 = (bf16[4800,128]{1,0:T(8,128)(2,1)}, bf16[1632,128]{1,0:T(8,128)(2,1)}, bf16[4800,128]{1,0:T(8,128)(2,1)}, bf16[1632,128]{1,0:T(8,128)(2,1)}) custom-call(s32[1]{0:T(128)} %bitcast.refs_0_, bf16[640,1024]{1,0:T(8,128)(2,1)} %get-tuple-element.116.refs_1_, bf16[640,512]{1,0:T(8,128)(2,1)} %get-tuple-element.117.refs_2_, ...), custom_call_target="tpu_custom_call" | custom-call | tf_op jit(solution)/shard_map/pallas_call | solution.py:139
  168.4 4.2 %shard_map.170 = (f32[960,128]{1,0:T(8,128)}, bf16[960,128]{1,0:T(8,128)(2,1)}, bf16[960,128]{1,0:T(8,128)(2,1)}, bf16[960,128]{1,0:T(8,128)(2,1)}) custom-call(s32[1]{0:T(128)} %bitcast.refs_0_, bf16[1920,128]{1,0:T(8,128)(2,1)} %get-tuple-element.103.refs_15_.refs_1_, bf16[1920,128]{1,0:T(8,128)(2,1)} %copy-done.16, bf16[1920,128]{1,0:T(8,128)(2,1)} %copy-done.10, ...), custom_call_target="tpu_custom_call" | custom-call | tf_op jit(solution)/shard_map/pallas_call | solution.py:139
  172.6 2.4 %collective-permute-start.45 = (bf16[960,128]{1,0:T(8,128)(2,1)}, bf16[960,128]{1,0:T(8,128)(2,1)S(1)}, u32[]{:S(2)}, u32[]{:S(2)}) collective-permute-start(bf16[960,128]{1,0:T(8,128)(2,1)} %get-tuple-element.133), channel_id=1, source_target_pairs={{0,8},{1,9},{2,10},{3,11},{4,12},{5,13},{6,14},{7,15},{8,0},{9,1},... | collective-permute-start | bytes 737288 | tf_op jit(solution)/shard_map/ppermute | solution.py:127
  176.1 3.2 %shard_map.171 = (bf16[1632,128]{1,0:T(8,128)(2,1)}, bf16[1632,128]{1,0:T(8,128)(2,1)}, bf16[1632,128]{1,0:T(8,128)(2,1)}, bf16[1632,128]{1,0:T(8,128)(2,1)}) custom-call(s32[1]{0:T(128)} %bitcast.refs_0_, bf16[4800,128]{1,0:T(8,128)(2,1)} %get-tuple-element.120.refs_1_, bf16[1632,128]{1,0:T(8,128)(2,1)} %get-tuple-element.121.refs_7_.refs_2_, ...), custom_call_target="tpu_custom_call" | custom-call | tf_op jit(solution)/shard_map/pallas_call | solution.py:139
  182.8 2.0 collective-permute-start.46
  185.4 15.5 %collective-permute-done.46.refs_6_ = bf16[960,128]{1,0:T(8,128)(2,1)S(1)} collective-permute-done((bf16[960,128]{1,0:T(8,128)(2,1)S(1)}, bf16[960,128]{1,0:T(8,128)(2,1)S(1)}, u32[]{:S(2)}, u32[]{:S(2)}) %collective-permute-start.46) | collective-permute-done | bytes 245792 | tf_op jit(solution)/shard_map/ppermute | solution.py:127
  202.2 2.6 %shard_map.172 = (f32[432,128]{1,0:T(8,128)}, bf16[432,128]{1,0:T(8,128)(2,1)}, bf16[432,128]{1,0:T(8,128)(2,1)}, bf16[432,128]{1,0:T(8,128)(2,1)}) custom-call(s32[1]{0:T(128)} %bitcast.refs_0_, bf16[1632,128]{1,0:T(8,128)(2,1)} %get-tuple-element.129.refs_1_, bf16[1632,128]{1,0:T(8,128)(2,1)} %copy-done.44, bf16[1632,128]{1,0:T(8,128)(2,1)} %copy-done.45, ...), custom_call_target="tpu_custom_call" | custom-call | tf_op jit(solution)/shard_map/pallas_call | solution.py:139
  204.8 5.7 %collective-permute-start.48 = (bf16[432,128]{1,0:T(8,128)(2,1)}, bf16[432,128]{1,0:T(8,128)(2,1)S(1)}, u32[]{:S(2)}, u32[]{:S(2)}) collective-permute-start(bf16[432,128]{1,0:T(8,128)(2,1)} %get-tuple-element.137), channel_id=1, source_target_pairs={{0,8},{1,9},{2,10},{3,11},{4,12},{5,13},{6,14},{7,15},{8,0},{9,1},... | collective-permute-start | bytes 331784 | tf_op jit(solution)/shard_map/ppermute | solution.py:127
  214.5 7.3 %collective-permute-done.49 = bf16[432,128]{1,0:T(8,128)(2,1)S(1)} collective-permute-done((bf16[432,128]{1,0:T(8,128)(2,1)}, bf16[432,128]{1,0:T(8,128)(2,1)S(1)}, u32[]{:S(2)}, u32[]{:S(2)}) %collective-permute-start.49) | collective-permute-done | bytes 110624 | tf_op jit(solution)/shard_map/ppermute | solution.py:127
  (245 shorter events, 70.1 us)
Async XLA Ops:
  1.8 16.7 %collective-permute-start.3 = (bf16[960,128]{1,0:T(8,128)(2,1)S(1)}, bf16[960,128]{1,0:T(8,128)(2,1)S(1)}, u32[]{:S(2)}, u32[]{:S(2)}) collective-permute-start(bf16[960,128]{1,0:T(8,128)(2,1)S(1)} %slice.70.refs_1_), channel_id=1, source_target_pairs={{0,8},{1,9},{2,10},{3,11},{4,12},{5,13},{6,14},{7,15},{8,0},{9,1},... | collective-permute-start | bytes 737288 | tf_op jit(solution)/shard_map/ppermute | solution.py:127
  4.9 11.5 %collective-permute-start.2 = (bf16[400,128]{1,0:T(8,128)(2,1)S(1)}, bf16[400,128]{1,0:T(8,128)(2,1)S(1)}, u32[]{:S(2)}, u32[]{:S(2)}) collective-permute-start(bf16[400,128]{1,0:T(8,128)(2,1)S(1)} %slice.69.refs_1_), channel_id=1, source_target_pairs={{0,24},{1,25},{2,26},{3,27},{4,28},{5,29},{6,30},{7,31},{8,16},{9,... | collective-permute-start | bytes 307208 | tf_op jit(solution)/shard_map/ppermute | solution.py:127
  7.5 11.0 %collective-permute-start.1 = (bf16[400,128]{1,0:T(8,128)(2,1)S(1)}, bf16[400,128]{1,0:T(8,128)(2,1)S(1)}, u32[]{:S(2)}, u32[]{:S(2)}) collective-permute-start(bf16[400,128]{1,0:T(8,128)(2,1)S(1)} %slice.69.refs_1_), channel_id=1, source_target_pairs={{0,16},{1,17},{2,18},{3,19},{4,20},{5,21},{6,22},{7,23},{8,24},{9,... | collective-permute-start | bytes 307208 | tf_op jit(solution)/shard_map/ppermute | solution.py:127
  7.7 10.8 %collective-permute-start = (bf16[400,128]{1,0:T(8,128)(2,1)S(1)}, bf16[400,128]{1,0:T(8,128)(2,1)S(1)}, u32[]{:S(2)}, u32[]{:S(2)}) collective-permute-start(bf16[400,128]{1,0:T(8,128)(2,1)S(1)} %slice.69.refs_1_), channel_id=1, source_target_pairs={{0,8},{1,9},{2,10},{3,11},{4,12},{5,13},{6,14},{7,15},{8,0},{9,1},... | collective-permute-start | bytes 307208 | tf_op jit(solution)/shard_map/ppermute | solution.py:127
  9.4 16.8 %collective-permute-start.8 = (bf16[960,128]{1,0:T(8,128)(2,1)S(1)}, bf16[960,128]{1,0:T(8,128)(2,1)S(1)}, u32[]{:S(2)}, u32[]{:S(2)}) collective-permute-start(bf16[960,128]{1,0:T(8,128)(2,1)S(1)} %slice.70.refs_1_), channel_id=1, source_target_pairs={{0,24},{1,25},{2,26},{3,27},{4,28},{5,29},{6,30},{7,31},{8,16},{9,... | collective-permute-start | bytes 737288 | tf_op jit(solution)/shard_map/ppermute | solution.py:127
  16.5 21.5 %collective-permute-start.7 = (bf16[960,128]{1,0:T(8,128)(2,1)S(1)}, bf16[960,128]{1,0:T(8,128)(2,1)S(1)}, u32[]{:S(2)}, u32[]{:S(2)}) collective-permute-start(bf16[960,128]{1,0:T(8,128)(2,1)S(1)} %slice.70.refs_1_), channel_id=1, source_target_pairs={{0,16},{1,17},{2,18},{3,19},{4,20},{5,21},{6,22},{7,23},{8,24},{9,... | collective-permute-start | bytes 737288 | tf_op jit(solution)/shard_map/ppermute | solution.py:127
  21.2 16.7 %collective-permute-start.6 = (bf16[1600,128]{1,0:T(8,128)(2,1)}, bf16[1600,128]{1,0:T(8,128)(2,1)S(1)}, u32[]{:S(2)}, u32[]{:S(2)}) collective-permute-start(bf16[1600,128]{1,0:T(8,128)(2,1)} %shard_map.152.refs_0_), channel_id=1, source_target_pairs={{0,6},{1,7},{2,4},{3,5},{4,2},{5,3},{6,0},{7,1},{8,14},{9,15},{10,... | collective-permute-start | bytes 1228808 | tf_op jit(solution)/shard_map/ppermute | solution.py:127
  23.7 16.1 %collective-permute-start.5 = (bf16[1600,128]{1,0:T(8,128)(2,1)}, bf16[1600,128]{1,0:T(8,128)(2,1)S(1)}, u32[]{:S(2)}, u32[]{:S(2)}) collective-permute-start(bf16[1600,128]{1,0:T(8,128)(2,1)} %shard_map.152.refs_0_), channel_id=1, source_target_pairs={{0,2},{1,3},{2,0},{3,1},{4,6},{5,7},{6,4},{7,5},{8,10},{9,11},{10,... | collective-permute-start | bytes 1228808 | tf_op jit(solution)/shard_map/ppermute | solution.py:127
  24.2 15.6 %collective-permute-start.4 = (bf16[1600,128]{1,0:T(8,128)(2,1)}, bf16[1600,128]{1,0:T(8,128)(2,1)S(1)}, u32[]{:S(2)}, u32[]{:S(2)}) collective-permute-start(bf16[1600,128]{1,0:T(8,128)(2,1)} %shard_map.152.refs_0_), channel_id=1, source_target_pairs={{0,4},{1,5},{2,6},{3,7},{4,0},{5,1},{6,2},{7,3},{8,12},{9,13},{10,... | collective-permute-start | bytes 1228808 | tf_op jit(solution)/shard_map/ppermute | solution.py:127
  46.2 13.7 %collective-permute-start.18 = (bf16[1920,128]{1,0:T(8,128)(2,1)}, bf16[1920,128]{1,0:T(8,128)(2,1)S(1)}, u32[]{:S(2)}, u32[]{:S(2)}) collective-permute-start(bf16[1920,128]{1,0:T(8,128)(2,1)} %get-tuple-element.81.refs_1_.refs_6_), channel_id=1, source_target_pairs={{0,2},{1,3},{2,0},{3,1},{4,6},{5,7},{6,4},{7,5},{8,10},{9,11},{10,... | collective-permute-start | bytes 1474568 | tf_op jit(solution)/shard_map/ppermute | solution.py:127
  47.6 14.0 %collective-permute-start.17 = (bf16[1920,128]{1,0:T(8,128)(2,1)}, bf16[1920,128]{1,0:T(8,128)(2,1)S(1)}, u32[]{:S(2)}, u32[]{:S(2)}) collective-permute-start(bf16[1920,128]{1,0:T(8,128)(2,1)} %get-tuple-element.82.refs_7_), channel_id=1, source_target_pairs={{0,4},{1,5},{2,6},{3,7},{4,0},{5,1},{6,2},{7,3},{8,12},{9,13},{10,... | collective-permute-start | bytes 1474568 | tf_op jit(solution)/shard_map/ppermute | solution.py:127
  59.9 12.9 %collective-permute-start.20 = (bf16[1920,128]{1,0:T(8,128)(2,1)S(1)}, bf16[1920,128]{1,0:T(8,128)(2,1)S(1)}, u32[]{:S(2)}, u32[]{:S(2)}) collective-permute-start(bf16[1920,128]{1,0:T(8,128)(2,1)S(1)} %collective-permute-done.18.refs_10_), channel_id=1, source_target_pairs={{0,4},{1,5},{2,6},{3,7},{4,0},{5,1},{6,2},{7,3},{8,12},{9,13},{10,... | collective-permute-start | bytes 1474568 | tf_op jit(solution)/shard_map/ppermute | solution.py:127
  68.3 14.3 %collective-permute-start.21 = (bf16[1920,128]{1,0:T(8,128)(2,1)}, bf16[1920,128]{1,0:T(8,128)(2,1)S(1)}, u32[]{:S(2)}, u32[]{:S(2)}) collective-permute-start(bf16[1920,128]{1,0:T(8,128)(2,1)} %shard_map.158), channel_id=1, source_target_pairs={{0,2},{1,3},{2,0},{3,1},{4,6},{5,7},{6,4},{7,5},{8,10},{9,11},{10,... | collective-permute-start | bytes 1474568 | tf_op jit(solution)/shard_map/ppermute | solution.py:127
  69.8 20.1 %collective-permute-start.22 = (bf16[1920,128]{1,0:T(8,128)(2,1)S(1)}, bf16[1920,128]{1,0:T(8,128)(2,1)S(1)}, u32[]{:S(2)}, u32[]{:S(2)}) collective-permute-start(bf16[1920,128]{1,0:T(8,128)(2,1)S(1)} %copy-done.12), channel_id=1, source_target_pairs={{0,1},{1,0},{2,3},{3,2},{4,5},{5,4},{6,7},{7,6},{8,9},{9,8},{10,11... | collective-permute-start | bytes 1474568 | tf_op jit(solution)/shard_map/ppermute | solution.py:127
  69.9 22.7 %collective-permute-start.23 = (bf16[1920,128]{1,0:T(8,128)(2,1)S(1)}, bf16[1920,128]{1,0:T(8,128)(2,1)}, u32[]{:S(2)}, u32[]{:S(2)}) collective-permute-start(bf16[1920,128]{1,0:T(8,128)(2,1)S(1)} %copy-done.34), channel_id=1, source_target_pairs={{0,1},{1,0},{2,3},{3,2},{4,5},{5,4},{6,7},{7,6},{8,9},{9,8},{10,11... | collective-permute-start | bytes 1474568 | tf_op jit(solution)/shard_map/ppermute | solution.py:127
  70.4 21.7 %collective-permute-start.19 = (bf16[1920,128]{1,0:T(8,128)(2,1)S(1)}, bf16[1920,128]{1,0:T(8,128)(2,1)}, u32[]{:S(2)}, u32[]{:S(2)}) collective-permute-start(bf16[1920,128]{1,0:T(8,128)(2,1)S(1)} %copy-done.34), channel_id=1, source_target_pairs={{0,2},{1,3},{2,0},{3,1},{4,6},{5,7},{6,4},{7,5},{8,10},{9,11},{10,... | collective-permute-start | bytes 1474568 | tf_op jit(solution)/shard_map/ppermute | solution.py:127
  72.8 19.2 %collective-permute-start.16 = (bf16[1920,128]{1,0:T(8,128)(2,1)}, bf16[1920,128]{1,0:T(8,128)(2,1)}, u32[]{:S(2)}, u32[]{:S(2)}) collective-permute-start(bf16[1920,128]{1,0:T(8,128)(2,1)} %shard_map.157), channel_id=1, source_target_pairs={{0,4},{1,5},{2,6},{3,7},{4,0},{5,1},{6,2},{7,3},{8,12},{9,13},{10,... | collective-permute-start | bytes 1474568 | tf_op jit(solution)/shard_map/ppermute | solution.py:127
  111.9 22.6 %collective-permute-start.32 = (bf16[11520,128]{1,0:T(8,128)(2,1)}, bf16[11520,128]{1,0:T(8,128)(2,1)S(1)}, u32[]{:S(2)}, u32[]{:S(2)}) collective-permute-start(bf16[11520,128]{1,0:T(8,128)(2,1)} %get-tuple-element.99), channel_id=1, source_target_pairs={{0,1},{1,0},{2,3},{3,2},{4,5},{5,4},{6,7},{7,6},{8,9},{9,8},{10,11... | collective-permute-start | bytes 8847368 | tf_op jit(solution)/shard_map/ppermute | solution.py:127
  122.5 23.7 %collective-permute-start.36 = (bf16[1920,128]{1,0:T(8,128)(2,1)}, bf16[1920,128]{1,0:T(8,128)(2,1)S(1)}, u32[]{:S(2)}, u32[]{:S(2)}) collective-permute-start(bf16[1920,128]{1,0:T(8,128)(2,1)} %get-tuple-element.113), channel_id=1, source_target_pairs={{0,2},{1,3},{2,0},{3,1},{4,6},{5,7},{6,4},{7,5},{8,10},{9,11},{10,... | collective-permute-start | bytes 1474568 | tf_op jit(solution)/shard_map/ppermute | solution.py:127
  123.6 22.6 %collective-permute-start.35 = (bf16[1920,128]{1,0:T(8,128)(2,1)}, bf16[1920,128]{1,0:T(8,128)(2,1)S(1)}, u32[]{:S(2)}, u32[]{:S(2)}) collective-permute-start(bf16[1920,128]{1,0:T(8,128)(2,1)} %get-tuple-element.96), channel_id=1, source_target_pairs={{0,4},{1,5},{2,6},{3,7},{4,0},{5,1},{6,2},{7,3},{8,12},{9,13},{10,... | collective-permute-start | bytes 1474568 | tf_op jit(solution)/shard_map/ppermute | solution.py:127
  140.0 17.1 %collective-permute-start.34 = (bf16[2432,128]{1,0:T(8,128)(2,1)}, bf16[2432,128]{1,0:T(8,128)(2,1)S(1)}, u32[]{:S(2)}, u32[]{:S(2)}) collective-permute-start(bf16[2432,128]{1,0:T(8,128)(2,1)} %get-tuple-element.110), channel_id=1, source_target_pairs={{0,2},{1,3},{2,0},{3,1},{4,6},{5,7},{6,4},{7,5},{8,10},{9,11},{10,... | collective-permute-start | bytes 1867784 | tf_op jit(solution)/shard_map/ppermute | solution.py:127
  141.2 15.1 %collective-permute-start.37 = (bf16[1920,128]{1,0:T(8,128)(2,1)}, bf16[1920,128]{1,0:T(8,128)(2,1)S(1)}, u32[]{:S(2)}, u32[]{:S(2)}) collective-permute-start(bf16[1920,128]{1,0:T(8,128)(2,1)} %get-tuple-element.102.refs_3_), channel_id=1, source_target_pairs={{0,4},{1,5},{2,6},{3,7},{4,0},{5,1},{6,2},{7,3},{8,12},{9,13},{10,... | collective-permute-start | bytes 1474568 | tf_op jit(solution)/shard_map/ppermute | solution.py:127
  149.8 17.2 %collective-permute-start.38 = (bf16[1920,128]{1,0:T(8,128)(2,1)}, bf16[1920,128]{1,0:T(8,128)(2,1)S(1)}, u32[]{:S(2)}, u32[]{:S(2)}) collective-permute-start(bf16[1920,128]{1,0:T(8,128)(2,1)} %get-tuple-element.124), channel_id=1, source_target_pairs={{0,2},{1,3},{2,0},{3,1},{4,6},{5,7},{6,4},{7,5},{8,10},{9,11},{10,... | collective-permute-start | bytes 1474568 | tf_op jit(solution)/shard_map/ppermute | solution.py:127
  150.9 16.1 %collective-permute-start.39 = (bf16[1920,128]{1,0:T(8,128)(2,1)}, bf16[1920,128]{1,0:T(8,128)(2,1)S(1)}, u32[]{:S(2)}, u32[]{:S(2)}) collective-permute-start(bf16[1920,128]{1,0:T(8,128)(2,1)} %get-tuple-element.114.refs_26_), channel_id=1, source_target_pairs={{0,4},{1,5},{2,6},{3,7},{4,0},{5,1},{6,2},{7,3},{8,12},{9,13},{10,... | collective-permute-start | bytes 1474568 | tf_op jit(solution)/shard_map/ppermute | solution.py:127
  172.6 12.2 %collective-permute-start.45 = (bf16[960,128]{1,0:T(8,128)(2,1)}, bf16[960,128]{1,0:T(8,128)(2,1)S(1)}, u32[]{:S(2)}, u32[]{:S(2)}) collective-permute-start(bf16[960,128]{1,0:T(8,128)(2,1)} %get-tuple-element.133), channel_id=1, source_target_pairs={{0,8},{1,9},{2,10},{3,11},{4,12},{5,13},{6,14},{7,15},{8,0},{9,1},... | collective-permute-start | bytes 737288 | tf_op jit(solution)/shard_map/ppermute | solution.py:127
  179.3 21.6 %collective-permute-start.42 = (bf16[1632,128]{1,0:T(8,128)(2,1)}, bf16[1632,128]{1,0:T(8,128)(2,1)S(1)}, u32[]{:S(2)}, u32[]{:S(2)}) collective-permute-start(bf16[1632,128]{1,0:T(8,128)(2,1)} %get-tuple-element.130), channel_id=1, source_target_pairs={{0,4},{1,5},{2,6},{3,7},{4,0},{5,1},{6,2},{7,3},{8,12},{9,13},{10,... | collective-permute-start | bytes 1253384 | tf_op jit(solution)/shard_map/ppermute | solution.py:127
  180.6 20.4 %collective-permute-start.43 = (bf16[1632,128]{1,0:T(8,128)(2,1)}, bf16[1632,128]{1,0:T(8,128)(2,1)S(1)}, u32[]{:S(2)}, u32[]{:S(2)}) collective-permute-start(bf16[1632,128]{1,0:T(8,128)(2,1)} %get-tuple-element.131), channel_id=1, source_target_pairs={{0,2},{1,3},{2,0},{3,1},{4,6},{5,7},{6,4},{7,5},{8,10},{9,11},{10,... | collective-permute-start | bytes 1253384 | tf_op jit(solution)/shard_map/ppermute | solution.py:127
  181.4 19.6 %collective-permute-start.44 = (bf16[1632,128]{1,0:T(8,128)(2,1)}, bf16[1632,128]{1,0:T(8,128)(2,1)S(1)}, u32[]{:S(2)}, u32[]{:S(2)}) collective-permute-start(bf16[1632,128]{1,0:T(8,128)(2,1)} %get-tuple-element.132), channel_id=1, source_target_pairs={{0,6},{1,7},{2,4},{3,5},{4,2},{5,3},{6,0},{7,1},{8,14},{9,15},{10,... | collective-permute-start | bytes 1253384 | tf_op jit(solution)/shard_map/ppermute | solution.py:127
  182.8 18.1 %collective-permute-start.46 = (bf16[960,128]{1,0:T(8,128)(2,1)S(1)}, bf16[960,128]{1,0:T(8,128)(2,1)S(1)}, u32[]{:S(2)}, u32[]{:S(2)}) collective-permute-start(bf16[960,128]{1,0:T(8,128)(2,1)S(1)} %copy-done.59), channel_id=1, source_target_pairs={{0,16},{1,17},{2,18},{3,19},{4,20},{5,21},{6,22},{7,23},{8,24},{9,... | collective-permute-start | bytes 737288 | tf_op jit(solution)/shard_map/ppermute | solution.py:127
  184.8 16.1 %collective-permute-start.47 = (bf16[960,128]{1,0:T(8,128)(2,1)S(1)}, bf16[960,128]{1,0:T(8,128)(2,1)S(1)}, u32[]{:S(2)}, u32[]{:S(2)}) collective-permute-start(bf16[960,128]{1,0:T(8,128)(2,1)S(1)} %copy-done.58), channel_id=1, source_target_pairs={{0,24},{1,25},{2,26},{3,27},{4,28},{5,29},{6,30},{7,31},{8,16},{9,... | collective-permute-start | bytes 737288 | tf_op jit(solution)/shard_map/ppermute | solution.py:127
  210.4 11.4 %collective-permute-start.49 = (bf16[432,128]{1,0:T(8,128)(2,1)}, bf16[432,128]{1,0:T(8,128)(2,1)S(1)}, u32[]{:S(2)}, u32[]{:S(2)}) collective-permute-start(bf16[432,128]{1,0:T(8,128)(2,1)} %get-tuple-element.138), channel_id=1, source_target_pairs={{0,16},{1,17},{2,18},{3,19},{4,20},{5,21},{6,22},{7,23},{8,24},{9,... | collective-permute-start | bytes 331784 | tf_op jit(solution)/shard_map/ppermute | solution.py:127
  211.7 10.1 %collective-permute-start.50 = (bf16[432,128]{1,0:T(8,128)(2,1)}, bf16[432,128]{1,0:T(8,128)(2,1)S(1)}, u32[]{:S(2)}, u32[]{:S(2)}) collective-permute-start(bf16[432,128]{1,0:T(8,128)(2,1)} %get-tuple-element.139), channel_id=1, source_target_pairs={{0,24},{1,25},{2,26},{3,27},{4,28},{5,29},{6,30},{7,31},{8,16},{9,... | collective-permute-start | bytes 331784 | tf_op jit(solution)/shard_map/ppermute | solution.py:127
  (79 other events, 481.0 us)

commit v15 on v12

--- a/solution.py
+++ b/solution.py
@@ -347,8 +347,7 @@
 
 
 def gather_wholes(own):
-    beside, across = swap(own, 4), swap(own, 2)
-    return own, beside, across, swap(across, 4)
+    return own, swap(own, 4), swap(own, 2), swap(own, 6)
 
 
 def gather_cores(near):
@@ -479,6 +478,10 @@
         (((left_axis,), (right_axis,)), ((), ())),
         preferred_element_type=jnp.float32,
     )
+
+
+def turned_over(rows_low):
+    return rows_low.astype(jnp.float32).T.astype(jnp.bfloat16)
 
 
 def unordered(rows_in, order_low):
@@ -567,6 +570,7 @@
     order_low = order_ref[...]
     normed = (normal_in * (1.0 + gain_in_ref[...])).astype(jnp.bfloat16)
     normed = product(normed, order_low, 1, 0).astype(jnp.bfloat16)
+    normed_turned = turned_over(normed)
     for step in range(FF // width):
         columns = slice(step * width, (step + 1) * width)
         gate_weight, up_weight = wide_tiles(step)
@@ -600,7 +604,7 @@
             (grad_hidden * gelu_ref[:, columns]).astype(jnp.bfloat16),
         ]
         for place, (grad, weight) in enumerate(zip(grads, wide_tiles(step))):
-            grad_weight = product(normed, grad, 0, 0).astype(jnp.bfloat16)
+            grad_weight = product(normed_turned, grad, 1, 0).astype(jnp.bfloat16)
             for side in range(2):
                 put_wide_tile(
                     grad_refs,
@@ -807,7 +811,7 @@
     size = sum(piece.size for piece in pieces)
     rows = pieces[0].block_rows
     cosine, sine = cosine_ref[...], sine_ref[...]
-    normed = normed_ref[...]
+    normed_turned = turned_over(normed_ref[...])
     grad_normed = jnp.zeros(grad_normed_ref.shape, jnp.float32)
     grad_gain = jnp.zeros((1, HD), jnp.float32)
     for head, start in enumerate(head_starts(pieces)[:HQ]):
@@ -819,7 +823,7 @@
         grad = grad.astype(jnp.bfloat16)
         weight = wide_head(weight_refs, size, start, rows)
         grad_normed = grad_normed + product(grad, weight, 1, 1)
-        grad_weight_ref[:, columns] = product(normed, grad, 0, 0).astype(jnp.bfloat16)
+        grad_weight_ref[:, columns] = product(normed_turned, grad, 1, 0).astype(jnp.bfloat16)
     grad_normed_ref[...] = grad_normed
     grad_gain_ref[...] = grad_gain
 
@@ -961,6 +965,7 @@
     attention_near = gather_wholes(
         *gather_own(attention_pieces, attention_parts, 1, (ffn_parts[1],))
     )
+    attention_near = tuple(held(attention_near, ffn_parts[2:]))
     attention_blocks = gather_cores(attention_near)
     ffn_own = gather_own(ffn_pieces, ffn_parts, 2, attention_near[1:])
     ffn_passed = gather_halves(*ffn_own)

time: 217 us -> 212 us (0.977)
  starting transfers between devices: 51.7 us -> 48.7 us
    ppermute x53, starting transfers between devices: 51.7 us -> 48.7 us  [swap(): lax.ppermute(value, ALL_AXES, [(source, source ^ mask) for source in rang...]
  transfers between devices with their start and end apart: 53 -> 53, of which waited for: 23 -> 24; matrix products, arithmetic and copies ran while one was open for 4% -> 4% of each run, Pallas kernels for 27% -> 27%
where the time goes in v15:
time: 212 us
  Pallas kernels  74.7 us (35%)
  waiting for transfers between devices  61.5 us (29%)
  starting transfers between devices  48.7 us (23%)
  local copies, waits for them, and re-layouts  17.6 us (8%)
  other arithmetic  8.28 us (4%)
    pallas_call x18, Pallas kernels, local_call(): pl.pallas_call(body, out_shape=outs, in_specs=specs, out_specs=tuple((pl....  74.7 us
    ppermute x53, waiting for transfers between devices, swap(): lax.ppermute(value, ALL_AXES, [(source, source ^ mask) for source in rang...  61.5 us
    ppermute x53, starting transfers between devices, swap(): lax.ppermute(value, ALL_AXES, [(source, source ^ mask) for source in rang...  48.7 us
    unnamed x130, local copies, waits for them, and re-layouts  14.3 us
  transfers between devices with their start and end apart: 53, of which 24 were waited for; matrix products, arithmetic and copies ran while one was open for 4% of the time, Pallas kernels for 27%

profile of v15, /device:TPU:0, one launch (start us, length us, event | category | flops | bytes accessed | tf_op | source)
XLA Modules:
  0.0 211.9 jit_solution(14370284722013772636)
XLA Ops:
  1.8 3.1 %collective-permute-start.3 = (bf16[960,128]{1,0:T(8,128)(2,1)S(1)}, bf16[960,128]{1,0:T(8,128)(2,1)S(1)}, u32[]{:S(2)}, u32[]{:S(2)}) collective-permute-start(bf16[960,128]{1,0:T(8,128)(2,1)S(1)} %slice.66.refs_1_), channel_id=1, source_target_pairs={{0,8},{1,9},{2,10},{3,11},{4,12},{5,13},{6,14},{7,15},{8,0},{9,1},... | collective-permute-start | bytes 737288 | tf_op jit(solution)/shard_map/ppermute | solution.py:127
  4.9 2.5 %collective-permute-start.2 = (bf16[400,128]{1,0:T(8,128)(2,1)S(1)}, bf16[400,128]{1,0:T(8,128)(2,1)S(1)}, u32[]{:S(2)}, u32[]{:S(2)}) collective-permute-start(bf16[400,128]{1,0:T(8,128)(2,1)S(1)} %slice.65.refs_1_), channel_id=1, source_target_pairs={{0,24},{1,25},{2,26},{3,27},{4,28},{5,29},{6,30},{7,31},{8,16},{9,... | collective-permute-start | bytes 307208 | tf_op jit(solution)/shard_map/ppermute | solution.py:127
  9.4 2.5 %collective-permute-start.8 = (bf16[960,128]{1,0:T(8,128)(2,1)S(1)}, bf16[960,128]{1,0:T(8,128)(2,1)S(1)}, u32[]{:S(2)}, u32[]{:S(2)}) collective-permute-start(bf16[960,128]{1,0:T(8,128)(2,1)S(1)} %slice.66.refs_1_), channel_id=1, source_target_pairs={{0,24},{1,25},{2,26},{3,27},{4,28},{5,29},{6,30},{7,31},{8,16},{9,... | collective-permute-start | bytes 737288 | tf_op jit(solution)/shard_map/ppermute | solution.py:127
  12.5 4.0 %collective-permute-done.2.refs_4_ = bf16[400,128]{1,0:T(8,128)(2,1)S(1)} collective-permute-done((bf16[400,128]{1,0:T(8,128)(2,1)S(1)}, bf16[400,128]{1,0:T(8,128)(2,1)S(1)}, u32[]{:S(2)}, u32[]{:S(2)}) %collective-permute-start.2) | collective-permute-done | bytes 102432 | tf_op jit(solution)/shard_map/ppermute | solution.py:127
  16.5 2.0 collective-permute-done.1.refs_3_
  21.2 2.4 %collective-permute-start.6 = (bf16[1600,128]{1,0:T(8,128)(2,1)}, bf16[1600,128]{1,0:T(8,128)(2,1)S(1)}, u32[]{:S(2)}, u32[]{:S(2)}) collective-permute-start(bf16[1600,128]{1,0:T(8,128)(2,1)} %shard_map.152.refs_0_), channel_id=1, source_target_pairs={{0,6},{1,7},{2,4},{3,5},{4,2},{5,3},{6,0},{7,1},{8,14},{9,15},{10,... | collective-permute-start | bytes 1228808 | tf_op jit(solution)/shard_map/ppermute | solution.py:127
  26.2 11.8 %collective-permute-done.7.refs_4_.refs_3_ = bf16[960,128]{1,0:T(8,128)(2,1)S(1)} collective-permute-done((bf16[960,128]{1,0:T(8,128)(2,1)S(1)}, bf16[960,128]{1,0:T(8,128)(2,1)S(1)}, u32[]{:S(2)}, u32[]{:S(2)}) %collective-permute-start.7) | collective-permute-done | bytes 245792 | tf_op jit(solution)/shard_map/ppermute | solution.py:127
  43.3 2.9 %shard_map.156 = (bf16[1920,128]{1,0:T(8,128)(2,1)}, bf16[1920,128]{1,0:T(8,128)(2,1)}) custom-call(s32[1]{0:T(128)} %bitcast.refs_0_, bf16[960,128]{1,0:T(8,128)(2,1)} %copy-done.28, bf16[960,128]{1,0:T(8,128)(2,1)} %copy-done.29, bf16[960,128]{1,0:T(8,128)(2,1)} %copy-done.33, bf16[960,128]{1,0:T(8,128)(2,1)} %copy-done.32, ...), custom_call_target="tpu_custom_call" | custom-call | tf_op jit(solution)/shard_map/pallas_call | solution.py:139
  51.8 3.9 %shard_map.154 = (bf16[128,640]{1,0:T(8,128)(2,1)}, f32[128,1024]{1,0:T(8,128)}, f32[128,256]{1,0:T(8,128)}, bf16[128,1024]{1,0:T(8,128)(2,1)}, bf16[128,512]{1,0:T(8,128)(2,1)}) custom-call(s32[1]{0:T(128)} %bitcast.refs_0_, bf16[128,640]{1,0:T(8,128)(2,1)} %refs_1_.5, f32[1,640]{1,0:T(1,128)} %broadcast_in_dim.30.refs_2_, f32[1,256]{1,0:T(1,128)} %bitcast.29, ...), custom_call_target="tpu_custom_call" | custom-call | tf_op jit(solution)/shard_map/pallas_call | solution.py:139
  57.6 2.3 %collective-permute-done.18.refs_10_ = bf16[1920,128]{1,0:T(8,128)(2,1)S(1)} collective-permute-done((bf16[1920,128]{1,0:T(8,128)(2,1)}, bf16[1920,128]{1,0:T(8,128)(2,1)S(1)}, u32[]{:S(2)}, u32[]{:S(2)}) %collective-permute-start.18) | collective-permute-done | bytes 491552 | tf_op jit(solution)/shard_map/ppermute | solution.py:127
  62.1 3.0 %collective-permute-done.14.refs_15_.refs_3_.refs_10_ = bf16[128,512]{1,0:T(8,128)(2,1)S(1)} collective-permute-done((bf16[128,512]{1,0:T(8,128)(2,1)}, bf16[128,512]{1,0:T(8,128)(2,1)S(1)}, u32[]{:S(2)}, u32[]{:S(2)}) %collective-permute-start.14) | collective-permute-done | bytes 131104 | tf_op jit(solution)/shard_map/ppermute | solution.py:127
  74.2 8.5 %collective-permute-done.21.refs_1_ = bf16[1920,128]{1,0:T(8,128)(2,1)S(1)} collective-permute-done((bf16[1920,128]{1,0:T(8,128)(2,1)}, bf16[1920,128]{1,0:T(8,128)(2,1)S(1)}, u32[]{:S(2)}, u32[]{:S(2)}) %collective-permute-start.21) | collective-permute-done | bytes 491552 | tf_op jit(solution)/shard_map/ppermute | solution.py:127
  84.1 5.7 %shard_map.155 = (f32[128,2048]{1,0:T(8,128)}, bf16[128,1024]{1,0:T(8,128)(2,1)}, f32[128,640]{1,0:T(8,128)}, f32[128,640]{1,0:T(8,128)}, bf16[1024,640]{1,0:T(8,128)(2,1)}) custom-call(s32[1]{0:T(128)} %bitcast.refs_0_, bf16[128,640]{1,0:T(8,128)(2,1)} %refs_1_.5, f32[1,640]{1,0:T(1,128)} %broadcast_in_dim.14.refs_2_.refs_3_, f32[128,512]{1,0:T(8,128)} %fusion.4.refs_3_, ...), custom_call_target="tpu_custom_call" | custom-call | tf_op jit(solution)/shard_map/pallas_call | solution.py:139
  96.9 14.9 %shard_map.160 = (bf16[128,640]{1,0:T(8,128)(2,1)}, f32[128,640]{1,0:T(8,128)}, f32[1,640]{1,0:T(1,128)}, f32[1,640]{1,0:T(1,128)}, bf16[11520,128]{1,0:T(8,128)...) custom-call(s32[1]{0:T(128)} %bitcast.refs_0_, ...), custom_call_target="tpu_custom_call" | custom-call | tf_op jit(solution)/shard_map/pallas_call | solution.py:139
  112.4 5.8 %shard_map.161 = (bf16[1024,640]{1,0:T(8,128)(2,1)}, f32[128,1024]{1,0:T(8,128)}, f32[1,640]{1,0:T(1,128)}, f32[128,512]{1,0:T(8,128)}, f32[128,512]{1,0:T(8,128)}, /*index=5*/bf16[256,512]{1,0:T(8,128)(2,1)}) custom-call(s32[1]{0:T(128)} %bitcast.refs_0_, f32[128,640]{1,0:T(8,128)} %get-tuple-element.95.refs_1_.refs_10_, ...), custom_call_target="tpu_custom_call" | custom-call | tf_op jit(solution)/shard_map/pallas_call | solution.py:139
  119.8 2.6 %shard_map.162 = (bf16[1920,128]{1,0:T(8,128)(2,1)}, bf16[1920,128]{1,0:T(8,128)(2,1)}) custom-call(s32[1]{0:T(128)} %bitcast.refs_0_, bf16[3840,128]{1,0:T(8,128)(2,1)} %get-tuple-element.105.refs_1_.refs_5_, bf16[3840,128]{1,0:T(8,128)(2,1)} %copy-done.7, f32[128,1024]{1,0:T(8,128)} %get-tuple-element.100.refs_3_.refs_6_), custom_call_target="tpu_custom_call" | custom-call | tf_op jit(solution)/shard_map/pallas_call | solution.py:139
  127.7 4.6 %shard_map.163 = (bf16[3840,128]{1,0:T(8,128)(2,1)}, bf16[1920,128]{1,0:T(8,128)(2,1)}, bf16[1920,128]{1,0:T(8,128)(2,1)}, bf16[1920,128]{1,0:T(8,128)(2,1)}, bf16[2432,128]{1,0:T(8,128)(2,1)}) custom-call(s32[1]{0:T(128)} %bitcast.refs_0_, bf16[11520,128]{1,0:T(8,128)(2,1)} %get-tuple-element.101.refs_1_, bf16[11520,128]{1,0:T(8,128)(2,1)} %copy-done.8, ...), custom_call_target="tpu_custom_call" | custom-call | tf_op jit(solution)/shard_map/pallas_call | solution.py:139
  134.2 4.5 %shard_map.164 = (bf16[640,1024]{1,0:T(8,128)(2,1)}, f32[128,640]{1,0:T(8,128)}, f32[1,256]{1,0:T(1,128)}) custom-call(s32[1]{0:T(128)} %bitcast.refs_0_, f32[1,256]{1,0:T(1,128)} %bitcast.30, f32[128,128]{1,0:T(8,128)} %get-tuple-element.169.refs_5_.refs_2_.refs_4_, f32[128,128]{1,0:T(8,128)} %get-tuple-element.168.refs_6_.refs_3_.refs_5_, ...), custom_call_target="tpu_custom_call" | custom-call | tf_op jit(solution)/shard_map/pallas_call | solution.py:139
  139.7 3.2 %shard_map.165 = (bf16[1920,128]{1,0:T(8,128)(2,1)}, bf16[1920,128]{1,0:T(8,128)(2,1)}, f32[8,128]{1,0:T(8,128)}) custom-call(s32[1]{0:T(128)} %bitcast.refs_0_, bf16[1920,128]{1,0:T(8,128)(2,1)} %get-tuple-element.116.refs_1_, bf16[1920,128]{1,0:T(8,128)(2,1)} %get-tuple-element.117.refs_2_, bf16[1920,128]{1,0:T(8,128)(2,1)} %copy-done.42, ...), custom_call_target="tpu_custom_call" | custom-call | tf_op jit(solution)/shard_map/pallas_call | solution.py:139
  146.9 4.3 %collective-permute-done.33.refs_17_.refs_5_ = bf16[2432,128]{1,0:T(8,128)(2,1)S(1)} collective-permute-done((bf16[2432,128]{1,0:T(8,128)(2,1)}, bf16[2432,128]{1,0:T(8,128)(2,1)S(1)}, u32[]{:S(2)}, u32[]{:S(2)}) %collective-permute-start.33) | collective-permute-done | bytes 622624 | tf_op jit(solution)/shard_map/ppermute | solution.py:127
  152.1 4.7 %shard_map.166 = (bf16[640,512]{1,0:T(8,128)(2,1)}, bf16[128,640]{1,0:T(8,128)(2,1)}, f32[32,128]{1,0:T(8,128)}) custom-call(s32[1]{0:T(128)} %bitcast.refs_0_, bf16[128,640]{1,0:T(8,128)(2,1)} %refs_1_.5, f32[1,640]{1,0:T(1,128)} %broadcast_in_dim.30.refs_2_, f32[1,256]{1,0:T(1,128)} %bitcast.28, f32[128,128]{1,0:T(8,128)} %get-tuple-element.169.refs_5_.refs_2_.refs_4_, ...), custom_call_target="tpu_custom_call" | custom-call | tf_op jit(solution)/shard_map/pallas_call | solution.py:139
  156.8 4.3 %shard_map.167 = (bf16[4800,128]{1,0:T(8,128)(2,1)}, bf16[1632,128]{1,0:T(8,128)(2,1)}, bf16[4800,128]{1,0:T(8,128)(2,1)}, bf16[1632,128]{1,0:T(8,128)(2,1)}) custom-call(s32[1]{0:T(128)} %bitcast.refs_0_, bf16[640,1024]{1,0:T(8,128)(2,1)} %get-tuple-element.122.refs_1_, bf16[640,512]{1,0:T(8,128)(2,1)} %get-tuple-element.123.refs_2_, ...), custom_call_target="tpu_custom_call" | custom-call | tf_op jit(solution)/shard_map/pallas_call | solution.py:139
  162.5 4.2 %shard_map.169 = (f32[960,128]{1,0:T(8,128)}, bf16[960,128]{1,0:T(8,128)(2,1)}, bf16[960,128]{1,0:T(8,128)(2,1)}, bf16[960,128]{1,0:T(8,128)(2,1)}) custom-call(s32[1]{0:T(128)} %bitcast.refs_0_, bf16[3840,128]{1,0:T(8,128)(2,1)} %get-tuple-element.108.refs_15_.refs_1_, bf16[1920,128]{1,0:T(8,128)(2,1)} %copy-done.19, bf16[1920,128]{1,0:T(8,128)(2,1)} %copy-done.14, ...), custom_call_target="tpu_custom_call" | custom-call | tf_op jit(solution)/shard_map/pallas_call | solution.py:139
  166.7 2.5 %collective-permute-start.44 = (bf16[960,128]{1,0:T(8,128)(2,1)}, bf16[960,128]{1,0:T(8,128)(2,1)S(1)}, u32[]{:S(2)}, u32[]{:S(2)}) collective-permute-start(bf16[960,128]{1,0:T(8,128)(2,1)} %get-tuple-element.141), channel_id=1, source_target_pairs={{0,8},{1,9},{2,10},{3,11},{4,12},{5,13},{6,14},{7,15},{8,0},{9,1},... | collective-permute-start | bytes 737288 | tf_op jit(solution)/shard_map/ppermute | solution.py:127
  172.3 3.1 %shard_map.170 = (bf16[832,128]{1,0:T(8,128)(2,1)}, bf16[800,128]{1,0:T(8,128)(2,1)}, bf16[1600,128]{1,0:T(8,128)(2,1)}, bf16[800,128]{1,0:T(8,128)(2,1)}, bf16[...) custom-call(s32[1]{0:T(128)} %bitcast.refs_0_, ...), custom_call_target="tpu_custom_call" | custom-call | tf_op jit(solution)/shard_map/pallas_call | solution.py:139
  178.0 2.6 %collective-permute-done.44.refs_7_ = bf16[960,128]{1,0:T(8,128)(2,1)S(1)} collective-permute-done((bf16[960,128]{1,0:T(8,128)(2,1)}, bf16[960,128]{1,0:T(8,128)(2,1)S(1)}, u32[]{:S(2)}, u32[]{:S(2)}) %collective-permute-start.44) | collective-permute-done | bytes 245792 | tf_op jit(solution)/shard_map/ppermute | solution.py:127
  180.6 2.0 collective-permute-done.43.refs_4_
  183.3 2.3 %shard_map.171 = (bf16[800,128]{1,0:T(8,128)(2,1)}, bf16[832,128]{1,0:T(8,128)(2,1)}, f32[32,128]{1,0:T(8,128)}) custom-call(s32[1]{0:T(128)} %bitcast.refs_0_, bf16[800,128]{1,0:T(8,128)(2,1)} %get-tuple-element.137.refs_1_, bf16[800,128]{1,0:T(8,128)(2,1)} %get-tuple-element.138.refs_2_, bf16[832,128]{1,0:T(8,128)(2,1)} %copy-done.49, ...), custom_call_target="tpu_custom_call" | custom-call | tf_op jit(solution)/shard_map/pallas_call | solution.py:139
  189.8 4.3 %collective-permute-done.41.refs_2_ = bf16[800,128]{1,0:T(8,128)(2,1)S(1)} collective-permute-done((bf16[800,128]{1,0:T(8,128)(2,1)S(1)}, bf16[800,128]{1,0:T(8,128)(2,1)S(1)}, u32[]{:S(2)}, u32[]{:S(2)}) %collective-permute-start.41) | collective-permute-done | bytes 204832 | tf_op jit(solution)/shard_map/ppermute | solution.py:127
  197.1 2.5 %shard_map.172 = (f32[432,128]{1,0:T(8,128)}, bf16[432,128]{1,0:T(8,128)(2,1)}, bf16[432,128]{1,0:T(8,128)(2,1)}, bf16[432,128]{1,0:T(8,128)(2,1)}) custom-call(s32[1]{0:T(128)} %bitcast.refs_0_, bf16[1600,128]{1,0:T(8,128)(2,1)} %get-tuple-element.135.refs_1_, bf16[800,128]{1,0:T(8,128)(2,1)} %copy-done.50, bf16[800,128]{1,0:T(8,128)(2,1)} %copy-done.52, ...), custom_call_target="tpu_custom_call" | custom-call | tf_op jit(solution)/shard_map/pallas_call | solution.py:139
  201.9 2.2 %collective-permute-start.52 = (bf16[432,128]{1,0:T(8,128)(2,1)}, bf16[432,128]{1,0:T(8,128)(2,1)S(1)}, u32[]{:S(2)}, u32[]{:S(2)}) collective-permute-start(bf16[432,128]{1,0:T(8,128)(2,1)} %get-tuple-element.151), channel_id=1, source_target_pairs={{0,24},{1,25},{2,26},{3,27},{4,28},{5,29},{6,30},{7,31},{8,16},{9,... | collective-permute-start | bytes 331784 | tf_op jit(solution)/shard_map/ppermute | solution.py:127
  206.2 3.3 %collective-permute-done.51 = bf16[432,128]{1,0:T(8,128)(2,1)S(1)} collective-permute-done((bf16[432,128]{1,0:T(8,128)(2,1)}, bf16[432,128]{1,0:T(8,128)(2,1)S(1)}, u32[]{:S(2)}, u32[]{:S(2)}) %collective-permute-start.51) | collective-permute-done | bytes 110624 | tf_op jit(solution)/shard_map/ppermute | solution.py:127
  (258 shorter events, 78.2 us)
Async XLA Ops:
  1.8 16.7 %collective-permute-start.3 = (bf16[960,128]{1,0:T(8,128)(2,1)S(1)}, bf16[960,128]{1,0:T(8,128)(2,1)S(1)}, u32[]{:S(2)}, u32[]{:S(2)}) collective-permute-start(bf16[960,128]{1,0:T(8,128)(2,1)S(1)} %slice.66.refs_1_), channel_id=1, source_target_pairs={{0,8},{1,9},{2,10},{3,11},{4,12},{5,13},{6,14},{7,15},{8,0},{9,1},... | collective-permute-start | bytes 737288 | tf_op jit(solution)/shard_map/ppermute | solution.py:127
  4.9 11.5 %collective-permute-start.2 = (bf16[400,128]{1,0:T(8,128)(2,1)S(1)}, bf16[400,128]{1,0:T(8,128)(2,1)S(1)}, u32[]{:S(2)}, u32[]{:S(2)}) collective-permute-start(bf16[400,128]{1,0:T(8,128)(2,1)S(1)} %slice.65.refs_1_), channel_id=1, source_target_pairs={{0,24},{1,25},{2,26},{3,27},{4,28},{5,29},{6,30},{7,31},{8,16},{9,... | collective-permute-start | bytes 307208 | tf_op jit(solution)/shard_map/ppermute | solution.py:127
  7.5 11.0 %collective-permute-start.1 = (bf16[400,128]{1,0:T(8,128)(2,1)S(1)}, bf16[400,128]{1,0:T(8,128)(2,1)S(1)}, u32[]{:S(2)}, u32[]{:S(2)}) collective-permute-start(bf16[400,128]{1,0:T(8,128)(2,1)S(1)} %slice.65.refs_1_), channel_id=1, source_target_pairs={{0,16},{1,17},{2,18},{3,19},{4,20},{5,21},{6,22},{7,23},{8,24},{9,... | collective-permute-start | bytes 307208 | tf_op jit(solution)/shard_map/ppermute | solution.py:127
  7.7 10.8 %collective-permute-start = (bf16[400,128]{1,0:T(8,128)(2,1)S(1)}, bf16[400,128]{1,0:T(8,128)(2,1)S(1)}, u32[]{:S(2)}, u32[]{:S(2)}) collective-permute-start(bf16[400,128]{1,0:T(8,128)(2,1)S(1)} %slice.65.refs_1_), channel_id=1, source_target_pairs={{0,8},{1,9},{2,10},{3,11},{4,12},{5,13},{6,14},{7,15},{8,0},{9,1},... | collective-permute-start | bytes 307208 | tf_op jit(solution)/shard_map/ppermute | solution.py:127
  9.4 16.8 %collective-permute-start.8 = (bf16[960,128]{1,0:T(8,128)(2,1)S(1)}, bf16[960,128]{1,0:T(8,128)(2,1)S(1)}, u32[]{:S(2)}, u32[]{:S(2)}) collective-permute-start(bf16[960,128]{1,0:T(8,128)(2,1)S(1)} %slice.66.refs_1_), channel_id=1, source_target_pairs={{0,24},{1,25},{2,26},{3,27},{4,28},{5,29},{6,30},{7,31},{8,16},{9,... | collective-permute-start | bytes 737288 | tf_op jit(solution)/shard_map/ppermute | solution.py:127
  16.5 21.5 %collective-permute-start.7 = (bf16[960,128]{1,0:T(8,128)(2,1)S(1)}, bf16[960,128]{1,0:T(8,128)(2,1)S(1)}, u32[]{:S(2)}, u32[]{:S(2)}) collective-permute-start(bf16[960,128]{1,0:T(8,128)(2,1)S(1)} %slice.66.refs_1_), channel_id=1, source_target_pairs={{0,16},{1,17},{2,18},{3,19},{4,20},{5,21},{6,22},{7,23},{8,24},{9,... | collective-permute-start | bytes 737288 | tf_op jit(solution)/shard_map/ppermute | solution.py:127
  21.2 16.7 %collective-permute-start.6 = (bf16[1600,128]{1,0:T(8,128)(2,1)}, bf16[1600,128]{1,0:T(8,128)(2,1)S(1)}, u32[]{:S(2)}, u32[]{:S(2)}) collective-permute-start(bf16[1600,128]{1,0:T(8,128)(2,1)} %shard_map.152.refs_0_), channel_id=1, source_target_pairs={{0,6},{1,7},{2,4},{3,5},{4,2},{5,3},{6,0},{7,1},{8,14},{9,15},{10,... | collective-permute-start | bytes 1228808 | tf_op jit(solution)/shard_map/ppermute | solution.py:127
  23.7 16.1 %collective-permute-start.5 = (bf16[1600,128]{1,0:T(8,128)(2,1)}, bf16[1600,128]{1,0:T(8,128)(2,1)S(1)}, u32[]{:S(2)}, u32[]{:S(2)}) collective-permute-start(bf16[1600,128]{1,0:T(8,128)(2,1)} %shard_map.152.refs_0_), channel_id=1, source_target_pairs={{0,2},{1,3},{2,0},{3,1},{4,6},{5,7},{6,4},{7,5},{8,10},{9,11},{10,... | collective-permute-start | bytes 1228808 | tf_op jit(solution)/shard_map/ppermute | solution.py:127
  24.2 15.6 %collective-permute-start.4 = (bf16[1600,128]{1,0:T(8,128)(2,1)}, bf16[1600,128]{1,0:T(8,128)(2,1)S(1)}, u32[]{:S(2)}, u32[]{:S(2)}) collective-permute-start(bf16[1600,128]{1,0:T(8,128)(2,1)} %shard_map.152.refs_0_), channel_id=1, source_target_pairs={{0,4},{1,5},{2,6},{3,7},{4,0},{5,1},{6,2},{7,3},{8,12},{9,13},{10,... | collective-permute-start | bytes 1228808 | tf_op jit(solution)/shard_map/ppermute | solution.py:127
  46.2 13.8 %collective-permute-start.18 = (bf16[1920,128]{1,0:T(8,128)(2,1)}, bf16[1920,128]{1,0:T(8,128)(2,1)S(1)}, u32[]{:S(2)}, u32[]{:S(2)}) collective-permute-start(bf16[1920,128]{1,0:T(8,128)(2,1)} %get-tuple-element.87.refs_1_.refs_6_), channel_id=1, source_target_pairs={{0,2},{1,3},{2,0},{3,1},{4,6},{5,7},{6,4},{7,5},{8,10},{9,11},{10,... | collective-permute-start | bytes 1474568 | tf_op jit(solution)/shard_map/ppermute | solution.py:127
  47.6 14.0 %collective-permute-start.17 = (bf16[1920,128]{1,0:T(8,128)(2,1)}, bf16[1920,128]{1,0:T(8,128)(2,1)S(1)}, u32[]{:S(2)}, u32[]{:S(2)}) collective-permute-start(bf16[1920,128]{1,0:T(8,128)(2,1)} %get-tuple-element.88.refs_7_), channel_id=1, source_target_pairs={{0,4},{1,5},{2,6},{3,7},{4,0},{5,1},{6,2},{7,3},{8,12},{9,13},{10,... | collective-permute-start | bytes 1474568 | tf_op jit(solution)/shard_map/ppermute | solution.py:127
  56.0 9.2 %collective-permute-start.14 = (bf16[128,512]{1,0:T(8,128)(2,1)}, bf16[128,512]{1,0:T(8,128)(2,1)S(1)}, u32[]{:S(2)}, u32[]{:S(2)}) collective-permute-start(bf16[128,512]{1,0:T(8,128)(2,1)} %get-tuple-element.85.refs_13_.refs_2_.refs_8_), channel_id=1, source_target_pairs={{0,2},{1,3},{2,0},{3,1},{4,6},{5,7},{6,4},{7,5},{8,10},{9,11},{10,... | collective-permute-start | bytes 393224 | tf_op jit(solution)/shard_map/ppermute | solution.py:127
  60.0 12.8 %collective-permute-start.20 = (bf16[1920,128]{1,0:T(8,128)(2,1)S(1)}, bf16[1920,128]{1,0:T(8,128)(2,1)S(1)}, u32[]{:S(2)}, u32[]{:S(2)}) collective-permute-start(bf16[1920,128]{1,0:T(8,128)(2,1)S(1)} %collective-permute-done.18.refs_10_), channel_id=1, source_target_pairs={{0,4},{1,5},{2,6},{3,7},{4,0},{5,1},{6,2},{7,3},{8,12},{9,13},{10,... | collective-permute-start | bytes 1474568 | tf_op jit(solution)/shard_map/ppermute | solution.py:127
  68.3 14.3 %collective-permute-start.21 = (bf16[1920,128]{1,0:T(8,128)(2,1)}, bf16[1920,128]{1,0:T(8,128)(2,1)S(1)}, u32[]{:S(2)}, u32[]{:S(2)}) collective-permute-start(bf16[1920,128]{1,0:T(8,128)(2,1)} %shard_map.158), channel_id=1, source_target_pairs={{0,2},{1,3},{2,0},{3,1},{4,6},{5,7},{6,4},{7,5},{8,10},{9,11},{10,... | collective-permute-start | bytes 1474568 | tf_op jit(solution)/shard_map/ppermute | solution.py:127
  69.7 20.1 %collective-permute-start.22 = (bf16[1920,128]{1,0:T(8,128)(2,1)S(1)}, bf16[1920,128]{1,0:T(8,128)(2,1)S(1)}, u32[]{:S(2)}, u32[]{:S(2)}) collective-permute-start(bf16[1920,128]{1,0:T(8,128)(2,1)S(1)} %copy-done.15), channel_id=1, source_target_pairs={{0,1},{1,0},{2,3},{3,2},{4,5},{5,4},{6,7},{7,6},{8,9},{9,8},{10,11... | collective-permute-start | bytes 1474568 | tf_op jit(solution)/shard_map/ppermute | solution.py:127
  69.8 22.6 %collective-permute-start.23 = (bf16[1920,128]{1,0:T(8,128)(2,1)S(1)}, bf16[1920,128]{1,0:T(8,128)(2,1)}, u32[]{:S(2)}, u32[]{:S(2)}) collective-permute-start(bf16[1920,128]{1,0:T(8,128)(2,1)S(1)} %copy-done.36), channel_id=1, source_target_pairs={{0,1},{1,0},{2,3},{3,2},{4,5},{5,4},{6,7},{7,6},{8,9},{9,8},{10,11... | collective-permute-start | bytes 1474568 | tf_op jit(solution)/shard_map/ppermute | solution.py:127
  70.3 21.6 %collective-permute-start.19 = (bf16[1920,128]{1,0:T(8,128)(2,1)S(1)}, bf16[1920,128]{1,0:T(8,128)(2,1)}, u32[]{:S(2)}, u32[]{:S(2)}) collective-permute-start(bf16[1920,128]{1,0:T(8,128)(2,1)S(1)} %copy-done.36), channel_id=1, source_target_pairs={{0,2},{1,3},{2,0},{3,1},{4,6},{5,7},{6,4},{7,5},{8,10},{9,11},{10,... | collective-permute-start | bytes 1474568 | tf_op jit(solution)/shard_map/ppermute | solution.py:127
  72.8 19.2 %collective-permute-start.16 = (bf16[1920,128]{1,0:T(8,128)(2,1)}, bf16[1920,128]{1,0:T(8,128)(2,1)}, u32[]{:S(2)}, u32[]{:S(2)}) collective-permute-start(bf16[1920,128]{1,0:T(8,128)(2,1)} %shard_map.157), channel_id=1, source_target_pairs={{0,4},{1,5},{2,6},{3,7},{4,0},{5,1},{6,2},{7,3},{8,12},{9,13},{10,... | collective-permute-start | bytes 1474568 | tf_op jit(solution)/shard_map/ppermute | solution.py:127
  82.6 9.9 %collective-permute-start.26 = (bf16[1920,128]{1,0:T(8,128)(2,1)S(1)}, bf16[1920,128]{1,0:T(8,128)(2,1)}, u32[]{:S(2)}, u32[]{:S(2)}) collective-permute-start(bf16[1920,128]{1,0:T(8,128)(2,1)S(1)} %collective-permute-done.18.refs_10_), channel_id=1, source_target_pairs={{0,1},{1,0},{2,3},{3,2},{4,5},{5,4},{6,7},{7,6},{8,9},{9,8},{10,11... | collective-permute-start | bytes 1474568 | tf_op jit(solution)/shard_map/ppermute | solution.py:127
  111.8 14.3 %collective-permute-start.30 = (bf16[11520,128]{1,0:T(8,128)(2,1)}, bf16[11520,128]{1,0:T(8,128)(2,1)S(1)}, u32[]{:S(2)}, u32[]{:S(2)}) collective-permute-start(bf16[11520,128]{1,0:T(8,128)(2,1)} %get-tuple-element.102), channel_id=1, source_target_pairs={{0,1},{1,0},{2,3},{3,2},{4,5},{5,4},{6,7},{7,6},{8,9},{9,8},{10,11... | collective-permute-start | bytes 8847368 | tf_op jit(solution)/shard_map/ppermute | solution.py:127
  122.4 16.3 %collective-permute-start.34 = (bf16[1920,128]{1,0:T(8,128)(2,1)}, bf16[1920,128]{1,0:T(8,128)(2,1)S(1)}, u32[]{:S(2)}, u32[]{:S(2)}) collective-permute-start(bf16[1920,128]{1,0:T(8,128)(2,1)} %get-tuple-element.118), channel_id=1, source_target_pairs={{0,4},{1,5},{2,6},{3,7},{4,0},{5,1},{6,2},{7,3},{8,12},{9,13},{10,... | collective-permute-start | bytes 1474568 | tf_op jit(solution)/shard_map/ppermute | solution.py:127
  123.6 15.2 %collective-permute-start.35 = (bf16[1920,128]{1,0:T(8,128)(2,1)}, bf16[1920,128]{1,0:T(8,128)(2,1)S(1)}, u32[]{:S(2)}, u32[]{:S(2)}) collective-permute-start(bf16[1920,128]{1,0:T(8,128)(2,1)} %get-tuple-element.107.refs_5_), channel_id=1, source_target_pairs={{0,2},{1,3},{2,0},{3,1},{4,6},{5,7},{6,4},{7,5},{8,10},{9,11},{10,... | collective-permute-start | bytes 1474568 | tf_op jit(solution)/shard_map/ppermute | solution.py:127
  132.3 19.0 %collective-permute-start.33 = (bf16[2432,128]{1,0:T(8,128)(2,1)}, bf16[2432,128]{1,0:T(8,128)(2,1)S(1)}, u32[]{:S(2)}, u32[]{:S(2)}) collective-permute-start(bf16[2432,128]{1,0:T(8,128)(2,1)} %get-tuple-element.115), channel_id=1, source_target_pairs={{0,2},{1,3},{2,0},{3,1},{4,6},{5,7},{6,4},{7,5},{8,10},{9,11},{10,... | collective-permute-start | bytes 1867784 | tf_op jit(solution)/shard_map/ppermute | solution.py:127
  133.4 13.5 %collective-permute-start.36 = (bf16[1920,128]{1,0:T(8,128)(2,1)}, bf16[1920,128]{1,0:T(8,128)(2,1)S(1)}, u32[]{:S(2)}, u32[]{:S(2)}) collective-permute-start(bf16[1920,128]{1,0:T(8,128)(2,1)} %get-tuple-element.120), channel_id=1, source_target_pairs={{0,4},{1,5},{2,6},{3,7},{4,0},{5,1},{6,2},{7,3},{8,12},{9,13},{10,... | collective-permute-start | bytes 1474568 | tf_op jit(solution)/shard_map/ppermute | solution.py:127
  142.9 18.1 %collective-permute-start.38 = (bf16[1920,128]{1,0:T(8,128)(2,1)}, bf16[1920,128]{1,0:T(8,128)(2,1)S(1)}, u32[]{:S(2)}, u32[]{:S(2)}) collective-permute-start(bf16[1920,128]{1,0:T(8,128)(2,1)} %get-tuple-element.130), channel_id=1, source_target_pairs={{0,2},{1,3},{2,0},{3,1},{4,6},{5,7},{6,4},{7,5},{8,10},{9,11},{10,... | collective-permute-start | bytes 1474568 | tf_op jit(solution)/shard_map/ppermute | solution.py:127
  144.1 16.9 %collective-permute-start.37 = (bf16[1920,128]{1,0:T(8,128)(2,1)}, bf16[1920,128]{1,0:T(8,128)(2,1)S(1)}, u32[]{:S(2)}, u32[]{:S(2)}) collective-permute-start(bf16[1920,128]{1,0:T(8,128)(2,1)} %get-tuple-element.119.refs_26_), channel_id=1, source_target_pairs={{0,4},{1,5},{2,6},{3,7},{4,0},{5,1},{6,2},{7,3},{8,12},{9,13},{10,... | collective-permute-start | bytes 1474568 | tf_op jit(solution)/shard_map/ppermute | solution.py:127
  162.0 9.1 %collective-permute-start.39 = (bf16[4800,128]{1,0:T(8,128)(2,1)}, bf16[4800,128]{1,0:T(8,128)(2,1)S(1)}, u32[]{:S(2)}, u32[]{:S(2)}) collective-permute-start(bf16[4800,128]{1,0:T(8,128)(2,1)} %get-tuple-element.131), channel_id=1, source_target_pairs={{0,1},{1,0},{2,3},{3,2},{4,5},{5,4},{6,7},{7,6},{8,9},{9,8},{10,11... | collective-permute-start | bytes 3686408 | tf_op jit(solution)/shard_map/ppermute | solution.py:127
  162.0 9.1 %collective-permute-start.40 = (bf16[1632,128]{1,0:T(8,128)(2,1)}, bf16[1632,128]{1,0:T(8,128)(2,1)S(1)}, u32[]{:S(2)}, u32[]{:S(2)}) collective-permute-start(bf16[1632,128]{1,0:T(8,128)(2,1)} %get-tuple-element.132), channel_id=1, source_target_pairs={{0,1},{1,0},{2,3},{3,2},{4,5},{5,4},{6,7},{7,6},{8,9},{9,8},{10,11... | collective-permute-start | bytes 1253384 | tf_op jit(solution)/shard_map/ppermute | solution.py:127
  166.7 14.0 %collective-permute-start.44 = (bf16[960,128]{1,0:T(8,128)(2,1)}, bf16[960,128]{1,0:T(8,128)(2,1)S(1)}, u32[]{:S(2)}, u32[]{:S(2)}) collective-permute-start(bf16[960,128]{1,0:T(8,128)(2,1)} %get-tuple-element.141), channel_id=1, source_target_pairs={{0,8},{1,9},{2,10},{3,11},{4,12},{5,13},{6,14},{7,15},{8,0},{9,1},... | collective-permute-start | bytes 737288 | tf_op jit(solution)/shard_map/ppermute | solution.py:127
  169.1 19.9 %collective-permute-start.48 = (bf16[960,128]{1,0:T(8,128)(2,1)}, bf16[960,128]{1,0:T(8,128)(2,1)S(1)}, u32[]{:S(2)}, u32[]{:S(2)}) collective-permute-start(bf16[960,128]{1,0:T(8,128)(2,1)} %get-tuple-element.146), channel_id=1, source_target_pairs={{0,16},{1,17},{2,18},{3,19},{4,20},{5,21},{6,22},{7,23},{8,24},{9,... | collective-permute-start | bytes 737288 | tf_op jit(solution)/shard_map/ppermute | solution.py:127
  177.5 12.3 %collective-permute-start.49 = (bf16[960,128]{1,0:T(8,128)(2,1)S(1)}, bf16[960,128]{1,0:T(8,128)(2,1)S(1)}, u32[]{:S(2)}, u32[]{:S(2)}) collective-permute-start(bf16[960,128]{1,0:T(8,128)(2,1)S(1)} %copy-done.62), channel_id=1, source_target_pairs={{0,24},{1,25},{2,26},{3,27},{4,28},{5,29},{6,30},{7,31},{8,16},{9,... | collective-permute-start | bytes 737288 | tf_op jit(solution)/shard_map/ppermute | solution.py:127
  185.7 10.7 %collective-permute-start.46 = (bf16[832,128]{1,0:T(8,128)(2,1)}, bf16[832,128]{1,0:T(8,128)(2,1)S(1)}, u32[]{:S(2)}, u32[]{:S(2)}) collective-permute-start(bf16[832,128]{1,0:T(8,128)(2,1)} %get-tuple-element.143), channel_id=1, source_target_pairs={{0,2},{1,3},{2,0},{3,1},{4,6},{5,7},{6,4},{7,5},{8,10},{9,11},{10,... | collective-permute-start | bytes 638984 | tf_op jit(solution)/shard_map/ppermute | solution.py:127
  (86 other events, 502.4 us)

commit v16 on v15

--- a/solution.py
+++ b/solution.py
@@ -341,7 +341,8 @@
 
 def gather_rest(first, second, beside_second, across_first, keys, behind):
     beside_first, across_second = swap(copied(first, keys[:1]), 4), swap(second, 2)
-    over_x, over_y = swap(across_first, 4), swap(copied(beside_second, keys[1:]), 2)
+    over_x = swap(across_first, 4)
+    over_y = swap(copied(beside_second, (*keys[1:], across_second)), 2)
     diagonal = held((over_x, over_y), behind)
     return first, second, beside_first, beside_second, across_first, across_second, *diagonal
 

time: 212 us -> 222 us (1.047)
  waiting for transfers between devices: 61.5 us -> 70.3 us
    ppermute x53, waiting for transfers between devices: 61.5 us -> 70.3 us  [swap(): lax.ppermute(value, ALL_AXES, [(source, source ^ mask) for source in rang...]
    unnamed x130 -> x136, local copies, waits for them, and re-layouts: 14.3 us -> 13.3 us
  transfers between devices with their start and end apart: 53 -> 53, of which waited for: 24 -> 24; matrix products, arithmetic and copies ran while one was open for 4% -> 4% of each run, Pallas kernels for 27% -> 26%
where the time goes in v16:
time: 222 us; the launch traced here: 221 us
  Pallas kernels  74.9 us (34%)
  waiting for transfers between devices  70.3 us (32%)
  starting transfers between devices  49.6 us (22%)
  local copies, waits for them, and re-layouts  16.5 us (7%)
  other arithmetic  8.77 us (4%)
    pallas_call x18, Pallas kernels, local_call(): pl.pallas_call(body, out_shape=outs, in_specs=specs, out_specs=tuple((pl....  74.9 us
    ppermute x53, waiting for transfers between devices, swap(): lax.ppermute(value, ALL_AXES, [(source, source ^ mask) for source in rang...  70.3 us
    ppermute x53, starting transfers between devices, swap(): lax.ppermute(value, ALL_AXES, [(source, source ^ mask) for source in rang...  49.6 us
    unnamed x136, local copies, waits for them, and re-layouts  13.3 us
  transfers between devices with their start and end apart: 53, of which 24 were waited for; matrix products, arithmetic and copies ran while one was open for 4% of the time, Pallas kernels for 26%

profile of v16, /device:TPU:0, one launch (start us, length us, event | category | flops | bytes accessed | tf_op | source)
XLA Modules:
  0.0 221.2 jit_solution(15931129045784782406)
XLA Ops:
  1.8 5.1 %collective-permute-start.2 = (bf16[400,128]{1,0:T(8,128)(2,1)S(1)}, bf16[400,128]{1,0:T(8,128)(2,1)S(1)}, u32[]{:S(2)}, u32[]{:S(2)}) collective-permute-start(bf16[400,128]{1,0:T(8,128)(2,1)S(1)} %slice.65.refs_1_), channel_id=1, source_target_pairs={{0,24},{1,25},{2,26},{3,27},{4,28},{5,29},{6,30},{7,31},{8,16},{9,... | collective-permute-start | bytes 307208 | tf_op jit(solution)/shard_map/ppermute | solution.py:127
  7.6 3.8 %collective-permute-start.8 = (bf16[960,128]{1,0:T(8,128)(2,1)S(1)}, bf16[960,128]{1,0:T(8,128)(2,1)S(1)}, u32[]{:S(2)}, u32[]{:S(2)}) collective-permute-start(bf16[960,128]{1,0:T(8,128)(2,1)S(1)} %slice.66.refs_1_), channel_id=1, source_target_pairs={{0,24},{1,25},{2,26},{3,27},{4,28},{5,29},{6,30},{7,31},{8,16},{9,... | collective-permute-start | bytes 737288 | tf_op jit(solution)/shard_map/ppermute | solution.py:127
  12.1 4.2 %collective-permute-start.7 = (bf16[960,128]{1,0:T(8,128)(2,1)S(1)}, bf16[960,128]{1,0:T(8,128)(2,1)S(1)}, u32[]{:S(2)}, u32[]{:S(2)}) collective-permute-start(bf16[960,128]{1,0:T(8,128)(2,1)S(1)} %slice.66.refs_1_), channel_id=1, source_target_pairs={{0,16},{1,17},{2,18},{3,19},{4,20},{5,21},{6,22},{7,23},{8,24},{9,... | collective-permute-start | bytes 737288 | tf_op jit(solution)/shard_map/ppermute | solution.py:127
  16.4 5.4 %collective-permute-done.1.refs_3_ = bf16[400,128]{1,0:T(8,128)(2,1)S(1)} collective-permute-done((bf16[400,128]{1,0:T(8,128)(2,1)S(1)}, bf16[400,128]{1,0:T(8,128)(2,1)S(1)}, u32[]{:S(2)}, u32[]{:S(2)}) %collective-permute-start.1) | collective-permute-done | bytes 102432 | tf_op jit(solution)/shard_map/ppermute | solution.py:127
  21.8 3.5 %collective-permute-done.3.refs_5_.refs_2_ = bf16[960,128]{1,0:T(8,128)(2,1)S(1)} collective-permute-done((bf16[960,128]{1,0:T(8,128)(2,1)S(1)}, bf16[960,128]{1,0:T(8,128)(2,1)S(1)}, u32[]{:S(2)}, u32[]{:S(2)}) %collective-permute-start.3) | collective-permute-done | bytes 245792 | tf_op jit(solution)/shard_map/ppermute | solution.py:127
  27.9 2.5 %collective-permute-start.6 = (bf16[1600,128]{1,0:T(8,128)(2,1)}, bf16[1600,128]{1,0:T(8,128)(2,1)S(1)}, u32[]{:S(2)}, u32[]{:S(2)}) collective-permute-start(bf16[1600,128]{1,0:T(8,128)(2,1)} %shard_map.152.refs_0_), channel_id=1, source_target_pairs={{0,6},{1,7},{2,4},{3,5},{4,2},{5,3},{6,0},{7,1},{8,14},{9,15},{10,... | collective-permute-start | bytes 1228808 | tf_op jit(solution)/shard_map/ppermute | solution.py:127
  32.5 4.1 %collective-permute-done.7.refs_4_.refs_3_ = bf16[960,128]{1,0:T(8,128)(2,1)S(1)} collective-permute-done((bf16[960,128]{1,0:T(8,128)(2,1)S(1)}, bf16[960,128]{1,0:T(8,128)(2,1)S(1)}, u32[]{:S(2)}, u32[]{:S(2)}) %collective-permute-start.7) | collective-permute-done | bytes 245792 | tf_op jit(solution)/shard_map/ppermute | solution.py:127
  36.6 4.8 %collective-permute-done.6.refs_3_ = bf16[1600,128]{1,0:T(8,128)(2,1)S(1)} collective-permute-done((bf16[1600,128]{1,0:T(8,128)(2,1)}, bf16[1600,128]{1,0:T(8,128)(2,1)S(1)}, u32[]{:S(2)}, u32[]{:S(2)}) %collective-permute-start.6) | collective-permute-done | bytes 409632 | tf_op jit(solution)/shard_map/ppermute | solution.py:127
  41.5 7.0 %collective-permute-done.5.refs_2_ = bf16[1600,128]{1,0:T(8,128)(2,1)S(1)} collective-permute-done((bf16[1600,128]{1,0:T(8,128)(2,1)}, bf16[1600,128]{1,0:T(8,128)(2,1)S(1)}, u32[]{:S(2)}, u32[]{:S(2)}) %collective-permute-start.5) | collective-permute-done | bytes 409632 | tf_op jit(solution)/shard_map/ppermute | solution.py:127
  50.5 2.9 %shard_map.156 = (bf16[1920,128]{1,0:T(8,128)(2,1)}, bf16[1920,128]{1,0:T(8,128)(2,1)}) custom-call(s32[1]{0:T(128)} %bitcast.refs_0_, bf16[960,128]{1,0:T(8,128)(2,1)} %copy-done.30, bf16[960,128]{1,0:T(8,128)(2,1)} %copy-done.32, bf16[960,128]{1,0:T(8,128)(2,1)} %copy-done.35, bf16[960,128]{1,0:T(8,128)(2,1)} %copy-done.34, ...), custom_call_target="tpu_custom_call" | custom-call | tf_op jit(solution)/shard_map/pallas_call | solution.py:139
  58.2 9.6 %collective-permute-done.18.refs_10_ = bf16[1920,128]{1,0:T(8,128)(2,1)} collective-permute-done((bf16[1920,128]{1,0:T(8,128)(2,1)}, bf16[1920,128]{1,0:T(8,128)(2,1)}, u32[]{:S(2)}, u32[]{:S(2)}) %collective-permute-start.18) | collective-permute-done | bytes 491552 | tf_op jit(solution)/shard_map/ppermute | solution.py:127
  72.5 3.9 %shard_map.154 = (bf16[128,640]{1,0:T(8,128)(2,1)}, f32[128,1024]{1,0:T(8,128)}, f32[128,256]{1,0:T(8,128)}, bf16[128,1024]{1,0:T(8,128)(2,1)}, bf16[128,512]{1,0:T(8,128)(2,1)}) custom-call(s32[1]{0:T(128)} %bitcast.refs_0_, bf16[128,640]{1,0:T(8,128)(2,1)} %refs_1_.5, f32[1,640]{1,0:T(1,128)} %broadcast_in_dim.30.refs_2_, f32[1,256]{1,0:T(1,128)} %bitcast.29, ...), custom_call_target="tpu_custom_call" | custom-call | tf_op jit(solution)/shard_map/pallas_call | solution.py:139
  89.8 5.8 %shard_map.155 = (f32[128,2048]{1,0:T(8,128)}, bf16[128,1024]{1,0:T(8,128)(2,1)}, f32[128,640]{1,0:T(8,128)}, f32[128,640]{1,0:T(8,128)}, bf16[1024,640]{1,0:T(8,128)(2,1)}) custom-call(s32[1]{0:T(128)} %bitcast.refs_0_, bf16[128,640]{1,0:T(8,128)(2,1)} %refs_1_.5, f32[1,640]{1,0:T(1,128)} %broadcast_in_dim.14.refs_2_.refs_3_, f32[128,512]{1,0:T(8,128)} %fusion.4.refs_3_, ...), custom_call_target="tpu_custom_call" | custom-call | tf_op jit(solution)/shard_map/pallas_call | solution.py:139
  95.6 5.9 %collective-permute-done.21.refs_1_ = bf16[1920,128]{1,0:T(8,128)(2,1)S(1)} collective-permute-done((bf16[1920,128]{1,0:T(8,128)(2,1)}, bf16[1920,128]{1,0:T(8,128)(2,1)S(1)}, u32[]{:S(2)}, u32[]{:S(2)}) %collective-permute-start.21) | collective-permute-done | bytes 491552 | tf_op jit(solution)/shard_map/ppermute | solution.py:127
  107.4 14.9 %shard_map.160 = (bf16[128,640]{1,0:T(8,128)(2,1)}, f32[128,640]{1,0:T(8,128)}, f32[1,640]{1,0:T(1,128)}, f32[1,640]{1,0:T(1,128)}, bf16[11520,128]{1,0:T(8,128)...) custom-call(s32[1]{0:T(128)} %bitcast.refs_0_, ...), custom_call_target="tpu_custom_call" | custom-call | tf_op jit(solution)/shard_map/pallas_call | solution.py:139
  122.8 5.8 %shard_map.161 = (bf16[1024,640]{1,0:T(8,128)(2,1)}, f32[128,1024]{1,0:T(8,128)}, f32[1,640]{1,0:T(1,128)}, f32[128,512]{1,0:T(8,128)}, f32[128,512]{1,0:T(8,128)}, /*index=5*/bf16[256,512]{1,0:T(8,128)(2,1)}) custom-call(s32[1]{0:T(128)} %bitcast.refs_0_, f32[128,640]{1,0:T(8,128)} %get-tuple-element.95.refs_1_.refs_10_, ...), custom_call_target="tpu_custom_call" | custom-call | tf_op jit(solution)/shard_map/pallas_call | solution.py:139
  130.2 2.6 %shard_map.162 = (bf16[1920,128]{1,0:T(8,128)(2,1)}, bf16[1920,128]{1,0:T(8,128)(2,1)}) custom-call(s32[1]{0:T(128)} %bitcast.refs_0_, bf16[3840,128]{1,0:T(8,128)(2,1)} %get-tuple-element.105.refs_1_.refs_5_, bf16[3840,128]{1,0:T(8,128)(2,1)} %copy-done.9, f32[128,1024]{1,0:T(8,128)} %get-tuple-element.100.refs_3_.refs_6_), custom_call_target="tpu_custom_call" | custom-call | tf_op jit(solution)/shard_map/pallas_call | solution.py:139
  137.8 4.6 %shard_map.163 = (bf16[3840,128]{1,0:T(8,128)(2,1)}, bf16[1920,128]{1,0:T(8,128)(2,1)}, bf16[1920,128]{1,0:T(8,128)(2,1)}, bf16[1920,128]{1,0:T(8,128)(2,1)}, bf16[2432,128]{1,0:T(8,128)(2,1)}) custom-call(s32[1]{0:T(128)} %bitcast.refs_0_, bf16[11520,128]{1,0:T(8,128)(2,1)} %get-tuple-element.101.refs_1_, bf16[11520,128]{1,0:T(8,128)(2,1)} %copy-done.10, ...), custom_call_target="tpu_custom_call" | custom-call | tf_op jit(solution)/shard_map/pallas_call | solution.py:139
  144.6 4.5 %shard_map.164 = (bf16[640,1024]{1,0:T(8,128)(2,1)}, f32[128,640]{1,0:T(8,128)}, f32[1,256]{1,0:T(1,128)}) custom-call(s32[1]{0:T(128)} %bitcast.refs_0_, f32[1,256]{1,0:T(1,128)} %bitcast.30, f32[128,128]{1,0:T(8,128)} %get-tuple-element.169.refs_5_.refs_2_.refs_4_, f32[128,128]{1,0:T(8,128)} %get-tuple-element.168.refs_6_.refs_3_.refs_5_, ...), custom_call_target="tpu_custom_call" | custom-call | tf_op jit(solution)/shard_map/pallas_call | solution.py:139
  150.1 3.2 %shard_map.165 = (bf16[1920,128]{1,0:T(8,128)(2,1)}, bf16[1920,128]{1,0:T(8,128)(2,1)}, f32[8,128]{1,0:T(8,128)}) custom-call(s32[1]{0:T(128)} %bitcast.refs_0_, bf16[1920,128]{1,0:T(8,128)(2,1)} %get-tuple-element.116.refs_1_, bf16[1920,128]{1,0:T(8,128)(2,1)} %get-tuple-element.117.refs_2_, bf16[1920,128]{1,0:T(8,128)(2,1)} %copy-done.44, ...), custom_call_target="tpu_custom_call" | custom-call | tf_op jit(solution)/shard_map/pallas_call | solution.py:139
  157.5 3.6 %collective-permute-done.33.refs_17_.refs_5_ = bf16[2432,128]{1,0:T(8,128)(2,1)S(1)} collective-permute-done((bf16[2432,128]{1,0:T(8,128)(2,1)}, bf16[2432,128]{1,0:T(8,128)(2,1)S(1)}, u32[]{:S(2)}, u32[]{:S(2)}) %collective-permute-start.33) | collective-permute-done | bytes 622624 | tf_op jit(solution)/shard_map/ppermute | solution.py:127
  161.9 4.7 %shard_map.166 = (bf16[640,512]{1,0:T(8,128)(2,1)}, bf16[128,640]{1,0:T(8,128)(2,1)}, f32[32,128]{1,0:T(8,128)}) custom-call(s32[1]{0:T(128)} %bitcast.refs_0_, bf16[128,640]{1,0:T(8,128)(2,1)} %refs_1_.5, f32[1,640]{1,0:T(1,128)} %broadcast_in_dim.30.refs_2_, f32[1,256]{1,0:T(1,128)} %bitcast.28, f32[128,128]{1,0:T(8,128)} %get-tuple-element.169.refs_5_.refs_2_.refs_4_, ...), custom_call_target="tpu_custom_call" | custom-call | tf_op jit(solution)/shard_map/pallas_call | solution.py:139
  166.6 4.2 %shard_map.167 = (bf16[4800,128]{1,0:T(8,128)(2,1)}, bf16[1632,128]{1,0:T(8,128)(2,1)}, bf16[4800,128]{1,0:T(8,128)(2,1)}, bf16[1632,128]{1,0:T(8,128)(2,1)}) custom-call(s32[1]{0:T(128)} %bitcast.refs_0_, bf16[640,1024]{1,0:T(8,128)(2,1)} %get-tuple-element.122.refs_1_, bf16[640,512]{1,0:T(8,128)(2,1)} %get-tuple-element.123.refs_2_, ...), custom_call_target="tpu_custom_call" | custom-call | tf_op jit(solution)/shard_map/pallas_call | solution.py:139
  172.3 4.1 %shard_map.169 = (f32[960,128]{1,0:T(8,128)}, bf16[960,128]{1,0:T(8,128)(2,1)}, bf16[960,128]{1,0:T(8,128)(2,1)}, bf16[960,128]{1,0:T(8,128)(2,1)}) custom-call(s32[1]{0:T(128)} %bitcast.refs_0_, bf16[3840,128]{1,0:T(8,128)(2,1)} %get-tuple-element.108.refs_15_.refs_1_, bf16[1920,128]{1,0:T(8,128)(2,1)} %copy-done.19, bf16[1920,128]{1,0:T(8,128)(2,1)} %copy-done.16, ...), custom_call_target="tpu_custom_call" | custom-call | tf_op jit(solution)/shard_map/pallas_call | solution.py:139
  177.5 2.8 %collective-permute-start.48 = (bf16[960,128]{1,0:T(8,128)(2,1)}, bf16[960,128]{1,0:T(8,128)(2,1)S(1)}, u32[]{:S(2)}, u32[]{:S(2)}) collective-permute-start(bf16[960,128]{1,0:T(8,128)(2,1)} %get-tuple-element.146), channel_id=1, source_target_pairs={{0,16},{1,17},{2,18},{3,19},{4,20},{5,21},{6,22},{7,23},{8,24},{9,... | collective-permute-start | bytes 737288 | tf_op jit(solution)/shard_map/ppermute | solution.py:127
  181.4 3.1 %shard_map.170 = (bf16[832,128]{1,0:T(8,128)(2,1)}, bf16[800,128]{1,0:T(8,128)(2,1)}, bf16[1600,128]{1,0:T(8,128)(2,1)}, bf16[800,128]{1,0:T(8,128)(2,1)}, bf16[...) custom-call(s32[1]{0:T(128)} %bitcast.refs_0_, ...), custom_call_target="tpu_custom_call" | custom-call | tf_op jit(solution)/shard_map/pallas_call | solution.py:139
  186.6 2.9 %collective-permute-done.44.refs_7_ = bf16[960,128]{1,0:T(8,128)(2,1)S(1)} collective-permute-done((bf16[960,128]{1,0:T(8,128)(2,1)}, bf16[960,128]{1,0:T(8,128)(2,1)S(1)}, u32[]{:S(2)}, u32[]{:S(2)}) %collective-permute-start.44) | collective-permute-done | bytes 245792 | tf_op jit(solution)/shard_map/ppermute | solution.py:127
  189.6 2.8 %collective-permute-done.43.refs_4_ = bf16[800,128]{1,0:T(8,128)(2,1)S(1)} collective-permute-done((bf16[800,128]{1,0:T(8,128)(2,1)}, bf16[800,128]{1,0:T(8,128)(2,1)S(1)}, u32[]{:S(2)}, u32[]{:S(2)}) %collective-permute-start.43) | collective-permute-done | bytes 204832 | tf_op jit(solution)/shard_map/ppermute | solution.py:127
  199.7 3.6 %collective-permute-done.41.refs_2_ = bf16[800,128]{1,0:T(8,128)(2,1)S(1)} collective-permute-done((bf16[800,128]{1,0:T(8,128)(2,1)S(1)}, bf16[800,128]{1,0:T(8,128)(2,1)S(1)}, u32[]{:S(2)}, u32[]{:S(2)}) %collective-permute-start.41) | collective-permute-done | bytes 204832 | tf_op jit(solution)/shard_map/ppermute | solution.py:127
  206.5 2.5 %shard_map.172 = (f32[432,128]{1,0:T(8,128)}, bf16[432,128]{1,0:T(8,128)(2,1)}, bf16[432,128]{1,0:T(8,128)(2,1)}, bf16[432,128]{1,0:T(8,128)(2,1)}) custom-call(s32[1]{0:T(128)} %bitcast.refs_0_, bf16[1600,128]{1,0:T(8,128)(2,1)} %get-tuple-element.135.refs_1_, bf16[800,128]{1,0:T(8,128)(2,1)} %copy-done.52, bf16[800,128]{1,0:T(8,128)(2,1)} %copy-done.54, ...), custom_call_target="tpu_custom_call" | custom-call | tf_op jit(solution)/shard_map/pallas_call | solution.py:139
  210.5 3.0 %collective-permute-start.52 = (bf16[432,128]{1,0:T(8,128)(2,1)}, bf16[432,128]{1,0:T(8,128)(2,1)S(1)}, u32[]{:S(2)}, u32[]{:S(2)}) collective-permute-start(bf16[432,128]{1,0:T(8,128)(2,1)} %get-tuple-element.151), channel_id=1, source_target_pairs={{0,24},{1,25},{2,26},{3,27},{4,28},{5,29},{6,30},{7,31},{8,16},{9,... | collective-permute-start | bytes 331784 | tf_op jit(solution)/shard_map/ppermute | solution.py:127
  215.4 3.4 %collective-permute-done.51 = bf16[432,128]{1,0:T(8,128)(2,1)S(1)} collective-permute-done((bf16[432,128]{1,0:T(8,128)(2,1)}, bf16[432,128]{1,0:T(8,128)(2,1)S(1)}, u32[]{:S(2)}, u32[]{:S(2)}) %collective-permute-start.51) | collective-permute-done | bytes 110624 | tf_op jit(solution)/shard_map/ppermute | solution.py:127
  (264 shorter events, 75.3 us)
Async XLA Ops:
  1.8 10.3 %collective-permute-start.2 = (bf16[400,128]{1,0:T(8,128)(2,1)S(1)}, bf16[400,128]{1,0:T(8,128)(2,1)S(1)}, u32[]{:S(2)}, u32[]{:S(2)}) collective-permute-start(bf16[400,128]{1,0:T(8,128)(2,1)S(1)} %slice.65.refs_1_), channel_id=1, source_target_pairs={{0,24},{1,25},{2,26},{3,27},{4,28},{5,29},{6,30},{7,31},{8,16},{9,... | collective-permute-start | bytes 307208 | tf_op jit(solution)/shard_map/ppermute | solution.py:127
  6.9 14.8 %collective-permute-start.1 = (bf16[400,128]{1,0:T(8,128)(2,1)S(1)}, bf16[400,128]{1,0:T(8,128)(2,1)S(1)}, u32[]{:S(2)}, u32[]{:S(2)}) collective-permute-start(bf16[400,128]{1,0:T(8,128)(2,1)S(1)} %slice.65.refs_1_), channel_id=1, source_target_pairs={{0,16},{1,17},{2,18},{3,19},{4,20},{5,21},{6,22},{7,23},{8,24},{9,... | collective-permute-start | bytes 307208 | tf_op jit(solution)/shard_map/ppermute | solution.py:127
  6.9 14.8 %collective-permute-start = (bf16[400,128]{1,0:T(8,128)(2,1)S(1)}, bf16[400,128]{1,0:T(8,128)(2,1)S(1)}, u32[]{:S(2)}, u32[]{:S(2)}) collective-permute-start(bf16[400,128]{1,0:T(8,128)(2,1)S(1)} %slice.65.refs_1_), channel_id=1, source_target_pairs={{0,8},{1,9},{2,10},{3,11},{4,12},{5,13},{6,14},{7,15},{8,0},{9,1},... | collective-permute-start | bytes 307208 | tf_op jit(solution)/shard_map/ppermute | solution.py:127
  7.6 24.9 %collective-permute-start.8 = (bf16[960,128]{1,0:T(8,128)(2,1)S(1)}, bf16[960,128]{1,0:T(8,128)(2,1)S(1)}, u32[]{:S(2)}, u32[]{:S(2)}) collective-permute-start(bf16[960,128]{1,0:T(8,128)(2,1)S(1)} %slice.66.refs_1_), channel_id=1, source_target_pairs={{0,24},{1,25},{2,26},{3,27},{4,28},{5,29},{6,30},{7,31},{8,16},{9,... | collective-permute-start | bytes 737288 | tf_op jit(solution)/shard_map/ppermute | solution.py:127
  11.4 13.8 %collective-permute-start.3 = (bf16[960,128]{1,0:T(8,128)(2,1)S(1)}, bf16[960,128]{1,0:T(8,128)(2,1)S(1)}, u32[]{:S(2)}, u32[]{:S(2)}) collective-permute-start(bf16[960,128]{1,0:T(8,128)(2,1)S(1)} %slice.66.refs_1_), channel_id=1, source_target_pairs={{0,8},{1,9},{2,10},{3,11},{4,12},{5,13},{6,14},{7,15},{8,0},{9,1},... | collective-permute-start | bytes 737288 | tf_op jit(solution)/shard_map/ppermute | solution.py:127
  12.1 24.5 %collective-permute-start.7 = (bf16[960,128]{1,0:T(8,128)(2,1)S(1)}, bf16[960,128]{1,0:T(8,128)(2,1)S(1)}, u32[]{:S(2)}, u32[]{:S(2)}) collective-permute-start(bf16[960,128]{1,0:T(8,128)(2,1)S(1)} %slice.66.refs_1_), channel_id=1, source_target_pairs={{0,16},{1,17},{2,18},{3,19},{4,20},{5,21},{6,22},{7,23},{8,24},{9,... | collective-permute-start | bytes 737288 | tf_op jit(solution)/shard_map/ppermute | solution.py:127
  27.9 13.6 %collective-permute-start.6 = (bf16[1600,128]{1,0:T(8,128)(2,1)}, bf16[1600,128]{1,0:T(8,128)(2,1)S(1)}, u32[]{:S(2)}, u32[]{:S(2)}) collective-permute-start(bf16[1600,128]{1,0:T(8,128)(2,1)} %shard_map.152.refs_0_), channel_id=1, source_target_pairs={{0,6},{1,7},{2,4},{3,5},{4,2},{5,3},{6,0},{7,1},{8,14},{9,15},{10,... | collective-permute-start | bytes 1228808 | tf_op jit(solution)/shard_map/ppermute | solution.py:127
  30.4 18.1 %collective-permute-start.5 = (bf16[1600,128]{1,0:T(8,128)(2,1)}, bf16[1600,128]{1,0:T(8,128)(2,1)S(1)}, u32[]{:S(2)}, u32[]{:S(2)}) collective-permute-start(bf16[1600,128]{1,0:T(8,128)(2,1)} %shard_map.152.refs_0_), channel_id=1, source_target_pairs={{0,2},{1,3},{2,0},{3,1},{4,6},{5,7},{6,4},{7,5},{8,10},{9,11},{10,... | collective-permute-start | bytes 1228808 | tf_op jit(solution)/shard_map/ppermute | solution.py:127
  30.9 17.7 %collective-permute-start.4 = (bf16[1600,128]{1,0:T(8,128)(2,1)}, bf16[1600,128]{1,0:T(8,128)(2,1)S(1)}, u32[]{:S(2)}, u32[]{:S(2)}) collective-permute-start(bf16[1600,128]{1,0:T(8,128)(2,1)} %shard_map.152.refs_0_), channel_id=1, source_target_pairs={{0,4},{1,5},{2,6},{3,7},{4,0},{5,1},{6,2},{7,3},{8,12},{9,13},{10,... | collective-permute-start | bytes 1228808 | tf_op jit(solution)/shard_map/ppermute | solution.py:127
  53.4 14.4 %collective-permute-start.18 = (bf16[1920,128]{1,0:T(8,128)(2,1)}, bf16[1920,128]{1,0:T(8,128)(2,1)}, u32[]{:S(2)}, u32[]{:S(2)}) collective-permute-start(bf16[1920,128]{1,0:T(8,128)(2,1)} %get-tuple-element.87.refs_1_.refs_6_), channel_id=1, source_target_pairs={{0,2},{1,3},{2,0},{3,1},{4,6},{5,7},{6,4},{7,5},{8,10},{9,11},{10,... | collective-permute-start | bytes 1474568 | tf_op jit(solution)/shard_map/ppermute | solution.py:127
  54.9 22.4 %collective-permute-start.19 = (bf16[1920,128]{1,0:T(8,128)(2,1)}, bf16[1920,128]{1,0:T(8,128)(2,1)S(1)}, u32[]{:S(2)}, u32[]{:S(2)}) collective-permute-start(bf16[1920,128]{1,0:T(8,128)(2,1)} %get-tuple-element.88.refs_7_), channel_id=1, source_target_pairs={{0,2},{1,3},{2,0},{3,1},{4,6},{5,7},{6,4},{7,5},{8,10},{9,11},{10,... | collective-permute-start | bytes 1474568 | tf_op jit(solution)/shard_map/ppermute | solution.py:127
  56.0 15.6 %collective-permute-start.11 = (bf16[1600,128]{1,0:T(8,128)(2,1)S(1)}, bf16[1600,128]{1,0:T(8,128)(2,1)S(1)}, u32[]{:S(2)}, u32[]{:S(2)}) collective-permute-start(bf16[1600,128]{1,0:T(8,128)(2,1)S(1)} %copy-done.3), channel_id=1, source_target_pairs={{0,1},{1,0},{2,3},{3,2},{4,5},{5,4},{6,7},{7,6},{8,9},{9,8},{10,11... | collective-permute-start | bytes 1228808 | tf_op jit(solution)/shard_map/ppermute | solution.py:127
  56.0 15.5 %collective-permute-start.12 = (bf16[1600,128]{1,0:T(8,128)(2,1)S(1)}, bf16[1600,128]{1,0:T(8,128)(2,1)S(1)}, u32[]{:S(2)}, u32[]{:S(2)}) collective-permute-start(bf16[1600,128]{1,0:T(8,128)(2,1)S(1)} %copy-done.1), channel_id=1, source_target_pairs={{0,1},{1,0},{2,3},{3,2},{4,5},{5,4},{6,7},{7,6},{8,9},{9,8},{10,11... | collective-permute-start | bytes 1228808 | tf_op jit(solution)/shard_map/ppermute | solution.py:127
  56.6 23.5 %collective-permute-start.17 = (bf16[1920,128]{1,0:T(8,128)(2,1)}, bf16[1920,128]{1,0:T(8,128)(2,1)}, u32[]{:S(2)}, u32[]{:S(2)}) collective-permute-start(bf16[1920,128]{1,0:T(8,128)(2,1)} %get-tuple-element.88.refs_7_), channel_id=1, source_target_pairs={{0,4},{1,5},{2,6},{3,7},{4,0},{5,1},{6,2},{7,3},{8,12},{9,13},{10,... | collective-permute-start | bytes 1474568 | tf_op jit(solution)/shard_map/ppermute | solution.py:127
  67.8 20.5 %collective-permute-start.20 = (bf16[1920,128]{1,0:T(8,128)(2,1)}, bf16[1920,128]{1,0:T(8,128)(2,1)S(1)}, u32[]{:S(2)}, u32[]{:S(2)}) collective-permute-start(bf16[1920,128]{1,0:T(8,128)(2,1)} %collective-permute-done.18.refs_10_), channel_id=1, source_target_pairs={{0,4},{1,5},{2,6},{3,7},{4,0},{5,1},{6,2},{7,3},{8,12},{9,13},{10,... | collective-permute-start | bytes 1474568 | tf_op jit(solution)/shard_map/ppermute | solution.py:127
  80.2 22.1 %collective-permute-start.22 = (bf16[1920,128]{1,0:T(8,128)(2,1)S(1)}, bf16[1920,128]{1,0:T(8,128)(2,1)S(1)}, u32[]{:S(2)}, u32[]{:S(2)}) collective-permute-start(bf16[1920,128]{1,0:T(8,128)(2,1)S(1)} %copy-done.17), channel_id=1, source_target_pairs={{0,1},{1,0},{2,3},{3,2},{4,5},{5,4},{6,7},{7,6},{8,9},{9,8},{10,11... | collective-permute-start | bytes 1474568 | tf_op jit(solution)/shard_map/ppermute | solution.py:127
  82.4 20.4 %collective-permute-start.23 = (bf16[1920,128]{1,0:T(8,128)(2,1)}, bf16[1920,128]{1,0:T(8,128)(2,1)S(1)}, u32[]{:S(2)}, u32[]{:S(2)}) collective-permute-start(bf16[1920,128]{1,0:T(8,128)(2,1)} %get-tuple-element.88.refs_7_), channel_id=1, source_target_pairs={{0,1},{1,0},{2,3},{3,2},{4,5},{5,4},{6,7},{7,6},{8,9},{9,8},{10,11... | collective-permute-start | bytes 1474568 | tf_op jit(solution)/shard_map/ppermute | solution.py:127
  84.0 18.3 %collective-permute-start.16 = (bf16[1920,128]{1,0:T(8,128)(2,1)}, bf16[1920,128]{1,0:T(8,128)(2,1)S(1)}, u32[]{:S(2)}, u32[]{:S(2)}) collective-permute-start(bf16[1920,128]{1,0:T(8,128)(2,1)} %shard_map.157), channel_id=1, source_target_pairs={{0,4},{1,5},{2,6},{3,7},{4,0},{5,1},{6,2},{7,3},{8,12},{9,13},{10,... | collective-permute-start | bytes 1474568 | tf_op jit(solution)/shard_map/ppermute | solution.py:127
  85.8 17.1 %collective-permute-start.26 = (bf16[1920,128]{1,0:T(8,128)(2,1)}, bf16[1920,128]{1,0:T(8,128)(2,1)}, u32[]{:S(2)}, u32[]{:S(2)}) collective-permute-start(bf16[1920,128]{1,0:T(8,128)(2,1)} %collective-permute-done.18.refs_10_), channel_id=1, source_target_pairs={{0,1},{1,0},{2,3},{3,2},{4,5},{5,4},{6,7},{7,6},{8,9},{9,8},{10,11... | collective-permute-start | bytes 1474568 | tf_op jit(solution)/shard_map/ppermute | solution.py:127
  88.3 13.2 %collective-permute-start.21 = (bf16[1920,128]{1,0:T(8,128)(2,1)}, bf16[1920,128]{1,0:T(8,128)(2,1)S(1)}, u32[]{:S(2)}, u32[]{:S(2)}) collective-permute-start(bf16[1920,128]{1,0:T(8,128)(2,1)} %shard_map.158), channel_id=1, source_target_pairs={{0,2},{1,3},{2,0},{3,1},{4,6},{5,7},{6,4},{7,5},{8,10},{9,11},{10,... | collective-permute-start | bytes 1474568 | tf_op jit(solution)/shard_map/ppermute | solution.py:127
  122.2 14.0 %collective-permute-start.30 = (bf16[11520,128]{1,0:T(8,128)(2,1)}, bf16[11520,128]{1,0:T(8,128)(2,1)S(1)}, u32[]{:S(2)}, u32[]{:S(2)}) collective-permute-start(bf16[11520,128]{1,0:T(8,128)(2,1)} %get-tuple-element.102), channel_id=1, source_target_pairs={{0,1},{1,0},{2,3},{3,2},{4,5},{5,4},{6,7},{7,6},{8,9},{9,8},{10,11... | collective-permute-start | bytes 8847368 | tf_op jit(solution)/shard_map/ppermute | solution.py:127
  132.8 16.3 %collective-permute-start.34 = (bf16[1920,128]{1,0:T(8,128)(2,1)}, bf16[1920,128]{1,0:T(8,128)(2,1)S(1)}, u32[]{:S(2)}, u32[]{:S(2)}) collective-permute-start(bf16[1920,128]{1,0:T(8,128)(2,1)} %get-tuple-element.118), channel_id=1, source_target_pairs={{0,4},{1,5},{2,6},{3,7},{4,0},{5,1},{6,2},{7,3},{8,12},{9,13},{10,... | collective-permute-start | bytes 1474568 | tf_op jit(solution)/shard_map/ppermute | solution.py:127
  133.4 15.8 %collective-permute-start.35 = (bf16[1920,128]{1,0:T(8,128)(2,1)}, bf16[1920,128]{1,0:T(8,128)(2,1)S(1)}, u32[]{:S(2)}, u32[]{:S(2)}) collective-permute-start(bf16[1920,128]{1,0:T(8,128)(2,1)} %get-tuple-element.107.refs_5_), channel_id=1, source_target_pairs={{0,2},{1,3},{2,0},{3,1},{4,6},{5,7},{6,4},{7,5},{8,10},{9,11},{10,... | collective-permute-start | bytes 1474568 | tf_op jit(solution)/shard_map/ppermute | solution.py:127
  142.4 18.7 %collective-permute-start.33 = (bf16[2432,128]{1,0:T(8,128)(2,1)}, bf16[2432,128]{1,0:T(8,128)(2,1)S(1)}, u32[]{:S(2)}, u32[]{:S(2)}) collective-permute-start(bf16[2432,128]{1,0:T(8,128)(2,1)} %get-tuple-element.115), channel_id=1, source_target_pairs={{0,2},{1,3},{2,0},{3,1},{4,6},{5,7},{6,4},{7,5},{8,10},{9,11},{10,... | collective-permute-start | bytes 1867784 | tf_op jit(solution)/shard_map/ppermute | solution.py:127
  143.2 14.3 %collective-permute-start.36 = (bf16[1920,128]{1,0:T(8,128)(2,1)}, bf16[1920,128]{1,0:T(8,128)(2,1)S(1)}, u32[]{:S(2)}, u32[]{:S(2)}) collective-permute-start(bf16[1920,128]{1,0:T(8,128)(2,1)} %get-tuple-element.120), channel_id=1, source_target_pairs={{0,4},{1,5},{2,6},{3,7},{4,0},{5,1},{6,2},{7,3},{8,12},{9,13},{10,... | collective-permute-start | bytes 1474568 | tf_op jit(solution)/shard_map/ppermute | solution.py:127
  153.3 17.6 %collective-permute-start.38 = (bf16[1920,128]{1,0:T(8,128)(2,1)}, bf16[1920,128]{1,0:T(8,128)(2,1)S(1)}, u32[]{:S(2)}, u32[]{:S(2)}) collective-permute-start(bf16[1920,128]{1,0:T(8,128)(2,1)} %get-tuple-element.130), channel_id=1, source_target_pairs={{0,2},{1,3},{2,0},{3,1},{4,6},{5,7},{6,4},{7,5},{8,10},{9,11},{10,... | collective-permute-start | bytes 1474568 | tf_op jit(solution)/shard_map/ppermute | solution.py:127
  153.6 17.3 %collective-permute-start.37 = (bf16[1920,128]{1,0:T(8,128)(2,1)}, bf16[1920,128]{1,0:T(8,128)(2,1)S(1)}, u32[]{:S(2)}, u32[]{:S(2)}) collective-permute-start(bf16[1920,128]{1,0:T(8,128)(2,1)} %get-tuple-element.119.refs_26_), channel_id=1, source_target_pairs={{0,4},{1,5},{2,6},{3,7},{4,0},{5,1},{6,2},{7,3},{8,12},{9,13},{10,... | collective-permute-start | bytes 1474568 | tf_op jit(solution)/shard_map/ppermute | solution.py:127
  176.5 13.1 %collective-permute-start.44 = (bf16[960,128]{1,0:T(8,128)(2,1)}, bf16[960,128]{1,0:T(8,128)(2,1)S(1)}, u32[]{:S(2)}, u32[]{:S(2)}) collective-permute-start(bf16[960,128]{1,0:T(8,128)(2,1)} %get-tuple-element.141), channel_id=1, source_target_pairs={{0,8},{1,9},{2,10},{3,11},{4,12},{5,13},{6,14},{7,15},{8,0},{9,1},... | collective-permute-start | bytes 737288 | tf_op jit(solution)/shard_map/ppermute | solution.py:127
  177.5 20.7 %collective-permute-start.48 = (bf16[960,128]{1,0:T(8,128)(2,1)}, bf16[960,128]{1,0:T(8,128)(2,1)S(1)}, u32[]{:S(2)}, u32[]{:S(2)}) collective-permute-start(bf16[960,128]{1,0:T(8,128)(2,1)} %get-tuple-element.146), channel_id=1, source_target_pairs={{0,16},{1,17},{2,18},{3,19},{4,20},{5,21},{6,22},{7,23},{8,24},{9,... | collective-permute-start | bytes 737288 | tf_op jit(solution)/shard_map/ppermute | solution.py:127
  186.1 13.6 %collective-permute-start.49 = (bf16[960,128]{1,0:T(8,128)(2,1)S(1)}, bf16[960,128]{1,0:T(8,128)(2,1)S(1)}, u32[]{:S(2)}, u32[]{:S(2)}) collective-permute-start(bf16[960,128]{1,0:T(8,128)(2,1)S(1)} %copy-done.65), channel_id=1, source_target_pairs={{0,24},{1,25},{2,26},{3,27},{4,28},{5,29},{6,30},{7,31},{8,16},{9,... | collective-permute-start | bytes 737288 | tf_op jit(solution)/shard_map/ppermute | solution.py:127
  195.6 10.1 %collective-permute-start.46 = (bf16[832,128]{1,0:T(8,128)(2,1)}, bf16[832,128]{1,0:T(8,128)(2,1)S(1)}, u32[]{:S(2)}, u32[]{:S(2)}) collective-permute-start(bf16[832,128]{1,0:T(8,128)(2,1)} %get-tuple-element.143), channel_id=1, source_target_pairs={{0,2},{1,3},{2,0},{3,1},{4,6},{5,7},{6,4},{7,5},{8,10},{9,11},{10,... | collective-permute-start | bytes 638984 | tf_op jit(solution)/shard_map/ppermute | solution.py:127
  209.5 9.3 %collective-permute-start.51 = (bf16[432,128]{1,0:T(8,128)(2,1)}, bf16[432,128]{1,0:T(8,128)(2,1)S(1)}, u32[]{:S(2)}, u32[]{:S(2)}) collective-permute-start(bf16[432,128]{1,0:T(8,128)(2,1)} %get-tuple-element.150), channel_id=1, source_target_pairs={{0,16},{1,17},{2,18},{3,19},{4,20},{5,21},{6,22},{7,23},{8,24},{9,... | collective-permute-start | bytes 331784 | tf_op jit(solution)/shard_map/ppermute | solution.py:127
  (89 other events, 541.1 us)

commit v17 on v15

--- a/solution.py
+++ b/solution.py
@@ -114,6 +114,7 @@
 LOW_MASKS = (0, 4, 2, 6, 1, 5, 3, 7)
 GELU_SCALE = (2.0 / math.pi) ** 0.5
 GELU_CUBE = 0.044715
+SPARE_ROWS = 128
 VMEM_BYTES = 56 * 1024 * 1024
 
 
@@ -169,7 +170,7 @@
     parts, out_refs, flat, packed = refs[:high_count], refs[high_count:-2], refs[-2], refs[-1]
     high = index_ref[0] // LOW_COUNT
     for step, part in enumerate(parts):
-        flat[high ^ step] = part[...].astype(jnp.float32)
+        flat[high ^ step, : part.shape[0], :] = part[...].astype(jnp.float32)
     start, target = 0, 0
     for piece in pieces:
         for block in range(piece.blocks):
@@ -289,7 +290,7 @@
                 source = source + piece.own_rows
         start = start + piece.flat_rows
     for step, out_ref in enumerate(outs):
-        out_ref[:flat_rows, :] = flat[high ^ step].astype(out_ref.dtype)
+        out_ref[:flat_rows, :] = flat[high ^ step, :flat_rows, :].astype(out_ref.dtype)
         if out_ref.shape[0] > flat_rows:
             extra = extra_ref[...] + across_first_ref[half:, :].astype(jnp.float32)
             out_ref[flat_rows:, :] = extra.astype(out_ref.dtype)
@@ -312,7 +313,7 @@
         (array((size // count, LANES), jnp.bfloat16),) * count,
         parts,
         (
-            pltpu.VMEM((high_count, parts[0].shape[0], LANES), jnp.float32),
+            pltpu.VMEM((high_count, parts[0].shape[0] + SPARE_ROWS, LANES), jnp.float32),
             pltpu.VMEM((size, LANES), jnp.float32),
         ),
         behind,
@@ -451,7 +452,7 @@
         + (array((out_rows, LANES), jnp.bfloat16),) * (high_count - 1),
         terms,
         (
-            pltpu.VMEM((high_count, flat_rows, LANES), jnp.float32),
+            pltpu.VMEM((high_count, flat_rows + SPARE_ROWS, LANES), jnp.float32),
             pltpu.VMEM((size, LANES), jnp.float32),
         ),
         behind,

time: 212 us -> 212 us (level)
  no operation moved by 1% of the time
where the time goes in v17:
time: 212 us
  Pallas kernels  74.7 us (35%)
  waiting for transfers between devices  61.5 us (29%)
  starting transfers between devices  48.7 us (23%)
  local copies, waits for them, and re-layouts  17.6 us (8%)
  other arithmetic  8.28 us (4%)
    pallas_call x18, Pallas kernels, local_call(): pl.pallas_call(body, out_shape=outs, in_specs=specs, out_specs=tuple((pl....  74.7 us
    ppermute x53, waiting for transfers between devices, swap(): lax.ppermute(value, ALL_AXES, [(source, source ^ mask) for source in rang...  61.5 us
    ppermute x53, starting transfers between devices, swap(): lax.ppermute(value, ALL_AXES, [(source, source ^ mask) for source in rang...  48.7 us
    unnamed x130, local copies, waits for them, and re-layouts  14.3 us
  transfers between devices with their start and end apart: 53, of which 24 were waited for; matrix products, arithmetic and copies ran while one was open for 4% of the time, Pallas kernels for 27%

profile of v17, /device:TPU:0, one launch (start us, length us, event | category | flops | bytes accessed | tf_op | source)
XLA Modules:
  0.0 211.9 jit_solution(964031428628272296)
XLA Ops:
  1.8 3.1 %collective-permute-start.3 = (bf16[960,128]{1,0:T(8,128)(2,1)S(1)}, bf16[960,128]{1,0:T(8,128)(2,1)S(1)}, u32[]{:S(2)}, u32[]{:S(2)}) collective-permute-start(bf16[960,128]{1,0:T(8,128)(2,1)S(1)} %slice.66.refs_1_), channel_id=1, source_target_pairs={{0,8},{1,9},{2,10},{3,11},{4,12},{5,13},{6,14},{7,15},{8,0},{9,1},... | collective-permute-start | bytes 737288 | tf_op jit(solution)/shard_map/ppermute | solution.py:128
  4.9 2.5 %collective-permute-start.2 = (bf16[400,128]{1,0:T(8,128)(2,1)S(1)}, bf16[400,128]{1,0:T(8,128)(2,1)S(1)}, u32[]{:S(2)}, u32[]{:S(2)}) collective-permute-start(bf16[400,128]{1,0:T(8,128)(2,1)S(1)} %slice.65.refs_1_), channel_id=1, source_target_pairs={{0,24},{1,25},{2,26},{3,27},{4,28},{5,29},{6,30},{7,31},{8,16},{9,... | collective-permute-start | bytes 307208 | tf_op jit(solution)/shard_map/ppermute | solution.py:128
  9.4 2.5 %collective-permute-start.8 = (bf16[960,128]{1,0:T(8,128)(2,1)S(1)}, bf16[960,128]{1,0:T(8,128)(2,1)S(1)}, u32[]{:S(2)}, u32[]{:S(2)}) collective-permute-start(bf16[960,128]{1,0:T(8,128)(2,1)S(1)} %slice.66.refs_1_), channel_id=1, source_target_pairs={{0,24},{1,25},{2,26},{3,27},{4,28},{5,29},{6,30},{7,31},{8,16},{9,... | collective-permute-start | bytes 737288 | tf_op jit(solution)/shard_map/ppermute | solution.py:128
  12.5 4.0 %collective-permute-done.2.refs_4_ = bf16[400,128]{1,0:T(8,128)(2,1)S(1)} collective-permute-done((bf16[400,128]{1,0:T(8,128)(2,1)S(1)}, bf16[400,128]{1,0:T(8,128)(2,1)S(1)}, u32[]{:S(2)}, u32[]{:S(2)}) %collective-permute-start.2) | collective-permute-done | bytes 102432 | tf_op jit(solution)/shard_map/ppermute | solution.py:128
  16.5 2.0 collective-permute-done.1.refs_3_
  21.2 2.4 %collective-permute-start.6 = (bf16[1600,128]{1,0:T(8,128)(2,1)}, bf16[1600,128]{1,0:T(8,128)(2,1)S(1)}, u32[]{:S(2)}, u32[]{:S(2)}) collective-permute-start(bf16[1600,128]{1,0:T(8,128)(2,1)} %shard_map.152.refs_0_), channel_id=1, source_target_pairs={{0,6},{1,7},{2,4},{3,5},{4,2},{5,3},{6,0},{7,1},{8,14},{9,15},{10,... | collective-permute-start | bytes 1228808 | tf_op jit(solution)/shard_map/ppermute | solution.py:128
  26.2 11.8 %collective-permute-done.7.refs_4_.refs_3_ = bf16[960,128]{1,0:T(8,128)(2,1)S(1)} collective-permute-done((bf16[960,128]{1,0:T(8,128)(2,1)S(1)}, bf16[960,128]{1,0:T(8,128)(2,1)S(1)}, u32[]{:S(2)}, u32[]{:S(2)}) %collective-permute-start.7) | collective-permute-done | bytes 245792 | tf_op jit(solution)/shard_map/ppermute | solution.py:128
  43.3 2.9 %shard_map.156 = (bf16[1920,128]{1,0:T(8,128)(2,1)}, bf16[1920,128]{1,0:T(8,128)(2,1)}) custom-call(s32[1]{0:T(128)} %bitcast.refs_0_, bf16[960,128]{1,0:T(8,128)(2,1)} %copy-done.28, bf16[960,128]{1,0:T(8,128)(2,1)} %copy-done.29, bf16[960,128]{1,0:T(8,128)(2,1)} %copy-done.33, bf16[960,128]{1,0:T(8,128)(2,1)} %copy-done.32, ...), custom_call_target="tpu_custom_call" | custom-call | tf_op jit(solution)/shard_map/pallas_call | solution.py:140
  51.8 3.9 %shard_map.154 = (bf16[128,640]{1,0:T(8,128)(2,1)}, f32[128,1024]{1,0:T(8,128)}, f32[128,256]{1,0:T(8,128)}, bf16[128,1024]{1,0:T(8,128)(2,1)}, bf16[128,512]{1,0:T(8,128)(2,1)}) custom-call(s32[1]{0:T(128)} %bitcast.refs_0_, bf16[128,640]{1,0:T(8,128)(2,1)} %refs_1_.5, f32[1,640]{1,0:T(1,128)} %broadcast_in_dim.30.refs_2_, f32[1,256]{1,0:T(1,128)} %bitcast.29, ...), custom_call_target="tpu_custom_call" | custom-call | tf_op jit(solution)/shard_map/pallas_call | solution.py:140
  57.6 2.3 %collective-permute-done.18.refs_10_ = bf16[1920,128]{1,0:T(8,128)(2,1)S(1)} collective-permute-done((bf16[1920,128]{1,0:T(8,128)(2,1)}, bf16[1920,128]{1,0:T(8,128)(2,1)S(1)}, u32[]{:S(2)}, u32[]{:S(2)}) %collective-permute-start.18) | collective-permute-done | bytes 491552 | tf_op jit(solution)/shard_map/ppermute | solution.py:128
  62.1 3.0 %collective-permute-done.14.refs_15_.refs_3_.refs_10_ = bf16[128,512]{1,0:T(8,128)(2,1)S(1)} collective-permute-done((bf16[128,512]{1,0:T(8,128)(2,1)}, bf16[128,512]{1,0:T(8,128)(2,1)S(1)}, u32[]{:S(2)}, u32[]{:S(2)}) %collective-permute-start.14) | collective-permute-done | bytes 131104 | tf_op jit(solution)/shard_map/ppermute | solution.py:128
  74.2 8.5 %collective-permute-done.21.refs_1_ = bf16[1920,128]{1,0:T(8,128)(2,1)S(1)} collective-permute-done((bf16[1920,128]{1,0:T(8,128)(2,1)}, bf16[1920,128]{1,0:T(8,128)(2,1)S(1)}, u32[]{:S(2)}, u32[]{:S(2)}) %collective-permute-start.21) | collective-permute-done | bytes 491552 | tf_op jit(solution)/shard_map/ppermute | solution.py:128
  84.1 5.7 %shard_map.155 = (f32[128,2048]{1,0:T(8,128)}, bf16[128,1024]{1,0:T(8,128)(2,1)}, f32[128,640]{1,0:T(8,128)}, f32[128,640]{1,0:T(8,128)}, bf16[1024,640]{1,0:T(8,128)(2,1)}) custom-call(s32[1]{0:T(128)} %bitcast.refs_0_, bf16[128,640]{1,0:T(8,128)(2,1)} %refs_1_.5, f32[1,640]{1,0:T(1,128)} %broadcast_in_dim.14.refs_2_.refs_3_, f32[128,512]{1,0:T(8,128)} %fusion.4.refs_3_, ...), custom_call_target="tpu_custom_call" | custom-call | tf_op jit(solution)/shard_map/pallas_call | solution.py:140
  96.9 14.9 %shard_map.160 = (bf16[128,640]{1,0:T(8,128)(2,1)}, f32[128,640]{1,0:T(8,128)}, f32[1,640]{1,0:T(1,128)}, f32[1,640]{1,0:T(1,128)}, bf16[11520,128]{1,0:T(8,128)...) custom-call(s32[1]{0:T(128)} %bitcast.refs_0_, ...), custom_call_target="tpu_custom_call" | custom-call | tf_op jit(solution)/shard_map/pallas_call | solution.py:140
  112.4 5.8 %shard_map.161 = (bf16[1024,640]{1,0:T(8,128)(2,1)}, f32[128,1024]{1,0:T(8,128)}, f32[1,640]{1,0:T(1,128)}, f32[128,512]{1,0:T(8,128)}, f32[128,512]{1,0:T(8,128)}, /*index=5*/bf16[256,512]{1,0:T(8,128)(2,1)}) custom-call(s32[1]{0:T(128)} %bitcast.refs_0_, f32[128,640]{1,0:T(8,128)} %get-tuple-element.95.refs_1_.refs_10_, ...), custom_call_target="tpu_custom_call" | custom-call | tf_op jit(solution)/shard_map/pallas_call | solution.py:140
  119.8 2.6 %shard_map.162 = (bf16[1920,128]{1,0:T(8,128)(2,1)}, bf16[1920,128]{1,0:T(8,128)(2,1)}) custom-call(s32[1]{0:T(128)} %bitcast.refs_0_, bf16[3840,128]{1,0:T(8,128)(2,1)} %get-tuple-element.105.refs_1_.refs_5_, bf16[3840,128]{1,0:T(8,128)(2,1)} %copy-done.7, f32[128,1024]{1,0:T(8,128)} %get-tuple-element.100.refs_3_.refs_6_), custom_call_target="tpu_custom_call" | custom-call | tf_op jit(solution)/shard_map/pallas_call | solution.py:140
  127.7 4.6 %shard_map.163 = (bf16[3840,128]{1,0:T(8,128)(2,1)}, bf16[1920,128]{1,0:T(8,128)(2,1)}, bf16[1920,128]{1,0:T(8,128)(2,1)}, bf16[1920,128]{1,0:T(8,128)(2,1)}, bf16[2432,128]{1,0:T(8,128)(2,1)}) custom-call(s32[1]{0:T(128)} %bitcast.refs_0_, bf16[11520,128]{1,0:T(8,128)(2,1)} %get-tuple-element.101.refs_1_, bf16[11520,128]{1,0:T(8,128)(2,1)} %copy-done.8, ...), custom_call_target="tpu_custom_call" | custom-call | tf_op jit(solution)/shard_map/pallas_call | solution.py:140
  134.2 4.5 %shard_map.164 = (bf16[640,1024]{1,0:T(8,128)(2,1)}, f32[128,640]{1,0:T(8,128)}, f32[1,256]{1,0:T(1,128)}) custom-call(s32[1]{0:T(128)} %bitcast.refs_0_, f32[1,256]{1,0:T(1,128)} %bitcast.30, f32[128,128]{1,0:T(8,128)} %get-tuple-element.169.refs_5_.refs_2_.refs_4_, f32[128,128]{1,0:T(8,128)} %get-tuple-element.168.refs_6_.refs_3_.refs_5_, ...), custom_call_target="tpu_custom_call" | custom-call | tf_op jit(solution)/shard_map/pallas_call | solution.py:140
  139.7 3.2 %shard_map.165 = (bf16[1920,128]{1,0:T(8,128)(2,1)}, bf16[1920,128]{1,0:T(8,128)(2,1)}, f32[8,128]{1,0:T(8,128)}) custom-call(s32[1]{0:T(128)} %bitcast.refs_0_, bf16[1920,128]{1,0:T(8,128)(2,1)} %get-tuple-element.116.refs_1_, bf16[1920,128]{1,0:T(8,128)(2,1)} %get-tuple-element.117.refs_2_, bf16[1920,128]{1,0:T(8,128)(2,1)} %copy-done.42, ...), custom_call_target="tpu_custom_call" | custom-call | tf_op jit(solution)/shard_map/pallas_call | solution.py:140
  146.9 4.3 %collective-permute-done.33.refs_17_.refs_5_ = bf16[2432,128]{1,0:T(8,128)(2,1)S(1)} collective-permute-done((bf16[2432,128]{1,0:T(8,128)(2,1)}, bf16[2432,128]{1,0:T(8,128)(2,1)S(1)}, u32[]{:S(2)}, u32[]{:S(2)}) %collective-permute-start.33) | collective-permute-done | bytes 622624 | tf_op jit(solution)/shard_map/ppermute | solution.py:128
  152.1 4.7 %shard_map.166 = (bf16[640,512]{1,0:T(8,128)(2,1)}, bf16[128,640]{1,0:T(8,128)(2,1)}, f32[32,128]{1,0:T(8,128)}) custom-call(s32[1]{0:T(128)} %bitcast.refs_0_, bf16[128,640]{1,0:T(8,128)(2,1)} %refs_1_.5, f32[1,640]{1,0:T(1,128)} %broadcast_in_dim.30.refs_2_, f32[1,256]{1,0:T(1,128)} %bitcast.28, f32[128,128]{1,0:T(8,128)} %get-tuple-element.169.refs_5_.refs_2_.refs_4_, ...), custom_call_target="tpu_custom_call" | custom-call | tf_op jit(solution)/shard_map/pallas_call | solution.py:140
  156.8 4.3 %shard_map.167 = (bf16[4800,128]{1,0:T(8,128)(2,1)}, bf16[1632,128]{1,0:T(8,128)(2,1)}, bf16[4800,128]{1,0:T(8,128)(2,1)}, bf16[1632,128]{1,0:T(8,128)(2,1)}) custom-call(s32[1]{0:T(128)} %bitcast.refs_0_, bf16[640,1024]{1,0:T(8,128)(2,1)} %get-tuple-element.122.refs_1_, bf16[640,512]{1,0:T(8,128)(2,1)} %get-tuple-element.123.refs_2_, ...), custom_call_target="tpu_custom_call" | custom-call | tf_op jit(solution)/shard_map/pallas_call | solution.py:140
  162.5 4.2 %shard_map.169 = (f32[960,128]{1,0:T(8,128)}, bf16[960,128]{1,0:T(8,128)(2,1)}, bf16[960,128]{1,0:T(8,128)(2,1)}, bf16[960,128]{1,0:T(8,128)(2,1)}) custom-call(s32[1]{0:T(128)} %bitcast.refs_0_, bf16[3840,128]{1,0:T(8,128)(2,1)} %get-tuple-element.108.refs_15_.refs_1_, bf16[1920,128]{1,0:T(8,128)(2,1)} %copy-done.19, bf16[1920,128]{1,0:T(8,128)(2,1)} %copy-done.14, ...), custom_call_target="tpu_custom_call" | custom-call | tf_op jit(solution)/shard_map/pallas_call | solution.py:140
  166.7 2.5 %collective-permute-start.44 = (bf16[960,128]{1,0:T(8,128)(2,1)}, bf16[960,128]{1,0:T(8,128)(2,1)S(1)}, u32[]{:S(2)}, u32[]{:S(2)}) collective-permute-start(bf16[960,128]{1,0:T(8,128)(2,1)} %get-tuple-element.141), channel_id=1, source_target_pairs={{0,8},{1,9},{2,10},{3,11},{4,12},{5,13},{6,14},{7,15},{8,0},{9,1},... | collective-permute-start | bytes 737288 | tf_op jit(solution)/shard_map/ppermute | solution.py:128
  172.3 3.1 %shard_map.170 = (bf16[832,128]{1,0:T(8,128)(2,1)}, bf16[800,128]{1,0:T(8,128)(2,1)}, bf16[1600,128]{1,0:T(8,128)(2,1)}, bf16[800,128]{1,0:T(8,128)(2,1)}, bf16[...) custom-call(s32[1]{0:T(128)} %bitcast.refs_0_, ...), custom_call_target="tpu_custom_call" | custom-call | tf_op jit(solution)/shard_map/pallas_call | solution.py:140
  178.0 2.6 %collective-permute-done.44.refs_7_ = bf16[960,128]{1,0:T(8,128)(2,1)S(1)} collective-permute-done((bf16[960,128]{1,0:T(8,128)(2,1)}, bf16[960,128]{1,0:T(8,128)(2,1)S(1)}, u32[]{:S(2)}, u32[]{:S(2)}) %collective-permute-start.44) | collective-permute-done | bytes 245792 | tf_op jit(solution)/shard_map/ppermute | solution.py:128
  180.6 2.0 collective-permute-done.43.refs_4_
  183.3 2.3 %shard_map.171 = (bf16[800,128]{1,0:T(8,128)(2,1)}, bf16[832,128]{1,0:T(8,128)(2,1)}, f32[32,128]{1,0:T(8,128)}) custom-call(s32[1]{0:T(128)} %bitcast.refs_0_, bf16[800,128]{1,0:T(8,128)(2,1)} %get-tuple-element.137.refs_1_, bf16[800,128]{1,0:T(8,128)(2,1)} %get-tuple-element.138.refs_2_, bf16[832,128]{1,0:T(8,128)(2,1)} %copy-done.49, ...), custom_call_target="tpu_custom_call" | custom-call | tf_op jit(solution)/shard_map/pallas_call | solution.py:140
  189.8 4.3 %collective-permute-done.41.refs_2_ = bf16[800,128]{1,0:T(8,128)(2,1)S(1)} collective-permute-done((bf16[800,128]{1,0:T(8,128)(2,1)S(1)}, bf16[800,128]{1,0:T(8,128)(2,1)S(1)}, u32[]{:S(2)}, u32[]{:S(2)}) %collective-permute-start.41) | collective-permute-done | bytes 204832 | tf_op jit(solution)/shard_map/ppermute | solution.py:128
  197.1 2.5 %shard_map.172 = (f32[432,128]{1,0:T(8,128)}, bf16[432,128]{1,0:T(8,128)(2,1)}, bf16[432,128]{1,0:T(8,128)(2,1)}, bf16[432,128]{1,0:T(8,128)(2,1)}) custom-call(s32[1]{0:T(128)} %bitcast.refs_0_, bf16[1600,128]{1,0:T(8,128)(2,1)} %get-tuple-element.135.refs_1_, bf16[800,128]{1,0:T(8,128)(2,1)} %copy-done.50, bf16[800,128]{1,0:T(8,128)(2,1)} %copy-done.52, ...), custom_call_target="tpu_custom_call" | custom-call | tf_op jit(solution)/shard_map/pallas_call | solution.py:140
  201.9 2.2 %collective-permute-start.52 = (bf16[432,128]{1,0:T(8,128)(2,1)}, bf16[432,128]{1,0:T(8,128)(2,1)S(1)}, u32[]{:S(2)}, u32[]{:S(2)}) collective-permute-start(bf16[432,128]{1,0:T(8,128)(2,1)} %get-tuple-element.151), channel_id=1, source_target_pairs={{0,24},{1,25},{2,26},{3,27},{4,28},{5,29},{6,30},{7,31},{8,16},{9,... | collective-permute-start | bytes 331784 | tf_op jit(solution)/shard_map/ppermute | solution.py:128
  206.2 3.3 %collective-permute-done.51 = bf16[432,128]{1,0:T(8,128)(2,1)S(1)} collective-permute-done((bf16[432,128]{1,0:T(8,128)(2,1)}, bf16[432,128]{1,0:T(8,128)(2,1)S(1)}, u32[]{:S(2)}, u32[]{:S(2)}) %collective-permute-start.51) | collective-permute-done | bytes 110624 | tf_op jit(solution)/shard_map/ppermute | solution.py:128
  (258 shorter events, 78.2 us)
Async XLA Ops:
  1.8 16.7 %collective-permute-start.3 = (bf16[960,128]{1,0:T(8,128)(2,1)S(1)}, bf16[960,128]{1,0:T(8,128)(2,1)S(1)}, u32[]{:S(2)}, u32[]{:S(2)}) collective-permute-start(bf16[960,128]{1,0:T(8,128)(2,1)S(1)} %slice.66.refs_1_), channel_id=1, source_target_pairs={{0,8},{1,9},{2,10},{3,11},{4,12},{5,13},{6,14},{7,15},{8,0},{9,1},... | collective-permute-start | bytes 737288 | tf_op jit(solution)/shard_map/ppermute | solution.py:128
  4.9 11.5 %collective-permute-start.2 = (bf16[400,128]{1,0:T(8,128)(2,1)S(1)}, bf16[400,128]{1,0:T(8,128)(2,1)S(1)}, u32[]{:S(2)}, u32[]{:S(2)}) collective-permute-start(bf16[400,128]{1,0:T(8,128)(2,1)S(1)} %slice.65.refs_1_), channel_id=1, source_target_pairs={{0,24},{1,25},{2,26},{3,27},{4,28},{5,29},{6,30},{7,31},{8,16},{9,... | collective-permute-start | bytes 307208 | tf_op jit(solution)/shard_map/ppermute | solution.py:128
  7.5 11.0 %collective-permute-start.1 = (bf16[400,128]{1,0:T(8,128)(2,1)S(1)}, bf16[400,128]{1,0:T(8,128)(2,1)S(1)}, u32[]{:S(2)}, u32[]{:S(2)}) collective-permute-start(bf16[400,128]{1,0:T(8,128)(2,1)S(1)} %slice.65.refs_1_), channel_id=1, source_target_pairs={{0,16},{1,17},{2,18},{3,19},{4,20},{5,21},{6,22},{7,23},{8,24},{9,... | collective-permute-start | bytes 307208 | tf_op jit(solution)/shard_map/ppermute | solution.py:128
  7.7 10.8 %collective-permute-start = (bf16[400,128]{1,0:T(8,128)(2,1)S(1)}, bf16[400,128]{1,0:T(8,128)(2,1)S(1)}, u32[]{:S(2)}, u32[]{:S(2)}) collective-permute-start(bf16[400,128]{1,0:T(8,128)(2,1)S(1)} %slice.65.refs_1_), channel_id=1, source_target_pairs={{0,8},{1,9},{2,10},{3,11},{4,12},{5,13},{6,14},{7,15},{8,0},{9,1},... | collective-permute-start | bytes 307208 | tf_op jit(solution)/shard_map/ppermute | solution.py:128
  9.4 16.8 %collective-permute-start.8 = (bf16[960,128]{1,0:T(8,128)(2,1)S(1)}, bf16[960,128]{1,0:T(8,128)(2,1)S(1)}, u32[]{:S(2)}, u32[]{:S(2)}) collective-permute-start(bf16[960,128]{1,0:T(8,128)(2,1)S(1)} %slice.66.refs_1_), channel_id=1, source_target_pairs={{0,24},{1,25},{2,26},{3,27},{4,28},{5,29},{6,30},{7,31},{8,16},{9,... | collective-permute-start | bytes 737288 | tf_op jit(solution)/shard_map/ppermute | solution.py:128
  16.5 21.5 %collective-permute-start.7 = (bf16[960,128]{1,0:T(8,128)(2,1)S(1)}, bf16[960,128]{1,0:T(8,128)(2,1)S(1)}, u32[]{:S(2)}, u32[]{:S(2)}) collective-permute-start(bf16[960,128]{1,0:T(8,128)(2,1)S(1)} %slice.66.refs_1_), channel_id=1, source_target_pairs={{0,16},{1,17},{2,18},{3,19},{4,20},{5,21},{6,22},{7,23},{8,24},{9,... | collective-permute-start | bytes 737288 | tf_op jit(solution)/shard_map/ppermute | solution.py:128
  21.2 16.7 %collective-permute-start.6 = (bf16[1600,128]{1,0:T(8,128)(2,1)}, bf16[1600,128]{1,0:T(8,128)(2,1)S(1)}, u32[]{:S(2)}, u32[]{:S(2)}) collective-permute-start(bf16[1600,128]{1,0:T(8,128)(2,1)} %shard_map.152.refs_0_), channel_id=1, source_target_pairs={{0,6},{1,7},{2,4},{3,5},{4,2},{5,3},{6,0},{7,1},{8,14},{9,15},{10,... | collective-permute-start | bytes 1228808 | tf_op jit(solution)/shard_map/ppermute | solution.py:128
  23.7 16.1 %collective-permute-start.5 = (bf16[1600,128]{1,0:T(8,128)(2,1)}, bf16[1600,128]{1,0:T(8,128)(2,1)S(1)}, u32[]{:S(2)}, u32[]{:S(2)}) collective-permute-start(bf16[1600,128]{1,0:T(8,128)(2,1)} %shard_map.152.refs_0_), channel_id=1, source_target_pairs={{0,2},{1,3},{2,0},{3,1},{4,6},{5,7},{6,4},{7,5},{8,10},{9,11},{10,... | collective-permute-start | bytes 1228808 | tf_op jit(solution)/shard_map/ppermute | solution.py:128
  24.2 15.6 %collective-permute-start.4 = (bf16[1600,128]{1,0:T(8,128)(2,1)}, bf16[1600,128]{1,0:T(8,128)(2,1)S(1)}, u32[]{:S(2)}, u32[]{:S(2)}) collective-permute-start(bf16[1600,128]{1,0:T(8,128)(2,1)} %shard_map.152.refs_0_), channel_id=1, source_target_pairs={{0,4},{1,5},{2,6},{3,7},{4,0},{5,1},{6,2},{7,3},{8,12},{9,13},{10,... | collective-permute-start | bytes 1228808 | tf_op jit(solution)/shard_map/ppermute | solution.py:128
  46.2 13.8 %collective-permute-start.18 = (bf16[1920,128]{1,0:T(8,128)(2,1)}, bf16[1920,128]{1,0:T(8,128)(2,1)S(1)}, u32[]{:S(2)}, u32[]{:S(2)}) collective-permute-start(bf16[1920,128]{1,0:T(8,128)(2,1)} %get-tuple-element.87.refs_1_.refs_6_), channel_id=1, source_target_pairs={{0,2},{1,3},{2,0},{3,1},{4,6},{5,7},{6,4},{7,5},{8,10},{9,11},{10,... | collective-permute-start | bytes 1474568 | tf_op jit(solution)/shard_map/ppermute | solution.py:128
  47.6 14.0 %collective-permute-start.17 = (bf16[1920,128]{1,0:T(8,128)(2,1)}, bf16[1920,128]{1,0:T(8,128)(2,1)S(1)}, u32[]{:S(2)}, u32[]{:S(2)}) collective-permute-start(bf16[1920,128]{1,0:T(8,128)(2,1)} %get-tuple-element.88.refs_7_), channel_id=1, source_target_pairs={{0,4},{1,5},{2,6},{3,7},{4,0},{5,1},{6,2},{7,3},{8,12},{9,13},{10,... | collective-permute-start | bytes 1474568 | tf_op jit(solution)/shard_map/ppermute | solution.py:128
  56.0 9.2 %collective-permute-start.14 = (bf16[128,512]{1,0:T(8,128)(2,1)}, bf16[128,512]{1,0:T(8,128)(2,1)S(1)}, u32[]{:S(2)}, u32[]{:S(2)}) collective-permute-start(bf16[128,512]{1,0:T(8,128)(2,1)} %get-tuple-element.85.refs_13_.refs_2_.refs_8_), channel_id=1, source_target_pairs={{0,2},{1,3},{2,0},{3,1},{4,6},{5,7},{6,4},{7,5},{8,10},{9,11},{10,... | collective-permute-start | bytes 393224 | tf_op jit(solution)/shard_map/ppermute | solution.py:128
  60.0 12.8 %collective-permute-start.20 = (bf16[1920,128]{1,0:T(8,128)(2,1)S(1)}, bf16[1920,128]{1,0:T(8,128)(2,1)S(1)}, u32[]{:S(2)}, u32[]{:S(2)}) collective-permute-start(bf16[1920,128]{1,0:T(8,128)(2,1)S(1)} %collective-permute-done.18.refs_10_), channel_id=1, source_target_pairs={{0,4},{1,5},{2,6},{3,7},{4,0},{5,1},{6,2},{7,3},{8,12},{9,13},{10,... | collective-permute-start | bytes 1474568 | tf_op jit(solution)/shard_map/ppermute | solution.py:128
  68.3 14.3 %collective-permute-start.21 = (bf16[1920,128]{1,0:T(8,128)(2,1)}, bf16[1920,128]{1,0:T(8,128)(2,1)S(1)}, u32[]{:S(2)}, u32[]{:S(2)}) collective-permute-start(bf16[1920,128]{1,0:T(8,128)(2,1)} %shard_map.158), channel_id=1, source_target_pairs={{0,2},{1,3},{2,0},{3,1},{4,6},{5,7},{6,4},{7,5},{8,10},{9,11},{10,... | collective-permute-start | bytes 1474568 | tf_op jit(solution)/shard_map/ppermute | solution.py:128
  69.7 20.1 %collective-permute-start.22 = (bf16[1920,128]{1,0:T(8,128)(2,1)S(1)}, bf16[1920,128]{1,0:T(8,128)(2,1)S(1)}, u32[]{:S(2)}, u32[]{:S(2)}) collective-permute-start(bf16[1920,128]{1,0:T(8,128)(2,1)S(1)} %copy-done.15), channel_id=1, source_target_pairs={{0,1},{1,0},{2,3},{3,2},{4,5},{5,4},{6,7},{7,6},{8,9},{9,8},{10,11... | collective-permute-start | bytes 1474568 | tf_op jit(solution)/shard_map/ppermute | solution.py:128
  69.8 22.6 %collective-permute-start.23 = (bf16[1920,128]{1,0:T(8,128)(2,1)S(1)}, bf16[1920,128]{1,0:T(8,128)(2,1)}, u32[]{:S(2)}, u32[]{:S(2)}) collective-permute-start(bf16[1920,128]{1,0:T(8,128)(2,1)S(1)} %copy-done.36), channel_id=1, source_target_pairs={{0,1},{1,0},{2,3},{3,2},{4,5},{5,4},{6,7},{7,6},{8,9},{9,8},{10,11... | collective-permute-start | bytes 1474568 | tf_op jit(solution)/shard_map/ppermute | solution.py:128
  70.3 21.6 %collective-permute-start.19 = (bf16[1920,128]{1,0:T(8,128)(2,1)S(1)}, bf16[1920,128]{1,0:T(8,128)(2,1)}, u32[]{:S(2)}, u32[]{:S(2)}) collective-permute-start(bf16[1920,128]{1,0:T(8,128)(2,1)S(1)} %copy-done.36), channel_id=1, source_target_pairs={{0,2},{1,3},{2,0},{3,1},{4,6},{5,7},{6,4},{7,5},{8,10},{9,11},{10,... | collective-permute-start | bytes 1474568 | tf_op jit(solution)/shard_map/ppermute | solution.py:128
  72.8 19.2 %collective-permute-start.16 = (bf16[1920,128]{1,0:T(8,128)(2,1)}, bf16[1920,128]{1,0:T(8,128)(2,1)}, u32[]{:S(2)}, u32[]{:S(2)}) collective-permute-start(bf16[1920,128]{1,0:T(8,128)(2,1)} %shard_map.157), channel_id=1, source_target_pairs={{0,4},{1,5},{2,6},{3,7},{4,0},{5,1},{6,2},{7,3},{8,12},{9,13},{10,... | collective-permute-start | bytes 1474568 | tf_op jit(solution)/shard_map/ppermute | solution.py:128
  82.6 9.9 %collective-permute-start.26 = (bf16[1920,128]{1,0:T(8,128)(2,1)S(1)}, bf16[1920,128]{1,0:T(8,128)(2,1)}, u32[]{:S(2)}, u32[]{:S(2)}) collective-permute-start(bf16[1920,128]{1,0:T(8,128)(2,1)S(1)} %collective-permute-done.18.refs_10_), channel_id=1, source_target_pairs={{0,1},{1,0},{2,3},{3,2},{4,5},{5,4},{6,7},{7,6},{8,9},{9,8},{10,11... | collective-permute-start | bytes 1474568 | tf_op jit(solution)/shard_map/ppermute | solution.py:128
  111.8 14.3 %collective-permute-start.30 = (bf16[11520,128]{1,0:T(8,128)(2,1)}, bf16[11520,128]{1,0:T(8,128)(2,1)S(1)}, u32[]{:S(2)}, u32[]{:S(2)}) collective-permute-start(bf16[11520,128]{1,0:T(8,128)(2,1)} %get-tuple-element.102), channel_id=1, source_target_pairs={{0,1},{1,0},{2,3},{3,2},{4,5},{5,4},{6,7},{7,6},{8,9},{9,8},{10,11... | collective-permute-start | bytes 8847368 | tf_op jit(solution)/shard_map/ppermute | solution.py:128
  122.4 16.3 %collective-permute-start.34 = (bf16[1920,128]{1,0:T(8,128)(2,1)}, bf16[1920,128]{1,0:T(8,128)(2,1)S(1)}, u32[]{:S(2)}, u32[]{:S(2)}) collective-permute-start(bf16[1920,128]{1,0:T(8,128)(2,1)} %get-tuple-element.118), channel_id=1, source_target_pairs={{0,4},{1,5},{2,6},{3,7},{4,0},{5,1},{6,2},{7,3},{8,12},{9,13},{10,... | collective-permute-start | bytes 1474568 | tf_op jit(solution)/shard_map/ppermute | solution.py:128
  123.6 15.2 %collective-permute-start.35 = (bf16[1920,128]{1,0:T(8,128)(2,1)}, bf16[1920,128]{1,0:T(8,128)(2,1)S(1)}, u32[]{:S(2)}, u32[]{:S(2)}) collective-permute-start(bf16[1920,128]{1,0:T(8,128)(2,1)} %get-tuple-element.107.refs_5_), channel_id=1, source_target_pairs={{0,2},{1,3},{2,0},{3,1},{4,6},{5,7},{6,4},{7,5},{8,10},{9,11},{10,... | collective-permute-start | bytes 1474568 | tf_op jit(solution)/shard_map/ppermute | solution.py:128
  132.3 19.0 %collective-permute-start.33 = (bf16[2432,128]{1,0:T(8,128)(2,1)}, bf16[2432,128]{1,0:T(8,128)(2,1)S(1)}, u32[]{:S(2)}, u32[]{:S(2)}) collective-permute-start(bf16[2432,128]{1,0:T(8,128)(2,1)} %get-tuple-element.115), channel_id=1, source_target_pairs={{0,2},{1,3},{2,0},{3,1},{4,6},{5,7},{6,4},{7,5},{8,10},{9,11},{10,... | collective-permute-start | bytes 1867784 | tf_op jit(solution)/shard_map/ppermute | solution.py:128
  133.4 13.5 %collective-permute-start.36 = (bf16[1920,128]{1,0:T(8,128)(2,1)}, bf16[1920,128]{1,0:T(8,128)(2,1)S(1)}, u32[]{:S(2)}, u32[]{:S(2)}) collective-permute-start(bf16[1920,128]{1,0:T(8,128)(2,1)} %get-tuple-element.120), channel_id=1, source_target_pairs={{0,4},{1,5},{2,6},{3,7},{4,0},{5,1},{6,2},{7,3},{8,12},{9,13},{10,... | collective-permute-start | bytes 1474568 | tf_op jit(solution)/shard_map/ppermute | solution.py:128
  142.9 18.1 %collective-permute-start.38 = (bf16[1920,128]{1,0:T(8,128)(2,1)}, bf16[1920,128]{1,0:T(8,128)(2,1)S(1)}, u32[]{:S(2)}, u32[]{:S(2)}) collective-permute-start(bf16[1920,128]{1,0:T(8,128)(2,1)} %get-tuple-element.130), channel_id=1, source_target_pairs={{0,2},{1,3},{2,0},{3,1},{4,6},{5,7},{6,4},{7,5},{8,10},{9,11},{10,... | collective-permute-start | bytes 1474568 | tf_op jit(solution)/shard_map/ppermute | solution.py:128
  144.1 16.9 %collective-permute-start.37 = (bf16[1920,128]{1,0:T(8,128)(2,1)}, bf16[1920,128]{1,0:T(8,128)(2,1)S(1)}, u32[]{:S(2)}, u32[]{:S(2)}) collective-permute-start(bf16[1920,128]{1,0:T(8,128)(2,1)} %get-tuple-element.119.refs_26_), channel_id=1, source_target_pairs={{0,4},{1,5},{2,6},{3,7},{4,0},{5,1},{6,2},{7,3},{8,12},{9,13},{10,... | collective-permute-start | bytes 1474568 | tf_op jit(solution)/shard_map/ppermute | solution.py:128
  162.0 9.1 %collective-permute-start.39 = (bf16[4800,128]{1,0:T(8,128)(2,1)}, bf16[4800,128]{1,0:T(8,128)(2,1)S(1)}, u32[]{:S(2)}, u32[]{:S(2)}) collective-permute-start(bf16[4800,128]{1,0:T(8,128)(2,1)} %get-tuple-element.131), channel_id=1, source_target_pairs={{0,1},{1,0},{2,3},{3,2},{4,5},{5,4},{6,7},{7,6},{8,9},{9,8},{10,11... | collective-permute-start | bytes 3686408 | tf_op jit(solution)/shard_map/ppermute | solution.py:128
  162.0 9.1 %collective-permute-start.40 = (bf16[1632,128]{1,0:T(8,128)(2,1)}, bf16[1632,128]{1,0:T(8,128)(2,1)S(1)}, u32[]{:S(2)}, u32[]{:S(2)}) collective-permute-start(bf16[1632,128]{1,0:T(8,128)(2,1)} %get-tuple-element.132), channel_id=1, source_target_pairs={{0,1},{1,0},{2,3},{3,2},{4,5},{5,4},{6,7},{7,6},{8,9},{9,8},{10,11... | collective-permute-start | bytes 1253384 | tf_op jit(solution)/shard_map/ppermute | solution.py:128
  166.7 14.0 %collective-permute-start.44 = (bf16[960,128]{1,0:T(8,128)(2,1)}, bf16[960,128]{1,0:T(8,128)(2,1)S(1)}, u32[]{:S(2)}, u32[]{:S(2)}) collective-permute-start(bf16[960,128]{1,0:T(8,128)(2,1)} %get-tuple-element.141), channel_id=1, source_target_pairs={{0,8},{1,9},{2,10},{3,11},{4,12},{5,13},{6,14},{7,15},{8,0},{9,1},... | collective-permute-start | bytes 737288 | tf_op jit(solution)/shard_map/ppermute | solution.py:128
  169.1 19.9 %collective-permute-start.48 = (bf16[960,128]{1,0:T(8,128)(2,1)}, bf16[960,128]{1,0:T(8,128)(2,1)S(1)}, u32[]{:S(2)}, u32[]{:S(2)}) collective-permute-start(bf16[960,128]{1,0:T(8,128)(2,1)} %get-tuple-element.146), channel_id=1, source_target_pairs={{0,16},{1,17},{2,18},{3,19},{4,20},{5,21},{6,22},{7,23},{8,24},{9,... | collective-permute-start | bytes 737288 | tf_op jit(solution)/shard_map/ppermute | solution.py:128
  177.5 12.3 %collective-permute-start.49 = (bf16[960,128]{1,0:T(8,128)(2,1)S(1)}, bf16[960,128]{1,0:T(8,128)(2,1)S(1)}, u32[]{:S(2)}, u32[]{:S(2)}) collective-permute-start(bf16[960,128]{1,0:T(8,128)(2,1)S(1)} %copy-done.62), channel_id=1, source_target_pairs={{0,24},{1,25},{2,26},{3,27},{4,28},{5,29},{6,30},{7,31},{8,16},{9,... | collective-permute-start | bytes 737288 | tf_op jit(solution)/shard_map/ppermute | solution.py:128
  185.7 10.7 %collective-permute-start.46 = (bf16[832,128]{1,0:T(8,128)(2,1)}, bf16[832,128]{1,0:T(8,128)(2,1)S(1)}, u32[]{:S(2)}, u32[]{:S(2)}) collective-permute-start(bf16[832,128]{1,0:T(8,128)(2,1)} %get-tuple-element.143), channel_id=1, source_target_pairs={{0,2},{1,3},{2,0},{3,1},{4,6},{5,7},{6,4},{7,5},{8,10},{9,11},{10,... | collective-permute-start | bytes 638984 | tf_op jit(solution)/shard_map/ppermute | solution.py:128
  (86 other events, 502.4 us)
